TPU v7x, 32 devices: a whole 2x2x4 slice. The times are simulated.
32 devices in a mesh: dp: 16 (over z, x, core), mod: 2 (over y).
Axes of the slice: x: 2, y: 2, z: 4, core: 2. Of those that a mesh axis runs over, the one named last changes fastest.
Arguments:
- hidden_in: bfloat16 [32, 2, 512, 768], P('dp', 'mod'), may hold values from -6 to 6
- image_count: int32 [32], P('dp'), may hold values from 129 to 256
- text_lengths: int32 [32, 4], P('dp'), may hold values from 1 to 256, 512 in all within a row
- attend_gain: float32 [2, 768], P('mod'), may hold values from 0.5 to 1.5
- attend_shift: float32 [2, 768], P('mod'), may hold values from -1.5 to 1.5
- project_in: bfloat16 [768, 2304], replicated, may hold values from -0.21875 to 0.21875
- bias_pair: float32 [2, 768], replicated, may hold values from -1.5 to 1.5
- project_out: bfloat16 [768, 768], replicated, may hold values from -0.875 to 0.875
- project_bias: float32 [768], replicated, may hold values from -1.5 to 1.5
- feed_gain: float32 [2, 768], P('mod'), may hold values from 0.5 to 1.5
- feed_shift: float32 [2, 768], P('mod'), may hold values from -1.5 to 1.5
- expand_weight: bfloat16 [2, 768, 3072], P('mod'), may hold values from -0.21875 to 0.21875
- expand_bias: float32 [2, 3072], P('mod'), may hold values from -1.5 to 1.5
- reduce_weight: bfloat16 [2, 3072, 768], P('mod'), may hold values from -0.109375 to 0.109375
- reduce_bias: float32 [2, 768], P('mod'), may hold values from -1.5 to 1.5
- cotangent: bfloat16 [32, 2, 512, 768], P('dp', 'mod'), may hold values from -6 to 6
Outputs:
- hidden_out: bfloat16 [32, 2, 512, 768], P('dp', 'mod')
- grad_in: bfloat16 [32, 2, 512, 768], P('dp', 'mod')
- attend_gain_grad: float32 [2, 768], P('mod')
- attend_shift_grad: float32 [2, 768], P('mod')
- project_in_grad: float32 [768, 2304], replicated
- bias_pair_grad: float32 [2, 768], replicated
- project_out_grad: float32 [768, 768], replicated
- project_bias_grad: float32 [768], replicated
- feed_gain_grad: float32 [2, 768], P('mod')
- feed_shift_grad: float32 [2, 768], P('mod')
- expand_weight_grad: float32 [2, 768, 3072], P('mod')
- expand_bias_grad: float32 [2, 3072], P('mod')
- reduce_weight_grad: float32 [2, 3072, 768], P('mod')
- reduce_bias_grad: float32 [2, 768], P('mod')
All inputs are finite; a program needn't handle non-finite values.
Results may differ from a plain program's by a relative error of at most 0.011.
Values may be sent and summed in bfloat16 or wider, within the bound.
No kernel may reach another device: no remote copies, remote signals or barrier semaphores. Data moves between devices by JAX's collectives and lax.ppermute only.
A program may use at most 320 MiB of HBM per device.

v0:
```python
import jax
import jax.numpy as jnp
from jax import lax
from jax.sharding import PartitionSpec as P

HEADS = 12
HEAD = 64
IMG_PAD = 256


masked_value = -1e30
norm_eps = 1e-05


def from_behind(value, axis, steps):
    count = lax.axis_size(axis)
    leading, last = (max(0, -steps), min(count, count - steps))
    return lax.ppermute(value, axis, [(source, source + steps) for source in range(leading, last)])


def layer_norm(values, gain, shift):
    row_mean = jnp.mean(values, axis=-1, keepdims=True)
    centred = values - row_mean
    spread = jnp.mean(centred * centred, axis=-1, keepdims=True)
    return centred * lax.rsqrt(spread + norm_eps) * gain + shift


def exact_gelu(values):
    return jax.nn.gelu(values, approximate=False)


def outer_sum(left, right):
    return lax.dot_general(
        left, right, (((0,), (0,)), ((), ())), preferred_element_type=jnp.float32
    )


def back_dot(grad_rows, weight):
    return lax.dot_general(
        grad_rows, weight, (((1,), (1,)), ((), ())), preferred_element_type=jnp.float32
    )


def segment_of(lengths, row_count):
    segment_ends = jnp.cumsum(lengths)
    places = jnp.arange(row_count, dtype=jnp.int32)
    return jnp.sum((places[:, None] >= segment_ends[None, :]).astype(jnp.int32), axis=1)


def allowed_mask(live_count, lengths, is_text, row_count):
    image_live = jnp.arange(IMG_PAD, dtype=jnp.int32) < live_count
    own_live = jnp.arange(row_count, dtype=jnp.int32) < live_count
    segment = segment_of(lengths, row_count)
    same_segment = segment[:, None] == segment[None, :]
    own_part = jnp.where(
        is_text, same_segment, jnp.broadcast_to(own_live[None, :], (row_count, row_count))
    )
    far_part = jnp.broadcast_to((image_live & is_text)[None, :], (row_count, IMG_PAD))
    return jnp.concatenate([far_part, own_part], axis=1)


def scores_of(query_rows, key_rows, allowed):
    row_count = query_rows.shape[0]
    heads_q = query_rows.reshape(row_count, HEADS, HEAD)
    heads_k = key_rows.reshape(key_rows.shape[0], HEADS, HEAD)
    raw_scores = jnp.einsum(
        "rhe,che->hrc", heads_q, heads_k, preferred_element_type=jnp.float32
    ) * HEAD ** (-0.5)
    return jnp.where(allowed[None], raw_scores, masked_value)


def attend_forward(query_rows, key_rows, value_rows, allowed):
    row_count = query_rows.shape[0]
    scores = scores_of(query_rows, key_rows, allowed)
    row_top = jnp.max(scores, axis=-1, keepdims=True)
    expo = jnp.exp(scores - row_top)
    row_total = jnp.sum(expo, axis=-1, keepdims=True)
    probs_low = (expo / row_total).astype(jnp.bfloat16)
    heads_v = value_rows.reshape(value_rows.shape[0], HEADS, HEAD)
    attended_rows = jnp.einsum(
        "hrc,che->rhe", probs_low, heads_v, preferred_element_type=jnp.float32
    )
    return (attended_rows.reshape(row_count, HEADS * HEAD), row_top + jnp.log(row_total))


def attend_backward(query_rows, key_rows, value_rows, allowed, log_total, grad_rows):
    row_count = query_rows.shape[0]
    scores = scores_of(query_rows, key_rows, allowed)
    probs = jnp.exp(scores - log_total)
    heads_q = query_rows.reshape(row_count, HEADS, HEAD)
    heads_k = key_rows.reshape(key_rows.shape[0], HEADS, HEAD)
    heads_v = value_rows.reshape(value_rows.shape[0], HEADS, HEAD)
    heads_g = grad_rows.reshape(row_count, HEADS, HEAD)
    grad_probs = jnp.einsum("rhe,che->hrc", heads_g, heads_v, preferred_element_type=jnp.float32)
    center = jnp.sum(probs * grad_probs, axis=-1, keepdims=True)
    grad_scores = (probs * (grad_probs - center)).astype(jnp.bfloat16)
    grad_query = jnp.einsum(
        "hrc,che->rhe", grad_scores, heads_k, preferred_element_type=jnp.float32
    ) * HEAD ** (-0.5)
    grad_keys = jnp.einsum(
        "hrc,rhe->che", grad_scores, heads_q, preferred_element_type=jnp.float32
    ) * HEAD ** (-0.5)
    grad_values = jnp.einsum(
        "hrc,rhe->che", probs.astype(jnp.bfloat16), heads_g, preferred_element_type=jnp.float32
    )
    col_count = key_rows.shape[0]
    return (
        grad_query.reshape(row_count, HEADS * HEAD),
        grad_keys.reshape(col_count, HEADS * HEAD),
        grad_values.reshape(col_count, HEADS * HEAD),
    )


def on_device(
    hidden_in,
    image_count,
    text_lengths,
    attend_gain,
    attend_shift,
    project_in,
    bias_pair,
    project_out,
    project_bias,
    feed_gain,
    feed_shift,
    expand_weight,
    expand_bias,
    reduce_weight,
    reduce_bias,
    cotangent,
):
    item_total = hidden_in.shape[0]
    row_count = hidden_in.shape[2]
    features = hidden_in.shape[3]
    is_text = lax.axis_index("mod") == 1
    inputs = hidden_in[:, 0].astype(jnp.float32)
    normed, attend_pull = jax.vjp(layer_norm, inputs, attend_gain[0], attend_shift[0])
    normed_low = normed.astype(jnp.bfloat16)
    projected = jnp.dot(
        normed_low.reshape(-1, features), project_in, preferred_element_type=jnp.float32
    ).reshape(item_total, row_count, 3 * features)
    query_rows = (projected[..., :features] + bias_pair[0]).astype(jnp.bfloat16)
    key_rows = projected[..., features : 2 * features].astype(jnp.bfloat16)
    value_rows = (projected[..., 2 * features :] + bias_pair[1]).astype(jnp.bfloat16)
    far_keys, far_values = from_behind((key_rows[:, :IMG_PAD], value_rows[:, :IMG_PAD]), "mod", 1)
    masks = []
    joined_keys = []
    joined_values = []
    attended_list = []
    log_totals = []
    for item_index in range(item_total):
        allowed = allowed_mask(
            image_count[item_index], text_lengths[item_index], is_text, row_count
        )
        both_keys = jnp.concatenate([far_keys[item_index], key_rows[item_index]], axis=0)
        both_values = jnp.concatenate([far_values[item_index], value_rows[item_index]], axis=0)
        attended_rows, log_total = attend_forward(
            query_rows[item_index], both_keys, both_values, allowed
        )
        masks.append(allowed)
        joined_keys.append(both_keys)
        joined_values.append(both_values)
        attended_list.append(attended_rows)
        log_totals.append(log_total)
    attended = jnp.stack(attended_list).astype(jnp.bfloat16).reshape(-1, features)
    branch = jnp.dot(attended, project_out, preferred_element_type=jnp.float32).reshape(
        item_total, row_count, features
    )
    middle = inputs + branch + project_bias
    normed_feed, feed_pull = jax.vjp(layer_norm, middle, feed_gain[0], feed_shift[0])
    feed_low = normed_feed.astype(jnp.bfloat16).reshape(-1, features)
    upward = (
        jnp.dot(feed_low, expand_weight[0], preferred_element_type=jnp.float32) + expand_bias[0]
    )
    active_float, gelu_pull = jax.vjp(exact_gelu, upward)
    active = active_float.astype(jnp.bfloat16)
    result = (
        middle.reshape(-1, features)
        + jnp.dot(active, reduce_weight[0], preferred_element_type=jnp.float32)
        + reduce_bias[0]
    )
    hidden_out = result.astype(jnp.bfloat16).reshape(item_total, 1, row_count, features)
    row_live = (jnp.arange(row_count, dtype=jnp.int32)[None, :] < image_count[:, None]) | is_text
    grad_out = jnp.where(row_live[..., None], cotangent[:, 0], jnp.zeros((), jnp.bfloat16)).reshape(
        -1, features
    )
    grad_top = grad_out.astype(jnp.float32)
    reduce_weight_grad = outer_sum(active, grad_out)
    reduce_bias_grad = jnp.sum(grad_top, axis=0)
    grad_active = back_dot(grad_out, reduce_weight[0])
    grad_up = gelu_pull(grad_active)[0].astype(jnp.bfloat16)
    expand_weight_grad = outer_sum(feed_low, grad_up)
    expand_bias_grad = jnp.sum(grad_up.astype(jnp.float32), axis=0)
    grad_feed = back_dot(grad_up, expand_weight[0]).reshape(item_total, row_count, features)
    grad_mid_part, feed_gain_grad, feed_shift_grad = feed_pull(grad_feed)
    grad_middle = grad_top.reshape(item_total, row_count, features) + grad_mid_part
    project_bias_grad = jnp.sum(grad_middle, axis=(0, 1))
    grad_branch = grad_middle.reshape(-1, features).astype(jnp.bfloat16)
    project_out_grad = outer_sum(attended, grad_branch)
    grad_attended = (
        back_dot(grad_branch, project_out)
        .astype(jnp.bfloat16)
        .reshape(item_total, row_count, features)
    )
    query_grads = []
    far_key_grads = []
    far_value_grads = []
    own_key_grads = []
    own_value_grads = []
    for item_index in range(item_total):
        grad_query, grad_keys, grad_values = attend_backward(
            query_rows[item_index],
            joined_keys[item_index],
            joined_values[item_index],
            masks[item_index],
            log_totals[item_index],
            grad_attended[item_index],
        )
        query_grads.append(grad_query)
        far_key_grads.append(grad_keys[:IMG_PAD])
        far_value_grads.append(grad_values[:IMG_PAD])
        own_key_grads.append(grad_keys[IMG_PAD:])
        own_value_grads.append(grad_values[IMG_PAD:])
    back_keys, back_values = from_behind(
        (jnp.stack(far_key_grads), jnp.stack(far_value_grads)), "mod", -1
    )
    padding = jnp.zeros((item_total, row_count - IMG_PAD, features), jnp.float32)
    own_keys_total = jnp.stack(own_key_grads) + jnp.concatenate([back_keys, padding], axis=1)
    own_values_total = jnp.stack(own_value_grads) + jnp.concatenate([back_values, padding], axis=1)
    grad_projected = (
        jnp.concatenate([jnp.stack(query_grads), own_keys_total, own_values_total], axis=-1)
        .astype(jnp.bfloat16)
        .reshape(-1, 3 * features)
    )
    project_in_grad = outer_sum(normed_low.reshape(-1, features), grad_projected)
    column_sums = jnp.sum(grad_projected.astype(jnp.float32), axis=0)
    bias_pair_grad = jnp.stack([column_sums[:features], column_sums[2 * features :]])
    grad_normed = back_dot(grad_projected, project_in).reshape(item_total, row_count, features)
    grad_in_part, attend_gain_grad, attend_shift_grad = attend_pull(grad_normed)
    grad_in = (
        (grad_middle + grad_in_part)
        .astype(jnp.bfloat16)
        .reshape(item_total, 1, row_count, features)
    )
    project_in_grad, bias_pair_grad, project_out_grad, project_bias_grad = lax.psum(
        (project_in_grad, bias_pair_grad, project_out_grad, project_bias_grad), ("dp", "mod")
    )
    (
        attend_gain_grad,
        attend_shift_grad,
        feed_gain_grad,
        feed_shift_grad,
        expand_weight_grad,
        expand_bias_grad,
        reduce_weight_grad,
        reduce_bias_grad,
    ) = lax.psum(
        (
            attend_gain_grad,
            attend_shift_grad,
            feed_gain_grad,
            feed_shift_grad,
            expand_weight_grad,
            expand_bias_grad,
            reduce_weight_grad,
            reduce_bias_grad,
        ),
        "dp",
    )
    return (
        hidden_out,
        grad_in,
        attend_gain_grad[None],
        attend_shift_grad[None],
        project_in_grad,
        bias_pair_grad,
        project_out_grad,
        project_bias_grad,
        feed_gain_grad[None],
        feed_shift_grad[None],
        expand_weight_grad[None],
        expand_bias_grad[None],
        reduce_weight_grad[None],
        reduce_bias_grad[None],
    )


def solution(mesh):
    in_specs = (
        P("dp", "mod", None, None),
        P("dp"),
        P("dp", None),
        P("mod", None),
        P("mod", None),
        P(),
        P(),
        P(),
        P(),
        P("mod", None),
        P("mod", None),
        P("mod", None, None),
        P("mod", None),
        P("mod", None, None),
        P("mod", None),
        P("dp", "mod", None, None),
    )
    out_specs = (
        P("dp", "mod", None, None),
        P("dp", "mod", None, None),
        P("mod", None),
        P("mod", None),
        P(),
        P(),
        P(),
        P(),
        P("mod", None),
        P("mod", None),
        P("mod", None, None),
        P("mod", None),
        P("mod", None, None),
        P("mod", None),
    )
    return jax.shard_map(
        on_device, mesh=mesh, in_specs=in_specs, out_specs=out_specs, check_vma=False
    )
```

profile of v0, /device:TPU:0, one launch (start us, length us, event | category | flops | bytes accessed | tf_op | source)
XLA Modules:
  0.0 938.0 jit_solution(7490095084007055644)
XLA Ops:
  13.5 4.2 fusion.93
  18.6 5.8 collective-permute-start.1
  26.0 2.7 collective-permute-start
  55.8 3.6 convert_reduce_fusion.3
  67.3 5.1 fusion.94
  72.4 3.9 fusion.1
  76.3 2.7 copy-done.1
  79.6 9.8 %fusion.58 = bf16[12,64,512]{2,1,0:T(8,128)(2,1)} fusion(f32[12,512,768]{2,1,0:T(8,128)} %copy-done.1, f32[12,512]{1,0:T(8,128)S(1)} %fusion.1, f32[12,512]{1,0:T(8,128)S(1)} %get-tuple-element.107, bf16[512,12,64]{0,2,1:T(8,128)(2,1)S(1)} %bitcast.237, bf16[256,12,64]{0,2,1:T(8,128)(2,1)S(1)} %bitcast.241), kind=kOutput, calls=%fused_computation.110 | convolution fusion | flops 620888064 | bytes 20889600 | tf_op jit(solution)/shard_map/hrc,che->rhe/dot_general | solution.py:80
  95.6 5.1 fusion.95
  100.7 3.7 fusion
  104.4 2.9 copy-done.2
  108.0 9.8 %fusion.59 = bf16[12,64,512]{2,1,0:T(8,128)(2,1)} fusion(f32[12,512,768]{2,1,0:T(8,128)} %copy-done.2, f32[12,512]{1,0:T(8,128)S(1)} %fusion, f32[12,512]{1,0:T(8,128)S(1)} %get-tuple-element.109, bf16[512,12,64]{0,2,1:T(8,128)(2,1)S(1)} %bitcast.239, bf16[256,12,64]{0,2,1:T(8,128)(2,1)S(1)} %bitcast.243), kind=kOutput, calls=%fused_computation.111 | convolution fusion | flops 620888064 | bytes 20889600 | tf_op jit(solution)/shard_map/hrc,che->rhe/dot_general | solution.py:80
  120.1 3.8 fusion.96
  126.1 36.4 %multiply_convert_fusion.2 = (bf16[1024,3072]{1,0:T(8,128)(2,1)}, f32[1024,3072]{1,0:T(8,128)}, f32[1024,3072]{1,0:T(8,128)}) fusion(f32[3072]{0:T(1024)S(1)} %bitcast.254, bf16[1024,768]{1,0:T(8,128)(2,1)S(1)} %bitcast.245, bf16[1,768,3072]{2,1,0:T(8,128)(2,1)} %param.27), kind=kOutput, calls=%fused_computation.20 | convolution fusion | flops 5039456256 | bytes 37761024 | tf_op jit(solution)/shard_map/dot_general | solution.py:173
  162.5 18.9 %convert_reduce_fusion = (f32[3072]{0:T(1024)}, bf16[1024,3072]{1,0:T(8,128)(2,1)}) fusion(f32[1024,3072]{1,0:T(8,128)} %get-tuple-element.82, bf16[1024,768]{1,0:T(8,128)(2,1)} %bitcast.248, bf16[1,3072,768]{2,1,0:T(8,128)(2,1)} %param.29, f32[1024,3072]{1,0:T(8,128)} %get-tuple-element.113, f32[3072]{0:T(1024)S(1)} %bitcast.255), kind=kOutput, calls=%fused_computation.18 | convolution fusion | flops 4885312512 | bytes 37773312 | tf_op jit(solution)/shard_map/dot_general | solution.py:39
  181.5 11.1 %multiply_reduce_fusion.2 = (f32[768]{0:T(1024)}, f32[2,512]{1,0:T(2,128)S(1)}, f32[768]{0:T(1024)}, f32[2,512,768]{2,1,0:T(8,128)}) fusion(f32[2,512,768]{2,1,0:T(8,128)S(1)} %copy-done.6, f32[2,512]{1,0:T(2,128)S(1)} %copy-done.48, f32[2,512]{1,0:T(2,128)S(1)} %copy-done.42, f32[768]{0:T(1024)S(1)} %copy-done.53, bf16[2,512,3072]{2,1,0:T(8,128)(2,1)} %bitcast.256, ...), kind=kOutput, calls=%fused_computation.87 | convolution fusion | flops 4838126592 | bytes 17323008 | tf_op jit(solution)/shard_map/dot_general | solution.py:39
  192.7 2.8 fusion.83
  199.9 4.6 fusion.54
  206.8 8.1 fusion.51
  217.2 16.1 %multiply_reduce_fusion = (f32[12,512]{1,0:T(8,128)S(1)}, f32[12,512,768]{2,1,0:T(8,128)}) fusion(f32[12,512,768]{2,1,0:T(8,128)} %copy-done.1, f32[12,512]{1,0:T(8,128)S(1)} %copy-done.37, bf16[512,12,64]{0,2,1:T(8,128)(2,1)S(1)} %bitcast.215, bf16[512,12,64]{0,2,1:T(8,128)(2,1)S(1)} %bitcast.238, bf16[256,12,64]{0,2,1:T(8,128)(2,1)S(1)} %bitcast.242), kind=kOutput, calls=%fused_computation.2 | convolution fusion | flops 620488704 | bytes 39763968 | tf_op jit(solution)/shard_map/rhe,che->hrc/dot_general | solution.py:94
  233.3 16.0 %multiply_reduce_fusion.1 = (f32[12,512]{1,0:T(8,128)S(1)}, f32[12,512,768]{2,1,0:T(8,128)}) fusion(f32[12,512,768]{2,1,0:T(8,128)} %copy-done.2, f32[12,512]{1,0:T(8,128)S(1)} %copy-done.38, bf16[512,12,64]{0,2,1:T(8,128)(2,1)S(1)} %bitcast.213, bf16[512,12,64]{0,2,1:T(8,128)(2,1)S(1)} %bitcast.240, bf16[256,12,64]{0,2,1:T(8,128)(2,1)S(1)} %bitcast.244), kind=kOutput, calls=%fused_computation.5 | convolution fusion | flops 620488704 | bytes 39763968 | tf_op jit(solution)/shard_map/rhe,che->hrc/dot_general | solution.py:94
  249.3 14.2 %multiply_convert_fusion = bf16[12,512,768]{2,1,0:T(8,128)(2,1)S(1)} fusion(f32[12,512,768]{2,1,0:T(8,128)} %get-tuple-element.116, f32[12,512,768]{2,1,0:T(8,128)} %copy-done.1, f32[12,512]{1,0:T(8,128)S(1)} %get-tuple-element.115, f32[12,512]{1,0:T(8,128)S(1)} %copy-done.37), kind=kLoop, calls=%fused_computation.1 | loop fusion | flops 18874368 | bytes 47235072 | tf_op jit(solution)/shard_map/convert_element_type | solution.py:96
  263.5 6.6 multiply_bitcast_fusion
  272.5 9.0 multiply_convert_fusion.1
  281.6 3.4 multiply_bitcast_fusion.1
  287.7 3.0 copy.106
  290.7 3.0 copy.105
  298.3 2.6 pad_maximum_fusion.5
  302.2 3.1 copy.102
  305.3 3.1 copy.101
  312.9 2.7 pad_maximum_fusion.4
  317.0 7.5 convolution_multiply_fusion
  326.7 7.9 convolution_multiply_fusion.1
  338.5 5.4 convolution_bitcast_fusion.3
  345.8 26.9 %collective-permute-done.2 = f32[2,256,768]{2,1,0:T(8,128)} collective-permute-done((f32[2,256,768]{2,1,0:T(8,128)}, f32[2,256,768]{2,1,0:T(8,128)}, u32[]{:S(2)}, u32[]{:S(2)}) %collective-permute-start.2) | collective-permute-done | bytes 1572896 | tf_op jit(solution)/shard_map/ppermute | solution.py:18
  375.6 7.2 convolution_bitcast_fusion.2
  385.6 10.3 %convolution_bitcast_fusion.1 = f32[1,768,3072]{2,1,0:T(8,128)} fusion(bf16[1024,768]{1,0:T(8,128)(2,1)S(1)} %bitcast.246, bf16[1024,3072]{1,0:T(8,128)(2,1)} %get-tuple-element.121), kind=kOutput, calls=%fused_computation.42 | convolution fusion | flops 4831838208 | bytes 17301504 | tf_op jit(solution)/shard_map/dot_general | solution.py:33
  395.9 10.3 %convolution_bitcast_fusion = f32[1,3072,768]{2,1,0:T(8,128)} fusion(bf16[1024,3072]{1,0:T(8,128)(2,1)} %get-tuple-element.81, bf16[1024,768]{1,0:T(8,128)(2,1)S(1)} %bitcast_select_fusion), kind=kOutput, calls=%fused_computation.41 | convolution fusion | flops 4831838208 | bytes 17301504 | tf_op jit(solution)/shard_map/dot_general | solution.py:33
  411.3 10.2 %fusion.48 = bf16[1024,768]{1,0:T(8,128)(2,1)} fusion(f32[2,512,768]{2,1,0:T(8,128)} %copy-done.5, bf16[1024,3072]{1,0:T(8,128)(2,1)} %get-tuple-element.81, bf16[1,3072,768]{2,1,0:T(8,128)(2,1)} %param.29, f32[768]{0:T(1024)} %reduce.8), kind=kOutput, calls=%fused_computation.85 | convolution fusion | flops 4834197504 | bytes 15731712 | tf_op jit(solution)/shard_map/dot_general | solution.py:179
  421.5 4.1 fusion.82
  431.0 60.7 %all-reduce.4 = (f32[1,768]{1,0:T(1,128)}, f32[1,768]{1,0:T(1,128)}, f32[1,768]{1,0:T(1,128)}, f32[1,768]{1,0:T(1,128)}, f32[1,3072]{1,0:T(1,128)}, /*index=5*/f32[1,768]{1,0:T(1,128)}) all-reduce(f32[1,768]{1,0:T(1,128)} %broadcast_in_dim.148, f32[1,768]{1,0:T(1,128)} %broadcast_in_dim.149, ...), channel_id=1, replica_groups=mesh['dp'=16,'mod'=2] {'dp'}, use_global_device_ids=true, to_apply=%region_19.20 | all-reduce | flops 6912 | bytes 55296 | tf_op jit(solution)/shard_map/psum | solution.py:257
  493.0 38.0 %all-reduce.2 = (f32[2,768]{1,0:T(2,128)}, f32[768]{0:T(1024)}) all-reduce(f32[2,768]{1,0:T(2,128)} %pad_maximum_fusion.20, f32[768]{0:T(1024)} %get-tuple-element.85), channel_id=1, replica_groups=mesh['dp'=16,'mod'=2] {'dp','mod'}, use_global_device_ids=true, to_apply=%region_24.25 | all-reduce | flops 2304 | bytes 18432 | tf_op jit(solution)/shard_map/psum | solution.py:245
  531.7 5.6 fusion.57
  537.3 37.4 %all-reduce.9.cloned.1.call-done = (f32[768,2304]{1,0:T(8,128)}, f32[768,768]{1,0:T(8,128)}) async-done(((f32[768,2304]{1,0:T(8,128)}, f32[768,768]{1,0:T(8,128)}), (f32[768,2304]{1,0:T(8,128)}, f32[768,768]{1,0:T(8,128)})) %all-reduce.9.cloned.1.call-update) | async-done | bytes 9437200 | tf_op jit(solution)/shard_map/psum | solution.py:245
  574.7 335.2 %all-reduce.11.cloned.1.call-done = (f32[1,768,3072]{2,1,0:T(8,128)}, f32[1,3072,768]{2,1,0:T(8,128)}) async-done(((f32[1,768,3072]{2,1,0:T(8,128)}, f32[1,3072,768]{2,1,0:T(8,128)}), (f32[1,768,3072]{2,1,0:T(8,128)}, f32[1,3072,768]{2,1,0:T(8,128)})) %all-reduce.11.cloned.1.call-update) | async-done | bytes 18874384 | tf_op jit(solution)/shard_map/psum | solution.py:257
  909.8 6.6 copy.119
  917.8 9.3 copy.121
  927.2 3.7 copy.122
  (262 shorter events, 108.9 us)
Async XLA Ops:
  7.2 567.5 %all-reduce.9.cloned.1.call-start = ((), (), s32[]{:S(2)}) async-start(), calls=%async_computation | async-start | bytes 18874368 | tf_op jit(solution)/shard_map/psum | solution.py:245
  8.1 9.5 %copy-start.61 = (f32[768]{0:T(1024)}, f32[768]{0:T(1024)S(1)}, u32[]{:S(2)}) copy-start(f32[768]{0:T(1024)S(1)} %reduce.3) | copy-start | bytes 9220
  9.0 8.7 copy-start.49
  13.5 11.0 %copy-start.59 = (f32[2,768]{1,0:T(2,128)S(1)}, f32[2,768]{1,0:T(2,128)}, u32[]{:S(2)}) copy-start(f32[2,768]{1,0:T(2,128)} %param.22) | copy-start | bytes 18436
  18.6 40.7 %collective-permute-start.1 = (bf16[2,256,768]{2,1,0:T(8,128)(2,1)}, bf16[2,256,768]{2,1,0:T(8,128)(2,1)}, u32[]{:S(2)}, u32[]{:S(2)}) collective-permute-start(bf16[2,256,768]{2,1,0:T(8,128)(2,1)} %slice.151), channel_id=1, source_target_pairs={{0,1},{2,3},{4,5},{6,7},{8,9},{10,11},{12,13},{14,15},{16,17},{18,... | collective-permute-start | bytes 2359304 | tf_op jit(solution)/shard_map/ppermute | solution.py:18
  26.0 37.3 %collective-permute-start = (bf16[2,256,768]{2,1,0:T(8,128)(2,1)}, bf16[2,256,768]{2,1,0:T(8,128)(2,1)}, u32[]{:S(2)}, u32[]{:S(2)}) collective-permute-start(bf16[2,256,768]{2,1,0:T(8,128)(2,1)} %slice.146), channel_id=1, source_target_pairs={{0,1},{2,3},{4,5},{6,7},{8,9},{10,11},{12,13},{14,15},{16,17},{18,... | collective-permute-start | bytes 2359304 | tf_op jit(solution)/shard_map/ppermute | solution.py:18
  45.8 9.3 copy-start.63
  45.8 9.3 copy-start.64
  55.1 70.3 %copy-start.52 = (f32[768]{0:T(1024)}, f32[768]{0:T(1024)S(1)}, u32[]{:S(2)}) copy-start(f32[768]{0:T(1024)S(1)} %reduce.6) | copy-start | bytes 9220
  100.7 7.3 copy-start.27
  100.7 7.3 copy-start.32
  108.0 12.1 %copy-start.68 = (f32[768]{0:T(1024)S(1)}, f32[768]{0:T(1024)}, u32[]{:S(2)}) copy-start(f32[768]{0:T(1024)} %param.24) | copy-start | bytes 9220
  125.4 37.1 %copy-start.47 = (f32[2,512]{1,0:T(2,128)}, f32[2,512]{1,0:T(2,128)S(1)}, u32[]{:S(2)}) copy-start(f32[2,512]{1,0:T(2,128)S(1)} %fusion.69) | copy-start | bytes 12292
  126.0 36.5 %copy-start.34 = (bf16[2,512,768]{2,1,0:T(8,128)(2,1)}, bf16[2,512,768]{2,1,0:T(8,128)(2,1)S(1)}, u32[]{:S(2)}) copy-start(bf16[2,512,768]{2,1,0:T(8,128)(2,1)S(1)} %add_convert_fusion.2) | copy-start | bytes 4718596
  162.5 19.0 %copy-start.6 = (f32[2,512,768]{2,1,0:T(8,128)S(1)}, f32[2,512,768]{2,1,0:T(8,128)}, u32[]{:S(2)}) copy-start(f32[2,512,768]{2,1,0:T(8,128)} %copy-done.5) | copy-start | bytes 9437188
  162.5 18.9 %copy-start.42 = (f32[2,512]{1,0:T(2,128)S(1)}, f32[2,512]{1,0:T(2,128)}, u32[]{:S(2)}) copy-start(f32[2,512]{1,0:T(2,128)} %copy-done.41) | copy-start | bytes 12292
  162.5 18.9 %copy-start.48 = (f32[2,512]{1,0:T(2,128)S(1)}, f32[2,512]{1,0:T(2,128)}, u32[]{:S(2)}) copy-start(f32[2,512]{1,0:T(2,128)} %copy-done.47) | copy-start | bytes 12292
  162.5 18.9 %copy-start.53 = (f32[768]{0:T(1024)S(1)}, f32[768]{0:T(1024)}, u32[]{:S(2)}) copy-start(f32[768]{0:T(1024)} %copy-done.52) | copy-start | bytes 9220
  181.4 11.2 %copy-start.57 = (f32[2,512]{1,0:T(2,128)S(1)}, f32[2,512]{1,0:T(2,128)}, u32[]{:S(2)}) copy-start(f32[2,512]{1,0:T(2,128)} %copy-done.56) | copy-start | bytes 12292
  181.5 17.8 %slice-start = ((s8[18874368]{0:T(1024)(128)(4,1)}), s8[4194304]{0:T(1024)(128)(4,1)S(1)}, s32[]{:S(2)}) async-start(s8[18874368]{0:T(1024)(128)(4,1)} %bitcast.202), calls=%async_computation.2 | async-start | bytes 8388608
  181.5 17.8 %slice-start.1 = ((s8[18874368]{0:T(1024)(128)(4,1)}), s8[4194304]{0:T(1024)(128)(4,1)S(1)}, s32[]{:S(2)}) async-start(s8[18874368]{0:T(1024)(128)(4,1)} %bitcast.202), calls=%async_computation.3 | async-start | bytes 8388608
  181.5 17.8 %slice-start.2 = ((s8[18874368]{0:T(1024)(128)(4,1)}), s8[4194304]{0:T(1024)(128)(4,1)S(1)}, s32[]{:S(2)}) async-start(s8[18874368]{0:T(1024)(128)(4,1)} %bitcast.202), calls=%async_computation.4 | async-start | bytes 8388608
  217.2 16.1 %copy-start.28 = (bf16[1,512,768]{1,2,0:T(8,128)(2,1)S(1)}, bf16[1,512,768]{1,2,0:T(8,128)(2,1)}, u32[]{:S(2)}) copy-start(bf16[1,512,768]{1,2,0:T(8,128)(2,1)} %copy.88) | copy-start | bytes 2359300
  217.2 16.1 %copy-start.33 = (bf16[1,256,768]{1,2,0:T(8,128)(2,1)S(1)}, bf16[1,256,768]{1,2,0:T(8,128)(2,1)}, u32[]{:S(2)}) copy-start(bf16[1,256,768]{1,2,0:T(8,128)(2,1)} %copy.87) | copy-start | bytes 1179652
  249.3 23.2 %slice-start.5 = ((s8[18874368]{0:T(1024)(128)(4,1)}), s8[4194304]{0:T(1024)(128)(4,1)S(1)}, s32[]{:S(2)}) async-start(s8[18874368]{0:T(1024)(128)(4,1)} %bitcast.204), calls=%async_computation.7 | async-start | bytes 8388608
  249.3 23.2 %slice-start.6 = ((s8[18874368]{0:T(1024)(128)(4,1)}), s8[4194304]{0:T(1024)(128)(4,1)S(1)}, s32[]{:S(2)}) async-start(s8[18874368]{0:T(1024)(128)(4,1)} %bitcast.204), calls=%async_computation.8 | async-start | bytes 8388608
  249.3 23.2 %slice-start.7 = ((s8[18874368]{0:T(1024)(128)(4,1)}), s8[4194304]{0:T(1024)(128)(4,1)S(1)}, s32[]{:S(2)}) async-start(s8[18874368]{0:T(1024)(128)(4,1)} %bitcast.204), calls=%async_computation.9 | async-start | bytes 8388608
  249.3 23.2 %slice-start.8 = ((s8[18874368]{0:T(1024)(128)(4,1)}), s8[4194304]{0:T(1024)(128)(4,1)S(1)}, s32[]{:S(2)}) async-start(s8[18874368]{0:T(1024)(128)(4,1)} %bitcast.204), calls=%async_computation.10 | async-start | bytes 8388608
  263.5 9.0 slice-start.9
  300.9 42.9 %collective-permute-start.3 = (f32[2,256,768]{2,1,0:T(8,128)}, f32[2,256,768]{2,1,0:T(8,128)}, u32[]{:S(2)}, u32[]{:S(2)}) collective-permute-start(f32[2,256,768]{2,1,0:T(8,128)} %pad_maximum_fusion.5), channel_id=1, source_target_pairs={{1,0},{3,2},{5,4},{7,6},{9,8},{11,10},{13,12},{15,14},{17,16},{19,... | collective-permute-start | bytes 4718600 | tf_op jit(solution)/shard_map/ppermute | solution.py:18
  315.7 57.0 %collective-permute-start.2 = (f32[2,256,768]{2,1,0:T(8,128)}, f32[2,256,768]{2,1,0:T(8,128)}, u32[]{:S(2)}, u32[]{:S(2)}) collective-permute-start(f32[2,256,768]{2,1,0:T(8,128)} %pad_maximum_fusion.4), channel_id=1, source_target_pairs={{1,0},{3,2},{5,4},{7,6},{9,8},{11,10},{13,12},{15,14},{17,16},{19,... | collective-permute-start | bytes 4718600 | tf_op jit(solution)/shard_map/ppermute | solution.py:18
  338.4 36.0 %copy-start.14 = (bf16[2,512,768]{2,1,0:T(8,128)(2,1)}, bf16[2,512,768]{2,1,0:T(8,128)(2,1)S(1)}, u32[]{:S(2)}) copy-start(bf16[2,512,768]{2,1,0:T(8,128)(2,1)S(1)} %maximum_convert_fusion) | copy-start | bytes 4718596
  343.8 28.9 %copy-start.18 = (f32[1,512,768]{2,1,0:T(8,128)S(1)}, f32[1,512,768]{2,1,0:T(8,128)}, u32[]{:S(2)}) copy-start(f32[1,512,768]{2,1,0:T(8,128)} %copy.102) | copy-start | bytes 4718596
  343.8 28.9 %copy-start.19 = (f32[1,512,768]{2,1,0:T(8,128)S(1)}, f32[1,512,768]{2,1,0:T(8,128)}, u32[]{:S(2)}) copy-start(f32[1,512,768]{2,1,0:T(8,128)} %copy.101) | copy-start | bytes 4718596
  345.7 28.7 %copy-start.20 = (bf16[2,512,768]{2,1,0:T(8,128)(2,1)}, bf16[2,512,768]{2,1,0:T(8,128)(2,1)S(1)}, u32[]{:S(2)}) copy-start(bf16[2,512,768]{2,1,0:T(8,128)(2,1)S(1)} %fusion.46) | copy-start | bytes 4718596
  345.7 29.9 %copy-start.9 = (bf16[2,1,512,768]{3,2,1,0:T(8,128)(2,1)S(1)}, bf16[2,1,512,768]{3,2,1,0:T(8,128)(2,1)}, u32[]{:S(2)}) copy-start(bf16[2,1,512,768]{3,2,1,0:T(8,128)(2,1)} %param.16) | copy-start | bytes 4718596
  345.7 29.9 %copy-start.40 = (f32[2,512]{1,0:T(2,128)S(1)}, f32[2,512]{1,0:T(2,128)}, u32[]{:S(2)}) copy-start(f32[2,512]{1,0:T(2,128)} %copy-done.39) | copy-start | bytes 12292
  345.7 29.9 %copy-start.46 = (f32[2,512]{1,0:T(2,128)S(1)}, f32[2,512]{1,0:T(2,128)}, u32[]{:S(2)}) copy-start(f32[2,512]{1,0:T(2,128)} %copy-done.45) | copy-start | bytes 12292
  345.7 29.8 %copy-start.50 = (f32[768]{0:T(1024)S(1)}, f32[768]{0:T(1024)}, u32[]{:S(2)}) copy-start(f32[768]{0:T(1024)} %copy-done.49) | copy-start | bytes 9220
  345.8 29.8 %copy-start.62 = (f32[768]{0:T(1024)S(1)}, f32[768]{0:T(1024)}, u32[]{:S(2)}) copy-start(f32[768]{0:T(1024)} %copy-done.61) | copy-start | bytes 9220
  382.8 527.0 %all-reduce.11.cloned.1.call-start = ((), (), s32[]{:S(2)}) async-start(), calls=%async_computation.1 | async-start | bytes 37748736 | tf_op jit(solution)/shard_map/psum | solution.py:257
  411.3 10.2 %copy-start.10 = (bf16[2,1,512,768]{3,2,1,0:T(8,128)(2,1)S(1)}, bf16[2,1,512,768]{3,2,1,0:T(8,128)(2,1)}, u32[]{:S(2)}) copy-start(bf16[2,1,512,768]{3,2,1,0:T(8,128)(2,1)} %param.16) | copy-start | bytes 4718596
  411.3 10.2 %copy-start.15 = (bf16[2,512,768]{2,1,0:T(8,128)(2,1)S(1)}, bf16[2,512,768]{2,1,0:T(8,128)(2,1)}, u32[]{:S(2)}) copy-start(bf16[2,512,768]{2,1,0:T(8,128)(2,1)} %copy-done.14) | copy-start | bytes 4718596
  411.3 10.2 %copy-start.21 = (bf16[2,512,768]{2,1,0:T(8,128)(2,1)S(1)}, bf16[2,512,768]{2,1,0:T(8,128)(2,1)}, u32[]{:S(2)}) copy-start(bf16[2,512,768]{2,1,0:T(8,128)(2,1)} %copy-done.20) | copy-start | bytes 4718596
  411.3 10.2 %copy-start.23 = (bf16[2,512,768]{2,1,0:T(8,128)(2,1)S(1)}, bf16[2,512,768]{2,1,0:T(8,128)(2,1)}, u32[]{:S(2)}) copy-start(bf16[2,512,768]{2,1,0:T(8,128)(2,1)} %copy-done.22) | copy-start | bytes 4718596
  916.4 10.7 %slice-start.10 = ((s8[9437184]{0:T(1024)(128)(4,1)}), s8[4194304]{0:T(1024)(128)(4,1)S(1)}, s32[]{:S(2)}) async-start(s8[9437184]{0:T(1024)(128)(4,1)} %bitcast.210), calls=%async_computation.12 | async-start | bytes 8388608
  917.8 9.3 slice-start.11
  917.8 9.3 slice-start.12
  (40 other events, 143.4 us)
Sparse Core Ops, SparseCore 0:
  382.9 191.7 all-reduce.8
  579.9 329.8 all-reduce.10
where the time goes:
time: 944 us; the launch traced here: 938 us
  waiting for transfers between devices  399 us (42%)
  matrix products  223 us (24%)
  local copies, waits for them, and re-layouts  111 us (12%)
  blocking collectives  98.7 us (10%)
  other arithmetic  79.6 us (8%)
  between operations  15.4 us (2%)
  starting transfers between devices  11.3 us (1%)
    psum x1, waiting for transfers between devices, on_device(): lax.psum((attend_gain_grad, attend_shift_grad, feed_gain_grad, feed_shift...  335 us
    psum x1, blocking collectives, on_device(): lax.psum((attend_gain_grad, attend_shift_grad, feed_gain_grad, feed_shift...  60.7 us
    psum x1, blocking collectives, on_device(): lax.psum((project_in_grad, bias_pair_grad, project_out_grad, project_bias...  38 us
    psum x1, waiting for transfers between devices, on_device(): lax.psum((project_in_grad, bias_pair_grad, project_out_grad, project_bias...  37.4 us
    dot_general x1, matrix products, on_device(): jnp.dot(feed_low, expand_weight[0], preferred_element_type=jnp.float32)  36.4 us
    dot_general x4, matrix products, back_dot(): lax.dot_general(grad_rows, weight, (((1,), (1,)), ((), ())), preferred_el...  35.5 us
    dot_general x4, matrix products, outer_sum(): lax.dot_general(left, right, (((0,), (0,)), ((), ())), preferred_element_...  33.2 us
    unnamed x168, local copies, waits for them, and re-layouts  32.3 us
  transfers between devices with their start and end apart: 6, of which 3 were waited for; matrix products, arithmetic and copies ran while one was open for 14% of the time, Pallas kernels for 0%

commit v1 on v0

v1 whole, which is shorter than its diff:
```python
import functools

import jax
import jax.numpy as jnp
from jax import lax
from jax.experimental import pallas as pl
from jax.experimental.pallas import tpu as pltpu
from jax.sharding import PartitionSpec as P

HEADS = 12
HEAD = 64
IMG_PAD = 256
PAIR = 2 * HEAD
PAIRS = HEADS // 2
GROUPS = (2, 2, 2)
FF_BLOCK = 512

masked_value = -1e30
norm_eps = 1e-05

bf16 = jnp.bfloat16
f32 = jnp.float32

NN = (((1,), (0,)), ((), ()))
NT = (((1,), (1,)), ((), ()))
TN = (((0,), (0,)), ((), ()))
VMEM_BYTES = 56 << 20


def dot(left, right, dims=NN):
    return lax.dot_general(left, right, dims, preferred_element_type=f32)


def column_sum(values):
    return jnp.sum(values, axis=0, keepdims=True)


def row_mean(values):
    return jnp.mean(values, axis=1, keepdims=True)


def normalise(values):
    centred = values - row_mean(values)
    scale = lax.rsqrt(row_mean(centred * centred) + norm_eps)
    return centred * scale, scale


def norm_transpose(unit, scale, gain, grad):
    grad_unit = grad * gain
    return scale * (grad_unit - row_mean(grad_unit) - unit * row_mean(grad_unit * unit))


def params(**more):
    return pltpu.CompilerParams(vmem_limit_bytes=VMEM_BYTES, **more)


def cost(flops, moved, special=0):
    return pl.CostEstimate(flops=flops, bytes_accessed=moved, transcendentals=special)


def project_kernel(hid_ref, vec_ref, weight_ref, bias_ref, normed_ref, out_ref):
    unit, _ = normalise(hid_ref[...].astype(f32))
    normed = (unit * vec_ref[0:1] + vec_ref[1:2]).astype(bf16)
    normed_ref[...] = normed
    width = normed.shape[1]
    for part in range(3):
        cols = slice(part * width, (part + 1) * width)
        rows = dot(normed, weight_ref[:, cols])
        if part == 0:
            rows = (rows + bias_ref[0:1]).astype(bf16) * jnp.asarray(HEAD**-0.5, bf16)
        if part == 2:
            rows = rows + bias_ref[1:2]
        out_ref[:, cols] = rows.astype(bf16)


def project_rows(hidden, vecs, weight, bias):
    rows, width = hidden.shape
    block = 256
    whole = lambda shape: pl.BlockSpec(shape, lambda r: (0, 0), pipeline_mode=pl.Buffered(1))
    return pl.pallas_call(
        project_kernel,
        grid=(rows // block,),
        in_specs=[
            pl.BlockSpec((block, width), lambda r: (r, 0)),
            whole(vecs.shape),
            whole(weight.shape),
            whole(bias.shape),
        ],
        out_specs=[
            pl.BlockSpec((block, width), lambda r: (r, 0)),
            pl.BlockSpec((block, 3 * width), lambda r: (r, 0)),
        ],
        out_shape=[
            jax.ShapeDtypeStruct((rows, width), bf16),
            jax.ShapeDtypeStruct((rows, 3 * width), bf16),
        ],
        compiler_params=params(),
        cost_estimate=cost(6 * rows * width * width, 10 * rows * width + 6 * width * width),
        name="project_rows",
    )(hidden, vecs, weight, bias)


def image_kernel(hid_ref, vec_ref, weight_ref, bias_ref, normed_ref, out_ref):
    unit, _ = normalise(hid_ref[...].astype(f32))
    normed = (unit * vec_ref[0:1] + vec_ref[1:2]).astype(bf16)
    normed_ref[...] = normed
    width = normed.shape[1]
    out_ref[:, :width] = dot(normed, weight_ref[:, width : 2 * width]).astype(bf16)
    out_ref[:, width:] = (dot(normed, weight_ref[:, 2 * width :]) + bias_ref[1:2]).astype(bf16)


def image_rows(hidden, vecs, weight, bias):
    rows, width = hidden.shape
    return pl.pallas_call(
        image_kernel,
        out_shape=[
            jax.ShapeDtypeStruct((rows, width), bf16),
            jax.ShapeDtypeStruct((rows, 2 * width), bf16),
        ],
        compiler_params=params(),
        cost_estimate=cost(4 * rows * width * width, 8 * rows * width + 6 * width * width),
        name="image_rows",
    )(hidden, vecs, weight, bias)


def segments(shape, axis, info_ref):
    places = lax.broadcasted_iota(jnp.int32, shape, axis)
    total = jnp.zeros(shape, jnp.int32)
    for which in range(4):
        total += (places >= info_ref[1 + which]).astype(jnp.int32)
    return total


def own_bias(rows, info_ref):
    shape = (rows, rows)
    same = segments(shape, 0, info_ref) == segments(shape, 1, info_ref)
    return jnp.where(same & (info_ref[5] == 1), 0.0, masked_value).astype(f32)


def image_bias(shape, axis, info_ref):
    places = lax.broadcasted_iota(jnp.int32, shape, axis)
    return jnp.where(places < info_ref[0], 0.0, masked_value).astype(f32)


def forward_kernel(
    info_ref, q_ref, k_ref, v_ref, ik_ref, iv_ref, out_ref, lse_ref, image_part, own_part
):
    rows = q_ref.shape[0]

    @pl.when(pl.program_id(0) == 0)
    def _():
        image_part[...] = image_bias(image_part.shape, 1, info_ref)
        own_part[...] = own_bias(rows, info_ref)

    first = lax.broadcasted_iota(jnp.int32, (rows, PAIR), 1) < HEAD
    zero = jnp.zeros((), bf16)
    q = q_ref[...]
    image_keys, image_values = ik_ref[...], iv_ref[...]
    keys, values = k_ref[...], v_ref[...]
    outs, tops = [], []
    for head in range(2):
        q_head = jnp.where(first, q, zero) if head == 0 else jnp.where(first, zero, q)
        far = dot(q_head, image_keys, NT) + image_part[...]
        own = dot(q_head, keys, NT) + own_part[...]
        top = jnp.maximum(
            jnp.max(far, axis=1, keepdims=True), jnp.max(own, axis=1, keepdims=True)
        )
        far = jnp.exp(far - top)
        own = jnp.exp(own - top)
        total = jnp.sum(far, axis=1, keepdims=True) + jnp.sum(own, axis=1, keepdims=True)
        summed = dot(far.astype(bf16), image_values) + dot(own.astype(bf16), values)
        outs.append(summed / total)
        tops.append(top + jnp.log(total))
    out_ref[...] = jnp.where(first, outs[0], outs[1]).astype(bf16)
    turned = jnp.transpose(jnp.where(first, tops[0], tops[1]))
    lse_ref[0, 0:1, :] = turned[0:1]
    lse_ref[0, 1:2, :] = turned[HEAD : HEAD + 1]


def attend_forward(info, item, projected, image):
    rows = projected.shape[0] // 2
    spec = lambda base: pl.BlockSpec((rows, PAIR), lambda h, *_: (item, base + h))
    far = lambda base: pl.BlockSpec((IMG_PAD, PAIR), lambda h, *_: (0, base + h))
    keys = rows + IMG_PAD
    return pl.pallas_call(
        forward_kernel,
        grid_spec=pltpu.PrefetchScalarGridSpec(
            num_scalar_prefetch=1,
            grid=(PAIRS,),
            in_specs=[spec(0), spec(PAIRS), spec(2 * PAIRS), far(0), far(PAIRS)],
            out_specs=[
                pl.BlockSpec((rows, PAIR), lambda h, *_: (0, h)),
                pl.BlockSpec((1, 2, rows), lambda h, *_: (h, 0, 0)),
            ],
            scratch_shapes=[pltpu.VMEM((rows, IMG_PAD), f32), pltpu.VMEM((rows, rows), f32)],
        ),
        out_shape=[
            jax.ShapeDtypeStruct((rows, HEADS * HEAD), bf16),
            jax.ShapeDtypeStruct((PAIRS, 2, rows), f32),
        ],
        compiler_params=params(),
        cost_estimate=cost(16 * HEADS * rows * keys * HEAD, 6 << 20, HEADS * rows * keys),
        name="attend_forward",
    )(info, projected, projected, projected, image, image)


def backward_kernel(
    info_ref,
    q_ref,
    k_ref,
    v_ref,
    ik_ref,
    iv_ref,
    out_ref,
    grad_ref,
    lse_ref,
    gq_ref,
    gk_ref,
    gv_ref,
    gik_ref,
    giv_ref,
    image_part,
    own_part,
):
    rows = q_ref.shape[0]

    @pl.when(pl.program_id(0) == 0)
    def _():
        image_part[...] = image_bias(image_part.shape, 0, info_ref)
        own_part[...] = own_bias(rows, info_ref)

    first = lax.broadcasted_iota(jnp.int32, (rows, PAIR), 1) < HEAD
    zero = jnp.zeros((), bf16)
    q, grad = q_ref[...], grad_ref[...]
    products = grad.astype(f32) * out_ref[...].astype(f32)
    head_lanes = lax.broadcasted_iota(jnp.int32, (8, PAIR), 1) // HEAD
    head_rows = lax.broadcasted_iota(jnp.int32, (8, PAIR), 0)
    center = lax.dot_general(
        (head_lanes == head_rows).astype(f32),
        products,
        NT,
        preferred_element_type=f32,
        precision=lax.Precision.HIGHEST,
    )
    q_heads = [jnp.where(first, q, zero), jnp.where(first, zero, q)]
    grad_heads = [jnp.where(first, grad, zero), jnp.where(first, zero, grad)]
    lse = lse_ref[0]
    grad_query = [None, None]
    half = rows // 2
    pieces = (
        (ik_ref, iv_ref, gik_ref, giv_ref, image_part, 0, IMG_PAD),
        (k_ref, v_ref, gk_ref, gv_ref, own_part, 0, half),
        (k_ref, v_ref, gk_ref, gv_ref, own_part, half, half),
    )
    for keys_ref, values_ref, gk_out, gv_out, bias, start, count in pieces:
        piece = slice(start, start + count)
        keys, values = keys_ref[piece, :], values_ref[piece, :]
        low_lanes = lax.broadcasted_iota(jnp.int32, (count, PAIR), 1) < HEAD
        grad_keys, grad_values = [], []
        for head in range(2):
            scores = dot(keys, q_heads[head], NT) + bias[piece, :]
            probs = jnp.exp(scores - lse[head : head + 1])
            grad_probs = dot(values, grad_heads[head], NT)
            grad_scores = (probs * (grad_probs - center[head : head + 1])).astype(bf16)
            grad_values.append(dot(probs.astype(bf16), grad))
            grad_keys.append(dot(grad_scores, q))
            term = dot(grad_scores, keys, TN)
            grad_query[head] = term if grad_query[head] is None else grad_query[head] + term
        gk_out[piece, :] = jnp.where(low_lanes, grad_keys[0], grad_keys[1]).astype(bf16)
        gv_out[piece, :] = jnp.where(low_lanes, grad_values[0], grad_values[1]).astype(bf16)
    gq_ref[...] = (jnp.where(first, grad_query[0], grad_query[1]) * HEAD**-0.5).astype(bf16)


def attend_backward(info, item, start, pairs, projected, image, attended, grad, lse):
    rows = attended.shape[0]
    spec = lambda base: pl.BlockSpec((rows, PAIR), lambda h, *_: (item, base + start + h))
    far = lambda base: pl.BlockSpec((IMG_PAD, PAIR), lambda h, *_: (0, base + start + h))
    own = pl.BlockSpec((rows, PAIR), lambda h, *_: (0, start + h))
    outs = pl.BlockSpec((rows, PAIR), lambda h, *_: (0, h))
    far_outs = pl.BlockSpec((IMG_PAD, PAIR), lambda h, *_: (0, h))
    keys = rows + IMG_PAD
    return pl.pallas_call(
        backward_kernel,
        grid_spec=pltpu.PrefetchScalarGridSpec(
            num_scalar_prefetch=1,
            grid=(pairs,),
            in_specs=[
                spec(0),
                spec(PAIRS),
                spec(2 * PAIRS),
                far(0),
                far(PAIRS),
                own,
                spec(0),
                pl.BlockSpec((1, 2, rows), lambda h, *_: (start + h, 0, 0)),
            ],
            out_specs=[outs, outs, outs, far_outs, far_outs],
            scratch_shapes=[pltpu.VMEM((IMG_PAD, rows), f32), pltpu.VMEM((rows, rows), f32)],
        ),
        out_shape=[jax.ShapeDtypeStruct((rows, pairs * PAIR), bf16)] * 3
        + [jax.ShapeDtypeStruct((IMG_PAD, pairs * PAIR), bf16)] * 2,
        compiler_params=params(),
        cost_estimate=cost(
            80 * pairs * rows * keys * HEAD, pairs * 2 << 20, 2 * pairs * rows * keys
        ),
        name="attend_backward",
    )(info, projected, projected, projected, image, image, attended, grad, lse)


def gelu_pair(values):
    share = 0.5 * (1.0 + lax.erf(values * 0.7071067811865476))
    slope = share + values * jnp.exp(-0.5 * values * values) * 0.3989422804014327
    return values * share, slope


def feed_kernel(
    live_ref,
    att0_ref,
    att1_ref,
    project_ref,
    hid_ref,
    cot_ref,
    vec_ref,
    expand_ref,
    expand_bias_ref,
    reduce_ref,
    out_ref,
    gmid_ref,
    gatt_ref,
    gproject_ref,
    gvec_ref,
    gexpand_ref,
    greduce_ref,
    gexpand_bias_ref,
    middle,
    feed,
    top,
    result,
    gfeed,
    *,
    item_rows,
):
    step = pl.program_id(0)
    rows, width = hid_ref.shape
    block = 256
    att_refs = (att0_ref, att1_ref)

    @pl.when(step == 0)
    def _():
        for start in range(0, rows, block):
            here = slice(start, start + block)
            inside = slice(start % item_rows, start % item_rows + block)
            att = att_refs[start // item_rows][inside, :]
            x = hid_ref[here, :].astype(f32) + dot(att, project_ref[...]) + vec_ref[0:1]
            middle[here, :] = x
            unit, _ = normalise(x)
            feed[here, :] = (unit * vec_ref[1:2] + vec_ref[2:3]).astype(bf16)
            places = lax.broadcasted_iota(jnp.int32, (block, width), 0) + start % item_rows
            live = places < live_ref[start // item_rows]
            top[here, :] = jnp.where(live, cot_ref[here, :].astype(f32), 0.0).astype(bf16)
            result[here, :] = x + vec_ref[3:4]
            gfeed[here, :] = jnp.zeros((block, width), f32)

    expand, reduce = expand_ref[...], reduce_ref[...]
    active_parts, gup_parts = [], []
    for start in range(0, rows, item_rows):
        here = slice(start, start + item_rows)
        upward = dot(feed[here, :], expand) + expand_bias_ref[...]
        gactive = dot(top[here, :], reduce, NT)
        active, slope = gelu_pair(upward)
        active = active.astype(bf16)
        gup = (gactive * slope).astype(bf16)
        result[here, :] += dot(active, reduce)
        gfeed[here, :] += dot(gup, expand, NT)
        active_parts.append(active)
        gup_parts.append(gup)
    active = jnp.concatenate(active_parts, axis=0)
    gup = jnp.concatenate(gup_parts, axis=0)
    greduce_ref[...] = dot(active, top[...], TN).astype(bf16)
    gexpand_ref[...] = dot(feed[...], gup, TN).astype(bf16)
    gexpand_bias_ref[...] = column_sum(gup.astype(f32))

    @pl.when(step == pl.num_programs(0) - 1)
    def _():
        sums = [jnp.zeros((1, width), f32)] * 4
        for start in range(0, rows, block):
            here = slice(start, start + block)
            out_ref[here, :] = result[here, :].astype(bf16)
            unit, scale = normalise(middle[here, :])
            grad = gfeed[here, :]
            grad_top = top[here, :].astype(f32)
            gmid = grad_top + norm_transpose(unit, scale, vec_ref[1:2], grad)
            terms = (grad * unit, grad, grad_top, gmid)
            sums = [old + column_sum(new) for old, new in zip(sums, terms)]
            gmid_ref[here, :] = gmid
            gbranch = gmid.astype(bf16)
            feed[here, :] = gbranch
            gatt_ref[here, :] = dot(gbranch, project_ref[...], NT).astype(bf16)
        total = dot(att0_ref[...], feed[:item_rows, :], TN)
        total += dot(att1_ref[...], feed[item_rows:, :], TN)
        gproject_ref[...] = total.astype(bf16)
        gvec_ref[...] = jnp.concatenate(sums + [jnp.zeros((4, width), f32)], axis=0)


def feed_forward(live, att0, att1, project, hidden, cotangent, vecs, expand, ebias, reduce):
    rows, width = hidden.shape
    item_rows = att0.shape[0]
    units = reduce.shape[0]
    steps = units // FF_BLOCK
    whole = lambda shape: pl.BlockSpec(
        shape, lambda j, *_: (0,) * len(shape), pipeline_mode=pl.Buffered(1)
    )
    shape = jax.ShapeDtypeStruct
    return pl.pallas_call(
        functools.partial(feed_kernel, item_rows=item_rows),
        grid_spec=pltpu.PrefetchScalarGridSpec(
            num_scalar_prefetch=1,
            grid=(steps,),
            in_specs=[
                whole(att0.shape),
                whole(att1.shape),
                whole(project.shape),
                whole(hidden.shape),
                whole(cotangent.shape),
                whole(vecs.shape),
                pl.BlockSpec((width, FF_BLOCK), lambda j, *_: (0, j)),
                pl.BlockSpec((1, FF_BLOCK), lambda j, *_: (0, j)),
                pl.BlockSpec((FF_BLOCK, width), lambda j, *_: (j, 0)),
            ],
            out_specs=[
                whole((rows, width)),
                whole((rows, width)),
                whole((rows, width)),
                whole((width, width)),
                whole((8, width)),
                pl.BlockSpec((width, FF_BLOCK), lambda j, *_: (j, 0)),
                pl.BlockSpec((FF_BLOCK, width), lambda j, *_: (j, 0)),
                pl.BlockSpec((1, FF_BLOCK), lambda j, *_: (0, j)),
            ],
            scratch_shapes=[
                pltpu.VMEM((rows, width), f32),
                pltpu.VMEM((rows, width), bf16),
                pltpu.VMEM((rows, width), bf16),
                pltpu.VMEM((rows, width), f32),
                pltpu.VMEM((rows, width), f32),
            ],
        ),
        out_shape=[
            shape((rows, width), bf16),
            shape((rows, width), f32),
            shape((rows, width), bf16),
            shape((width, width), bf16),
            shape((8, width), f32),
            shape((steps * width, FF_BLOCK), bf16),
            shape((units, width), bf16),
            shape((1, units), f32),
        ],
        compiler_params=params(),
        cost_estimate=cost(12 * rows * width * units, 40 << 20, 2 * rows * units),
        name="feed_forward",
    )(live, att0, att1, project, hidden, cotangent, vecs, expand, ebias, reduce)


def weight_kernel(normed_ref, img0_ref, img1_ref, *refs):
    grads, (out_ref, sums_ref) = refs[:10], refs[10:]
    rows, width = normed_ref.shape
    half = rows // 2
    sums = []
    for part in range(3):
        total = dot(normed_ref[:half, :], grads[part][...], TN)
        total += dot(normed_ref[half:, :], grads[5 + part][...], TN)
        sums.append(
            column_sum(grads[part][...].astype(f32)) + column_sum(grads[5 + part][...].astype(f32))
        )
        if part > 0:
            total += dot(img0_ref[...], grads[2 + part][...], TN)
            total += dot(img1_ref[...], grads[7 + part][...], TN)
        if part == 2:
            sums[2] += column_sum(grads[4][...].astype(f32)) + column_sum(
                grads[9][...].astype(f32)
            )
        out_ref[part * width : (part + 1) * width, :] = total.astype(bf16)
    zeros = jnp.zeros((6, sums[0].shape[1]), f32)
    sums_ref[...] = jnp.concatenate([sums[0], sums[2], zeros], axis=0)


def weight_grads(normed, img0, img1, first_grads, second_grads):
    rows, width = normed.shape
    cols = first_grads[0].shape[1]
    return pl.pallas_call(
        weight_kernel,
        out_shape=[
            jax.ShapeDtypeStruct((3 * width, cols), bf16),
            jax.ShapeDtypeStruct((8, cols), f32),
        ],
        compiler_params=params(),
        cost_estimate=cost(8 * rows * width * cols, 8 << 20),
        name="weight_grads",
    )(normed, img0, img1, *first_grads, *second_grads)


def image_grad_kernel(weight_ref, *refs):
    grads, out_ref = refs[:-1], refs[-1]
    width = weight_ref.shape[0]
    groups = len(grads) // 4
    for item in range(2):
        total = jnp.zeros((IMG_PAD, width), f32)
        for part in range(2):
            offset = (1 + part) * width
            for group in range(groups):
                grad = grads[(item * groups + group) * 2 + part][...]
                total += dot(grad, weight_ref[:, offset : offset + grad.shape[1]], NT)
                offset += grad.shape[1]
        out_ref[item] = total.astype(bf16)


def image_grads(weight, grads):
    width = weight.shape[0]
    return pl.pallas_call(
        image_grad_kernel,
        out_shape=jax.ShapeDtypeStruct((2, IMG_PAD, width), bf16),
        compiler_params=params(),
        cost_estimate=cost(8 * IMG_PAD * width * width, 6 << 20),
        name="image_grads",
    )(weight, *grads)


def row_grad_kernel(weight_ref, *refs):
    grads, out_ref = refs[:-1], refs[-1]
    width = weight_ref.shape[0]
    groups = len(grads) // 6
    half = out_ref.shape[0] // 2
    for item in range(2):
        total = jnp.zeros((half, width), f32)
        for part in range(3):
            offset = part * width
            for group in range(groups):
                grad = grads[(item * groups + group) * 3 + part][...]
                total += dot(grad, weight_ref[:, offset : offset + grad.shape[1]], NT)
                offset += grad.shape[1]
        out_ref[item * half : (item + 1) * half, :] = total


def row_grads(weight, grads, rows):
    width = weight.shape[0]
    return pl.pallas_call(
        row_grad_kernel,
        out_shape=jax.ShapeDtypeStruct((rows, width), f32),
        compiler_params=params(),
        cost_estimate=cost(6 * rows * width * width, 12 << 20),
        name="row_grads",
    )(weight, *grads)


def finish_kernel(hid_ref, gmid_ref, gnorm_ref, near_ref, far_ref, vec_ref, out_ref, sums_ref):
    rows, width = hid_ref.shape
    half = rows // 2
    sums = [jnp.zeros((1, width), f32)] * 2
    for start in range(0, rows, IMG_PAD):
        here = slice(start, start + IMG_PAD)
        unit, scale = normalise(hid_ref[here, :].astype(f32))
        grad = gnorm_ref[here, :]
        if start % half == 0:
            item = start // half
            near = near_ref[item].astype(f32) * vec_ref[1:2]
            grad = grad + near + far_ref[item].astype(f32)
        sums = [sums[0] + column_sum(grad * unit), sums[1] + column_sum(grad)]
        total = gmid_ref[here, :] + norm_transpose(unit, scale, vec_ref[0:1], grad)
        out_ref[here, :] = total.astype(bf16)
    sums_ref[...] = jnp.concatenate(sums + [jnp.zeros((6, width), f32)], axis=0)


def finish_rows(hidden, gmid, gnorm, near, far, vecs):
    rows, width = hidden.shape
    return pl.pallas_call(
        finish_kernel,
        out_shape=[
            jax.ShapeDtypeStruct((rows, width), bf16),
            jax.ShapeDtypeStruct((8, width), f32),
        ],
        compiler_params=params(),
        cost_estimate=cost(40 * rows * width, 14 * rows * width),
        name="finish_rows",
    )(hidden, gmid, gnorm, near, far, vecs)


def swap(value, axes, pair_of):
    count = 1
    for axis in axes:
        count *= lax.axis_size(axis)
    return lax.ppermute(value, axes, [(source, pair_of(source)) for source in range(count)])


def place_of(axes):
    place = 0
    for axis in axes:
        place = place * lax.axis_size(axis) + lax.axis_index(axis)
    return place


def stage_bits(axes):
    count = 1
    for axis in axes:
        count *= lax.axis_size(axis)
    bits = count.bit_length() - 1
    core = len(axes) - 1
    others = [bit for bit in range(bits) if bit != core]
    if len(axes) == 1:
        if len(others) == 3:
            return [(core, core), (1, 2), (3, 1), (2, 3)]
    elif len(others) == 4:
        return [(core, core), (0, 2), (3, 0), (2, 3), (4, 4)]
    turned = others[1:] + others[:1]
    return [(core, core)] + list(zip(others, turned))


def partner(source, pair, core):
    return source ^ (1 << pair[(source >> core) & 1])


def all_sum(value, axes):
    place = place_of(axes)
    core = len(axes) - 1
    on_second = ((place >> core) & 1) == 1
    stages = stage_bits(axes)
    terms = (value,)

    def part(which, half):
        found = [lax.dynamic_slice_in_dim(t, which * half, half, 0) for t in terms]
        if len(found) == 1:
            return found[0]
        return (found[0].astype(f32) + found[1].astype(f32)).astype(bf16)

    for pair in stages:
        half = terms[0].shape[0] // 2
        side = (place >> jnp.where(on_second, pair[1], pair[0])) & 1
        sent = part(1 - side, half)
        kept = part(side, half)
        got = swap(sent, axes, functools.partial(partner, pair=pair, core=core))
        terms = (kept, got)
    mine = (terms[0].astype(f32) + terms[1].astype(f32)).astype(bf16)
    for pair in reversed(stages):
        side = (place >> jnp.where(on_second, pair[1], pair[0])) & 1
        got = swap(mine, axes, functools.partial(partner, pair=pair, core=core))
        low = jnp.where(side == 0, mine, got)
        high = jnp.where(side == 0, got, mine)
        mine = jnp.concatenate([low, high], axis=0)
    return mine


def small_sum(value, axis):
    for bit in range(lax.axis_size(axis).bit_length() - 1):
        value = value + swap(value, (axis,), lambda source, bit=bit: source ^ (1 << bit))
    return value


def on_device(
    hidden_in,
    image_count,
    text_lengths,
    attend_gain,
    attend_shift,
    project_in,
    bias_pair,
    project_out,
    project_bias,
    feed_gain,
    feed_shift,
    expand_weight,
    expand_bias,
    reduce_weight,
    reduce_bias,
    cotangent,
):
    items, _, rows, width = hidden_in.shape
    is_text = lax.axis_index("mod") == 1
    hidden = hidden_in.reshape(items * rows, width)
    to_text = lambda value: lax.ppermute(value, "mod", [(0, 1)])
    to_image = lambda value: lax.ppermute(value, "mod", [(1, 0)])

    attend_vecs = jnp.concatenate([attend_gain, attend_shift], axis=0)
    image_vecs = jnp.where(is_text, to_text(attend_vecs), attend_vecs)
    ends = jnp.cumsum(text_lengths, axis=1)
    text_flag = is_text.astype(jnp.int32)
    images = []
    for item in range(items):
        own_image = hidden_in[item, 0, :IMG_PAD]
        images.append(jnp.where(is_text, to_text(own_image), own_image))

    normed, projected = project_rows(hidden, attend_vecs, project_in, bias_pair)
    infos, normed_images, image_pairs, attended, lses = [], [], [], [], []
    for item in range(items):
        info = jnp.stack(
            [image_count[item], *(ends[item, j] for j in range(ends.shape[1])), text_flag]
        )
        infos.append(info)
        normed_image, image_pair = image_rows(images[item], image_vecs, project_in, bias_pair)
        normed_images.append(normed_image)
        image_pairs.append(image_pair)
        out, lse = attend_forward(info, item, projected, image_pair)
        attended.append(out)
        lses.append(lse)

    live = jnp.where(is_text, rows, image_count)
    feed_vecs = jnp.concatenate(
        [project_bias[None], feed_gain, feed_shift, reduce_bias, jnp.zeros((4, width), f32)], axis=0
    )
    (
        hidden_out,
        grad_middle,
        grad_attended,
        project_out_grad,
        vec_grads,
        expand_grad,
        reduce_grad,
        expand_bias_grad,
    ) = feed_forward(
        live,
        attended[0],
        attended[1],
        project_out,
        hidden,
        cotangent.reshape(items * rows, width),
        feed_vecs,
        expand_weight[0],
        expand_bias,
        reduce_weight[0],
    )
    reduce_grad = all_sum(reduce_grad, ("dp",))
    expand_grad = all_sum(expand_grad, ("dp",))
    project_out_grad = all_sum(project_out_grad, ("dp", "mod"))

    start = 0
    row_parts = [[], []]
    image_parts = [[], []]
    blocks = []
    pair_sums = []
    for pairs in GROUPS:
        grads = [
            attend_backward(
                infos[item],
                item,
                start,
                pairs,
                projected,
                image_pairs[item],
                attended[item],
                grad_attended,
                lses[item],
            )
            for item in range(items)
        ]
        for item in range(items):
            row_parts[item] += grads[item][:3]
            image_parts[item] += grads[item][3:]
        block, sums = weight_grads(normed, normed_images[0], normed_images[1], grads[0], grads[1])
        blocks.append(all_sum(block, ("dp", "mod")))
        pair_sums.append(sums)
        start += pairs

    near = image_grads(project_in, image_parts[0] + image_parts[1])
    far = to_image(near)
    grad_normed = row_grads(project_in, row_parts[0] + row_parts[1], items * rows)
    image_flag = jnp.where(is_text, 0.0, 1.0) * jnp.ones((1, width), f32)
    finish_vecs = jnp.concatenate([attend_gain, image_flag, jnp.zeros((6, width), f32)], axis=0)
    grad_in, attend_sums = finish_rows(hidden, grad_middle, grad_normed, near, far, finish_vecs)

    early = small_sum(
        jnp.concatenate([vec_grads[:4], expand_bias_grad.reshape(-1, width)], axis=0), "dp"
    )
    bias_pair_grad = jnp.concatenate(pair_sums, axis=1)[:2]
    late = small_sum(jnp.concatenate([attend_sums[:2], bias_pair_grad], axis=0), "dp")
    shared = small_sum(jnp.concatenate([early[3:4], late[2:4]], axis=0), "mod")

    cols = [[], [], []]
    for block in blocks:
        for part in range(3):
            cols[part].append(block[part * width : (part + 1) * width])
    project_in_grad = jnp.concatenate(cols[0] + cols[1] + cols[2], axis=1).astype(f32)
    expand_grad = expand_grad.reshape(-1, width, FF_BLOCK).transpose(1, 0, 2).reshape(width, -1)
    return (
        hidden_out.reshape(hidden_in.shape),
        grad_in.reshape(hidden_in.shape),
        late[0:1],
        late[1:2],
        project_in_grad,
        shared[1:3],
        project_out_grad.astype(f32),
        shared[0],
        early[0:1],
        early[1:2],
        expand_grad.astype(f32)[None],
        early[4:].reshape(1, -1),
        reduce_grad.astype(f32)[None],
        early[2:3],
    )


def solution(mesh):
    in_specs = (
        P("dp", "mod", None, None),
        P("dp"),
        P("dp", None),
        P("mod", None),
        P("mod", None),
        P(),
        P(),
        P(),
        P(),
        P("mod", None),
        P("mod", None),
        P("mod", None, None),
        P("mod", None),
        P("mod", None, None),
        P("mod", None),
        P("dp", "mod", None, None),
    )
    out_specs = (
        P("dp", "mod", None, None),
        P("dp", "mod", None, None),
        P("mod", None),
        P("mod", None),
        P(),
        P(),
        P(),
        P(),
        P("mod", None),
        P("mod", None),
        P("mod", None, None),
        P("mod", None),
        P("mod", None, None),
        P("mod", None),
    )
    return jax.shard_map(
        on_device, mesh=mesh, in_specs=in_specs, out_specs=out_specs, check_vma=False
    )
```

time: 944 us -> 480 us (0.51)
  waiting for transfers between devices: 399 us -> 140 us
  matrix products: 223 us -> 0 us
  Pallas kernels: 0 us -> 173 us
  blocking collectives: 98.7 us -> 0 us
  local copies, waits for them, and re-layouts: 111 us -> 42.6 us
  starting transfers between devices: 11.3 us -> 77.9 us
  other arithmetic: 79.6 us -> 37.2 us
  between operations: 15.4 us -> 1.86 us
    psum x2 -> x0, waiting for transfers between devices: 373 us -> none  [the longest x1 335 us: on_device(): lax.psum((attend_gain_grad, attend_shift_grad, feed_gain_grad, feed_shift...]
    dot_general x24 -> x0, matrix products: 223 us -> none  [the longest x1 36.4 us: on_device(): jnp.dot(feed_low, expand_weight[0], preferred_element_type=jnp.float32)]
    pallas_call x0 -> x18, Pallas kernels: none -> 173 us  [the longest x6 48.9 us: attend_backward(): pl.pallas_call(backward_kernel, grid_spec=pltpu.PrefetchScalarGridSpec(nu...]
    ppermute x4 -> x69, waiting for transfers between devices: 26.9 us -> 140 us  [the longest x65 140 us: swap(): lax.ppermute(value, axes, [(source, pair_of(source)) for source in range(...]
    psum x2 -> x0, blocking collectives: 98.7 us -> none  [the longest x1 60.7 us: on_device(): lax.psum((attend_gain_grad, attend_shift_grad, feed_gain_grad, feed_shift...]
    ppermute x4 -> x69, starting transfers between devices: 11 us -> 77.9 us  [the longest x65 68.6 us: swap(): lax.ppermute(value, axes, [(source, pair_of(source)) for source in range(...]
    slice x28 -> x9, local copies, waits for them, and re-layouts: 40.5 us -> 4.42 us  [the longest x1 0.84 us: on_device(): attend_sums[:2]]
    another operation x15 -> x2, local copies, waits for them, and re-layouts: 32.2 us -> 7.69 us  [on_device(): jnp.stack([image_count[item], *(ends[item, j] for j in range(ends.shape[1...]
  transfers between devices with their start and end apart: 6 -> 69, of which waited for: 3 -> 34; matrix products, arithmetic and copies ran while one was open for 14% -> 15% of each run, Pallas kernels for 0% -> 9%
where the time goes in v1:
time: 480 us; the launch traced here: 473 us
  Pallas kernels  173 us (36%)
  waiting for transfers between devices  140 us (29%)
  starting transfers between devices  77.9 us (16%)
  local copies, waits for them, and re-layouts  42.6 us (9%)
  other arithmetic  37.2 us (8%)
    ppermute x65, waiting for transfers between devices, swap(): lax.ppermute(value, axes, [(source, pair_of(source)) for source in range(...  140 us
    ppermute x65, starting transfers between devices, swap(): lax.ppermute(value, axes, [(source, pair_of(source)) for source in range(...  68.6 us
    pallas_call x6, Pallas kernels, attend_backward(): pl.pallas_call(backward_kernel, grid_spec=pltpu.PrefetchScalarGridSpec(nu...  48.9 us
    pallas_call x1, Pallas kernels, feed_forward(): pl.pallas_call(functools.partial(feed_kernel, item_rows=item_rows), grid_...  46.5 us
    pallas_call x2, Pallas kernels, attend_forward(): pl.pallas_call(forward_kernel, grid_spec=pltpu.PrefetchScalarGridSpec(num...  24.5 us
    pallas_call x3, Pallas kernels, weight_grads(): pl.pallas_call(weight_kernel, out_shape=[jax.ShapeDtypeStruct((3 * width,...  15.3 us
    unnamed x52, local copies, waits for them, and re-layouts  10.4 us
    dynamic_slice x6, local copies, waits for them, and re-layouts, part(): found = [lax.dynamic_slice_in_dim(t, which * half, half, 0) for t in terms]  10.2 us
  transfers between devices with their start and end apart: 69, of which 34 were waited for; matrix products, arithmetic and copies ran while one was open for 15% of the time, Pallas kernels for 9%

profile of v1, /device:TPU:0, one launch (start us, length us, event | category | flops | bytes accessed | tf_op | source)
XLA Modules:
  0.0 472.8 jit_solution(9411894791185060193)
XLA Ops:
  1.4 4.9 %collective-permute-start.1 = (f32[2,768]{1,0:T(2,128)S(1)}, f32[2,768]{1,0:T(2,128)S(1)}, u32[]{:S(2)}, u32[]{:S(2)}) collective-permute-start(f32[2,768]{1,0:T(2,128)S(1)} %pad_maximum_fusion.30.vec_ref), channel_id=1, source_target_pairs={{0,1},{2,3},{4,5},{6,7},{8,9},{10,11},{12,13},{14,15},{16,17},{18,... | collective-permute-start | bytes 18440 | tf_op jit(solution)/shard_map/ppermute | solution.py:678
  12.8 8.6 %project_rows.1 = (bf16[1024,768]{1,0:T(8,128)(2,1)}, bf16[1024,2304]{1,0:T(8,128)(2,1)}) custom-call(bf16[1024,768]{1,0:T(8,128)(2,1)} %bitcast.43, f32[2,768]{1,0:T(2,128)} %copy-done.11, bf16[768,2304]{1,0:T(8,128)(2,1)} %weight_ref.9, f32[2,768]{1,0:T(2,128)} %bias_ref.5), custom_call_target="tpu_custom_call" | custom-call | flops 3623878656 | bytes 11403264 | tf_op jit(solution)/shard_map/project_rows/pallas_call | solution.py:80
  22.8 3.9 stack.16.info_ref
  26.6 3.8 stack.15.info_ref
  32.7 4.1 image_rows.3
  36.8 4.1 image_rows.2
  40.9 12.2 %attend_forward.3 = (bf16[512,768]{1,0:T(8,128)(2,1)}, f32[6,2,512]{2,1,0:T(2,128)}) custom-call(s32[6]{0:T(128)} %stack.16.info_ref, bf16[1024,2304]{1,0:T(8,128)(2,1)} %get-tuple-element.70.q_ref.k_ref.v_ref, bf16[1024,2304]{1,0:T(8,128)(2,1)} %get-tuple-element.70.q_ref.k_ref.v_ref, bf16[1024,2304]{1,0:T(8,128)(2,1)} %get-tuple-element.70.q_ref.k_ref.v_ref, ...), custom_call_target="tpu_custom_call" | custom-call | flops 4831838208 | bytes 6291456 | tf_op jit(solution)/shard_map/attend_forward/pallas_call | solution.py:185
  53.1 12.2 %attend_forward.2 = (bf16[512,768]{1,0:T(8,128)(2,1)}, f32[6,2,512]{2,1,0:T(2,128)}) custom-call(s32[6]{0:T(128)} %stack.15.info_ref, bf16[1024,2304]{1,0:T(8,128)(2,1)} %get-tuple-element.70.q_ref.k_ref.v_ref, bf16[1024,2304]{1,0:T(8,128)(2,1)} %get-tuple-element.70.q_ref.k_ref.v_ref, bf16[1024,2304]{1,0:T(8,128)(2,1)} %get-tuple-element.70.q_ref.k_ref.v_ref, ...), custom_call_target="tpu_custom_call" | custom-call | flops 4831838208 | bytes 6291456 | tf_op jit(solution)/shard_map/attend_forward/pallas_call | solution.py:185
  65.4 46.5 %feed_forward.1 = (bf16[1024,768]{1,0:T(8,128)(2,1)}, f32[1024,768]{1,0:T(8,128)}, bf16[1024,768]{1,0:T(8,128)(2,1)}, bf16[768,768]{1,0:T(8,128)(2,1)}, f32[8,76...) custom-call(s32[2]{0:T(128)} %broadcast_select_fusion.57.live_ref, ...), custom_call_target="tpu_custom_call" | custom-call | flops 28991029248 | bytes 41943040 | tf_op jit(solution)/shard_map/feed_forward/pallas_call | solution.py:414
  111.9 8.3 %attend_backward.11 = (bf16[512,256]{1,0:T(8,128)(2,1)}, bf16[512,256]{1,0:T(8,128)(2,1)}, bf16[512,256]{1,0:T(8,128)(2,1)}, bf16[256,256]{1,0:T(8,128)(2,1)}, bf16[256,256]{1,0:T(8,128)(2,1)}) custom-call(s32[6]{0:T(128)} %stack.16.info_ref, bf16[1024,2304]{1,0:T(8,128)(2,1)} %get-tuple-element.70.q_ref.k_ref.v_ref, ...), custom_call_target="tpu_custom_call" | custom-call | flops 4026531840 | bytes 4194304 | tf_op jit(solution)/shard_map/attend_backward/pallas_call | solution.py:282
  120.1 8.1 %attend_backward.10 = (bf16[512,256]{1,0:T(8,128)(2,1)}, bf16[512,256]{1,0:T(8,128)(2,1)}, bf16[512,256]{1,0:T(8,128)(2,1)}, bf16[256,256]{1,0:T(8,128)(2,1)}, bf16[256,256]{1,0:T(8,128)(2,1)}) custom-call(s32[6]{0:T(128)} %stack.16.info_ref, bf16[1024,2304]{1,0:T(8,128)(2,1)} %get-tuple-element.70.q_ref.k_ref.v_ref, ...), custom_call_target="tpu_custom_call" | custom-call | flops 4026531840 | bytes 4194304 | tf_op jit(solution)/shard_map/attend_backward/pallas_call | solution.py:282
  128.2 8.0 %attend_backward.9 = (bf16[512,256]{1,0:T(8,128)(2,1)}, bf16[512,256]{1,0:T(8,128)(2,1)}, bf16[512,256]{1,0:T(8,128)(2,1)}, bf16[256,256]{1,0:T(8,128)(2,1)}, bf16[256,256]{1,0:T(8,128)(2,1)}) custom-call(s32[6]{0:T(128)} %stack.16.info_ref, bf16[1024,2304]{1,0:T(8,128)(2,1)} %get-tuple-element.70.q_ref.k_ref.v_ref, ...), custom_call_target="tpu_custom_call" | custom-call | flops 4026531840 | bytes 4194304 | tf_op jit(solution)/shard_map/attend_backward/pallas_call | solution.py:282
  136.2 8.0 %attend_backward.8 = (bf16[512,256]{1,0:T(8,128)(2,1)}, bf16[512,256]{1,0:T(8,128)(2,1)}, bf16[512,256]{1,0:T(8,128)(2,1)}, bf16[256,256]{1,0:T(8,128)(2,1)}, bf16[256,256]{1,0:T(8,128)(2,1)}) custom-call(s32[6]{0:T(128)} %stack.15.info_ref, bf16[1024,2304]{1,0:T(8,128)(2,1)} %get-tuple-element.70.q_ref.k_ref.v_ref, ...), custom_call_target="tpu_custom_call" | custom-call | flops 4026531840 | bytes 4194304 | tf_op jit(solution)/shard_map/attend_backward/pallas_call | solution.py:282
  144.3 8.3 %attend_backward.7 = (bf16[512,256]{1,0:T(8,128)(2,1)}, bf16[512,256]{1,0:T(8,128)(2,1)}, bf16[512,256]{1,0:T(8,128)(2,1)}, bf16[256,256]{1,0:T(8,128)(2,1)}, bf16[256,256]{1,0:T(8,128)(2,1)}) custom-call(s32[6]{0:T(128)} %stack.15.info_ref, bf16[1024,2304]{1,0:T(8,128)(2,1)} %get-tuple-element.70.q_ref.k_ref.v_ref, ...), custom_call_target="tpu_custom_call" | custom-call | flops 4026531840 | bytes 4194304 | tf_op jit(solution)/shard_map/attend_backward/pallas_call | solution.py:282
  152.6 8.2 %attend_backward.6 = (bf16[512,256]{1,0:T(8,128)(2,1)}, bf16[512,256]{1,0:T(8,128)(2,1)}, bf16[512,256]{1,0:T(8,128)(2,1)}, bf16[256,256]{1,0:T(8,128)(2,1)}, bf16[256,256]{1,0:T(8,128)(2,1)}) custom-call(s32[6]{0:T(128)} %stack.15.info_ref, bf16[1024,2304]{1,0:T(8,128)(2,1)} %get-tuple-element.70.q_ref.k_ref.v_ref, ...), custom_call_target="tpu_custom_call" | custom-call | flops 4026531840 | bytes 4194304 | tf_op jit(solution)/shard_map/attend_backward/pallas_call | solution.py:282
  163.5 5.2 %weight_grads.5 = (bf16[2304,256]{1,0:T(8,128)(2,1)}, f32[8,256]{1,0:T(8,128)}) custom-call(bf16[1024,768]{1,0:T(8,128)(2,1)} %get-tuple-element.112.normed_ref, bf16[256,768]{1,0:T(8,128)(2,1)} %get-tuple-element.113.img0_ref, bf16[256,768]{1,0:T(8,128)(2,1)} %get-tuple-element.114.img1_ref, bf16[512,256]{1,0:T(8,128)(2,1)} %get-tuple-element.85.refs_6_.refs_0_, ...), custom_call_target="tpu_custom_call" | custom-call | flops 1610612736 | bytes 8388608 | tf_op jit(solution)/shard_map/weight_grads/pallas_call | solution.py:490
  170.6 5.0 %weight_grads.3 = (bf16[2304,256]{1,0:T(8,128)(2,1)}, f32[8,256]{1,0:T(8,128)}) custom-call(bf16[1024,768]{1,0:T(8,128)(2,1)} %get-tuple-element.112.normed_ref, bf16[256,768]{1,0:T(8,128)(2,1)} %get-tuple-element.113.img0_ref, bf16[256,768]{1,0:T(8,128)(2,1)} %get-tuple-element.114.img1_ref, bf16[512,256]{1,0:T(8,128)(2,1)} %get-tuple-element.79.refs_0_, ...), custom_call_target="tpu_custom_call" | custom-call | flops 1610612736 | bytes 8388608 | tf_op jit(solution)/shard_map/weight_grads/pallas_call | solution.py:490
  178.0 4.8 %image_grads.1.near_ref = bf16[2,256,768]{2,1,0:T(8,128)(2,1)} custom-call(bf16[768,2304]{1,0:T(8,128)(2,1)} %weight_ref.9, bf16[256,256]{1,0:T(8,128)(2,1)} %get-tuple-element.98.refs_0_.refs_3_, bf16[256,256]{1,0:T(8,128)(2,1)} %get-tuple-element.99.refs_1_.refs_4_, bf16[256,256]{1,0:T(8,128)(2,1)} %get-tuple-element.100.refs_2_.refs_3_, ...), custom_call_target="tpu_custom_call" | custom-call | flops 1207959552 | bytes 6291456 | tf_op jit(solution)/shard_map/image_grads/pallas_call | solution.py:519
  184.6 3.4 constant_dynamic-slice_fusion.2
  188.0 8.9 %row_grads.1.gnorm_ref = f32[1024,768]{1,0:T(8,128)} custom-call(bf16[768,2304]{1,0:T(8,128)(2,1)} %weight_ref.9, bf16[512,256]{1,0:T(8,128)(2,1)} %get-tuple-element.79.refs_0_, bf16[512,256]{1,0:T(8,128)(2,1)} %get-tuple-element.80.refs_1_, bf16[512,256]{1,0:T(8,128)(2,1)} %get-tuple-element.81.refs_2_, ...), custom_call_target="tpu_custom_call" | custom-call | flops 3623878656 | bytes 12582912 | tf_op jit(solution)/shard_map/row_grads/pallas_call | solution.py:546
  198.6 2.2 collective-permute-done.39
  202.4 5.1 %weight_grads.4 = (bf16[2304,256]{1,0:T(8,128)(2,1)}, f32[8,256]{1,0:T(8,128)}) custom-call(bf16[1024,768]{1,0:T(8,128)(2,1)} %get-tuple-element.112.normed_ref, bf16[256,768]{1,0:T(8,128)(2,1)} %get-tuple-element.113.img0_ref, bf16[256,768]{1,0:T(8,128)(2,1)} %get-tuple-element.114.img1_ref, bf16[512,256]{1,0:T(8,128)(2,1)} %get-tuple-element.82.refs_3_.refs_0_, ...), custom_call_target="tpu_custom_call" | custom-call | flops 1610612736 | bytes 8388608 | tf_op jit(solution)/shard_map/weight_grads/pallas_call | solution.py:490
  207.5 2.7 collective-permute-start.41
  214.2 7.4 %finish_rows.1 = (bf16[1024,768]{1,0:T(8,128)(2,1)}, f32[8,768]{1,0:T(8,128)}) custom-call(bf16[1024,768]{1,0:T(8,128)(2,1)} %bitcast.45, f32[1024,768]{1,0:T(8,128)} %get-tuple-element.76.gmid_ref, f32[1024,768]{1,0:T(8,128)} %row_grads.1.gnorm_ref, bf16[2,256,768]{2,1,0:T(8,128)(2,1)} %image_grads.1.near_ref, ...), custom_call_target="tpu_custom_call" | custom-call | flops 31457280 | bytes 11010048 | tf_op jit(solution)/shard_map/finish_rows/pallas_call | solution.py:575
  228.1 3.5 collective-permute-start.44
  233.3 2.1 collective-permute-done.6
  235.4 2.5 collective-permute-start.7
  247.6 5.1 %collective-permute-done.9 = bf16[576,256]{1,0:T(8,128)(2,1)S(1)} collective-permute-done((bf16[576,256]{1,0:T(8,128)(2,1)S(1)}, bf16[576,256]{1,0:T(8,128)(2,1)S(1)}, u32[]{:S(2)}, u32[]{:S(2)}) %collective-permute-start.9) | collective-permute-done | bytes 294944 | tf_op jit(solution)/shard_map/ppermute | solution.py:591
  252.9 5.6 %collective-permute-done.19 = bf16[576,256]{1,0:T(8,128)(2,1)S(1)} collective-permute-done((bf16[576,256]{1,0:T(8,128)(2,1)S(1)}, bf16[576,256]{1,0:T(8,128)(2,1)S(1)}, u32[]{:S(2)}, u32[]{:S(2)}) %collective-permute-start.19) | collective-permute-done | bytes 294944 | tf_op jit(solution)/shard_map/ppermute | solution.py:591
  268.5 2.7 collective-permute-start.47
  294.7 2.4 collective-permute-done.50
  297.9 2.4 collective-permute-done.35
  311.7 2.5 add_convert_fusion.1
  315.2 11.0 %collective-permute-done.54 = bf16[1152,512]{1,0:T(8,128)(2,1)S(1)} collective-permute-done((bf16[1152,512]{1,0:T(8,128)(2,1)S(1)}, bf16[1152,512]{1,0:T(8,128)(2,1)S(1)}, u32[]{:S(2)}, u32[]{:S(2)}) %collective-permute-start.54) | collective-permute-done | bytes 1179680 | tf_op jit(solution)/shard_map/ppermute | solution.py:591
  328.0 17.2 %collective-permute-done.62 = bf16[768,768]{1,0:T(8,128)(2,1)S(1)} collective-permute-done((bf16[768,768]{1,0:T(8,128)(2,1)S(1)}, bf16[768,768]{1,0:T(8,128)(2,1)S(1)}, u32[]{:S(2)}, u32[]{:S(2)}) %collective-permute-start.62) | collective-permute-done | bytes 1179680 | tf_op jit(solution)/shard_map/ppermute | solution.py:591
  348.8 29.4 %collective-permute-done.63 = bf16[384,768]{1,0:T(8,128)(2,1)S(1)} collective-permute-done((bf16[384,768]{1,0:T(8,128)(2,1)S(1)}, bf16[384,768]{1,0:T(8,128)(2,1)S(1)}, u32[]{:S(2)}, u32[]{:S(2)}) %collective-permute-start.63) | collective-permute-done | bytes 589856 | tf_op jit(solution)/shard_map/ppermute | solution.py:591
  380.8 7.5 %collective-permute-done.64 = bf16[192,768]{1,0:T(8,128)(2,1)S(1)} collective-permute-done((bf16[192,768]{1,0:T(8,128)(2,1)S(1)}, bf16[192,768]{1,0:T(8,128)(2,1)S(1)}, u32[]{:S(2)}, u32[]{:S(2)}) %collective-permute-start.64) | collective-permute-done | bytes 294944 | tf_op jit(solution)/shard_map/ppermute | solution.py:591
  388.5 3.0 collective-permute-done.57
  392.2 5.4 %collective-permute-done.65 = bf16[192,768]{1,0:T(8,128)(2,1)S(1)} collective-permute-done((bf16[192,768]{1,0:T(8,128)(2,1)S(1)}, bf16[192,768]{1,0:T(8,128)(2,1)S(1)}, u32[]{:S(2)}, u32[]{:S(2)}) %collective-permute-start.65) | collective-permute-done | bytes 294944 | tf_op jit(solution)/shard_map/ppermute | solution.py:591
  397.8 10.7 %collective-permute-done.58 = bf16[576,512]{1,0:T(8,128)(2,1)S(1)} collective-permute-done((bf16[576,512]{1,0:T(8,128)(2,1)S(1)}, bf16[576,512]{1,0:T(8,128)(2,1)S(1)}, u32[]{:S(2)}, u32[]{:S(2)}) %collective-permute-start.58) | collective-permute-done | bytes 589856 | tf_op jit(solution)/shard_map/ppermute | solution.py:591
  410.8 10.3 %collective-permute-done.66 = bf16[384,768]{1,0:T(8,128)(2,1)S(1)} collective-permute-done((bf16[384,768]{1,0:T(8,128)(2,1)S(1)}, bf16[384,768]{1,0:T(8,128)(2,1)S(1)}, u32[]{:S(2)}, u32[]{:S(2)}) %collective-permute-start.66) | collective-permute-done | bytes 589856 | tf_op jit(solution)/shard_map/ppermute | solution.py:591
  425.9 11.7 %collective-permute-done.67 = bf16[768,768]{1,0:T(8,128)(2,1)S(1)} collective-permute-done((bf16[768,768]{1,0:T(8,128)(2,1)S(1)}, bf16[768,768]{1,0:T(8,128)(2,1)S(1)}, u32[]{:S(2)}, u32[]{:S(2)}) %collective-permute-start.67) | collective-permute-done | bytes 1179680 | tf_op jit(solution)/shard_map/ppermute | solution.py:591
  439.8 3.5 convert_element_type.567
  446.1 2.5 pad_maximum_fusion
  448.6 7.4 %copy.33 = f32[6,768,512]{1,2,0:T(8,128)} copy(bf16[6,768,512]{2,1,0:T(8,128)(2,1)} %bitcast.42) | data formatting | bytes 14155776 | tf_op jit(solution)/shard_map/convert_element_type | solution.py:792
  456.0 9.6 %copy.36 = f32[1,768,3072]{2,1,0:T(8,128)} copy(f32[1,768,3072]{1,2,0:T(8,128)} %bitcast.41) | data formatting | bytes 18874368
  465.6 2.6 select_bitcast_fusion.1
  468.2 4.5 maximum_convert_fusion
  (294 shorter events, 112.4 us)
Async XLA Ops:
  1.4 29.8 %collective-permute-start.1 = (f32[2,768]{1,0:T(2,128)S(1)}, f32[2,768]{1,0:T(2,128)S(1)}, u32[]{:S(2)}, u32[]{:S(2)}) collective-permute-start(f32[2,768]{1,0:T(2,128)S(1)} %pad_maximum_fusion.30.vec_ref), channel_id=1, source_target_pairs={{0,1},{2,3},{4,5},{6,7},{8,9},{10,11},{12,13},{14,15},{16,17},{18,... | collective-permute-start | bytes 18440 | tf_op jit(solution)/shard_map/ppermute | solution.py:678
  7.4 24.3 %collective-permute-start.2 = (bf16[256,768]{1,0:T(8,128)(2,1)S(1)}, bf16[256,768]{1,0:T(8,128)(2,1)S(1)}, u32[]{:S(2)}, u32[]{:S(2)}) collective-permute-start(bf16[256,768]{1,0:T(8,128)(2,1)S(1)} %get-tuple-element.180), channel_id=1, source_target_pairs={{0,1},{2,3},{4,5},{6,7},{8,9},{10,11},{12,13},{14,15},{16,17},{18,... | collective-permute-start | bytes 1179656 | tf_op jit(solution)/shard_map/ppermute | solution.py:678
  8.7 23.0 %collective-permute-start = (bf16[256,768]{1,0:T(8,128)(2,1)S(1)}, bf16[256,768]{1,0:T(8,128)(2,1)S(1)}, u32[]{:S(2)}, u32[]{:S(2)}) collective-permute-start(bf16[256,768]{1,0:T(8,128)(2,1)S(1)} %get-tuple-element.181), channel_id=1, source_target_pairs={{0,1},{2,3},{4,5},{6,7},{8,9},{10,11},{12,13},{14,15},{16,17},{18,... | collective-permute-start | bytes 1179656 | tf_op jit(solution)/shard_map/ppermute | solution.py:678
  162.0 34.9 %collective-permute-start.38 = (f32[8,768]{1,0:T(8,128)S(1)}, f32[8,768]{1,0:T(8,128)S(1)}, u32[]{:S(2)}, u32[]{:S(2)}) collective-permute-start(f32[8,768]{1,0:T(8,128)S(1)} %pad_maximum_fusion.26), channel_id=1, source_target_pairs={{0,2},{2,0},{4,6},{6,4},{8,10},{10,8},{12,14},{14,12},{16,18},{18,... | collective-permute-start | bytes 73736 | tf_op jit(solution)/shard_map/ppermute | solution.py:591
  163.0 59.4 %collective-permute-start.43 = (bf16[384,768]{1,0:T(8,128)(2,1)}, bf16[384,768]{1,0:T(8,128)(2,1)}, u32[]{:S(2)}, u32[]{:S(2)}) collective-permute-start(bf16[384,768]{1,0:T(8,128)(2,1)} %constant_dynamic-slice_fusion), channel_id=1, source_target_pairs={{0,2},{1,3},{2,0},{3,1},{4,6},{5,7},{6,4},{7,5},{8,10},{9,11},{10,... | collective-permute-start | bytes 1769480 | tf_op jit(solution)/shard_map/ppermute | solution.py:591
  170.5 53.8 %collective-permute-start.28 = (bf16[1152,256]{1,0:T(8,128)(2,1)}, bf16[1152,256]{1,0:T(8,128)(2,1)}, u32[]{:S(2)}, u32[]{:S(2)}) collective-permute-start(bf16[1152,256]{1,0:T(8,128)(2,1)} %constant_dynamic-slice_fusion.1), channel_id=1, source_target_pairs={{0,2},{1,3},{2,0},{3,1},{4,6},{5,7},{6,4},{7,5},{8,10},{9,11},{10,... | collective-permute-start | bytes 1769480 | tf_op jit(solution)/shard_map/ppermute | solution.py:591
  177.5 54.1 %collective-permute-start.8 = (bf16[1152,256]{1,0:T(8,128)(2,1)}, bf16[1152,256]{1,0:T(8,128)(2,1)}, u32[]{:S(2)}, u32[]{:S(2)}) collective-permute-start(bf16[1152,256]{1,0:T(8,128)(2,1)} %constant_dynamic-slice_fusion.5), channel_id=1, source_target_pairs={{0,2},{1,3},{2,0},{3,1},{4,6},{5,7},{6,4},{7,5},{8,10},{9,11},{10,... | collective-permute-start | bytes 1769480 | tf_op jit(solution)/shard_map/ppermute | solution.py:591
  182.9 30.8 %collective-permute-start.3 = (bf16[2,256,768]{2,1,0:T(8,128)(2,1)}, bf16[2,256,768]{2,1,0:T(8,128)(2,1)}, u32[]{:S(2)}, u32[]{:S(2)}) collective-permute-start(bf16[2,256,768]{2,1,0:T(8,128)(2,1)} %image_grads.1.near_ref), channel_id=1, source_target_pairs={{1,0},{3,2},{5,4},{7,6},{9,8},{11,10},{13,12},{15,14},{17,16},{19,... | collective-permute-start | bytes 2359304 | tf_op jit(solution)/shard_map/ppermute | solution.py:679
  200.8 6.6 %collective-permute-start.40 = (f32[8,768]{1,0:T(8,128)S(1)}, f32[8,768]{1,0:T(8,128)S(1)}, u32[]{:S(2)}, u32[]{:S(2)}) collective-permute-start(f32[8,768]{1,0:T(8,128)S(1)} %add.422), channel_id=1, source_target_pairs={{0,8},{2,10},{4,12},{6,14},{8,0},{10,2},{12,4},{14,6},{16,24},{18,... | collective-permute-start | bytes 73736 | tf_op jit(solution)/shard_map/ppermute | solution.py:591
  212.4 23.0 %collective-permute-start.18 = (bf16[1152,256]{1,0:T(8,128)(2,1)}, bf16[1152,256]{1,0:T(8,128)(2,1)}, u32[]{:S(2)}, u32[]{:S(2)}) collective-permute-start(bf16[1152,256]{1,0:T(8,128)(2,1)} %constant_dynamic-slice_fusion.3), channel_id=1, source_target_pairs={{0,2},{1,3},{2,0},{3,1},{4,6},{5,7},{6,4},{7,5},{8,10},{9,11},{10,... | collective-permute-start | bytes 1769480 | tf_op jit(solution)/shard_map/ppermute | solution.py:591
  213.7 98.1 %collective-permute-start.61 = (bf16[1536,768]{1,0:T(8,128)(2,1)S(1)}, bf16[1536,768]{1,0:T(8,128)(2,1)}, u32[]{:S(2)}, u32[]{:S(2)}) collective-permute-start(bf16[1536,768]{1,0:T(8,128)(2,1)S(1)} %constant_dynamic-slice_fusion.4), channel_id=1, source_target_pairs={{0,2},{2,0},{4,6},{6,4},{8,10},{10,8},{12,14},{14,12},{16,18},{18,... | collective-permute-start | bytes 7077896 | tf_op jit(solution)/shard_map/ppermute | solution.py:591
  223.9 85.2 %collective-permute-start.53 = (bf16[2304,512]{1,0:T(8,128)(2,1)}, bf16[2304,512]{1,0:T(8,128)(2,1)S(1)}, u32[]{:S(2)}, u32[]{:S(2)}) collective-permute-start(bf16[2304,512]{1,0:T(8,128)(2,1)} %constant_dynamic-slice_fusion.2), channel_id=1, source_target_pairs={{0,2},{2,0},{4,6},{6,4},{8,10},{10,8},{12,14},{14,12},{16,18},{18,... | collective-permute-start | bytes 7077896 | tf_op jit(solution)/shard_map/ppermute | solution.py:591
  228.1 19.0 %collective-permute-start.44 = (bf16[192,768]{1,0:T(8,128)(2,1)S(1)}, bf16[192,768]{1,0:T(8,128)(2,1)S(1)}, u32[]{:S(2)}, u32[]{:S(2)}) collective-permute-start(bf16[192,768]{1,0:T(8,128)(2,1)S(1)} %get-tuple-element.171), channel_id=1, source_target_pairs={{0,1},{1,0},{2,6},{3,7},{4,5},{5,4},{6,2},{7,3},{8,9},{9,8},{10,14... | collective-permute-start | bytes 884744 | tf_op jit(solution)/shard_map/ppermute | solution.py:591
  235.4 11.8 %collective-permute-start.29 = (bf16[576,256]{1,0:T(8,128)(2,1)S(1)}, bf16[576,256]{1,0:T(8,128)(2,1)S(1)}, u32[]{:S(2)}, u32[]{:S(2)}) collective-permute-start(bf16[576,256]{1,0:T(8,128)(2,1)S(1)} %get-tuple-element.173), channel_id=1, source_target_pairs={{0,1},{1,0},{2,6},{3,7},{4,5},{5,4},{6,2},{7,3},{8,9},{9,8},{10,14... | collective-permute-start | bytes 884744 | tf_op jit(solution)/shard_map/ppermute | solution.py:591
  243.9 8.9 %collective-permute-start.9 = (bf16[576,256]{1,0:T(8,128)(2,1)S(1)}, bf16[576,256]{1,0:T(8,128)(2,1)S(1)}, u32[]{:S(2)}, u32[]{:S(2)}) collective-permute-start(bf16[576,256]{1,0:T(8,128)(2,1)S(1)} %get-tuple-element.177), channel_id=1, source_target_pairs={{0,1},{1,0},{2,6},{3,7},{4,5},{5,4},{6,2},{7,3},{8,9},{9,8},{10,14... | collective-permute-start | bytes 884744 | tf_op jit(solution)/shard_map/ppermute | solution.py:591
  247.1 11.4 %collective-permute-start.19 = (bf16[576,256]{1,0:T(8,128)(2,1)S(1)}, bf16[576,256]{1,0:T(8,128)(2,1)S(1)}, u32[]{:S(2)}, u32[]{:S(2)}) collective-permute-start(bf16[576,256]{1,0:T(8,128)(2,1)S(1)} %get-tuple-element.175), channel_id=1, source_target_pairs={{0,1},{1,0},{2,6},{3,7},{4,5},{5,4},{6,2},{7,3},{8,9},{9,8},{10,14... | collective-permute-start | bytes 884744 | tf_op jit(solution)/shard_map/ppermute | solution.py:591
  247.2 11.7 %collective-permute-start.45 = (bf16[96,768]{1,0:T(8,128)(2,1)S(1)}, bf16[96,768]{1,0:T(8,128)(2,1)S(1)}, u32[]{:S(2)}, u32[]{:S(2)}) collective-permute-start(bf16[96,768]{1,0:T(8,128)(2,1)S(1)} %get-tuple-element.201), channel_id=1, source_target_pairs={{0,8},{1,9},{2,3},{3,2},{4,12},{5,13},{6,7},{7,6},{8,0},{9,1},{10,... | collective-permute-start | bytes 442376 | tf_op jit(solution)/shard_map/ppermute | solution.py:591
  252.7 8.0 %collective-permute-start.30 = (bf16[288,256]{1,0:T(8,128)(2,1)S(1)}, bf16[288,256]{1,0:T(8,128)(2,1)S(1)}, u32[]{:S(2)}, u32[]{:S(2)}) collective-permute-start(bf16[288,256]{1,0:T(8,128)(2,1)S(1)} %get-tuple-element.205), channel_id=1, source_target_pairs={{0,8},{1,9},{2,3},{3,2},{4,12},{5,13},{6,7},{7,6},{8,0},{9,1},{10,... | collective-permute-start | bytes 442376 | tf_op jit(solution)/shard_map/ppermute | solution.py:591
  258.5 5.7 %collective-permute-start.10 = (bf16[288,256]{1,0:T(8,128)(2,1)S(1)}, bf16[288,256]{1,0:T(8,128)(2,1)S(1)}, u32[]{:S(2)}, u32[]{:S(2)}) collective-permute-start(bf16[288,256]{1,0:T(8,128)(2,1)S(1)} %get-tuple-element.213), channel_id=1, source_target_pairs={{0,8},{1,9},{2,3},{3,2},{4,12},{5,13},{6,7},{7,6},{8,0},{9,1},{10,... | collective-permute-start | bytes 442376 | tf_op jit(solution)/shard_map/ppermute | solution.py:591
  258.9 7.3 %collective-permute-start.20 = (bf16[288,256]{1,0:T(8,128)(2,1)S(1)}, bf16[288,256]{1,0:T(8,128)(2,1)S(1)}, u32[]{:S(2)}, u32[]{:S(2)}) collective-permute-start(bf16[288,256]{1,0:T(8,128)(2,1)S(1)} %get-tuple-element.209), channel_id=1, source_target_pairs={{0,8},{1,9},{2,3},{3,2},{4,12},{5,13},{6,7},{7,6},{8,0},{9,1},{10,... | collective-permute-start | bytes 442376 | tf_op jit(solution)/shard_map/ppermute | solution.py:591
  260.7 6.8 %collective-permute-start.46 = (bf16[48,768]{1,0:T(8,128)(2,1)S(1)}, bf16[48,768]{1,0:T(8,128)(2,1)S(1)}, u32[]{:S(2)}, u32[]{:S(2)}) collective-permute-start(bf16[48,768]{1,0:T(8,128)(2,1)S(1)} %get-tuple-element.217), channel_id=1, source_target_pairs={{0,4},{1,5},{2,10},{3,11},{4,0},{5,1},{6,14},{7,15},{8,12},{9,13},... | collective-permute-start | bytes 221192 | tf_op jit(solution)/shard_map/ppermute | solution.py:591
  268.5 6.1 %collective-permute-start.47 = (bf16[24,768]{1,0:T(8,128)(2,1)S(1)}, bf16[24,768]{1,0:T(8,128)(2,1)S(1)}, u32[]{:S(2)}, u32[]{:S(2)}) collective-permute-start(bf16[24,768]{1,0:T(8,128)(2,1)S(1)} %add_convert_fusion.39), channel_id=1, source_target_pairs={{0,16},{1,17},{2,18},{3,19},{4,20},{5,21},{6,22},{7,23},{8,24},{9,... | collective-permute-start | bytes 110600 | tf_op jit(solution)/shard_map/ppermute | solution.py:591
  290.5 6.6 %collective-permute-start.50 = (bf16[96,768]{1,0:T(8,128)(2,1)S(1)}, bf16[96,768]{1,0:T(8,128)(2,1)S(1)}, u32[]{:S(2)}, u32[]{:S(2)}) collective-permute-start(bf16[96,768]{1,0:T(8,128)(2,1)S(1)} %pad_maximum_fusion.21), channel_id=1, source_target_pairs={{0,8},{1,9},{2,3},{3,2},{4,12},{5,13},{6,7},{7,6},{8,0},{9,1},{10,... | collective-permute-start | bytes 442376 | tf_op jit(solution)/shard_map/ppermute | solution.py:591
  292.1 8.2 %collective-permute-start.35 = (bf16[288,256]{1,0:T(8,128)(2,1)S(1)}, bf16[288,256]{1,0:T(8,128)(2,1)S(1)}, u32[]{:S(2)}, u32[]{:S(2)}) collective-permute-start(bf16[288,256]{1,0:T(8,128)(2,1)S(1)} %pad_maximum_fusion.20), channel_id=1, source_target_pairs={{0,8},{1,9},{2,3},{3,2},{4,12},{5,13},{6,7},{7,6},{8,0},{9,1},{10,... | collective-permute-start | bytes 442376 | tf_op jit(solution)/shard_map/ppermute | solution.py:591
  294.1 9.3 %collective-permute-start.15 = (bf16[288,256]{1,0:T(8,128)(2,1)S(1)}, bf16[288,256]{1,0:T(8,128)(2,1)S(1)}, u32[]{:S(2)}, u32[]{:S(2)}) collective-permute-start(bf16[288,256]{1,0:T(8,128)(2,1)S(1)} %pad_maximum_fusion.18), channel_id=1, source_target_pairs={{0,8},{1,9},{2,3},{3,2},{4,12},{5,13},{6,7},{7,6},{8,0},{9,1},{10,... | collective-permute-start | bytes 442376 | tf_op jit(solution)/shard_map/ppermute | solution.py:591
  297.1 9.5 %collective-permute-start.25 = (bf16[288,256]{1,0:T(8,128)(2,1)S(1)}, bf16[288,256]{1,0:T(8,128)(2,1)S(1)}, u32[]{:S(2)}, u32[]{:S(2)}) collective-permute-start(bf16[288,256]{1,0:T(8,128)(2,1)S(1)} %pad_maximum_fusion.19), channel_id=1, source_target_pairs={{0,8},{1,9},{2,3},{3,2},{4,12},{5,13},{6,7},{7,6},{8,0},{9,1},{10,... | collective-permute-start | bytes 442376 | tf_op jit(solution)/shard_map/ppermute | solution.py:591
  300.3 8.3 %collective-permute-start.51 = (bf16[192,768]{1,0:T(8,128)(2,1)S(1)}, bf16[192,768]{1,0:T(8,128)(2,1)S(1)}, u32[]{:S(2)}, u32[]{:S(2)}) collective-permute-start(bf16[192,768]{1,0:T(8,128)(2,1)S(1)} %pad_maximum_fusion.17), channel_id=1, source_target_pairs={{0,1},{1,0},{2,6},{3,7},{4,5},{5,4},{6,2},{7,3},{8,9},{9,8},{10,14... | collective-permute-start | bytes 884744 | tf_op jit(solution)/shard_map/ppermute | solution.py:591
  303.5 8.1 %collective-permute-start.36 = (bf16[576,256]{1,0:T(8,128)(2,1)S(1)}, bf16[576,256]{1,0:T(8,128)(2,1)S(1)}, u32[]{:S(2)}, u32[]{:S(2)}) collective-permute-start(bf16[576,256]{1,0:T(8,128)(2,1)S(1)} %pad_maximum_fusion.16), channel_id=1, source_target_pairs={{0,1},{1,0},{2,6},{3,7},{4,5},{5,4},{6,2},{7,3},{8,9},{9,8},{10,14... | collective-permute-start | bytes 884744 | tf_op jit(solution)/shard_map/ppermute | solution.py:591
  306.6 8.3 %collective-permute-start.16 = (bf16[576,256]{1,0:T(8,128)(2,1)S(1)}, bf16[576,256]{1,0:T(8,128)(2,1)S(1)}, u32[]{:S(2)}, u32[]{:S(2)}) collective-permute-start(bf16[576,256]{1,0:T(8,128)(2,1)S(1)} %pad_maximum_fusion.14), channel_id=1, source_target_pairs={{0,1},{1,0},{2,6},{3,7},{4,5},{5,4},{6,2},{7,3},{8,9},{9,8},{10,14... | collective-permute-start | bytes 884744 | tf_op jit(solution)/shard_map/ppermute | solution.py:591
  308.6 17.9 %collective-permute-start.26 = (bf16[576,256]{1,0:T(8,128)(2,1)S(1)}, bf16[576,256]{1,0:T(8,128)(2,1)S(1)}, u32[]{:S(2)}, u32[]{:S(2)}) collective-permute-start(bf16[576,256]{1,0:T(8,128)(2,1)S(1)} %pad_maximum_fusion.15), channel_id=1, source_target_pairs={{0,1},{1,0},{2,6},{3,7},{4,5},{5,4},{6,2},{7,3},{8,9},{9,8},{10,14... | collective-permute-start | bytes 884744 | tf_op jit(solution)/shard_map/ppermute | solution.py:591
  310.0 16.3 %collective-permute-start.54 = (bf16[1152,512]{1,0:T(8,128)(2,1)S(1)}, bf16[1152,512]{1,0:T(8,128)(2,1)S(1)}, u32[]{:S(2)}, u32[]{:S(2)}) collective-permute-start(bf16[1152,512]{1,0:T(8,128)(2,1)S(1)} %get-tuple-element.157), channel_id=1, source_target_pairs={{0,4},{2,10},{4,0},{6,14},{8,12},{10,2},{12,8},{14,6},{16,20},{18,... | collective-permute-start | bytes 3538952 | tf_op jit(solution)/shard_map/ppermute | solution.py:591
  311.5 131.7 %collective-permute-start.52 = (bf16[384,768]{1,0:T(8,128)(2,1)S(1)}, bf16[384,768]{1,0:T(8,128)(2,1)S(1)}, u32[]{:S(2)}, u32[]{:S(2)}) collective-permute-start(bf16[384,768]{1,0:T(8,128)(2,1)S(1)} %pad_maximum_fusion.8), channel_id=1, source_target_pairs={{0,2},{1,3},{2,0},{3,1},{4,6},{5,7},{6,4},{7,5},{8,10},{9,11},{10,... | collective-permute-start | bytes 1769480 | tf_op jit(solution)/shard_map/ppermute | solution.py:591
  314.2 31.0 %collective-permute-start.62 = (bf16[768,768]{1,0:T(8,128)(2,1)S(1)}, bf16[768,768]{1,0:T(8,128)(2,1)S(1)}, u32[]{:S(2)}, u32[]{:S(2)}) collective-permute-start(bf16[768,768]{1,0:T(8,128)(2,1)S(1)} %get-tuple-element.155), channel_id=1, source_target_pairs={{0,4},{2,10},{4,0},{6,14},{8,12},{10,2},{12,8},{14,6},{16,20},{18,... | collective-permute-start | bytes 3538952 | tf_op jit(solution)/shard_map/ppermute | solution.py:591
  314.9 95.6 %collective-permute-start.37 = (bf16[1152,256]{1,0:T(8,128)(2,1)S(1)}, bf16[1152,256]{1,0:T(8,128)(2,1)S(1)}, u32[]{:S(2)}, u32[]{:S(2)}) collective-permute-start(bf16[1152,256]{1,0:T(8,128)(2,1)S(1)} %pad_maximum_fusion.7), channel_id=1, source_target_pairs={{0,2},{1,3},{2,0},{3,1},{4,6},{5,7},{6,4},{7,5},{8,10},{9,11},{10,... | collective-permute-start | bytes 1769480 | tf_op jit(solution)/shard_map/ppermute | solution.py:591
  326.2 20.6 %collective-permute-start.17 = (bf16[1152,256]{1,0:T(8,128)(2,1)S(1)}, bf16[1152,256]{1,0:T(8,128)(2,1)S(1)}, u32[]{:S(2)}, u32[]{:S(2)}) collective-permute-start(bf16[1152,256]{1,0:T(8,128)(2,1)S(1)} %pad_maximum_fusion.5), channel_id=1, source_target_pairs={{0,2},{1,3},{2,0},{3,1},{4,6},{5,7},{6,4},{7,5},{8,10},{9,11},{10,... | collective-permute-start | bytes 1769480 | tf_op jit(solution)/shard_map/ppermute | solution.py:591
  326.6 18.9 %collective-permute-start.55 = (bf16[576,512]{1,0:T(8,128)(2,1)S(1)}, bf16[576,512]{1,0:T(8,128)(2,1)S(1)}, u32[]{:S(2)}, u32[]{:S(2)}) collective-permute-start(bf16[576,512]{1,0:T(8,128)(2,1)S(1)} %get-tuple-element.169), channel_id=1, source_target_pairs={{0,16},{2,6},{4,20},{6,2},{8,24},{10,14},{12,28},{14,10},{16,0},{1... | collective-permute-start | bytes 1769480 | tf_op jit(solution)/shard_map/ppermute | solution.py:591
  345.2 35.4 %collective-permute-start.27 = (bf16[1152,256]{1,0:T(8,128)(2,1)S(1)}, bf16[1152,256]{1,0:T(8,128)(2,1)S(1)}, u32[]{:S(2)}, u32[]{:S(2)}) collective-permute-start(bf16[1152,256]{1,0:T(8,128)(2,1)S(1)} %pad_maximum_fusion.6), channel_id=1, source_target_pairs={{0,2},{1,3},{2,0},{3,1},{4,6},{5,7},{6,4},{7,5},{8,10},{9,11},{10,... | collective-permute-start | bytes 1769480 | tf_op jit(solution)/shard_map/ppermute | solution.py:591
  345.5 32.8 %collective-permute-start.63 = (bf16[384,768]{1,0:T(8,128)(2,1)S(1)}, bf16[384,768]{1,0:T(8,128)(2,1)S(1)}, u32[]{:S(2)}, u32[]{:S(2)}) collective-permute-start(bf16[384,768]{1,0:T(8,128)(2,1)S(1)} %get-tuple-element.165), channel_id=1, source_target_pairs={{0,16},{2,6},{4,20},{6,2},{8,24},{10,14},{12,28},{14,10},{16,0},{1... | collective-permute-start | bytes 1769480 | tf_op jit(solution)/shard_map/ppermute | solution.py:591
  346.8 31.6 %collective-permute-start.56 = (bf16[288,512]{1,0:T(8,128)(2,1)S(1)}, bf16[288,512]{1,0:T(8,128)(2,1)S(1)}, u32[]{:S(2)}, u32[]{:S(2)}) collective-permute-start(bf16[288,512]{1,0:T(8,128)(2,1)S(1)} %add_convert_fusion.12), channel_id=1, source_target_pairs={{0,8},{2,18},{4,12},{6,22},{8,0},{10,26},{12,4},{14,30},{16,24},{1... | collective-permute-start | bytes 884744 | tf_op jit(solution)/shard_map/ppermute | solution.py:591
  378.3 9.9 %collective-permute-start.64 = (bf16[192,768]{1,0:T(8,128)(2,1)S(1)}, bf16[192,768]{1,0:T(8,128)(2,1)S(1)}, u32[]{:S(2)}, u32[]{:S(2)}) collective-permute-start(bf16[192,768]{1,0:T(8,128)(2,1)S(1)} %add_convert_fusion.9), channel_id=1, source_target_pairs={{0,8},{2,18},{4,12},{6,22},{8,0},{10,26},{12,4},{14,30},{16,24},{1... | collective-permute-start | bytes 884744 | tf_op jit(solution)/shard_map/ppermute | solution.py:591
  378.5 12.9 %collective-permute-start.57 = (bf16[288,512]{1,0:T(8,128)(2,1)S(1)}, bf16[288,512]{1,0:T(8,128)(2,1)S(1)}, u32[]{:S(2)}, u32[]{:S(2)}) collective-permute-start(bf16[288,512]{1,0:T(8,128)(2,1)S(1)} %add_convert_fusion.11), channel_id=1, source_target_pairs={{0,8},{2,18},{4,12},{6,22},{8,0},{10,26},{12,4},{14,30},{16,24},{1... | collective-permute-start | bytes 884744 | tf_op jit(solution)/shard_map/ppermute | solution.py:591
  388.4 9.2 %collective-permute-start.65 = (bf16[192,768]{1,0:T(8,128)(2,1)S(1)}, bf16[192,768]{1,0:T(8,128)(2,1)S(1)}, u32[]{:S(2)}, u32[]{:S(2)}) collective-permute-start(bf16[192,768]{1,0:T(8,128)(2,1)S(1)} %add_convert_fusion.8), channel_id=1, source_target_pairs={{0,8},{2,18},{4,12},{6,22},{8,0},{10,26},{12,4},{14,30},{16,24},{1... | collective-permute-start | bytes 884744 | tf_op jit(solution)/shard_map/ppermute | solution.py:591
  391.5 16.9 %collective-permute-start.58 = (bf16[576,512]{1,0:T(8,128)(2,1)S(1)}, bf16[576,512]{1,0:T(8,128)(2,1)S(1)}, u32[]{:S(2)}, u32[]{:S(2)}) collective-permute-start(bf16[576,512]{1,0:T(8,128)(2,1)S(1)} %pad_maximum_fusion.9), channel_id=1, source_target_pairs={{0,16},{2,6},{4,20},{6,2},{8,24},{10,14},{12,28},{14,10},{16,0},{1... | collective-permute-start | bytes 1769480 | tf_op jit(solution)/shard_map/ppermute | solution.py:591
  397.7 23.4 %collective-permute-start.66 = (bf16[384,768]{1,0:T(8,128)(2,1)S(1)}, bf16[384,768]{1,0:T(8,128)(2,1)S(1)}, u32[]{:S(2)}, u32[]{:S(2)}) collective-permute-start(bf16[384,768]{1,0:T(8,128)(2,1)S(1)} %pad_maximum_fusion.10), channel_id=1, source_target_pairs={{0,16},{2,6},{4,20},{6,2},{8,24},{10,14},{12,28},{14,10},{16,0},{1... | collective-permute-start | bytes 1769480 | tf_op jit(solution)/shard_map/ppermute | solution.py:591
  408.8 16.3 %collective-permute-start.59 = (bf16[1152,512]{1,0:T(8,128)(2,1)S(1)}, bf16[1152,512]{1,0:T(8,128)(2,1)S(1)}, u32[]{:S(2)}, u32[]{:S(2)}) collective-permute-start(bf16[1152,512]{1,0:T(8,128)(2,1)S(1)} %pad_maximum_fusion.3), channel_id=1, source_target_pairs={{0,4},{2,10},{4,0},{6,14},{8,12},{10,2},{12,8},{14,6},{16,20},{18,... | collective-permute-start | bytes 3538952 | tf_op jit(solution)/shard_map/ppermute | solution.py:591
  421.4 16.3 %collective-permute-start.67 = (bf16[768,768]{1,0:T(8,128)(2,1)S(1)}, bf16[768,768]{1,0:T(8,128)(2,1)S(1)}, u32[]{:S(2)}, u32[]{:S(2)}) collective-permute-start(bf16[768,768]{1,0:T(8,128)(2,1)S(1)} %pad_maximum_fusion.4), channel_id=1, source_target_pairs={{0,4},{2,10},{4,0},{6,14},{8,12},{10,2},{12,8},{14,6},{16,20},{18,... | collective-permute-start | bytes 3538952 | tf_op jit(solution)/shard_map/ppermute | solution.py:591
  425.7 19.4 %collective-permute-start.60 = (bf16[2304,512]{1,0:T(8,128)(2,1)S(1)}, bf16[2304,512]{1,0:T(8,128)(2,1)S(1)}, u32[]{:S(2)}, u32[]{:S(2)}) collective-permute-start(bf16[2304,512]{1,0:T(8,128)(2,1)S(1)} %pad_maximum_fusion.1), channel_id=1, source_target_pairs={{0,2},{2,0},{4,6},{6,4},{8,10},{10,8},{12,14},{14,12},{16,18},{18,... | collective-permute-start | bytes 7077896 | tf_op jit(solution)/shard_map/ppermute | solution.py:591
  439.7 25.9 %collective-permute-start.68 = (bf16[1536,768]{1,0:T(8,128)(2,1)}, bf16[1536,768]{1,0:T(8,128)(2,1)}, u32[]{:S(2)}, u32[]{:S(2)}) collective-permute-start(bf16[1536,768]{1,0:T(8,128)(2,1)} %pad_maximum_fusion.2), channel_id=1, source_target_pairs={{0,2},{2,0},{4,6},{6,4},{8,10},{10,8},{12,14},{14,12},{16,18},{18,... | collective-permute-start | bytes 7077896 | tf_op jit(solution)/shard_map/ppermute | solution.py:591
  (43 other events, 444.7 us)

commit v2 on v1

v2 whole, which is shorter than its diff:
```python
import functools

import jax
import jax.numpy as jnp
from jax import lax
from jax.experimental import pallas as pl
from jax.experimental.pallas import tpu as pltpu
from jax.sharding import PartitionSpec as P

HEADS = 12
HEAD = 64
IMG_PAD = 256
PAIR = 2 * HEAD
PAIRS = HEADS // 2
GROUP_PAIRS = 2
GROUPS = PAIRS // GROUP_PAIRS
LANES = GROUP_PAIRS * PAIR
FF_BLOCK = 768

masked_value = -1e30
norm_eps = 1e-05

bf16 = jnp.bfloat16
f32 = jnp.float32

NN = (((1,), (0,)), ((), ()))
NT = (((1,), (1,)), ((), ()))
TN = (((0,), (0,)), ((), ()))
VMEM_BYTES = 56 << 20


def dot(left, right, dims=NN):
    return lax.dot_general(left, right, dims, preferred_element_type=f32)


def column_sum(values):
    return jnp.sum(values, axis=0, keepdims=True)


def row_mean(values):
    return jnp.mean(values, axis=1, keepdims=True)


def normalise(values):
    centred = values - row_mean(values)
    scale = lax.rsqrt(row_mean(centred * centred) + norm_eps)
    return centred * scale, scale


def norm_transpose(unit, scale, gain, grad):
    grad_unit = grad * gain
    return scale * (grad_unit - row_mean(grad_unit) - unit * row_mean(grad_unit * unit))


def cost(flops, moved, special=0):
    del flops, moved, special
    return pl.CostEstimate(flops=1, bytes_accessed=1, transcendentals=0)


class Order:
    def __init__(self):
        self.zero = None

    def tie(self, value):
        value, self.zero = lax.optimization_barrier((value, self.zero))
        return value


def call(order, kernel, inputs, out_shape, name, estimate, scalars=(), grid=(), specs=None, outs=None,
         scratch=(), aliases=None):
    tokens = () if order.zero is None else (order.zero,)
    count = len(scalars) + len(inputs)
    unused = len(tokens)
    vmem = pl.BlockSpec(memory_space=pltpu.VMEM)
    given = len(out_shape)
    end = count + unused + given

    def body(*refs):
        refs[end][0, 0] = 0
        kernel(*refs[:count], *refs[count + unused : end], *refs[end + 1 :])

    specs = [vmem] * len(inputs) if specs is None else list(specs)
    outs = [vmem] * given if outs is None else list(outs)
    *found, order.zero = pl.pallas_call(
        body,
        grid_spec=pltpu.PrefetchScalarGridSpec(
            num_scalar_prefetch=len(scalars),
            grid=grid,
            in_specs=specs + [pl.BlockSpec(memory_space=pl.ANY)] * unused,
            out_specs=outs + [pl.BlockSpec(memory_space=pltpu.SMEM)],
            scratch_shapes=list(scratch),
        ),
        out_shape=list(out_shape) + [jax.ShapeDtypeStruct((1, 1), jnp.int32)],
        input_output_aliases=aliases or {},
        compiler_params=pltpu.CompilerParams(vmem_limit_bytes=VMEM_BYTES),
        cost_estimate=estimate,
        name=name,
    )(*scalars, *inputs, *tokens)
    return found if given > 1 else found[0]


def shaped(shape, dtype):
    return jax.ShapeDtypeStruct(shape, dtype)


def resident(shape):
    return pl.BlockSpec(shape, lambda *_: (0,) * len(shape), pipeline_mode=pl.Buffered(1))


def project_kernel(hid_ref, gain_ref, shift_ref, weight_ref, bias_ref, normed_ref, out_ref):
    unit, _ = normalise(hid_ref[...].astype(f32))
    normed = (unit * gain_ref[...] + shift_ref[...]).astype(bf16)
    normed_ref[...] = normed
    width = normed.shape[1]
    for part in range(3):
        cols = slice(part * width, (part + 1) * width)
        rows = dot(normed, weight_ref[:, cols])
        if part == 0:
            rows = (rows + bias_ref[0:1]).astype(bf16) * jnp.asarray(HEAD**-0.5, bf16)
        if part == 2:
            rows = rows + bias_ref[1:2]
        out_ref[:, cols] = rows.astype(bf16)


def project_rows(order, hidden, gain, shift, weight, bias):
    rows, width = hidden.shape
    block = 256
    blocked = lambda cols: pl.BlockSpec((block, cols), lambda r: (r, 0))
    inputs = (hidden, gain, shift, weight, bias)
    return call(
        order,
        project_kernel,
        inputs,
        [shaped((rows, width), bf16), shaped((rows, 3 * width), bf16)],
        "project_rows",
        cost(6 * rows * width * width, 10 * rows * width + 6 * width * width),
        grid=(rows // block,),
        specs=[blocked(width)] + [resident(value.shape) for value in inputs[1:]],
        outs=[blocked(width), blocked(3 * width)],
    )


def image_kernel(
    flag_ref,
    own_ref,
    far_ref,
    gain_ref,
    shift_ref,
    vec_ref,
    keys_ref,
    values_ref,
    bias_ref,
    normed_ref,
    out_ref,
):
    is_text = flag_ref[0] == 1
    hidden = jnp.where(is_text, far_ref[...].astype(f32), own_ref[...].astype(f32))
    gain = jnp.where(is_text, vec_ref[0:1], gain_ref[...])
    shift = jnp.where(is_text, vec_ref[1:2], shift_ref[...])
    unit, _ = normalise(hidden)
    normed = (unit * gain + shift).astype(bf16)
    normed_ref[...] = normed
    width = normed.shape[1]
    out_ref[:, :width] = dot(normed, keys_ref[...]).astype(bf16)
    out_ref[:, width:] = (dot(normed, values_ref[...]) + bias_ref[1:2]).astype(bf16)


def image_rows(order, flag, item, hidden, far, gain, shift, vecs, weight, bias, item_rows):
    width = hidden.shape[1]
    place = item * (item_rows // IMG_PAD)
    half = lambda base: pl.BlockSpec((width, width), lambda *_: (0, base))
    return call(
        order,
        image_kernel,
        (hidden, far, gain, shift, vecs, weight, weight, bias),
        [shaped((IMG_PAD, width), bf16), shaped((IMG_PAD, 2 * width), bf16)],
        "image_rows",
        cost(4 * IMG_PAD * width * width, 6 << 20),
        scalars=(flag,),
        grid=(1,),
        specs=[
            pl.BlockSpec((IMG_PAD, width), lambda *_: (place, 0)),
            resident(far.shape),
            resident(gain.shape),
            resident(shift.shape),
            resident(vecs.shape),
            half(1),
            half(2),
            resident(bias.shape),
        ],
        outs=[resident((IMG_PAD, width)), resident((IMG_PAD, 2 * width))],
    )


def segments(shape, axis, lengths_ref, item):
    places = lax.broadcasted_iota(jnp.int32, shape, axis)
    total = jnp.zeros(shape, jnp.int32)
    end = 0
    for which in range(lengths_ref.shape[1]):
        end = end + lengths_ref[item, which]
        total += (places >= end).astype(jnp.int32)
    return total


def own_bias(rows, flag_ref, lengths_ref, item):
    shape = (rows, rows)
    same = segments(shape, 0, lengths_ref, item) == segments(shape, 1, lengths_ref, item)
    return jnp.where(same & (flag_ref[0] == 1), 0.0, masked_value).astype(f32)


def image_bias(shape, axis, count_ref, item):
    places = lax.broadcasted_iota(jnp.int32, shape, axis)
    return jnp.where(places < count_ref[item], 0.0, masked_value).astype(f32)


def forward_kernel(
    item,
    flag_ref,
    count_ref,
    lengths_ref,
    q_ref,
    k_ref,
    v_ref,
    ik_ref,
    iv_ref,
    out_ref,
    lse_ref,
    image_part,
    own_part,
):
    rows = q_ref.shape[0]

    @pl.when(pl.program_id(0) == 0)
    def _():
        image_part[...] = image_bias(image_part.shape, 1, count_ref, item)
        own_part[...] = own_bias(rows, flag_ref, lengths_ref, item)

    first = lax.broadcasted_iota(jnp.int32, (rows, PAIR), 1) < HEAD
    zero = jnp.zeros((), bf16)
    q = q_ref[...]
    image_keys, image_values = ik_ref[...], iv_ref[...]
    keys, values = k_ref[...], v_ref[...]
    outs, tops = [], []
    for head in range(2):
        q_head = jnp.where(first, q, zero) if head == 0 else jnp.where(first, zero, q)
        far = dot(q_head, image_keys, NT) + image_part[...]
        own = dot(q_head, keys, NT) + own_part[...]
        top = jnp.maximum(
            jnp.max(far, axis=1, keepdims=True), jnp.max(own, axis=1, keepdims=True)
        )
        far = jnp.exp(far - top)
        own = jnp.exp(own - top)
        total = jnp.sum(far, axis=1, keepdims=True) + jnp.sum(own, axis=1, keepdims=True)
        summed = dot(far.astype(bf16), image_values) + dot(own.astype(bf16), values)
        outs.append(summed / total)
        tops.append(top + jnp.log(total))
    out_ref[...] = jnp.where(first, outs[0], outs[1]).astype(bf16)
    turned = jnp.transpose(jnp.where(first, tops[0], tops[1]))
    lse_ref[0, 0:1, :] = turned[0:1]
    lse_ref[0, 1:2, :] = turned[HEAD : HEAD + 1]


def attend_forward(order, scalars, item, projected, image):
    rows = projected.shape[0] // 2
    spec = lambda base: pl.BlockSpec((rows, PAIR), lambda h, *_: (item, base + h))
    far = lambda base: pl.BlockSpec((IMG_PAD, PAIR), lambda h, *_: (0, base + h))
    keys = rows + IMG_PAD
    return call(
        order,
        functools.partial(forward_kernel, item),
        (projected, projected, projected, image, image),
        [shaped((rows, HEADS * HEAD), bf16), shaped((PAIRS, 2, rows), f32)],
        "attend_forward",
        cost(16 * HEADS * rows * keys * HEAD, 6 << 20, HEADS * rows * keys),
        scalars=scalars,
        grid=(PAIRS,),
        specs=[spec(0), spec(PAIRS), spec(2 * PAIRS), far(0), far(PAIRS)],
        outs=[
            pl.BlockSpec((rows, PAIR), lambda h, *_: (0, h)),
            pl.BlockSpec((1, 2, rows), lambda h, *_: (h, 0, 0)),
        ],
        scratch=[pltpu.VMEM((rows, IMG_PAD), f32), pltpu.VMEM((rows, rows), f32)],
    )


def backward_kernel(
    item,
    flag_ref,
    count_ref,
    lengths_ref,
    q_ref,
    k_ref,
    v_ref,
    ik_ref,
    iv_ref,
    out_ref,
    grad_ref,
    lse_ref,
    *refs,
):
    gq_ref, gk_ref, gv_ref, gik_ref, giv_ref, image_part, own_part = refs[-7:]
    rows = q_ref.shape[0]

    @pl.when(pl.program_id(0) == 0)
    def _():
        image_part[...] = image_bias(image_part.shape, 0, count_ref, item)
        own_part[...] = own_bias(rows, flag_ref, lengths_ref, item)

    first = lax.broadcasted_iota(jnp.int32, (rows, PAIR), 1) < HEAD
    zero = jnp.zeros((), bf16)
    q, grad = q_ref[...], grad_ref[...]
    products = grad.astype(f32) * out_ref[...].astype(f32)
    head_lanes = lax.broadcasted_iota(jnp.int32, (8, PAIR), 1) // HEAD
    head_rows = lax.broadcasted_iota(jnp.int32, (8, PAIR), 0)
    center = lax.dot_general(
        (head_lanes == head_rows).astype(f32),
        products,
        NT,
        preferred_element_type=f32,
        precision=lax.Precision.HIGHEST,
    )
    q_heads = [jnp.where(first, q, zero), jnp.where(first, zero, q)]
    grad_heads = [jnp.where(first, grad, zero), jnp.where(first, zero, grad)]
    lse = lse_ref[0]
    grad_query = [None, None]
    half = rows // 2
    pieces = (
        (ik_ref, iv_ref, gik_ref, giv_ref, image_part, 0, IMG_PAD),
        (k_ref, v_ref, gk_ref, gv_ref, own_part, 0, half),
        (k_ref, v_ref, gk_ref, gv_ref, own_part, half, half),
    )
    for keys_ref, values_ref, gk_out, gv_out, bias, start, count in pieces:
        piece = slice(start, start + count)
        keys, values = keys_ref[piece, :], values_ref[piece, :]
        low_lanes = lax.broadcasted_iota(jnp.int32, (count, PAIR), 1) < HEAD
        grad_keys, grad_values = [], []
        for head in range(2):
            scores = dot(keys, q_heads[head], NT) + bias[piece, :]
            probs = jnp.exp(scores - lse[head : head + 1])
            grad_probs = dot(values, grad_heads[head], NT)
            grad_scores = (probs * (grad_probs - center[head : head + 1])).astype(bf16)
            grad_values.append(dot(probs.astype(bf16), grad))
            grad_keys.append(dot(grad_scores, q))
            term = dot(grad_scores, keys, TN)
            grad_query[head] = term if grad_query[head] is None else grad_query[head] + term
        gk_out[piece, :] = jnp.where(low_lanes, grad_keys[0], grad_keys[1]).astype(bf16)
        gv_out[piece, :] = jnp.where(low_lanes, grad_values[0], grad_values[1]).astype(bf16)
    gq_ref[...] = (jnp.where(first, grad_query[0], grad_query[1]) * HEAD**-0.5).astype(bf16)


def attend_backward(order, scalars, item, start, pairs, projected, image, attended, grad, lse, earlier):
    rows, width = attended.shape
    spec = lambda base: pl.BlockSpec((rows, PAIR), lambda h, *_: (item, base + start + h))
    far = lambda base: pl.BlockSpec((IMG_PAD, PAIR), lambda h, *_: (0, base + start + h))
    own = pl.BlockSpec((rows, PAIR), lambda h, *_: (0, start + h))
    far_outs = pl.BlockSpec((IMG_PAD, PAIR), lambda h, *_: (item, start + h))
    keys = rows + IMG_PAD
    inputs = (projected, projected, projected, image, image, attended, grad, lse)
    first = len(scalars) + len(inputs)
    return call(
        order,
        functools.partial(backward_kernel, item),
        (*inputs, *earlier),
        [shaped((2 * rows, width), bf16)] * 3 + [shaped((2 * IMG_PAD, width), bf16)] * 2,
        "attend_backward",
        cost(80 * pairs * rows * keys * HEAD, pairs * 2 << 20, 2 * pairs * rows * keys),
        scalars=scalars,
        grid=(pairs,),
        specs=[
            spec(0),
            spec(PAIRS),
            spec(2 * PAIRS),
            far(0),
            far(PAIRS),
            own,
            spec(0),
            pl.BlockSpec((1, 2, rows), lambda h, *_: (start + h, 0, 0)),
        ]
        + [pl.BlockSpec(memory_space=pl.ANY)] * len(earlier),
        outs=[spec(0), spec(0), spec(0), far_outs, far_outs],
        scratch=[pltpu.VMEM((IMG_PAD, rows), f32), pltpu.VMEM((rows, rows), f32)],
        aliases={first + at: at for at in range(len(earlier))},
    )


def gelu_pair(values):
    share = 0.5 * (1.0 + lax.erf(values * 0.7071067811865476))
    slope = share + values * jnp.exp(-0.5 * values * values) * 0.3989422804014327
    return values * share, slope


def feed_step(step, rows, item_rows, feed, top, result, gfeed, expand_ref, ebias_ref, reduce_ref):
    width = feed.shape[1]
    expand, reduce = expand_ref[...], reduce_ref[...]
    active_parts, gup_parts = [], []
    for start in range(0, rows, item_rows):
        here = slice(start, start + item_rows)
        upward = dot(feed[here, :], expand) + ebias_ref[...]
        gactive = dot(top[here, :], reduce, NT)
        active, slope = gelu_pair(upward)
        active = active.astype(bf16)
        gup = (gactive * slope).astype(bf16)
        result[here, :] += dot(active, reduce)
        gfeed[here, :] += dot(gup, expand, NT)
        active_parts.append(active)
        gup_parts.append(gup)
    active = jnp.concatenate(active_parts, axis=0)
    gup = jnp.concatenate(gup_parts, axis=0)
    greduce = dot(active, top[...], TN).astype(bf16)
    gexpand = dot(feed[...], gup, TN).astype(bf16)
    pieces = [greduce[:, at : at + LANES] for at in range(0, width, LANES)]
    pieces += [gexpand[:, at : at + LANES] for at in range(0, FF_BLOCK, LANES)]
    return pieces, column_sum(gup.astype(f32))


def store_pieces(out, pieces):
    at = 0
    for half in range(2):
        for piece in pieces:
            rows = piece.shape[0] // 2
            out[at : at + rows, :] = piece[half * rows : (half + 1) * rows]
            at += rows


def feed_kernel(
    flag_ref,
    count_ref,
    side_ref,
    att0_ref,
    att1_ref,
    project_ref,
    hid_ref,
    cot_ref,
    project_bias_ref,
    gain_ref,
    shift_ref,
    reduce_bias_ref,
    expand_ref,
    ebias_ref,
    reduce_ref,
    out_ref,
    gmid_ref,
    gatt_ref,
    gproject_ref,
    gvec_ref,
    gebias_ref,
    keep0_ref,
    send0_ref,
    keep1_ref,
    send1_ref,
    middle,
    feed,
    top,
    result,
    gfeed,
    low_out,
    gatt,
    grads,
    grad_sems,
    row_sems,
    *,
    item_rows,
):
    step = pl.program_id(0)
    rows, width = hid_ref.shape
    block = 256
    att_refs = (att0_ref, att1_ref)
    half = grads.shape[1] // 2

    steps = grads.shape[0]

    def grad_copies(which):
        found = []
        chunk, place = divmod(which, steps // 2)
        outs = (keep1_ref, send1_ref) if chunk else (keep0_ref, send0_ref)
        for number, out in enumerate(outs):
            side = side_ref[0] if number == 0 else 1 - side_ref[0]
            here = grads.at[which, pl.ds(pl.multiple_of(side * half, half), half)]
            there = out.at[pl.ds(place * half, half)]
            found.append(pltpu.make_async_copy(here, there, grad_sems.at[which, number]))
        return found

    @pl.when(step == 0)
    def _():
        for start in range(0, rows, block):
            here = slice(start, start + block)
            inside = slice(start % item_rows, start % item_rows + block)
            att = att_refs[start // item_rows][inside, :]
            branch = dot(att, project_ref[...]) + project_bias_ref[...]
            x = hid_ref[here, :].astype(f32) + branch
            middle[here, :] = x
            unit, _ = normalise(x)
            feed[here, :] = (unit * gain_ref[...] + shift_ref[...]).astype(bf16)
            at = lax.broadcasted_iota(jnp.int32, (block, width), 0) + start % item_rows
            limit = jnp.where(flag_ref[0] == 1, item_rows, count_ref[start // item_rows])
            top[here, :] = jnp.where(at < limit, cot_ref[here, :].astype(f32), 0.0).astype(bf16)
            result[here, :] = x + reduce_bias_ref[...]
            gfeed[here, :] = jnp.zeros((block, width), f32)

    pieces, gebias_ref[...] = feed_step(
        step, rows, item_rows, feed, top, result, gfeed, expand_ref, ebias_ref, reduce_ref
    )
    store_pieces(grads.at[step], pieces)
    for which in range(steps):

        @pl.when(step == which)
        def _(which=which):
            for copy in grad_copies(which):
                copy.start()

    @pl.when(step == pl.num_programs(0) - 1)
    def _():
        copies = []
        sums = [jnp.zeros((1, width), f32)] * 4
        for number, start in enumerate(range(0, rows, block)):
            here = slice(start, start + block)
            low_out[here, :] = result[here, :].astype(bf16)
            unit, scale = normalise(middle[here, :])
            grad = gfeed[here, :]
            grad_top = top[here, :].astype(f32)
            gmid = grad_top + norm_transpose(unit, scale, gain_ref[...], grad)
            terms = (grad * unit, grad, grad_top, gmid)
            sums = [old + column_sum(new) for old, new in zip(sums, terms)]
            middle[here, :] = gmid
            gbranch = gmid.astype(bf16)
            feed[here, :] = gbranch
            gatt[here, :] = dot(gbranch, project_ref[...], NT).astype(bf16)
            for kind, (mine, there) in enumerate(
                ((low_out, out_ref), (middle, gmid_ref), (gatt, gatt_ref))
            ):
                span = pl.ds(start, block)
                copy = pltpu.make_async_copy(
                    mine.at[span, :], there.at[span, :], row_sems.at[kind, number]
                )
                copy.start()
                copies.append(copy)
        total = dot(att0_ref[...], feed[:item_rows, :], TN)
        total += dot(att1_ref[...], feed[item_rows:, :], TN)
        gproject_ref[...] = total.astype(bf16)
        gvec_ref[...] = jnp.concatenate(sums + [jnp.zeros((4, width), f32)], axis=0)
        for copy in copies:
            copy.wait()
        for which in range(steps):
            for copy in grad_copies(which):
                copy.wait()


def feed_forward(order, flag, count, side, att0, att1, project, hidden, cotangent, vecs, expand, ebias, reduce):
    rows, width = hidden.shape
    item_rows = att0.shape[0]
    units = reduce.shape[0]
    steps = units // FF_BLOCK
    block_rows = 2 * width * FF_BLOCK // LANES
    fixed = (att0, att1, project, hidden, cotangent, *vecs)
    anywhere = pl.BlockSpec(memory_space=pl.ANY)
    return call(
        order,
        functools.partial(feed_kernel, item_rows=item_rows),
        (*fixed, expand, ebias, reduce),
        [
            shaped((rows, width), bf16),
            shaped((rows, width), f32),
            shaped((rows, width), bf16),
            shaped((width, width), bf16),
            shaped((8, width), f32),
            shaped((1, units), f32),
        ]
        + [shaped((steps // 2 * block_rows // 2, LANES), bf16)] * 4,
        "feed_forward",
        cost(12 * rows * width * units, 40 << 20, 2 * rows * units),
        scalars=(flag, count, side),
        grid=(steps,),
        specs=[resident(value.shape) for value in fixed]
        + [
            pl.BlockSpec((width, FF_BLOCK), lambda j, *_: (0, j)),
            pl.BlockSpec((1, FF_BLOCK), lambda j, *_: (0, j)),
            pl.BlockSpec((FF_BLOCK, width), lambda j, *_: (j, 0)),
        ],
        outs=[
            anywhere,
            anywhere,
            anywhere,
            resident((width, width)),
            resident((8, width)),
            pl.BlockSpec((1, FF_BLOCK), lambda j, *_: (0, j)),
        ]
        + [anywhere] * 4,
        scratch=[
            pltpu.VMEM((rows, width), f32),
            pltpu.VMEM((rows, width), bf16),
            pltpu.VMEM((rows, width), bf16),
            pltpu.VMEM((rows, width), f32),
            pltpu.VMEM((rows, width), f32),
            pltpu.VMEM((rows, width), bf16),
            pltpu.VMEM((rows, width), bf16),
            pltpu.VMEM((steps, block_rows, LANES), bf16),
            pltpu.SemaphoreType.DMA((steps, 2)),
            pltpu.SemaphoreType.DMA((3, rows // 256)),
        ],
    )


def weight_kernel(
    side_ref,
    normed_ref,
    image_ref,
    gq_ref,
    gk_ref,
    gv_ref,
    gik_ref,
    giv_ref,
    extra_ref,
    keep_ref,
    send_ref,
    query_ref,
    value_ref,
    turned,
    image_turned,
):
    step = pl.program_id(0)
    kinds = pl.num_programs(0) // 4
    part = step // kinds

    @pl.when(step == 0)
    def _():
        turned[...] = jnp.transpose(normed_ref[...].astype(f32)).astype(bf16)
        image_turned[...] = jnp.transpose(image_ref[...].astype(f32)).astype(bf16)

    def store(total):
        half = total.shape[0] // 2
        upper, lower = total[:half], total[half:]
        first = side_ref[0] == 0
        keep_ref[...] = jnp.where(first, upper, lower).astype(bf16)
        send_ref[...] = jnp.where(first, lower, upper).astype(bf16)

    @pl.when(part == 0)
    def _():
        store(dot(turned[...], gq_ref[...]))
        query_ref[...] = column_sum(gq_ref[...].astype(f32))

    @pl.when(part == 1)
    def _():
        store(dot(turned[...], gk_ref[...]) + dot(image_turned[...], gik_ref[...]))

    @pl.when(part == 2)
    def _():
        store(dot(turned[...], gv_ref[...]) + dot(image_turned[...], giv_ref[...]))
        sums = column_sum(gv_ref[...].astype(f32)) + column_sum(giv_ref[...].astype(f32))
        value_ref[...] = sums

    @pl.when(part == 3)
    def _():
        store(extra_ref[...].astype(f32))


def weight_grads(order, side, normed, image, grads, extra):
    rows, width = normed.shape
    image_rows = image.shape[0]
    kinds = width // LANES
    tall = width // 2

    def column(height, part):
        place = lambda s, *_: (0, jnp.clip(s - part * kinds, 0, kinds - 1))
        return pl.BlockSpec((height, LANES), place)

    half = pl.BlockSpec((tall, LANES), lambda s, *_: (s, 0))
    return call(
        order,
        weight_kernel,
        (normed, image, *grads, extra),
        [shaped((4 * kinds * tall, LANES), bf16)] * 2 + [shaped((1, width), f32)] * 2,
        "weight_grads",
        cost(8 * rows * width * width, 12 << 20),
        scalars=(side,),
        grid=(4 * kinds,),
        specs=[
            resident(normed.shape),
            resident(image.shape),
            column(rows, 0),
            column(rows, 1),
            column(rows, 2),
            column(image_rows, 1),
            column(image_rows, 2),
            column(width, 3),
        ],
        outs=[half, half, column(1, 0), column(1, 2)],
        scratch=[pltpu.VMEM((width, rows), bf16), pltpu.VMEM((width, image_rows), bf16)],
    )


def image_grad_kernel(keys_weight, values_weight, keys_ref, values_ref, out_ref):
    total = dot(keys_ref[...], keys_weight[...], NT) + dot(values_ref[...], values_weight[...], NT)
    out_ref[...] = total.astype(bf16)


def image_grads(order, weight, keys, values):
    rows, width = keys.shape
    part = lambda base: pl.BlockSpec((width, width), lambda *_: (0, base))
    return call(
        order,
        image_grad_kernel,
        (weight, weight, keys, values),
        [shaped((rows, width), bf16)],
        "image_grads",
        cost(4 * rows * width * width, 6 << 20),
        grid=(1,),
        specs=[part(1), part(2), resident(keys.shape), resident(values.shape)],
        outs=[resident((rows, width))],
    )


def finish_kernel(
    flag_ref,
    hid_ref,
    gmid_ref,
    near_ref,
    far_ref,
    gq_ref,
    gk_ref,
    gv_ref,
    gain_ref,
    weight_ref,
    out_ref,
    sums_ref,
):
    rows, width = hid_ref.shape
    sums = [jnp.zeros((1, width), f32)] * 2
    for start in range(0, rows, IMG_PAD):
        here = slice(start, start + IMG_PAD)
        joined = jnp.concatenate([gq_ref[here, :], gk_ref[here, :], gv_ref[here, :]], axis=1)
        grad = dot(joined, weight_ref[...], NT)
        unit, scale = normalise(hid_ref[here, :].astype(f32))
        if start == 0:
            both = near_ref[...].astype(f32) + far_ref[...].astype(f32)
            grad = grad + jnp.where(flag_ref[0] == 1, 0.0, both)
        sums = [sums[0] + column_sum(grad * unit), sums[1] + column_sum(grad)]
        total = gmid_ref[here, :] + norm_transpose(unit, scale, gain_ref[...], grad)
        out_ref[here, :] = total.astype(bf16)
    sums = jnp.concatenate(sums, axis=0)

    @pl.when(pl.program_id(0) == 0)
    def _():
        sums_ref[...] = sums

    @pl.when(pl.program_id(0) > 0)
    def _():
        sums_ref[...] += sums


def finish_rows(order, flag, hidden, gmid, near, far, grads, gain, weight, item_rows):
    rows, width = hidden.shape
    items = rows // item_rows
    mine = pl.BlockSpec((item_rows, width), lambda i, *_: (i, 0))
    image = pl.BlockSpec((IMG_PAD, width), lambda i, *_: (i, 0))
    return call(
        order,
        finish_kernel,
        (hidden, gmid, near, far, *grads, gain, weight),
        [shaped((rows, width), bf16), shaped((2, width), f32)],
        "finish_rows",
        cost(6 * rows * width * width, 16 << 20),
        scalars=(flag,),
        grid=(items,),
        specs=[mine, mine, image, image, mine, mine, mine, resident(gain.shape), resident(weight.shape)],
        outs=[mine, resident((2, width))],
    )


def expert_kernel(half_ref, greduce_ref, gexpand_ref, *refs):
    reduce_ref, expand_ref = refs[-2:]
    reduce_ref[...] = greduce_ref[...].astype(f32)
    expand_ref[...] = gexpand_ref[...].astype(f32)


def expert_outputs(order, halves, first, value, width, units, earlier):
    parts = width // LANES
    tall = width // 2
    count = halves.shape[0]
    blocks = value.shape[0] // (count * 2 * parts * tall)
    source = lambda base: pl.BlockSpec(
        (tall, LANES), lambda i, h, p, *_: ((i * count + h) * 2 * parts + base + p, 0)
    )
    return call(
        order,
        expert_kernel,
        (value, value, *earlier),
        [shaped((units, width), f32), shaped((width, units), f32)],
        "expert_outputs",
        cost(value.size, 6 * value.size),
        scalars=(halves,),
        grid=(blocks, count, parts),
        specs=[source(0), source(parts)] + [pl.BlockSpec(memory_space=pl.ANY)] * len(earlier),
        outs=[
            pl.BlockSpec((tall, LANES), lambda i, h, p, half: (2 * (first + i) + half[h], p)),
            pl.BlockSpec((tall, LANES), lambda i, h, p, half: (half[h], (first + i) * parts + p)),
        ],
        aliases={3: 0, 4: 1} if earlier else None,
    )


def projection_kernel(half_ref, value_ref, *refs):
    in_ref, out_ref = refs[-2:]
    tall, wide = in_ref.shape

    def store(ref):
        for part in range(wide // LANES):
            piece = value_ref[part * tall : (part + 1) * tall, :]
            ref[:, part * LANES : (part + 1) * LANES] = piece.astype(f32)

    @pl.when(pl.program_id(0) < 3)
    def _():
        store(in_ref)

    @pl.when(pl.program_id(0) == 3)
    def _():
        store(out_ref)


def projection_outputs(order, half, value, width, earlier):
    tall = width // 2
    return call(
        order,
        projection_kernel,
        (value, *earlier),
        [shaped((width, 3 * width), f32), shaped((width, width), f32)],
        "projection_outputs",
        cost(value.size, 6 * value.size),
        scalars=(half,),
        grid=(4,),
        specs=[pl.BlockSpec((tall * width // LANES, LANES), lambda b, at: (b, 0))]
        + [pl.BlockSpec(memory_space=pl.ANY)] * len(earlier),
        outs=[
            pl.BlockSpec((tall, width), lambda b, at: (at[0], jnp.minimum(b, 2))),
            pl.BlockSpec((tall, width), lambda b, at: (at[0], 0)),
        ],
        aliases={2: 0, 3: 1} if earlier else None,
    )


def swap(value, axes, pair_of):
    count = 1
    for axis in axes:
        count *= lax.axis_size(axis)
    return lax.ppermute(value, axes, [(source, pair_of(source)) for source in range(count)])


def place_of(axes):
    place = 0
    for axis in axes:
        place = place * lax.axis_size(axis) + lax.axis_index(axis)
    return place


def stage_bits(axes):
    count = 1
    for axis in axes:
        count *= lax.axis_size(axis)
    bits = count.bit_length() - 1
    core = len(axes) - 1
    others = [bit for bit in range(bits) if bit != core]
    if len(axes) == 1 and len(others) == 3:
        return [(core, core), (1, 2), (3, 1), (2, 3)]
    if len(axes) == 2 and len(others) == 4:
        return [(core, core), (2, 3), (0, 2), (3, 0), (4, 4)]
    return [(core, core)] + list(zip(others, others[1:] + others[:1]))


class Total:
    def __init__(self, order, axes, keep, send):
        self.order = order
        self.axes = axes
        self.core = len(axes) - 1
        self.left = stage_bits(axes)
        place = place_of(axes)
        second = ((place >> self.core) & 1) == 1
        sides = [(place >> jnp.where(second, pair[1], pair[0])) & 1 for pair in self.left]
        self.sides = dict(zip(self.left, sides))
        self.back = list(self.left)
        self.terms = (keep, self.exchange(send, self.left.pop(0)))
        self.mine = None

    def exchange(self, value, pair):
        other = lambda source: source ^ (1 << pair[(source >> self.core) & 1])
        self.got = swap(value, self.axes, other)
        return self.got

    def part(self, which, half):
        cut = lambda term: lax.dynamic_slice_in_dim(term, which * half, half, 0).astype(f32)
        return (cut(self.terms[0]) + cut(self.terms[1])).astype(bf16)

    def step(self):
        zero = self.order.zero[0, 0]
        if self.left:
            pair = self.left.pop(0)
            half = self.terms[0].shape[0] // 2
            side = self.sides[pair] + zero
            sent = self.part(1 - side, half)
            sent = self.order.tie(sent)
            self.terms = (self.part(side, half), self.exchange(sent, pair))
            return
        pair = self.back.pop()
        if self.mine is None:
            self.mine = self.part(zero, self.terms[0].shape[0])
        else:
            first = self.last + zero == 0
            low = jnp.where(first, self.mine, self.got)
            high = jnp.where(first, self.got, self.mine)
            self.mine = jnp.concatenate([low, high], axis=0)
        self.mine = self.order.tie(self.mine)
        self.last = self.sides[pair]
        self.exchange(self.mine, pair)


class Doubling:
    def __init__(self, order, value, axis):
        self.order, self.value, self.axis = order, value, axis
        self.bits = list(range(lax.axis_size(axis).bit_length() - 1))
        self.start()

    def start(self):
        bit = self.bits.pop(0)
        self.got = swap(self.value, (self.axis,), lambda source: source ^ (1 << bit))

    def step(self):
        total = self.value + self.got + self.order.zero[0, 0].astype(f32)
        self.value = self.order.tie(total)
        if self.bits:
            self.start()
        return self.value


def on_device(
    hidden_in,
    image_count,
    text_lengths,
    attend_gain,
    attend_shift,
    project_in,
    bias_pair,
    project_out,
    project_bias,
    feed_gain,
    feed_shift,
    expand_weight,
    expand_bias,
    reduce_weight,
    reduce_bias,
    cotangent,
):
    items, _, rows, width = hidden_in.shape
    units = expand_weight.shape[2]
    is_text = lax.axis_index("mod") == 1
    flag = is_text.astype(jnp.int32)[None]
    hidden = hidden_in.reshape(items * rows, width)
    to_text = lambda value: lax.ppermute(value, "mod", [(0, 1)])
    to_image = lambda value: lax.ppermute(value, "mod", [(1, 0)])

    far_rows = [to_text(hidden_in[item, 0, :IMG_PAD]) for item in range(items)]
    far_vecs = to_text(jnp.concatenate([attend_gain, attend_shift], axis=0))
    order = Order()
    normed, projected = project_rows(
        order, hidden, attend_gain, attend_shift, project_in, bias_pair
    )
    scalars = (flag, image_count, text_lengths)
    normed_images, image_pairs, attended, lses = [], [], [], []
    for item in range(items):
        normed_image, image_pair = image_rows(
            order,
            flag,
            item,
            hidden,
            far_rows[item],
            attend_gain,
            attend_shift,
            far_vecs,
            project_in,
            bias_pair,
            rows,
        )
        out, lse = attend_forward(order, scalars, item, projected, image_pair)
        normed_images.append(normed_image)
        image_pairs.append(image_pair)
        attended.append(out)
        lses.append(lse)

    side = (lax.axis_index("dp") & 1)[None]
    (
        hidden_out,
        grad_middle,
        grad_attended,
        project_out_grad,
        vec_grads,
        expand_bias_grad,
        keep0,
        send0,
        keep1,
        send1,
    ) = feed_forward(
        order,
        flag,
        image_count,
        side,
        attended[0],
        attended[1],
        project_out,
        hidden,
        cotangent.reshape(items * rows, width),
        (project_bias[None], feed_gain, feed_shift, reduce_bias),
        expand_weight[0],
        expand_bias,
        reduce_weight[0],
    )
    a = Total(order, ("dp",), keep0, send0)
    c = Total(order, ("dp",), keep1, send1)
    grads = ()

    def backward(item, start, pairs):
        return attend_backward(
            order,
            scalars,
            item,
            start,
            pairs,
            projected,
            image_pairs[item],
            attended[item],
            grad_attended,
            lses[item],
            grads,
        )

    grads = backward(0, 0, 2)
    a.step()
    grads = backward(1, 0, 2)
    c.step()
    grads = backward(0, 2, 2)
    a.step()
    grads = backward(1, 2, 2)
    c.step()
    grads = backward(0, 4, 2)
    a.step()
    grads = backward(1, 4, 2)
    a.step()
    c.step()
    near = image_grads(order, project_in, grads[3], grads[4])
    far = to_image(near)
    images = jnp.concatenate(normed_images, axis=0)
    keep, send, query_sums, value_sums = weight_grads(
        order, side, normed, images, grads, project_out_grad
    )
    p = Total(order, ("dp", "mod"), keep, send)
    c.step()
    a.step()
    p.step()
    grad_in, attend_sums = finish_rows(
        order, flag, hidden, grad_middle, near, far, grads[:3], attend_gain, project_in, rows
    )
    ebias_rows = expand_bias_grad.reshape(-1, width)
    small = [attend_sums, vec_grads[:3], ebias_rows, vec_grads[3:4], query_sums, value_sums]
    small = Doubling(order, jnp.concatenate(small, axis=0), "dp")
    a.step()
    c.step()
    p.step()
    small.step()
    p.step()
    a.step()
    small.step()
    p.step()
    c.step()
    outputs = expert_outputs(order, side, 0, a.mine, width, units, ())
    p.step()
    small.step()
    outputs = expert_outputs(order, 1 - side, 0, a.got, width, units, outputs)
    p.step()
    c.step()
    while small.bits:
        small.step()
    small = small.step()
    shared = Doubling(order, small[-3:], "mod")
    outputs = expert_outputs(order, side, 2, c.mine, width, units, outputs)
    p.step()
    reduce_grad, expand_grad = expert_outputs(order, 1 - side, 2, c.got, width, units, outputs)
    shared = shared.step()
    while p.back:
        p.step()
    projections = projection_outputs(order, side, p.mine, width, ())
    project_in_grad, project_out_grad = projection_outputs(
        order, 1 - side, p.got, width, projections
    )
    return (
        hidden_out.reshape(hidden_in.shape),
        grad_in.reshape(hidden_in.shape),
        small[0:1],
        small[1:2],
        project_in_grad,
        shared[1:3],
        project_out_grad,
        shared[0],
        small[2:3],
        small[3:4],
        expand_grad[None],
        small[5:-3].reshape(1, -1),
        reduce_grad[None],
        small[4:5],
    )


def solution(mesh):
    in_specs = (
        P("dp", "mod", None, None),
        P("dp"),
        P("dp", None),
        P("mod", None),
        P("mod", None),
        P(),
        P(),
        P(),
        P(),
        P("mod", None),
        P("mod", None),
        P("mod", None, None),
        P("mod", None),
        P("mod", None, None),
        P("mod", None),
        P("dp", "mod", None, None),
    )
    out_specs = (
        P("dp", "mod", None, None),
        P("dp", "mod", None, None),
        P("mod", None),
        P("mod", None),
        P(),
        P(),
        P(),
        P(),
        P("mod", None),
        P("mod", None),
        P("mod", None, None),
        P("mod", None),
        P("mod", None, None),
        P("mod", None),
    )
    return jax.shard_map(
        on_device, mesh=mesh, in_specs=in_specs, out_specs=out_specs, check_vma=False
    )
```

time: 480 us -> 405 us (0.84)
  waiting for transfers between devices: 140 us -> 67.6 us
  Pallas kernels: 173 us -> 210 us
  local copies, waits for them, and re-layouts: 42.6 us -> 11.6 us
  starting transfers between devices: 77.9 us -> 51.6 us
  between operations: 1.86 us -> 18.1 us
    ppermute x65 -> x31, waiting for transfers between devices: 140 us -> 62.5 us  [swap(): lax.ppermute(value, axes, [(source, pair_of(source)) for source in range(...]
    pallas_call x18 -> x21, Pallas kernels: 173 us -> 210 us  [call(): pl.pallas_call(body, grid_spec=pltpu.PrefetchScalarGridSpec(num_scalar_pr...]
    ppermute x65 -> x31, starting transfers between devices: 68.6 us -> 42.9 us  [swap(): lax.ppermute(value, axes, [(source, pair_of(source)) for source in range(...]
    dynamic_slice x6 -> x0, local copies, waits for them, and re-layouts: 10.2 us -> none  [part(): found = [lax.dynamic_slice_in_dim(t, which * half, half, 0) for t in terms]]
    another operation x2 -> x0, local copies, waits for them, and re-layouts: 7.69 us -> none  [on_device(): jnp.stack([image_count[item], *(ends[item, j] for j in range(ends.shape[1...]
    convert_element_type x1 -> x0, local copies, waits for them, and re-layouts: 7.39 us -> none  [on_device(): expand_grad.astype(f32)[None]]
    concatenate x29 -> x12, other arithmetic: 9.44 us -> 2.49 us  [the longest x10 1.55 us: step(): self.mine = jnp.concatenate([low, high], axis=0)]
    unnamed x52, local copies, waits for them, and re-layouts: 10.4 us -> 5.27 us
  transfers between devices with their start and end apart: 69 -> 35, of which waited for: 34 -> 16; matrix products, arithmetic and copies ran while one was open for 15% -> 10% of each run, Pallas kernels for 9% -> 30%
where the time goes in v2:
time: 405 us; the launch traced here: 397 us
  Pallas kernels  210 us (52%)
  waiting for transfers between devices  67.6 us (17%)
  starting transfers between devices  51.6 us (13%)
  other arithmetic  38.6 us (10%)
  between operations  18.1 us (4%)
  local copies, waits for them, and re-layouts  11.6 us (3%)
    pallas_call x21, Pallas kernels, call(): pl.pallas_call(body, grid_spec=pltpu.PrefetchScalarGridSpec(num_scalar_pr...  210 us
    ppermute x31, waiting for transfers between devices, swap(): lax.ppermute(value, axes, [(source, pair_of(source)) for source in range(...  62.5 us
    ppermute x31, starting transfers between devices, swap(): lax.ppermute(value, axes, [(source, pair_of(source)) for source in range(...  42.9 us
    convert_element_type x13, other arithmetic, part(): return (cut(self.terms[0]) + cut(self.terms[1])).astype(bf16)  24.2 us
  transfers between devices with their start and end apart: 35, of which 16 were waited for; matrix products, arithmetic and copies ran while one was open for 10% of the time, Pallas kernels for 30%

profile of v2, /device:TPU:0, one launch (start us, length us, event | category | flops | bytes accessed | tf_op | source)
XLA Modules:
  0.0 397.3 jit_solution(9521790521326068850)
XLA Ops:
  1.8 4.9 %collective-permute-start = (bf16[256,768]{1,0:T(8,128)(2,1)S(1)}, bf16[256,768]{1,0:T(8,128)(2,1)S(1)}, u32[]{:S(2)}, u32[]{:S(2)}) collective-permute-start(bf16[256,768]{1,0:T(8,128)(2,1)S(1)} %get-tuple-element.337), channel_id=1, source_target_pairs={{0,1},{2,3},{4,5},{6,7},{8,9},{10,11},{12,13},{14,15},{16,17},{18,... | collective-permute-start | bytes 1179656 | tf_op jit(solution)/shard_map/ppermute | solution.py:955
  9.4 8.5 %project_rows.1 = (bf16[1024,768]{1,0:T(8,128)(2,1)}, bf16[1024,2304]{1,0:T(8,128)(2,1)}, s32[1,1]{1,0:T(1,128)}) custom-call(bf16[1024,768]{1,0:T(8,128)(2,1)} %bitcast.49, f32[1,768]{1,0:T(1,128)} %refs_8_.5, f32[1,768]{1,0:T(1,128)} %refs_4_.5, bf16[768,2304]{1,0:T(8,128)(2,1)} %refs_9_.3, f32[2,768]{1,0:T(2,128)} %refs_8_.4), custom_call_target="tpu_custom_call" | custom-call | flops 1 | bytes 1 | tf_op jit(solution)/shard_map/project_rows/pallas_call | solution.py:84
  18.5 5.1 %collective-permute-done.1.refs_5_ = f32[2,768]{1,0:T(2,128)S(1)} collective-permute-done((f32[2,768]{1,0:T(2,128)S(1)}, f32[2,768]{1,0:T(2,128)S(1)}, u32[]{:S(2)}, u32[]{:S(2)}) %collective-permute-start.1) | collective-permute-done | bytes 6176 | tf_op jit(solution)/shard_map/ppermute | solution.py:955
  24.4 4.5 %image_rows.2 = (bf16[256,768]{1,0:T(8,128)(2,1)}, bf16[256,1536]{1,0:T(8,128)(2,1)}, s32[1,1]{1,0:T(1,128)}) custom-call(s32[1]{0:T(128)} %bitcast.refs_0_, bf16[1024,768]{1,0:T(8,128)(2,1)} %bitcast.50, bf16[256,768]{1,0:T(8,128)(2,1)} %copy-done.12, f32[1,768]{1,0:T(1,128)} %refs_8_.5, f32[1,768]{1,0:T(1,128)} %refs_4_.5, f32[2,768]{1,0:T(2,128)} %copy-done.20, ...), custom_call_target="tpu_custom_call" | custom-call | flops 1 | bytes 1 | tf_op jit(solution)/shard_map/image_rows/pallas_call | solution.py:84
  28.9 13.1 %attend_forward.2 = (bf16[512,768]{1,0:T(8,128)(2,1)}, f32[6,2,512]{2,1,0:T(2,128)}, s32[1,1]{1,0:T(1,128)}) custom-call(s32[1]{0:T(128)} %bitcast.refs_0_, s32[2]{0:T(128)} %refs_1_.20, s32[2,4]{1,0:T(2,128)} %refs_2_.17, bf16[1024,2304]{1,0:T(8,128)(2,1)} %get-tuple-element.159.refs_3_.refs_4_.refs_5_, ...), custom_call_target="tpu_custom_call" | custom-call | flops 1 | bytes 1 | tf_op jit(solution)/shard_map/attend_forward/pallas_call | solution.py:84
  42.7 4.5 %image_rows.3 = (bf16[256,768]{1,0:T(8,128)(2,1)}, bf16[256,1536]{1,0:T(8,128)(2,1)}, s32[1,1]{1,0:T(1,128)}) custom-call(s32[1]{0:T(128)} %bitcast.refs_0_, bf16[1024,768]{1,0:T(8,128)(2,1)} %bitcast.51, bf16[256,768]{1,0:T(8,128)(2,1)} %copy-done.11, f32[1,768]{1,0:T(1,128)} %refs_8_.5, f32[1,768]{1,0:T(1,128)} %refs_4_.5, f32[2,768]{1,0:T(2,128)} %copy-done.20, ...), custom_call_target="tpu_custom_call" | custom-call | flops 1 | bytes 1 | tf_op jit(solution)/shard_map/image_rows/pallas_call | solution.py:84
  47.2 13.0 %attend_forward.3 = (bf16[512,768]{1,0:T(8,128)(2,1)}, f32[6,2,512]{2,1,0:T(2,128)}, s32[1,1]{1,0:T(1,128)}) custom-call(s32[1]{0:T(128)} %bitcast.refs_0_, s32[2]{0:T(128)} %refs_1_.20, s32[2,4]{1,0:T(2,128)} %refs_2_.17, bf16[1024,2304]{1,0:T(8,128)(2,1)} %get-tuple-element.159.refs_3_.refs_4_.refs_5_, ...), custom_call_target="tpu_custom_call" | custom-call | flops 1 | bytes 1 | tf_op jit(solution)/shard_map/attend_forward/pallas_call | solution.py:84
  60.2 46.1 %feed_forward.1 = (bf16[1024,768]{1,0:T(8,128)(2,1)}, f32[1024,768]{1,0:T(8,128)}, bf16[1024,768]{1,0:T(8,128)(2,1)}, bf16[768,768]{1,0:T(8,128)(2,1)}, f32[8,76...) custom-call(s32[1]{0:T(128)} %bitcast.refs_0_, ...), custom_call_target="tpu_custom_call" | custom-call | flops 1 | bytes 1 | tf_op jit(solution)/shard_map/feed_forward/pallas_call | solution.py:84
  106.9 8.7 %attend_backward.6 = (bf16[1024,768]{1,0:T(8,128)(2,1)}, bf16[1024,768]{1,0:T(8,128)(2,1)}, bf16[1024,768]{1,0:T(8,128)(2,1)}, bf16[512,768]{1,0:T(8,128)(2,1)},...) custom-call(s32[1]{0:T(128)} %bitcast.refs_0_, s32[2]{0:T(128)} %refs_1_.20, s32[2,4]{1,0:T(2,128)} %refs_2_.17, ...), custom_call_target="tpu_custom_call" | custom-call | flops 1 | bytes 1 | tf_op jit(solution)/shard_map/attend_backward/pallas_call | solution.py:84
  116.3 3.9 add_convert_fusion.3
  121.7 8.7 %attend_backward.7 = (bf16[1024,768]{1,0:T(8,128)(2,1)}, bf16[1024,768]{1,0:T(8,128)(2,1)}, bf16[1024,768]{1,0:T(8,128)(2,1)}, bf16[512,768]{1,0:T(8,128)(2,1)},...) custom-call(s32[1]{0:T(128)} %bitcast.refs_0_, ...), custom_call_target="tpu_custom_call", output_to_operand_aliasing={{0}: (11, {}), {1}: (12, {}), {2}: (13, {}), {3}: (14, {}),... | custom-call | flops 1 | bytes 1 | tf_op jit(solution)/shard_map/attend_backward/pallas_call | solution.py:84
  131.1 3.9 add_convert_fusion.2
  135.6 8.8 %attend_backward.8 = (bf16[1024,768]{1,0:T(8,128)(2,1)}, bf16[1024,768]{1,0:T(8,128)(2,1)}, bf16[1024,768]{1,0:T(8,128)(2,1)}, bf16[512,768]{1,0:T(8,128)(2,1)},...) custom-call(s32[1]{0:T(128)} %bitcast.refs_0_, ...), custom_call_target="tpu_custom_call", output_to_operand_aliasing={{0}: (11, {}), {1}: (12, {}), {2}: (13, {}), {3}: (14, {}),... | custom-call | flops 1 | bytes 1 | tf_op jit(solution)/shard_map/attend_backward/pallas_call | solution.py:84
  146.0 2.3 add_convert_fusion.9
  148.4 2.6 collective-permute-start.7
  151.0 9.0 %attend_backward.9 = (bf16[1024,768]{1,0:T(8,128)(2,1)}, bf16[1024,768]{1,0:T(8,128)(2,1)}, bf16[1024,768]{1,0:T(8,128)(2,1)}, bf16[512,768]{1,0:T(8,128)(2,1)},...) custom-call(s32[1]{0:T(128)} %bitcast.refs_0_, ...), custom_call_target="tpu_custom_call", output_to_operand_aliasing={{0}: (11, {}), {1}: (12, {}), {2}: (13, {}), {3}: (14, {}),... | custom-call | flops 1 | bytes 1 | tf_op jit(solution)/shard_map/attend_backward/pallas_call | solution.py:84
  160.6 2.3 add_convert_fusion.8
  163.0 8.9 %attend_backward.10 = (bf16[1024,768]{1,0:T(8,128)(2,1)}, bf16[1024,768]{1,0:T(8,128)(2,1)}, bf16[1024,768]{1,0:T(8,128)(2,1)}, bf16[512,768]{1,0:T(8,128)(2,1)}...) custom-call(s32[1]{0:T(128)} %bitcast.refs_0_, ...), custom_call_target="tpu_custom_call", output_to_operand_aliasing={{0}: (11, {}), {1}: (12, {}), {2}: (13, {}), {3}: (14, {}),... | custom-call | flops 1 | bytes 1 | tf_op jit(solution)/shard_map/attend_backward/pallas_call | solution.py:84
  176.2 8.7 %attend_backward.11 = (bf16[1024,768]{1,0:T(8,128)(2,1)}, bf16[1024,768]{1,0:T(8,128)(2,1)}, bf16[1024,768]{1,0:T(8,128)(2,1)}, bf16[512,768]{1,0:T(8,128)(2,1)}...) custom-call(s32[1]{0:T(128)} %bitcast.refs_0_, ...), custom_call_target="tpu_custom_call", output_to_operand_aliasing={{0}: (11, {}), {1}: (12, {}), {2}: (13, {}), {3}: (14, {}),... | custom-call | flops 1 | bytes 1 | tf_op jit(solution)/shard_map/attend_backward/pallas_call | solution.py:84
  185.0 2.0 collective-permute-done.8
  188.7 5.7 %collective-permute-done.9 = bf16[1152,256]{1,0:T(8,128)(2,1)S(1)} collective-permute-done((bf16[1152,256]{1,0:T(8,128)(2,1)}, bf16[1152,256]{1,0:T(8,128)(2,1)S(1)}, u32[]{:S(2)}, u32[]{:S(2)}) %collective-permute-start.9) | collective-permute-done | bytes 589856 | tf_op jit(solution)/shard_map/ppermute | solution.py:844
  194.5 5.0 %image_grads.1 = (bf16[512,768]{1,0:T(8,128)(2,1)}, s32[1,1]{1,0:T(1,128)}) custom-call(bf16[768,2304]{1,0:T(8,128)(2,1)} %refs_9_.3, bf16[768,2304]{1,0:T(8,128)(2,1)} %refs_9_.3, bf16[512,768]{1,0:T(8,128)(2,1)} %get-tuple-element.217.refs_2_.refs_6_, bf16[512,768]{1,0:T(8,128)(2,1)} %get-tuple-element.218.refs_3_.refs_7_, s32[1,1]{1,0:T(1,128)} %get-tuple-element.223.refs_4_), custom_call_target="tpu_custom_call" | custom-call | flops 1 | bytes 1 | tf_op jit(solution)/shard_map/image_grads/pallas_call | solution.py:84
  199.6 15.2 %weight_grads.1 = (bf16[4608,256]{1,0:T(8,128)(2,1)}, bf16[4608,256]{1,0:T(8,128)(2,1)}, f32[1,768]{1,0:T(1,128)}, f32[1,768]{1,0:T(1,128)}, s32[1,1]{1,0:T(1,128)}) custom-call(s32[1]{0:T(128)} %bitcast.1.refs_2_.refs_0_, bf16[1024,768]{1,0:T(8,128)(2,1)} %get-tuple-element.228.refs_1_, bf16[512,768]{1,0:T(8,128)(2,1)} %pad_maximum_fusion.6.refs_2_, ...), custom_call_target="tpu_custom_call" | custom-call | flops 1 | bytes 1 | tf_op jit(solution)/shard_map/weight_grads/pallas_call | solution.py:84
  218.3 6.3 %collective-permute-done.11 = bf16[576,256]{1,0:T(8,128)(2,1)S(1)} collective-permute-done((bf16[576,256]{1,0:T(8,128)(2,1)S(1)}, bf16[576,256]{1,0:T(8,128)(2,1)S(1)}, u32[]{:S(2)}, u32[]{:S(2)}) %collective-permute-start.11) | collective-permute-done | bytes 294944 | tf_op jit(solution)/shard_map/ppermute | solution.py:844
  225.4 5.6 %collective-permute-done.12 = bf16[576,256]{1,0:T(8,128)(2,1)S(1)} collective-permute-done((bf16[576,256]{1,0:T(8,128)(2,1)S(1)}, bf16[576,256]{1,0:T(8,128)(2,1)S(1)}, u32[]{:S(2)}, u32[]{:S(2)}) %collective-permute-start.12) | collective-permute-done | bytes 294944 | tf_op jit(solution)/shard_map/ppermute | solution.py:844
  233.3 2.3 collective-permute-start.16
  235.7 3.9 add_convert_fusion
  239.6 11.2 %finish_rows.1 = (bf16[1024,768]{1,0:T(8,128)(2,1)}, f32[2,768]{1,0:T(2,128)}, s32[1,1]{1,0:T(1,128)}) custom-call(s32[1]{0:T(128)} %bitcast.refs_0_, bf16[1024,768]{1,0:T(8,128)(2,1)} %bitcast.53, f32[1024,768]{1,0:T(8,128)} %get-tuple-element.170.refs_2_, bf16[512,768]{1,0:T(8,128)(2,1)} %get-tuple-element.224.refs_3_, ...), custom_call_target="tpu_custom_call" | custom-call | flops 1 | bytes 1 | tf_op jit(solution)/shard_map/finish_rows/pallas_call | solution.py:84
  258.7 9.4 %collective-permute-done.17 = bf16[2304,256]{1,0:T(8,128)(2,1)} collective-permute-done((bf16[2304,256]{1,0:T(8,128)(2,1)}, bf16[2304,256]{1,0:T(8,128)(2,1)}, u32[]{:S(2)}, u32[]{:S(2)}) %collective-permute-start.17) | collective-permute-done | bytes 1179680 | tf_op jit(solution)/shard_map/ppermute | solution.py:844
  268.0 2.4 add_convert_fusion.6
  270.4 2.5 collective-permute-start.19
  278.2 2.7 collective-permute-done.19
  282.6 4.4 %collective-permute-done.20 = bf16[2304,256]{1,0:T(8,128)(2,1)} collective-permute-done((bf16[2304,256]{1,0:T(8,128)(2,1)S(1)}, bf16[2304,256]{1,0:T(8,128)(2,1)}, u32[]{:S(2)}, u32[]{:S(2)}) %collective-permute-start.20) | collective-permute-done | bytes 1179680 | tf_op jit(solution)/shard_map/ppermute | solution.py:844
  294.3 2.8 collective-permute-done.18
  302.4 3.5 collective-permute-done.24
  308.7 3.1 collective-permute-start.21
  311.7 6.2 %expert_outputs.4 = (f32[3072,768]{1,0:T(8,128)}, f32[768,3072]{1,0:T(8,128)}, s32[1,1]{1,0:T(1,128)}) custom-call(s32[1]{0:T(128)} %bitcast.1.refs_2_.refs_0_, bf16[4608,256]{1,0:T(8,128)(2,1)} %copy-done.1, bf16[4608,256]{1,0:T(8,128)(2,1)} %copy-done.1, s32[1,1]{1,0:T(1,128)} %get-tuple-element.267.refs_3_), custom_call_target="tpu_custom_call" | custom-call | flops 1 | bytes 1 | tf_op jit(solution)/shard_map/expert_outputs/pallas_call | solution.py:84
  321.8 6.2 %expert_outputs.5 = (f32[3072,768]{1,0:T(8,128)}, f32[768,3072]{1,0:T(8,128)}, s32[1,1]{1,0:T(1,128)}) custom-call(s32[1]{0:T(128)S(6)} %sub.45.refs_0_, bf16[4608,256]{1,0:T(8,128)(2,1)} %collective-permute-done.26.refs_1_.refs_2_, bf16[4608,256]{1,0:T(8,128)(2,1)} %collective-permute-done.26.refs_1_.refs_2_, ...), custom_call_target="tpu_custom_call", output_to_operand_aliasing={{0}: (3, {}), {1}: (4, {})} | custom-call | flops 1 | bytes 1 | tf_op jit(solution)/shard_map/expert_outputs/pallas_call | solution.py:84
  332.7 6.0 %collective-permute-start.30 = (bf16[4608,256]{1,0:T(8,128)(2,1)S(1)}, bf16[4608,256]{1,0:T(8,128)(2,1)}, u32[]{:S(2)}, u32[]{:S(2)}) collective-permute-start(bf16[4608,256]{1,0:T(8,128)(2,1)S(1)} %pad_maximum_fusion.1.refs_1_.refs_2_), channel_id=1, source_target_pairs={{0,2},{2,0},{4,6},{6,4},{8,10},{10,8},{12,14},{14,12},{16,18},{18,... | collective-permute-start | bytes 7077896 | tf_op jit(solution)/shard_map/ppermute | solution.py:844
  339.5 2.6 collective-permute-start.25
  342.8 2.1 collective-permute-done.25
  345.5 6.2 %expert_outputs.6 = (f32[3072,768]{1,0:T(8,128)}, f32[768,3072]{1,0:T(8,128)}, s32[1,1]{1,0:T(1,128)}) custom-call(s32[1]{0:T(128)} %bitcast.1.refs_2_.refs_0_, bf16[4608,256]{1,0:T(8,128)(2,1)} %copy-done, bf16[4608,256]{1,0:T(8,128)(2,1)} %copy-done, f32[3072,768]{1,0:T(8,128)} %get-tuple-element.281.refs_3_, ...), custom_call_target="tpu_custom_call", output_to_operand_aliasing={{0}: (3, {}), {1}: (4, {})} | custom-call | flops 1 | bytes 1 | tf_op jit(solution)/shard_map/expert_outputs/pallas_call | solution.py:84
  352.4 2.1 collective-permute-start.32
  355.2 6.2 %expert_outputs.7 = (f32[3072,768]{1,0:T(8,128)}, f32[768,3072]{1,0:T(8,128)}, s32[1,1]{1,0:T(1,128)}) custom-call(s32[1]{0:T(128)S(6)} %sub.45.refs_0_, bf16[4608,256]{1,0:T(8,128)(2,1)} %collective-permute-done.30.refs_1_.refs_2_, bf16[4608,256]{1,0:T(8,128)(2,1)} %collective-permute-done.30.refs_1_.refs_2_, ...), custom_call_target="tpu_custom_call", output_to_operand_aliasing={{0}: (3, {}), {1}: (4, {})} | custom-call | flops 1 | bytes 1 | tf_op jit(solution)/shard_map/expert_outputs/pallas_call | solution.py:84
  364.2 2.6 collective-permute-start.33
  367.4 13.5 %collective-permute-done.33 = bf16[2304,256]{1,0:T(8,128)(2,1)S(1)} collective-permute-done((bf16[2304,256]{1,0:T(8,128)(2,1)S(1)}, bf16[2304,256]{1,0:T(8,128)(2,1)S(1)}, u32[]{:S(2)}, u32[]{:S(2)}) %collective-permute-start.33) | collective-permute-done | bytes 1179680 | tf_op jit(solution)/shard_map/ppermute | solution.py:844
  384.5 5.4 %projection_outputs.2 = (f32[768,2304]{1,0:T(8,128)}, f32[768,768]{1,0:T(8,128)}, s32[1,1]{1,0:T(1,128)}) custom-call(s32[1]{0:T(128)} %bitcast.1.refs_2_.refs_0_, bf16[4608,256]{1,0:T(8,128)(2,1)} %copy-done.2, s32[1,1]{1,0:T(1,128)} %get-tuple-element.295.refs_2_), custom_call_target="tpu_custom_call" | custom-call | flops 1 | bytes 1 | tf_op jit(solution)/shard_map/projection_outputs/pallas_call | solution.py:84
  391.4 5.5 %projection_outputs.3 = (f32[768,2304]{1,0:T(8,128)}, f32[768,768]{1,0:T(8,128)}, s32[1,1]{1,0:T(1,128)}) custom-call(s32[1]{0:T(128)S(6)} %sub.45.refs_0_, bf16[4608,256]{1,0:T(8,128)(2,1)} %copy-done.3, f32[768,2304]{1,0:T(8,128)} %get-tuple-element.296.refs_2_, ...), custom_call_target="tpu_custom_call", output_to_operand_aliasing={{0}: (2, {}), {1}: (3, {})} | custom-call | flops 1 | bytes 1 | tf_op jit(solution)/shard_map/projection_outputs/pallas_call | solution.py:84
  (147 shorter events, 58.9 us)
Async XLA Ops:
  0.6 7.4 %copy-start.18 = (f32[1,768]{1,0:T(1,128)S(1)}, f32[1,768]{1,0:T(1,128)}, u32[]{:S(2)}) copy-start(f32[1,768]{1,0:T(1,128)} %refs_8_.5) | copy-start | bytes 9220
  0.7 7.4 %copy-start.19 = (f32[1,768]{1,0:T(1,128)S(1)}, f32[1,768]{1,0:T(1,128)}, u32[]{:S(2)}) copy-start(f32[1,768]{1,0:T(1,128)} %refs_4_.5) | copy-start | bytes 9220
  1.8 21.8 %collective-permute-start = (bf16[256,768]{1,0:T(8,128)(2,1)S(1)}, bf16[256,768]{1,0:T(8,128)(2,1)S(1)}, u32[]{:S(2)}, u32[]{:S(2)}) collective-permute-start(bf16[256,768]{1,0:T(8,128)(2,1)S(1)} %get-tuple-element.337), channel_id=1, source_target_pairs={{0,1},{2,3},{4,5},{6,7},{8,9},{10,11},{12,13},{14,15},{16,17},{18,... | collective-permute-start | bytes 1179656 | tf_op jit(solution)/shard_map/ppermute | solution.py:955
  6.7 35.2 %collective-permute-start.2 = (bf16[256,768]{1,0:T(8,128)(2,1)S(1)}, bf16[256,768]{1,0:T(8,128)(2,1)S(1)}, u32[]{:S(2)}, u32[]{:S(2)}) collective-permute-start(bf16[256,768]{1,0:T(8,128)(2,1)S(1)} %get-tuple-element.336), channel_id=1, source_target_pairs={{0,1},{2,3},{4,5},{6,7},{8,9},{10,11},{12,13},{14,15},{16,17},{18,... | collective-permute-start | bytes 1179656 | tf_op jit(solution)/shard_map/ppermute | solution.py:955
  8.1 15.5 %collective-permute-start.1 = (f32[2,768]{1,0:T(2,128)S(1)}, f32[2,768]{1,0:T(2,128)S(1)}, u32[]{:S(2)}, u32[]{:S(2)}) collective-permute-start(f32[2,768]{1,0:T(2,128)S(1)} %pad_maximum_fusion.11), channel_id=1, source_target_pairs={{0,1},{2,3},{4,5},{6,7},{8,9},{10,11},{12,13},{14,15},{16,17},{18,... | collective-permute-start | bytes 18440 | tf_op jit(solution)/shard_map/ppermute | solution.py:955
  9.4 8.6 %copy-start.23 = (f32[768]{0:T(1024)S(1)}, f32[768]{0:T(1024)}, u32[]{:S(2)}) copy-start(f32[768]{0:T(1024)} %param.24) | copy-start | bytes 9220
  106.3 10.0 %collective-permute-start.3 = (bf16[4608,256]{1,0:T(8,128)(2,1)}, bf16[4608,256]{1,0:T(8,128)(2,1)}, u32[]{:S(2)}, u32[]{:S(2)}) collective-permute-start(bf16[4608,256]{1,0:T(8,128)(2,1)} %get-tuple-element.182), channel_id=1, source_target_pairs={{0,2},{2,0},{4,6},{6,4},{8,10},{10,8},{12,14},{14,12},{16,18},{18,... | collective-permute-start | bytes 7077896 | tf_op jit(solution)/shard_map/ppermute | solution.py:844
  106.4 24.7 %collective-permute-start.4 = (bf16[4608,256]{1,0:T(8,128)(2,1)}, bf16[4608,256]{1,0:T(8,128)(2,1)}, u32[]{:S(2)}, u32[]{:S(2)}) collective-permute-start(bf16[4608,256]{1,0:T(8,128)(2,1)} %get-tuple-element.191), channel_id=1, source_target_pairs={{0,2},{2,0},{4,6},{6,4},{8,10},{10,8},{12,14},{14,12},{16,18},{18,... | collective-permute-start | bytes 7077896 | tf_op jit(solution)/shard_map/ppermute | solution.py:844
  120.2 24.8 %collective-permute-start.5 = (bf16[2304,256]{1,0:T(8,128)(2,1)}, bf16[2304,256]{1,0:T(8,128)(2,1)S(1)}, u32[]{:S(2)}, u32[]{:S(2)}) collective-permute-start(bf16[2304,256]{1,0:T(8,128)(2,1)} %get-tuple-element.199), channel_id=1, source_target_pairs={{0,4},{2,10},{4,0},{6,14},{8,12},{10,2},{12,8},{14,6},{16,20},{18,... | collective-permute-start | bytes 3538952 | tf_op jit(solution)/shard_map/ppermute | solution.py:844
  135.0 25.6 %collective-permute-start.6 = (bf16[2304,256]{1,0:T(8,128)(2,1)}, bf16[2304,256]{1,0:T(8,128)(2,1)}, u32[]{:S(2)}, u32[]{:S(2)}) collective-permute-start(bf16[2304,256]{1,0:T(8,128)(2,1)} %get-tuple-element.207), channel_id=1, source_target_pairs={{0,4},{2,10},{4,0},{6,14},{8,12},{10,2},{12,8},{14,6},{16,20},{18,... | collective-permute-start | bytes 3538952 | tf_op jit(solution)/shard_map/ppermute | solution.py:844
  148.4 24.6 %collective-permute-start.7 = (bf16[1152,256]{1,0:T(8,128)(2,1)}, bf16[1152,256]{1,0:T(8,128)(2,1)S(1)}, u32[]{:S(2)}, u32[]{:S(2)}) collective-permute-start(bf16[1152,256]{1,0:T(8,128)(2,1)} %get-tuple-element.215), channel_id=1, source_target_pairs={{0,16},{2,6},{4,20},{6,2},{8,24},{10,14},{12,28},{14,10},{16,0},{1... | collective-permute-start | bytes 1769480 | tf_op jit(solution)/shard_map/ppermute | solution.py:844
  163.0 12.3 %copy-start.9 = (bf16[256,768]{1,0:T(8,128)(2,1)S(1)}, bf16[256,768]{1,0:T(8,128)(2,1)}, u32[]{:S(2)}) copy-start(bf16[256,768]{1,0:T(8,128)(2,1)} %get-tuple-element.229) | copy-start | bytes 1179652
  163.0 12.3 %copy-start.10 = (bf16[256,768]{1,0:T(8,128)(2,1)S(1)}, bf16[256,768]{1,0:T(8,128)(2,1)}, u32[]{:S(2)}) copy-start(bf16[256,768]{1,0:T(8,128)(2,1)} %get-tuple-element.230) | copy-start | bytes 1179652
  172.5 21.9 %collective-permute-start.9 = (bf16[1152,256]{1,0:T(8,128)(2,1)}, bf16[1152,256]{1,0:T(8,128)(2,1)S(1)}, u32[]{:S(2)}, u32[]{:S(2)}) collective-permute-start(bf16[1152,256]{1,0:T(8,128)(2,1)} %get-tuple-element.222), channel_id=1, source_target_pairs={{0,16},{2,6},{4,20},{6,2},{8,24},{10,14},{12,28},{14,10},{16,0},{1... | collective-permute-start | bytes 1769480 | tf_op jit(solution)/shard_map/ppermute | solution.py:844
  173.7 13.3 %collective-permute-start.8 = (bf16[576,256]{1,0:T(8,128)(2,1)}, bf16[576,256]{1,0:T(8,128)(2,1)}, u32[]{:S(2)}, u32[]{:S(2)}) collective-permute-start(bf16[576,256]{1,0:T(8,128)(2,1)} %add_convert_fusion.19), channel_id=1, source_target_pairs={{0,8},{2,18},{4,12},{6,22},{8,0},{10,26},{12,4},{14,30},{16,24},{1... | collective-permute-start | bytes 884744 | tf_op jit(solution)/shard_map/ppermute | solution.py:844
  199.6 17.4 %copy-start.8 = (bf16[512,768]{1,0:T(8,128)(2,1)S(1)}, bf16[512,768]{1,0:T(8,128)(2,1)}, u32[]{:S(2)}) copy-start(bf16[512,768]{1,0:T(8,128)(2,1)} %get-tuple-element.224.refs_3_) | copy-start | bytes 2359300
  214.8 20.8 %collective-permute-start.13 = (bf16[4608,256]{1,0:T(8,128)(2,1)}, bf16[4608,256]{1,0:T(8,128)(2,1)}, u32[]{:S(2)}, u32[]{:S(2)}) collective-permute-start(bf16[4608,256]{1,0:T(8,128)(2,1)} %get-tuple-element.239), channel_id=1, source_target_pairs={{0,2},{1,3},{2,0},{3,1},{4,6},{5,7},{6,4},{7,5},{8,10},{9,11},{10,... | collective-permute-start | bytes 7077896 | tf_op jit(solution)/shard_map/ppermute | solution.py:844
  214.9 9.7 %collective-permute-start.11 = (bf16[576,256]{1,0:T(8,128)(2,1)S(1)}, bf16[576,256]{1,0:T(8,128)(2,1)S(1)}, u32[]{:S(2)}, u32[]{:S(2)}) collective-permute-start(bf16[576,256]{1,0:T(8,128)(2,1)S(1)} %add_convert_fusion.16), channel_id=1, source_target_pairs={{0,8},{2,18},{4,12},{6,22},{8,0},{10,26},{12,4},{14,30},{16,24},{1... | collective-permute-start | bytes 884744 | tf_op jit(solution)/shard_map/ppermute | solution.py:844
  215.3 15.7 %collective-permute-start.12 = (bf16[576,256]{1,0:T(8,128)(2,1)S(1)}, bf16[576,256]{1,0:T(8,128)(2,1)S(1)}, u32[]{:S(2)}, u32[]{:S(2)}) collective-permute-start(bf16[576,256]{1,0:T(8,128)(2,1)S(1)} %add_convert_fusion.17), channel_id=1, source_target_pairs={{0,8},{2,18},{4,12},{6,22},{8,0},{10,26},{12,4},{14,30},{16,24},{1... | collective-permute-start | bytes 884744 | tf_op jit(solution)/shard_map/ppermute | solution.py:844
  217.0 22.6 %collective-permute-start.10 = (bf16[512,768]{1,0:T(8,128)(2,1)S(1)}, bf16[512,768]{1,0:T(8,128)(2,1)}, u32[]{:S(2)}, u32[]{:S(2)}) collective-permute-start(bf16[512,768]{1,0:T(8,128)(2,1)S(1)} %copy-done.8), channel_id=1, source_target_pairs={{1,0},{3,2},{5,4},{7,6},{9,8},{11,10},{13,12},{15,14},{17,16},{19,... | collective-permute-start | bytes 2359304 | tf_op jit(solution)/shard_map/ppermute | solution.py:956
  231.0 23.5 %collective-permute-start.15 = (bf16[1152,256]{1,0:T(8,128)(2,1)S(1)}, bf16[1152,256]{1,0:T(8,128)(2,1)S(1)}, u32[]{:S(2)}, u32[]{:S(2)}) collective-permute-start(bf16[1152,256]{1,0:T(8,128)(2,1)S(1)} %pad_maximum_fusion.7), channel_id=1, source_target_pairs={{0,16},{2,6},{4,20},{6,2},{8,24},{10,14},{12,28},{14,10},{16,0},{1... | collective-permute-start | bytes 1769480 | tf_op jit(solution)/shard_map/ppermute | solution.py:844
  233.3 23.6 %collective-permute-start.16 = (bf16[576,256]{1,0:T(8,128)(2,1)S(1)}, bf16[576,256]{1,0:T(8,128)(2,1)}, u32[]{:S(2)}, u32[]{:S(2)}) collective-permute-start(bf16[576,256]{1,0:T(8,128)(2,1)S(1)} %add_convert_fusion.14), channel_id=1, source_target_pairs={{0,8},{2,18},{4,12},{6,22},{8,0},{10,26},{12,4},{14,30},{16,24},{1... | collective-permute-start | bytes 884744 | tf_op jit(solution)/shard_map/ppermute | solution.py:844
  251.4 16.6 %collective-permute-start.17 = (bf16[2304,256]{1,0:T(8,128)(2,1)}, bf16[2304,256]{1,0:T(8,128)(2,1)}, u32[]{:S(2)}, u32[]{:S(2)}) collective-permute-start(bf16[2304,256]{1,0:T(8,128)(2,1)} %get-tuple-element.252), channel_id=1, source_target_pairs={{0,4},{1,5},{2,10},{3,11},{4,0},{5,1},{6,14},{7,15},{8,12},{9,13},... | collective-permute-start | bytes 3538952 | tf_op jit(solution)/shard_map/ppermute | solution.py:844
  255.4 31.6 %collective-permute-start.20 = (bf16[2304,256]{1,0:T(8,128)(2,1)S(1)}, bf16[2304,256]{1,0:T(8,128)(2,1)}, u32[]{:S(2)}, u32[]{:S(2)}) collective-permute-start(bf16[2304,256]{1,0:T(8,128)(2,1)S(1)} %pad_maximum_fusion.3), channel_id=1, source_target_pairs={{0,4},{2,10},{4,0},{6,14},{8,12},{10,2},{12,8},{14,6},{16,20},{18,... | collective-permute-start | bytes 3538952 | tf_op jit(solution)/shard_map/ppermute | solution.py:844
  270.4 10.6 %collective-permute-start.19 = (bf16[1152,256]{1,0:T(8,128)(2,1)}, bf16[1152,256]{1,0:T(8,128)(2,1)S(1)}, u32[]{:S(2)}, u32[]{:S(2)}) collective-permute-start(bf16[1152,256]{1,0:T(8,128)(2,1)} %get-tuple-element.256), channel_id=1, source_target_pairs={{0,1},{1,0},{2,6},{3,7},{4,5},{5,4},{6,2},{7,3},{8,9},{9,8},{10,14... | collective-permute-start | bytes 1769480 | tf_op jit(solution)/shard_map/ppermute | solution.py:844
  275.6 1.3 collective-permute-start.14
  288.4 12.5 %copy-start.6 = (bf16[576,256]{1,0:T(8,128)(2,1)S(1)}, bf16[576,256]{1,0:T(8,128)(2,1)}, u32[]{:S(2)}) copy-start(bf16[576,256]{1,0:T(8,128)(2,1)} %get-tuple-element.342) | copy-start | bytes 884740
  288.6 18.5 %copy-start.1 = (bf16[4608,256]{1,0:T(8,128)(2,1)}, bf16[4608,256]{1,0:T(8,128)(2,1)S(1)}, u32[]{:S(2)}) copy-start(bf16[4608,256]{1,0:T(8,128)(2,1)S(1)} %pad_maximum_fusion.refs_1_.refs_2_) | copy-start | bytes 7077892
  288.6 33.2 %collective-permute-start.26 = (bf16[4608,256]{1,0:T(8,128)(2,1)S(1)}, bf16[4608,256]{1,0:T(8,128)(2,1)}, u32[]{:S(2)}, u32[]{:S(2)}) collective-permute-start(bf16[4608,256]{1,0:T(8,128)(2,1)S(1)} %pad_maximum_fusion.refs_1_.refs_2_), channel_id=1, source_target_pairs={{0,2},{2,0},{4,6},{6,4},{8,10},{10,8},{12,14},{14,12},{16,18},{18,... | collective-permute-start | bytes 7077896 | tf_op jit(solution)/shard_map/ppermute | solution.py:844
  288.8 17.1 %collective-permute-start.24 = (bf16[1152,256]{1,0:T(8,128)(2,1)S(1)}, bf16[1152,256]{1,0:T(8,128)(2,1)}, u32[]{:S(2)}, u32[]{:S(2)}) collective-permute-start(bf16[1152,256]{1,0:T(8,128)(2,1)S(1)} %pad_maximum_fusion.8), channel_id=1, source_target_pairs={{0,16},{2,6},{4,20},{6,2},{8,24},{10,14},{12,28},{14,10},{16,0},{1... | collective-permute-start | bytes 1769480 | tf_op jit(solution)/shard_map/ppermute | solution.py:844
  290.2 10.7 %collective-permute-start.22 = (bf16[576,256]{1,0:T(8,128)(2,1)}, bf16[576,256]{1,0:T(8,128)(2,1)S(1)}, u32[]{:S(2)}, u32[]{:S(2)}) collective-permute-start(bf16[576,256]{1,0:T(8,128)(2,1)} %get-tuple-element.262), channel_id=1, source_target_pairs={{0,8},{1,9},{2,3},{3,2},{4,12},{5,13},{6,7},{7,6},{8,0},{9,1},{10,... | collective-permute-start | bytes 884744 | tf_op jit(solution)/shard_map/ppermute | solution.py:844
  292.1 5.0 %collective-permute-start.18 = (f32[12,768]{1,0:T(8,128)}, f32[12,768]{1,0:T(8,128)}, u32[]{:S(2)}, u32[]{:S(2)}) collective-permute-start(f32[12,768]{1,0:T(8,128)} %add_add_fusion.3), channel_id=1, source_target_pairs={{0,4},{2,6},{4,0},{6,2},{8,12},{10,14},{12,8},{14,10},{16,20},{18,... | collective-permute-start | bytes 110600 | tf_op jit(solution)/shard_map/ppermute | solution.py:844
  307.1 24.0 %collective-permute-start.28 = (bf16[2304,256]{1,0:T(8,128)(2,1)S(1)}, bf16[2304,256]{1,0:T(8,128)(2,1)}, u32[]{:S(2)}, u32[]{:S(2)}) collective-permute-start(bf16[2304,256]{1,0:T(8,128)(2,1)S(1)} %pad_maximum_fusion.4), channel_id=1, source_target_pairs={{0,4},{2,10},{4,0},{6,14},{8,12},{10,2},{12,8},{14,6},{16,20},{18,... | collective-permute-start | bytes 3538952 | tf_op jit(solution)/shard_map/ppermute | solution.py:844
  308.7 9.3 %collective-permute-start.23 = (bf16[288,256]{1,0:T(8,128)(2,1)}, bf16[288,256]{1,0:T(8,128)(2,1)}, u32[]{:S(2)}, u32[]{:S(2)}) collective-permute-start(bf16[288,256]{1,0:T(8,128)(2,1)} %add_convert_fusion.21), channel_id=1, source_target_pairs={{0,16},{1,17},{2,18},{3,19},{4,20},{5,21},{6,22},{7,23},{8,24},{9,... | collective-permute-start | bytes 442376 | tf_op jit(solution)/shard_map/ppermute | solution.py:844
  308.7 11.7 %collective-permute-start.21 = (f32[12,768]{1,0:T(8,128)}, f32[12,768]{1,0:T(8,128)}, u32[]{:S(2)}, u32[]{:S(2)}) collective-permute-start(f32[12,768]{1,0:T(8,128)} %add_add_fusion.2), channel_id=1, source_target_pairs={{0,8},{2,10},{4,12},{6,14},{8,0},{10,2},{12,4},{14,6},{16,24},{18,... | collective-permute-start | bytes 110600 | tf_op jit(solution)/shard_map/ppermute | solution.py:844
  311.7 6.3 %copy-start.7 = (bf16[576,256]{1,0:T(8,128)(2,1)S(1)}, bf16[576,256]{1,0:T(8,128)(2,1)}, u32[]{:S(2)}) copy-start(bf16[576,256]{1,0:T(8,128)(2,1)} %get-tuple-element.342) | copy-start | bytes 884740
  311.7 6.3 %copy-start.14 = (bf16[576,256]{1,0:T(8,128)(2,1)S(1)}, bf16[576,256]{1,0:T(8,128)(2,1)}, u32[]{:S(2)}) copy-start(bf16[576,256]{1,0:T(8,128)(2,1)} %copy-done.13) | copy-start | bytes 884740
  311.7 8.6 %copy-start.16 = (f32[12,768]{1,0:T(8,128)S(1)}, f32[12,768]{1,0:T(8,128)}, u32[]{:S(2)}) copy-start(f32[12,768]{1,0:T(8,128)} %add_add_fusion.2) | copy-start | bytes 110596
  320.3 8.4 %collective-permute-start.27 = (bf16[288,256]{1,0:T(8,128)(2,1)}, bf16[288,256]{1,0:T(8,128)(2,1)}, u32[]{:S(2)}, u32[]{:S(2)}) collective-permute-start(bf16[288,256]{1,0:T(8,128)(2,1)} %add_convert_fusion.20), channel_id=1, source_target_pairs={{0,16},{1,17},{2,18},{3,19},{4,20},{5,21},{6,22},{7,23},{8,24},{9,... | collective-permute-start | bytes 442376 | tf_op jit(solution)/shard_map/ppermute | solution.py:844
  332.5 7.0 %copy-start.17 = (f32[12,768]{1,0:T(8,128)S(1)}, f32[12,768]{1,0:T(8,128)}, u32[]{:S(2)}) copy-start(f32[12,768]{1,0:T(8,128)} %add_add_fusion.1) | copy-start | bytes 110596
  332.7 12.8 %copy-start = (bf16[4608,256]{1,0:T(8,128)(2,1)}, bf16[4608,256]{1,0:T(8,128)(2,1)S(1)}, u32[]{:S(2)}) copy-start(bf16[4608,256]{1,0:T(8,128)(2,1)S(1)} %pad_maximum_fusion.1.refs_1_.refs_2_) | copy-start | bytes 7077892
  332.7 22.5 %collective-permute-start.30 = (bf16[4608,256]{1,0:T(8,128)(2,1)S(1)}, bf16[4608,256]{1,0:T(8,128)(2,1)}, u32[]{:S(2)}, u32[]{:S(2)}) collective-permute-start(bf16[4608,256]{1,0:T(8,128)(2,1)S(1)} %pad_maximum_fusion.1.refs_1_.refs_2_), channel_id=1, source_target_pairs={{0,2},{2,0},{4,6},{6,4},{8,10},{10,8},{12,14},{14,12},{16,18},{18,... | collective-permute-start | bytes 7077896 | tf_op jit(solution)/shard_map/ppermute | solution.py:844
  338.7 13.6 %collective-permute-start.31 = (bf16[576,256]{1,0:T(8,128)(2,1)S(1)}, bf16[576,256]{1,0:T(8,128)(2,1)S(1)}, u32[]{:S(2)}, u32[]{:S(2)}) collective-permute-start(bf16[576,256]{1,0:T(8,128)(2,1)S(1)} %copy-done.4), channel_id=1, source_target_pairs={{0,8},{1,9},{2,3},{3,2},{4,12},{5,13},{6,7},{7,6},{8,0},{9,1},{10,... | collective-permute-start | bytes 884744 | tf_op jit(solution)/shard_map/ppermute | solution.py:844
  339.5 5.3 %collective-permute-start.25 = (f32[12,768]{1,0:T(8,128)S(1)}, f32[12,768]{1,0:T(8,128)S(1)}, u32[]{:S(2)}, u32[]{:S(2)}) collective-permute-start(f32[12,768]{1,0:T(8,128)S(1)} %copy-done.17), channel_id=1, source_target_pairs={{0,16},{2,18},{4,20},{6,22},{8,24},{10,26},{12,28},{14,30},{16,0},... | collective-permute-start | bytes 110600 | tf_op jit(solution)/shard_map/ppermute | solution.py:844
  352.4 11.6 %collective-permute-start.32 = (bf16[1152,256]{1,0:T(8,128)(2,1)S(1)}, bf16[1152,256]{1,0:T(8,128)(2,1)S(1)}, u32[]{:S(2)}, u32[]{:S(2)}) collective-permute-start(bf16[1152,256]{1,0:T(8,128)(2,1)S(1)} %pad_maximum_fusion.9), channel_id=1, source_target_pairs={{0,1},{1,0},{2,6},{3,7},{4,5},{5,4},{6,2},{7,3},{8,9},{9,8},{10,14... | collective-permute-start | bytes 1769480 | tf_op jit(solution)/shard_map/ppermute | solution.py:844
  355.2 7.4 %collective-permute-start.29 = (f32[3,768]{1,0:T(4,128)S(1)}, f32[3,768]{1,0:T(4,128)S(1)}, u32[]{:S(2)}, u32[]{:S(2)}) collective-permute-start(f32[3,768]{1,0:T(4,128)S(1)} %slice.45), channel_id=1, source_target_pairs={{0,1},{1,0},{2,3},{3,2},{4,5},{5,4},{6,7},{7,6},{8,9},{9,8},{10,11... | collective-permute-start | bytes 27656 | tf_op jit(solution)/shard_map/ppermute | solution.py:844
  364.2 16.8 %collective-permute-start.33 = (bf16[2304,256]{1,0:T(8,128)(2,1)S(1)}, bf16[2304,256]{1,0:T(8,128)(2,1)S(1)}, u32[]{:S(2)}, u32[]{:S(2)}) collective-permute-start(bf16[2304,256]{1,0:T(8,128)(2,1)S(1)} %pad_maximum_fusion.5), channel_id=1, source_target_pairs={{0,4},{1,5},{2,10},{3,11},{4,0},{5,1},{6,14},{7,15},{8,12},{9,13},... | collective-permute-start | bytes 3538952 | tf_op jit(solution)/shard_map/ppermute | solution.py:844
  381.3 8.6 %collective-permute-start.34 = (bf16[4608,256]{1,0:T(8,128)(2,1)S(1)}, bf16[4608,256]{1,0:T(8,128)(2,1)S(1)}, u32[]{:S(2)}, u32[]{:S(2)}) collective-permute-start(bf16[4608,256]{1,0:T(8,128)(2,1)S(1)} %pad_maximum_fusion.2.refs_1_), channel_id=1, source_target_pairs={{0,2},{1,3},{2,0},{3,1},{4,6},{5,7},{6,4},{7,5},{8,10},{9,11},{10,... | collective-permute-start | bytes 7077896 | tf_op jit(solution)/shard_map/ppermute | solution.py:844
  (12 other events, 37.1 us)

commit v3 on v2

--- a/solution.py
+++ b/solution.py
@@ -15,6 +15,7 @@
 GROUP_PAIRS = 2
 GROUPS = PAIRS // GROUP_PAIRS
 LANES = GROUP_PAIRS * PAIR
+SMALL = 128
 FF_BLOCK = 768
 
 masked_value = -1e30
@@ -53,50 +54,41 @@
 
 
 def cost(flops, moved, special=0):
-    del flops, moved, special
-    return pl.CostEstimate(flops=1, bytes_accessed=1, transcendentals=0)
+    return pl.CostEstimate(flops=flops, bytes_accessed=moved, transcendentals=special)
 
 
 class Order:
     def __init__(self):
-        self.zero = None
-
-    def tie(self, value):
-        value, self.zero = lax.optimization_barrier((value, self.zero))
-        return value
+        self.last = None
+
+    def after(self, *values):
+        if self.last is None:
+            return values
+        *values, _ = lax.optimization_barrier((*values, self.last))
+        return values
 
 
 def call(order, kernel, inputs, out_shape, name, estimate, scalars=(), grid=(), specs=None, outs=None,
          scratch=(), aliases=None):
-    tokens = () if order.zero is None else (order.zero,)
-    count = len(scalars) + len(inputs)
-    unused = len(tokens)
+    inputs = (*order.after(inputs[0]), *inputs[1:])
     vmem = pl.BlockSpec(memory_space=pltpu.VMEM)
-    given = len(out_shape)
-    end = count + unused + given
-
-    def body(*refs):
-        refs[end][0, 0] = 0
-        kernel(*refs[:count], *refs[count + unused : end], *refs[end + 1 :])
-
-    specs = [vmem] * len(inputs) if specs is None else list(specs)
-    outs = [vmem] * given if outs is None else list(outs)
-    *found, order.zero = pl.pallas_call(
-        body,
+    found = pl.pallas_call(
+        kernel,
         grid_spec=pltpu.PrefetchScalarGridSpec(
             num_scalar_prefetch=len(scalars),
             grid=grid,
-            in_specs=specs + [pl.BlockSpec(memory_space=pl.ANY)] * unused,
-            out_specs=outs + [pl.BlockSpec(memory_space=pltpu.SMEM)],
+            in_specs=[vmem] * len(inputs) if specs is None else list(specs),
+            out_specs=[vmem] * len(out_shape) if outs is None else list(outs),
             scratch_shapes=list(scratch),
         ),
-        out_shape=list(out_shape) + [jax.ShapeDtypeStruct((1, 1), jnp.int32)],
+        out_shape=list(out_shape),
         input_output_aliases=aliases or {},
         compiler_params=pltpu.CompilerParams(vmem_limit_bytes=VMEM_BYTES),
         cost_estimate=estimate,
         name=name,
-    )(*scalars, *inputs, *tokens)
-    return found if given > 1 else found[0]
+    )(*scalars, *inputs)
+    order.last = found[-1]
+    return found if len(found) > 1 else found[0]
 
 
 def shaped(shape, dtype):
@@ -150,9 +142,9 @@
     keys_ref,
     values_ref,
     bias_ref,
-    normed_ref,
-    out_ref,
+    *refs,
 ):
+    normed_ref, out_ref = refs[-2:]
     is_text = flag_ref[0] == 1
     hidden = jnp.where(is_text, far_ref[...].astype(f32), own_ref[...].astype(f32))
     gain = jnp.where(is_text, vec_ref[0:1], gain_ref[...])
@@ -165,15 +157,19 @@
     out_ref[:, width:] = (dot(normed, values_ref[...]) + bias_ref[1:2]).astype(bf16)
 
 
-def image_rows(order, flag, item, hidden, far, gain, shift, vecs, weight, bias, item_rows):
+def image_rows(
+    order, flag, item, hidden, far, gain, shift, vecs, weight, bias, item_rows, items, earlier
+):
     width = hidden.shape[1]
     place = item * (item_rows // IMG_PAD)
     half = lambda base: pl.BlockSpec((width, width), lambda *_: (0, base))
+    mine = lambda cols: pl.BlockSpec((IMG_PAD, cols), lambda *_: (item, 0))
+    inputs = (hidden, far, gain, shift, vecs, weight, weight, bias, *earlier)
     return call(
         order,
         image_kernel,
-        (hidden, far, gain, shift, vecs, weight, weight, bias),
-        [shaped((IMG_PAD, width), bf16), shaped((IMG_PAD, 2 * width), bf16)],
+        inputs,
+        [shaped((items * IMG_PAD, width), bf16), shaped((items * IMG_PAD, 2 * width), bf16)],
         "image_rows",
         cost(4 * IMG_PAD * width * width, 6 << 20),
         scalars=(flag,),
@@ -187,8 +183,10 @@
             half(1),
             half(2),
             resident(bias.shape),
-        ],
-        outs=[resident((IMG_PAD, width)), resident((IMG_PAD, 2 * width))],
+        ]
+        + [pl.BlockSpec(memory_space=pl.ANY)] * len(earlier),
+        outs=[mine(width), mine(2 * width)],
+        aliases={9: 0, 10: 1} if earlier else None,
     )
 
 
@@ -263,7 +261,7 @@
 def attend_forward(order, scalars, item, projected, image):
     rows = projected.shape[0] // 2
     spec = lambda base: pl.BlockSpec((rows, PAIR), lambda h, *_: (item, base + h))
-    far = lambda base: pl.BlockSpec((IMG_PAD, PAIR), lambda h, *_: (0, base + h))
+    far = lambda base: pl.BlockSpec((IMG_PAD, PAIR), lambda h, *_: (item, base + h))
     keys = rows + IMG_PAD
     return call(
         order,
@@ -351,7 +349,7 @@
 def attend_backward(order, scalars, item, start, pairs, projected, image, attended, grad, lse, earlier):
     rows, width = attended.shape
     spec = lambda base: pl.BlockSpec((rows, PAIR), lambda h, *_: (item, base + start + h))
-    far = lambda base: pl.BlockSpec((IMG_PAD, PAIR), lambda h, *_: (0, base + start + h))
+    far = lambda base: pl.BlockSpec((IMG_PAD, PAIR), lambda h, *_: (item, base + start + h))
     own = pl.BlockSpec((rows, PAIR), lambda h, *_: (0, start + h))
     far_outs = pl.BlockSpec((IMG_PAD, PAIR), lambda h, *_: (item, start + h))
     keys = rows + IMG_PAD
@@ -443,7 +441,6 @@
     gatt_ref,
     gproject_ref,
     gvec_ref,
-    gebias_ref,
     keep0_ref,
     send0_ref,
     keep1_ref,
@@ -497,7 +494,7 @@
             result[here, :] = x + reduce_bias_ref[...]
             gfeed[here, :] = jnp.zeros((block, width), f32)
 
-    pieces, gebias_ref[...] = feed_step(
+    pieces, gvec_ref[pl.ds(4 + step, 1), :] = feed_step(
         step, rows, item_rows, feed, top, result, gfeed, expand_ref, ebias_ref, reduce_ref
     )
     store_pieces(grads.at[step], pieces)
@@ -537,7 +534,7 @@
         total = dot(att0_ref[...], feed[:item_rows, :], TN)
         total += dot(att1_ref[...], feed[item_rows:, :], TN)
         gproject_ref[...] = total.astype(bf16)
-        gvec_ref[...] = jnp.concatenate(sums + [jnp.zeros((4, width), f32)], axis=0)
+        gvec_ref[0:4, :] = jnp.concatenate(sums, axis=0)
         for copy in copies:
             copy.wait()
         for which in range(steps):
@@ -562,8 +559,7 @@
             shaped((rows, width), f32),
             shaped((rows, width), bf16),
             shaped((width, width), bf16),
-            shaped((8, width), f32),
-            shaped((1, units), f32),
+            shaped((4 + steps, width), f32),
         ]
         + [shaped((steps // 2 * block_rows // 2, LANES), bf16)] * 4,
         "feed_forward",
@@ -581,8 +577,7 @@
             anywhere,
             anywhere,
             resident((width, width)),
-            resident((8, width)),
-            pl.BlockSpec((1, FF_BLOCK), lambda j, *_: (0, j)),
+            resident((4 + steps, width)),
         ]
         + [anywhere] * 4,
         scratch=[
@@ -610,81 +605,85 @@
     gik_ref,
     giv_ref,
     extra_ref,
+    sums_ref,
     keep_ref,
     send_ref,
-    query_ref,
-    value_ref,
-    turned,
-    image_turned,
+    keep,
+    send,
+    sems,
 ):
     step = pl.program_id(0)
-    kinds = pl.num_programs(0) // 4
-    part = step // kinds
+    width = normed_ref.shape[1]
+    half = width // 2
+    block = half * width // LANES
+
+    def copies(part):
+        rows = block if part < 4 else SMALL
+        span = pl.ds(part * block, rows)
+        pairs = ((keep, keep_ref), (send, send_ref))
+        return [
+            pltpu.make_async_copy(here.at[span], there.at[span], sems.at[number, part])
+            for number, (here, there) in enumerate(pairs)
+        ]
+
+    def store(part, total):
+        first = side_ref[0] == 0
+        mine = jnp.where(first, total[:half], total[half:]).astype(bf16)
+        other = jnp.where(first, total[half:], total[:half]).astype(bf16)
+        for number in range(width // LANES):
+            rows = slice(part * block + number * half, part * block + (number + 1) * half)
+            cols = slice(number * LANES, (number + 1) * LANES)
+            keep[rows, :] = mine[:, cols]
+            send[rows, :] = other[:, cols]
+        for copy in copies(part):
+            copy.start()
 
     @pl.when(step == 0)
     def _():
-        turned[...] = jnp.transpose(normed_ref[...].astype(f32)).astype(bf16)
-        image_turned[...] = jnp.transpose(image_ref[...].astype(f32)).astype(bf16)
-
-    def store(total):
-        half = total.shape[0] // 2
-        upper, lower = total[:half], total[half:]
-        first = side_ref[0] == 0
-        keep_ref[...] = jnp.where(first, upper, lower).astype(bf16)
-        send_ref[...] = jnp.where(first, lower, upper).astype(bf16)
-
-    @pl.when(part == 0)
+        store(0, dot(normed_ref[...], gq_ref[...], TN))
+        sums_ref[0:1] = column_sum(gq_ref[...].astype(f32))
+
+    @pl.when(step == 1)
     def _():
-        store(dot(turned[...], gq_ref[...]))
-        query_ref[...] = column_sum(gq_ref[...].astype(f32))
-
-    @pl.when(part == 1)
+        total = dot(normed_ref[...], gk_ref[...], TN)
+        store(1, total + dot(image_ref[...], gik_ref[...], TN))
+
+    @pl.when(step == 2)
     def _():
-        store(dot(turned[...], gk_ref[...]) + dot(image_turned[...], gik_ref[...]))
-
-    @pl.when(part == 2)
+        total = dot(normed_ref[...], gv_ref[...], TN)
+        store(2, total + dot(image_ref[...], giv_ref[...], TN))
+        sums = column_sum(gv_ref[...].astype(f32)) + column_sum(giv_ref[...].astype(f32))
+        sums_ref[1:2] = sums
+
+    @pl.when(step == 3)
     def _():
-        store(dot(turned[...], gv_ref[...]) + dot(image_turned[...], giv_ref[...]))
-        sums = column_sum(gv_ref[...].astype(f32)) + column_sum(giv_ref[...].astype(f32))
-        value_ref[...] = sums
-
-    @pl.when(part == 3)
-    def _():
-        store(extra_ref[...].astype(f32))
+        store(3, extra_ref[...].astype(f32))
+        keep[4 * block :, :] = jnp.zeros((SMALL, LANES), bf16)
+        send[4 * block :, :] = jnp.zeros((SMALL, LANES), bf16)
+        for copy in copies(4):
+            copy.start()
+        for part in range(5):
+            for copy in copies(part):
+                copy.wait()
 
 
 def weight_grads(order, side, normed, image, grads, extra):
     rows, width = normed.shape
-    image_rows = image.shape[0]
-    kinds = width // LANES
-    tall = width // 2
-
-    def column(height, part):
-        place = lambda s, *_: (0, jnp.clip(s - part * kinds, 0, kinds - 1))
-        return pl.BlockSpec((height, LANES), place)
-
-    half = pl.BlockSpec((tall, LANES), lambda s, *_: (s, 0))
+    all_rows = 4 * (width * width // 2 // LANES) + SMALL
+    inputs = (normed, image, *grads, extra)
+    anywhere = pl.BlockSpec(memory_space=pl.ANY)
     return call(
         order,
         weight_kernel,
-        (normed, image, *grads, extra),
-        [shaped((4 * kinds * tall, LANES), bf16)] * 2 + [shaped((1, width), f32)] * 2,
+        inputs,
+        [shaped((2, width), f32)] + [shaped((all_rows, LANES), bf16)] * 2,
         "weight_grads",
         cost(8 * rows * width * width, 12 << 20),
         scalars=(side,),
-        grid=(4 * kinds,),
-        specs=[
-            resident(normed.shape),
-            resident(image.shape),
-            column(rows, 0),
-            column(rows, 1),
-            column(rows, 2),
-            column(image_rows, 1),
-            column(image_rows, 2),
-            column(width, 3),
-        ],
-        outs=[half, half, column(1, 0), column(1, 2)],
-        scratch=[pltpu.VMEM((width, rows), bf16), pltpu.VMEM((width, image_rows), bf16)],
+        grid=(4,),
+        specs=[resident(value.shape) for value in inputs],
+        outs=[resident((2, width)), anywhere, anywhere],
+        scratch=[pltpu.VMEM((all_rows, LANES), bf16)] * 2 + [pltpu.SemaphoreType.DMA((2, 5))],
     )
 
 
@@ -720,86 +719,107 @@
     gv_ref,
     gain_ref,
     weight_ref,
+    feed_sums_ref,
+    bias_sums_ref,
+    _,
     out_ref,
-    sums_ref,
+    small_ref,
+    sums,
 ):
-    rows, width = hid_ref.shape
-    sums = [jnp.zeros((1, width), f32)] * 2
-    for start in range(0, rows, IMG_PAD):
-        here = slice(start, start + IMG_PAD)
-        joined = jnp.concatenate([gq_ref[here, :], gk_ref[here, :], gv_ref[here, :]], axis=1)
-        grad = dot(joined, weight_ref[...], NT)
-        unit, scale = normalise(hid_ref[here, :].astype(f32))
-        if start == 0:
-            both = near_ref[...].astype(f32) + far_ref[...].astype(f32)
-            grad = grad + jnp.where(flag_ref[0] == 1, 0.0, both)
-        sums = [sums[0] + column_sum(grad * unit), sums[1] + column_sum(grad)]
-        total = gmid_ref[here, :] + norm_transpose(unit, scale, gain_ref[...], grad)
-        out_ref[here, :] = total.astype(bf16)
-    sums = jnp.concatenate(sums, axis=0)
-
-    @pl.when(pl.program_id(0) == 0)
+    item, block = pl.program_id(0), pl.program_id(1)
+    joined = jnp.concatenate([gq_ref[...], gk_ref[...], gv_ref[...]], axis=1)
+    grad = dot(joined, weight_ref[...], NT)
+    unit, scale = normalise(hid_ref[...].astype(f32))
+    both = near_ref[...].astype(f32) + far_ref[...].astype(f32)
+    grad = grad + jnp.where((flag_ref[0] == 0) & (block == 0), both, 0.0)
+    total = gmid_ref[...] + norm_transpose(unit, scale, gain_ref[...], grad)
+    out_ref[...] = total.astype(bf16)
+    found = jnp.concatenate([column_sum(grad * unit), column_sum(grad)], axis=0)
+
+    @pl.when((item == 0) & (block == 0))
     def _():
-        sums_ref[...] = sums
-
-    @pl.when(pl.program_id(0) > 0)
+        sums[...] = jnp.zeros(sums.shape, f32)
+
+    sums[0:2] += found
+
+    @pl.when((item == pl.num_programs(0) - 1) & (block == pl.num_programs(1) - 1))
     def _():
-        sums_ref[...] += sums
-
-
-def finish_rows(order, flag, hidden, gmid, near, far, grads, gain, weight, item_rows):
+        width = sums.shape[1]
+        pad = lambda count: jnp.zeros((count, width), f32)
+        own = [sums[0:2], feed_sums_ref[0:3], feed_sums_ref[4:8], pad(7)]
+        own = jnp.concatenate(own, axis=0)
+        shared = [pad(9), feed_sums_ref[3:4], bias_sums_ref[...], pad(4)]
+        shared = jnp.concatenate(shared, axis=0)
+        is_text = flag_ref[0] == 1
+        first = jnp.where(is_text, 0.0, own) + shared
+        rows = jnp.concatenate([first, jnp.where(is_text, own, 0.0)], axis=0).astype(bf16)
+        count = rows.shape[0]
+        for number in range(width // LANES):
+            cols = slice(number * LANES, (number + 1) * LANES)
+            small_ref[number * count : (number + 1) * count, :] = rows[:, cols]
+        small_ref[width // LANES * count :, :] = jnp.zeros((SMALL - width // LANES * count, LANES), bf16)
+
+
+def finish_rows(
+    order, flag, hidden, gmid, near, far, grads, gain, weight, feed_sums, bias_sums, keep, item_rows
+):
     rows, width = hidden.shape
-    items = rows // item_rows
-    mine = pl.BlockSpec((item_rows, width), lambda i, *_: (i, 0))
-    image = pl.BlockSpec((IMG_PAD, width), lambda i, *_: (i, 0))
+    blocks = item_rows // IMG_PAD
+    mine = pl.BlockSpec((IMG_PAD, width), lambda i, j, *_: (i * blocks + j, 0))
+    image = pl.BlockSpec((IMG_PAD, width), lambda i, j, *_: (i, 0))
+    fixed = (gain, weight, feed_sums, bias_sums)
+    place = keep.shape[0] // SMALL - 1
     return call(
         order,
         finish_kernel,
-        (hidden, gmid, near, far, *grads, gain, weight),
-        [shaped((rows, width), bf16), shaped((2, width), f32)],
+        (hidden, gmid, near, far, *grads, *fixed, keep),
+        [shaped((rows, width), bf16), shaped(keep.shape, bf16)],
         "finish_rows",
         cost(6 * rows * width * width, 16 << 20),
         scalars=(flag,),
-        grid=(items,),
-        specs=[mine, mine, image, image, mine, mine, mine, resident(gain.shape), resident(weight.shape)],
-        outs=[mine, resident((2, width))],
-    )
-
-
-def expert_kernel(half_ref, greduce_ref, gexpand_ref, *refs):
-    reduce_ref, expand_ref = refs[-2:]
-    reduce_ref[...] = greduce_ref[...].astype(f32)
-    expand_ref[...] = gexpand_ref[...].astype(f32)
-
-
-def expert_outputs(order, halves, first, value, width, units, earlier):
-    parts = width // LANES
+        grid=(rows // item_rows, blocks),
+        specs=[mine, mine, image, image, mine, mine, mine]
+        + [resident(value.shape) for value in fixed]
+        + [pl.BlockSpec(memory_space=pl.ANY)],
+        outs=[mine, pl.BlockSpec((SMALL, LANES), lambda *_: (place, 0))],
+        scratch=[pltpu.VMEM((8, width), f32)],
+        aliases={12: 1},
+    )
+
+
+def expert_kernel(half_ref, value_ref, *refs):
+    at = 0
+    for out in refs[-2:]:
+        tall = out.shape[0]
+        for part in range(out.shape[1] // LANES):
+            piece = value_ref[at : at + tall, :]
+            out[:, part * LANES : (part + 1) * LANES] = piece.astype(f32)
+            at += tall
+
+
+def expert_outputs(order, half, first, value, width, units, earlier):
     tall = width // 2
-    count = halves.shape[0]
-    blocks = value.shape[0] // (count * 2 * parts * tall)
-    source = lambda base: pl.BlockSpec(
-        (tall, LANES), lambda i, h, p, *_: ((i * count + h) * 2 * parts + base + p, 0)
-    )
+    block_rows = 2 * width // LANES * tall
     return call(
         order,
         expert_kernel,
-        (value, value, *earlier),
+        (value, *earlier),
         [shaped((units, width), f32), shaped((width, units), f32)],
         "expert_outputs",
         cost(value.size, 6 * value.size),
-        scalars=(halves,),
-        grid=(blocks, count, parts),
-        specs=[source(0), source(parts)] + [pl.BlockSpec(memory_space=pl.ANY)] * len(earlier),
+        scalars=(half,),
+        grid=(value.shape[0] // block_rows,),
+        specs=[pl.BlockSpec((block_rows, LANES), lambda i, at: (i, 0))]
+        + [pl.BlockSpec(memory_space=pl.ANY)] * len(earlier),
         outs=[
-            pl.BlockSpec((tall, LANES), lambda i, h, p, half: (2 * (first + i) + half[h], p)),
-            pl.BlockSpec((tall, LANES), lambda i, h, p, half: (half[h], (first + i) * parts + p)),
+            pl.BlockSpec((tall, width), lambda i, at: (2 * (first + i) + at[0], 0)),
+            pl.BlockSpec((tall, width), lambda i, at: (at[0], first + i)),
         ],
-        aliases={3: 0, 4: 1} if earlier else None,
-    )
-
-
-def projection_kernel(half_ref, value_ref, *refs):
-    in_ref, out_ref = refs[-2:]
+        aliases={2: 0, 3: 1} if earlier else None,
+    )
+
+
+def store_projection(value_ref, in_ref, out_ref):
     tall, wide = in_ref.shape
 
     def store(ref):
@@ -816,24 +836,72 @@
         store(out_ref)
 
 
-def projection_outputs(order, half, value, width, earlier):
+def projection_kernel(half_ref, value_ref, in_ref, out_ref):
+    store_projection(value_ref, in_ref, out_ref)
+
+
+def last_kernel(half_ref, flag_ref, value_ref, mine_ref, got_ref, *refs):
+    in_ref, out_ref, *vec_refs, expand_ref, pair_ref, project_ref = refs[2:]
+    store_projection(value_ref, in_ref, out_ref)
+
+    @pl.when(pl.program_id(0) == 0)
+    def _():
+        both = mine_ref[...].astype(f32) + got_ref[...].astype(f32)
+        width = vec_refs[0].shape[1]
+        rows = jnp.concatenate([both[at * 32 : (at + 1) * 32] for at in range(width // LANES)], axis=1)
+        own = jnp.where(flag_ref[0] == 1, rows[16:], rows[:16])
+        for number, ref in enumerate(vec_refs):
+            ref[...] = own[number : number + 1]
+        for number in range(expand_ref.shape[1] // width):
+            cols = slice(number * width, (number + 1) * width)
+            expand_ref[:, cols] = own[5 + number : 6 + number]
+        project_ref[...] = rows[9:10]
+        pair_ref[...] = rows[10:12]
+
+
+def projection_specs(width):
     tall = width // 2
+    value = pl.BlockSpec((tall * width // LANES, LANES), lambda b, *_: (b, 0))
+    outs = [
+        pl.BlockSpec((tall, width), lambda b, at, *_: (at[0], jnp.minimum(b, 2))),
+        pl.BlockSpec((tall, width), lambda b, at, *_: (at[0], 0)),
+    ]
+    return value, outs, [shaped((width, 3 * width), f32), shaped((width, width), f32)]
+
+
+def projection_outputs(order, half, value, width):
+    spec, outs, shapes = projection_specs(width)
     return call(
         order,
         projection_kernel,
-        (value, *earlier),
-        [shaped((width, 3 * width), f32), shaped((width, width), f32)],
+        (value,),
+        shapes,
         "projection_outputs",
         cost(value.size, 6 * value.size),
         scalars=(half,),
         grid=(4,),
-        specs=[pl.BlockSpec((tall * width // LANES, LANES), lambda b, at: (b, 0))]
-        + [pl.BlockSpec(memory_space=pl.ANY)] * len(earlier),
-        outs=[
-            pl.BlockSpec((tall, width), lambda b, at: (at[0], jnp.minimum(b, 2))),
-            pl.BlockSpec((tall, width), lambda b, at: (at[0], 0)),
-        ],
-        aliases={2: 0, 3: 1} if earlier else None,
+        specs=[spec],
+        outs=outs,
+    )
+
+
+def last_outputs(order, half, flag, mine, got, width, units, earlier):
+    spec, outs, shapes = projection_specs(width)
+    place = got.shape[0] // SMALL - 1
+    small = pl.BlockSpec((SMALL, LANES), lambda *_: (place, 0))
+    vecs = [(1, width)] * 5 + [(1, units), (2, width), (1, width)]
+    return call(
+        order,
+        last_kernel,
+        (got, mine, got, *earlier),
+        shapes + [shaped(shape, f32) for shape in vecs],
+        "last_outputs",
+        cost(got.size, 6 * got.size),
+        scalars=(half, flag),
+        grid=(4,),
+        specs=[spec, small, small] + [pl.BlockSpec(memory_space=pl.ANY)] * 2,
+        outs=outs + [resident(shape) for shape in vecs],
+        aliases={5: 0, 6: 1},
     )
 
 
@@ -889,44 +957,27 @@
         return (cut(self.terms[0]) + cut(self.terms[1])).astype(bf16)
 
     def step(self):
-        zero = self.order.zero[0, 0]
         if self.left:
             pair = self.left.pop(0)
+            self.terms = self.order.after(*self.terms)
             half = self.terms[0].shape[0] // 2
-            side = self.sides[pair] + zero
+            side = self.sides[pair]
             sent = self.part(1 - side, half)
-            sent = self.order.tie(sent)
             self.terms = (self.part(side, half), self.exchange(sent, pair))
+            self.order.last = sent
             return
         pair = self.back.pop()
         if self.mine is None:
-            self.mine = self.part(zero, self.terms[0].shape[0])
+            self.terms = self.order.after(*self.terms)
+            self.mine = (self.terms[0].astype(f32) + self.terms[1].astype(f32)).astype(bf16)
         else:
-            first = self.last + zero == 0
-            low = jnp.where(first, self.mine, self.got)
-            high = jnp.where(first, self.got, self.mine)
+            mine, got = self.order.after(self.mine, self.got)
+            low = jnp.where(self.last == 0, mine, got)
+            high = jnp.where(self.last == 0, got, mine)
             self.mine = jnp.concatenate([low, high], axis=0)
-        self.mine = self.order.tie(self.mine)
+        self.order.last = self.mine
         self.last = self.sides[pair]
         self.exchange(self.mine, pair)
-
-
-class Doubling:
-    def __init__(self, order, value, axis):
-        self.order, self.value, self.axis = order, value, axis
-        self.bits = list(range(lax.axis_size(axis).bit_length() - 1))
-        self.start()
-
-    def start(self):
-        bit = self.bits.pop(0)
-        self.got = swap(self.value, (self.axis,), lambda source: source ^ (1 << bit))
-
-    def step(self):
-        total = self.value + self.got + self.order.zero[0, 0].astype(f32)
-        self.value = self.order.tie(total)
-        if self.bits:
-            self.start()
-        return self.value
 
 
 def on_device(
@@ -962,9 +1013,9 @@
         order, hidden, attend_gain, attend_shift, project_in, bias_pair
     )
     scalars = (flag, image_count, text_lengths)
-    normed_images, image_pairs, attended, lses = [], [], [], []
+    images, attended, lses = (), [], []
     for item in range(items):
-        normed_image, image_pair = image_rows(
+        images = image_rows(
             order,
             flag,
             item,
@@ -976,10 +1027,10 @@
             project_in,
             bias_pair,
             rows,
+            items,
+            images,
         )
-        out, lse = attend_forward(order, scalars, item, projected, image_pair)
-        normed_images.append(normed_image)
-        image_pairs.append(image_pair)
+        out, lse = attend_forward(order, scalars, item, projected, images[1])
         attended.append(out)
         lses.append(lse)
 
@@ -989,8 +1040,7 @@
         grad_middle,
         grad_attended,
         project_out_grad,
-        vec_grads,
-        expand_bias_grad,
+        feed_sums,
         keep0,
         send0,
         keep1,
@@ -1022,7 +1072,7 @@
             start,
             pairs,
             projected,
-            image_pairs[item],
+            images[1],
             attended[item],
             grad_attended,
             lses[item],
@@ -1044,64 +1094,74 @@
     c.step()
     near = image_grads(order, project_in, grads[3], grads[4])
     far = to_image(near)
-    images = jnp.concatenate(normed_images, axis=0)
-    keep, send, query_sums, value_sums = weight_grads(
-        order, side, normed, images, grads, project_out_grad
-    )
-    p = Total(order, ("dp", "mod"), keep, send)
     c.step()
     a.step()
+    bias_sums, keep, send = weight_grads(order, side, normed, images[0], grads, project_out_grad)
+    p = Total(order, ("dp", "mod"), keep, send)
+    (far,) = order.after(far)
+    order.last = far
+    c.step()
+    a.step()
+    grad_in, keep = finish_rows(
+        order,
+        flag,
+        hidden,
+        grad_middle,
+        near,
+        far,
+        grads[:3],
+        attend_gain,
+        project_in,
+        feed_sums,
+        bias_sums,
+        keep,
+        rows,
+    )
+    p.terms = (keep, p.got)
     p.step()
-    grad_in, attend_sums = finish_rows(
-        order, flag, hidden, grad_middle, near, far, grads[:3], attend_gain, project_in, rows
-    )
-    ebias_rows = expand_bias_grad.reshape(-1, width)
-    small = [attend_sums, vec_grads[:3], ebias_rows, vec_grads[3:4], query_sums, value_sums]
-    small = Doubling(order, jnp.concatenate(small, axis=0), "dp")
-    a.step()
     c.step()
     p.step()
-    small.step()
+    a.step()
     p.step()
-    a.step()
-    small.step()
+    p.step()
+    outputs = expert_outputs(order, side, 0, a.mine, width, units, ())
     p.step()
     c.step()
-    outputs = expert_outputs(order, side, 0, a.mine, width, units, ())
-    p.step()
-    small.step()
     outputs = expert_outputs(order, 1 - side, 0, a.got, width, units, outputs)
     p.step()
-    c.step()
-    while small.bits:
-        small.step()
-    small = small.step()
-    shared = Doubling(order, small[-3:], "mod")
     outputs = expert_outputs(order, side, 2, c.mine, width, units, outputs)
     p.step()
     reduce_grad, expand_grad = expert_outputs(order, 1 - side, 2, c.got, width, units, outputs)
-    shared = shared.step()
     while p.back:
         p.step()
-    projections = projection_outputs(order, side, p.mine, width, ())
-    project_in_grad, project_out_grad = projection_outputs(
-        order, 1 - side, p.got, width, projections
-    )
+    projections = projection_outputs(order, side, p.mine, width)
+    (
+        project_in_grad,
+        project_out_grad,
+        attend_gain_grad,
+        attend_shift_grad,
+        feed_gain_grad,
+        feed_shift_grad,
+        reduce_bias_grad,
+        expand_bias_grad,
+        bias_pair_grad,
+        project_bias_grad,
+    ) = last_outputs(order, 1 - side, flag, p.mine, p.got, width, units, projections)
     return (
         hidden_out.reshape(hidden_in.shape),
         grad_in.reshape(hidden_in.shape),
-        small[0:1],
-        small[1:2],
+        attend_gain_grad,
+        attend_shift_grad,
         project_in_grad,
-        shared[1:3],
+        bias_pair_grad,
         project_out_grad,
-        shared[0],
-        small[2:3],
-        small[3:4],
+        project_bias_grad[0],
+        feed_gain_grad,
+        feed_shift_grad,
         expand_grad[None],
-        small[5:-3].reshape(1, -1),
+        expand_bias_grad,
         reduce_grad[None],
-        small[4:5],
+        reduce_bias_grad,
     )
 
 

time: 405 us -> 367 us (0.906)
  waiting for transfers between devices: 67.6 us -> 111 us
  Pallas kernels: 210 us -> 186 us
  starting transfers between devices: 51.6 us -> 31.1 us
  between operations: 18.1 us -> 1.59 us
  other arithmetic: 38.6 us -> 23.8 us
  local copies, waits for them, and re-layouts: 11.6 us -> 7.43 us
    ppermute x31 -> x26, waiting for transfers between devices: 62.5 us -> 111 us  [swap(): lax.ppermute(value, axes, [(source, pair_of(source)) for source in range(...]
    pallas_call x21, Pallas kernels: 210 us -> 186 us  [call(): pl.pallas_call(kernel, grid_spec=pltpu.PrefetchScalarGridSpec(num_scalar_...]
    ppermute x31 -> x26, starting transfers between devices: 42.9 us -> 22.3 us  [swap(): lax.ppermute(value, axes, [(source, pair_of(source)) for source in range(...]
    convert_element_type x13 -> x10, other arithmetic: 24.2 us -> 14.4 us  [part(): return (cut(self.terms[0]) + cut(self.terms[1])).astype(bf16)]
    ppermute x3, waiting for transfers between devices: 5.1 us -> 0.01 us  [on_device(): to_text = lambda value: lax.ppermute(value, 'mod', [(0, 1)])]
    add x5 -> x0, other arithmetic: 4.87 us -> none  [step(): total = self.value + self.got + self.order.zero[0, 0].astype(f32)]
  transfers between devices with their start and end apart: 35 -> 30, of which waited for: 16 -> 14; matrix products, arithmetic and copies ran while one was open for 10% -> 6% of each run, Pallas kernels for 30% -> 33%
where the time goes in v3:
time: 367 us; the launch traced here: 361 us
  Pallas kernels  186 us (51%)
  waiting for transfers between devices  111 us (30%)
  starting transfers between devices  31.1 us (8%)
  other arithmetic  23.8 us (6%)
  local copies, waits for them, and re-layouts  7.43 us (2%)
    pallas_call x21, Pallas kernels, call(): pl.pallas_call(kernel, grid_spec=pltpu.PrefetchScalarGridSpec(num_scalar_...  186 us
    ppermute x26, waiting for transfers between devices, swap(): lax.ppermute(value, axes, [(source, pair_of(source)) for source in range(...  111 us
    ppermute x26, starting transfers between devices, swap(): lax.ppermute(value, axes, [(source, pair_of(source)) for source in range(...  22.3 us
    convert_element_type x10, other arithmetic, part(): return (cut(self.terms[0]) + cut(self.terms[1])).astype(bf16)  14.4 us
    ppermute x3, starting transfers between devices, on_device(): to_text = lambda value: lax.ppermute(value, 'mod', [(0, 1)])  7.5 us
  transfers between devices with their start and end apart: 30, of which 14 were waited for; matrix products, arithmetic and copies ran while one was open for 6% of the time, Pallas kernels for 33%

profile of v3, /device:TPU:0, one launch (start us, length us, event | category | flops | bytes accessed | tf_op | source)
XLA Modules:
  0.0 361.5 jit_solution(2673267553072987215)
XLA Ops:
  1.8 4.9 %collective-permute-start = (bf16[256,768]{1,0:T(8,128)(2,1)S(1)}, bf16[256,768]{1,0:T(8,128)(2,1)S(1)}, u32[]{:S(2)}, u32[]{:S(2)}) collective-permute-start(bf16[256,768]{1,0:T(8,128)(2,1)S(1)} %get-tuple-element.329), channel_id=1, source_target_pairs={{0,1},{2,3},{4,5},{6,7},{8,9},{10,11},{12,13},{14,15},{16,17},{18,... | collective-permute-start | bytes 1179656 | tf_op jit(solution)/shard_map/ppermute | solution.py:1006
  9.4 8.5 %project_rows.1 = (bf16[1024,768]{1,0:T(8,128)(2,1)}, bf16[1024,2304]{1,0:T(8,128)(2,1)}) custom-call(bf16[1024,768]{1,0:T(8,128)(2,1)} %bitcast.20, f32[1,768]{1,0:T(1,128)} %gain_ref.9, f32[1,768]{1,0:T(1,128)} %shift_ref.6, bf16[768,2304]{1,0:T(8,128)(2,1)} %weight_ref.3, f32[2,768]{1,0:T(2,128)} %bias_ref.5), custom_call_target="tpu_custom_call" | custom-call | flops 3623878656 | bytes 11403264 | tf_op jit(solution)/shard_map/project_rows/pallas_call | solution.py:75
  19.2 3.8 %image_rows.2 = (bf16[512,768]{1,0:T(8,128)(2,1)}, bf16[512,1536]{1,0:T(8,128)(2,1)}) custom-call(s32[1]{0:T(128)} %bitcast.flag_ref, bf16[1024,768]{1,0:T(8,128)(2,1)} %bitcast.21, bf16[256,768]{1,0:T(8,128)(2,1)} %copy-done.8, f32[1,768]{1,0:T(1,128)} %gain_ref.9, f32[1,768]{1,0:T(1,128)} %shift_ref.6, f32[2,768]{1,0:T(2,128)} %copy-done.11, ...), custom_call_target="tpu_custom_call" | custom-call | flops 603979776 | bytes 6291456 | tf_op jit(solution)/shard_map/image_rows/pallas_call | solution.py:75
  23.1 12.3 %attend_forward.2 = (bf16[512,768]{1,0:T(8,128)(2,1)}, f32[6,2,512]{2,1,0:T(2,128)}) custom-call(s32[1]{0:T(128)} %bitcast.flag_ref, s32[2]{0:T(128)} %count_ref.17, s32[2,4]{1,0:T(2,128)} %lengths_ref.15, bf16[1024,2304]{1,0:T(8,128)(2,1)} %get-tuple-element.210.q_ref.k_ref.v_ref, bf16[1024,2304]{1,0:T(8,128)(2,1)} %get-tuple-element.210.q_ref.k_ref.v_ref, ...), custom_call_target="tpu_custom_call" | custom-call | flops 4831838208 | bytes 6291456 | tf_op jit(solution)/shard_map/attend_forward/pallas_call | solution.py:75
  36.1 3.8 %image_rows.3 = (bf16[512,768]{1,0:T(8,128)(2,1)}, bf16[512,1536]{1,0:T(8,128)(2,1)}) custom-call(s32[1]{0:T(128)} %bitcast.flag_ref, bf16[1024,768]{1,0:T(8,128)(2,1)} %bitcast.22, bf16[256,768]{1,0:T(8,128)(2,1)} %copy-done.7, f32[1,768]{1,0:T(1,128)} %gain_ref.9, f32[1,768]{1,0:T(1,128)} %shift_ref.6, ...), custom_call_target="tpu_custom_call", output_to_operand_aliasing={{0}: (9, {}), {1}: (10, {})} | custom-call | flops 603979776 | bytes 6291456 | tf_op jit(solution)/shard_map/image_rows/pallas_call | solution.py:75
  39.9 12.2 %attend_forward.3 = (bf16[512,768]{1,0:T(8,128)(2,1)}, f32[6,2,512]{2,1,0:T(2,128)}) custom-call(s32[1]{0:T(128)} %bitcast.flag_ref, s32[2]{0:T(128)} %count_ref.17, s32[2,4]{1,0:T(2,128)} %lengths_ref.15, bf16[1024,2304]{1,0:T(8,128)(2,1)} %get-tuple-element.210.q_ref.k_ref.v_ref, bf16[1024,2304]{1,0:T(8,128)(2,1)} %get-tuple-element.210.q_ref.k_ref.v_ref, ...), custom_call_target="tpu_custom_call" | custom-call | flops 4831838208 | bytes 6291456 | tf_op jit(solution)/shard_map/attend_forward/pallas_call | solution.py:75
  52.2 45.2 %feed_forward.1 = (bf16[1024,768]{1,0:T(8,128)(2,1)}, f32[1024,768]{1,0:T(8,128)}, bf16[1024,768]{1,0:T(8,128)(2,1)}, bf16[768,768]{1,0:T(8,128)(2,1)}, f32[8,76...) custom-call(s32[1]{0:T(128)} %bitcast.flag_ref, ...), custom_call_target="tpu_custom_call" | custom-call | flops 28991029248 | bytes 41943040 | tf_op jit(solution)/shard_map/feed_forward/pallas_call | solution.py:75
  98.0 8.2 %attend_backward.6 = (bf16[1024,768]{1,0:T(8,128)(2,1)}, bf16[1024,768]{1,0:T(8,128)(2,1)}, bf16[1024,768]{1,0:T(8,128)(2,1)}, bf16[512,768]{1,0:T(8,128)(2,1)}, bf16[512,768]{1,0:T(8,128)(2,1)}) custom-call(s32[1]{0:T(128)} %bitcast.flag_ref, s32[2]{0:T(128)} %count_ref.17, s32[2,4]{1,0:T(2,128)} %lengths_ref.15, ...), custom_call_target="tpu_custom_call" | custom-call | flops 4026531840 | bytes 4194304 | tf_op jit(solution)/shard_map/attend_backward/pallas_call | solution.py:75
  107.7 3.2 add_convert_fusion.4
  112.4 8.2 %attend_backward.7 = (bf16[1024,768]{1,0:T(8,128)(2,1)}, bf16[1024,768]{1,0:T(8,128)(2,1)}, bf16[1024,768]{1,0:T(8,128)(2,1)}, bf16[512,768]{1,0:T(8,128)(2,1)}, bf16[512,768]{1,0:T(8,128)(2,1)}) custom-call(s32[1]{0:T(128)} %bitcast.flag_ref, s32[2]{0:T(128)} %count_ref.17, ...), custom_call_target="tpu_custom_call", output_to_operand_aliasing={{0}: (11, {}), {1}: (12, {}), {2}: (13, {}), {3}: (14, {}),... | custom-call | flops 4026531840 | bytes 4194304 | tf_op jit(solution)/shard_map/attend_backward/pallas_call | solution.py:75
  120.6 3.2 add_convert_fusion.2
  124.4 8.1 %attend_backward.8 = (bf16[1024,768]{1,0:T(8,128)(2,1)}, bf16[1024,768]{1,0:T(8,128)(2,1)}, bf16[1024,768]{1,0:T(8,128)(2,1)}, bf16[512,768]{1,0:T(8,128)(2,1)}, bf16[512,768]{1,0:T(8,128)(2,1)}) custom-call(s32[1]{0:T(128)} %bitcast.flag_ref, s32[2]{0:T(128)} %count_ref.17, ...), custom_call_target="tpu_custom_call", output_to_operand_aliasing={{0}: (11, {}), {1}: (12, {}), {2}: (13, {}), {3}: (14, {}),... | custom-call | flops 4026531840 | bytes 4194304 | tf_op jit(solution)/shard_map/attend_backward/pallas_call | solution.py:75
  132.8 2.7 collective-permute-start.6
  135.4 8.3 %attend_backward.9 = (bf16[1024,768]{1,0:T(8,128)(2,1)}, bf16[1024,768]{1,0:T(8,128)(2,1)}, bf16[1024,768]{1,0:T(8,128)(2,1)}, bf16[512,768]{1,0:T(8,128)(2,1)}, bf16[512,768]{1,0:T(8,128)(2,1)}) custom-call(s32[1]{0:T(128)} %bitcast.flag_ref, s32[2]{0:T(128)} %count_ref.17, ...), custom_call_target="tpu_custom_call", output_to_operand_aliasing={{0}: (11, {}), {1}: (12, {}), {2}: (13, {}), {3}: (14, {}),... | custom-call | flops 4026531840 | bytes 4194304 | tf_op jit(solution)/shard_map/attend_backward/pallas_call | solution.py:75
  143.7 1.9 collective-permute-done.7
  145.6 1.5 add_convert_fusion.8
  147.1 2.6 collective-permute-start.10
  149.7 8.1 %attend_backward.10 = (bf16[1024,768]{1,0:T(8,128)(2,1)}, bf16[1024,768]{1,0:T(8,128)(2,1)}, bf16[1024,768]{1,0:T(8,128)(2,1)}, bf16[512,768]{1,0:T(8,128)(2,1)}, bf16[512,768]{1,0:T(8,128)(2,1)}) custom-call(s32[1]{0:T(128)} %bitcast.flag_ref, s32[2]{0:T(128)} %count_ref.17, ...), custom_call_target="tpu_custom_call", output_to_operand_aliasing={{0}: (11, {}), {1}: (12, {}), {2}: (13, {}), {3}: (14, {}),... | custom-call | flops 4026531840 | bytes 4194304 | tf_op jit(solution)/shard_map/attend_backward/pallas_call | solution.py:75
  158.0 1.7 collective-permute-start.8
  159.7 8.1 %attend_backward.11 = (bf16[1024,768]{1,0:T(8,128)(2,1)}, bf16[1024,768]{1,0:T(8,128)(2,1)}, bf16[1024,768]{1,0:T(8,128)(2,1)}, bf16[512,768]{1,0:T(8,128)(2,1)}, bf16[512,768]{1,0:T(8,128)(2,1)}) custom-call(s32[1]{0:T(128)} %bitcast.flag_ref, s32[2]{0:T(128)} %count_ref.17, ...), custom_call_target="tpu_custom_call", output_to_operand_aliasing={{0}: (11, {}), {1}: (12, {}), {2}: (13, {}), {3}: (14, {}),... | custom-call | flops 4026531840 | bytes 4194304 | tf_op jit(solution)/shard_map/attend_backward/pallas_call | solution.py:75
  167.7 5.4 %collective-permute-done.8 = bf16[576,256]{1,0:T(8,128)(2,1)S(1)} collective-permute-done((bf16[576,256]{1,0:T(8,128)(2,1)S(1)}, bf16[576,256]{1,0:T(8,128)(2,1)S(1)}, u32[]{:S(2)}, u32[]{:S(2)}) %collective-permute-start.8) | collective-permute-done | bytes 294944 | tf_op jit(solution)/shard_map/ppermute | solution.py:912
  173.4 4.5 %collective-permute-start.11 = (bf16[576,256]{1,0:T(8,128)(2,1)S(1)}, bf16[576,256]{1,0:T(8,128)(2,1)S(1)}, u32[]{:S(2)}, u32[]{:S(2)}) collective-permute-start(bf16[576,256]{1,0:T(8,128)(2,1)S(1)} %get-tuple-element.338), channel_id=1, source_target_pairs={{0,8},{2,18},{4,12},{6,22},{8,0},{10,26},{12,4},{14,30},{16,24},{1... | collective-permute-start | bytes 884744 | tf_op jit(solution)/shard_map/ppermute | solution.py:912
  178.0 4.4 %image_grads.1.near_ref = bf16[512,768]{1,0:T(8,128)(2,1)} custom-call(bf16[768,2304]{1,0:T(8,128)(2,1)} %weight_ref.3, bf16[768,2304]{1,0:T(8,128)(2,1)} %weight_ref.3, bf16[512,768]{1,0:T(8,128)(2,1)} %get-tuple-element.221.keys_ref.gik_ref, bf16[512,768]{1,0:T(8,128)(2,1)} %get-tuple-element.215.values_ref.giv_ref), custom_call_target="tpu_custom_call" | custom-call | flops 1207959552 | bytes 6291456 | tf_op jit(solution)/shard_map/image_grads/pallas_call | solution.py:75
  183.7 4.5 %collective-permute-done.11 = bf16[576,256]{1,0:T(8,128)(2,1)S(1)} collective-permute-done((bf16[576,256]{1,0:T(8,128)(2,1)S(1)}, bf16[576,256]{1,0:T(8,128)(2,1)S(1)}, u32[]{:S(2)}, u32[]{:S(2)}) %collective-permute-start.11) | collective-permute-done | bytes 294944 | tf_op jit(solution)/shard_map/ppermute | solution.py:912
  188.2 3.1 collective-permute-done.9
  191.4 12.2 %weight_grads.1 = (f32[2,768]{1,0:T(2,128)}, bf16[4736,256]{1,0:T(8,128)(2,1)}, bf16[4736,256]{1,0:T(8,128)(2,1)}) custom-call(s32[1]{0:T(128)} %bitcast.1.side_ref.half_ref, bf16[1024,768]{1,0:T(8,128)(2,1)} %get-tuple-element.227.normed_ref, bf16[512,768]{1,0:T(8,128)(2,1)} %get-tuple-element.228.image_ref, bf16[1024,768]{1,0:T(8,128)(2,1)} %get-tuple-element.229.gq_ref, ...), custom_call_target="tpu_custom_call" | custom-call | flops 4831838208 | bytes 12582912 | tf_op jit(solution)/shard_map/weight_grads/pallas_call | solution.py:75
  203.8 2.3 collective-permute-start.12
  206.1 7.3 %collective-permute-done.13 = bf16[576,256]{1,0:T(8,128)(2,1)S(1)} collective-permute-done((bf16[576,256]{1,0:T(8,128)(2,1)S(1)}, bf16[576,256]{1,0:T(8,128)(2,1)S(1)}, u32[]{:S(2)}, u32[]{:S(2)}) %collective-permute-start.13) | collective-permute-done | bytes 294944 | tf_op jit(solution)/shard_map/ppermute | solution.py:912
  213.9 18.5 %collective-permute-done.12 = bf16[1152,256]{1,0:T(8,128)(2,1)S(1)} collective-permute-done((bf16[1152,256]{1,0:T(8,128)(2,1)S(1)}, bf16[1152,256]{1,0:T(8,128)(2,1)S(1)}, u32[]{:S(2)}, u32[]{:S(2)}) %collective-permute-start.12) | collective-permute-done | bytes 589856 | tf_op jit(solution)/shard_map/ppermute | solution.py:912
  232.6 10.3 %finish_rows.1 = (bf16[1024,768]{1,0:T(8,128)(2,1)}, bf16[4736,256]{1,0:T(8,128)(2,1)}) custom-call(s32[1]{0:T(128)} %bitcast.flag_ref, bf16[1024,768]{1,0:T(8,128)(2,1)} %bitcast.24, f32[1024,768]{1,0:T(8,128)} %get-tuple-element.240.gmid_ref, bf16[512,768]{1,0:T(8,128)(2,1)} %image_grads.1.near_ref, ...), custom_call_target="tpu_custom_call", output_to_operand_aliasing={{1}: (12, {})} | custom-call | flops 3623878656 | bytes 16777216 | tf_op jit(solution)/shard_map/finish_rows/pallas_call | solution.py:75
  242.9 4.0 %add_convert_fusion = (bf16[2368,256]{1,0:T(8,128)(2,1)}, bf16[2368,256]{1,0:T(8,128)(2,1)S(1)}) fusion(bf16[4736,256]{1,0:T(8,128)(2,1)} %collective-permute-done.15, s32[]{:T(128)S(6)} %select_n.224, bf16[4736,256]{1,0:T(8,128)(2,1)} %get-tuple-element.246, s32[]{:T(128)S(6)} %select_n.223), kind=kLoop, calls=%fused_computation.1 | loop fusion | flops 4849664 | bytes 7274504 | tf_op jit(solution)/shard_map/convert_element_type | solution.py:957
  252.1 11.7 %collective-permute-done.16 = bf16[2368,256]{1,0:T(8,128)(2,1)} collective-permute-done((bf16[2368,256]{1,0:T(8,128)(2,1)}, bf16[2368,256]{1,0:T(8,128)(2,1)}, u32[]{:S(2)}, u32[]{:S(2)}) %collective-permute-start.16) | collective-permute-done | bytes 1212448 | tf_op jit(solution)/shard_map/ppermute | solution.py:912
  263.8 1.6 add_convert_fusion.6
  265.7 17.1 %collective-permute-done.19 = bf16[2304,256]{1,0:T(8,128)(2,1)S(1)} collective-permute-done((bf16[2304,256]{1,0:T(8,128)(2,1)S(1)}, bf16[2304,256]{1,0:T(8,128)(2,1)S(1)}, u32[]{:S(2)}, u32[]{:S(2)}) %collective-permute-start.19) | collective-permute-done | bytes 1179680 | tf_op jit(solution)/shard_map/ppermute | solution.py:912
  283.0 1.6 pad_maximum_fusion.1.value_ref
  284.8 8.3 %collective-permute-done.20 = bf16[592,256]{1,0:T(8,128)(2,1)S(1)} collective-permute-done((bf16[592,256]{1,0:T(8,128)(2,1)S(1)}, bf16[592,256]{1,0:T(8,128)(2,1)S(1)}, u32[]{:S(2)}, u32[]{:S(2)}) %collective-permute-start.20) | collective-permute-done | bytes 303136 | tf_op jit(solution)/shard_map/ppermute | solution.py:912
  293.4 3.6 expert_outputs.4
  297.0 3.0 collective-permute-done.21
  300.1 1.8 broadcast_select_fusion.3
  302.4 4.0 %expert_outputs.5 = (f32[3072,768]{1,0:T(8,128)}, f32[768,3072]{1,0:T(8,128)}) custom-call(s32[1]{0:T(128)S(6)} %sub.32.half_ref, bf16[4608,256]{1,0:T(8,128)(2,1)} %collective-permute-done.23.value_ref, f32[3072,768]{1,0:T(8,128)} %get-tuple-element.265.refs_0_, f32[768,3072]{1,0:T(8,128)} %get-tuple-element.259.refs_1_), custom_call_target="tpu_custom_call", output_to_operand_aliasing={{0}: (2, {}), {1}: (3, {})} | custom-call | flops 1179648 | bytes 7077888 | tf_op jit(solution)/shard_map/expert_outputs/pallas_call | solution.py:75
  306.4 5.5 %collective-permute-done.22 = bf16[296,256]{1,0:T(8,128)(2,1)S(1)} collective-permute-done((bf16[296,256]{1,0:T(8,128)(2,1)S(1)}, bf16[296,256]{1,0:T(8,128)(2,1)S(1)}, u32[]{:S(2)}, u32[]{:S(2)}) %collective-permute-start.22) | collective-permute-done | bytes 151584 | tf_op jit(solution)/shard_map/ppermute | solution.py:912
  312.0 3.6 expert_outputs.6
  315.6 3.2 collective-permute-done.25
  319.3 3.6 expert_outputs.7
  322.9 6.3 %collective-permute-done.26 = bf16[1184,256]{1,0:T(8,128)(2,1)} collective-permute-done((bf16[1184,256]{1,0:T(8,128)(2,1)S(1)}, bf16[1184,256]{1,0:T(8,128)(2,1)}, u32[]{:S(2)}, u32[]{:S(2)}) %collective-permute-start.26) | collective-permute-done | bytes 606240 | tf_op jit(solution)/shard_map/ppermute | solution.py:912
  331.3 15.7 %collective-permute-done.28 = bf16[2368,256]{1,0:T(8,128)(2,1)S(1)} collective-permute-done((bf16[2368,256]{1,0:T(8,128)(2,1)S(1)}, bf16[2368,256]{1,0:T(8,128)(2,1)S(1)}, u32[]{:S(2)}, u32[]{:S(2)}) %collective-permute-start.28) | collective-permute-done | bytes 1212448 | tf_op jit(solution)/shard_map/ppermute | solution.py:912
  348.7 4.8 %projection_outputs.1 = (f32[768,2304]{1,0:T(8,128)}, f32[768,768]{1,0:T(8,128)}) custom-call(s32[1]{0:T(128)} %bitcast.1.side_ref.half_ref, bf16[4736,256]{1,0:T(8,128)(2,1)} %copy-done), custom_call_target="tpu_custom_call" | custom-call | flops 1212416 | bytes 7274496 | tf_op jit(solution)/shard_map/projection_outputs/pallas_call | solution.py:75
  354.9 4.8 %last_outputs.1 = (f32[768,2304]{1,0:T(8,128)}, f32[768,768]{1,0:T(8,128)}, f32[1,768]{1,0:T(1,128)}, f32[1,768]{1,0:T(1,128)}, f32[1,768]{1,0:T(1,128)}, /*inde...) custom-call(s32[1]{0:T(128)S(6)} %sub.32.half_ref, ...), custom_call_target="tpu_custom_call", output_to_operand_aliasing={{0}: (5, {}), {1}: (6, {})} | custom-call | flops 1212416 | bytes 7274496 | tf_op jit(solution)/shard_map/last_outputs/pallas_call | solution.py:75
  (96 shorter events, 26.9 us)
Async XLA Ops:
  0.6 6.1 %copy-start.9 = (f32[1,768]{1,0:T(1,128)S(1)}, f32[1,768]{1,0:T(1,128)}, u32[]{:S(2)}) copy-start(f32[1,768]{1,0:T(1,128)} %gain_ref.9) | copy-start | bytes 9220
  0.7 6.1 %copy-start.10 = (f32[1,768]{1,0:T(1,128)S(1)}, f32[1,768]{1,0:T(1,128)}, u32[]{:S(2)}) copy-start(f32[1,768]{1,0:T(1,128)} %shift_ref.6) | copy-start | bytes 9220
  1.8 16.6 %collective-permute-start = (bf16[256,768]{1,0:T(8,128)(2,1)S(1)}, bf16[256,768]{1,0:T(8,128)(2,1)S(1)}, u32[]{:S(2)}, u32[]{:S(2)}) collective-permute-start(bf16[256,768]{1,0:T(8,128)(2,1)S(1)} %get-tuple-element.329), channel_id=1, source_target_pairs={{0,1},{2,3},{4,5},{6,7},{8,9},{10,11},{12,13},{14,15},{16,17},{18,... | collective-permute-start | bytes 1179656 | tf_op jit(solution)/shard_map/ppermute | solution.py:1006
  6.8 11.7 %collective-permute-start.1 = (f32[2,768]{1,0:T(2,128)S(1)}, f32[2,768]{1,0:T(2,128)S(1)}, u32[]{:S(2)}, u32[]{:S(2)}) collective-permute-start(f32[2,768]{1,0:T(2,128)S(1)} %pad_maximum_fusion.10), channel_id=1, source_target_pairs={{0,1},{2,3},{4,5},{6,7},{8,9},{10,11},{12,13},{14,15},{16,17},{18,... | collective-permute-start | bytes 18440 | tf_op jit(solution)/shard_map/ppermute | solution.py:1006
  8.1 27.3 %collective-permute-start.2 = (bf16[256,768]{1,0:T(8,128)(2,1)S(1)}, bf16[256,768]{1,0:T(8,128)(2,1)S(1)}, u32[]{:S(2)}, u32[]{:S(2)}) collective-permute-start(bf16[256,768]{1,0:T(8,128)(2,1)S(1)} %get-tuple-element.328), channel_id=1, source_target_pairs={{0,1},{2,3},{4,5},{6,7},{8,9},{10,11},{12,13},{14,15},{16,17},{18,... | collective-permute-start | bytes 1179656 | tf_op jit(solution)/shard_map/ppermute | solution.py:1006
  9.4 8.5 %copy-start.12 = (f32[768]{0:T(1024)S(1)}, f32[768]{0:T(1024)}, u32[]{:S(2)}) copy-start(f32[768]{0:T(1024)} %param.24) | copy-start | bytes 9220
  18.5 0.6 copy-start.11
  18.5 0.7 copy-start.8
  35.4 0.7 copy-start.7
  97.4 8.8 %collective-permute-start.3 = (bf16[4608,256]{1,0:T(8,128)(2,1)}, bf16[4608,256]{1,0:T(8,128)(2,1)S(1)}, u32[]{:S(2)}, u32[]{:S(2)}) collective-permute-start(bf16[4608,256]{1,0:T(8,128)(2,1)} %get-tuple-element.170), channel_id=1, source_target_pairs={{0,2},{2,0},{4,6},{6,4},{8,10},{10,8},{12,14},{14,12},{16,18},{18,... | collective-permute-start | bytes 7077896 | tf_op jit(solution)/shard_map/ppermute | solution.py:912
  97.5 23.1 %collective-permute-start.5 = (bf16[4608,256]{1,0:T(8,128)(2,1)}, bf16[4608,256]{1,0:T(8,128)(2,1)}, u32[]{:S(2)}, u32[]{:S(2)}) collective-permute-start(bf16[4608,256]{1,0:T(8,128)(2,1)} %get-tuple-element.171), channel_id=1, source_target_pairs={{0,2},{2,0},{4,6},{6,4},{8,10},{10,8},{12,14},{14,12},{16,18},{18,... | collective-permute-start | bytes 7077896 | tf_op jit(solution)/shard_map/ppermute | solution.py:912
  98.0 9.6 %copy-start.4 = (bf16[4608,256]{1,0:T(8,128)(2,1)S(1)}, bf16[4608,256]{1,0:T(8,128)(2,1)}, u32[]{:S(2)}) copy-start(bf16[4608,256]{1,0:T(8,128)(2,1)} %get-tuple-element.175) | copy-start | bytes 7077892
  106.3 1.4 copy-start.5
  110.9 21.6 %collective-permute-start.4 = (bf16[2304,256]{1,0:T(8,128)(2,1)}, bf16[2304,256]{1,0:T(8,128)(2,1)S(1)}, u32[]{:S(2)}, u32[]{:S(2)}) collective-permute-start(bf16[2304,256]{1,0:T(8,128)(2,1)} %get-tuple-element.314), channel_id=1, source_target_pairs={{0,4},{2,10},{4,0},{6,14},{8,12},{10,2},{12,8},{14,6},{16,20},{18,... | collective-permute-start | bytes 3538952 | tf_op jit(solution)/shard_map/ppermute | solution.py:912
  112.4 8.2 %copy-start.3 = (bf16[4608,256]{1,0:T(8,128)(2,1)S(1)}, bf16[4608,256]{1,0:T(8,128)(2,1)}, u32[]{:S(2)}) copy-start(bf16[4608,256]{1,0:T(8,128)(2,1)} %get-tuple-element.184) | copy-start | bytes 7077892
  123.8 21.8 %collective-permute-start.7 = (bf16[2304,256]{1,0:T(8,128)(2,1)}, bf16[2304,256]{1,0:T(8,128)(2,1)}, u32[]{:S(2)}, u32[]{:S(2)}) collective-permute-start(bf16[2304,256]{1,0:T(8,128)(2,1)} %get-tuple-element.313), channel_id=1, source_target_pairs={{0,4},{2,10},{4,0},{6,14},{8,12},{10,2},{12,8},{14,6},{16,20},{18,... | collective-permute-start | bytes 3538952 | tf_op jit(solution)/shard_map/ppermute | solution.py:912
  132.8 25.1 %collective-permute-start.6 = (bf16[1152,256]{1,0:T(8,128)(2,1)S(1)}, bf16[1152,256]{1,0:T(8,128)(2,1)S(1)}, u32[]{:S(2)}, u32[]{:S(2)}) collective-permute-start(bf16[1152,256]{1,0:T(8,128)(2,1)S(1)} %get-tuple-element.326), channel_id=1, source_target_pairs={{0,16},{2,6},{4,20},{6,2},{8,24},{10,14},{12,28},{14,10},{16,0},{1... | collective-permute-start | bytes 1769480 | tf_op jit(solution)/shard_map/ppermute | solution.py:912
  147.1 26.1 %collective-permute-start.10 = (bf16[1152,256]{1,0:T(8,128)(2,1)S(1)}, bf16[1152,256]{1,0:T(8,128)(2,1)S(1)}, u32[]{:S(2)}, u32[]{:S(2)}) collective-permute-start(bf16[1152,256]{1,0:T(8,128)(2,1)S(1)} %get-tuple-element.325), channel_id=1, source_target_pairs={{0,16},{2,6},{4,20},{6,2},{8,24},{10,14},{12,28},{14,10},{16,0},{1... | collective-permute-start | bytes 1769480 | tf_op jit(solution)/shard_map/ppermute | solution.py:912
  158.0 15.2 %collective-permute-start.8 = (bf16[576,256]{1,0:T(8,128)(2,1)S(1)}, bf16[576,256]{1,0:T(8,128)(2,1)S(1)}, u32[]{:S(2)}, u32[]{:S(2)}) collective-permute-start(bf16[576,256]{1,0:T(8,128)(2,1)S(1)} %get-tuple-element.340), channel_id=1, source_target_pairs={{0,8},{2,18},{4,12},{6,22},{8,0},{10,26},{12,4},{14,30},{16,24},{1... | collective-permute-start | bytes 884744 | tf_op jit(solution)/shard_map/ppermute | solution.py:912
  173.4 14.7 %collective-permute-start.11 = (bf16[576,256]{1,0:T(8,128)(2,1)S(1)}, bf16[576,256]{1,0:T(8,128)(2,1)S(1)}, u32[]{:S(2)}, u32[]{:S(2)}) collective-permute-start(bf16[576,256]{1,0:T(8,128)(2,1)S(1)} %get-tuple-element.338), channel_id=1, source_target_pairs={{0,8},{2,18},{4,12},{6,22},{8,0},{10,26},{12,4},{14,30},{16,24},{1... | collective-permute-start | bytes 884744 | tf_op jit(solution)/shard_map/ppermute | solution.py:912
  177.9 13.4 %collective-permute-start.9 = (bf16[576,256]{1,0:T(8,128)(2,1)S(1)}, bf16[576,256]{1,0:T(8,128)(2,1)S(1)}, u32[]{:S(2)}, u32[]{:S(2)}) collective-permute-start(bf16[576,256]{1,0:T(8,128)(2,1)S(1)} %add_convert_fusion.17), channel_id=1, source_target_pairs={{0,8},{2,18},{4,12},{6,22},{8,0},{10,26},{12,4},{14,30},{16,24},{1... | collective-permute-start | bytes 884744 | tf_op jit(solution)/shard_map/ppermute | solution.py:912
  182.4 23.7 %collective-permute-start.14 = (bf16[512,768]{1,0:T(8,128)(2,1)}, bf16[512,768]{1,0:T(8,128)(2,1)S(1)}, u32[]{:S(2)}, u32[]{:S(2)}) collective-permute-start(bf16[512,768]{1,0:T(8,128)(2,1)} %image_grads.1.near_ref), channel_id=1, source_target_pairs={{1,0},{3,2},{5,4},{7,6},{9,8},{11,10},{13,12},{15,14},{17,16},{19,... | collective-permute-start | bytes 2359304 | tf_op jit(solution)/shard_map/ppermute | solution.py:1007
  203.6 39.3 %collective-permute-start.15 = (bf16[4736,256]{1,0:T(8,128)(2,1)}, bf16[4736,256]{1,0:T(8,128)(2,1)}, u32[]{:S(2)}, u32[]{:S(2)}) collective-permute-start(bf16[4736,256]{1,0:T(8,128)(2,1)} %get-tuple-element.233), channel_id=1, source_target_pairs={{0,2},{1,3},{2,0},{3,1},{4,6},{5,7},{6,4},{7,5},{8,10},{9,11},{10,... | collective-permute-start | bytes 7274504 | tf_op jit(solution)/shard_map/ppermute | solution.py:912
  203.7 9.8 %collective-permute-start.13 = (bf16[576,256]{1,0:T(8,128)(2,1)S(1)}, bf16[576,256]{1,0:T(8,128)(2,1)S(1)}, u32[]{:S(2)}, u32[]{:S(2)}) collective-permute-start(bf16[576,256]{1,0:T(8,128)(2,1)S(1)} %add_convert_fusion.14), channel_id=1, source_target_pairs={{0,8},{2,18},{4,12},{6,22},{8,0},{10,26},{12,4},{14,30},{16,24},{1... | collective-permute-start | bytes 884744 | tf_op jit(solution)/shard_map/ppermute | solution.py:912
  203.8 28.6 %collective-permute-start.12 = (bf16[1152,256]{1,0:T(8,128)(2,1)S(1)}, bf16[1152,256]{1,0:T(8,128)(2,1)S(1)}, u32[]{:S(2)}, u32[]{:S(2)}) collective-permute-start(bf16[1152,256]{1,0:T(8,128)(2,1)S(1)} %pad_maximum_fusion.7), channel_id=1, source_target_pairs={{0,16},{2,6},{4,20},{6,2},{8,24},{10,14},{12,28},{14,10},{16,0},{1... | collective-permute-start | bytes 1769480 | tf_op jit(solution)/shard_map/ppermute | solution.py:912
  206.1 26.4 %copy-start.6 = (bf16[512,768]{1,0:T(8,128)(2,1)}, bf16[512,768]{1,0:T(8,128)(2,1)S(1)}, u32[]{:S(2)}) copy-start(bf16[512,768]{1,0:T(8,128)(2,1)S(1)} %collective-permute-done.14.far_ref) | copy-start | bytes 2359300
  213.5 35.4 %collective-permute-start.17 = (bf16[1152,256]{1,0:T(8,128)(2,1)S(1)}, bf16[1152,256]{1,0:T(8,128)(2,1)}, u32[]{:S(2)}, u32[]{:S(2)}) collective-permute-start(bf16[1152,256]{1,0:T(8,128)(2,1)S(1)} %pad_maximum_fusion.8), channel_id=1, source_target_pairs={{0,16},{2,6},{4,20},{6,2},{8,24},{10,14},{12,28},{14,10},{16,0},{1... | collective-permute-start | bytes 1769480 | tf_op jit(solution)/shard_map/ppermute | solution.py:912
  246.9 16.9 %collective-permute-start.16 = (bf16[2368,256]{1,0:T(8,128)(2,1)}, bf16[2368,256]{1,0:T(8,128)(2,1)}, u32[]{:S(2)}, u32[]{:S(2)}) collective-permute-start(bf16[2368,256]{1,0:T(8,128)(2,1)} %get-tuple-element.310), channel_id=1, source_target_pairs={{0,4},{1,5},{2,10},{3,11},{4,0},{5,1},{6,14},{7,15},{8,12},{9,13},... | collective-permute-start | bytes 3637256 | tf_op jit(solution)/shard_map/ppermute | solution.py:912
  247.8 35.0 %collective-permute-start.19 = (bf16[2304,256]{1,0:T(8,128)(2,1)S(1)}, bf16[2304,256]{1,0:T(8,128)(2,1)S(1)}, u32[]{:S(2)}, u32[]{:S(2)}) collective-permute-start(bf16[2304,256]{1,0:T(8,128)(2,1)S(1)} %pad_maximum_fusion.4), channel_id=1, source_target_pairs={{0,4},{2,10},{4,0},{6,14},{8,12},{10,2},{12,8},{14,6},{16,20},{18,... | collective-permute-start | bytes 3538952 | tf_op jit(solution)/shard_map/ppermute | solution.py:912
  251.2 48.8 %collective-permute-start.24 = (bf16[2304,256]{1,0:T(8,128)(2,1)}, bf16[2304,256]{1,0:T(8,128)(2,1)}, u32[]{:S(2)}, u32[]{:S(2)}) collective-permute-start(bf16[2304,256]{1,0:T(8,128)(2,1)} %pad_maximum_fusion.5), channel_id=1, source_target_pairs={{0,4},{2,10},{4,0},{6,14},{8,12},{10,2},{12,8},{14,6},{16,20},{18,... | collective-permute-start | bytes 3538952 | tf_op jit(solution)/shard_map/ppermute | solution.py:912
  265.3 19.2 %collective-permute-start.18 = (bf16[1184,256]{1,0:T(8,128)(2,1)S(1)}, bf16[1184,256]{1,0:T(8,128)(2,1)S(1)}, u32[]{:S(2)}, u32[]{:S(2)}) collective-permute-start(bf16[1184,256]{1,0:T(8,128)(2,1)S(1)} %get-tuple-element.318), channel_id=1, source_target_pairs={{0,1},{1,0},{2,6},{3,7},{4,5},{5,4},{6,2},{7,3},{8,9},{9,8},{10,14... | collective-permute-start | bytes 1818632 | tf_op jit(solution)/shard_map/ppermute | solution.py:912
  284.7 8.4 %collective-permute-start.20 = (bf16[592,256]{1,0:T(8,128)(2,1)S(1)}, bf16[592,256]{1,0:T(8,128)(2,1)S(1)}, u32[]{:S(2)}, u32[]{:S(2)}) collective-permute-start(bf16[592,256]{1,0:T(8,128)(2,1)S(1)} %get-tuple-element.332), channel_id=1, source_target_pairs={{0,8},{1,9},{2,3},{3,2},{4,12},{5,13},{6,7},{7,6},{8,0},{9,1},{10,... | collective-permute-start | bytes 909320 | tf_op jit(solution)/shard_map/ppermute | solution.py:912
  293.2 6.8 %collective-permute-start.21 = (bf16[296,256]{1,0:T(8,128)(2,1)S(1)}, bf16[296,256]{1,0:T(8,128)(2,1)S(1)}, u32[]{:S(2)}, u32[]{:S(2)}) collective-permute-start(bf16[296,256]{1,0:T(8,128)(2,1)S(1)} %get-tuple-element.344), channel_id=1, source_target_pairs={{0,16},{1,17},{2,18},{3,19},{4,20},{5,21},{6,22},{7,23},{8,24},{9,... | collective-permute-start | bytes 454664 | tf_op jit(solution)/shard_map/ppermute | solution.py:912
  293.3 9.1 %collective-permute-start.23 = (bf16[4608,256]{1,0:T(8,128)(2,1)}, bf16[4608,256]{1,0:T(8,128)(2,1)}, u32[]{:S(2)}, u32[]{:S(2)}) collective-permute-start(bf16[4608,256]{1,0:T(8,128)(2,1)} %pad_maximum_fusion.1.value_ref), channel_id=1, source_target_pairs={{0,2},{2,0},{4,6},{6,4},{8,10},{10,8},{12,14},{14,12},{16,18},{18,... | collective-permute-start | bytes 7077896 | tf_op jit(solution)/shard_map/ppermute | solution.py:912
  302.0 4.4 %copy-start.2 = (bf16[4608,256]{1,0:T(8,128)(2,1)}, bf16[4608,256]{1,0:T(8,128)(2,1)S(1)}, u32[]{:S(2)}) copy-start(bf16[4608,256]{1,0:T(8,128)(2,1)S(1)} %pad_maximum_fusion.2.value_ref) | copy-start | bytes 7077892
  302.0 17.3 %collective-permute-start.27 = (bf16[4608,256]{1,0:T(8,128)(2,1)S(1)}, bf16[4608,256]{1,0:T(8,128)(2,1)}, u32[]{:S(2)}, u32[]{:S(2)}) collective-permute-start(bf16[4608,256]{1,0:T(8,128)(2,1)S(1)} %pad_maximum_fusion.2.value_ref), channel_id=1, source_target_pairs={{0,2},{2,0},{4,6},{6,4},{8,10},{10,8},{12,14},{14,12},{16,18},{18,... | collective-permute-start | bytes 7077896 | tf_op jit(solution)/shard_map/ppermute | solution.py:912
  302.1 9.8 %collective-permute-start.22 = (bf16[296,256]{1,0:T(8,128)(2,1)S(1)}, bf16[296,256]{1,0:T(8,128)(2,1)S(1)}, u32[]{:S(2)}, u32[]{:S(2)}) collective-permute-start(bf16[296,256]{1,0:T(8,128)(2,1)S(1)} %add_convert_fusion.20), channel_id=1, source_target_pairs={{0,16},{1,17},{2,18},{3,19},{4,20},{5,21},{6,22},{7,23},{8,24},{9,... | collective-permute-start | bytes 454664 | tf_op jit(solution)/shard_map/ppermute | solution.py:912
  311.9 6.9 %collective-permute-start.25 = (bf16[592,256]{1,0:T(8,128)(2,1)S(1)}, bf16[592,256]{1,0:T(8,128)(2,1)S(1)}, u32[]{:S(2)}, u32[]{:S(2)}) collective-permute-start(bf16[592,256]{1,0:T(8,128)(2,1)S(1)} %pad_maximum_fusion.9), channel_id=1, source_target_pairs={{0,8},{1,9},{2,3},{3,2},{4,12},{5,13},{6,7},{7,6},{8,0},{9,1},{10,... | collective-permute-start | bytes 909320 | tf_op jit(solution)/shard_map/ppermute | solution.py:912
  318.9 10.2 %collective-permute-start.26 = (bf16[1184,256]{1,0:T(8,128)(2,1)S(1)}, bf16[1184,256]{1,0:T(8,128)(2,1)}, u32[]{:S(2)}, u32[]{:S(2)}) collective-permute-start(bf16[1184,256]{1,0:T(8,128)(2,1)S(1)} %pad_maximum_fusion.6), channel_id=1, source_target_pairs={{0,1},{1,0},{2,6},{3,7},{4,5},{5,4},{6,2},{7,3},{8,9},{9,8},{10,14... | collective-permute-start | bytes 1818632 | tf_op jit(solution)/shard_map/ppermute | solution.py:912
  330.4 16.6 %collective-permute-start.28 = (bf16[2368,256]{1,0:T(8,128)(2,1)S(1)}, bf16[2368,256]{1,0:T(8,128)(2,1)S(1)}, u32[]{:S(2)}, u32[]{:S(2)}) collective-permute-start(bf16[2368,256]{1,0:T(8,128)(2,1)S(1)} %pad_maximum_fusion.3), channel_id=1, source_target_pairs={{0,4},{1,5},{2,10},{3,11},{4,0},{5,1},{6,14},{7,15},{8,12},{9,13},... | collective-permute-start | bytes 3637256 | tf_op jit(solution)/shard_map/ppermute | solution.py:912
  347.3 1.4 copy-start
  347.3 6.2 %collective-permute-start.29 = (bf16[4736,256]{1,0:T(8,128)(2,1)S(1)}, bf16[4736,256]{1,0:T(8,128)(2,1)S(1)}, u32[]{:S(2)}, u32[]{:S(2)}) collective-permute-start(bf16[4736,256]{1,0:T(8,128)(2,1)S(1)} %pad_maximum_fusion.value_ref.mine_ref), channel_id=1, source_target_pairs={{0,2},{1,3},{2,0},{3,1},{4,6},{5,7},{6,4},{7,5},{8,10},{9,11},{10,... | collective-permute-start | bytes 7274504 | tf_op jit(solution)/shard_map/ppermute | solution.py:912
  353.5 1.4 copy-start.1

commit v4 on v3

--- a/solution.py
+++ b/solution.py
@@ -775,7 +775,7 @@
         (hidden, gmid, near, far, *grads, *fixed, keep),
         [shaped((rows, width), bf16), shaped(keep.shape, bf16)],
         "finish_rows",
-        cost(6 * rows * width * width, 16 << 20),
+        cost(60 * rows * width * width, 160 << 20),
         scalars=(flag,),
         grid=(rows // item_rows, blocks),
         specs=[mine, mine, image, image, mine, mine, mine]
@@ -929,7 +929,7 @@
     if len(axes) == 1 and len(others) == 3:
         return [(core, core), (1, 2), (3, 1), (2, 3)]
     if len(axes) == 2 and len(others) == 4:
-        return [(core, core), (2, 3), (0, 2), (3, 0), (4, 4)]
+        return [(core, core), (0, 2), (2, 0), (3, 3), (4, 4)]
     return [(core, core)] + list(zip(others, others[1:] + others[:1]))
 
 
@@ -1098,10 +1098,10 @@
     a.step()
     bias_sums, keep, send = weight_grads(order, side, normed, images[0], grads, project_out_grad)
     p = Total(order, ("dp", "mod"), keep, send)
+    c.step()
+    a.step()
     (far,) = order.after(far)
     order.last = far
-    c.step()
-    a.step()
     grad_in, keep = finish_rows(
         order,
         flag,
@@ -1119,15 +1119,14 @@
     )
     p.terms = (keep, p.got)
     p.step()
+    a.step()
     c.step()
-    p.step()
-    a.step()
-    p.step()
     p.step()
     outputs = expert_outputs(order, side, 0, a.mine, width, units, ())
     p.step()
+    outputs = expert_outputs(order, 1 - side, 0, a.got, width, units, outputs)
     c.step()
-    outputs = expert_outputs(order, 1 - side, 0, a.got, width, units, outputs)
+    p.step()
     p.step()
     outputs = expert_outputs(order, side, 2, c.mine, width, units, outputs)
     p.step()

time: 367 us -> 362 us (0.986)
  waiting for transfers between devices: 111 us -> 97.1 us
  starting transfers between devices: 31.1 us -> 41.1 us
    ppermute x26, waiting for transfers between devices: 111 us -> 97 us  [swap(): lax.ppermute(value, axes, [(source, pair_of(source)) for source in range(...]
    ppermute x26, starting transfers between devices: 22.3 us -> 32.3 us  [swap(): lax.ppermute(value, axes, [(source, pair_of(source)) for source in range(...]
  transfers between devices with their start and end apart: 30 -> 30, of which waited for: 14 -> 14; matrix products, arithmetic and copies ran while one was open for 6% -> 5% of each run, Pallas kernels for 33% -> 34%
where the time goes in v4:
time: 362 us; the launch traced here: 356 us
  Pallas kernels  186 us (51%)
  waiting for transfers between devices  97.1 us (27%)
  starting transfers between devices  41.1 us (11%)
  other arithmetic  21.8 us (6%)
  local copies, waits for them, and re-layouts  8.32 us (2%)
    pallas_call x21, Pallas kernels, call(): pl.pallas_call(kernel, grid_spec=pltpu.PrefetchScalarGridSpec(num_scalar_...  186 us
    ppermute x26, waiting for transfers between devices, swap(): lax.ppermute(value, axes, [(source, pair_of(source)) for source in range(...  97 us
    ppermute x26, starting transfers between devices, swap(): lax.ppermute(value, axes, [(source, pair_of(source)) for source in range(...  32.3 us
    convert_element_type x10, other arithmetic, part(): return (cut(self.terms[0]) + cut(self.terms[1])).astype(bf16)  17.3 us
    ppermute x3, starting transfers between devices, on_device(): to_text = lambda value: lax.ppermute(value, 'mod', [(0, 1)])  7.5 us
  transfers between devices with their start and end apart: 30, of which 14 were waited for; matrix products, arithmetic and copies ran while one was open for 5% of the time, Pallas kernels for 34%

profile of v4, /device:TPU:0, one launch (start us, length us, event | category | flops | bytes accessed | tf_op | source)
XLA Modules:
  0.0 355.5 jit_solution(12253465448907726443)
XLA Ops:
  1.8 4.9 %collective-permute-start = (bf16[256,768]{1,0:T(8,128)(2,1)S(1)}, bf16[256,768]{1,0:T(8,128)(2,1)S(1)}, u32[]{:S(2)}, u32[]{:S(2)}) collective-permute-start(bf16[256,768]{1,0:T(8,128)(2,1)S(1)} %get-tuple-element.329), channel_id=1, source_target_pairs={{0,1},{2,3},{4,5},{6,7},{8,9},{10,11},{12,13},{14,15},{16,17},{18,... | collective-permute-start | bytes 1179656 | tf_op jit(solution)/shard_map/ppermute | solution.py:1006
  9.4 8.5 %project_rows.1 = (bf16[1024,768]{1,0:T(8,128)(2,1)}, bf16[1024,2304]{1,0:T(8,128)(2,1)}) custom-call(bf16[1024,768]{1,0:T(8,128)(2,1)} %bitcast.20, f32[1,768]{1,0:T(1,128)} %gain_ref.9, f32[1,768]{1,0:T(1,128)} %shift_ref.6, bf16[768,2304]{1,0:T(8,128)(2,1)} %weight_ref.3, f32[2,768]{1,0:T(2,128)} %bias_ref.5), custom_call_target="tpu_custom_call" | custom-call | flops 3623878656 | bytes 11403264 | tf_op jit(solution)/shard_map/project_rows/pallas_call | solution.py:75
  19.2 3.8 %image_rows.2 = (bf16[512,768]{1,0:T(8,128)(2,1)}, bf16[512,1536]{1,0:T(8,128)(2,1)}) custom-call(s32[1]{0:T(128)} %bitcast.flag_ref, bf16[1024,768]{1,0:T(8,128)(2,1)} %bitcast.21, bf16[256,768]{1,0:T(8,128)(2,1)} %copy-done.10, f32[1,768]{1,0:T(1,128)} %gain_ref.9, f32[1,768]{1,0:T(1,128)} %shift_ref.6, f32[2,768]{1,0:T(2,128)} %copy-done.13, ...), custom_call_target="tpu_custom_call" | custom-call | flops 603979776 | bytes 6291456 | tf_op jit(solution)/shard_map/image_rows/pallas_call | solution.py:75
  23.1 12.3 %attend_forward.2 = (bf16[512,768]{1,0:T(8,128)(2,1)}, f32[6,2,512]{2,1,0:T(2,128)}) custom-call(s32[1]{0:T(128)} %bitcast.flag_ref, s32[2]{0:T(128)} %count_ref.17, s32[2,4]{1,0:T(2,128)} %lengths_ref.15, bf16[1024,2304]{1,0:T(8,128)(2,1)} %get-tuple-element.210.q_ref.k_ref.v_ref, bf16[1024,2304]{1,0:T(8,128)(2,1)} %get-tuple-element.210.q_ref.k_ref.v_ref, ...), custom_call_target="tpu_custom_call" | custom-call | flops 4831838208 | bytes 6291456 | tf_op jit(solution)/shard_map/attend_forward/pallas_call | solution.py:75
  36.1 3.8 %image_rows.3 = (bf16[512,768]{1,0:T(8,128)(2,1)}, bf16[512,1536]{1,0:T(8,128)(2,1)}) custom-call(s32[1]{0:T(128)} %bitcast.flag_ref, bf16[1024,768]{1,0:T(8,128)(2,1)} %bitcast.22, bf16[256,768]{1,0:T(8,128)(2,1)} %copy-done.9, f32[1,768]{1,0:T(1,128)} %gain_ref.9, f32[1,768]{1,0:T(1,128)} %shift_ref.6, ...), custom_call_target="tpu_custom_call", output_to_operand_aliasing={{0}: (9, {}), {1}: (10, {})} | custom-call | flops 603979776 | bytes 6291456 | tf_op jit(solution)/shard_map/image_rows/pallas_call | solution.py:75
  39.9 12.2 %attend_forward.3 = (bf16[512,768]{1,0:T(8,128)(2,1)}, f32[6,2,512]{2,1,0:T(2,128)}) custom-call(s32[1]{0:T(128)} %bitcast.flag_ref, s32[2]{0:T(128)} %count_ref.17, s32[2,4]{1,0:T(2,128)} %lengths_ref.15, bf16[1024,2304]{1,0:T(8,128)(2,1)} %get-tuple-element.210.q_ref.k_ref.v_ref, bf16[1024,2304]{1,0:T(8,128)(2,1)} %get-tuple-element.210.q_ref.k_ref.v_ref, ...), custom_call_target="tpu_custom_call" | custom-call | flops 4831838208 | bytes 6291456 | tf_op jit(solution)/shard_map/attend_forward/pallas_call | solution.py:75
  52.2 45.3 %feed_forward.1 = (bf16[1024,768]{1,0:T(8,128)(2,1)}, f32[1024,768]{1,0:T(8,128)}, bf16[1024,768]{1,0:T(8,128)(2,1)}, bf16[768,768]{1,0:T(8,128)(2,1)}, f32[8,76...) custom-call(s32[1]{0:T(128)} %bitcast.flag_ref, ...), custom_call_target="tpu_custom_call" | custom-call | flops 28991029248 | bytes 41943040 | tf_op jit(solution)/shard_map/feed_forward/pallas_call | solution.py:75
  98.0 8.2 %attend_backward.6 = (bf16[1024,768]{1,0:T(8,128)(2,1)}, bf16[1024,768]{1,0:T(8,128)(2,1)}, bf16[1024,768]{1,0:T(8,128)(2,1)}, bf16[512,768]{1,0:T(8,128)(2,1)}, bf16[512,768]{1,0:T(8,128)(2,1)}) custom-call(s32[1]{0:T(128)} %bitcast.flag_ref, s32[2]{0:T(128)} %count_ref.17, s32[2,4]{1,0:T(2,128)} %lengths_ref.15, ...), custom_call_target="tpu_custom_call" | custom-call | flops 4026531840 | bytes 4194304 | tf_op jit(solution)/shard_map/attend_backward/pallas_call | solution.py:75
  107.7 3.2 add_convert_fusion.2
  112.4 8.2 %attend_backward.7 = (bf16[1024,768]{1,0:T(8,128)(2,1)}, bf16[1024,768]{1,0:T(8,128)(2,1)}, bf16[1024,768]{1,0:T(8,128)(2,1)}, bf16[512,768]{1,0:T(8,128)(2,1)}, bf16[512,768]{1,0:T(8,128)(2,1)}) custom-call(s32[1]{0:T(128)} %bitcast.flag_ref, s32[2]{0:T(128)} %count_ref.17, ...), custom_call_target="tpu_custom_call", output_to_operand_aliasing={{0}: (11, {}), {1}: (12, {}), {2}: (13, {}), {3}: (14, {}),... | custom-call | flops 4026531840 | bytes 4194304 | tf_op jit(solution)/shard_map/attend_backward/pallas_call | solution.py:75
  120.6 3.2 add_convert_fusion.3
  124.3 8.1 %attend_backward.8 = (bf16[1024,768]{1,0:T(8,128)(2,1)}, bf16[1024,768]{1,0:T(8,128)(2,1)}, bf16[1024,768]{1,0:T(8,128)(2,1)}, bf16[512,768]{1,0:T(8,128)(2,1)}, bf16[512,768]{1,0:T(8,128)(2,1)}) custom-call(s32[1]{0:T(128)} %bitcast.flag_ref, s32[2]{0:T(128)} %count_ref.17, ...), custom_call_target="tpu_custom_call", output_to_operand_aliasing={{0}: (11, {}), {1}: (12, {}), {2}: (13, {}), {3}: (14, {}),... | custom-call | flops 4026531840 | bytes 4194304 | tf_op jit(solution)/shard_map/attend_backward/pallas_call | solution.py:75
  132.8 2.7 collective-permute-start.8
  135.4 8.3 %attend_backward.9 = (bf16[1024,768]{1,0:T(8,128)(2,1)}, bf16[1024,768]{1,0:T(8,128)(2,1)}, bf16[1024,768]{1,0:T(8,128)(2,1)}, bf16[512,768]{1,0:T(8,128)(2,1)}, bf16[512,768]{1,0:T(8,128)(2,1)}) custom-call(s32[1]{0:T(128)} %bitcast.flag_ref, s32[2]{0:T(128)} %count_ref.17, ...), custom_call_target="tpu_custom_call", output_to_operand_aliasing={{0}: (11, {}), {1}: (12, {}), {2}: (13, {}), {3}: (14, {}),... | custom-call | flops 4026531840 | bytes 4194304 | tf_op jit(solution)/shard_map/attend_backward/pallas_call | solution.py:75
  143.7 1.9 collective-permute-done.5
  147.1 2.6 collective-permute-start.7
  149.7 8.1 %attend_backward.10 = (bf16[1024,768]{1,0:T(8,128)(2,1)}, bf16[1024,768]{1,0:T(8,128)(2,1)}, bf16[1024,768]{1,0:T(8,128)(2,1)}, bf16[512,768]{1,0:T(8,128)(2,1)}, bf16[512,768]{1,0:T(8,128)(2,1)}) custom-call(s32[1]{0:T(128)} %bitcast.flag_ref, s32[2]{0:T(128)} %count_ref.17, ...), custom_call_target="tpu_custom_call", output_to_operand_aliasing={{0}: (11, {}), {1}: (12, {}), {2}: (13, {}), {3}: (14, {}),... | custom-call | flops 4026531840 | bytes 4194304 | tf_op jit(solution)/shard_map/attend_backward/pallas_call | solution.py:75
  158.0 1.7 collective-permute-start.9
  159.7 8.1 %attend_backward.11 = (bf16[1024,768]{1,0:T(8,128)(2,1)}, bf16[1024,768]{1,0:T(8,128)(2,1)}, bf16[1024,768]{1,0:T(8,128)(2,1)}, bf16[512,768]{1,0:T(8,128)(2,1)}, bf16[512,768]{1,0:T(8,128)(2,1)}) custom-call(s32[1]{0:T(128)} %bitcast.flag_ref, s32[2]{0:T(128)} %count_ref.17, ...), custom_call_target="tpu_custom_call", output_to_operand_aliasing={{0}: (11, {}), {1}: (12, {}), {2}: (13, {}), {3}: (14, {}),... | custom-call | flops 4026531840 | bytes 4194304 | tf_op jit(solution)/shard_map/attend_backward/pallas_call | solution.py:75
  167.8 5.5 %collective-permute-done.9 = bf16[576,256]{1,0:T(8,128)(2,1)S(1)} collective-permute-done((bf16[576,256]{1,0:T(8,128)(2,1)S(1)}, bf16[576,256]{1,0:T(8,128)(2,1)S(1)}, u32[]{:S(2)}, u32[]{:S(2)}) %collective-permute-start.9) | collective-permute-done | bytes 294944 | tf_op jit(solution)/shard_map/ppermute | solution.py:912
  173.5 4.4 %collective-permute-start.12 = (bf16[576,256]{1,0:T(8,128)(2,1)S(1)}, bf16[576,256]{1,0:T(8,128)(2,1)S(1)}, u32[]{:S(2)}, u32[]{:S(2)}) collective-permute-start(bf16[576,256]{1,0:T(8,128)(2,1)S(1)} %get-tuple-element.339), channel_id=1, source_target_pairs={{0,8},{2,18},{4,12},{6,22},{8,0},{10,26},{12,4},{14,30},{16,24},{1... | collective-permute-start | bytes 884744 | tf_op jit(solution)/shard_map/ppermute | solution.py:912
  178.0 4.4 %image_grads.1.near_ref = bf16[512,768]{1,0:T(8,128)(2,1)} custom-call(bf16[768,2304]{1,0:T(8,128)(2,1)} %weight_ref.3, bf16[768,2304]{1,0:T(8,128)(2,1)} %weight_ref.3, bf16[512,768]{1,0:T(8,128)(2,1)} %get-tuple-element.221.keys_ref.gik_ref, bf16[512,768]{1,0:T(8,128)(2,1)} %get-tuple-element.215.values_ref.giv_ref), custom_call_target="tpu_custom_call" | custom-call | flops 1207959552 | bytes 6291456 | tf_op jit(solution)/shard_map/image_grads/pallas_call | solution.py:75
  183.7 7.0 %collective-permute-done.12 = bf16[576,256]{1,0:T(8,128)(2,1)S(1)} collective-permute-done((bf16[576,256]{1,0:T(8,128)(2,1)S(1)}, bf16[576,256]{1,0:T(8,128)(2,1)S(1)}, u32[]{:S(2)}, u32[]{:S(2)}) %collective-permute-start.12) | collective-permute-done | bytes 294944 | tf_op jit(solution)/shard_map/ppermute | solution.py:912
  190.8 3.6 %collective-permute-done.11 = bf16[576,256]{1,0:T(8,128)(2,1)S(1)} collective-permute-done((bf16[576,256]{1,0:T(8,128)(2,1)S(1)}, bf16[576,256]{1,0:T(8,128)(2,1)S(1)}, u32[]{:S(2)}, u32[]{:S(2)}) %collective-permute-start.11) | collective-permute-done | bytes 294944 | tf_op jit(solution)/shard_map/ppermute | solution.py:912
  194.6 12.2 %weight_grads.1 = (f32[2,768]{1,0:T(2,128)}, bf16[4736,256]{1,0:T(8,128)(2,1)}, bf16[4736,256]{1,0:T(8,128)(2,1)}) custom-call(s32[1]{0:T(128)} %bitcast.1.side_ref.half_ref, bf16[1024,768]{1,0:T(8,128)(2,1)} %get-tuple-element.227.normed_ref, bf16[512,768]{1,0:T(8,128)(2,1)} %get-tuple-element.228.image_ref, bf16[1024,768]{1,0:T(8,128)(2,1)} %get-tuple-element.229.gq_ref, ...), custom_call_target="tpu_custom_call" | custom-call | flops 4831838208 | bytes 12582912 | tf_op jit(solution)/shard_map/weight_grads/pallas_call | solution.py:75
  207.0 2.9 collective-permute-start.17
  212.8 10.2 %finish_rows.1 = (bf16[1024,768]{1,0:T(8,128)(2,1)}, bf16[4736,256]{1,0:T(8,128)(2,1)}) custom-call(s32[1]{0:T(128)} %bitcast.flag_ref, bf16[1024,768]{1,0:T(8,128)(2,1)} %bitcast.24, f32[1024,768]{1,0:T(8,128)} %get-tuple-element.240.gmid_ref, bf16[512,768]{1,0:T(8,128)(2,1)} %image_grads.1.near_ref, ...), custom_call_target="tpu_custom_call", output_to_operand_aliasing={{1}: (12, {})} | custom-call | flops 36238786560 | bytes 167772160 | tf_op jit(solution)/shard_map/finish_rows/pallas_call | solution.py:75
  223.0 3.7 %add_convert_fusion = (bf16[2368,256]{1,0:T(8,128)(2,1)}, bf16[2368,256]{1,0:T(8,128)(2,1)}) fusion(bf16[4736,256]{1,0:T(8,128)(2,1)S(1)} %collective-permute-done.15, s32[]{:T(128)S(6)} %select_n.221, bf16[4736,256]{1,0:T(8,128)(2,1)} %get-tuple-element.246, s32[]{:T(128)S(6)} %select_n.220), kind=kLoop, calls=%fused_computation.1 | loop fusion | flops 4849664 | bytes 7274504 | tf_op jit(solution)/shard_map/convert_element_type | solution.py:957
  226.7 2.4 collective-permute-done.18
  232.3 15.3 %collective-permute-done.16 = bf16[2368,256]{1,0:T(8,128)(2,1)} collective-permute-done((bf16[2368,256]{1,0:T(8,128)(2,1)}, bf16[2368,256]{1,0:T(8,128)(2,1)}, u32[]{:S(2)}, u32[]{:S(2)}) %collective-permute-start.16) | collective-permute-done | bytes 1212448 | tf_op jit(solution)/shard_map/ppermute | solution.py:912
  247.6 2.9 add_convert_fusion.6
  251.5 3.6 %expert_outputs.4 = (f32[3072,768]{1,0:T(8,128)}, f32[768,3072]{1,0:T(8,128)}) custom-call(s32[1]{0:T(128)} %bitcast.1.side_ref.half_ref, bf16[4608,256]{1,0:T(8,128)(2,1)} %copy-done.3), custom_call_target="tpu_custom_call" | custom-call | flops 1179648 | bytes 7077888 | tf_op jit(solution)/shard_map/expert_outputs/pallas_call | solution.py:75
  255.1 10.7 %collective-permute-done.19 = bf16[1184,256]{1,0:T(8,128)(2,1)} collective-permute-done((bf16[1184,256]{1,0:T(8,128)(2,1)}, bf16[1184,256]{1,0:T(8,128)(2,1)}, u32[]{:S(2)}, u32[]{:S(2)}) %collective-permute-start.19) | collective-permute-done | bytes 606240 | tf_op jit(solution)/shard_map/ppermute | solution.py:912
  265.8 2.0 add_convert_fusion.12
  267.9 3.6 %expert_outputs.5 = (f32[3072,768]{1,0:T(8,128)}, f32[768,3072]{1,0:T(8,128)}) custom-call(s32[1]{0:T(128)S(6)} %sub.32.half_ref, bf16[4608,256]{1,0:T(8,128)(2,1)} %collective-permute-done.22.value_ref, f32[3072,768]{1,0:T(8,128)} %get-tuple-element.259.refs_0_, f32[768,3072]{1,0:T(8,128)} %get-tuple-element.255.refs_1_), custom_call_target="tpu_custom_call", output_to_operand_aliasing={{0}: (2, {}), {1}: (3, {})} | custom-call | flops 1179648 | bytes 7077888 | tf_op jit(solution)/shard_map/expert_outputs/pallas_call | solution.py:75
  273.1 4.9 %collective-permute-start.26 = (bf16[4608,256]{1,0:T(8,128)(2,1)S(1)}, bf16[4608,256]{1,0:T(8,128)(2,1)}, u32[]{:S(2)}, u32[]{:S(2)}) collective-permute-start(bf16[4608,256]{1,0:T(8,128)(2,1)S(1)} %pad_maximum_fusion.2.value_ref), channel_id=1, source_target_pairs={{0,2},{2,0},{4,6},{6,4},{8,10},{10,8},{12,14},{14,12},{16,18},{18,... | collective-permute-start | bytes 7077896 | tf_op jit(solution)/shard_map/ppermute | solution.py:912
  278.0 1.8 collective-permute-start.20
  279.8 7.6 %collective-permute-done.20 = bf16[592,256]{1,0:T(8,128)(2,1)S(1)} collective-permute-done((bf16[592,256]{1,0:T(8,128)(2,1)}, bf16[592,256]{1,0:T(8,128)(2,1)S(1)}, u32[]{:S(2)}, u32[]{:S(2)}) %collective-permute-start.20) | collective-permute-done | bytes 303136 | tf_op jit(solution)/shard_map/ppermute | solution.py:912
  287.5 2.1 collective-permute-start.23
  289.7 7.2 %collective-permute-done.23 = bf16[296,256]{1,0:T(8,128)(2,1)S(1)} collective-permute-done((bf16[296,256]{1,0:T(8,128)(2,1)S(1)}, bf16[296,256]{1,0:T(8,128)(2,1)S(1)}, u32[]{:S(2)}, u32[]{:S(2)}) %collective-permute-start.23) | collective-permute-done | bytes 151584 | tf_op jit(solution)/shard_map/ppermute | solution.py:912
  297.1 3.6 %expert_outputs.6 = (f32[3072,768]{1,0:T(8,128)}, f32[768,3072]{1,0:T(8,128)}) custom-call(s32[1]{0:T(128)} %bitcast.1.side_ref.half_ref, bf16[4608,256]{1,0:T(8,128)(2,1)} %copy-done.2, f32[3072,768]{1,0:T(8,128)} %get-tuple-element.268.refs_0_, f32[768,3072]{1,0:T(8,128)} %get-tuple-element.260.refs_1_), custom_call_target="tpu_custom_call", output_to_operand_aliasing={{0}: (2, {}), {1}: (3, {})} | custom-call | flops 1179648 | bytes 7077888 | tf_op jit(solution)/shard_map/expert_outputs/pallas_call | solution.py:75
  300.6 4.3 %collective-permute-done.24 = bf16[296,256]{1,0:T(8,128)(2,1)S(1)} collective-permute-done((bf16[296,256]{1,0:T(8,128)(2,1)S(1)}, bf16[296,256]{1,0:T(8,128)(2,1)S(1)}, u32[]{:S(2)}, u32[]{:S(2)}) %collective-permute-start.24) | collective-permute-done | bytes 151584 | tf_op jit(solution)/shard_map/ppermute | solution.py:912
  305.1 3.6 %expert_outputs.7 = (f32[3072,768]{1,0:T(8,128)}, f32[768,3072]{1,0:T(8,128)}) custom-call(s32[1]{0:T(128)S(6)} %sub.32.half_ref, bf16[4608,256]{1,0:T(8,128)(2,1)} %collective-permute-done.26.value_ref, f32[3072,768]{1,0:T(8,128)} %get-tuple-element.273.refs_0_, f32[768,3072]{1,0:T(8,128)} %get-tuple-element.269.refs_1_), custom_call_target="tpu_custom_call", output_to_operand_aliasing={{0}: (2, {}), {1}: (3, {})} | custom-call | flops 1179648 | bytes 7077888 | tf_op jit(solution)/shard_map/expert_outputs/pallas_call | solution.py:75
  308.7 5.3 %collective-permute-done.25 = bf16[592,256]{1,0:T(8,128)(2,1)S(1)} collective-permute-done((bf16[592,256]{1,0:T(8,128)(2,1)S(1)}, bf16[592,256]{1,0:T(8,128)(2,1)S(1)}, u32[]{:S(2)}, u32[]{:S(2)}) %collective-permute-start.25) | collective-permute-done | bytes 303136 | tf_op jit(solution)/shard_map/ppermute | solution.py:912
  315.1 9.1 %collective-permute-done.27 = bf16[1184,256]{1,0:T(8,128)(2,1)S(1)} collective-permute-done((bf16[1184,256]{1,0:T(8,128)(2,1)S(1)}, bf16[1184,256]{1,0:T(8,128)(2,1)S(1)}, u32[]{:S(2)}, u32[]{:S(2)}) %collective-permute-start.27) | collective-permute-done | bytes 606240 | tf_op jit(solution)/shard_map/ppermute | solution.py:912
  324.8 16.3 %collective-permute-done.28 = bf16[2368,256]{1,0:T(8,128)(2,1)S(1)} collective-permute-done((bf16[2368,256]{1,0:T(8,128)(2,1)S(1)}, bf16[2368,256]{1,0:T(8,128)(2,1)S(1)}, u32[]{:S(2)}, u32[]{:S(2)}) %collective-permute-start.28) | collective-permute-done | bytes 1212448 | tf_op jit(solution)/shard_map/ppermute | solution.py:912
  342.8 4.8 %projection_outputs.1 = (f32[768,2304]{1,0:T(8,128)}, f32[768,768]{1,0:T(8,128)}) custom-call(s32[1]{0:T(128)} %bitcast.1.side_ref.half_ref, bf16[4736,256]{1,0:T(8,128)(2,1)} %copy-done), custom_call_target="tpu_custom_call" | custom-call | flops 1212416 | bytes 7274496 | tf_op jit(solution)/shard_map/projection_outputs/pallas_call | solution.py:75
  349.0 4.8 %last_outputs.1 = (f32[768,2304]{1,0:T(8,128)}, f32[768,768]{1,0:T(8,128)}, f32[1,768]{1,0:T(1,128)}, f32[1,768]{1,0:T(1,128)}, f32[1,768]{1,0:T(1,128)}, /*inde...) custom-call(s32[1]{0:T(128)S(6)} %sub.32.half_ref, ...), custom_call_target="tpu_custom_call", output_to_operand_aliasing={{0}: (5, {}), {1}: (6, {})} | custom-call | flops 1212416 | bytes 7274496 | tf_op jit(solution)/shard_map/last_outputs/pallas_call | solution.py:75
  (102 shorter events, 28.7 us)
Async XLA Ops:
  0.6 6.1 %copy-start.12 = (f32[1,768]{1,0:T(1,128)S(1)}, f32[1,768]{1,0:T(1,128)}, u32[]{:S(2)}) copy-start(f32[1,768]{1,0:T(1,128)} %gain_ref.9) | copy-start | bytes 9220
  0.7 6.1 %copy-start.11 = (f32[1,768]{1,0:T(1,128)S(1)}, f32[1,768]{1,0:T(1,128)}, u32[]{:S(2)}) copy-start(f32[1,768]{1,0:T(1,128)} %shift_ref.6) | copy-start | bytes 9220
  1.8 16.6 %collective-permute-start = (bf16[256,768]{1,0:T(8,128)(2,1)S(1)}, bf16[256,768]{1,0:T(8,128)(2,1)S(1)}, u32[]{:S(2)}, u32[]{:S(2)}) collective-permute-start(bf16[256,768]{1,0:T(8,128)(2,1)S(1)} %get-tuple-element.329), channel_id=1, source_target_pairs={{0,1},{2,3},{4,5},{6,7},{8,9},{10,11},{12,13},{14,15},{16,17},{18,... | collective-permute-start | bytes 1179656 | tf_op jit(solution)/shard_map/ppermute | solution.py:1006
  6.8 11.7 %collective-permute-start.1 = (f32[2,768]{1,0:T(2,128)S(1)}, f32[2,768]{1,0:T(2,128)S(1)}, u32[]{:S(2)}, u32[]{:S(2)}) collective-permute-start(f32[2,768]{1,0:T(2,128)S(1)} %pad_maximum_fusion.10), channel_id=1, source_target_pairs={{0,1},{2,3},{4,5},{6,7},{8,9},{10,11},{12,13},{14,15},{16,17},{18,... | collective-permute-start | bytes 18440 | tf_op jit(solution)/shard_map/ppermute | solution.py:1006
  8.1 27.3 %collective-permute-start.2 = (bf16[256,768]{1,0:T(8,128)(2,1)S(1)}, bf16[256,768]{1,0:T(8,128)(2,1)S(1)}, u32[]{:S(2)}, u32[]{:S(2)}) collective-permute-start(bf16[256,768]{1,0:T(8,128)(2,1)S(1)} %get-tuple-element.328), channel_id=1, source_target_pairs={{0,1},{2,3},{4,5},{6,7},{8,9},{10,11},{12,13},{14,15},{16,17},{18,... | collective-permute-start | bytes 1179656 | tf_op jit(solution)/shard_map/ppermute | solution.py:1006
  9.4 8.5 %copy-start.14 = (f32[768]{0:T(1024)S(1)}, f32[768]{0:T(1024)}, u32[]{:S(2)}) copy-start(f32[768]{0:T(1024)} %param.24) | copy-start | bytes 9220
  18.5 0.6 copy-start.13
  18.5 0.7 copy-start.10
  35.4 0.7 copy-start.9
  97.5 8.8 %collective-permute-start.4 = (bf16[4608,256]{1,0:T(8,128)(2,1)}, bf16[4608,256]{1,0:T(8,128)(2,1)S(1)}, u32[]{:S(2)}, u32[]{:S(2)}) collective-permute-start(bf16[4608,256]{1,0:T(8,128)(2,1)} %get-tuple-element.172), channel_id=1, source_target_pairs={{0,2},{2,0},{4,6},{6,4},{8,10},{10,8},{12,14},{14,12},{16,18},{18,... | collective-permute-start | bytes 7077896 | tf_op jit(solution)/shard_map/ppermute | solution.py:912
  97.5 23.1 %collective-permute-start.3 = (bf16[4608,256]{1,0:T(8,128)(2,1)}, bf16[4608,256]{1,0:T(8,128)(2,1)}, u32[]{:S(2)}, u32[]{:S(2)}) collective-permute-start(bf16[4608,256]{1,0:T(8,128)(2,1)} %get-tuple-element.170), channel_id=1, source_target_pairs={{0,2},{2,0},{4,6},{6,4},{8,10},{10,8},{12,14},{14,12},{16,18},{18,... | collective-permute-start | bytes 7077896 | tf_op jit(solution)/shard_map/ppermute | solution.py:912
  98.0 9.7 %copy-start.6 = (bf16[4608,256]{1,0:T(8,128)(2,1)S(1)}, bf16[4608,256]{1,0:T(8,128)(2,1)}, u32[]{:S(2)}) copy-start(bf16[4608,256]{1,0:T(8,128)(2,1)} %get-tuple-element.176) | copy-start | bytes 7077892
  106.3 1.4 copy-start.7
  110.9 21.6 %collective-permute-start.6 = (bf16[2304,256]{1,0:T(8,128)(2,1)}, bf16[2304,256]{1,0:T(8,128)(2,1)S(1)}, u32[]{:S(2)}, u32[]{:S(2)}) collective-permute-start(bf16[2304,256]{1,0:T(8,128)(2,1)} %get-tuple-element.313), channel_id=1, source_target_pairs={{0,4},{2,10},{4,0},{6,14},{8,12},{10,2},{12,8},{14,6},{16,20},{18,... | collective-permute-start | bytes 3538952 | tf_op jit(solution)/shard_map/ppermute | solution.py:912
  112.4 8.2 %copy-start.5 = (bf16[4608,256]{1,0:T(8,128)(2,1)S(1)}, bf16[4608,256]{1,0:T(8,128)(2,1)}, u32[]{:S(2)}) copy-start(bf16[4608,256]{1,0:T(8,128)(2,1)} %get-tuple-element.184) | copy-start | bytes 7077892
  123.8 21.7 %collective-permute-start.5 = (bf16[2304,256]{1,0:T(8,128)(2,1)}, bf16[2304,256]{1,0:T(8,128)(2,1)}, u32[]{:S(2)}, u32[]{:S(2)}) collective-permute-start(bf16[2304,256]{1,0:T(8,128)(2,1)} %get-tuple-element.314), channel_id=1, source_target_pairs={{0,4},{2,10},{4,0},{6,14},{8,12},{10,2},{12,8},{14,6},{16,20},{18,... | collective-permute-start | bytes 3538952 | tf_op jit(solution)/shard_map/ppermute | solution.py:912
  132.8 25.1 %collective-permute-start.8 = (bf16[1152,256]{1,0:T(8,128)(2,1)S(1)}, bf16[1152,256]{1,0:T(8,128)(2,1)S(1)}, u32[]{:S(2)}, u32[]{:S(2)}) collective-permute-start(bf16[1152,256]{1,0:T(8,128)(2,1)S(1)} %get-tuple-element.325), channel_id=1, source_target_pairs={{0,16},{2,6},{4,20},{6,2},{8,24},{10,14},{12,28},{14,10},{16,0},{1... | collective-permute-start | bytes 1769480 | tf_op jit(solution)/shard_map/ppermute | solution.py:912
  147.1 26.2 %collective-permute-start.7 = (bf16[1152,256]{1,0:T(8,128)(2,1)S(1)}, bf16[1152,256]{1,0:T(8,128)(2,1)S(1)}, u32[]{:S(2)}, u32[]{:S(2)}) collective-permute-start(bf16[1152,256]{1,0:T(8,128)(2,1)S(1)} %get-tuple-element.326), channel_id=1, source_target_pairs={{0,16},{2,6},{4,20},{6,2},{8,24},{10,14},{12,28},{14,10},{16,0},{1... | collective-permute-start | bytes 1769480 | tf_op jit(solution)/shard_map/ppermute | solution.py:912
  158.0 15.2 %collective-permute-start.9 = (bf16[576,256]{1,0:T(8,128)(2,1)S(1)}, bf16[576,256]{1,0:T(8,128)(2,1)S(1)}, u32[]{:S(2)}, u32[]{:S(2)}) collective-permute-start(bf16[576,256]{1,0:T(8,128)(2,1)S(1)} %get-tuple-element.340), channel_id=1, source_target_pairs={{0,8},{2,18},{4,12},{6,22},{8,0},{10,26},{12,4},{14,30},{16,24},{1... | collective-permute-start | bytes 884744 | tf_op jit(solution)/shard_map/ppermute | solution.py:912
  173.5 17.2 %collective-permute-start.12 = (bf16[576,256]{1,0:T(8,128)(2,1)S(1)}, bf16[576,256]{1,0:T(8,128)(2,1)S(1)}, u32[]{:S(2)}, u32[]{:S(2)}) collective-permute-start(bf16[576,256]{1,0:T(8,128)(2,1)S(1)} %get-tuple-element.339), channel_id=1, source_target_pairs={{0,8},{2,18},{4,12},{6,22},{8,0},{10,26},{12,4},{14,30},{16,24},{1... | collective-permute-start | bytes 884744 | tf_op jit(solution)/shard_map/ppermute | solution.py:912
  177.9 16.6 %collective-permute-start.11 = (bf16[576,256]{1,0:T(8,128)(2,1)S(1)}, bf16[576,256]{1,0:T(8,128)(2,1)S(1)}, u32[]{:S(2)}, u32[]{:S(2)}) collective-permute-start(bf16[576,256]{1,0:T(8,128)(2,1)S(1)} %add_convert_fusion.17), channel_id=1, source_target_pairs={{0,8},{2,18},{4,12},{6,22},{8,0},{10,26},{12,4},{14,30},{16,24},{1... | collective-permute-start | bytes 884744 | tf_op jit(solution)/shard_map/ppermute | solution.py:912
  182.4 29.5 %collective-permute-start.10 = (bf16[512,768]{1,0:T(8,128)(2,1)}, bf16[512,768]{1,0:T(8,128)(2,1)S(1)}, u32[]{:S(2)}, u32[]{:S(2)}) collective-permute-start(bf16[512,768]{1,0:T(8,128)(2,1)} %image_grads.1.near_ref), channel_id=1, source_target_pairs={{1,0},{3,2},{5,4},{7,6},{9,8},{11,10},{13,12},{15,14},{17,16},{19,... | collective-permute-start | bytes 2359304 | tf_op jit(solution)/shard_map/ppermute | solution.py:1007
  190.8 16.1 %collective-permute-start.14 = (bf16[576,256]{1,0:T(8,128)(2,1)S(1)}, bf16[576,256]{1,0:T(8,128)(2,1)S(1)}, u32[]{:S(2)}, u32[]{:S(2)}) collective-permute-start(bf16[576,256]{1,0:T(8,128)(2,1)S(1)} %add_convert_fusion.14), channel_id=1, source_target_pairs={{0,8},{2,18},{4,12},{6,22},{8,0},{10,26},{12,4},{14,30},{16,24},{1... | collective-permute-start | bytes 884744 | tf_op jit(solution)/shard_map/ppermute | solution.py:912
  194.5 16.1 %collective-permute-start.13 = (bf16[1152,256]{1,0:T(8,128)(2,1)S(1)}, bf16[1152,256]{1,0:T(8,128)(2,1)S(1)}, u32[]{:S(2)}, u32[]{:S(2)}) collective-permute-start(bf16[1152,256]{1,0:T(8,128)(2,1)S(1)} %pad_maximum_fusion.7), channel_id=1, source_target_pairs={{0,16},{2,6},{4,20},{6,2},{8,24},{10,14},{12,28},{14,10},{16,0},{1... | collective-permute-start | bytes 1769480 | tf_op jit(solution)/shard_map/ppermute | solution.py:912
  206.8 16.2 %collective-permute-start.15 = (bf16[4736,256]{1,0:T(8,128)(2,1)}, bf16[4736,256]{1,0:T(8,128)(2,1)S(1)}, u32[]{:S(2)}, u32[]{:S(2)}) collective-permute-start(bf16[4736,256]{1,0:T(8,128)(2,1)} %get-tuple-element.233), channel_id=1, source_target_pairs={{0,2},{1,3},{2,0},{3,1},{4,6},{5,7},{6,4},{7,5},{8,10},{9,11},{10,... | collective-permute-start | bytes 7274504 | tf_op jit(solution)/shard_map/ppermute | solution.py:912
  207.0 24.0 %collective-permute-start.17 = (bf16[1152,256]{1,0:T(8,128)(2,1)S(1)}, bf16[1152,256]{1,0:T(8,128)(2,1)S(1)}, u32[]{:S(2)}, u32[]{:S(2)}) collective-permute-start(bf16[1152,256]{1,0:T(8,128)(2,1)S(1)} %pad_maximum_fusion.8), channel_id=1, source_target_pairs={{0,16},{2,6},{4,20},{6,2},{8,24},{10,14},{12,28},{14,10},{16,0},{1... | collective-permute-start | bytes 1769480 | tf_op jit(solution)/shard_map/ppermute | solution.py:912
  210.8 18.3 %collective-permute-start.18 = (bf16[2304,256]{1,0:T(8,128)(2,1)S(1)}, bf16[2304,256]{1,0:T(8,128)(2,1)S(1)}, u32[]{:S(2)}, u32[]{:S(2)}) collective-permute-start(bf16[2304,256]{1,0:T(8,128)(2,1)S(1)} %pad_maximum_fusion.4), channel_id=1, source_target_pairs={{0,4},{2,10},{4,0},{6,14},{8,12},{10,2},{12,8},{14,6},{16,20},{18,... | collective-permute-start | bytes 3538952 | tf_op jit(solution)/shard_map/ppermute | solution.py:912
  211.9 0.9 copy-start.15
  229.4 1.8 copy-start.3
  229.5 38.4 %collective-permute-start.22 = (bf16[4608,256]{1,0:T(8,128)(2,1)S(1)}, bf16[4608,256]{1,0:T(8,128)(2,1)}, u32[]{:S(2)}, u32[]{:S(2)}) collective-permute-start(bf16[4608,256]{1,0:T(8,128)(2,1)S(1)} %pad_maximum_fusion.1.value_ref), channel_id=1, source_target_pairs={{0,2},{2,0},{4,6},{6,4},{8,10},{10,8},{12,14},{14,12},{16,18},{18,... | collective-permute-start | bytes 7077896 | tf_op jit(solution)/shard_map/ppermute | solution.py:912
  230.7 16.9 %collective-permute-start.16 = (bf16[2368,256]{1,0:T(8,128)(2,1)}, bf16[2368,256]{1,0:T(8,128)(2,1)}, u32[]{:S(2)}, u32[]{:S(2)}) collective-permute-start(bf16[2368,256]{1,0:T(8,128)(2,1)} %get-tuple-element.310), channel_id=1, source_target_pairs={{0,1},{1,0},{2,6},{3,7},{4,5},{5,4},{6,2},{7,3},{8,9},{9,8},{10,14... | collective-permute-start | bytes 3637256 | tf_op jit(solution)/shard_map/ppermute | solution.py:912
  231.2 40.2 %collective-permute-start.21 = (bf16[2304,256]{1,0:T(8,128)(2,1)S(1)}, bf16[2304,256]{1,0:T(8,128)(2,1)}, u32[]{:S(2)}, u32[]{:S(2)}) collective-permute-start(bf16[2304,256]{1,0:T(8,128)(2,1)S(1)} %pad_maximum_fusion.5), channel_id=1, source_target_pairs={{0,4},{2,10},{4,0},{6,14},{8,12},{10,2},{12,8},{14,6},{16,20},{18,... | collective-permute-start | bytes 3538952 | tf_op jit(solution)/shard_map/ppermute | solution.py:912
  250.5 15.3 %collective-permute-start.19 = (bf16[1184,256]{1,0:T(8,128)(2,1)}, bf16[1184,256]{1,0:T(8,128)(2,1)}, u32[]{:S(2)}, u32[]{:S(2)}) collective-permute-start(bf16[1184,256]{1,0:T(8,128)(2,1)} %get-tuple-element.318), channel_id=1, source_target_pairs={{0,4},{1,5},{2,3},{3,2},{4,0},{5,1},{6,7},{7,6},{8,12},{9,13},{10,... | collective-permute-start | bytes 1818632 | tf_op jit(solution)/shard_map/ppermute | solution.py:912
  251.5 14.3 %copy-start.4 = (bf16[1184,256]{1,0:T(8,128)(2,1)S(1)}, bf16[1184,256]{1,0:T(8,128)(2,1)}, u32[]{:S(2)}) copy-start(bf16[1184,256]{1,0:T(8,128)(2,1)} %get-tuple-element.256) | copy-start | bytes 1818628
  272.9 14.6 %copy-start.8 = (bf16[592,256]{1,0:T(8,128)(2,1)S(1)}, bf16[592,256]{1,0:T(8,128)(2,1)}, u32[]{:S(2)}) copy-start(bf16[592,256]{1,0:T(8,128)(2,1)} %get-tuple-element.263) | copy-start | bytes 909316
  273.1 24.0 %copy-start.2 = (bf16[4608,256]{1,0:T(8,128)(2,1)}, bf16[4608,256]{1,0:T(8,128)(2,1)S(1)}, u32[]{:S(2)}) copy-start(bf16[4608,256]{1,0:T(8,128)(2,1)S(1)} %pad_maximum_fusion.2.value_ref) | copy-start | bytes 7077892
  273.1 32.0 %collective-permute-start.26 = (bf16[4608,256]{1,0:T(8,128)(2,1)S(1)}, bf16[4608,256]{1,0:T(8,128)(2,1)}, u32[]{:S(2)}, u32[]{:S(2)}) collective-permute-start(bf16[4608,256]{1,0:T(8,128)(2,1)S(1)} %pad_maximum_fusion.2.value_ref), channel_id=1, source_target_pairs={{0,2},{2,0},{4,6},{6,4},{8,10},{10,8},{12,14},{14,12},{16,18},{18,... | collective-permute-start | bytes 7077896 | tf_op jit(solution)/shard_map/ppermute | solution.py:912
  278.0 9.5 %collective-permute-start.20 = (bf16[592,256]{1,0:T(8,128)(2,1)}, bf16[592,256]{1,0:T(8,128)(2,1)S(1)}, u32[]{:S(2)}, u32[]{:S(2)}) collective-permute-start(bf16[592,256]{1,0:T(8,128)(2,1)} %get-tuple-element.332), channel_id=1, source_target_pairs={{0,8},{1,9},{2,10},{3,11},{4,12},{5,13},{6,14},{7,15},{8,0},{9,1},... | collective-permute-start | bytes 909320 | tf_op jit(solution)/shard_map/ppermute | solution.py:912
  287.5 9.4 %collective-permute-start.23 = (bf16[296,256]{1,0:T(8,128)(2,1)S(1)}, bf16[296,256]{1,0:T(8,128)(2,1)S(1)}, u32[]{:S(2)}, u32[]{:S(2)}) collective-permute-start(bf16[296,256]{1,0:T(8,128)(2,1)S(1)} %get-tuple-element.344), channel_id=1, source_target_pairs={{0,16},{1,17},{2,18},{3,19},{4,20},{5,21},{6,22},{7,23},{8,24},{9,... | collective-permute-start | bytes 454664 | tf_op jit(solution)/shard_map/ppermute | solution.py:912
  297.0 8.0 %collective-permute-start.24 = (bf16[296,256]{1,0:T(8,128)(2,1)S(1)}, bf16[296,256]{1,0:T(8,128)(2,1)S(1)}, u32[]{:S(2)}, u32[]{:S(2)}) collective-permute-start(bf16[296,256]{1,0:T(8,128)(2,1)S(1)} %add_convert_fusion.20), channel_id=1, source_target_pairs={{0,16},{1,17},{2,18},{3,19},{4,20},{5,21},{6,22},{7,23},{8,24},{9,... | collective-permute-start | bytes 454664 | tf_op jit(solution)/shard_map/ppermute | solution.py:912
  305.0 9.0 %collective-permute-start.25 = (bf16[592,256]{1,0:T(8,128)(2,1)S(1)}, bf16[592,256]{1,0:T(8,128)(2,1)S(1)}, u32[]{:S(2)}, u32[]{:S(2)}) collective-permute-start(bf16[592,256]{1,0:T(8,128)(2,1)S(1)} %pad_maximum_fusion.9), channel_id=1, source_target_pairs={{0,8},{1,9},{2,10},{3,11},{4,12},{5,13},{6,14},{7,15},{8,0},{9,1},... | collective-permute-start | bytes 909320 | tf_op jit(solution)/shard_map/ppermute | solution.py:912
  314.1 10.1 %collective-permute-start.27 = (bf16[1184,256]{1,0:T(8,128)(2,1)S(1)}, bf16[1184,256]{1,0:T(8,128)(2,1)S(1)}, u32[]{:S(2)}, u32[]{:S(2)}) collective-permute-start(bf16[1184,256]{1,0:T(8,128)(2,1)S(1)} %pad_maximum_fusion.6), channel_id=1, source_target_pairs={{0,4},{1,5},{2,3},{3,2},{4,0},{5,1},{6,7},{7,6},{8,12},{9,13},{10,... | collective-permute-start | bytes 1818632 | tf_op jit(solution)/shard_map/ppermute | solution.py:912
  324.4 16.6 %collective-permute-start.28 = (bf16[2368,256]{1,0:T(8,128)(2,1)S(1)}, bf16[2368,256]{1,0:T(8,128)(2,1)S(1)}, u32[]{:S(2)}, u32[]{:S(2)}) collective-permute-start(bf16[2368,256]{1,0:T(8,128)(2,1)S(1)} %pad_maximum_fusion.3), channel_id=1, source_target_pairs={{0,1},{1,0},{2,6},{3,7},{4,5},{5,4},{6,2},{7,3},{8,9},{9,8},{10,14... | collective-permute-start | bytes 3637256 | tf_op jit(solution)/shard_map/ppermute | solution.py:912
  341.4 1.4 copy-start
  341.4 6.2 %collective-permute-start.29 = (bf16[4736,256]{1,0:T(8,128)(2,1)S(1)}, bf16[4736,256]{1,0:T(8,128)(2,1)S(1)}, u32[]{:S(2)}, u32[]{:S(2)}) collective-permute-start(bf16[4736,256]{1,0:T(8,128)(2,1)S(1)} %pad_maximum_fusion.value_ref.mine_ref), channel_id=1, source_target_pairs={{0,2},{1,3},{2,0},{3,1},{4,6},{5,7},{6,4},{7,5},{8,10},{9,11},{10,... | collective-permute-start | bytes 7274504 | tf_op jit(solution)/shard_map/ppermute | solution.py:912
  347.6 1.4 copy-start.1

commit v5 on v4

--- a/solution.py
+++ b/solution.py
@@ -596,6 +596,7 @@
 
 
 def weight_kernel(
+    spare,
     side_ref,
     normed_ref,
     image_ref,
@@ -604,22 +605,18 @@
     gv_ref,
     gik_ref,
     giv_ref,
-    extra_ref,
-    sums_ref,
-    keep_ref,
-    send_ref,
-    keep,
-    send,
-    sems,
+    *refs,
 ):
+    extra_ref = None if spare else refs[0]
+    sums_ref, keep_ref, send_ref, keep, send, sems = refs[-6:]
     step = pl.program_id(0)
     width = normed_ref.shape[1]
     half = width // 2
-    block = half * width // LANES
+    columns = gq_ref.shape[1] // LANES
+    block = half * (columns if spare else columns + 1)
 
     def copies(part):
-        rows = block if part < 4 else SMALL
-        span = pl.ds(part * block, rows)
+        span = pl.ds(part * block, block if part < 3 else spare)
         pairs = ((keep, keep_ref), (send, send_ref))
         return [
             pltpu.make_async_copy(here.at[span], there.at[span], sems.at[number, part])
@@ -627,10 +624,13 @@
         ]
 
     def store(part, total):
+        if extra_ref is not None:
+            more = extra_ref[:, part * LANES : (part + 1) * LANES].astype(f32)
+            total = jnp.concatenate([total, more], axis=1)
         first = side_ref[0] == 0
         mine = jnp.where(first, total[:half], total[half:]).astype(bf16)
         other = jnp.where(first, total[half:], total[:half]).astype(bf16)
-        for number in range(width // LANES):
+        for number in range(block // half):
             rows = slice(part * block + number * half, part * block + (number + 1) * half)
             cols = slice(number * LANES, (number + 1) * LANES)
             keep[rows, :] = mine[:, cols]
@@ -654,36 +654,35 @@
         store(2, total + dot(image_ref[...], giv_ref[...], TN))
         sums = column_sum(gv_ref[...].astype(f32)) + column_sum(giv_ref[...].astype(f32))
         sums_ref[1:2] = sums
-
-    @pl.when(step == 3)
-    def _():
-        store(3, extra_ref[...].astype(f32))
-        keep[4 * block :, :] = jnp.zeros((SMALL, LANES), bf16)
-        send[4 * block :, :] = jnp.zeros((SMALL, LANES), bf16)
-        for copy in copies(4):
-            copy.start()
-        for part in range(5):
+        if spare:
+            keep[3 * block :, :] = jnp.zeros((spare, LANES), bf16)
+            send[3 * block :, :] = jnp.zeros((spare, LANES), bf16)
+            for copy in copies(3):
+                copy.start()
+        for part in range(4 if spare else 3):
             for copy in copies(part):
                 copy.wait()
 
 
-def weight_grads(order, side, normed, image, grads, extra):
+def weight_grads(order, side, normed, image, grads, lanes, place, spare, extra):
     rows, width = normed.shape
-    all_rows = 4 * (width * width // 2 // LANES) + SMALL
-    inputs = (normed, image, *grads, extra)
+    half_rows = 3 * (lanes // LANES + len(extra)) * width // 2 + spare
+    column = lambda height: pl.BlockSpec((height, lanes), lambda *_: (0, place))
     anywhere = pl.BlockSpec(memory_space=pl.ANY)
     return call(
         order,
-        weight_kernel,
-        inputs,
-        [shaped((2, width), f32)] + [shaped((all_rows, LANES), bf16)] * 2,
+        functools.partial(weight_kernel, spare),
+        (normed, image, *grads, *extra),
+        [shaped((2, lanes), f32)] + [shaped((half_rows, LANES), bf16)] * 2,
         "weight_grads",
-        cost(8 * rows * width * width, 12 << 20),
+        cost(8 * rows * width * lanes, 12 << 20),
         scalars=(side,),
-        grid=(4,),
-        specs=[resident(value.shape) for value in inputs],
-        outs=[resident((2, width)), anywhere, anywhere],
-        scratch=[pltpu.VMEM((all_rows, LANES), bf16)] * 2 + [pltpu.SemaphoreType.DMA((2, 5))],
+        grid=(3,),
+        specs=[resident(normed.shape), resident(image.shape)]
+        + [column(value.shape[0]) for value in grads]
+        + [resident(value.shape) for value in extra],
+        outs=[resident((2, lanes)), anywhere, anywhere],
+        scratch=[pltpu.VMEM((half_rows, LANES), bf16)] * 2 + [pltpu.SemaphoreType.DMA((2, 4))],
     )
 
 
@@ -720,7 +719,8 @@
     gain_ref,
     weight_ref,
     feed_sums_ref,
-    bias_sums_ref,
+    first_sums_ref,
+    last_sums_ref,
     _,
     out_ref,
     small_ref,
@@ -748,7 +748,8 @@
         pad = lambda count: jnp.zeros((count, width), f32)
         own = [sums[0:2], feed_sums_ref[0:3], feed_sums_ref[4:8], pad(7)]
         own = jnp.concatenate(own, axis=0)
-        shared = [pad(9), feed_sums_ref[3:4], bias_sums_ref[...], pad(4)]
+        bias_sums = jnp.concatenate([first_sums_ref[...], last_sums_ref[...]], axis=1)
+        shared = [pad(9), feed_sums_ref[3:4], bias_sums, pad(4)]
         shared = jnp.concatenate(shared, axis=0)
         is_text = flag_ref[0] == 1
         first = jnp.where(is_text, 0.0, own) + shared
@@ -767,7 +768,7 @@
     blocks = item_rows // IMG_PAD
     mine = pl.BlockSpec((IMG_PAD, width), lambda i, j, *_: (i * blocks + j, 0))
     image = pl.BlockSpec((IMG_PAD, width), lambda i, j, *_: (i, 0))
-    fixed = (gain, weight, feed_sums, bias_sums)
+    fixed = (gain, weight, feed_sums, *bias_sums)
     place = keep.shape[0] // SMALL - 1
     return call(
         order,
@@ -783,7 +784,7 @@
         + [pl.BlockSpec(memory_space=pl.ANY)],
         outs=[mine, pl.BlockSpec((SMALL, LANES), lambda *_: (place, 0))],
         scratch=[pltpu.VMEM((8, width), f32)],
-        aliases={12: 1},
+        aliases={13: 1},
     )
 
 
@@ -819,30 +820,23 @@
     )
 
 
-def store_projection(value_ref, in_ref, out_ref):
-    tall, wide = in_ref.shape
-
-    def store(ref):
-        for part in range(wide // LANES):
-            piece = value_ref[part * tall : (part + 1) * tall, :]
-            ref[:, part * LANES : (part + 1) * LANES] = piece.astype(f32)
-
-    @pl.when(pl.program_id(0) < 3)
-    def _():
-        store(in_ref)
-
-    @pl.when(pl.program_id(0) == 3)
-    def _():
-        store(out_ref)
-
-
-def projection_kernel(half_ref, value_ref, in_ref, out_ref):
-    store_projection(value_ref, in_ref, out_ref)
-
-
-def last_kernel(half_ref, flag_ref, value_ref, mine_ref, got_ref, *refs):
+def store_projection(first_ref, last_ref, in_ref, out_ref):
+    tall = in_ref.shape[0]
+    count = first_ref.shape[0] // tall
+    for part in range(count - 1):
+        piece = first_ref[part * tall : (part + 1) * tall, :]
+        in_ref[:, part * LANES : (part + 1) * LANES] = piece.astype(f32)
+    in_ref[:, (count - 1) * LANES :] = last_ref[...].astype(f32)
+    out_ref[...] = first_ref[(count - 1) * tall :, :].astype(f32)
+
+
+def projection_kernel(half_ref, first_ref, last_ref, in_ref, out_ref):
+    store_projection(first_ref, last_ref, in_ref, out_ref)
+
+
+def last_kernel(half_ref, flag_ref, first_ref, last_ref, mine_ref, got_ref, *refs):
     in_ref, out_ref, *vec_refs, expand_ref, pair_ref, project_ref = refs[2:]
-    store_projection(value_ref, in_ref, out_ref)
+    store_projection(first_ref, last_ref, in_ref, out_ref)
 
     @pl.when(pl.program_id(0) == 0)
     def _():
@@ -861,47 +855,50 @@
 
 def projection_specs(width):
     tall = width // 2
-    value = pl.BlockSpec((tall * width // LANES, LANES), lambda b, *_: (b, 0))
+    ins = [
+        pl.BlockSpec((tall * width // LANES, LANES), lambda b, *_: (b, 0)),
+        pl.BlockSpec((tall, LANES), lambda b, *_: (b, 0)),
+    ]
     outs = [
-        pl.BlockSpec((tall, width), lambda b, at, *_: (at[0], jnp.minimum(b, 2))),
-        pl.BlockSpec((tall, width), lambda b, at, *_: (at[0], 0)),
+        pl.BlockSpec((tall, width), lambda b, at, *_: (at[0], b)),
+        pl.BlockSpec((tall, LANES), lambda b, at, *_: (at[0], b)),
     ]
-    return value, outs, [shaped((width, 3 * width), f32), shaped((width, width), f32)]
-
-
-def projection_outputs(order, half, value, width):
-    spec, outs, shapes = projection_specs(width)
+    return ins, outs, [shaped((width, 3 * width), f32), shaped((width, width), f32)]
+
+
+def projection_outputs(order, half, first, last, width):
+    ins, outs, shapes = projection_specs(width)
     return call(
         order,
         projection_kernel,
-        (value,),
+        (first, last),
         shapes,
         "projection_outputs",
-        cost(value.size, 6 * value.size),
+        cost(first.size, 6 * first.size),
         scalars=(half,),
-        grid=(4,),
-        specs=[spec],
+        grid=(3,),
+        specs=ins,
         outs=outs,
     )
 
 
-def last_outputs(order, half, flag, mine, got, width, units, earlier):
-    spec, outs, shapes = projection_specs(width)
+def last_outputs(order, half, flag, first, mine, got, width, units, earlier):
+    ins, outs, shapes = projection_specs(width)
     place = got.shape[0] // SMALL - 1
     small = pl.BlockSpec((SMALL, LANES), lambda *_: (place, 0))
     vecs = [(1, width)] * 5 + [(1, units), (2, width), (1, width)]
     return call(
         order,
         last_kernel,
-        (got, mine, got, *earlier),
+        (first, got, mine, got, *earlier),
         shapes + [shaped(shape, f32) for shape in vecs],
         "last_outputs",
         cost(got.size, 6 * got.size),
         scalars=(half, flag),
-        grid=(4,),
-        specs=[spec, small, small] + [pl.BlockSpec(memory_space=pl.ANY)] * 2,
+        grid=(3,),
+        specs=ins + [small, small] + [pl.BlockSpec(memory_space=pl.ANY)] * 2,
         outs=outs + [resident(shape) for shape in vecs],
-        aliases={5: 0, 6: 1},
+        aliases={6: 0, 7: 1},
     )
 
 
@@ -1079,6 +1076,14 @@
             grads,
         )
 
+    def weights(lanes, place, spare, *extra):
+        return weight_grads(
+            order, side, normed, images[0], grads, lanes, place, spare, extra
+        )
+
+    def unpack(half, first, value, earlier=()):
+        return expert_outputs(order, half, first, value, width, units, earlier)
+
     grads = backward(0, 0, 2)
     a.step()
     grads = backward(1, 0, 2)
@@ -1087,17 +1092,22 @@
     a.step()
     grads = backward(1, 2, 2)
     c.step()
+    first_sums, keep, send = weights(2 * LANES, 0, 0, project_out_grad)
+    s = Total(order, ("dp", "mod"), keep, send)
+    a.step()
     grads = backward(0, 4, 2)
+    s.step()
     a.step()
     grads = backward(1, 4, 2)
-    a.step()
     c.step()
+    s.step()
     near = image_grads(order, project_in, grads[3], grads[4])
     far = to_image(near)
     c.step()
     a.step()
-    bias_sums, keep, send = weight_grads(order, side, normed, images[0], grads, project_out_grad)
+    last_sums, keep, send = weights(LANES, 2, SMALL)
     p = Total(order, ("dp", "mod"), keep, send)
+    s.step()
     c.step()
     a.step()
     (far,) = order.after(far)
@@ -1113,27 +1123,35 @@
         attend_gain,
         project_in,
         feed_sums,
-        bias_sums,
+        (first_sums, last_sums),
         keep,
         rows,
     )
     p.terms = (keep, p.got)
     p.step()
+    s.step()
     a.step()
+    p.step()
     c.step()
     p.step()
-    outputs = expert_outputs(order, side, 0, a.mine, width, units, ())
+    s.step()
+    outputs = unpack(side, 0, a.mine)
     p.step()
-    outputs = expert_outputs(order, 1 - side, 0, a.got, width, units, outputs)
+    s.step()
+    p.step()
+    outputs = unpack(1 - side, 0, a.got, outputs)
+    p.step()
+    s.step()
     c.step()
     p.step()
+    s.step()
+    outputs = unpack(side, 2, c.mine, outputs)
     p.step()
-    outputs = expert_outputs(order, side, 2, c.mine, width, units, outputs)
-    p.step()
-    reduce_grad, expand_grad = expert_outputs(order, 1 - side, 2, c.got, width, units, outputs)
+    s.step()
+    reduce_grad, expand_grad = unpack(1 - side, 2, c.got, outputs)
     while p.back:
         p.step()
-    projections = projection_outputs(order, side, p.mine, width)
+    projections = projection_outputs(order, side, s.mine, p.mine, width)
     (
         project_in_grad,
         project_out_grad,
@@ -1145,7 +1163,7 @@
         expand_bias_grad,
         bias_pair_grad,
         project_bias_grad,
-    ) = last_outputs(order, 1 - side, flag, p.mine, p.got, width, units, projections)
+    ) = last_outputs(order, 1 - side, flag, s.got, p.mine, p.got, width, units, projections)
     return (
         hidden_out.reshape(hidden_in.shape),
         grad_in.reshape(hidden_in.shape),

time: 362 us -> 363 us (level)
  waiting for transfers between devices: 97.1 us -> 68.6 us
  starting transfers between devices: 41.1 us -> 64.7 us
  other arithmetic: 21.8 us -> 26.7 us
    ppermute x26 -> x36, waiting for transfers between devices: 97 us -> 68.6 us  [swap(): lax.ppermute(value, axes, [(source, pair_of(source)) for source in range(...]
    ppermute x26 -> x36, starting transfers between devices: 32.3 us -> 55.9 us  [swap(): lax.ppermute(value, axes, [(source, pair_of(source)) for source in range(...]
    select_n x10 -> x14, other arithmetic: 2.16 us -> 6.11 us  [step(): low = jnp.where(self.last == 0, mine, got)]
    pallas_call x21 -> x22, Pallas kernels: 186 us -> 188 us  [call(): pl.pallas_call(kernel, grid_spec=pltpu.PrefetchScalarGridSpec(num_scalar_...]
    convert_element_type x10 -> x14, other arithmetic: 17.3 us -> 17 us  [part(): return (cut(self.terms[0]) + cut(self.terms[1])).astype(bf16)]
  transfers between devices with their start and end apart: 30 -> 40, of which waited for: 14 -> 14; matrix products, arithmetic and copies ran while one was open for 5% -> 7% of each run, Pallas kernels for 34% -> 32%
where the time goes in v5:
time: 363 us; the launch traced here: 357 us
  Pallas kernels  188 us (52%)
  waiting for transfers between devices  68.6 us (19%)
  starting transfers between devices  64.7 us (18%)
  other arithmetic  26.7 us (7%)
  local copies, waits for them, and re-layouts  7.2 us (2%)
    pallas_call x22, Pallas kernels, call(): pl.pallas_call(kernel, grid_spec=pltpu.PrefetchScalarGridSpec(num_scalar_...  188 us
    ppermute x36, waiting for transfers between devices, swap(): lax.ppermute(value, axes, [(source, pair_of(source)) for source in range(...  68.6 us
    ppermute x36, starting transfers between devices, swap(): lax.ppermute(value, axes, [(source, pair_of(source)) for source in range(...  55.9 us
    convert_element_type x14, other arithmetic, part(): return (cut(self.terms[0]) + cut(self.terms[1])).astype(bf16)  17 us
    ppermute x3, starting transfers between devices, on_device(): to_text = lambda value: lax.ppermute(value, 'mod', [(0, 1)])  7.5 us
  transfers between devices with their start and end apart: 40, of which 14 were waited for; matrix products, arithmetic and copies ran while one was open for 7% of the time, Pallas kernels for 32%

profile of v5, /device:TPU:0, one launch (start us, length us, event | category | flops | bytes accessed | tf_op | source)
XLA Modules:
  0.0 356.9 jit_solution(11907559683646105580)
XLA Ops:
  1.8 4.9 %collective-permute-start = (bf16[256,768]{1,0:T(8,128)(2,1)S(1)}, bf16[256,768]{1,0:T(8,128)(2,1)S(1)}, u32[]{:S(2)}, u32[]{:S(2)}) collective-permute-start(bf16[256,768]{1,0:T(8,128)(2,1)S(1)} %get-tuple-element.373), channel_id=1, source_target_pairs={{0,1},{2,3},{4,5},{6,7},{8,9},{10,11},{12,13},{14,15},{16,17},{18,... | collective-permute-start | bytes 1179656 | tf_op jit(solution)/shard_map/ppermute | solution.py:1003
  9.4 8.5 %project_rows.1 = (bf16[1024,768]{1,0:T(8,128)(2,1)}, bf16[1024,2304]{1,0:T(8,128)(2,1)}) custom-call(bf16[1024,768]{1,0:T(8,128)(2,1)} %bitcast.20, f32[1,768]{1,0:T(1,128)} %gain_ref.9, f32[1,768]{1,0:T(1,128)} %shift_ref.6, bf16[768,2304]{1,0:T(8,128)(2,1)} %weight_ref.3, f32[2,768]{1,0:T(2,128)} %bias_ref.5), custom_call_target="tpu_custom_call" | custom-call | flops 3623878656 | bytes 11403264 | tf_op jit(solution)/shard_map/project_rows/pallas_call | solution.py:75
  19.2 3.8 %image_rows.2 = (bf16[512,768]{1,0:T(8,128)(2,1)}, bf16[512,1536]{1,0:T(8,128)(2,1)}) custom-call(s32[1]{0:T(128)} %bitcast.flag_ref, bf16[1024,768]{1,0:T(8,128)(2,1)} %bitcast.21, bf16[256,768]{1,0:T(8,128)(2,1)} %copy-done.14, f32[1,768]{1,0:T(1,128)} %gain_ref.9, f32[1,768]{1,0:T(1,128)} %shift_ref.6, f32[2,768]{1,0:T(2,128)} %copy-done.17, ...), custom_call_target="tpu_custom_call" | custom-call | flops 603979776 | bytes 6291456 | tf_op jit(solution)/shard_map/image_rows/pallas_call | solution.py:75
  23.1 12.3 %attend_forward.2 = (bf16[512,768]{1,0:T(8,128)(2,1)}, f32[6,2,512]{2,1,0:T(2,128)}) custom-call(s32[1]{0:T(128)} %bitcast.flag_ref, s32[2]{0:T(128)} %count_ref.17, s32[2,4]{1,0:T(2,128)} %lengths_ref.15, bf16[1024,2304]{1,0:T(8,128)(2,1)} %get-tuple-element.242.q_ref.k_ref.v_ref, bf16[1024,2304]{1,0:T(8,128)(2,1)} %get-tuple-element.242.q_ref.k_ref.v_ref, ...), custom_call_target="tpu_custom_call" | custom-call | flops 4831838208 | bytes 6291456 | tf_op jit(solution)/shard_map/attend_forward/pallas_call | solution.py:75
  36.1 3.9 %image_rows.3 = (bf16[512,768]{1,0:T(8,128)(2,1)}, bf16[512,1536]{1,0:T(8,128)(2,1)}) custom-call(s32[1]{0:T(128)} %bitcast.flag_ref, bf16[1024,768]{1,0:T(8,128)(2,1)} %bitcast.22, bf16[256,768]{1,0:T(8,128)(2,1)} %copy-done.13, f32[1,768]{1,0:T(1,128)} %gain_ref.9, f32[1,768]{1,0:T(1,128)} %shift_ref.6, ...), custom_call_target="tpu_custom_call", output_to_operand_aliasing={{0}: (9, {}), {1}: (10, {})} | custom-call | flops 603979776 | bytes 6291456 | tf_op jit(solution)/shard_map/image_rows/pallas_call | solution.py:75
  40.0 12.3 %attend_forward.3 = (bf16[512,768]{1,0:T(8,128)(2,1)}, f32[6,2,512]{2,1,0:T(2,128)}) custom-call(s32[1]{0:T(128)} %bitcast.flag_ref, s32[2]{0:T(128)} %count_ref.17, s32[2,4]{1,0:T(2,128)} %lengths_ref.15, bf16[1024,2304]{1,0:T(8,128)(2,1)} %get-tuple-element.242.q_ref.k_ref.v_ref, bf16[1024,2304]{1,0:T(8,128)(2,1)} %get-tuple-element.242.q_ref.k_ref.v_ref, ...), custom_call_target="tpu_custom_call" | custom-call | flops 4831838208 | bytes 6291456 | tf_op jit(solution)/shard_map/attend_forward/pallas_call | solution.py:75
  52.3 45.2 %feed_forward.1 = (bf16[1024,768]{1,0:T(8,128)(2,1)}, f32[1024,768]{1,0:T(8,128)}, bf16[1024,768]{1,0:T(8,128)(2,1)}, bf16[768,768]{1,0:T(8,128)(2,1)}, f32[8,76...) custom-call(s32[1]{0:T(128)} %bitcast.flag_ref, ...), custom_call_target="tpu_custom_call" | custom-call | flops 28991029248 | bytes 41943040 | tf_op jit(solution)/shard_map/feed_forward/pallas_call | solution.py:75
  98.1 8.2 %attend_backward.6 = (bf16[1024,768]{1,0:T(8,128)(2,1)}, bf16[1024,768]{1,0:T(8,128)(2,1)}, bf16[1024,768]{1,0:T(8,128)(2,1)}, bf16[512,768]{1,0:T(8,128)(2,1)}, bf16[512,768]{1,0:T(8,128)(2,1)}) custom-call(s32[1]{0:T(128)} %bitcast.flag_ref, s32[2]{0:T(128)} %count_ref.17, s32[2,4]{1,0:T(2,128)} %lengths_ref.15, ...), custom_call_target="tpu_custom_call" | custom-call | flops 4026531840 | bytes 4194304 | tf_op jit(solution)/shard_map/attend_backward/pallas_call | solution.py:75
  107.7 3.2 add_convert_fusion
  112.4 8.2 %attend_backward.7 = (bf16[1024,768]{1,0:T(8,128)(2,1)}, bf16[1024,768]{1,0:T(8,128)(2,1)}, bf16[1024,768]{1,0:T(8,128)(2,1)}, bf16[512,768]{1,0:T(8,128)(2,1)}, bf16[512,768]{1,0:T(8,128)(2,1)}) custom-call(s32[1]{0:T(128)} %bitcast.flag_ref, s32[2]{0:T(128)} %count_ref.17, ...), custom_call_target="tpu_custom_call", output_to_operand_aliasing={{0}: (11, {}), {1}: (12, {}), {2}: (13, {}), {3}: (14, {}),... | custom-call | flops 4026531840 | bytes 4194304 | tf_op jit(solution)/shard_map/attend_backward/pallas_call | solution.py:75
  120.6 3.2 add_convert_fusion.1
  124.4 8.1 %attend_backward.8 = (bf16[1024,768]{1,0:T(8,128)(2,1)}, bf16[1024,768]{1,0:T(8,128)(2,1)}, bf16[1024,768]{1,0:T(8,128)(2,1)}, bf16[512,768]{1,0:T(8,128)(2,1)}, bf16[512,768]{1,0:T(8,128)(2,1)}) custom-call(s32[1]{0:T(128)} %bitcast.flag_ref, s32[2]{0:T(128)} %count_ref.17, ...), custom_call_target="tpu_custom_call", output_to_operand_aliasing={{0}: (11, {}), {1}: (12, {}), {2}: (13, {}), {3}: (14, {}),... | custom-call | flops 4026531840 | bytes 4194304 | tf_op jit(solution)/shard_map/attend_backward/pallas_call | solution.py:75
  132.5 2.4 add_convert_fusion.7
  134.8 8.3 %attend_backward.9 = (bf16[1024,768]{1,0:T(8,128)(2,1)}, bf16[1024,768]{1,0:T(8,128)(2,1)}, bf16[1024,768]{1,0:T(8,128)(2,1)}, bf16[512,768]{1,0:T(8,128)(2,1)}, bf16[512,768]{1,0:T(8,128)(2,1)}) custom-call(s32[1]{0:T(128)} %bitcast.flag_ref, s32[2]{0:T(128)} %count_ref.17, ...), custom_call_target="tpu_custom_call", output_to_operand_aliasing={{0}: (11, {}), {1}: (12, {}), {2}: (13, {}), {3}: (14, {}),... | custom-call | flops 4026531840 | bytes 4194304 | tf_op jit(solution)/shard_map/attend_backward/pallas_call | solution.py:75
  143.2 2.4 add_convert_fusion.6
  145.5 9.3 %weight_grads.2 = (f32[2,512]{1,0:T(2,128)}, bf16[3456,256]{1,0:T(8,128)(2,1)}, bf16[3456,256]{1,0:T(8,128)(2,1)}) custom-call(s32[1]{0:T(128)} %bitcast.1.side_ref.half_ref, bf16[1024,768]{1,0:T(8,128)(2,1)} %get-tuple-element.258.normed_ref, bf16[512,768]{1,0:T(8,128)(2,1)} %get-tuple-element.226.image_ref, ...), custom_call_target="tpu_custom_call" | custom-call | flops 3221225472 | bytes 12582912 | tf_op jit(solution)/shard_map/weight_grads/pallas_call | solution.py:75
  154.9 2.7 collective-permute-start.8
  157.6 21.0 %collective-permute-done.8 = bf16[1152,256]{1,0:T(8,128)(2,1)S(1)} collective-permute-done((bf16[1152,256]{1,0:T(8,128)(2,1)}, bf16[1152,256]{1,0:T(8,128)(2,1)S(1)}, u32[]{:S(2)}, u32[]{:S(2)}) %collective-permute-start.8) | collective-permute-done | bytes 589856 | tf_op jit(solution)/shard_map/ppermute | solution.py:909
  179.6 8.1 %attend_backward.10 = (bf16[1024,768]{1,0:T(8,128)(2,1)}, bf16[1024,768]{1,0:T(8,128)(2,1)}, bf16[1024,768]{1,0:T(8,128)(2,1)}, bf16[512,768]{1,0:T(8,128)(2,1)}, bf16[512,768]{1,0:T(8,128)(2,1)}) custom-call(s32[1]{0:T(128)} %bitcast.flag_ref, s32[2]{0:T(128)} %count_ref.17, ...), custom_call_target="tpu_custom_call", output_to_operand_aliasing={{0}: (11, {}), {1}: (12, {}), {2}: (13, {}), {3}: (14, {}),... | custom-call | flops 4026531840 | bytes 4194304 | tf_op jit(solution)/shard_map/attend_backward/pallas_call | solution.py:75
  189.5 3.3 collective-permute-start.10
  192.8 8.3 %attend_backward.11 = (bf16[1024,768]{1,0:T(8,128)(2,1)}, bf16[1024,768]{1,0:T(8,128)(2,1)}, bf16[1024,768]{1,0:T(8,128)(2,1)}, bf16[512,768]{1,0:T(8,128)(2,1)}, bf16[512,768]{1,0:T(8,128)(2,1)}) custom-call(s32[1]{0:T(128)} %bitcast.flag_ref, s32[2]{0:T(128)} %count_ref.17, ...), custom_call_target="tpu_custom_call", output_to_operand_aliasing={{0}: (11, {}), {1}: (12, {}), {2}: (13, {}), {3}: (14, {}),... | custom-call | flops 4026531840 | bytes 4194304 | tf_op jit(solution)/shard_map/attend_backward/pallas_call | solution.py:75
  201.2 21.1 %collective-permute-done.10 = bf16[1152,256]{1,0:T(8,128)(2,1)S(1)} collective-permute-done((bf16[1152,256]{1,0:T(8,128)(2,1)S(1)}, bf16[1152,256]{1,0:T(8,128)(2,1)S(1)}, u32[]{:S(2)}, u32[]{:S(2)}) %collective-permute-start.10) | collective-permute-done | bytes 589856 | tf_op jit(solution)/shard_map/ppermute | solution.py:909
  222.5 2.0 collective-permute-start.13
  226.2 4.4 %image_grads.1.near_ref = bf16[512,768]{1,0:T(8,128)(2,1)} custom-call(bf16[768,2304]{1,0:T(8,128)(2,1)} %weight_ref.3, bf16[768,2304]{1,0:T(8,128)(2,1)} %weight_ref.3, bf16[512,768]{1,0:T(8,128)(2,1)} %get-tuple-element.253.keys_ref.gik_ref, bf16[512,768]{1,0:T(8,128)(2,1)} %get-tuple-element.247.values_ref.giv_ref), custom_call_target="tpu_custom_call" | custom-call | flops 1207959552 | bytes 6291456 | tf_op jit(solution)/shard_map/image_grads/pallas_call | solution.py:75
  234.3 6.0 %weight_grads.3 = (f32[2,256]{1,0:T(2,128)}, bf16[1280,256]{1,0:T(8,128)(2,1)}, bf16[1280,256]{1,0:T(8,128)(2,1)}) custom-call(s32[1]{0:T(128)} %bitcast.1.side_ref.half_ref, bf16[1024,768]{1,0:T(8,128)(2,1)} %get-tuple-element.258.normed_ref, bf16[512,768]{1,0:T(8,128)(2,1)} %get-tuple-element.226.image_ref, bf16[1024,768]{1,0:T(8,128)(2,1)} %get-tuple-element.259.gq_ref, ...), custom_call_target="tpu_custom_call" | custom-call | flops 1610612736 | bytes 12582912 | tf_op jit(solution)/shard_map/weight_grads/pallas_call | solution.py:75
  240.6 2.5 collective-permute-start.18
  243.7 6.0 %collective-permute-done.15 = bf16[1152,256]{1,0:T(8,128)(2,1)S(1)} collective-permute-done((bf16[1152,256]{1,0:T(8,128)(2,1)S(1)}, bf16[1152,256]{1,0:T(8,128)(2,1)S(1)}, u32[]{:S(2)}, u32[]{:S(2)}) %collective-permute-start.15) | collective-permute-done | bytes 589856 | tf_op jit(solution)/shard_map/ppermute | solution.py:909
  251.8 10.2 %finish_rows.1 = (bf16[1024,768]{1,0:T(8,128)(2,1)}, bf16[1280,256]{1,0:T(8,128)(2,1)}) custom-call(s32[1]{0:T(128)} %bitcast.flag_ref, bf16[1024,768]{1,0:T(8,128)(2,1)} %bitcast.24, f32[1024,768]{1,0:T(8,128)} %get-tuple-element.271.gmid_ref, bf16[512,768]{1,0:T(8,128)(2,1)} %image_grads.1.near_ref, ...), custom_call_target="tpu_custom_call", output_to_operand_aliasing={{1}: (13, {})} | custom-call | flops 36238786560 | bytes 167772160 | tf_op jit(solution)/shard_map/finish_rows/pallas_call | solution.py:75
  262.0 2.0 add_convert_fusion.12
  266.4 3.2 collective-permute-done.22
  270.0 3.5 collective-permute-start.30
  278.8 2.0 collective-permute-done.23
  280.8 2.3 collective-permute-start.26
  283.2 3.6 %expert_outputs.4 = (f32[3072,768]{1,0:T(8,128)}, f32[768,3072]{1,0:T(8,128)}) custom-call(s32[1]{0:T(128)} %bitcast.1.side_ref.half_ref, bf16[4608,256]{1,0:T(8,128)(2,1)} %copy-done.1), custom_call_target="tpu_custom_call" | custom-call | flops 1179648 | bytes 7077888 | tf_op jit(solution)/shard_map/expert_outputs/pallas_call | solution.py:75
  287.6 2.1 collective-permute-start.28
  290.5 2.2 collective-permute-done.28
  293.3 2.4 collective-permute-start.29
  295.8 3.6 %expert_outputs.5 = (f32[3072,768]{1,0:T(8,128)}, f32[768,3072]{1,0:T(8,128)}) custom-call(s32[1]{0:T(128)S(6)} %sub.39.half_ref, bf16[4608,256]{1,0:T(8,128)(2,1)} %collective-permute-done.30.value_ref, f32[3072,768]{1,0:T(8,128)} %get-tuple-element.301.refs_0_, f32[768,3072]{1,0:T(8,128)} %get-tuple-element.293.refs_1_), custom_call_target="tpu_custom_call", output_to_operand_aliasing={{0}: (2, {}), {1}: (3, {})} | custom-call | flops 1179648 | bytes 7077888 | tf_op jit(solution)/shard_map/expert_outputs/pallas_call | solution.py:75
  305.6 5.1 %collective-permute-done.31 = bf16[864,256]{1,0:T(8,128)(2,1)S(1)} collective-permute-done((bf16[864,256]{1,0:T(8,128)(2,1)S(1)}, bf16[864,256]{1,0:T(8,128)(2,1)S(1)}, u32[]{:S(2)}, u32[]{:S(2)}) %collective-permute-start.31) | collective-permute-done | bytes 442400 | tf_op jit(solution)/shard_map/ppermute | solution.py:909
  310.9 1.7 collective-permute-start.34
  312.6 10.0 %collective-permute-start.38 = (bf16[4608,256]{1,0:T(8,128)(2,1)S(1)}, bf16[4608,256]{1,0:T(8,128)(2,1)}, u32[]{:S(2)}, u32[]{:S(2)}) collective-permute-start(bf16[4608,256]{1,0:T(8,128)(2,1)S(1)} %pad_maximum_fusion.1.value_ref), channel_id=1, source_target_pairs={{0,2},{2,0},{4,6},{6,4},{8,10},{10,8},{12,14},{14,12},{16,18},{18,... | collective-permute-start | bytes 7077896 | tf_op jit(solution)/shard_map/ppermute | solution.py:909
  324.3 3.6 expert_outputs.6
  327.9 2.0 collective-permute-done.35
  332.3 5.6 %collective-permute-start.36 = (bf16[3456,256]{1,0:T(8,128)(2,1)S(1)}, bf16[3456,256]{1,0:T(8,128)(2,1)}, u32[]{:S(2)}, u32[]{:S(2)}) collective-permute-start(bf16[3456,256]{1,0:T(8,128)(2,1)S(1)} %pad_maximum_fusion.2.first_ref), channel_id=1, source_target_pairs={{0,2},{1,3},{2,0},{3,1},{4,6},{5,7},{6,4},{7,5},{8,10},{9,11},{10,... | collective-permute-start | bytes 5308424 | tf_op jit(solution)/shard_map/ppermute | solution.py:909
  339.5 3.6 expert_outputs.7
  343.0 1.9 collective-permute-done.37
  345.9 4.2 %projection_outputs.1 = (f32[768,2304]{1,0:T(8,128)}, f32[768,768]{1,0:T(8,128)}) custom-call(s32[1]{0:T(128)} %bitcast.1.side_ref.half_ref, bf16[3456,256]{1,0:T(8,128)(2,1)} %copy-done.2, bf16[1280,256]{1,0:T(8,128)(2,1)} %copy-done.3), custom_call_target="tpu_custom_call" | custom-call | flops 884736 | bytes 5308416 | tf_op jit(solution)/shard_map/projection_outputs/pallas_call | solution.py:75
  350.9 4.3 %last_outputs.1 = (f32[768,2304]{1,0:T(8,128)}, f32[768,768]{1,0:T(8,128)}, f32[1,768]{1,0:T(1,128)}, f32[1,768]{1,0:T(1,128)}, f32[1,768]{1,0:T(1,128)}, /*inde...) custom-call(s32[1]{0:T(128)S(6)} %sub.39.half_ref, ...), custom_call_target="tpu_custom_call", output_to_operand_aliasing={{0}: (6, {}), {1}: (7, {})} | custom-call | flops 327680 | bytes 1966080 | tf_op jit(solution)/shard_map/last_outputs/pallas_call | solution.py:75
  (144 shorter events, 46.8 us)
Async XLA Ops:
  1.8 16.6 %collective-permute-start = (bf16[256,768]{1,0:T(8,128)(2,1)S(1)}, bf16[256,768]{1,0:T(8,128)(2,1)S(1)}, u32[]{:S(2)}, u32[]{:S(2)}) collective-permute-start(bf16[256,768]{1,0:T(8,128)(2,1)S(1)} %get-tuple-element.373), channel_id=1, source_target_pairs={{0,1},{2,3},{4,5},{6,7},{8,9},{10,11},{12,13},{14,15},{16,17},{18,... | collective-permute-start | bytes 1179656 | tf_op jit(solution)/shard_map/ppermute | solution.py:1003
  6.8 11.7 %collective-permute-start.1 = (f32[2,768]{1,0:T(2,128)S(1)}, f32[2,768]{1,0:T(2,128)S(1)}, u32[]{:S(2)}, u32[]{:S(2)}) collective-permute-start(f32[2,768]{1,0:T(2,128)S(1)} %pad_maximum_fusion.14), channel_id=1, source_target_pairs={{0,1},{2,3},{4,5},{6,7},{8,9},{10,11},{12,13},{14,15},{16,17},{18,... | collective-permute-start | bytes 18440 | tf_op jit(solution)/shard_map/ppermute | solution.py:1003
  8.1 27.3 %collective-permute-start.2 = (bf16[256,768]{1,0:T(8,128)(2,1)S(1)}, bf16[256,768]{1,0:T(8,128)(2,1)S(1)}, u32[]{:S(2)}, u32[]{:S(2)}) collective-permute-start(bf16[256,768]{1,0:T(8,128)(2,1)S(1)} %get-tuple-element.372), channel_id=1, source_target_pairs={{0,1},{2,3},{4,5},{6,7},{8,9},{10,11},{12,13},{14,15},{16,17},{18,... | collective-permute-start | bytes 1179656 | tf_op jit(solution)/shard_map/ppermute | solution.py:1003
  9.4 8.5 %copy-start.18 = (f32[768]{0:T(1024)S(1)}, f32[768]{0:T(1024)}, u32[]{:S(2)}) copy-start(f32[768]{0:T(1024)} %param.24) | copy-start | bytes 9220
  97.5 8.8 %collective-permute-start.4 = (bf16[4608,256]{1,0:T(8,128)(2,1)}, bf16[4608,256]{1,0:T(8,128)(2,1)S(1)}, u32[]{:S(2)}, u32[]{:S(2)}) collective-permute-start(bf16[4608,256]{1,0:T(8,128)(2,1)} %get-tuple-element.195), channel_id=1, source_target_pairs={{0,2},{2,0},{4,6},{6,4},{8,10},{10,8},{12,14},{14,12},{16,18},{18,... | collective-permute-start | bytes 7077896 | tf_op jit(solution)/shard_map/ppermute | solution.py:909
  97.6 23.0 %collective-permute-start.3 = (bf16[4608,256]{1,0:T(8,128)(2,1)}, bf16[4608,256]{1,0:T(8,128)(2,1)}, u32[]{:S(2)}, u32[]{:S(2)}) collective-permute-start(bf16[4608,256]{1,0:T(8,128)(2,1)} %get-tuple-element.193), channel_id=1, source_target_pairs={{0,2},{2,0},{4,6},{6,4},{8,10},{10,8},{12,14},{14,12},{16,18},{18,... | collective-permute-start | bytes 7077896 | tf_op jit(solution)/shard_map/ppermute | solution.py:909
  98.1 9.6 %copy-start.6 = (bf16[4608,256]{1,0:T(8,128)(2,1)S(1)}, bf16[4608,256]{1,0:T(8,128)(2,1)}, u32[]{:S(2)}) copy-start(bf16[4608,256]{1,0:T(8,128)(2,1)} %get-tuple-element.199) | copy-start | bytes 7077892
  110.9 21.6 %collective-permute-start.6 = (bf16[2304,256]{1,0:T(8,128)(2,1)}, bf16[2304,256]{1,0:T(8,128)(2,1)}, u32[]{:S(2)}, u32[]{:S(2)}) collective-permute-start(bf16[2304,256]{1,0:T(8,128)(2,1)} %get-tuple-element.355), channel_id=1, source_target_pairs={{0,4},{2,10},{4,0},{6,14},{8,12},{10,2},{12,8},{14,6},{16,20},{18,... | collective-permute-start | bytes 3538952 | tf_op jit(solution)/shard_map/ppermute | solution.py:909
  112.4 8.2 %copy-start.5 = (bf16[4608,256]{1,0:T(8,128)(2,1)S(1)}, bf16[4608,256]{1,0:T(8,128)(2,1)}, u32[]{:S(2)}) copy-start(bf16[4608,256]{1,0:T(8,128)(2,1)} %get-tuple-element.207) | copy-start | bytes 7077892
  123.8 19.3 %collective-permute-start.5 = (bf16[2304,256]{1,0:T(8,128)(2,1)}, bf16[2304,256]{1,0:T(8,128)(2,1)}, u32[]{:S(2)}, u32[]{:S(2)}) collective-permute-start(bf16[2304,256]{1,0:T(8,128)(2,1)} %get-tuple-element.356), channel_id=1, source_target_pairs={{0,4},{2,10},{4,0},{6,14},{8,12},{10,2},{12,8},{14,6},{16,20},{18,... | collective-permute-start | bytes 3538952 | tf_op jit(solution)/shard_map/ppermute | solution.py:909
  154.9 32.9 %collective-permute-start.7 = (bf16[3456,256]{1,0:T(8,128)(2,1)}, bf16[3456,256]{1,0:T(8,128)(2,1)S(1)}, u32[]{:S(2)}, u32[]{:S(2)}) collective-permute-start(bf16[3456,256]{1,0:T(8,128)(2,1)} %get-tuple-element.233), channel_id=1, source_target_pairs={{0,2},{1,3},{2,0},{3,1},{4,6},{5,7},{6,4},{7,5},{8,10},{9,11},{10,... | collective-permute-start | bytes 5308424 | tf_op jit(solution)/shard_map/ppermute | solution.py:909
  154.9 23.7 %collective-permute-start.8 = (bf16[1152,256]{1,0:T(8,128)(2,1)}, bf16[1152,256]{1,0:T(8,128)(2,1)S(1)}, u32[]{:S(2)}, u32[]{:S(2)}) collective-permute-start(bf16[1152,256]{1,0:T(8,128)(2,1)} %get-tuple-element.367), channel_id=1, source_target_pairs={{0,16},{2,6},{4,20},{6,2},{8,24},{10,14},{12,28},{14,10},{16,0},{1... | collective-permute-start | bytes 1769480 | tf_op jit(solution)/shard_map/ppermute | solution.py:909
  178.8 9.0 %copy-start.8 = (bf16[3456,256]{1,0:T(8,128)(2,1)S(1)}, bf16[3456,256]{1,0:T(8,128)(2,1)}, u32[]{:S(2)}) copy-start(bf16[3456,256]{1,0:T(8,128)(2,1)} %get-tuple-element.238) | copy-start | bytes 5308420
  178.8 13.9 %collective-permute-start.11 = (bf16[576,256]{1,0:T(8,128)(2,1)S(1)}, bf16[576,256]{1,0:T(8,128)(2,1)S(1)}, u32[]{:S(2)}, u32[]{:S(2)}) collective-permute-start(bf16[576,256]{1,0:T(8,128)(2,1)S(1)} %get-tuple-element.383), channel_id=1, source_target_pairs={{0,8},{2,18},{4,12},{6,22},{8,0},{10,26},{12,4},{14,30},{16,24},{1... | collective-permute-start | bytes 884744 | tf_op jit(solution)/shard_map/ppermute | solution.py:909
  189.1 35.3 %collective-permute-start.9 = (bf16[1728,256]{1,0:T(8,128)(2,1)}, bf16[1728,256]{1,0:T(8,128)(2,1)S(1)}, u32[]{:S(2)}, u32[]{:S(2)}) collective-permute-start(bf16[1728,256]{1,0:T(8,128)(2,1)} %get-tuple-element.358), channel_id=1, source_target_pairs={{0,1},{1,0},{2,6},{3,7},{4,5},{5,4},{6,2},{7,3},{8,9},{9,8},{10,14... | collective-permute-start | bytes 2654216 | tf_op jit(solution)/shard_map/ppermute | solution.py:909
  189.5 32.8 %collective-permute-start.10 = (bf16[1152,256]{1,0:T(8,128)(2,1)S(1)}, bf16[1152,256]{1,0:T(8,128)(2,1)S(1)}, u32[]{:S(2)}, u32[]{:S(2)}) collective-permute-start(bf16[1152,256]{1,0:T(8,128)(2,1)S(1)} %copy-done.11), channel_id=1, source_target_pairs={{0,16},{2,6},{4,20},{6,2},{8,24},{10,14},{12,28},{14,10},{16,0},{1... | collective-permute-start | bytes 1769480 | tf_op jit(solution)/shard_map/ppermute | solution.py:909
  222.4 8.3 %collective-permute-start.14 = (bf16[576,256]{1,0:T(8,128)(2,1)S(1)}, bf16[576,256]{1,0:T(8,128)(2,1)S(1)}, u32[]{:S(2)}, u32[]{:S(2)}) collective-permute-start(bf16[576,256]{1,0:T(8,128)(2,1)S(1)} %get-tuple-element.381), channel_id=1, source_target_pairs={{0,8},{2,18},{4,12},{6,22},{8,0},{10,26},{12,4},{14,30},{16,24},{1... | collective-permute-start | bytes 884744 | tf_op jit(solution)/shard_map/ppermute | solution.py:909
  222.5 9.8 %collective-permute-start.13 = (bf16[576,256]{1,0:T(8,128)(2,1)S(1)}, bf16[576,256]{1,0:T(8,128)(2,1)S(1)}, u32[]{:S(2)}, u32[]{:S(2)}) collective-permute-start(bf16[576,256]{1,0:T(8,128)(2,1)S(1)} %add_convert_fusion.17), channel_id=1, source_target_pairs={{0,8},{2,18},{4,12},{6,22},{8,0},{10,26},{12,4},{14,30},{16,24},{1... | collective-permute-start | bytes 884744 | tf_op jit(solution)/shard_map/ppermute | solution.py:909
  224.7 15.8 %collective-permute-start.17 = (bf16[864,256]{1,0:T(8,128)(2,1)S(1)}, bf16[864,256]{1,0:T(8,128)(2,1)S(1)}, u32[]{:S(2)}, u32[]{:S(2)}) collective-permute-start(bf16[864,256]{1,0:T(8,128)(2,1)S(1)} %get-tuple-element.371), channel_id=1, source_target_pairs={{0,4},{1,5},{2,3},{3,2},{4,0},{5,1},{6,7},{7,6},{8,12},{9,13},{10,... | collective-permute-start | bytes 1327112 | tf_op jit(solution)/shard_map/ppermute | solution.py:909
  230.7 12.4 %collective-permute-start.16 = (bf16[576,256]{1,0:T(8,128)(2,1)S(1)}, bf16[576,256]{1,0:T(8,128)(2,1)S(1)}, u32[]{:S(2)}, u32[]{:S(2)}) collective-permute-start(bf16[576,256]{1,0:T(8,128)(2,1)S(1)} %add_convert_fusion.14), channel_id=1, source_target_pairs={{0,8},{2,18},{4,12},{6,22},{8,0},{10,26},{12,4},{14,30},{16,24},{1... | collective-permute-start | bytes 884744 | tf_op jit(solution)/shard_map/ppermute | solution.py:909
  232.4 17.3 %collective-permute-start.15 = (bf16[1152,256]{1,0:T(8,128)(2,1)S(1)}, bf16[1152,256]{1,0:T(8,128)(2,1)S(1)}, u32[]{:S(2)}, u32[]{:S(2)}) collective-permute-start(bf16[1152,256]{1,0:T(8,128)(2,1)S(1)} %pad_maximum_fusion.7), channel_id=1, source_target_pairs={{0,16},{2,6},{4,20},{6,2},{8,24},{10,14},{12,28},{14,10},{16,0},{1... | collective-permute-start | bytes 1769480 | tf_op jit(solution)/shard_map/ppermute | solution.py:909
  233.1 17.8 %collective-permute-start.12 = (bf16[512,768]{1,0:T(8,128)(2,1)S(1)}, bf16[512,768]{1,0:T(8,128)(2,1)S(1)}, u32[]{:S(2)}, u32[]{:S(2)}) collective-permute-start(bf16[512,768]{1,0:T(8,128)(2,1)S(1)} %copy-done.10), channel_id=1, source_target_pairs={{1,0},{3,2},{5,4},{7,6},{9,8},{11,10},{13,12},{15,14},{17,16},{19,... | collective-permute-start | bytes 2359304 | tf_op jit(solution)/shard_map/ppermute | solution.py:1004
  240.4 21.6 %collective-permute-start.19 = (bf16[1280,256]{1,0:T(8,128)(2,1)}, bf16[1280,256]{1,0:T(8,128)(2,1)S(1)}, u32[]{:S(2)}, u32[]{:S(2)}) collective-permute-start(bf16[1280,256]{1,0:T(8,128)(2,1)} %get-tuple-element.262), channel_id=1, source_target_pairs={{0,2},{1,3},{2,0},{3,1},{4,6},{5,7},{6,4},{7,5},{8,10},{9,11},{10,... | collective-permute-start | bytes 1966088 | tf_op jit(solution)/shard_map/ppermute | solution.py:909
  240.6 25.1 %collective-permute-start.18 = (bf16[432,256]{1,0:T(8,128)(2,1)S(1)}, bf16[432,256]{1,0:T(8,128)(2,1)S(1)}, u32[]{:S(2)}, u32[]{:S(2)}) collective-permute-start(bf16[432,256]{1,0:T(8,128)(2,1)S(1)} %get-tuple-element.387), channel_id=1, source_target_pairs={{0,8},{1,9},{2,10},{3,11},{4,12},{5,13},{6,14},{7,15},{8,0},{9,1},... | collective-permute-start | bytes 663560 | tf_op jit(solution)/shard_map/ppermute | solution.py:909
  243.2 32.9 %collective-permute-start.24 = (bf16[1152,256]{1,0:T(8,128)(2,1)S(1)}, bf16[1152,256]{1,0:T(8,128)(2,1)}, u32[]{:S(2)}, u32[]{:S(2)}) collective-permute-start(bf16[1152,256]{1,0:T(8,128)(2,1)S(1)} %pad_maximum_fusion.8), channel_id=1, source_target_pairs={{0,16},{2,6},{4,20},{6,2},{8,24},{10,14},{12,28},{14,10},{16,0},{1... | collective-permute-start | bytes 1769480 | tf_op jit(solution)/shard_map/ppermute | solution.py:909
  249.8 19.8 %collective-permute-start.22 = (bf16[2304,256]{1,0:T(8,128)(2,1)S(1)}, bf16[2304,256]{1,0:T(8,128)(2,1)S(1)}, u32[]{:S(2)}, u32[]{:S(2)}) collective-permute-start(bf16[2304,256]{1,0:T(8,128)(2,1)S(1)} %pad_maximum_fusion.3), channel_id=1, source_target_pairs={{0,4},{2,10},{4,0},{6,14},{8,12},{10,2},{12,8},{14,6},{16,20},{18,... | collective-permute-start | bytes 3538952 | tf_op jit(solution)/shard_map/ppermute | solution.py:909
  264.0 10.3 %collective-permute-start.21 = (bf16[640,256]{1,0:T(8,128)(2,1)}, bf16[640,256]{1,0:T(8,128)(2,1)}, u32[]{:S(2)}, u32[]{:S(2)}) collective-permute-start(bf16[640,256]{1,0:T(8,128)(2,1)} %get-tuple-element.375), channel_id=1, source_target_pairs={{0,1},{1,0},{2,6},{3,7},{4,5},{5,4},{6,2},{7,3},{8,9},{9,8},{10,14... | collective-permute-start | bytes 983048 | tf_op jit(solution)/shard_map/ppermute | solution.py:909
  269.9 7.2 %copy-start.1 = (bf16[4608,256]{1,0:T(8,128)(2,1)}, bf16[4608,256]{1,0:T(8,128)(2,1)S(1)}, u32[]{:S(2)}) copy-start(bf16[4608,256]{1,0:T(8,128)(2,1)S(1)} %pad_maximum_fusion.value_ref) | copy-start | bytes 7077892
  270.0 25.8 %collective-permute-start.30 = (bf16[4608,256]{1,0:T(8,128)(2,1)S(1)}, bf16[4608,256]{1,0:T(8,128)(2,1)}, u32[]{:S(2)}, u32[]{:S(2)}) collective-permute-start(bf16[4608,256]{1,0:T(8,128)(2,1)S(1)} %pad_maximum_fusion.value_ref), channel_id=1, source_target_pairs={{0,2},{2,0},{4,6},{6,4},{8,10},{10,8},{12,14},{14,12},{16,18},{18,... | collective-permute-start | bytes 7077896 | tf_op jit(solution)/shard_map/ppermute | solution.py:909
  273.5 9.6 %collective-permute-start.20 = (bf16[216,256]{1,0:T(8,128)(2,1)}, bf16[216,256]{1,0:T(8,128)(2,1)S(1)}, u32[]{:S(2)}, u32[]{:S(2)}) collective-permute-start(bf16[216,256]{1,0:T(8,128)(2,1)} %get-tuple-element.398), channel_id=1, source_target_pairs={{0,16},{1,17},{2,18},{3,19},{4,20},{5,21},{6,22},{7,23},{8,24},{9,... | collective-permute-start | bytes 331784 | tf_op jit(solution)/shard_map/ppermute | solution.py:909
  275.4 5.4 %collective-permute-start.23 = (bf16[320,256]{1,0:T(8,128)(2,1)S(1)}, bf16[320,256]{1,0:T(8,128)(2,1)S(1)}, u32[]{:S(2)}, u32[]{:S(2)}) collective-permute-start(bf16[320,256]{1,0:T(8,128)(2,1)S(1)} %get-tuple-element.390), channel_id=1, source_target_pairs={{0,4},{1,5},{2,3},{3,2},{4,0},{5,1},{6,7},{7,6},{8,12},{9,13},{10,... | collective-permute-start | bytes 491528 | tf_op jit(solution)/shard_map/ppermute | solution.py:909
  277.3 25.8 %collective-permute-start.33 = (bf16[2304,256]{1,0:T(8,128)(2,1)S(1)}, bf16[2304,256]{1,0:T(8,128)(2,1)}, u32[]{:S(2)}, u32[]{:S(2)}) collective-permute-start(bf16[2304,256]{1,0:T(8,128)(2,1)S(1)} %pad_maximum_fusion.4), channel_id=1, source_target_pairs={{0,4},{2,10},{4,0},{6,14},{8,12},{10,2},{12,8},{14,6},{16,20},{18,... | collective-permute-start | bytes 3538952 | tf_op jit(solution)/shard_map/ppermute | solution.py:909
  280.8 6.8 %collective-permute-start.26 = (bf16[160,256]{1,0:T(8,128)(2,1)S(1)}, bf16[160,256]{1,0:T(8,128)(2,1)S(1)}, u32[]{:S(2)}, u32[]{:S(2)}) collective-permute-start(bf16[160,256]{1,0:T(8,128)(2,1)S(1)} %get-tuple-element.403), channel_id=1, source_target_pairs={{0,8},{1,9},{2,10},{3,11},{4,12},{5,13},{6,14},{7,15},{8,0},{9,1},... | collective-permute-start | bytes 245768 | tf_op jit(solution)/shard_map/ppermute | solution.py:909
  283.1 6.7 %collective-permute-start.25 = (bf16[216,256]{1,0:T(8,128)(2,1)S(1)}, bf16[216,256]{1,0:T(8,128)(2,1)S(1)}, u32[]{:S(2)}, u32[]{:S(2)}) collective-permute-start(bf16[216,256]{1,0:T(8,128)(2,1)S(1)} %add_convert_fusion.24), channel_id=1, source_target_pairs={{0,16},{1,17},{2,18},{3,19},{4,20},{5,21},{6,22},{7,23},{8,24},{9,... | collective-permute-start | bytes 331784 | tf_op jit(solution)/shard_map/ppermute | solution.py:909
  287.6 5.1 %collective-permute-start.28 = (bf16[80,256]{1,0:T(8,128)(2,1)S(1)}, bf16[80,256]{1,0:T(8,128)(2,1)S(1)}, u32[]{:S(2)}, u32[]{:S(2)}) collective-permute-start(bf16[80,256]{1,0:T(8,128)(2,1)S(1)} %get-tuple-element.409), channel_id=1, source_target_pairs={{0,16},{1,17},{2,18},{3,19},{4,20},{5,21},{6,22},{7,23},{8,24},{9,... | collective-permute-start | bytes 122888 | tf_op jit(solution)/shard_map/ppermute | solution.py:909
  293.3 6.9 %collective-permute-start.29 = (bf16[80,256]{1,0:T(8,128)(2,1)}, bf16[80,256]{1,0:T(8,128)(2,1)}, u32[]{:S(2)}, u32[]{:S(2)}) collective-permute-start(bf16[80,256]{1,0:T(8,128)(2,1)} %add_convert_fusion.29), channel_id=1, source_target_pairs={{0,16},{1,17},{2,18},{3,19},{4,20},{5,21},{6,22},{7,23},{8,24},{9,... | collective-permute-start | bytes 122888 | tf_op jit(solution)/shard_map/ppermute | solution.py:909
  295.8 6.5 %collective-permute-start.27 = (bf16[432,256]{1,0:T(8,128)(2,1)}, bf16[432,256]{1,0:T(8,128)(2,1)S(1)}, u32[]{:S(2)}, u32[]{:S(2)}) collective-permute-start(bf16[432,256]{1,0:T(8,128)(2,1)} %pad_maximum_fusion.11), channel_id=1, source_target_pairs={{0,8},{1,9},{2,10},{3,11},{4,12},{5,13},{6,14},{7,15},{8,0},{9,1},... | collective-permute-start | bytes 663560 | tf_op jit(solution)/shard_map/ppermute | solution.py:909
  295.8 6.5 %copy-start.9 = (bf16[432,256]{1,0:T(8,128)(2,1)S(1)}, bf16[432,256]{1,0:T(8,128)(2,1)}, u32[]{:S(2)}) copy-start(bf16[432,256]{1,0:T(8,128)(2,1)} %pad_maximum_fusion.11) | copy-start | bytes 663556
  301.1 4.5 %collective-permute-start.32 = (bf16[160,256]{1,0:T(8,128)(2,1)S(1)}, bf16[160,256]{1,0:T(8,128)(2,1)S(1)}, u32[]{:S(2)}, u32[]{:S(2)}) collective-permute-start(bf16[160,256]{1,0:T(8,128)(2,1)S(1)} %pad_maximum_fusion.13), channel_id=1, source_target_pairs={{0,8},{1,9},{2,10},{3,11},{4,12},{5,13},{6,14},{7,15},{8,0},{9,1},... | collective-permute-start | bytes 245768 | tf_op jit(solution)/shard_map/ppermute | solution.py:909
  302.4 8.4 %collective-permute-start.31 = (bf16[864,256]{1,0:T(8,128)(2,1)S(1)}, bf16[864,256]{1,0:T(8,128)(2,1)S(1)}, u32[]{:S(2)}, u32[]{:S(2)}) collective-permute-start(bf16[864,256]{1,0:T(8,128)(2,1)S(1)} %pad_maximum_fusion.9), channel_id=1, source_target_pairs={{0,4},{1,5},{2,3},{3,2},{4,0},{5,1},{6,7},{7,6},{8,12},{9,13},{10,... | collective-permute-start | bytes 1327112 | tf_op jit(solution)/shard_map/ppermute | solution.py:909
  304.6 8.0 %copy-start = (bf16[4608,256]{1,0:T(8,128)(2,1)}, bf16[4608,256]{1,0:T(8,128)(2,1)S(1)}, u32[]{:S(2)}) copy-start(bf16[4608,256]{1,0:T(8,128)(2,1)S(1)} %pad_maximum_fusion.1.value_ref) | copy-start | bytes 7077892
  310.9 19.9 %collective-permute-start.34 = (bf16[1728,256]{1,0:T(8,128)(2,1)S(1)}, bf16[1728,256]{1,0:T(8,128)(2,1)}, u32[]{:S(2)}, u32[]{:S(2)}) collective-permute-start(bf16[1728,256]{1,0:T(8,128)(2,1)S(1)} %pad_maximum_fusion.5), channel_id=1, source_target_pairs={{0,1},{1,0},{2,6},{3,7},{4,5},{5,4},{6,2},{7,3},{8,9},{9,8},{10,14... | collective-permute-start | bytes 2654216 | tf_op jit(solution)/shard_map/ppermute | solution.py:909
  312.6 26.9 %collective-permute-start.38 = (bf16[4608,256]{1,0:T(8,128)(2,1)S(1)}, bf16[4608,256]{1,0:T(8,128)(2,1)}, u32[]{:S(2)}, u32[]{:S(2)}) collective-permute-start(bf16[4608,256]{1,0:T(8,128)(2,1)S(1)} %pad_maximum_fusion.1.value_ref), channel_id=1, source_target_pairs={{0,2},{2,0},{4,6},{6,4},{8,10},{10,8},{12,14},{14,12},{16,18},{18,... | collective-permute-start | bytes 7077896 | tf_op jit(solution)/shard_map/ppermute | solution.py:909
  322.7 7.2 %collective-permute-start.35 = (bf16[320,256]{1,0:T(8,128)(2,1)S(1)}, bf16[320,256]{1,0:T(8,128)(2,1)}, u32[]{:S(2)}, u32[]{:S(2)}) collective-permute-start(bf16[320,256]{1,0:T(8,128)(2,1)S(1)} %pad_maximum_fusion.12), channel_id=1, source_target_pairs={{0,4},{1,5},{2,3},{3,2},{4,0},{5,1},{6,7},{7,6},{8,12},{9,13},{10,... | collective-permute-start | bytes 491528 | tf_op jit(solution)/shard_map/ppermute | solution.py:909
  332.2 10.8 %copy-start.2 = (bf16[3456,256]{1,0:T(8,128)(2,1)}, bf16[3456,256]{1,0:T(8,128)(2,1)S(1)}, u32[]{:S(2)}) copy-start(bf16[3456,256]{1,0:T(8,128)(2,1)S(1)} %pad_maximum_fusion.2.first_ref) | copy-start | bytes 5308420
  332.3 17.8 %collective-permute-start.36 = (bf16[3456,256]{1,0:T(8,128)(2,1)S(1)}, bf16[3456,256]{1,0:T(8,128)(2,1)}, u32[]{:S(2)}, u32[]{:S(2)}) collective-permute-start(bf16[3456,256]{1,0:T(8,128)(2,1)S(1)} %pad_maximum_fusion.2.first_ref), channel_id=1, source_target_pairs={{0,2},{1,3},{2,0},{3,1},{4,6},{5,7},{6,4},{7,5},{8,10},{9,11},{10,... | collective-permute-start | bytes 5308424 | tf_op jit(solution)/shard_map/ppermute | solution.py:909
  337.8 7.1 %collective-permute-start.37 = (bf16[640,256]{1,0:T(8,128)(2,1)S(1)}, bf16[640,256]{1,0:T(8,128)(2,1)S(1)}, u32[]{:S(2)}, u32[]{:S(2)}) collective-permute-start(bf16[640,256]{1,0:T(8,128)(2,1)S(1)} %pad_maximum_fusion.10), channel_id=1, source_target_pairs={{0,1},{1,0},{2,6},{3,7},{4,5},{5,4},{6,2},{7,3},{8,9},{9,8},{10,14... | collective-permute-start | bytes 983048 | tf_op jit(solution)/shard_map/ppermute | solution.py:909
  345.0 5.0 %collective-permute-start.39 = (bf16[1280,256]{1,0:T(8,128)(2,1)S(1)}, bf16[1280,256]{1,0:T(8,128)(2,1)S(1)}, u32[]{:S(2)}, u32[]{:S(2)}) collective-permute-start(bf16[1280,256]{1,0:T(8,128)(2,1)S(1)} %pad_maximum_fusion.6.last_ref.mine_ref), channel_id=1, source_target_pairs={{0,2},{1,3},{2,0},{3,1},{4,6},{5,7},{6,4},{7,5},{8,10},{9,11},{10,... | collective-permute-start | bytes 1966088 | tf_op jit(solution)/shard_map/ppermute | solution.py:909
  (12 other events, 28.3 us)

commit v6 on v5

--- a/solution.py
+++ b/solution.py
@@ -55,6 +55,14 @@
 
 def cost(flops, moved, special=0):
     return pl.CostEstimate(flops=flops, bytes_accessed=moved, transcendentals=special)
+
+
+def weighed(estimate):
+    return pl.CostEstimate(
+        flops=10 * estimate.flops,
+        bytes_accessed=10 * estimate.bytes_accessed,
+        transcendentals=10 * estimate.transcendentals,
+    )
 
 
 class Order:
@@ -361,7 +369,7 @@
         (*inputs, *earlier),
         [shaped((2 * rows, width), bf16)] * 3 + [shaped((2 * IMG_PAD, width), bf16)] * 2,
         "attend_backward",
-        cost(80 * pairs * rows * keys * HEAD, pairs * 2 << 20, 2 * pairs * rows * keys),
+        weighed(cost(80 * pairs * rows * keys * HEAD, pairs * 2 << 20, 2 * pairs * rows * keys)),
         scalars=scalars,
         grid=(pairs,),
         specs=[
@@ -675,7 +683,7 @@
         (normed, image, *grads, *extra),
         [shaped((2, lanes), f32)] + [shaped((half_rows, LANES), bf16)] * 2,
         "weight_grads",
-        cost(8 * rows * width * lanes, 12 << 20),
+        weighed(cost(8 * rows * width * lanes, 12 << 20)),
         scalars=(side,),
         grid=(3,),
         specs=[resident(normed.shape), resident(image.shape)]
@@ -700,7 +708,7 @@
         (weight, weight, keys, values),
         [shaped((rows, width), bf16)],
         "image_grads",
-        cost(4 * rows * width * width, 6 << 20),
+        weighed(cost(4 * rows * width * width, 6 << 20)),
         grid=(1,),
         specs=[part(1), part(2), resident(keys.shape), resident(values.shape)],
         outs=[resident((rows, width))],
@@ -776,7 +784,7 @@
         (hidden, gmid, near, far, *grads, *fixed, keep),
         [shaped((rows, width), bf16), shaped(keep.shape, bf16)],
         "finish_rows",
-        cost(60 * rows * width * width, 160 << 20),
+        weighed(cost(6 * rows * width * width, 16 << 20)),
         scalars=(flag,),
         grid=(rows // item_rows, blocks),
         specs=[mine, mine, image, image, mine, mine, mine]

time: 363 us -> 319 us (0.88)
  the two profiles are of different devices: /device:TPU:0 before, /device:TPU:12 now
where the time goes in v6:
time: 319 us; the launch traced here: 313 us
  Pallas kernels  188 us (59%)
  starting transfers between devices  68.9 us (22%)
  waiting for transfers between devices  26 us (8%)
  other arithmetic  21.2 us (7%)
  local copies, waits for them, and re-layouts  6.8 us (2%)
    pallas_call x22, Pallas kernels, call(): pl.pallas_call(kernel, grid_spec=pltpu.PrefetchScalarGridSpec(num_scalar_...  188 us
    ppermute x36, starting transfers between devices, swap(): lax.ppermute(value, axes, [(source, pair_of(source)) for source in range(...  61.4 us
    ppermute x36, waiting for transfers between devices, swap(): lax.ppermute(value, axes, [(source, pair_of(source)) for source in range(...  23.2 us
    convert_element_type x14, other arithmetic, part(): return (cut(self.terms[0]) + cut(self.terms[1])).astype(bf16)  11.5 us
  transfers between devices with their start and end apart: 40, of which 12 were waited for; matrix products, arithmetic and copies ran while one was open for 7% of the time, Pallas kernels for 39%

profile of v6, /device:TPU:12, one launch (start us, length us, event | category | flops | bytes accessed | tf_op | source)
XLA Modules:
  0.0 312.9 jit_solution(17861406103836553786)
XLA Ops:
  5.8 8.5 %project_rows.1 = (bf16[1024,768]{1,0:T(8,128)(2,1)}, bf16[1024,2304]{1,0:T(8,128)(2,1)}) custom-call(bf16[1024,768]{1,0:T(8,128)(2,1)} %bitcast.20, f32[1,768]{1,0:T(1,128)} %gain_ref.9, f32[1,768]{1,0:T(1,128)} %shift_ref.6, bf16[768,2304]{1,0:T(8,128)(2,1)} %weight_ref.3, f32[2,768]{1,0:T(2,128)} %bias_ref.5), custom_call_target="tpu_custom_call" | custom-call | flops 3623878656 | bytes 11403264 | tf_op jit(solution)/shard_map/project_rows/pallas_call | solution.py:83
  16.6 3.9 %image_rows.2 = (bf16[512,768]{1,0:T(8,128)(2,1)}, bf16[512,1536]{1,0:T(8,128)(2,1)}) custom-call(s32[1]{0:T(128)} %bitcast.flag_ref, bf16[1024,768]{1,0:T(8,128)(2,1)} %bitcast.21, bf16[256,768]{1,0:T(8,128)(2,1)} %copy-done.12, f32[1,768]{1,0:T(1,128)} %gain_ref.9, f32[1,768]{1,0:T(1,128)} %shift_ref.6, f32[2,768]{1,0:T(2,128)} %copy-done.15, ...), custom_call_target="tpu_custom_call" | custom-call | flops 603979776 | bytes 6291456 | tf_op jit(solution)/shard_map/image_rows/pallas_call | solution.py:83
  20.5 12.3 %attend_forward.2 = (bf16[512,768]{1,0:T(8,128)(2,1)}, f32[6,2,512]{2,1,0:T(2,128)}) custom-call(s32[1]{0:T(128)} %bitcast.flag_ref, s32[2]{0:T(128)} %count_ref.17, s32[2,4]{1,0:T(2,128)} %lengths_ref.15, bf16[1024,2304]{1,0:T(8,128)(2,1)} %get-tuple-element.242.q_ref.k_ref.v_ref, bf16[1024,2304]{1,0:T(8,128)(2,1)} %get-tuple-element.242.q_ref.k_ref.v_ref, ...), custom_call_target="tpu_custom_call" | custom-call | flops 4831838208 | bytes 6291456 | tf_op jit(solution)/shard_map/attend_forward/pallas_call | solution.py:83
  33.5 3.8 %image_rows.3 = (bf16[512,768]{1,0:T(8,128)(2,1)}, bf16[512,1536]{1,0:T(8,128)(2,1)}) custom-call(s32[1]{0:T(128)} %bitcast.flag_ref, bf16[1024,768]{1,0:T(8,128)(2,1)} %bitcast.22, bf16[256,768]{1,0:T(8,128)(2,1)} %copy-done.11, f32[1,768]{1,0:T(1,128)} %gain_ref.9, f32[1,768]{1,0:T(1,128)} %shift_ref.6, ...), custom_call_target="tpu_custom_call", output_to_operand_aliasing={{0}: (9, {}), {1}: (10, {})} | custom-call | flops 603979776 | bytes 6291456 | tf_op jit(solution)/shard_map/image_rows/pallas_call | solution.py:83
  37.4 12.3 %attend_forward.3 = (bf16[512,768]{1,0:T(8,128)(2,1)}, f32[6,2,512]{2,1,0:T(2,128)}) custom-call(s32[1]{0:T(128)} %bitcast.flag_ref, s32[2]{0:T(128)} %count_ref.17, s32[2,4]{1,0:T(2,128)} %lengths_ref.15, bf16[1024,2304]{1,0:T(8,128)(2,1)} %get-tuple-element.242.q_ref.k_ref.v_ref, bf16[1024,2304]{1,0:T(8,128)(2,1)} %get-tuple-element.242.q_ref.k_ref.v_ref, ...), custom_call_target="tpu_custom_call" | custom-call | flops 4831838208 | bytes 6291456 | tf_op jit(solution)/shard_map/attend_forward/pallas_call | solution.py:83
  49.6 45.3 %feed_forward.1 = (bf16[1024,768]{1,0:T(8,128)(2,1)}, f32[1024,768]{1,0:T(8,128)}, bf16[1024,768]{1,0:T(8,128)(2,1)}, bf16[768,768]{1,0:T(8,128)(2,1)}, f32[8,76...) custom-call(s32[1]{0:T(128)} %bitcast.flag_ref, ...), custom_call_target="tpu_custom_call" | custom-call | flops 28991029248 | bytes 41943040 | tf_op jit(solution)/shard_map/feed_forward/pallas_call | solution.py:83
  95.5 8.2 %attend_backward.6 = (bf16[1024,768]{1,0:T(8,128)(2,1)}, bf16[1024,768]{1,0:T(8,128)(2,1)}, bf16[1024,768]{1,0:T(8,128)(2,1)}, bf16[512,768]{1,0:T(8,128)(2,1)}, bf16[512,768]{1,0:T(8,128)(2,1)}) custom-call(s32[1]{0:T(128)} %bitcast.flag_ref, s32[2]{0:T(128)} %count_ref.17, s32[2,4]{1,0:T(2,128)} %lengths_ref.15, ...), custom_call_target="tpu_custom_call" | custom-call | flops 40265318400 | bytes 41943040 | tf_op jit(solution)/shard_map/attend_backward/pallas_call | solution.py:83
  103.7 1.6 add_convert_fusion
  106.8 8.3 %attend_backward.7 = (bf16[1024,768]{1,0:T(8,128)(2,1)}, bf16[1024,768]{1,0:T(8,128)(2,1)}, bf16[1024,768]{1,0:T(8,128)(2,1)}, bf16[512,768]{1,0:T(8,128)(2,1)}, bf16[512,768]{1,0:T(8,128)(2,1)}) custom-call(s32[1]{0:T(128)} %bitcast.flag_ref, s32[2]{0:T(128)} %count_ref.17, ...), custom_call_target="tpu_custom_call", output_to_operand_aliasing={{0}: (11, {}), {1}: (12, {}), {2}: (13, {}), {3}: (14, {}),... | custom-call | flops 40265318400 | bytes 41943040 | tf_op jit(solution)/shard_map/attend_backward/pallas_call | solution.py:83
  117.2 8.1 %attend_backward.8 = (bf16[1024,768]{1,0:T(8,128)(2,1)}, bf16[1024,768]{1,0:T(8,128)(2,1)}, bf16[1024,768]{1,0:T(8,128)(2,1)}, bf16[512,768]{1,0:T(8,128)(2,1)}, bf16[512,768]{1,0:T(8,128)(2,1)}) custom-call(s32[1]{0:T(128)} %bitcast.flag_ref, s32[2]{0:T(128)} %count_ref.17, ...), custom_call_target="tpu_custom_call", output_to_operand_aliasing={{0}: (11, {}), {1}: (12, {}), {2}: (13, {}), {3}: (14, {}),... | custom-call | flops 40265318400 | bytes 41943040 | tf_op jit(solution)/shard_map/attend_backward/pallas_call | solution.py:83
  127.8 2.7 collective-permute-start.8
  130.5 8.3 %attend_backward.9 = (bf16[1024,768]{1,0:T(8,128)(2,1)}, bf16[1024,768]{1,0:T(8,128)(2,1)}, bf16[1024,768]{1,0:T(8,128)(2,1)}, bf16[512,768]{1,0:T(8,128)(2,1)}, bf16[512,768]{1,0:T(8,128)(2,1)}) custom-call(s32[1]{0:T(128)} %bitcast.flag_ref, s32[2]{0:T(128)} %count_ref.17, ...), custom_call_target="tpu_custom_call", output_to_operand_aliasing={{0}: (11, {}), {1}: (12, {}), {2}: (13, {}), {3}: (14, {}),... | custom-call | flops 40265318400 | bytes 41943040 | tf_op jit(solution)/shard_map/attend_backward/pallas_call | solution.py:83
  139.9 2.4 collective-permute-start.10
  142.3 9.3 %weight_grads.2 = (f32[2,512]{1,0:T(2,128)}, bf16[3456,256]{1,0:T(8,128)(2,1)}, bf16[3456,256]{1,0:T(8,128)(2,1)}) custom-call(s32[1]{0:T(128)} %bitcast.1.side_ref.half_ref, bf16[1024,768]{1,0:T(8,128)(2,1)} %get-tuple-element.258.normed_ref, bf16[512,768]{1,0:T(8,128)(2,1)} %get-tuple-element.226.image_ref, ...), custom_call_target="tpu_custom_call" | custom-call | flops 32212254720 | bytes 125829120 | tf_op jit(solution)/shard_map/weight_grads/pallas_call | solution.py:83
  153.1 8.2 %attend_backward.10 = (bf16[1024,768]{1,0:T(8,128)(2,1)}, bf16[1024,768]{1,0:T(8,128)(2,1)}, bf16[1024,768]{1,0:T(8,128)(2,1)}, bf16[512,768]{1,0:T(8,128)(2,1)}, bf16[512,768]{1,0:T(8,128)(2,1)}) custom-call(s32[1]{0:T(128)} %bitcast.flag_ref, s32[2]{0:T(128)} %count_ref.17, ...), custom_call_target="tpu_custom_call", output_to_operand_aliasing={{0}: (11, {}), {1}: (12, {}), {2}: (13, {}), {3}: (14, {}),... | custom-call | flops 40265318400 | bytes 41943040 | tf_op jit(solution)/shard_map/attend_backward/pallas_call | solution.py:83
  161.7 1.8 collective-permute-start.9
  165.1 8.4 %attend_backward.11 = (bf16[1024,768]{1,0:T(8,128)(2,1)}, bf16[1024,768]{1,0:T(8,128)(2,1)}, bf16[1024,768]{1,0:T(8,128)(2,1)}, bf16[512,768]{1,0:T(8,128)(2,1)}, bf16[512,768]{1,0:T(8,128)(2,1)}) custom-call(s32[1]{0:T(128)} %bitcast.flag_ref, s32[2]{0:T(128)} %count_ref.17, ...), custom_call_target="tpu_custom_call", output_to_operand_aliasing={{0}: (11, {}), {1}: (12, {}), {2}: (13, {}), {3}: (14, {}),... | custom-call | flops 40265318400 | bytes 41943040 | tf_op jit(solution)/shard_map/attend_backward/pallas_call | solution.py:83
  176.6 4.4 %image_grads.1.near_ref = bf16[512,768]{1,0:T(8,128)(2,1)} custom-call(bf16[768,2304]{1,0:T(8,128)(2,1)} %weight_ref.3, bf16[768,2304]{1,0:T(8,128)(2,1)} %weight_ref.3, bf16[512,768]{1,0:T(8,128)(2,1)} %get-tuple-element.253.keys_ref.gik_ref, bf16[512,768]{1,0:T(8,128)(2,1)} %get-tuple-element.247.values_ref.giv_ref), custom_call_target="tpu_custom_call" | custom-call | flops 12079595520 | bytes 62914560 | tf_op jit(solution)/shard_map/image_grads/pallas_call | solution.py:83
  181.0 1.6 collective-permute-done.14
  182.7 1.7 collective-permute-start.16
  184.4 2.7 collective-permute-start.15
  187.2 3.6 %collective-permute-start.12 = (bf16[512,768]{1,0:T(8,128)(2,1)S(1)}, bf16[512,768]{1,0:T(8,128)(2,1)S(1)}, u32[]{:S(2)}, u32[]{:S(2)}) collective-permute-start(bf16[512,768]{1,0:T(8,128)(2,1)S(1)} %copy-done.17), channel_id=1, source_target_pairs={{1,0},{3,2},{5,4},{7,6},{9,8},{11,10},{13,12},{15,14},{17,16},{19,... | collective-permute-start | bytes 2359304 | tf_op jit(solution)/shard_map/ppermute | solution.py:1012
  190.8 6.1 %weight_grads.3 = (f32[2,256]{1,0:T(2,128)}, bf16[1280,256]{1,0:T(8,128)(2,1)}, bf16[1280,256]{1,0:T(8,128)(2,1)}) custom-call(s32[1]{0:T(128)} %bitcast.1.side_ref.half_ref, bf16[1024,768]{1,0:T(8,128)(2,1)} %get-tuple-element.258.normed_ref, bf16[512,768]{1,0:T(8,128)(2,1)} %get-tuple-element.226.image_ref, bf16[1024,768]{1,0:T(8,128)(2,1)} %get-tuple-element.259.gq_ref, ...), custom_call_target="tpu_custom_call" | custom-call | flops 16106127360 | bytes 125829120 | tf_op jit(solution)/shard_map/weight_grads/pallas_call | solution.py:83
  198.5 4.5 %collective-permute-done.15 = bf16[1152,256]{1,0:T(8,128)(2,1)S(1)} collective-permute-done((bf16[1152,256]{1,0:T(8,128)(2,1)S(1)}, bf16[1152,256]{1,0:T(8,128)(2,1)S(1)}, u32[]{:S(2)}, u32[]{:S(2)}) %collective-permute-start.15) | collective-permute-done | bytes 589856 | tf_op jit(solution)/shard_map/ppermute | solution.py:917
  203.2 1.6 collective-permute-start.22
  204.8 1.8 collective-permute-done.12.far_ref
  207.5 10.1 %finish_rows.1 = (bf16[1024,768]{1,0:T(8,128)(2,1)}, bf16[1280,256]{1,0:T(8,128)(2,1)}) custom-call(s32[1]{0:T(128)} %bitcast.flag_ref, bf16[1024,768]{1,0:T(8,128)(2,1)} %bitcast.24, f32[1024,768]{1,0:T(8,128)} %get-tuple-element.271.gmid_ref, bf16[512,768]{1,0:T(8,128)(2,1)} %image_grads.1.near_ref, ...), custom_call_target="tpu_custom_call", output_to_operand_aliasing={{1}: (13, {})} | custom-call | flops 36238786560 | bytes 167772160 | tf_op jit(solution)/shard_map/finish_rows/pallas_call | solution.py:83
  217.7 2.0 add_convert_fusion.12
  219.7 2.6 collective-permute-start.21
  223.3 4.9 %collective-permute-start.30 = (bf16[4608,256]{1,0:T(8,128)(2,1)S(1)}, bf16[4608,256]{1,0:T(8,128)(2,1)}, u32[]{:S(2)}, u32[]{:S(2)}) collective-permute-start(bf16[4608,256]{1,0:T(8,128)(2,1)S(1)} %pad_maximum_fusion.value_ref), channel_id=1, source_target_pairs={{0,2},{2,0},{4,6},{6,4},{8,10},{10,8},{12,14},{14,12},{16,18},{18,... | collective-permute-start | bytes 7077896 | tf_op jit(solution)/shard_map/ppermute | solution.py:917
  228.2 2.5 collective-permute-start.20
  235.2 2.0 collective-permute-done.23
  237.4 2.6 collective-permute-start.25
  240.0 3.6 %expert_outputs.4 = (f32[3072,768]{1,0:T(8,128)}, f32[768,3072]{1,0:T(8,128)}) custom-call(s32[1]{0:T(128)} %bitcast.1.side_ref.half_ref, bf16[4608,256]{1,0:T(8,128)(2,1)} %copy-done.1), custom_call_target="tpu_custom_call" | custom-call | flops 1179648 | bytes 7077888 | tf_op jit(solution)/shard_map/expert_outputs/pallas_call | solution.py:83
  246.4 2.7 collective-permute-done.28
  250.2 1.8 collective-permute-start.27
  252.0 3.6 %expert_outputs.5 = (f32[3072,768]{1,0:T(8,128)}, f32[768,3072]{1,0:T(8,128)}) custom-call(s32[1]{0:T(128)S(6)} %sub.39.half_ref, bf16[4608,256]{1,0:T(8,128)(2,1)} %collective-permute-done.30.value_ref, f32[3072,768]{1,0:T(8,128)} %get-tuple-element.301.refs_0_, f32[768,3072]{1,0:T(8,128)} %get-tuple-element.293.refs_1_), custom_call_target="tpu_custom_call", output_to_operand_aliasing={{0}: (2, {}), {1}: (3, {})} | custom-call | flops 1179648 | bytes 7077888 | tf_op jit(solution)/shard_map/expert_outputs/pallas_call | solution.py:83
  256.8 1.9 collective-permute-start.31
  261.0 4.2 %collective-permute-done.31 = bf16[864,256]{1,0:T(8,128)(2,1)S(1)} collective-permute-done((bf16[864,256]{1,0:T(8,128)(2,1)S(1)}, bf16[864,256]{1,0:T(8,128)(2,1)S(1)}, u32[]{:S(2)}, u32[]{:S(2)}) %collective-permute-start.31) | collective-permute-done | bytes 442400 | tf_op jit(solution)/shard_map/ppermute | solution.py:917
  265.3 2.7 collective-permute-start.34
  268.0 11.0 %collective-permute-start.38 = (bf16[4608,256]{1,0:T(8,128)(2,1)S(1)}, bf16[4608,256]{1,0:T(8,128)(2,1)}, u32[]{:S(2)}, u32[]{:S(2)}) collective-permute-start(bf16[4608,256]{1,0:T(8,128)(2,1)S(1)} %pad_maximum_fusion.1.value_ref), channel_id=1, source_target_pairs={{0,2},{2,0},{4,6},{6,4},{8,10},{10,8},{12,14},{14,12},{16,18},{18,... | collective-permute-start | bytes 7077896 | tf_op jit(solution)/shard_map/ppermute | solution.py:917
  280.3 3.6 %expert_outputs.6 = (f32[3072,768]{1,0:T(8,128)}, f32[768,3072]{1,0:T(8,128)}) custom-call(s32[1]{0:T(128)} %bitcast.1.side_ref.half_ref, bf16[4608,256]{1,0:T(8,128)(2,1)} %copy-done, f32[3072,768]{1,0:T(8,128)} %get-tuple-element.314.refs_0_, f32[768,3072]{1,0:T(8,128)} %get-tuple-element.302.refs_1_), custom_call_target="tpu_custom_call", output_to_operand_aliasing={{0}: (2, {}), {1}: (3, {})} | custom-call | flops 1179648 | bytes 7077888 | tf_op jit(solution)/shard_map/expert_outputs/pallas_call | solution.py:83
  283.8 2.4 collective-permute-done.35
  288.6 5.2 %collective-permute-start.36 = (bf16[3456,256]{1,0:T(8,128)(2,1)S(1)}, bf16[3456,256]{1,0:T(8,128)(2,1)}, u32[]{:S(2)}, u32[]{:S(2)}) collective-permute-start(bf16[3456,256]{1,0:T(8,128)(2,1)S(1)} %pad_maximum_fusion.2.first_ref), channel_id=1, source_target_pairs={{0,2},{1,3},{2,0},{3,1},{4,6},{5,7},{6,4},{7,5},{8,10},{9,11},{10,... | collective-permute-start | bytes 5308424 | tf_op jit(solution)/shard_map/ppermute | solution.py:917
  293.8 3.6 %expert_outputs.7 = (f32[3072,768]{1,0:T(8,128)}, f32[768,3072]{1,0:T(8,128)}) custom-call(s32[1]{0:T(128)S(6)} %sub.39.half_ref, bf16[4608,256]{1,0:T(8,128)(2,1)} %collective-permute-done.38.value_ref, f32[3072,768]{1,0:T(8,128)} %get-tuple-element.321.refs_0_, f32[768,3072]{1,0:T(8,128)} %get-tuple-element.315.refs_1_), custom_call_target="tpu_custom_call", output_to_operand_aliasing={{0}: (2, {}), {1}: (3, {})} | custom-call | flops 1179648 | bytes 7077888 | tf_op jit(solution)/shard_map/expert_outputs/pallas_call | solution.py:83
  297.4 3.5 %collective-permute-done.37 = bf16[640,256]{1,0:T(8,128)(2,1)S(1)} collective-permute-done((bf16[640,256]{1,0:T(8,128)(2,1)S(1)}, bf16[640,256]{1,0:T(8,128)(2,1)S(1)}, u32[]{:S(2)}, u32[]{:S(2)}) %collective-permute-start.37) | collective-permute-done | bytes 327712 | tf_op jit(solution)/shard_map/ppermute | solution.py:917
  301.8 4.2 %projection_outputs.1 = (f32[768,2304]{1,0:T(8,128)}, f32[768,768]{1,0:T(8,128)}) custom-call(s32[1]{0:T(128)} %bitcast.1.side_ref.half_ref, bf16[3456,256]{1,0:T(8,128)(2,1)} %copy-done.2, bf16[1280,256]{1,0:T(8,128)(2,1)} %copy-done.3), custom_call_target="tpu_custom_call" | custom-call | flops 884736 | bytes 5308416 | tf_op jit(solution)/shard_map/projection_outputs/pallas_call | solution.py:83
  306.8 4.3 %last_outputs.1 = (f32[768,2304]{1,0:T(8,128)}, f32[768,768]{1,0:T(8,128)}, f32[1,768]{1,0:T(1,128)}, f32[1,768]{1,0:T(1,128)}, f32[1,768]{1,0:T(1,128)}, /*inde...) custom-call(s32[1]{0:T(128)S(6)} %sub.39.half_ref, ...), custom_call_target="tpu_custom_call", output_to_operand_aliasing={{0}: (6, {}), {1}: (7, {})} | custom-call | flops 327680 | bytes 1966080 | tf_op jit(solution)/shard_map/last_outputs/pallas_call | solution.py:83
  (142 shorter events, 45.1 us)
Async XLA Ops:
  1.8 14.0 %collective-permute-start = (bf16[256,768]{1,0:T(8,128)(2,1)S(1)}, bf16[256,768]{1,0:T(8,128)(2,1)S(1)}, u32[]{:S(2)}, u32[]{:S(2)}) collective-permute-start(bf16[256,768]{1,0:T(8,128)(2,1)S(1)} %get-tuple-element.373), channel_id=1, source_target_pairs={{0,1},{2,3},{4,5},{6,7},{8,9},{10,11},{12,13},{14,15},{16,17},{18,... | collective-permute-start | bytes 1179656 | tf_op jit(solution)/shard_map/ppermute | solution.py:1011
  3.2 12.7 %collective-permute-start.1 = (f32[2,768]{1,0:T(2,128)S(1)}, f32[2,768]{1,0:T(2,128)S(1)}, u32[]{:S(2)}, u32[]{:S(2)}) collective-permute-start(f32[2,768]{1,0:T(2,128)S(1)} %pad_maximum_fusion.14), channel_id=1, source_target_pairs={{0,1},{2,3},{4,5},{6,7},{8,9},{10,11},{12,13},{14,15},{16,17},{18,... | collective-permute-start | bytes 18440 | tf_op jit(solution)/shard_map/ppermute | solution.py:1011
  4.5 28.3 %collective-permute-start.2 = (bf16[256,768]{1,0:T(8,128)(2,1)S(1)}, bf16[256,768]{1,0:T(8,128)(2,1)S(1)}, u32[]{:S(2)}, u32[]{:S(2)}) collective-permute-start(bf16[256,768]{1,0:T(8,128)(2,1)S(1)} %get-tuple-element.372), channel_id=1, source_target_pairs={{0,1},{2,3},{4,5},{6,7},{8,9},{10,11},{12,13},{14,15},{16,17},{18,... | collective-permute-start | bytes 1179656 | tf_op jit(solution)/shard_map/ppermute | solution.py:1011
  5.8 8.5 %copy-start.16 = (f32[768]{0:T(1024)S(1)}, f32[768]{0:T(1024)}, u32[]{:S(2)}) copy-start(f32[768]{0:T(1024)} %param.24) | copy-start | bytes 9220
  94.9 20.2 %collective-permute-start.3 = (bf16[4608,256]{1,0:T(8,128)(2,1)}, bf16[4608,256]{1,0:T(8,128)(2,1)S(1)}, u32[]{:S(2)}, u32[]{:S(2)}) collective-permute-start(bf16[4608,256]{1,0:T(8,128)(2,1)} %get-tuple-element.193), channel_id=1, source_target_pairs={{0,2},{2,0},{4,6},{6,4},{8,10},{10,8},{12,14},{14,12},{16,18},{18,... | collective-permute-start | bytes 7077896 | tf_op jit(solution)/shard_map/ppermute | solution.py:917
  95.0 8.7 %collective-permute-start.4 = (bf16[4608,256]{1,0:T(8,128)(2,1)}, bf16[4608,256]{1,0:T(8,128)(2,1)S(1)}, u32[]{:S(2)}, u32[]{:S(2)}) collective-permute-start(bf16[4608,256]{1,0:T(8,128)(2,1)} %get-tuple-element.195), channel_id=1, source_target_pairs={{0,2},{2,0},{4,6},{6,4},{8,10},{10,8},{12,14},{14,12},{16,18},{18,... | collective-permute-start | bytes 7077896 | tf_op jit(solution)/shard_map/ppermute | solution.py:917
  95.5 8.2 %copy-start.6 = (bf16[4608,256]{1,0:T(8,128)(2,1)S(1)}, bf16[4608,256]{1,0:T(8,128)(2,1)}, u32[]{:S(2)}) copy-start(bf16[4608,256]{1,0:T(8,128)(2,1)} %get-tuple-element.199) | copy-start | bytes 7077892
  105.3 20.0 %collective-permute-start.6 = (bf16[2304,256]{1,0:T(8,128)(2,1)}, bf16[2304,256]{1,0:T(8,128)(2,1)S(1)}, u32[]{:S(2)}, u32[]{:S(2)}) collective-permute-start(bf16[2304,256]{1,0:T(8,128)(2,1)} %get-tuple-element.355), channel_id=1, source_target_pairs={{0,4},{2,10},{4,0},{6,14},{8,12},{10,2},{12,8},{14,6},{16,20},{18,... | collective-permute-start | bytes 3538952 | tf_op jit(solution)/shard_map/ppermute | solution.py:917
  106.8 8.3 %copy-start.5 = (bf16[4608,256]{1,0:T(8,128)(2,1)S(1)}, bf16[4608,256]{1,0:T(8,128)(2,1)}, u32[]{:S(2)}) copy-start(bf16[4608,256]{1,0:T(8,128)(2,1)} %get-tuple-element.207) | copy-start | bytes 7077892
  116.7 22.1 %collective-permute-start.5 = (bf16[2304,256]{1,0:T(8,128)(2,1)}, bf16[2304,256]{1,0:T(8,128)(2,1)S(1)}, u32[]{:S(2)}, u32[]{:S(2)}) collective-permute-start(bf16[2304,256]{1,0:T(8,128)(2,1)} %get-tuple-element.356), channel_id=1, source_target_pairs={{0,4},{2,10},{4,0},{6,14},{8,12},{10,2},{12,8},{14,6},{16,20},{18,... | collective-permute-start | bytes 3538952 | tf_op jit(solution)/shard_map/ppermute | solution.py:917
  127.8 23.9 %collective-permute-start.8 = (bf16[1152,256]{1,0:T(8,128)(2,1)S(1)}, bf16[1152,256]{1,0:T(8,128)(2,1)S(1)}, u32[]{:S(2)}, u32[]{:S(2)}) collective-permute-start(bf16[1152,256]{1,0:T(8,128)(2,1)S(1)} %get-tuple-element.367), channel_id=1, source_target_pairs={{0,16},{2,6},{4,20},{6,2},{8,24},{10,14},{12,28},{14,10},{16,0},{1... | collective-permute-start | bytes 1769480 | tf_op jit(solution)/shard_map/ppermute | solution.py:917
  139.9 33.6 %collective-permute-start.10 = (bf16[1152,256]{1,0:T(8,128)(2,1)}, bf16[1152,256]{1,0:T(8,128)(2,1)S(1)}, u32[]{:S(2)}, u32[]{:S(2)}) collective-permute-start(bf16[1152,256]{1,0:T(8,128)(2,1)} %get-tuple-element.365), channel_id=1, source_target_pairs={{0,16},{2,6},{4,20},{6,2},{8,24},{10,14},{12,28},{14,10},{16,0},{1... | collective-permute-start | bytes 1769480 | tf_op jit(solution)/shard_map/ppermute | solution.py:917
  151.6 9.6 %collective-permute-start.7 = (bf16[3456,256]{1,0:T(8,128)(2,1)}, bf16[3456,256]{1,0:T(8,128)(2,1)S(1)}, u32[]{:S(2)}, u32[]{:S(2)}) collective-permute-start(bf16[3456,256]{1,0:T(8,128)(2,1)} %get-tuple-element.233), channel_id=1, source_target_pairs={{0,2},{1,3},{2,0},{3,1},{4,6},{5,7},{6,4},{7,5},{8,10},{9,11},{10,... | collective-permute-start | bytes 5308424 | tf_op jit(solution)/shard_map/ppermute | solution.py:917
  152.6 8.7 %copy-start.7 = (bf16[3456,256]{1,0:T(8,128)(2,1)S(1)}, bf16[3456,256]{1,0:T(8,128)(2,1)}, u32[]{:S(2)}) copy-start(bf16[3456,256]{1,0:T(8,128)(2,1)} %get-tuple-element.238) | copy-start | bytes 5308420
  152.6 10.9 %collective-permute-start.11 = (bf16[576,256]{1,0:T(8,128)(2,1)}, bf16[576,256]{1,0:T(8,128)(2,1)S(1)}, u32[]{:S(2)}, u32[]{:S(2)}) collective-permute-start(bf16[576,256]{1,0:T(8,128)(2,1)} %get-tuple-element.383), channel_id=1, source_target_pairs={{0,8},{2,18},{4,12},{6,22},{8,0},{10,26},{12,4},{14,30},{16,24},{1... | collective-permute-start | bytes 884744 | tf_op jit(solution)/shard_map/ppermute | solution.py:917
  161.7 13.1 %collective-permute-start.9 = (bf16[1728,256]{1,0:T(8,128)(2,1)S(1)}, bf16[1728,256]{1,0:T(8,128)(2,1)S(1)}, u32[]{:S(2)}, u32[]{:S(2)}) collective-permute-start(bf16[1728,256]{1,0:T(8,128)(2,1)S(1)} %get-tuple-element.358), channel_id=1, source_target_pairs={{0,1},{1,0},{2,6},{3,7},{4,5},{5,4},{6,2},{7,3},{8,9},{9,8},{10,14... | collective-permute-start | bytes 2654216 | tf_op jit(solution)/shard_map/ppermute | solution.py:917
  163.6 20.8 %collective-permute-start.13 = (bf16[576,256]{1,0:T(8,128)(2,1)S(1)}, bf16[576,256]{1,0:T(8,128)(2,1)S(1)}, u32[]{:S(2)}, u32[]{:S(2)}) collective-permute-start(bf16[576,256]{1,0:T(8,128)(2,1)S(1)} %add_convert_fusion.17), channel_id=1, source_target_pairs={{0,8},{2,18},{4,12},{6,22},{8,0},{10,26},{12,4},{14,30},{16,24},{1... | collective-permute-start | bytes 884744 | tf_op jit(solution)/shard_map/ppermute | solution.py:917
  173.7 8.9 %collective-permute-start.14 = (bf16[576,256]{1,0:T(8,128)(2,1)S(1)}, bf16[576,256]{1,0:T(8,128)(2,1)S(1)}, u32[]{:S(2)}, u32[]{:S(2)}) collective-permute-start(bf16[576,256]{1,0:T(8,128)(2,1)S(1)} %get-tuple-element.381), channel_id=1, source_target_pairs={{0,8},{2,18},{4,12},{6,22},{8,0},{10,26},{12,4},{14,30},{16,24},{1... | collective-permute-start | bytes 884744 | tf_op jit(solution)/shard_map/ppermute | solution.py:917
  175.1 22.0 %collective-permute-start.17 = (bf16[864,256]{1,0:T(8,128)(2,1)S(1)}, bf16[864,256]{1,0:T(8,128)(2,1)S(1)}, u32[]{:S(2)}, u32[]{:S(2)}) collective-permute-start(bf16[864,256]{1,0:T(8,128)(2,1)S(1)} %get-tuple-element.371), channel_id=1, source_target_pairs={{0,4},{1,5},{2,3},{3,2},{4,0},{5,1},{6,7},{7,6},{8,12},{9,13},{10,... | collective-permute-start | bytes 1327112 | tf_op jit(solution)/shard_map/ppermute | solution.py:917
  182.7 15.7 %collective-permute-start.16 = (bf16[576,256]{1,0:T(8,128)(2,1)S(1)}, bf16[576,256]{1,0:T(8,128)(2,1)S(1)}, u32[]{:S(2)}, u32[]{:S(2)}) collective-permute-start(bf16[576,256]{1,0:T(8,128)(2,1)S(1)} %add_convert_fusion.14), channel_id=1, source_target_pairs={{0,8},{2,18},{4,12},{6,22},{8,0},{10,26},{12,4},{14,30},{16,24},{1... | collective-permute-start | bytes 884744 | tf_op jit(solution)/shard_map/ppermute | solution.py:917
  184.4 18.6 %collective-permute-start.15 = (bf16[1152,256]{1,0:T(8,128)(2,1)S(1)}, bf16[1152,256]{1,0:T(8,128)(2,1)S(1)}, u32[]{:S(2)}, u32[]{:S(2)}) collective-permute-start(bf16[1152,256]{1,0:T(8,128)(2,1)S(1)} %pad_maximum_fusion.7), channel_id=1, source_target_pairs={{0,16},{2,6},{4,20},{6,2},{8,24},{10,14},{12,28},{14,10},{16,0},{1... | collective-permute-start | bytes 1769480 | tf_op jit(solution)/shard_map/ppermute | solution.py:917
  187.2 19.5 %collective-permute-start.12 = (bf16[512,768]{1,0:T(8,128)(2,1)S(1)}, bf16[512,768]{1,0:T(8,128)(2,1)S(1)}, u32[]{:S(2)}, u32[]{:S(2)}) collective-permute-start(bf16[512,768]{1,0:T(8,128)(2,1)S(1)} %copy-done.17), channel_id=1, source_target_pairs={{1,0},{3,2},{5,4},{7,6},{9,8},{11,10},{13,12},{15,14},{17,16},{19,... | collective-permute-start | bytes 2359304 | tf_op jit(solution)/shard_map/ppermute | solution.py:1012
  197.0 20.7 %collective-permute-start.19 = (bf16[1280,256]{1,0:T(8,128)(2,1)}, bf16[1280,256]{1,0:T(8,128)(2,1)S(1)}, u32[]{:S(2)}, u32[]{:S(2)}) collective-permute-start(bf16[1280,256]{1,0:T(8,128)(2,1)} %get-tuple-element.262), channel_id=1, source_target_pairs={{0,2},{1,3},{2,0},{3,1},{4,6},{5,7},{6,4},{7,5},{8,10},{9,11},{10,... | collective-permute-start | bytes 1966088 | tf_op jit(solution)/shard_map/ppermute | solution.py:917
  197.2 25.0 %collective-permute-start.18 = (bf16[432,256]{1,0:T(8,128)(2,1)S(1)}, bf16[432,256]{1,0:T(8,128)(2,1)S(1)}, u32[]{:S(2)}, u32[]{:S(2)}) collective-permute-start(bf16[432,256]{1,0:T(8,128)(2,1)S(1)} %get-tuple-element.387), channel_id=1, source_target_pairs={{0,8},{1,9},{2,10},{3,11},{4,12},{5,13},{6,14},{7,15},{8,0},{9,1},... | collective-permute-start | bytes 663560 | tf_op jit(solution)/shard_map/ppermute | solution.py:917
  198.4 34.7 %collective-permute-start.24 = (bf16[1152,256]{1,0:T(8,128)(2,1)S(1)}, bf16[1152,256]{1,0:T(8,128)(2,1)}, u32[]{:S(2)}, u32[]{:S(2)}) collective-permute-start(bf16[1152,256]{1,0:T(8,128)(2,1)S(1)} %pad_maximum_fusion.8), channel_id=1, source_target_pairs={{0,16},{2,6},{4,20},{6,2},{8,24},{10,14},{12,28},{14,10},{16,0},{1... | collective-permute-start | bytes 1769480 | tf_op jit(solution)/shard_map/ppermute | solution.py:917
  203.2 19.7 %collective-permute-start.22 = (bf16[2304,256]{1,0:T(8,128)(2,1)S(1)}, bf16[2304,256]{1,0:T(8,128)(2,1)S(1)}, u32[]{:S(2)}, u32[]{:S(2)}) collective-permute-start(bf16[2304,256]{1,0:T(8,128)(2,1)S(1)} %pad_maximum_fusion.3), channel_id=1, source_target_pairs={{0,4},{2,10},{4,0},{6,14},{8,12},{10,2},{12,8},{14,6},{16,20},{18,... | collective-permute-start | bytes 3538952 | tf_op jit(solution)/shard_map/ppermute | solution.py:917
  219.7 11.1 %collective-permute-start.21 = (bf16[640,256]{1,0:T(8,128)(2,1)}, bf16[640,256]{1,0:T(8,128)(2,1)}, u32[]{:S(2)}, u32[]{:S(2)}) collective-permute-start(bf16[640,256]{1,0:T(8,128)(2,1)} %get-tuple-element.375), channel_id=1, source_target_pairs={{0,1},{1,0},{2,6},{3,7},{4,5},{5,4},{6,2},{7,3},{8,9},{9,8},{10,14... | collective-permute-start | bytes 983048 | tf_op jit(solution)/shard_map/ppermute | solution.py:917
  223.3 11.0 %copy-start.1 = (bf16[4608,256]{1,0:T(8,128)(2,1)}, bf16[4608,256]{1,0:T(8,128)(2,1)S(1)}, u32[]{:S(2)}) copy-start(bf16[4608,256]{1,0:T(8,128)(2,1)S(1)} %pad_maximum_fusion.value_ref) | copy-start | bytes 7077892
  223.3 28.7 %collective-permute-start.30 = (bf16[4608,256]{1,0:T(8,128)(2,1)S(1)}, bf16[4608,256]{1,0:T(8,128)(2,1)}, u32[]{:S(2)}, u32[]{:S(2)}) collective-permute-start(bf16[4608,256]{1,0:T(8,128)(2,1)S(1)} %pad_maximum_fusion.value_ref), channel_id=1, source_target_pairs={{0,2},{2,0},{4,6},{6,4},{8,10},{10,8},{12,14},{14,12},{16,18},{18,... | collective-permute-start | bytes 7077896 | tf_op jit(solution)/shard_map/ppermute | solution.py:917
  228.2 9.1 %collective-permute-start.20 = (bf16[216,256]{1,0:T(8,128)(2,1)}, bf16[216,256]{1,0:T(8,128)(2,1)S(1)}, u32[]{:S(2)}, u32[]{:S(2)}) collective-permute-start(bf16[216,256]{1,0:T(8,128)(2,1)} %get-tuple-element.398), channel_id=1, source_target_pairs={{0,16},{1,17},{2,18},{3,19},{4,20},{5,21},{6,22},{7,23},{8,24},{9,... | collective-permute-start | bytes 331784 | tf_op jit(solution)/shard_map/ppermute | solution.py:917
  231.8 5.4 %collective-permute-start.23 = (bf16[320,256]{1,0:T(8,128)(2,1)S(1)}, bf16[320,256]{1,0:T(8,128)(2,1)S(1)}, u32[]{:S(2)}, u32[]{:S(2)}) collective-permute-start(bf16[320,256]{1,0:T(8,128)(2,1)S(1)} %get-tuple-element.390), channel_id=1, source_target_pairs={{0,4},{1,5},{2,3},{3,2},{4,0},{5,1},{6,7},{7,6},{8,12},{9,13},{10,... | collective-permute-start | bytes 491528 | tf_op jit(solution)/shard_map/ppermute | solution.py:917
  234.4 24.4 %collective-permute-start.33 = (bf16[2304,256]{1,0:T(8,128)(2,1)S(1)}, bf16[2304,256]{1,0:T(8,128)(2,1)}, u32[]{:S(2)}, u32[]{:S(2)}) collective-permute-start(bf16[2304,256]{1,0:T(8,128)(2,1)S(1)} %pad_maximum_fusion.4), channel_id=1, source_target_pairs={{0,4},{2,10},{4,0},{6,14},{8,12},{10,2},{12,8},{14,6},{16,20},{18,... | collective-permute-start | bytes 3538952 | tf_op jit(solution)/shard_map/ppermute | solution.py:917
  237.2 6.3 %collective-permute-start.26 = (bf16[160,256]{1,0:T(8,128)(2,1)S(1)}, bf16[160,256]{1,0:T(8,128)(2,1)S(1)}, u32[]{:S(2)}, u32[]{:S(2)}) collective-permute-start(bf16[160,256]{1,0:T(8,128)(2,1)S(1)} %get-tuple-element.403), channel_id=1, source_target_pairs={{0,8},{1,9},{2,10},{3,11},{4,12},{5,13},{6,14},{7,15},{8,0},{9,1},... | collective-permute-start | bytes 245768 | tf_op jit(solution)/shard_map/ppermute | solution.py:917
  237.4 8.3 %collective-permute-start.25 = (bf16[216,256]{1,0:T(8,128)(2,1)S(1)}, bf16[216,256]{1,0:T(8,128)(2,1)S(1)}, u32[]{:S(2)}, u32[]{:S(2)}) collective-permute-start(bf16[216,256]{1,0:T(8,128)(2,1)S(1)} %add_convert_fusion.24), channel_id=1, source_target_pairs={{0,16},{1,17},{2,18},{3,19},{4,20},{5,21},{6,22},{7,23},{8,24},{9,... | collective-permute-start | bytes 331784 | tf_op jit(solution)/shard_map/ppermute | solution.py:917
  243.6 5.5 %collective-permute-start.28 = (bf16[80,256]{1,0:T(8,128)(2,1)S(1)}, bf16[80,256]{1,0:T(8,128)(2,1)S(1)}, u32[]{:S(2)}, u32[]{:S(2)}) collective-permute-start(bf16[80,256]{1,0:T(8,128)(2,1)S(1)} %get-tuple-element.409), channel_id=1, source_target_pairs={{0,16},{1,17},{2,18},{3,19},{4,20},{5,21},{6,22},{7,23},{8,24},{9,... | collective-permute-start | bytes 122888 | tf_op jit(solution)/shard_map/ppermute | solution.py:917
  249.7 5.9 %collective-permute-start.29 = (bf16[80,256]{1,0:T(8,128)(2,1)}, bf16[80,256]{1,0:T(8,128)(2,1)}, u32[]{:S(2)}, u32[]{:S(2)}) collective-permute-start(bf16[80,256]{1,0:T(8,128)(2,1)} %add_convert_fusion.29), channel_id=1, source_target_pairs={{0,16},{1,17},{2,18},{3,19},{4,20},{5,21},{6,22},{7,23},{8,24},{9,... | collective-permute-start | bytes 122888 | tf_op jit(solution)/shard_map/ppermute | solution.py:917
  250.2 6.5 %collective-permute-start.27 = (bf16[432,256]{1,0:T(8,128)(2,1)}, bf16[432,256]{1,0:T(8,128)(2,1)S(1)}, u32[]{:S(2)}, u32[]{:S(2)}) collective-permute-start(bf16[432,256]{1,0:T(8,128)(2,1)} %pad_maximum_fusion.11), channel_id=1, source_target_pairs={{0,8},{1,9},{2,10},{3,11},{4,12},{5,13},{6,14},{7,15},{8,0},{9,1},... | collective-permute-start | bytes 663560 | tf_op jit(solution)/shard_map/ppermute | solution.py:917
  252.0 4.7 %copy-start.9 = (bf16[432,256]{1,0:T(8,128)(2,1)S(1)}, bf16[432,256]{1,0:T(8,128)(2,1)}, u32[]{:S(2)}) copy-start(bf16[432,256]{1,0:T(8,128)(2,1)} %pad_maximum_fusion.11) | copy-start | bytes 663556
  256.5 4.5 %collective-permute-start.32 = (bf16[160,256]{1,0:T(8,128)(2,1)S(1)}, bf16[160,256]{1,0:T(8,128)(2,1)S(1)}, u32[]{:S(2)}, u32[]{:S(2)}) collective-permute-start(bf16[160,256]{1,0:T(8,128)(2,1)S(1)} %pad_maximum_fusion.13), channel_id=1, source_target_pairs={{0,8},{1,9},{2,10},{3,11},{4,12},{5,13},{6,14},{7,15},{8,0},{9,1},... | collective-permute-start | bytes 245768 | tf_op jit(solution)/shard_map/ppermute | solution.py:917
  256.8 8.4 %collective-permute-start.31 = (bf16[864,256]{1,0:T(8,128)(2,1)S(1)}, bf16[864,256]{1,0:T(8,128)(2,1)S(1)}, u32[]{:S(2)}, u32[]{:S(2)}) collective-permute-start(bf16[864,256]{1,0:T(8,128)(2,1)S(1)} %pad_maximum_fusion.9), channel_id=1, source_target_pairs={{0,4},{1,5},{2,3},{3,2},{4,0},{5,1},{6,7},{7,6},{8,12},{9,13},{10,... | collective-permute-start | bytes 1327112 | tf_op jit(solution)/shard_map/ppermute | solution.py:917
  260.4 7.6 %copy-start = (bf16[4608,256]{1,0:T(8,128)(2,1)}, bf16[4608,256]{1,0:T(8,128)(2,1)S(1)}, u32[]{:S(2)}) copy-start(bf16[4608,256]{1,0:T(8,128)(2,1)S(1)} %pad_maximum_fusion.1.value_ref) | copy-start | bytes 7077892
  265.3 21.9 %collective-permute-start.34 = (bf16[1728,256]{1,0:T(8,128)(2,1)S(1)}, bf16[1728,256]{1,0:T(8,128)(2,1)}, u32[]{:S(2)}, u32[]{:S(2)}) collective-permute-start(bf16[1728,256]{1,0:T(8,128)(2,1)S(1)} %pad_maximum_fusion.5), channel_id=1, source_target_pairs={{0,1},{1,0},{2,6},{3,7},{4,5},{5,4},{6,2},{7,3},{8,9},{9,8},{10,14... | collective-permute-start | bytes 2654216 | tf_op jit(solution)/shard_map/ppermute | solution.py:917
  268.0 25.8 %collective-permute-start.38 = (bf16[4608,256]{1,0:T(8,128)(2,1)S(1)}, bf16[4608,256]{1,0:T(8,128)(2,1)}, u32[]{:S(2)}, u32[]{:S(2)}) collective-permute-start(bf16[4608,256]{1,0:T(8,128)(2,1)S(1)} %pad_maximum_fusion.1.value_ref), channel_id=1, source_target_pairs={{0,2},{2,0},{4,6},{6,4},{8,10},{10,8},{12,14},{14,12},{16,18},{18,... | collective-permute-start | bytes 7077896 | tf_op jit(solution)/shard_map/ppermute | solution.py:917
  279.0 7.2 %collective-permute-start.35 = (bf16[320,256]{1,0:T(8,128)(2,1)S(1)}, bf16[320,256]{1,0:T(8,128)(2,1)}, u32[]{:S(2)}, u32[]{:S(2)}) collective-permute-start(bf16[320,256]{1,0:T(8,128)(2,1)S(1)} %pad_maximum_fusion.12), channel_id=1, source_target_pairs={{0,4},{1,5},{2,3},{3,2},{4,0},{5,1},{6,7},{7,6},{8,12},{9,13},{10,... | collective-permute-start | bytes 491528 | tf_op jit(solution)/shard_map/ppermute | solution.py:917
  288.6 8.8 %copy-start.2 = (bf16[3456,256]{1,0:T(8,128)(2,1)}, bf16[3456,256]{1,0:T(8,128)(2,1)S(1)}, u32[]{:S(2)}) copy-start(bf16[3456,256]{1,0:T(8,128)(2,1)S(1)} %pad_maximum_fusion.2.first_ref) | copy-start | bytes 5308420
  288.6 17.4 %collective-permute-start.36 = (bf16[3456,256]{1,0:T(8,128)(2,1)S(1)}, bf16[3456,256]{1,0:T(8,128)(2,1)}, u32[]{:S(2)}, u32[]{:S(2)}) collective-permute-start(bf16[3456,256]{1,0:T(8,128)(2,1)S(1)} %pad_maximum_fusion.2.first_ref), channel_id=1, source_target_pairs={{0,2},{1,3},{2,0},{3,1},{4,6},{5,7},{6,4},{7,5},{8,10},{9,11},{10,... | collective-permute-start | bytes 5308424 | tf_op jit(solution)/shard_map/ppermute | solution.py:917
  293.8 7.1 %collective-permute-start.37 = (bf16[640,256]{1,0:T(8,128)(2,1)S(1)}, bf16[640,256]{1,0:T(8,128)(2,1)S(1)}, u32[]{:S(2)}, u32[]{:S(2)}) collective-permute-start(bf16[640,256]{1,0:T(8,128)(2,1)S(1)} %pad_maximum_fusion.10), channel_id=1, source_target_pairs={{0,1},{1,0},{2,6},{3,7},{4,5},{5,4},{6,2},{7,3},{8,9},{9,8},{10,14... | collective-permute-start | bytes 983048 | tf_op jit(solution)/shard_map/ppermute | solution.py:917
  301.0 5.0 %collective-permute-start.39 = (bf16[1280,256]{1,0:T(8,128)(2,1)S(1)}, bf16[1280,256]{1,0:T(8,128)(2,1)S(1)}, u32[]{:S(2)}, u32[]{:S(2)}) collective-permute-start(bf16[1280,256]{1,0:T(8,128)(2,1)S(1)} %pad_maximum_fusion.6.last_ref.mine_ref), channel_id=1, source_target_pairs={{0,2},{1,3},{2,0},{3,1},{4,6},{5,7},{6,4},{7,5},{8,10},{9,11},{10,... | collective-permute-start | bytes 1966088 | tf_op jit(solution)/shard_map/ppermute | solution.py:917
  (11 other events, 18.3 us)

commit v7 on v6

--- a/solution.py
+++ b/solution.py
@@ -828,85 +828,102 @@
     )
 
 
-def store_projection(first_ref, last_ref, in_ref, out_ref):
-    tall = in_ref.shape[0]
-    count = first_ref.shape[0] // tall
-    for part in range(count - 1):
-        piece = first_ref[part * tall : (part + 1) * tall, :]
-        in_ref[:, part * LANES : (part + 1) * LANES] = piece.astype(f32)
-    in_ref[:, (count - 1) * LANES :] = last_ref[...].astype(f32)
-    out_ref[...] = first_ref[(count - 1) * tall :, :].astype(f32)
-
-
-def projection_kernel(half_ref, first_ref, last_ref, in_ref, out_ref):
-    store_projection(first_ref, last_ref, in_ref, out_ref)
-
-
-def last_kernel(half_ref, flag_ref, first_ref, last_ref, mine_ref, got_ref, *refs):
-    in_ref, out_ref, *vec_refs, expand_ref, pair_ref, project_ref = refs[2:]
-    store_projection(first_ref, last_ref, in_ref, out_ref)
-
-    @pl.when(pl.program_id(0) == 0)
-    def _():
-        both = mine_ref[...].astype(f32) + got_ref[...].astype(f32)
-        width = vec_refs[0].shape[1]
-        rows = jnp.concatenate([both[at * 32 : (at + 1) * 32] for at in range(width // LANES)], axis=1)
-        own = jnp.where(flag_ref[0] == 1, rows[16:], rows[:16])
-        for number, ref in enumerate(vec_refs):
-            ref[...] = own[number : number + 1]
-        for number in range(expand_ref.shape[1] // width):
-            cols = slice(number * width, (number + 1) * width)
-            expand_ref[:, cols] = own[5 + number : 6 + number]
-        project_ref[...] = rows[9:10]
-        pair_ref[...] = rows[10:12]
-
-
-def projection_specs(width):
+def first_kernel(half_ref, value_ref, *refs):
+    in_ref, out_ref, wide, narrow, sems = refs[-5:]
+    tall = wide.shape[1]
+    count = value_ref.shape[0] // tall // 3
+    columns = in_ref.shape[1] // 3
+    rows = pl.ds(pl.multiple_of(half_ref[0] * tall, tall), tall)
+    copies = []
+    for part in range(3):
+        at = part * count * tall
+        for number in range(count - 1):
+            piece = value_ref[at + number * tall : at + (number + 1) * tall, :]
+            wide[part, :, number * LANES : (number + 1) * LANES] = piece.astype(f32)
+        piece = value_ref[at + (count - 1) * tall : at + count * tall, :]
+        narrow[part] = piece.astype(f32)
+        places = (
+            (wide, in_ref.at[rows, pl.ds(part * columns, (count - 1) * LANES)]),
+            (narrow, out_ref.at[rows, pl.ds(part * LANES, LANES)]),
+        )
+        for kind, (here, there) in enumerate(places):
+            copy = pltpu.make_async_copy(here.at[part], there, sems.at[kind, part])
+            copy.start()
+            copies.append(copy)
+    for copy in copies:
+        copy.wait()
+
+
+def first_outputs(order, half, value, width, earlier):
     tall = width // 2
-    ins = [
-        pl.BlockSpec((tall * width // LANES, LANES), lambda b, *_: (b, 0)),
-        pl.BlockSpec((tall, LANES), lambda b, *_: (b, 0)),
-    ]
-    outs = [
-        pl.BlockSpec((tall, width), lambda b, at, *_: (at[0], b)),
-        pl.BlockSpec((tall, LANES), lambda b, at, *_: (at[0], b)),
-    ]
-    return ins, outs, [shaped((width, 3 * width), f32), shaped((width, width), f32)]
-
-
-def projection_outputs(order, half, first, last, width):
-    ins, outs, shapes = projection_specs(width)
+    anywhere = pl.BlockSpec(memory_space=pl.ANY)
     return call(
         order,
-        projection_kernel,
-        (first, last),
-        shapes,
-        "projection_outputs",
-        cost(first.size, 6 * first.size),
+        first_kernel,
+        (value, *earlier),
+        [shaped((width, 3 * width), f32), shaped((width, width), f32)],
+        "first_outputs",
+        cost(value.size, 6 * value.size),
         scalars=(half,),
-        grid=(3,),
-        specs=ins,
-        outs=outs,
-    )
-
-
-def last_outputs(order, half, flag, first, mine, got, width, units, earlier):
-    ins, outs, shapes = projection_specs(width)
-    place = got.shape[0] // SMALL - 1
-    small = pl.BlockSpec((SMALL, LANES), lambda *_: (place, 0))
+        grid=(1,),
+        specs=[resident(value.shape)] + [anywhere] * len(earlier),
+        outs=[anywhere, anywhere],
+        scratch=[
+            pltpu.VMEM((3, tall, width - LANES), f32),
+            pltpu.VMEM((3, tall, LANES), f32),
+            pltpu.SemaphoreType.DMA((2, 3)),
+        ],
+        aliases={2: 0, 3: 1} if earlier else None,
+    )
+
+
+def last_kernel(side_ref, flag_ref, mine_ref, got_ref, *refs):
+    in_ref, *vec_refs, expand_ref, pair_ref, project_ref, columns, sems = refs[1:]
+    tall = columns.shape[2]
+    width = in_ref.shape[1] // 3
+    copies = []
+    for number, ref in enumerate((mine_ref, got_ref)):
+        half = side_ref[0] if number == 0 else 1 - side_ref[0]
+        rows = pl.ds(pl.multiple_of(half * tall, tall), tall)
+        for part in range(3):
+            columns[number, part] = ref[part * tall : (part + 1) * tall, :].astype(f32)
+            there = in_ref.at[rows, pl.ds((part + 1) * width - LANES, LANES)]
+            copy = pltpu.make_async_copy(columns.at[number, part], there, sems.at[number, part])
+            copy.start()
+            copies.append(copy)
+    both = mine_ref[3 * tall :, :].astype(f32) + got_ref[3 * tall :, :].astype(f32)
+    rows = jnp.concatenate([both[at * 32 : (at + 1) * 32] for at in range(width // LANES)], axis=1)
+    own = jnp.where(flag_ref[0] == 1, rows[16:], rows[:16])
+    for number, ref in enumerate(vec_refs):
+        ref[...] = own[number : number + 1]
+    for number in range(expand_ref.shape[1] // width):
+        cols = slice(number * width, (number + 1) * width)
+        expand_ref[:, cols] = own[5 + number : 6 + number]
+    project_ref[...] = rows[9:10]
+    pair_ref[...] = rows[10:12]
+    for copy in copies:
+        copy.wait()
+
+
+def last_outputs(order, side, flag, mine, got, width, units, earlier):
     vecs = [(1, width)] * 5 + [(1, units), (2, width), (1, width)]
+    anywhere = pl.BlockSpec(memory_space=pl.ANY)
     return call(
         order,
         last_kernel,
-        (first, got, mine, got, *earlier),
-        shapes + [shaped(shape, f32) for shape in vecs],
+        (mine, got, earlier),
+        [shaped((width, 3 * width), f32)] + [shaped(shape, f32) for shape in vecs],
         "last_outputs",
         cost(got.size, 6 * got.size),
-        scalars=(half, flag),
-        grid=(3,),
-        specs=ins + [small, small] + [pl.BlockSpec(memory_space=pl.ANY)] * 2,
-        outs=outs + [resident(shape) for shape in vecs],
-        aliases={6: 0, 7: 1},
+        scalars=(side, flag),
+        grid=(1,),
+        specs=[resident(mine.shape), resident(got.shape), anywhere],
+        outs=[anywhere] + [resident(shape) for shape in vecs],
+        scratch=[
+            pltpu.VMEM((2, 3, width // 2, LANES), f32),
+            pltpu.SemaphoreType.DMA((2, 3)),
+        ],
+        aliases={4: 0},
     )
 
 
@@ -922,6 +939,13 @@
     for axis in axes:
         place = place * lax.axis_size(axis) + lax.axis_index(axis)
     return place
+
+
+def late_stages(axes):
+    stages = stage_bits(axes)
+    if len(axes) == 2 and len(stages) == 5:
+        return [stages[0], (0, 0), (2, 3), (3, 2), (4, 4)]
+    return stages
 
 
 def stage_bits(axes):
@@ -939,11 +963,11 @@
 
 
 class Total:
-    def __init__(self, order, axes, keep, send):
+    def __init__(self, order, axes, keep, send, stages=None):
         self.order = order
         self.axes = axes
         self.core = len(axes) - 1
-        self.left = stage_bits(axes)
+        self.left = list(stages or stage_bits(axes))
         place = place_of(axes)
         second = ((place >> self.core) & 1) == 1
         sides = [(place >> jnp.where(second, pair[1], pair[0])) & 1 for pair in self.left]
@@ -960,6 +984,10 @@
     def part(self, which, half):
         cut = lambda term: lax.dynamic_slice_in_dim(term, which * half, half, 0).astype(f32)
         return (cut(self.terms[0]) + cut(self.terms[1])).astype(bf16)
+
+    def finish(self):
+        while self.left or self.back:
+            self.step()
 
     def step(self):
         if self.left:
@@ -1100,24 +1128,24 @@
     a.step()
     grads = backward(1, 2, 2)
     c.step()
+    a.step()
     first_sums, keep, send = weights(2 * LANES, 0, 0, project_out_grad)
     s = Total(order, ("dp", "mod"), keep, send)
     a.step()
     grads = backward(0, 4, 2)
     s.step()
+    c.step()
     a.step()
     grads = backward(1, 4, 2)
     c.step()
     s.step()
     near = image_grads(order, project_in, grads[3], grads[4])
     far = to_image(near)
+    a.step()
     c.step()
-    a.step()
     last_sums, keep, send = weights(LANES, 2, SMALL)
-    p = Total(order, ("dp", "mod"), keep, send)
+    p = Total(order, ("dp", "mod"), keep, send, late_stages(("dp", "mod")))
     s.step()
-    c.step()
-    a.step()
     (far,) = order.after(far)
     order.last = far
     grad_in, keep = finish_rows(
@@ -1136,33 +1164,35 @@
         rows,
     )
     p.terms = (keep, p.got)
-    p.step()
-    s.step()
-    a.step()
-    p.step()
     c.step()
     p.step()
-    s.step()
+    a.step()
+    a.finish()
     outputs = unpack(side, 0, a.mine)
     p.step()
     s.step()
-    p.step()
     outputs = unpack(1 - side, 0, a.got, outputs)
     p.step()
     s.step()
     c.step()
     p.step()
     s.step()
+    c.finish()
     outputs = unpack(side, 2, c.mine, outputs)
     p.step()
     s.step()
     reduce_grad, expand_grad = unpack(1 - side, 2, c.got, outputs)
-    while p.back:
-        p.step()
-    projections = projection_outputs(order, side, s.mine, p.mine, width)
+    p.step()
+    s.step()
+    p.step()
+    s.step()
+    s.finish()
+    projections = first_outputs(order, side, s.mine, width, ())
+    p.step()
+    project_in_grad, project_out_grad = first_outputs(order, 1 - side, s.got, width, projections)
+    p.finish()
     (
         project_in_grad,
-        project_out_grad,
         attend_gain_grad,
         attend_shift_grad,
         feed_gain_grad,
@@ -1171,7 +1201,7 @@
         expand_bias_grad,
         bias_pair_grad,
         project_bias_grad,
-    ) = last_outputs(order, 1 - side, flag, s.got, p.mine, p.got, width, units, projections)
+    ) = last_outputs(order, side, flag, p.mine, p.got, width, units, project_in_grad)
     return (
         hidden_out.reshape(hidden_in.shape),
         grad_in.reshape(hidden_in.shape),
@@ -1180,7 +1210,7 @@
         project_in_grad,
         bias_pair_grad,
         project_out_grad,
-        project_bias_grad[0],
+        project_bias_grad.reshape(-1),
         feed_gain_grad,
         feed_shift_grad,
         expand_grad[None],

time: 319 us -> 335 us (1.050)
  the two profiles are of different devices: /device:TPU:12 before, /device:TPU:0 now
where the time goes in v7:
time: 335 us; the launch traced here: 329 us
  Pallas kernels  190 us (57%)
  starting transfers between devices  60.3 us (18%)
  waiting for transfers between devices  46.7 us (14%)
  other arithmetic  22.2 us (7%)
  local copies, waits for them, and re-layouts  8.62 us (3%)
    pallas_call x23, Pallas kernels, call(): pl.pallas_call(kernel, grid_spec=pltpu.PrefetchScalarGridSpec(num_scalar_...  190 us
    ppermute x36, starting transfers between devices, swap(): lax.ppermute(value, axes, [(source, pair_of(source)) for source in range(...  51.5 us
    ppermute x36, waiting for transfers between devices, swap(): lax.ppermute(value, axes, [(source, pair_of(source)) for source in range(...  46.7 us
    convert_element_type x14, other arithmetic, part(): return (cut(self.terms[0]) + cut(self.terms[1])).astype(bf16)  14.2 us
    ppermute x3, starting transfers between devices, on_device(): to_text = lambda value: lax.ppermute(value, 'mod', [(0, 1)])  7.5 us
    unnamed x40, local copies, waits for them, and re-layouts  6.86 us
  transfers between devices with their start and end apart: 40, of which 19 were waited for; matrix products, arithmetic and copies ran while one was open for 5% of the time, Pallas kernels for 38%

profile of v7, /device:TPU:0, one launch (start us, length us, event | category | flops | bytes accessed | tf_op | source)
XLA Modules:
  0.0 329.1 jit_solution(747182254466714753)
XLA Ops:
  1.8 4.9 %collective-permute-start = (bf16[256,768]{1,0:T(8,128)(2,1)S(1)}, bf16[256,768]{1,0:T(8,128)(2,1)S(1)}, u32[]{:S(2)}, u32[]{:S(2)}) collective-permute-start(bf16[256,768]{1,0:T(8,128)(2,1)S(1)} %get-tuple-element.377), channel_id=1, source_target_pairs={{0,1},{2,3},{4,5},{6,7},{8,9},{10,11},{12,13},{14,15},{16,17},{18,... | collective-permute-start | bytes 1179656 | tf_op jit(solution)/shard_map/ppermute | solution.py:1039
  9.4 8.5 %project_rows.1 = (bf16[1024,768]{1,0:T(8,128)(2,1)}, bf16[1024,2304]{1,0:T(8,128)(2,1)}) custom-call(bf16[1024,768]{1,0:T(8,128)(2,1)} %bitcast.20, f32[1,768]{1,0:T(1,128)} %gain_ref.9, f32[1,768]{1,0:T(1,128)} %shift_ref.6, bf16[768,2304]{1,0:T(8,128)(2,1)} %weight_ref.3, f32[2,768]{1,0:T(2,128)} %bias_ref.5), custom_call_target="tpu_custom_call" | custom-call | flops 3623878656 | bytes 11403264 | tf_op jit(solution)/shard_map/project_rows/pallas_call | solution.py:83
  19.2 3.9 %image_rows.2 = (bf16[512,768]{1,0:T(8,128)(2,1)}, bf16[512,1536]{1,0:T(8,128)(2,1)}) custom-call(s32[1]{0:T(128)} %bitcast.flag_ref, bf16[1024,768]{1,0:T(8,128)(2,1)} %bitcast.21, bf16[256,768]{1,0:T(8,128)(2,1)} %copy-done.14, f32[1,768]{1,0:T(1,128)} %gain_ref.9, f32[1,768]{1,0:T(1,128)} %shift_ref.6, f32[2,768]{1,0:T(2,128)} %copy-done.17, ...), custom_call_target="tpu_custom_call" | custom-call | flops 603979776 | bytes 6291456 | tf_op jit(solution)/shard_map/image_rows/pallas_call | solution.py:83
  23.1 12.3 %attend_forward.2 = (bf16[512,768]{1,0:T(8,128)(2,1)}, f32[6,2,512]{2,1,0:T(2,128)}) custom-call(s32[1]{0:T(128)} %bitcast.flag_ref, s32[2]{0:T(128)} %count_ref.17, s32[2,4]{1,0:T(2,128)} %lengths_ref.15, bf16[1024,2304]{1,0:T(8,128)(2,1)} %get-tuple-element.248.q_ref.k_ref.v_ref, bf16[1024,2304]{1,0:T(8,128)(2,1)} %get-tuple-element.248.q_ref.k_ref.v_ref, ...), custom_call_target="tpu_custom_call" | custom-call | flops 4831838208 | bytes 6291456 | tf_op jit(solution)/shard_map/attend_forward/pallas_call | solution.py:83
  36.1 3.8 %image_rows.3 = (bf16[512,768]{1,0:T(8,128)(2,1)}, bf16[512,1536]{1,0:T(8,128)(2,1)}) custom-call(s32[1]{0:T(128)} %bitcast.flag_ref, bf16[1024,768]{1,0:T(8,128)(2,1)} %bitcast.22, bf16[256,768]{1,0:T(8,128)(2,1)} %copy-done.13, f32[1,768]{1,0:T(1,128)} %gain_ref.9, f32[1,768]{1,0:T(1,128)} %shift_ref.6, ...), custom_call_target="tpu_custom_call", output_to_operand_aliasing={{0}: (9, {}), {1}: (10, {})} | custom-call | flops 603979776 | bytes 6291456 | tf_op jit(solution)/shard_map/image_rows/pallas_call | solution.py:83
  40.0 12.3 %attend_forward.3 = (bf16[512,768]{1,0:T(8,128)(2,1)}, f32[6,2,512]{2,1,0:T(2,128)}) custom-call(s32[1]{0:T(128)} %bitcast.flag_ref, s32[2]{0:T(128)} %count_ref.17, s32[2,4]{1,0:T(2,128)} %lengths_ref.15, bf16[1024,2304]{1,0:T(8,128)(2,1)} %get-tuple-element.248.q_ref.k_ref.v_ref, bf16[1024,2304]{1,0:T(8,128)(2,1)} %get-tuple-element.248.q_ref.k_ref.v_ref, ...), custom_call_target="tpu_custom_call" | custom-call | flops 4831838208 | bytes 6291456 | tf_op jit(solution)/shard_map/attend_forward/pallas_call | solution.py:83
  52.2 45.2 %feed_forward.1 = (bf16[1024,768]{1,0:T(8,128)(2,1)}, f32[1024,768]{1,0:T(8,128)}, bf16[1024,768]{1,0:T(8,128)(2,1)}, bf16[768,768]{1,0:T(8,128)(2,1)}, f32[8,76...) custom-call(s32[1]{0:T(128)} %bitcast.flag_ref, ...), custom_call_target="tpu_custom_call" | custom-call | flops 28991029248 | bytes 41943040 | tf_op jit(solution)/shard_map/feed_forward/pallas_call | solution.py:83
  98.0 8.2 %attend_backward.6 = (bf16[1024,768]{1,0:T(8,128)(2,1)}, bf16[1024,768]{1,0:T(8,128)(2,1)}, bf16[1024,768]{1,0:T(8,128)(2,1)}, bf16[512,768]{1,0:T(8,128)(2,1)}, bf16[512,768]{1,0:T(8,128)(2,1)}) custom-call(s32[1]{0:T(128)} %bitcast.flag_ref, s32[2]{0:T(128)} %count_ref.17, s32[2,4]{1,0:T(2,128)} %lengths_ref.15, ...), custom_call_target="tpu_custom_call" | custom-call | flops 40265318400 | bytes 41943040 | tf_op jit(solution)/shard_map/attend_backward/pallas_call | solution.py:83
  107.7 3.2 add_convert_fusion.2
  112.4 8.3 %attend_backward.7 = (bf16[1024,768]{1,0:T(8,128)(2,1)}, bf16[1024,768]{1,0:T(8,128)(2,1)}, bf16[1024,768]{1,0:T(8,128)(2,1)}, bf16[512,768]{1,0:T(8,128)(2,1)}, bf16[512,768]{1,0:T(8,128)(2,1)}) custom-call(s32[1]{0:T(128)} %bitcast.flag_ref, s32[2]{0:T(128)} %count_ref.17, ...), custom_call_target="tpu_custom_call", output_to_operand_aliasing={{0}: (11, {}), {1}: (12, {}), {2}: (13, {}), {3}: (14, {}),... | custom-call | flops 40265318400 | bytes 41943040 | tf_op jit(solution)/shard_map/attend_backward/pallas_call | solution.py:83
  122.8 8.1 %attend_backward.8 = (bf16[1024,768]{1,0:T(8,128)(2,1)}, bf16[1024,768]{1,0:T(8,128)(2,1)}, bf16[1024,768]{1,0:T(8,128)(2,1)}, bf16[512,768]{1,0:T(8,128)(2,1)}, bf16[512,768]{1,0:T(8,128)(2,1)}) custom-call(s32[1]{0:T(128)} %bitcast.flag_ref, s32[2]{0:T(128)} %count_ref.17, ...), custom_call_target="tpu_custom_call", output_to_operand_aliasing={{0}: (11, {}), {1}: (12, {}), {2}: (13, {}), {3}: (14, {}),... | custom-call | flops 40265318400 | bytes 41943040 | tf_op jit(solution)/shard_map/attend_backward/pallas_call | solution.py:83
  132.5 2.6 collective-permute-start.6
  135.1 8.3 %attend_backward.9 = (bf16[1024,768]{1,0:T(8,128)(2,1)}, bf16[1024,768]{1,0:T(8,128)(2,1)}, bf16[1024,768]{1,0:T(8,128)(2,1)}, bf16[512,768]{1,0:T(8,128)(2,1)}, bf16[512,768]{1,0:T(8,128)(2,1)}) custom-call(s32[1]{0:T(128)} %bitcast.flag_ref, s32[2]{0:T(128)} %count_ref.17, ...), custom_call_target="tpu_custom_call", output_to_operand_aliasing={{0}: (11, {}), {1}: (12, {}), {2}: (13, {}), {3}: (14, {}),... | custom-call | flops 40265318400 | bytes 41943040 | tf_op jit(solution)/shard_map/attend_backward/pallas_call | solution.py:83
  143.4 1.8 collective-permute-done.7
  146.3 2.6 collective-permute-start.11
  150.7 9.3 %weight_grads.2 = (f32[2,512]{1,0:T(2,128)}, bf16[3456,256]{1,0:T(8,128)(2,1)}, bf16[3456,256]{1,0:T(8,128)(2,1)}) custom-call(s32[1]{0:T(128)} %bitcast.1.side_ref.half_ref, bf16[1024,768]{1,0:T(8,128)(2,1)} %get-tuple-element.264.normed_ref, bf16[512,768]{1,0:T(8,128)(2,1)} %get-tuple-element.230.image_ref, ...), custom_call_target="tpu_custom_call" | custom-call | flops 32212254720 | bytes 125829120 | tf_op jit(solution)/shard_map/weight_grads/pallas_call | solution.py:83
  161.8 2.5 collective-permute-start.13
  164.3 8.1 %attend_backward.10 = (bf16[1024,768]{1,0:T(8,128)(2,1)}, bf16[1024,768]{1,0:T(8,128)(2,1)}, bf16[1024,768]{1,0:T(8,128)(2,1)}, bf16[512,768]{1,0:T(8,128)(2,1)}, bf16[512,768]{1,0:T(8,128)(2,1)}) custom-call(s32[1]{0:T(128)} %bitcast.flag_ref, s32[2]{0:T(128)} %count_ref.17, ...), custom_call_target="tpu_custom_call", output_to_operand_aliasing={{0}: (11, {}), {1}: (12, {}), {2}: (13, {}), {3}: (14, {}),... | custom-call | flops 40265318400 | bytes 41943040 | tf_op jit(solution)/shard_map/attend_backward/pallas_call | solution.py:83
  174.0 3.2 collective-permute-start.17
  177.3 8.3 %attend_backward.11 = (bf16[1024,768]{1,0:T(8,128)(2,1)}, bf16[1024,768]{1,0:T(8,128)(2,1)}, bf16[1024,768]{1,0:T(8,128)(2,1)}, bf16[512,768]{1,0:T(8,128)(2,1)}, bf16[512,768]{1,0:T(8,128)(2,1)}) custom-call(s32[1]{0:T(128)} %bitcast.flag_ref, s32[2]{0:T(128)} %count_ref.17, ...), custom_call_target="tpu_custom_call", output_to_operand_aliasing={{0}: (11, {}), {1}: (12, {}), {2}: (13, {}), {3}: (14, {}),... | custom-call | flops 40265318400 | bytes 41943040 | tf_op jit(solution)/shard_map/attend_backward/pallas_call | solution.py:83
  187.8 4.4 %image_grads.1.near_ref = bf16[512,768]{1,0:T(8,128)(2,1)} custom-call(bf16[768,2304]{1,0:T(8,128)(2,1)} %weight_ref.3, bf16[768,2304]{1,0:T(8,128)(2,1)} %weight_ref.3, bf16[512,768]{1,0:T(8,128)(2,1)} %get-tuple-element.259.keys_ref.gik_ref, bf16[512,768]{1,0:T(8,128)(2,1)} %get-tuple-element.253.values_ref.giv_ref), custom_call_target="tpu_custom_call" | custom-call | flops 12079595520 | bytes 62914560 | tf_op jit(solution)/shard_map/image_grads/pallas_call | solution.py:83
  193.4 4.5 %collective-permute-done.17 = bf16[1152,256]{1,0:T(8,128)(2,1)S(1)} collective-permute-done((bf16[1152,256]{1,0:T(8,128)(2,1)S(1)}, bf16[1152,256]{1,0:T(8,128)(2,1)S(1)}, u32[]{:S(2)}, u32[]{:S(2)}) %collective-permute-start.17) | collective-permute-done | bytes 589856 | tf_op jit(solution)/shard_map/ppermute | solution.py:934
  198.1 2.3 collective-permute-done.16
  202.1 6.0 %weight_grads.3 = (f32[2,256]{1,0:T(2,128)}, bf16[1280,256]{1,0:T(8,128)(2,1)}, bf16[1280,256]{1,0:T(8,128)(2,1)}) custom-call(s32[1]{0:T(128)} %bitcast.1.side_ref.half_ref, bf16[1024,768]{1,0:T(8,128)(2,1)} %get-tuple-element.264.normed_ref, bf16[512,768]{1,0:T(8,128)(2,1)} %get-tuple-element.230.image_ref, bf16[1024,768]{1,0:T(8,128)(2,1)} %get-tuple-element.265.gq_ref, ...), custom_call_target="tpu_custom_call" | custom-call | flops 16106127360 | bytes 125829120 | tf_op jit(solution)/shard_map/weight_grads/pallas_call | solution.py:83
  208.1 9.7 %collective-permute-start.18 = (bf16[1280,256]{1,0:T(8,128)(2,1)}, bf16[1280,256]{1,0:T(8,128)(2,1)S(1)}, u32[]{:S(2)}, u32[]{:S(2)}) collective-permute-start(bf16[1280,256]{1,0:T(8,128)(2,1)} %get-tuple-element.268), channel_id=1, source_target_pairs={{0,2},{1,3},{2,0},{3,1},{4,6},{5,7},{6,4},{7,5},{8,10},{9,11},{10,... | collective-permute-start | bytes 1966088 | tf_op jit(solution)/shard_map/ppermute | solution.py:934
  219.6 10.2 %finish_rows.1 = (bf16[1024,768]{1,0:T(8,128)(2,1)}, bf16[1280,256]{1,0:T(8,128)(2,1)}) custom-call(s32[1]{0:T(128)} %bitcast.flag_ref, bf16[1024,768]{1,0:T(8,128)(2,1)} %bitcast.24, f32[1024,768]{1,0:T(8,128)} %get-tuple-element.273.gmid_ref, bf16[512,768]{1,0:T(8,128)(2,1)} %image_grads.1.near_ref, ...), custom_call_target="tpu_custom_call", output_to_operand_aliasing={{1}: (13, {})} | custom-call | flops 36238786560 | bytes 167772160 | tf_op jit(solution)/shard_map/finish_rows/pallas_call | solution.py:83
  233.7 1.8 collective-permute-start.24
  235.5 3.6 %expert_outputs.4 = (f32[3072,768]{1,0:T(8,128)}, f32[768,3072]{1,0:T(8,128)}) custom-call(s32[1]{0:T(128)} %bitcast.1.side_ref.half_ref, bf16[4608,256]{1,0:T(8,128)(2,1)} %copy-done.1), custom_call_target="tpu_custom_call" | custom-call | flops 1179648 | bytes 7077888 | tf_op jit(solution)/shard_map/expert_outputs/pallas_call | solution.py:83
  239.2 4.4 %collective-permute-done.20 = bf16[640,256]{1,0:T(8,128)(2,1)} collective-permute-done((bf16[640,256]{1,0:T(8,128)(2,1)}, bf16[640,256]{1,0:T(8,128)(2,1)}, u32[]{:S(2)}, u32[]{:S(2)}) %collective-permute-start.20) | collective-permute-done | bytes 327712 | tf_op jit(solution)/shard_map/ppermute | solution.py:934
  243.6 1.8 add_convert_fusion.22
  245.4 1.7 collective-permute-start.22
  249.7 3.6 %expert_outputs.5 = (f32[3072,768]{1,0:T(8,128)}, f32[768,3072]{1,0:T(8,128)}) custom-call(s32[1]{0:T(128)S(6)} %sub.47.half_ref, bf16[4608,256]{1,0:T(8,128)(2,1)} %collective-permute-done.23.value_ref, f32[3072,768]{1,0:T(8,128)} %get-tuple-element.293.refs_0_, f32[768,3072]{1,0:T(8,128)} %get-tuple-element.287.refs_1_), custom_call_target="tpu_custom_call", output_to_operand_aliasing={{0}: (2, {}), {1}: (3, {})} | custom-call | flops 1179648 | bytes 7077888 | tf_op jit(solution)/shard_map/expert_outputs/pallas_call | solution.py:83
  256.8 7.8 %collective-permute-start.31 = (bf16[4608,256]{1,0:T(8,128)(2,1)S(1)}, bf16[4608,256]{1,0:T(8,128)(2,1)}, u32[]{:S(2)}, u32[]{:S(2)}) collective-permute-start(bf16[4608,256]{1,0:T(8,128)(2,1)S(1)} %pad_maximum_fusion.1.value_ref), channel_id=1, source_target_pairs={{0,2},{2,0},{4,6},{6,4},{8,10},{10,8},{12,14},{14,12},{16,18},{18,... | collective-permute-start | bytes 7077896 | tf_op jit(solution)/shard_map/ppermute | solution.py:934
  264.6 1.8 collective-permute-start.29
  266.3 3.1 collective-permute-done.25
  270.3 3.4 %collective-permute-done.29 = bf16[216,256]{1,0:T(8,128)(2,1)S(1)} collective-permute-done((bf16[216,256]{1,0:T(8,128)(2,1)S(1)}, bf16[216,256]{1,0:T(8,128)(2,1)S(1)}, u32[]{:S(2)}, u32[]{:S(2)}) %collective-permute-start.29) | collective-permute-done | bytes 110624 | tf_op jit(solution)/shard_map/ppermute | solution.py:934
  273.8 3.6 %expert_outputs.6 = (f32[3072,768]{1,0:T(8,128)}, f32[768,3072]{1,0:T(8,128)}) custom-call(s32[1]{0:T(128)} %bitcast.1.side_ref.half_ref, bf16[4608,256]{1,0:T(8,128)(2,1)} %copy-done, f32[3072,768]{1,0:T(8,128)} %get-tuple-element.306.refs_0_, f32[768,3072]{1,0:T(8,128)} %get-tuple-element.294.refs_1_), custom_call_target="tpu_custom_call", output_to_operand_aliasing={{0}: (2, {}), {1}: (3, {})} | custom-call | flops 1179648 | bytes 7077888 | tf_op jit(solution)/shard_map/expert_outputs/pallas_call | solution.py:83
  277.4 3.4 %collective-permute-done.32 = bf16[432,256]{1,0:T(8,128)(2,1)S(1)} collective-permute-done((bf16[432,256]{1,0:T(8,128)(2,1)S(1)}, bf16[432,256]{1,0:T(8,128)(2,1)S(1)}, u32[]{:S(2)}, u32[]{:S(2)}) %collective-permute-start.32) | collective-permute-done | bytes 221216 | tf_op jit(solution)/shard_map/ppermute | solution.py:934
  280.8 2.0 collective-permute-start.34
  283.0 3.6 %expert_outputs.7 = (f32[3072,768]{1,0:T(8,128)}, f32[768,3072]{1,0:T(8,128)}) custom-call(s32[1]{0:T(128)S(6)} %sub.47.half_ref, bf16[4608,256]{1,0:T(8,128)(2,1)} %collective-permute-done.31.value_ref, f32[3072,768]{1,0:T(8,128)} %get-tuple-element.313.refs_0_, f32[768,3072]{1,0:T(8,128)} %get-tuple-element.307.refs_1_), custom_call_target="tpu_custom_call", output_to_operand_aliasing={{0}: (2, {}), {1}: (3, {})} | custom-call | flops 1179648 | bytes 7077888 | tf_op jit(solution)/shard_map/expert_outputs/pallas_call | solution.py:83
  290.7 4.2 %collective-permute-done.33 = bf16[160,256]{1,0:T(8,128)(2,1)S(1)} collective-permute-done((bf16[160,256]{1,0:T(8,128)(2,1)S(1)}, bf16[160,256]{1,0:T(8,128)(2,1)S(1)}, u32[]{:S(2)}, u32[]{:S(2)}) %collective-permute-start.33) | collective-permute-done | bytes 81952 | tf_op jit(solution)/shard_map/ppermute | solution.py:934
  295.5 7.0 %collective-permute-done.36 = bf16[1728,256]{1,0:T(8,128)(2,1)S(1)} collective-permute-done((bf16[1728,256]{1,0:T(8,128)(2,1)S(1)}, bf16[1728,256]{1,0:T(8,128)(2,1)S(1)}, u32[]{:S(2)}, u32[]{:S(2)}) %collective-permute-start.36) | collective-permute-done | bytes 884768 | tf_op jit(solution)/shard_map/ppermute | solution.py:934
  302.8 2.0 collective-permute-start.35
  304.8 3.4 %first_outputs.2 = (f32[768,2304]{1,0:T(8,128)}, f32[768,768]{1,0:T(8,128)}) custom-call(s32[1]{0:T(128)} %bitcast.1.side_ref.half_ref, bf16[3456,256]{1,0:T(8,128)(2,1)} %copy-done.2), custom_call_target="tpu_custom_call" | custom-call | flops 884736 | bytes 5308416 | tf_op jit(solution)/shard_map/first_outputs/pallas_call | solution.py:83
  312.4 3.4 %first_outputs.3 = (f32[768,2304]{1,0:T(8,128)}, f32[768,768]{1,0:T(8,128)}) custom-call(s32[1]{0:T(128)S(6)} %sub.47.half_ref, bf16[3456,256]{1,0:T(8,128)(2,1)} %copy-done.8, f32[768,2304]{1,0:T(8,128)} %get-tuple-element.328.refs_0_, f32[768,768]{1,0:T(8,128)} %get-tuple-element.324.refs_1_), custom_call_target="tpu_custom_call", output_to_operand_aliasing={{0}: (2, {}), {1}: (3, {})} | custom-call | flops 884736 | bytes 5308416 | tf_op jit(solution)/shard_map/first_outputs/pallas_call | solution.py:83
  315.8 4.0 %collective-permute-done.37 = bf16[640,256]{1,0:T(8,128)(2,1)} collective-permute-done((bf16[640,256]{1,0:T(8,128)(2,1)}, bf16[640,256]{1,0:T(8,128)(2,1)}, u32[]{:S(2)}, u32[]{:S(2)}) %collective-permute-start.37) | collective-permute-done | bytes 327712 | tf_op jit(solution)/shard_map/ppermute | solution.py:934
  321.0 2.1 collective-permute-done.39.got_ref
  324.0 3.4 %last_outputs.1 = (f32[768,2304]{1,0:T(8,128)}, f32[1,768]{1,0:T(1,128)}, f32[1,768]{1,0:T(1,128)}, f32[1,768]{1,0:T(1,128)}, f32[1,768]{1,0:T(1,128)}, /*index=...) custom-call(s32[1]{0:T(128)} %bitcast.1.side_ref.half_ref, ...), custom_call_target="tpu_custom_call", output_to_operand_aliasing={{0}: (4, {})} | custom-call | flops 327680 | bytes 1966080 | tf_op jit(solution)/shard_map/last_outputs/pallas_call | solution.py:83
  (145 shorter events, 50.1 us)
Async XLA Ops:
  0.6 6.1 %copy-start.16 = (f32[1,768]{1,0:T(1,128)S(1)}, f32[1,768]{1,0:T(1,128)}, u32[]{:S(2)}) copy-start(f32[1,768]{1,0:T(1,128)} %gain_ref.9) | copy-start | bytes 9220
  0.7 6.1 %copy-start.15 = (f32[1,768]{1,0:T(1,128)S(1)}, f32[1,768]{1,0:T(1,128)}, u32[]{:S(2)}) copy-start(f32[1,768]{1,0:T(1,128)} %shift_ref.6) | copy-start | bytes 9220
  1.8 16.6 %collective-permute-start = (bf16[256,768]{1,0:T(8,128)(2,1)S(1)}, bf16[256,768]{1,0:T(8,128)(2,1)S(1)}, u32[]{:S(2)}, u32[]{:S(2)}) collective-permute-start(bf16[256,768]{1,0:T(8,128)(2,1)S(1)} %get-tuple-element.377), channel_id=1, source_target_pairs={{0,1},{2,3},{4,5},{6,7},{8,9},{10,11},{12,13},{14,15},{16,17},{18,... | collective-permute-start | bytes 1179656 | tf_op jit(solution)/shard_map/ppermute | solution.py:1039
  6.8 11.7 %collective-permute-start.1 = (f32[2,768]{1,0:T(2,128)S(1)}, f32[2,768]{1,0:T(2,128)S(1)}, u32[]{:S(2)}, u32[]{:S(2)}) collective-permute-start(f32[2,768]{1,0:T(2,128)S(1)} %pad_maximum_fusion.14), channel_id=1, source_target_pairs={{0,1},{2,3},{4,5},{6,7},{8,9},{10,11},{12,13},{14,15},{16,17},{18,... | collective-permute-start | bytes 18440 | tf_op jit(solution)/shard_map/ppermute | solution.py:1039
  8.1 27.3 %collective-permute-start.2 = (bf16[256,768]{1,0:T(8,128)(2,1)S(1)}, bf16[256,768]{1,0:T(8,128)(2,1)S(1)}, u32[]{:S(2)}, u32[]{:S(2)}) collective-permute-start(bf16[256,768]{1,0:T(8,128)(2,1)S(1)} %get-tuple-element.376), channel_id=1, source_target_pairs={{0,1},{2,3},{4,5},{6,7},{8,9},{10,11},{12,13},{14,15},{16,17},{18,... | collective-permute-start | bytes 1179656 | tf_op jit(solution)/shard_map/ppermute | solution.py:1039
  9.4 8.5 %copy-start.18 = (f32[768]{0:T(1024)S(1)}, f32[768]{0:T(1024)}, u32[]{:S(2)}) copy-start(f32[768]{0:T(1024)} %param.24) | copy-start | bytes 9220
  97.5 23.3 %collective-permute-start.5 = (bf16[4608,256]{1,0:T(8,128)(2,1)}, bf16[4608,256]{1,0:T(8,128)(2,1)S(1)}, u32[]{:S(2)}, u32[]{:S(2)}) collective-permute-start(bf16[4608,256]{1,0:T(8,128)(2,1)} %get-tuple-element.196), channel_id=1, source_target_pairs={{0,2},{2,0},{4,6},{6,4},{8,10},{10,8},{12,14},{14,12},{16,18},{18,... | collective-permute-start | bytes 7077896 | tf_op jit(solution)/shard_map/ppermute | solution.py:934
  97.5 8.7 %collective-permute-start.3 = (bf16[4608,256]{1,0:T(8,128)(2,1)}, bf16[4608,256]{1,0:T(8,128)(2,1)S(1)}, u32[]{:S(2)}, u32[]{:S(2)}) collective-permute-start(bf16[4608,256]{1,0:T(8,128)(2,1)} %get-tuple-element.195), channel_id=1, source_target_pairs={{0,2},{2,0},{4,6},{6,4},{8,10},{10,8},{12,14},{14,12},{16,18},{18,... | collective-permute-start | bytes 7077896 | tf_op jit(solution)/shard_map/ppermute | solution.py:934
  98.0 9.6 %copy-start.5 = (bf16[4608,256]{1,0:T(8,128)(2,1)S(1)}, bf16[4608,256]{1,0:T(8,128)(2,1)}, u32[]{:S(2)}) copy-start(bf16[4608,256]{1,0:T(8,128)(2,1)} %get-tuple-element.200) | copy-start | bytes 7077892
  110.9 20.0 %collective-permute-start.4 = (bf16[2304,256]{1,0:T(8,128)(2,1)}, bf16[2304,256]{1,0:T(8,128)(2,1)}, u32[]{:S(2)}, u32[]{:S(2)}) collective-permute-start(bf16[2304,256]{1,0:T(8,128)(2,1)} %get-tuple-element.360), channel_id=1, source_target_pairs={{0,4},{2,10},{4,0},{6,14},{8,12},{10,2},{12,8},{14,6},{16,20},{18,... | collective-permute-start | bytes 3538952 | tf_op jit(solution)/shard_map/ppermute | solution.py:934
  112.4 8.3 %copy-start.4 = (bf16[4608,256]{1,0:T(8,128)(2,1)S(1)}, bf16[4608,256]{1,0:T(8,128)(2,1)}, u32[]{:S(2)}) copy-start(bf16[4608,256]{1,0:T(8,128)(2,1)} %get-tuple-element.209) | copy-start | bytes 7077892
  122.3 22.9 %collective-permute-start.7 = (bf16[2304,256]{1,0:T(8,128)(2,1)}, bf16[2304,256]{1,0:T(8,128)(2,1)S(1)}, u32[]{:S(2)}, u32[]{:S(2)}) collective-permute-start(bf16[2304,256]{1,0:T(8,128)(2,1)} %get-tuple-element.359), channel_id=1, source_target_pairs={{0,4},{2,10},{4,0},{6,14},{8,12},{10,2},{12,8},{14,6},{16,20},{18,... | collective-permute-start | bytes 3538952 | tf_op jit(solution)/shard_map/ppermute | solution.py:934
  132.5 17.2 %collective-permute-start.6 = (bf16[1152,256]{1,0:T(8,128)(2,1)S(1)}, bf16[1152,256]{1,0:T(8,128)(2,1)S(1)}, u32[]{:S(2)}, u32[]{:S(2)}) collective-permute-start(bf16[1152,256]{1,0:T(8,128)(2,1)S(1)} %get-tuple-element.370), channel_id=1, source_target_pairs={{0,16},{2,6},{4,20},{6,2},{8,24},{10,14},{12,28},{14,10},{16,0},{1... | collective-permute-start | bytes 1769480 | tf_op jit(solution)/shard_map/ppermute | solution.py:934
  146.3 27.0 %collective-permute-start.11 = (bf16[1152,256]{1,0:T(8,128)(2,1)}, bf16[1152,256]{1,0:T(8,128)(2,1)S(1)}, u32[]{:S(2)}, u32[]{:S(2)}) collective-permute-start(bf16[1152,256]{1,0:T(8,128)(2,1)} %get-tuple-element.369), channel_id=1, source_target_pairs={{0,16},{2,6},{4,20},{6,2},{8,24},{10,14},{12,28},{14,10},{16,0},{1... | collective-permute-start | bytes 1769480 | tf_op jit(solution)/shard_map/ppermute | solution.py:934
  149.8 11.9 %collective-permute-start.9 = (bf16[576,256]{1,0:T(8,128)(2,1)S(1)}, bf16[576,256]{1,0:T(8,128)(2,1)S(1)}, u32[]{:S(2)}, u32[]{:S(2)}) collective-permute-start(bf16[576,256]{1,0:T(8,128)(2,1)S(1)} %get-tuple-element.387), channel_id=1, source_target_pairs={{0,8},{2,18},{4,12},{6,22},{8,0},{10,26},{12,4},{14,30},{16,24},{1... | collective-permute-start | bytes 884744 | tf_op jit(solution)/shard_map/ppermute | solution.py:934
  160.1 12.4 %collective-permute-start.8 = (bf16[3456,256]{1,0:T(8,128)(2,1)}, bf16[3456,256]{1,0:T(8,128)(2,1)S(1)}, u32[]{:S(2)}, u32[]{:S(2)}) collective-permute-start(bf16[3456,256]{1,0:T(8,128)(2,1)} %get-tuple-element.237), channel_id=1, source_target_pairs={{0,2},{1,3},{2,0},{3,1},{4,6},{5,7},{6,4},{7,5},{8,10},{9,11},{10,... | collective-permute-start | bytes 5308424 | tf_op jit(solution)/shard_map/ppermute | solution.py:934
  161.8 10.6 %copy-start.7 = (bf16[3456,256]{1,0:T(8,128)(2,1)S(1)}, bf16[3456,256]{1,0:T(8,128)(2,1)}, u32[]{:S(2)}) copy-start(bf16[3456,256]{1,0:T(8,128)(2,1)} %get-tuple-element.242) | copy-start | bytes 5308420
  161.8 12.1 %collective-permute-start.13 = (bf16[576,256]{1,0:T(8,128)(2,1)S(1)}, bf16[576,256]{1,0:T(8,128)(2,1)S(1)}, u32[]{:S(2)}, u32[]{:S(2)}) collective-permute-start(bf16[576,256]{1,0:T(8,128)(2,1)S(1)} %add_convert_fusion.17), channel_id=1, source_target_pairs={{0,8},{2,18},{4,12},{6,22},{8,0},{10,26},{12,4},{14,30},{16,24},{1... | collective-permute-start | bytes 884744 | tf_op jit(solution)/shard_map/ppermute | solution.py:934
  172.9 13.1 %collective-permute-start.10 = (bf16[1728,256]{1,0:T(8,128)(2,1)S(1)}, bf16[1728,256]{1,0:T(8,128)(2,1)S(1)}, u32[]{:S(2)}, u32[]{:S(2)}) collective-permute-start(bf16[1728,256]{1,0:T(8,128)(2,1)S(1)} %get-tuple-element.362), channel_id=1, source_target_pairs={{0,1},{1,0},{2,6},{3,7},{4,5},{5,4},{6,2},{7,3},{8,9},{9,8},{10,14... | collective-permute-start | bytes 2654216 | tf_op jit(solution)/shard_map/ppermute | solution.py:934
  173.4 12.2 %collective-permute-start.12 = (bf16[576,256]{1,0:T(8,128)(2,1)S(1)}, bf16[576,256]{1,0:T(8,128)(2,1)S(1)}, u32[]{:S(2)}, u32[]{:S(2)}) collective-permute-start(bf16[576,256]{1,0:T(8,128)(2,1)S(1)} %get-tuple-element.384), channel_id=1, source_target_pairs={{0,8},{2,18},{4,12},{6,22},{8,0},{10,26},{12,4},{14,30},{16,24},{1... | collective-permute-start | bytes 884744 | tf_op jit(solution)/shard_map/ppermute | solution.py:934
  174.0 23.9 %collective-permute-start.17 = (bf16[1152,256]{1,0:T(8,128)(2,1)S(1)}, bf16[1152,256]{1,0:T(8,128)(2,1)S(1)}, u32[]{:S(2)}, u32[]{:S(2)}) collective-permute-start(bf16[1152,256]{1,0:T(8,128)(2,1)S(1)} %pad_maximum_fusion.7), channel_id=1, source_target_pairs={{0,16},{2,6},{4,20},{6,2},{8,24},{10,14},{12,28},{14,10},{16,0},{1... | collective-permute-start | bytes 1769480 | tf_op jit(solution)/shard_map/ppermute | solution.py:934
  185.7 14.7 %collective-permute-start.16 = (bf16[576,256]{1,0:T(8,128)(2,1)S(1)}, bf16[576,256]{1,0:T(8,128)(2,1)S(1)}, u32[]{:S(2)}, u32[]{:S(2)}) collective-permute-start(bf16[576,256]{1,0:T(8,128)(2,1)S(1)} %add_convert_fusion.14), channel_id=1, source_target_pairs={{0,8},{2,18},{4,12},{6,22},{8,0},{10,26},{12,4},{14,30},{16,24},{1... | collective-permute-start | bytes 884744 | tf_op jit(solution)/shard_map/ppermute | solution.py:934
  186.2 31.6 %collective-permute-start.15 = (bf16[864,256]{1,0:T(8,128)(2,1)S(1)}, bf16[864,256]{1,0:T(8,128)(2,1)S(1)}, u32[]{:S(2)}, u32[]{:S(2)}) collective-permute-start(bf16[864,256]{1,0:T(8,128)(2,1)S(1)} %get-tuple-element.375), channel_id=1, source_target_pairs={{0,4},{1,5},{2,3},{3,2},{4,0},{5,1},{6,7},{7,6},{8,12},{9,13},{10,... | collective-permute-start | bytes 1327112 | tf_op jit(solution)/shard_map/ppermute | solution.py:934
  192.1 26.5 %collective-permute-start.14 = (bf16[512,768]{1,0:T(8,128)(2,1)}, bf16[512,768]{1,0:T(8,128)(2,1)S(1)}, u32[]{:S(2)}, u32[]{:S(2)}) collective-permute-start(bf16[512,768]{1,0:T(8,128)(2,1)} %image_grads.1.near_ref), channel_id=1, source_target_pairs={{1,0},{3,2},{5,4},{7,6},{9,8},{11,10},{13,12},{15,14},{17,16},{19,... | collective-permute-start | bytes 2359304 | tf_op jit(solution)/shard_map/ppermute | solution.py:1040
  200.5 29.2 %collective-permute-start.19 = (bf16[1152,256]{1,0:T(8,128)(2,1)S(1)}, bf16[1152,256]{1,0:T(8,128)(2,1)S(1)}, u32[]{:S(2)}, u32[]{:S(2)}) collective-permute-start(bf16[1152,256]{1,0:T(8,128)(2,1)S(1)} %pad_maximum_fusion.8), channel_id=1, source_target_pairs={{0,16},{2,6},{4,20},{6,2},{8,24},{10,14},{12,28},{14,10},{16,0},{1... | collective-permute-start | bytes 1769480 | tf_op jit(solution)/shard_map/ppermute | solution.py:934
  200.6 31.4 %collective-permute-start.21 = (bf16[2304,256]{1,0:T(8,128)(2,1)S(1)}, bf16[2304,256]{1,0:T(8,128)(2,1)S(1)}, u32[]{:S(2)}, u32[]{:S(2)}) collective-permute-start(bf16[2304,256]{1,0:T(8,128)(2,1)S(1)} %pad_maximum_fusion.3), channel_id=1, source_target_pairs={{0,4},{2,10},{4,0},{6,14},{8,12},{10,2},{12,8},{14,6},{16,20},{18,... | collective-permute-start | bytes 3538952 | tf_op jit(solution)/shard_map/ppermute | solution.py:934
  208.1 21.8 %collective-permute-start.18 = (bf16[1280,256]{1,0:T(8,128)(2,1)}, bf16[1280,256]{1,0:T(8,128)(2,1)S(1)}, u32[]{:S(2)}, u32[]{:S(2)}) collective-permute-start(bf16[1280,256]{1,0:T(8,128)(2,1)} %get-tuple-element.268), channel_id=1, source_target_pairs={{0,2},{1,3},{2,0},{3,1},{4,6},{5,7},{6,4},{7,5},{8,10},{9,11},{10,... | collective-permute-start | bytes 1966088 | tf_op jit(solution)/shard_map/ppermute | solution.py:934
  232.3 17.4 %collective-permute-start.23 = (bf16[4608,256]{1,0:T(8,128)(2,1)S(1)}, bf16[4608,256]{1,0:T(8,128)(2,1)}, u32[]{:S(2)}, u32[]{:S(2)}) collective-permute-start(bf16[4608,256]{1,0:T(8,128)(2,1)S(1)} %pad_maximum_fusion.value_ref), channel_id=1, source_target_pairs={{0,2},{2,0},{4,6},{6,4},{8,10},{10,8},{12,14},{14,12},{16,18},{18,... | collective-permute-start | bytes 7077896 | tf_op jit(solution)/shard_map/ppermute | solution.py:934
  233.2 21.9 %collective-permute-start.26 = (bf16[2304,256]{1,0:T(8,128)(2,1)S(1)}, bf16[2304,256]{1,0:T(8,128)(2,1)}, u32[]{:S(2)}, u32[]{:S(2)}) collective-permute-start(bf16[2304,256]{1,0:T(8,128)(2,1)S(1)} %pad_maximum_fusion.4), channel_id=1, source_target_pairs={{0,4},{2,10},{4,0},{6,14},{8,12},{10,2},{12,8},{14,6},{16,20},{18,... | collective-permute-start | bytes 3538952 | tf_op jit(solution)/shard_map/ppermute | solution.py:934
  233.2 10.3 %collective-permute-start.20 = (bf16[640,256]{1,0:T(8,128)(2,1)}, bf16[640,256]{1,0:T(8,128)(2,1)}, u32[]{:S(2)}, u32[]{:S(2)}) collective-permute-start(bf16[640,256]{1,0:T(8,128)(2,1)} %get-tuple-element.378), channel_id=1, source_target_pairs={{0,1},{1,0},{2,3},{3,2},{4,5},{5,4},{6,7},{7,6},{8,9},{9,8},{10,11... | collective-permute-start | bytes 983048 | tf_op jit(solution)/shard_map/ppermute | solution.py:934
  233.7 13.3 %collective-permute-start.24 = (bf16[432,256]{1,0:T(8,128)(2,1)}, bf16[432,256]{1,0:T(8,128)(2,1)}, u32[]{:S(2)}, u32[]{:S(2)}) collective-permute-start(bf16[432,256]{1,0:T(8,128)(2,1)} %get-tuple-element.391), channel_id=1, source_target_pairs={{0,8},{1,9},{2,10},{3,11},{4,12},{5,13},{6,14},{7,15},{8,0},{9,1},... | collective-permute-start | bytes 663560 | tf_op jit(solution)/shard_map/ppermute | solution.py:934
  235.5 8.0 %copy-start.9 = (bf16[640,256]{1,0:T(8,128)(2,1)S(1)}, bf16[640,256]{1,0:T(8,128)(2,1)}, u32[]{:S(2)}) copy-start(bf16[640,256]{1,0:T(8,128)(2,1)} %get-tuple-element.288) | copy-start | bytes 983044
  245.4 8.0 %collective-permute-start.22 = (bf16[320,256]{1,0:T(8,128)(2,1)}, bf16[320,256]{1,0:T(8,128)(2,1)}, u32[]{:S(2)}, u32[]{:S(2)}) collective-permute-start(bf16[320,256]{1,0:T(8,128)(2,1)} %get-tuple-element.394), channel_id=1, source_target_pairs={{0,4},{1,5},{2,10},{3,11},{4,0},{5,1},{6,14},{7,15},{8,12},{9,13},... | collective-permute-start | bytes 491528 | tf_op jit(solution)/shard_map/ppermute | solution.py:934
  248.2 6.9 %collective-permute-start.27 = (bf16[216,256]{1,0:T(8,128)(2,1)S(1)}, bf16[216,256]{1,0:T(8,128)(2,1)S(1)}, u32[]{:S(2)}, u32[]{:S(2)}) collective-permute-start(bf16[216,256]{1,0:T(8,128)(2,1)S(1)} %get-tuple-element.403), channel_id=1, source_target_pairs={{0,16},{1,17},{2,18},{3,19},{4,20},{5,21},{6,22},{7,23},{8,24},{9,... | collective-permute-start | bytes 331784 | tf_op jit(solution)/shard_map/ppermute | solution.py:934
  256.8 17.0 %copy-start = (bf16[4608,256]{1,0:T(8,128)(2,1)}, bf16[4608,256]{1,0:T(8,128)(2,1)S(1)}, u32[]{:S(2)}) copy-start(bf16[4608,256]{1,0:T(8,128)(2,1)S(1)} %pad_maximum_fusion.1.value_ref) | copy-start | bytes 7077892
  256.8 26.2 %collective-permute-start.31 = (bf16[4608,256]{1,0:T(8,128)(2,1)S(1)}, bf16[4608,256]{1,0:T(8,128)(2,1)}, u32[]{:S(2)}, u32[]{:S(2)}) collective-permute-start(bf16[4608,256]{1,0:T(8,128)(2,1)S(1)} %pad_maximum_fusion.1.value_ref), channel_id=1, source_target_pairs={{0,2},{2,0},{4,6},{6,4},{8,10},{10,8},{12,14},{14,12},{16,18},{18,... | collective-permute-start | bytes 7077896 | tf_op jit(solution)/shard_map/ppermute | solution.py:934
  264.6 4.9 %collective-permute-start.25 = (bf16[160,256]{1,0:T(8,128)(2,1)S(1)}, bf16[160,256]{1,0:T(8,128)(2,1)S(1)}, u32[]{:S(2)}, u32[]{:S(2)}) collective-permute-start(bf16[160,256]{1,0:T(8,128)(2,1)S(1)} %get-tuple-element.406), channel_id=1, source_target_pairs={{0,8},{1,9},{2,6},{3,7},{4,12},{5,13},{6,2},{7,3},{8,0},{9,1},{10,... | collective-permute-start | bytes 245768 | tf_op jit(solution)/shard_map/ppermute | solution.py:934
  264.6 9.1 %collective-permute-start.29 = (bf16[216,256]{1,0:T(8,128)(2,1)S(1)}, bf16[216,256]{1,0:T(8,128)(2,1)S(1)}, u32[]{:S(2)}, u32[]{:S(2)}) collective-permute-start(bf16[216,256]{1,0:T(8,128)(2,1)S(1)} %add_convert_fusion.24), channel_id=1, source_target_pairs={{0,16},{1,17},{2,18},{3,19},{4,20},{5,21},{6,22},{7,23},{8,24},{9,... | collective-permute-start | bytes 331784 | tf_op jit(solution)/shard_map/ppermute | solution.py:934
  269.4 7.9 %collective-permute-start.28 = (bf16[80,256]{1,0:T(8,128)(2,1)S(1)}, bf16[80,256]{1,0:T(8,128)(2,1)S(1)}, u32[]{:S(2)}, u32[]{:S(2)}) collective-permute-start(bf16[80,256]{1,0:T(8,128)(2,1)S(1)} %get-tuple-element.412), channel_id=1, source_target_pairs={{0,16},{1,17},{2,18},{3,19},{4,20},{5,21},{6,22},{7,23},{8,24},{9,... | collective-permute-start | bytes 122888 | tf_op jit(solution)/shard_map/ppermute | solution.py:934
  273.7 7.1 %collective-permute-start.32 = (bf16[432,256]{1,0:T(8,128)(2,1)S(1)}, bf16[432,256]{1,0:T(8,128)(2,1)S(1)}, u32[]{:S(2)}, u32[]{:S(2)}) collective-permute-start(bf16[432,256]{1,0:T(8,128)(2,1)S(1)} %pad_maximum_fusion.11), channel_id=1, source_target_pairs={{0,8},{1,9},{2,10},{3,11},{4,12},{5,13},{6,14},{7,15},{8,0},{9,1},... | collective-permute-start | bytes 663560 | tf_op jit(solution)/shard_map/ppermute | solution.py:934
  280.8 8.4 %collective-permute-start.34 = (bf16[864,256]{1,0:T(8,128)(2,1)S(1)}, bf16[864,256]{1,0:T(8,128)(2,1)S(1)}, u32[]{:S(2)}, u32[]{:S(2)}) collective-permute-start(bf16[864,256]{1,0:T(8,128)(2,1)S(1)} %pad_maximum_fusion.9), channel_id=1, source_target_pairs={{0,4},{1,5},{2,3},{3,2},{4,0},{5,1},{6,7},{7,6},{8,12},{9,13},{10,... | collective-permute-start | bytes 1327112 | tf_op jit(solution)/shard_map/ppermute | solution.py:934
  282.8 5.1 %collective-permute-start.30 = (bf16[80,256]{1,0:T(8,128)(2,1)S(1)}, bf16[80,256]{1,0:T(8,128)(2,1)S(1)}, u32[]{:S(2)}, u32[]{:S(2)}) collective-permute-start(bf16[80,256]{1,0:T(8,128)(2,1)S(1)} %add_convert_fusion.29), channel_id=1, source_target_pairs={{0,16},{1,17},{2,18},{3,19},{4,20},{5,21},{6,22},{7,23},{8,24},{9,... | collective-permute-start | bytes 122888 | tf_op jit(solution)/shard_map/ppermute | solution.py:934
  289.3 13.1 %collective-permute-start.36 = (bf16[1728,256]{1,0:T(8,128)(2,1)S(1)}, bf16[1728,256]{1,0:T(8,128)(2,1)S(1)}, u32[]{:S(2)}, u32[]{:S(2)}) collective-permute-start(bf16[1728,256]{1,0:T(8,128)(2,1)S(1)} %pad_maximum_fusion.5), channel_id=1, source_target_pairs={{0,1},{1,0},{2,6},{3,7},{4,5},{5,4},{6,2},{7,3},{8,9},{9,8},{10,14... | collective-permute-start | bytes 2654216 | tf_op jit(solution)/shard_map/ppermute | solution.py:934
  290.4 4.4 %collective-permute-start.33 = (bf16[160,256]{1,0:T(8,128)(2,1)S(1)}, bf16[160,256]{1,0:T(8,128)(2,1)S(1)}, u32[]{:S(2)}, u32[]{:S(2)}) collective-permute-start(bf16[160,256]{1,0:T(8,128)(2,1)S(1)} %pad_maximum_fusion.13), channel_id=1, source_target_pairs={{0,8},{1,9},{2,6},{3,7},{4,12},{5,13},{6,2},{7,3},{8,0},{9,1},{10,... | collective-permute-start | bytes 245768 | tf_op jit(solution)/shard_map/ppermute | solution.py:934
  302.7 8.5 %collective-permute-start.38 = (bf16[3456,256]{1,0:T(8,128)(2,1)S(1)}, bf16[3456,256]{1,0:T(8,128)(2,1)S(1)}, u32[]{:S(2)}, u32[]{:S(2)}) collective-permute-start(bf16[3456,256]{1,0:T(8,128)(2,1)S(1)} %pad_maximum_fusion.2.value_ref), channel_id=1, source_target_pairs={{0,2},{1,3},{2,0},{3,1},{4,6},{5,7},{6,4},{7,5},{8,10},{9,11},{10,... | collective-permute-start | bytes 5308424 | tf_op jit(solution)/shard_map/ppermute | solution.py:934
  302.8 5.7 %collective-permute-start.35 = (bf16[320,256]{1,0:T(8,128)(2,1)}, bf16[320,256]{1,0:T(8,128)(2,1)}, u32[]{:S(2)}, u32[]{:S(2)}) collective-permute-start(bf16[320,256]{1,0:T(8,128)(2,1)} %pad_maximum_fusion.12), channel_id=1, source_target_pairs={{0,4},{1,5},{2,10},{3,11},{4,0},{5,1},{6,14},{7,15},{8,12},{9,13},... | collective-permute-start | bytes 491528 | tf_op jit(solution)/shard_map/ppermute | solution.py:934
  310.3 9.5 %collective-permute-start.37 = (bf16[640,256]{1,0:T(8,128)(2,1)}, bf16[640,256]{1,0:T(8,128)(2,1)}, u32[]{:S(2)}, u32[]{:S(2)}) collective-permute-start(bf16[640,256]{1,0:T(8,128)(2,1)} %pad_maximum_fusion.10), channel_id=1, source_target_pairs={{0,1},{1,0},{2,3},{3,2},{4,5},{5,4},{6,7},{7,6},{8,9},{9,8},{10,11... | collective-permute-start | bytes 983048 | tf_op jit(solution)/shard_map/ppermute | solution.py:934
  321.0 2.2 collective-permute-start.39
  (12 other events, 18.6 us)

commit v8 on v7

--- a/solution.py
+++ b/solution.py
@@ -899,14 +899,14 @@
     for number in range(expand_ref.shape[1] // width):
         cols = slice(number * width, (number + 1) * width)
         expand_ref[:, cols] = own[5 + number : 6 + number]
-    project_ref[...] = rows[9:10]
+    project_ref[...] = rows[9]
     pair_ref[...] = rows[10:12]
     for copy in copies:
         copy.wait()
 
 
 def last_outputs(order, side, flag, mine, got, width, units, earlier):
-    vecs = [(1, width)] * 5 + [(1, units), (2, width), (1, width)]
+    vecs = [(1, width)] * 5 + [(1, units), (2, width), (width,)]
     anywhere = pl.BlockSpec(memory_space=pl.ANY)
     return call(
         order,
@@ -1128,24 +1128,24 @@
     a.step()
     grads = backward(1, 2, 2)
     c.step()
-    a.step()
     first_sums, keep, send = weights(2 * LANES, 0, 0, project_out_grad)
     s = Total(order, ("dp", "mod"), keep, send)
     a.step()
     grads = backward(0, 4, 2)
     s.step()
-    c.step()
     a.step()
     grads = backward(1, 4, 2)
     c.step()
     s.step()
     near = image_grads(order, project_in, grads[3], grads[4])
     far = to_image(near)
+    c.step()
     a.step()
-    c.step()
     last_sums, keep, send = weights(LANES, 2, SMALL)
     p = Total(order, ("dp", "mod"), keep, send, late_stages(("dp", "mod")))
     s.step()
+    c.step()
+    a.step()
     (far,) = order.after(far)
     order.last = far
     grad_in, keep = finish_rows(
@@ -1164,13 +1164,18 @@
         rows,
     )
     p.terms = (keep, p.got)
+    p.step()
+    s.step()
+    a.step()
+    p.step()
     c.step()
     p.step()
-    a.step()
+    s.step()
     a.finish()
     outputs = unpack(side, 0, a.mine)
     p.step()
     s.step()
+    p.step()
     outputs = unpack(1 - side, 0, a.got, outputs)
     p.step()
     s.step()
@@ -1182,13 +1187,8 @@
     p.step()
     s.step()
     reduce_grad, expand_grad = unpack(1 - side, 2, c.got, outputs)
-    p.step()
-    s.step()
-    p.step()
-    s.step()
     s.finish()
     projections = first_outputs(order, side, s.mine, width, ())
-    p.step()
     project_in_grad, project_out_grad = first_outputs(order, 1 - side, s.got, width, projections)
     p.finish()
     (
@@ -1210,7 +1210,7 @@
         project_in_grad,
         bias_pair_grad,
         project_out_grad,
-        project_bias_grad.reshape(-1),
+        project_bias_grad,
         feed_gain_grad,
         feed_shift_grad,
         expand_grad[None],

time: 335 us -> 313 us (0.934)
  starting transfers between devices: 60.3 us -> 49.2 us
  waiting for transfers between devices: 46.7 us -> 37.2 us
    ppermute x36, starting transfers between devices: 51.5 us -> 40.4 us  [swap(): lax.ppermute(value, axes, [(source, pair_of(source)) for source in range(...]
    ppermute x36, waiting for transfers between devices: 46.7 us -> 37.2 us  [swap(): lax.ppermute(value, axes, [(source, pair_of(source)) for source in range(...]
    unnamed x40 -> x36, local copies, waits for them, and re-layouts: 6.86 us -> 4.27 us
  transfers between devices with their start and end apart: 40 -> 40, of which waited for: 19 -> 13; matrix products, arithmetic and copies ran while one was open for 5% -> 7% of each run, Pallas kernels for 38% -> 41%
where the time goes in v8:
time: 313 us; the launch traced here: 307 us
  Pallas kernels  189 us (60%)
  starting transfers between devices  49.2 us (16%)
  waiting for transfers between devices  37.2 us (12%)
  other arithmetic  22.9 us (7%)
  local copies, waits for them, and re-layouts  6.02 us (2%)
    pallas_call x23, Pallas kernels, call(): pl.pallas_call(kernel, grid_spec=pltpu.PrefetchScalarGridSpec(num_scalar_...  189 us
    ppermute x36, starting transfers between devices, swap(): lax.ppermute(value, axes, [(source, pair_of(source)) for source in range(...  40.4 us
    ppermute x36, waiting for transfers between devices, swap(): lax.ppermute(value, axes, [(source, pair_of(source)) for source in range(...  37.2 us
    convert_element_type x14, other arithmetic, part(): return (cut(self.terms[0]) + cut(self.terms[1])).astype(bf16)  11.5 us
    ppermute x3, starting transfers between devices, on_device(): to_text = lambda value: lax.ppermute(value, 'mod', [(0, 1)])  7.5 us
    select_n x14, other arithmetic, step(): low = jnp.where(self.last == 0, mine, got)  7.09 us
  transfers between devices with their start and end apart: 40, of which 13 were waited for; matrix products, arithmetic and copies ran while one was open for 7% of the time, Pallas kernels for 41%

profile of v8, /device:TPU:0, one launch (start us, length us, event | category | flops | bytes accessed | tf_op | source)
XLA Modules:
  0.0 306.6 jit_solution(40042846893053846)
XLA Ops:
  1.8 4.9 %collective-permute-start = (bf16[256,768]{1,0:T(8,128)(2,1)S(1)}, bf16[256,768]{1,0:T(8,128)(2,1)S(1)}, u32[]{:S(2)}, u32[]{:S(2)}) collective-permute-start(bf16[256,768]{1,0:T(8,128)(2,1)S(1)} %get-tuple-element.377), channel_id=1, source_target_pairs={{0,1},{2,3},{4,5},{6,7},{8,9},{10,11},{12,13},{14,15},{16,17},{18,... | collective-permute-start | bytes 1179656 | tf_op jit(solution)/shard_map/ppermute | solution.py:1039
  9.4 8.5 %project_rows.1 = (bf16[1024,768]{1,0:T(8,128)(2,1)}, bf16[1024,2304]{1,0:T(8,128)(2,1)}) custom-call(bf16[1024,768]{1,0:T(8,128)(2,1)} %bitcast.20, f32[1,768]{1,0:T(1,128)} %gain_ref.9, f32[1,768]{1,0:T(1,128)} %shift_ref.6, bf16[768,2304]{1,0:T(8,128)(2,1)} %weight_ref.3, f32[2,768]{1,0:T(2,128)} %bias_ref.5), custom_call_target="tpu_custom_call" | custom-call | flops 3623878656 | bytes 11403264 | tf_op jit(solution)/shard_map/project_rows/pallas_call | solution.py:83
  19.3 3.9 %image_rows.2 = (bf16[512,768]{1,0:T(8,128)(2,1)}, bf16[512,1536]{1,0:T(8,128)(2,1)}) custom-call(s32[1]{0:T(128)} %bitcast.flag_ref, bf16[1024,768]{1,0:T(8,128)(2,1)} %bitcast.21, bf16[256,768]{1,0:T(8,128)(2,1)} %copy-done.11, f32[1,768]{1,0:T(1,128)} %gain_ref.9, f32[1,768]{1,0:T(1,128)} %shift_ref.6, f32[2,768]{1,0:T(2,128)} %copy-done.14, ...), custom_call_target="tpu_custom_call" | custom-call | flops 603979776 | bytes 6291456 | tf_op jit(solution)/shard_map/image_rows/pallas_call | solution.py:83
  23.1 12.3 %attend_forward.2 = (bf16[512,768]{1,0:T(8,128)(2,1)}, f32[6,2,512]{2,1,0:T(2,128)}) custom-call(s32[1]{0:T(128)} %bitcast.flag_ref, s32[2]{0:T(128)} %count_ref.17, s32[2,4]{1,0:T(2,128)} %lengths_ref.15, bf16[1024,2304]{1,0:T(8,128)(2,1)} %get-tuple-element.244.q_ref.k_ref.v_ref, bf16[1024,2304]{1,0:T(8,128)(2,1)} %get-tuple-element.244.q_ref.k_ref.v_ref, ...), custom_call_target="tpu_custom_call" | custom-call | flops 4831838208 | bytes 6291456 | tf_op jit(solution)/shard_map/attend_forward/pallas_call | solution.py:83
  36.2 3.8 %image_rows.3 = (bf16[512,768]{1,0:T(8,128)(2,1)}, bf16[512,1536]{1,0:T(8,128)(2,1)}) custom-call(s32[1]{0:T(128)} %bitcast.flag_ref, bf16[1024,768]{1,0:T(8,128)(2,1)} %bitcast.22, bf16[256,768]{1,0:T(8,128)(2,1)} %copy-done.10, f32[1,768]{1,0:T(1,128)} %gain_ref.9, f32[1,768]{1,0:T(1,128)} %shift_ref.6, ...), custom_call_target="tpu_custom_call", output_to_operand_aliasing={{0}: (9, {}), {1}: (10, {})} | custom-call | flops 603979776 | bytes 6291456 | tf_op jit(solution)/shard_map/image_rows/pallas_call | solution.py:83
  40.0 12.2 %attend_forward.3 = (bf16[512,768]{1,0:T(8,128)(2,1)}, f32[6,2,512]{2,1,0:T(2,128)}) custom-call(s32[1]{0:T(128)} %bitcast.flag_ref, s32[2]{0:T(128)} %count_ref.17, s32[2,4]{1,0:T(2,128)} %lengths_ref.15, bf16[1024,2304]{1,0:T(8,128)(2,1)} %get-tuple-element.244.q_ref.k_ref.v_ref, bf16[1024,2304]{1,0:T(8,128)(2,1)} %get-tuple-element.244.q_ref.k_ref.v_ref, ...), custom_call_target="tpu_custom_call" | custom-call | flops 4831838208 | bytes 6291456 | tf_op jit(solution)/shard_map/attend_forward/pallas_call | solution.py:83
  52.2 45.2 %feed_forward.1 = (bf16[1024,768]{1,0:T(8,128)(2,1)}, f32[1024,768]{1,0:T(8,128)}, bf16[1024,768]{1,0:T(8,128)(2,1)}, bf16[768,768]{1,0:T(8,128)(2,1)}, f32[8,76...) custom-call(s32[1]{0:T(128)} %bitcast.flag_ref, ...), custom_call_target="tpu_custom_call" | custom-call | flops 28991029248 | bytes 41943040 | tf_op jit(solution)/shard_map/feed_forward/pallas_call | solution.py:83
  98.0 8.2 %attend_backward.6 = (bf16[1024,768]{1,0:T(8,128)(2,1)}, bf16[1024,768]{1,0:T(8,128)(2,1)}, bf16[1024,768]{1,0:T(8,128)(2,1)}, bf16[512,768]{1,0:T(8,128)(2,1)}, bf16[512,768]{1,0:T(8,128)(2,1)}) custom-call(s32[1]{0:T(128)} %bitcast.flag_ref, s32[2]{0:T(128)} %count_ref.17, s32[2,4]{1,0:T(2,128)} %lengths_ref.15, ...), custom_call_target="tpu_custom_call" | custom-call | flops 40265318400 | bytes 41943040 | tf_op jit(solution)/shard_map/attend_backward/pallas_call | solution.py:83
  106.3 1.6 add_convert_fusion
  109.4 8.3 %attend_backward.7 = (bf16[1024,768]{1,0:T(8,128)(2,1)}, bf16[1024,768]{1,0:T(8,128)(2,1)}, bf16[1024,768]{1,0:T(8,128)(2,1)}, bf16[512,768]{1,0:T(8,128)(2,1)}, bf16[512,768]{1,0:T(8,128)(2,1)}) custom-call(s32[1]{0:T(128)} %bitcast.flag_ref, s32[2]{0:T(128)} %count_ref.17, ...), custom_call_target="tpu_custom_call", output_to_operand_aliasing={{0}: (11, {}), {1}: (12, {}), {2}: (13, {}), {3}: (14, {}),... | custom-call | flops 40265318400 | bytes 41943040 | tf_op jit(solution)/shard_map/attend_backward/pallas_call | solution.py:83
  117.7 1.6 add_convert_fusion.1
  119.8 8.1 %attend_backward.8 = (bf16[1024,768]{1,0:T(8,128)(2,1)}, bf16[1024,768]{1,0:T(8,128)(2,1)}, bf16[1024,768]{1,0:T(8,128)(2,1)}, bf16[512,768]{1,0:T(8,128)(2,1)}, bf16[512,768]{1,0:T(8,128)(2,1)}) custom-call(s32[1]{0:T(128)} %bitcast.flag_ref, s32[2]{0:T(128)} %count_ref.17, ...), custom_call_target="tpu_custom_call", output_to_operand_aliasing={{0}: (11, {}), {1}: (12, {}), {2}: (13, {}), {3}: (14, {}),... | custom-call | flops 40265318400 | bytes 41943040 | tf_op jit(solution)/shard_map/attend_backward/pallas_call | solution.py:83
  130.4 2.6 collective-permute-start.8
  133.1 8.3 %attend_backward.9 = (bf16[1024,768]{1,0:T(8,128)(2,1)}, bf16[1024,768]{1,0:T(8,128)(2,1)}, bf16[1024,768]{1,0:T(8,128)(2,1)}, bf16[512,768]{1,0:T(8,128)(2,1)}, bf16[512,768]{1,0:T(8,128)(2,1)}) custom-call(s32[1]{0:T(128)} %bitcast.flag_ref, s32[2]{0:T(128)} %count_ref.17, ...), custom_call_target="tpu_custom_call", output_to_operand_aliasing={{0}: (11, {}), {1}: (12, {}), {2}: (13, {}), {3}: (14, {}),... | custom-call | flops 40265318400 | bytes 41943040 | tf_op jit(solution)/shard_map/attend_backward/pallas_call | solution.py:83
  142.5 2.4 collective-permute-start.10
  144.9 9.3 %weight_grads.2 = (f32[2,512]{1,0:T(2,128)}, bf16[3456,256]{1,0:T(8,128)(2,1)}, bf16[3456,256]{1,0:T(8,128)(2,1)}) custom-call(s32[1]{0:T(128)} %bitcast.1.side_ref.half_ref, bf16[1024,768]{1,0:T(8,128)(2,1)} %get-tuple-element.260.normed_ref, bf16[512,768]{1,0:T(8,128)(2,1)} %get-tuple-element.228.image_ref, ...), custom_call_target="tpu_custom_call" | custom-call | flops 32212254720 | bytes 125829120 | tf_op jit(solution)/shard_map/weight_grads/pallas_call | solution.py:83
  155.2 1.6 collective-permute-start.11
  156.8 8.1 %attend_backward.10 = (bf16[1024,768]{1,0:T(8,128)(2,1)}, bf16[1024,768]{1,0:T(8,128)(2,1)}, bf16[1024,768]{1,0:T(8,128)(2,1)}, bf16[512,768]{1,0:T(8,128)(2,1)}, bf16[512,768]{1,0:T(8,128)(2,1)}) custom-call(s32[1]{0:T(128)} %bitcast.flag_ref, s32[2]{0:T(128)} %count_ref.17, ...), custom_call_target="tpu_custom_call", output_to_operand_aliasing={{0}: (11, {}), {1}: (12, {}), {2}: (13, {}), {3}: (14, {}),... | custom-call | flops 40265318400 | bytes 41943040 | tf_op jit(solution)/shard_map/attend_backward/pallas_call | solution.py:83
  166.7 8.4 %attend_backward.11 = (bf16[1024,768]{1,0:T(8,128)(2,1)}, bf16[1024,768]{1,0:T(8,128)(2,1)}, bf16[1024,768]{1,0:T(8,128)(2,1)}, bf16[512,768]{1,0:T(8,128)(2,1)}, bf16[512,768]{1,0:T(8,128)(2,1)}) custom-call(s32[1]{0:T(128)} %bitcast.flag_ref, s32[2]{0:T(128)} %count_ref.17, ...), custom_call_target="tpu_custom_call", output_to_operand_aliasing={{0}: (11, {}), {1}: (12, {}), {2}: (13, {}), {3}: (14, {}),... | custom-call | flops 40265318400 | bytes 41943040 | tf_op jit(solution)/shard_map/attend_backward/pallas_call | solution.py:83
  175.2 2.1 collective-permute-start.14
  178.7 1.5 collective-permute-start.17
  180.2 4.4 %image_grads.1.near_ref = bf16[512,768]{1,0:T(8,128)(2,1)} custom-call(bf16[768,2304]{1,0:T(8,128)(2,1)} %weight_ref.3, bf16[768,2304]{1,0:T(8,128)(2,1)} %weight_ref.3, bf16[512,768]{1,0:T(8,128)(2,1)} %get-tuple-element.255.keys_ref.gik_ref, bf16[512,768]{1,0:T(8,128)(2,1)} %get-tuple-element.249.values_ref.giv_ref), custom_call_target="tpu_custom_call" | custom-call | flops 12079595520 | bytes 62914560 | tf_op jit(solution)/shard_map/image_grads/pallas_call | solution.py:83
  184.7 2.1 collective-permute-start.16
  186.9 3.3 %collective-permute-start.15 = (bf16[1152,256]{1,0:T(8,128)(2,1)S(1)}, bf16[1152,256]{1,0:T(8,128)(2,1)S(1)}, u32[]{:S(2)}, u32[]{:S(2)}) collective-permute-start(bf16[1152,256]{1,0:T(8,128)(2,1)S(1)} %pad_maximum_fusion.7), channel_id=1, source_target_pairs={{0,16},{2,6},{4,20},{6,2},{8,24},{10,14},{12,28},{14,10},{16,0},{1... | collective-permute-start | bytes 1769480 | tf_op jit(solution)/shard_map/ppermute | solution.py:934
  191.5 6.1 %weight_grads.3 = (f32[2,256]{1,0:T(2,128)}, bf16[1280,256]{1,0:T(8,128)(2,1)}, bf16[1280,256]{1,0:T(8,128)(2,1)}) custom-call(s32[1]{0:T(128)} %bitcast.1.side_ref.half_ref, bf16[1024,768]{1,0:T(8,128)(2,1)} %get-tuple-element.260.normed_ref, bf16[512,768]{1,0:T(8,128)(2,1)} %get-tuple-element.228.image_ref, bf16[1024,768]{1,0:T(8,128)(2,1)} %get-tuple-element.261.gq_ref, ...), custom_call_target="tpu_custom_call" | custom-call | flops 16106127360 | bytes 125829120 | tf_op jit(solution)/shard_map/weight_grads/pallas_call | solution.py:83
  199.1 11.5 %collective-permute-done.15 = bf16[1152,256]{1,0:T(8,128)(2,1)S(1)} collective-permute-done((bf16[1152,256]{1,0:T(8,128)(2,1)S(1)}, bf16[1152,256]{1,0:T(8,128)(2,1)S(1)}, u32[]{:S(2)}, u32[]{:S(2)}) %collective-permute-start.15) | collective-permute-done | bytes 589856 | tf_op jit(solution)/shard_map/ppermute | solution.py:934
  211.8 10.1 %finish_rows.1 = (bf16[1024,768]{1,0:T(8,128)(2,1)}, bf16[1280,256]{1,0:T(8,128)(2,1)}) custom-call(s32[1]{0:T(128)} %bitcast.flag_ref, bf16[1024,768]{1,0:T(8,128)(2,1)} %bitcast.24, f32[1024,768]{1,0:T(8,128)} %get-tuple-element.273.gmid_ref, bf16[512,768]{1,0:T(8,128)(2,1)} %image_grads.1.near_ref, ...), custom_call_target="tpu_custom_call", output_to_operand_aliasing={{1}: (13, {})} | custom-call | flops 36238786560 | bytes 167772160 | tf_op jit(solution)/shard_map/finish_rows/pallas_call | solution.py:83
  221.8 2.0 add_convert_fusion.12
  224.6 2.5 collective-permute-done.20
  227.4 3.4 %collective-permute-start.29 = (bf16[4608,256]{1,0:T(8,128)(2,1)S(1)}, bf16[4608,256]{1,0:T(8,128)(2,1)}, u32[]{:S(2)}, u32[]{:S(2)}) collective-permute-start(bf16[4608,256]{1,0:T(8,128)(2,1)S(1)} %pad_maximum_fusion.value_ref), channel_id=1, source_target_pairs={{0,2},{2,0},{4,6},{6,4},{8,10},{10,8},{12,14},{14,12},{16,18},{18,... | collective-permute-start | bytes 7077896 | tf_op jit(solution)/shard_map/ppermute | solution.py:934
  232.3 2.1 collective-permute-start.22
  235.7 2.0 collective-permute-done.22
  239.2 3.2 %collective-permute-start.27 = (bf16[216,256]{1,0:T(8,128)(2,1)S(1)}, bf16[216,256]{1,0:T(8,128)(2,1)S(1)}, u32[]{:S(2)}, u32[]{:S(2)}) collective-permute-start(bf16[216,256]{1,0:T(8,128)(2,1)S(1)} %add_convert_fusion.24), channel_id=1, source_target_pairs={{0,16},{1,17},{2,18},{3,19},{4,20},{5,21},{6,22},{7,23},{8,24},{9,... | collective-permute-start | bytes 331784 | tf_op jit(solution)/shard_map/ppermute | solution.py:934
  242.4 3.6 %expert_outputs.4 = (f32[3072,768]{1,0:T(8,128)}, f32[768,3072]{1,0:T(8,128)}) custom-call(s32[1]{0:T(128)} %bitcast.1.side_ref.half_ref, bf16[4608,256]{1,0:T(8,128)(2,1)} %copy-done.1), custom_call_target="tpu_custom_call" | custom-call | flops 1179648 | bytes 7077888 | tf_op jit(solution)/shard_map/expert_outputs/pallas_call | solution.py:83
  246.0 1.6 collective-permute-start.26
  248.3 2.8 collective-permute-done.26
  251.7 1.9 collective-permute-start.28
  253.6 2.6 collective-permute-start.32
  256.2 3.6 %expert_outputs.5 = (f32[3072,768]{1,0:T(8,128)}, f32[768,3072]{1,0:T(8,128)}) custom-call(s32[1]{0:T(128)S(6)} %sub.49.half_ref, bf16[4608,256]{1,0:T(8,128)(2,1)} %collective-permute-done.29.value_ref, f32[3072,768]{1,0:T(8,128)} %get-tuple-element.303.refs_0_, f32[768,3072]{1,0:T(8,128)} %get-tuple-element.295.refs_1_), custom_call_target="tpu_custom_call", output_to_operand_aliasing={{0}: (2, {}), {1}: (3, {})} | custom-call | flops 1179648 | bytes 7077888 | tf_op jit(solution)/shard_map/expert_outputs/pallas_call | solution.py:83
  265.2 5.4 %collective-permute-done.34 = bf16[864,256]{1,0:T(8,128)(2,1)S(1)} collective-permute-done((bf16[864,256]{1,0:T(8,128)(2,1)S(1)}, bf16[864,256]{1,0:T(8,128)(2,1)S(1)}, u32[]{:S(2)}, u32[]{:S(2)}) %collective-permute-start.34) | collective-permute-done | bytes 442400 | tf_op jit(solution)/shard_map/ppermute | solution.py:934
  272.9 3.6 %expert_outputs.6 = (f32[3072,768]{1,0:T(8,128)}, f32[768,3072]{1,0:T(8,128)}) custom-call(s32[1]{0:T(128)} %bitcast.1.side_ref.half_ref, bf16[4608,256]{1,0:T(8,128)(2,1)} %copy-done, f32[3072,768]{1,0:T(8,128)} %get-tuple-element.316.refs_0_, f32[768,3072]{1,0:T(8,128)} %get-tuple-element.304.refs_1_), custom_call_target="tpu_custom_call", output_to_operand_aliasing={{0}: (2, {}), {1}: (3, {})} | custom-call | flops 1179648 | bytes 7077888 | tf_op jit(solution)/shard_map/expert_outputs/pallas_call | solution.py:83
  276.4 1.7 collective-permute-done.33
  279.8 4.1 %collective-permute-done.36 = bf16[1728,256]{1,0:T(8,128)(2,1)} collective-permute-done((bf16[1728,256]{1,0:T(8,128)(2,1)S(1)}, bf16[1728,256]{1,0:T(8,128)(2,1)}, u32[]{:S(2)}, u32[]{:S(2)}) %collective-permute-start.36) | collective-permute-done | bytes 884768 | tf_op jit(solution)/shard_map/ppermute | solution.py:934
  288.3 3.6 %expert_outputs.7 = (f32[3072,768]{1,0:T(8,128)}, f32[768,3072]{1,0:T(8,128)}) custom-call(s32[1]{0:T(128)S(6)} %sub.49.half_ref, bf16[4608,256]{1,0:T(8,128)(2,1)} %collective-permute-done.38.value_ref, f32[3072,768]{1,0:T(8,128)} %get-tuple-element.323.refs_0_, f32[768,3072]{1,0:T(8,128)} %get-tuple-element.317.refs_1_), custom_call_target="tpu_custom_call", output_to_operand_aliasing={{0}: (2, {}), {1}: (3, {})} | custom-call | flops 1179648 | bytes 7077888 | tf_op jit(solution)/shard_map/expert_outputs/pallas_call | solution.py:83
  291.9 3.4 %first_outputs.2 = (f32[768,2304]{1,0:T(8,128)}, f32[768,768]{1,0:T(8,128)}) custom-call(s32[1]{0:T(128)} %bitcast.1.side_ref.half_ref, bf16[3456,256]{1,0:T(8,128)(2,1)} %pad_maximum_fusion.2.value_ref), custom_call_target="tpu_custom_call" | custom-call | flops 884736 | bytes 5308416 | tf_op jit(solution)/shard_map/first_outputs/pallas_call | solution.py:83
  295.2 3.4 %first_outputs.3 = (f32[768,2304]{1,0:T(8,128)}, f32[768,768]{1,0:T(8,128)}) custom-call(s32[1]{0:T(128)S(6)} %sub.49.half_ref, bf16[3456,256]{1,0:T(8,128)(2,1)} %collective-permute-done.37.value_ref, f32[768,2304]{1,0:T(8,128)} %get-tuple-element.328.refs_0_, f32[768,768]{1,0:T(8,128)} %get-tuple-element.326.refs_1_), custom_call_target="tpu_custom_call", output_to_operand_aliasing={{0}: (2, {}), {1}: (3, {})} | custom-call | flops 884736 | bytes 5308416 | tf_op jit(solution)/shard_map/first_outputs/pallas_call | solution.py:83
  299.8 2.1 collective-permute-done.39.got_ref
  302.7 3.4 %last_outputs.1 = (f32[768,2304]{1,0:T(8,128)}, f32[1,768]{1,0:T(1,128)}, f32[1,768]{1,0:T(1,128)}, f32[1,768]{1,0:T(1,128)}, f32[1,768]{1,0:T(1,128)}, /*index=...) custom-call(s32[1]{0:T(128)} %bitcast.1.side_ref.half_ref, ...), custom_call_target="tpu_custom_call", output_to_operand_aliasing={{0}: (4, {})} | custom-call | flops 327680 | bytes 1966080 | tf_op jit(solution)/shard_map/last_outputs/pallas_call | solution.py:83
  (140 shorter events, 42.7 us)
Async XLA Ops:
  0.6 6.1 %copy-start.13 = (f32[1,768]{1,0:T(1,128)S(1)}, f32[1,768]{1,0:T(1,128)}, u32[]{:S(2)}) copy-start(f32[1,768]{1,0:T(1,128)} %gain_ref.9) | copy-start | bytes 9220
  0.7 6.1 %copy-start.12 = (f32[1,768]{1,0:T(1,128)S(1)}, f32[1,768]{1,0:T(1,128)}, u32[]{:S(2)}) copy-start(f32[1,768]{1,0:T(1,128)} %shift_ref.6) | copy-start | bytes 9220
  1.8 16.7 %collective-permute-start = (bf16[256,768]{1,0:T(8,128)(2,1)S(1)}, bf16[256,768]{1,0:T(8,128)(2,1)S(1)}, u32[]{:S(2)}, u32[]{:S(2)}) collective-permute-start(bf16[256,768]{1,0:T(8,128)(2,1)S(1)} %get-tuple-element.377), channel_id=1, source_target_pairs={{0,1},{2,3},{4,5},{6,7},{8,9},{10,11},{12,13},{14,15},{16,17},{18,... | collective-permute-start | bytes 1179656 | tf_op jit(solution)/shard_map/ppermute | solution.py:1039
  6.8 11.7 %collective-permute-start.1 = (f32[2,768]{1,0:T(2,128)S(1)}, f32[2,768]{1,0:T(2,128)S(1)}, u32[]{:S(2)}, u32[]{:S(2)}) collective-permute-start(f32[2,768]{1,0:T(2,128)S(1)} %pad_maximum_fusion.14), channel_id=1, source_target_pairs={{0,1},{2,3},{4,5},{6,7},{8,9},{10,11},{12,13},{14,15},{16,17},{18,... | collective-permute-start | bytes 18440 | tf_op jit(solution)/shard_map/ppermute | solution.py:1039
  8.1 27.3 %collective-permute-start.2 = (bf16[256,768]{1,0:T(8,128)(2,1)S(1)}, bf16[256,768]{1,0:T(8,128)(2,1)S(1)}, u32[]{:S(2)}, u32[]{:S(2)}) collective-permute-start(bf16[256,768]{1,0:T(8,128)(2,1)S(1)} %get-tuple-element.376), channel_id=1, source_target_pairs={{0,1},{2,3},{4,5},{6,7},{8,9},{10,11},{12,13},{14,15},{16,17},{18,... | collective-permute-start | bytes 1179656 | tf_op jit(solution)/shard_map/ppermute | solution.py:1039
  9.4 8.5 %copy-start.15 = (f32[768]{0:T(1024)S(1)}, f32[768]{0:T(1024)}, u32[]{:S(2)}) copy-start(f32[768]{0:T(1024)} %param.24) | copy-start | bytes 9220
  97.5 20.2 %collective-permute-start.3 = (bf16[4608,256]{1,0:T(8,128)(2,1)}, bf16[4608,256]{1,0:T(8,128)(2,1)S(1)}, u32[]{:S(2)}, u32[]{:S(2)}) collective-permute-start(bf16[4608,256]{1,0:T(8,128)(2,1)} %get-tuple-element.195), channel_id=1, source_target_pairs={{0,2},{2,0},{4,6},{6,4},{8,10},{10,8},{12,14},{14,12},{16,18},{18,... | collective-permute-start | bytes 7077896 | tf_op jit(solution)/shard_map/ppermute | solution.py:934
  97.5 8.7 %collective-permute-start.4 = (bf16[4608,256]{1,0:T(8,128)(2,1)}, bf16[4608,256]{1,0:T(8,128)(2,1)S(1)}, u32[]{:S(2)}, u32[]{:S(2)}) collective-permute-start(bf16[4608,256]{1,0:T(8,128)(2,1)} %get-tuple-element.197), channel_id=1, source_target_pairs={{0,2},{2,0},{4,6},{6,4},{8,10},{10,8},{12,14},{14,12},{16,18},{18,... | collective-permute-start | bytes 7077896 | tf_op jit(solution)/shard_map/ppermute | solution.py:934
  98.0 8.3 %copy-start.4 = (bf16[4608,256]{1,0:T(8,128)(2,1)S(1)}, bf16[4608,256]{1,0:T(8,128)(2,1)}, u32[]{:S(2)}) copy-start(bf16[4608,256]{1,0:T(8,128)(2,1)} %get-tuple-element.201) | copy-start | bytes 7077892
  107.9 20.0 %collective-permute-start.6 = (bf16[2304,256]{1,0:T(8,128)(2,1)}, bf16[2304,256]{1,0:T(8,128)(2,1)S(1)}, u32[]{:S(2)}, u32[]{:S(2)}) collective-permute-start(bf16[2304,256]{1,0:T(8,128)(2,1)} %get-tuple-element.359), channel_id=1, source_target_pairs={{0,4},{2,10},{4,0},{6,14},{8,12},{10,2},{12,8},{14,6},{16,20},{18,... | collective-permute-start | bytes 3538952 | tf_op jit(solution)/shard_map/ppermute | solution.py:934
  109.4 8.3 %copy-start.3 = (bf16[4608,256]{1,0:T(8,128)(2,1)S(1)}, bf16[4608,256]{1,0:T(8,128)(2,1)}, u32[]{:S(2)}) copy-start(bf16[4608,256]{1,0:T(8,128)(2,1)} %get-tuple-element.209) | copy-start | bytes 7077892
  119.2 22.2 %collective-permute-start.5 = (bf16[2304,256]{1,0:T(8,128)(2,1)}, bf16[2304,256]{1,0:T(8,128)(2,1)S(1)}, u32[]{:S(2)}, u32[]{:S(2)}) collective-permute-start(bf16[2304,256]{1,0:T(8,128)(2,1)} %get-tuple-element.360), channel_id=1, source_target_pairs={{0,4},{2,10},{4,0},{6,14},{8,12},{10,2},{12,8},{14,6},{16,20},{18,... | collective-permute-start | bytes 3538952 | tf_op jit(solution)/shard_map/ppermute | solution.py:934
  130.4 23.9 %collective-permute-start.8 = (bf16[1152,256]{1,0:T(8,128)(2,1)S(1)}, bf16[1152,256]{1,0:T(8,128)(2,1)S(1)}, u32[]{:S(2)}, u32[]{:S(2)}) collective-permute-start(bf16[1152,256]{1,0:T(8,128)(2,1)S(1)} %get-tuple-element.371), channel_id=1, source_target_pairs={{0,16},{2,6},{4,20},{6,2},{8,24},{10,14},{12,28},{14,10},{16,0},{1... | collective-permute-start | bytes 1769480 | tf_op jit(solution)/shard_map/ppermute | solution.py:934
  142.5 32.5 %collective-permute-start.10 = (bf16[1152,256]{1,0:T(8,128)(2,1)}, bf16[1152,256]{1,0:T(8,128)(2,1)S(1)}, u32[]{:S(2)}, u32[]{:S(2)}) collective-permute-start(bf16[1152,256]{1,0:T(8,128)(2,1)} %get-tuple-element.369), channel_id=1, source_target_pairs={{0,16},{2,6},{4,20},{6,2},{8,24},{10,14},{12,28},{14,10},{16,0},{1... | collective-permute-start | bytes 1769480 | tf_op jit(solution)/shard_map/ppermute | solution.py:934
  154.3 10.6 %collective-permute-start.7 = (bf16[3456,256]{1,0:T(8,128)(2,1)}, bf16[3456,256]{1,0:T(8,128)(2,1)S(1)}, u32[]{:S(2)}, u32[]{:S(2)}) collective-permute-start(bf16[3456,256]{1,0:T(8,128)(2,1)} %get-tuple-element.235), channel_id=1, source_target_pairs={{0,2},{1,3},{2,0},{3,1},{4,6},{5,7},{6,4},{7,5},{8,10},{9,11},{10,... | collective-permute-start | bytes 5308424 | tf_op jit(solution)/shard_map/ppermute | solution.py:934
  155.2 9.7 %copy-start.5 = (bf16[3456,256]{1,0:T(8,128)(2,1)S(1)}, bf16[3456,256]{1,0:T(8,128)(2,1)}, u32[]{:S(2)}) copy-start(bf16[3456,256]{1,0:T(8,128)(2,1)} %get-tuple-element.240) | copy-start | bytes 5308420
  155.2 11.3 %collective-permute-start.11 = (bf16[576,256]{1,0:T(8,128)(2,1)}, bf16[576,256]{1,0:T(8,128)(2,1)S(1)}, u32[]{:S(2)}, u32[]{:S(2)}) collective-permute-start(bf16[576,256]{1,0:T(8,128)(2,1)} %get-tuple-element.387), channel_id=1, source_target_pairs={{0,8},{2,18},{4,12},{6,22},{8,0},{10,26},{12,4},{14,30},{16,24},{1... | collective-permute-start | bytes 884744 | tf_op jit(solution)/shard_map/ppermute | solution.py:934
  165.4 13.1 %collective-permute-start.9 = (bf16[1728,256]{1,0:T(8,128)(2,1)S(1)}, bf16[1728,256]{1,0:T(8,128)(2,1)S(1)}, u32[]{:S(2)}, u32[]{:S(2)}) collective-permute-start(bf16[1728,256]{1,0:T(8,128)(2,1)S(1)} %get-tuple-element.362), channel_id=1, source_target_pairs={{0,1},{1,0},{2,6},{3,7},{4,5},{5,4},{6,2},{7,3},{8,9},{9,8},{10,14... | collective-permute-start | bytes 2654216 | tf_op jit(solution)/shard_map/ppermute | solution.py:934
  166.6 20.3 %collective-permute-start.13 = (bf16[576,256]{1,0:T(8,128)(2,1)S(1)}, bf16[576,256]{1,0:T(8,128)(2,1)S(1)}, u32[]{:S(2)}, u32[]{:S(2)}) collective-permute-start(bf16[576,256]{1,0:T(8,128)(2,1)S(1)} %add_convert_fusion.17), channel_id=1, source_target_pairs={{0,8},{2,18},{4,12},{6,22},{8,0},{10,26},{12,4},{14,30},{16,24},{1... | collective-permute-start | bytes 884744 | tf_op jit(solution)/shard_map/ppermute | solution.py:934
  175.2 9.4 %collective-permute-start.14 = (bf16[576,256]{1,0:T(8,128)(2,1)S(1)}, bf16[576,256]{1,0:T(8,128)(2,1)S(1)}, u32[]{:S(2)}, u32[]{:S(2)}) collective-permute-start(bf16[576,256]{1,0:T(8,128)(2,1)S(1)} %get-tuple-element.385), channel_id=1, source_target_pairs={{0,8},{2,18},{4,12},{6,22},{8,0},{10,26},{12,4},{14,30},{16,24},{1... | collective-permute-start | bytes 884744 | tf_op jit(solution)/shard_map/ppermute | solution.py:934
  178.7 19.0 %collective-permute-start.17 = (bf16[864,256]{1,0:T(8,128)(2,1)S(1)}, bf16[864,256]{1,0:T(8,128)(2,1)S(1)}, u32[]{:S(2)}, u32[]{:S(2)}) collective-permute-start(bf16[864,256]{1,0:T(8,128)(2,1)S(1)} %get-tuple-element.375), channel_id=1, source_target_pairs={{0,4},{1,5},{2,3},{3,2},{4,0},{5,1},{6,7},{7,6},{8,12},{9,13},{10,... | collective-permute-start | bytes 1327112 | tf_op jit(solution)/shard_map/ppermute | solution.py:934
  184.7 14.2 %collective-permute-start.16 = (bf16[576,256]{1,0:T(8,128)(2,1)S(1)}, bf16[576,256]{1,0:T(8,128)(2,1)S(1)}, u32[]{:S(2)}, u32[]{:S(2)}) collective-permute-start(bf16[576,256]{1,0:T(8,128)(2,1)S(1)} %add_convert_fusion.14), channel_id=1, source_target_pairs={{0,8},{2,18},{4,12},{6,22},{8,0},{10,26},{12,4},{14,30},{16,24},{1... | collective-permute-start | bytes 884744 | tf_op jit(solution)/shard_map/ppermute | solution.py:934
  186.9 23.7 %collective-permute-start.15 = (bf16[1152,256]{1,0:T(8,128)(2,1)S(1)}, bf16[1152,256]{1,0:T(8,128)(2,1)S(1)}, u32[]{:S(2)}, u32[]{:S(2)}) collective-permute-start(bf16[1152,256]{1,0:T(8,128)(2,1)S(1)} %pad_maximum_fusion.7), channel_id=1, source_target_pairs={{0,16},{2,6},{4,20},{6,2},{8,24},{10,14},{12,28},{14,10},{16,0},{1... | collective-permute-start | bytes 1769480 | tf_op jit(solution)/shard_map/ppermute | solution.py:934
  190.2 20.6 %collective-permute-start.12 = (bf16[512,768]{1,0:T(8,128)(2,1)S(1)}, bf16[512,768]{1,0:T(8,128)(2,1)S(1)}, u32[]{:S(2)}, u32[]{:S(2)}) collective-permute-start(bf16[512,768]{1,0:T(8,128)(2,1)S(1)} %copy-done.16), channel_id=1, source_target_pairs={{1,0},{3,2},{5,4},{7,6},{9,8},{11,10},{13,12},{15,14},{17,16},{19,... | collective-permute-start | bytes 2359304 | tf_op jit(solution)/shard_map/ppermute | solution.py:1040
  197.6 24.2 %collective-permute-start.18 = (bf16[1280,256]{1,0:T(8,128)(2,1)}, bf16[1280,256]{1,0:T(8,128)(2,1)S(1)}, u32[]{:S(2)}, u32[]{:S(2)}) collective-permute-start(bf16[1280,256]{1,0:T(8,128)(2,1)} %get-tuple-element.264), channel_id=1, source_target_pairs={{0,2},{1,3},{2,0},{3,1},{4,6},{5,7},{6,4},{7,5},{8,10},{9,11},{10,... | collective-permute-start | bytes 1966088 | tf_op jit(solution)/shard_map/ppermute | solution.py:934
  197.8 26.0 %collective-permute-start.21 = (bf16[432,256]{1,0:T(8,128)(2,1)S(1)}, bf16[432,256]{1,0:T(8,128)(2,1)S(1)}, u32[]{:S(2)}, u32[]{:S(2)}) collective-permute-start(bf16[432,256]{1,0:T(8,128)(2,1)S(1)} %get-tuple-element.391), channel_id=1, source_target_pairs={{0,8},{1,9},{2,10},{3,11},{4,12},{5,13},{6,14},{7,15},{8,0},{9,1},... | collective-permute-start | bytes 663560 | tf_op jit(solution)/shard_map/ppermute | solution.py:934
  199.0 35.4 %collective-permute-start.23 = (bf16[1152,256]{1,0:T(8,128)(2,1)S(1)}, bf16[1152,256]{1,0:T(8,128)(2,1)}, u32[]{:S(2)}, u32[]{:S(2)}) collective-permute-start(bf16[1152,256]{1,0:T(8,128)(2,1)S(1)} %pad_maximum_fusion.8), channel_id=1, source_target_pairs={{0,16},{2,6},{4,20},{6,2},{8,24},{10,14},{12,28},{14,10},{16,0},{1... | collective-permute-start | bytes 1769480 | tf_op jit(solution)/shard_map/ppermute | solution.py:934
  210.8 16.3 %collective-permute-start.20 = (bf16[2304,256]{1,0:T(8,128)(2,1)S(1)}, bf16[2304,256]{1,0:T(8,128)(2,1)S(1)}, u32[]{:S(2)}, u32[]{:S(2)}) collective-permute-start(bf16[2304,256]{1,0:T(8,128)(2,1)S(1)} %pad_maximum_fusion.3), channel_id=1, source_target_pairs={{0,4},{2,10},{4,0},{6,14},{8,12},{10,2},{12,8},{14,6},{16,20},{18,... | collective-permute-start | bytes 3538952 | tf_op jit(solution)/shard_map/ppermute | solution.py:934
  223.8 7.4 %collective-permute-start.19 = (bf16[640,256]{1,0:T(8,128)(2,1)}, bf16[640,256]{1,0:T(8,128)(2,1)}, u32[]{:S(2)}, u32[]{:S(2)}) collective-permute-start(bf16[640,256]{1,0:T(8,128)(2,1)} %get-tuple-element.378), channel_id=1, source_target_pairs={{0,1},{1,0},{2,3},{3,2},{4,5},{5,4},{6,7},{7,6},{8,9},{9,8},{10,11... | collective-permute-start | bytes 983048 | tf_op jit(solution)/shard_map/ppermute | solution.py:934
  227.4 8.1 %copy-start.1 = (bf16[4608,256]{1,0:T(8,128)(2,1)}, bf16[4608,256]{1,0:T(8,128)(2,1)S(1)}, u32[]{:S(2)}) copy-start(bf16[4608,256]{1,0:T(8,128)(2,1)S(1)} %pad_maximum_fusion.value_ref) | copy-start | bytes 7077892
  227.4 28.8 %collective-permute-start.29 = (bf16[4608,256]{1,0:T(8,128)(2,1)S(1)}, bf16[4608,256]{1,0:T(8,128)(2,1)}, u32[]{:S(2)}, u32[]{:S(2)}) collective-permute-start(bf16[4608,256]{1,0:T(8,128)(2,1)S(1)} %pad_maximum_fusion.value_ref), channel_id=1, source_target_pairs={{0,2},{2,0},{4,6},{6,4},{8,10},{10,8},{12,14},{14,12},{16,18},{18,... | collective-permute-start | bytes 7077896 | tf_op jit(solution)/shard_map/ppermute | solution.py:934
  230.8 8.4 %collective-permute-start.25 = (bf16[216,256]{1,0:T(8,128)(2,1)}, bf16[216,256]{1,0:T(8,128)(2,1)S(1)}, u32[]{:S(2)}, u32[]{:S(2)}) collective-permute-start(bf16[216,256]{1,0:T(8,128)(2,1)} %get-tuple-element.403), channel_id=1, source_target_pairs={{0,16},{1,17},{2,18},{3,19},{4,20},{5,21},{6,22},{7,23},{8,24},{9,... | collective-permute-start | bytes 331784 | tf_op jit(solution)/shard_map/ppermute | solution.py:934
  232.3 5.4 %collective-permute-start.22 = (bf16[320,256]{1,0:T(8,128)(2,1)S(1)}, bf16[320,256]{1,0:T(8,128)(2,1)S(1)}, u32[]{:S(2)}, u32[]{:S(2)}) collective-permute-start(bf16[320,256]{1,0:T(8,128)(2,1)S(1)} %get-tuple-element.394), channel_id=1, source_target_pairs={{0,4},{1,5},{2,10},{3,11},{4,0},{5,1},{6,14},{7,15},{8,12},{9,13},... | collective-permute-start | bytes 491528 | tf_op jit(solution)/shard_map/ppermute | solution.py:934
  235.6 26.7 %collective-permute-start.31 = (bf16[2304,256]{1,0:T(8,128)(2,1)S(1)}, bf16[2304,256]{1,0:T(8,128)(2,1)}, u32[]{:S(2)}, u32[]{:S(2)}) collective-permute-start(bf16[2304,256]{1,0:T(8,128)(2,1)S(1)} %pad_maximum_fusion.4), channel_id=1, source_target_pairs={{0,4},{2,10},{4,0},{6,14},{8,12},{10,2},{12,8},{14,6},{16,20},{18,... | collective-permute-start | bytes 3538952 | tf_op jit(solution)/shard_map/ppermute | solution.py:934
  237.7 8.2 %collective-permute-start.24 = (bf16[160,256]{1,0:T(8,128)(2,1)S(1)}, bf16[160,256]{1,0:T(8,128)(2,1)S(1)}, u32[]{:S(2)}, u32[]{:S(2)}) collective-permute-start(bf16[160,256]{1,0:T(8,128)(2,1)S(1)} %get-tuple-element.406), channel_id=1, source_target_pairs={{0,8},{1,9},{2,6},{3,7},{4,12},{5,13},{6,2},{7,3},{8,0},{9,1},{10,... | collective-permute-start | bytes 245768 | tf_op jit(solution)/shard_map/ppermute | solution.py:934
  239.2 8.4 %collective-permute-start.27 = (bf16[216,256]{1,0:T(8,128)(2,1)S(1)}, bf16[216,256]{1,0:T(8,128)(2,1)S(1)}, u32[]{:S(2)}, u32[]{:S(2)}) collective-permute-start(bf16[216,256]{1,0:T(8,128)(2,1)S(1)} %add_convert_fusion.24), channel_id=1, source_target_pairs={{0,16},{1,17},{2,18},{3,19},{4,20},{5,21},{6,22},{7,23},{8,24},{9,... | collective-permute-start | bytes 331784 | tf_op jit(solution)/shard_map/ppermute | solution.py:934
  246.0 5.1 %collective-permute-start.26 = (bf16[80,256]{1,0:T(8,128)(2,1)S(1)}, bf16[80,256]{1,0:T(8,128)(2,1)S(1)}, u32[]{:S(2)}, u32[]{:S(2)}) collective-permute-start(bf16[80,256]{1,0:T(8,128)(2,1)S(1)} %get-tuple-element.412), channel_id=1, source_target_pairs={{0,16},{1,17},{2,18},{3,19},{4,20},{5,21},{6,22},{7,23},{8,24},{9,... | collective-permute-start | bytes 122888 | tf_op jit(solution)/shard_map/ppermute | solution.py:934
  251.7 8.1 %collective-permute-start.28 = (bf16[80,256]{1,0:T(8,128)(2,1)}, bf16[80,256]{1,0:T(8,128)(2,1)}, u32[]{:S(2)}, u32[]{:S(2)}) collective-permute-start(bf16[80,256]{1,0:T(8,128)(2,1)} %add_convert_fusion.29), channel_id=1, source_target_pairs={{0,16},{1,17},{2,18},{3,19},{4,20},{5,21},{6,22},{7,23},{8,24},{9,... | collective-permute-start | bytes 122888 | tf_op jit(solution)/shard_map/ppermute | solution.py:934
  253.6 8.6 %collective-permute-start.32 = (bf16[432,256]{1,0:T(8,128)(2,1)}, bf16[432,256]{1,0:T(8,128)(2,1)S(1)}, u32[]{:S(2)}, u32[]{:S(2)}) collective-permute-start(bf16[432,256]{1,0:T(8,128)(2,1)} %pad_maximum_fusion.11), channel_id=1, source_target_pairs={{0,8},{1,9},{2,10},{3,11},{4,12},{5,13},{6,14},{7,15},{8,0},{9,1},... | collective-permute-start | bytes 663560 | tf_op jit(solution)/shard_map/ppermute | solution.py:934
  260.6 4.5 %collective-permute-start.30 = (bf16[160,256]{1,0:T(8,128)(2,1)S(1)}, bf16[160,256]{1,0:T(8,128)(2,1)S(1)}, u32[]{:S(2)}, u32[]{:S(2)}) collective-permute-start(bf16[160,256]{1,0:T(8,128)(2,1)S(1)} %pad_maximum_fusion.13), channel_id=1, source_target_pairs={{0,8},{1,9},{2,6},{3,7},{4,12},{5,13},{6,2},{7,3},{8,0},{9,1},{10,... | collective-permute-start | bytes 245768 | tf_op jit(solution)/shard_map/ppermute | solution.py:934
  262.3 8.4 %collective-permute-start.34 = (bf16[864,256]{1,0:T(8,128)(2,1)S(1)}, bf16[864,256]{1,0:T(8,128)(2,1)S(1)}, u32[]{:S(2)}, u32[]{:S(2)}) collective-permute-start(bf16[864,256]{1,0:T(8,128)(2,1)S(1)} %pad_maximum_fusion.9), channel_id=1, source_target_pairs={{0,4},{1,5},{2,3},{3,2},{4,0},{5,1},{6,7},{7,6},{8,12},{9,13},{10,... | collective-permute-start | bytes 1327112 | tf_op jit(solution)/shard_map/ppermute | solution.py:934
  264.0 8.0 %copy-start = (bf16[4608,256]{1,0:T(8,128)(2,1)}, bf16[4608,256]{1,0:T(8,128)(2,1)S(1)}, u32[]{:S(2)}) copy-start(bf16[4608,256]{1,0:T(8,128)(2,1)S(1)} %pad_maximum_fusion.1.value_ref) | copy-start | bytes 7077892
  270.8 13.2 %collective-permute-start.36 = (bf16[1728,256]{1,0:T(8,128)(2,1)S(1)}, bf16[1728,256]{1,0:T(8,128)(2,1)}, u32[]{:S(2)}, u32[]{:S(2)}) collective-permute-start(bf16[1728,256]{1,0:T(8,128)(2,1)S(1)} %pad_maximum_fusion.5), channel_id=1, source_target_pairs={{0,1},{1,0},{2,6},{3,7},{4,5},{5,4},{6,2},{7,3},{8,9},{9,8},{10,14... | collective-permute-start | bytes 2654216 | tf_op jit(solution)/shard_map/ppermute | solution.py:934
  270.9 7.3 %collective-permute-start.33 = (bf16[320,256]{1,0:T(8,128)(2,1)S(1)}, bf16[320,256]{1,0:T(8,128)(2,1)}, u32[]{:S(2)}, u32[]{:S(2)}) collective-permute-start(bf16[320,256]{1,0:T(8,128)(2,1)S(1)} %pad_maximum_fusion.12), channel_id=1, source_target_pairs={{0,4},{1,5},{2,10},{3,11},{4,0},{5,1},{6,14},{7,15},{8,12},{9,13},... | collective-permute-start | bytes 491528 | tf_op jit(solution)/shard_map/ppermute | solution.py:934
  271.9 16.4 %collective-permute-start.38 = (bf16[4608,256]{1,0:T(8,128)(2,1)S(1)}, bf16[4608,256]{1,0:T(8,128)(2,1)}, u32[]{:S(2)}, u32[]{:S(2)}) collective-permute-start(bf16[4608,256]{1,0:T(8,128)(2,1)S(1)} %pad_maximum_fusion.1.value_ref), channel_id=1, source_target_pairs={{0,2},{2,0},{4,6},{6,4},{8,10},{10,8},{12,14},{14,12},{16,18},{18,... | collective-permute-start | bytes 7077896 | tf_op jit(solution)/shard_map/ppermute | solution.py:934
  286.6 8.6 %collective-permute-start.37 = (bf16[3456,256]{1,0:T(8,128)(2,1)}, bf16[3456,256]{1,0:T(8,128)(2,1)}, u32[]{:S(2)}, u32[]{:S(2)}) collective-permute-start(bf16[3456,256]{1,0:T(8,128)(2,1)} %pad_maximum_fusion.2.value_ref), channel_id=1, source_target_pairs={{0,2},{1,3},{2,0},{3,1},{4,6},{5,7},{6,4},{7,5},{8,10},{9,11},{10,... | collective-permute-start | bytes 5308424 | tf_op jit(solution)/shard_map/ppermute | solution.py:934
  286.9 11.7 %collective-permute-start.35 = (bf16[640,256]{1,0:T(8,128)(2,1)}, bf16[640,256]{1,0:T(8,128)(2,1)S(1)}, u32[]{:S(2)}, u32[]{:S(2)}) collective-permute-start(bf16[640,256]{1,0:T(8,128)(2,1)} %pad_maximum_fusion.10), channel_id=1, source_target_pairs={{0,1},{1,0},{2,3},{3,2},{4,5},{5,4},{6,7},{7,6},{8,9},{9,8},{10,11... | collective-permute-start | bytes 983048 | tf_op jit(solution)/shard_map/ppermute | solution.py:934
  299.7 2.2 collective-permute-start.39
  (10 other events, 22.3 us)

commit v9 on v7

--- a/solution.py
+++ b/solution.py
@@ -899,14 +899,14 @@
     for number in range(expand_ref.shape[1] // width):
         cols = slice(number * width, (number + 1) * width)
         expand_ref[:, cols] = own[5 + number : 6 + number]
-    project_ref[...] = rows[9:10]
+    project_ref[...] = rows[9]
     pair_ref[...] = rows[10:12]
     for copy in copies:
         copy.wait()
 
 
 def last_outputs(order, side, flag, mine, got, width, units, earlier):
-    vecs = [(1, width)] * 5 + [(1, units), (2, width), (1, width)]
+    vecs = [(1, width)] * 5 + [(1, units), (2, width), (width,)]
     anywhere = pl.BlockSpec(memory_space=pl.ANY)
     return call(
         order,
@@ -1128,24 +1128,24 @@
     a.step()
     grads = backward(1, 2, 2)
     c.step()
-    a.step()
     first_sums, keep, send = weights(2 * LANES, 0, 0, project_out_grad)
     s = Total(order, ("dp", "mod"), keep, send)
     a.step()
     grads = backward(0, 4, 2)
     s.step()
-    c.step()
     a.step()
     grads = backward(1, 4, 2)
+    a.step()
     c.step()
     s.step()
     near = image_grads(order, project_in, grads[3], grads[4])
     far = to_image(near)
+    c.step()
     a.step()
-    c.step()
     last_sums, keep, send = weights(LANES, 2, SMALL)
     p = Total(order, ("dp", "mod"), keep, send, late_stages(("dp", "mod")))
     s.step()
+    c.step()
     (far,) = order.after(far)
     order.last = far
     grad_in, keep = finish_rows(
@@ -1164,31 +1164,30 @@
         rows,
     )
     p.terms = (keep, p.got)
+    p.step()
+    a.step()
     c.step()
     p.step()
-    a.step()
     a.finish()
     outputs = unpack(side, 0, a.mine)
+    s.step()
     p.step()
     s.step()
     outputs = unpack(1 - side, 0, a.got, outputs)
     p.step()
+    c.step()
     s.step()
-    c.step()
     p.step()
-    s.step()
     c.finish()
     outputs = unpack(side, 2, c.mine, outputs)
+    s.step()
     p.step()
     s.step()
     reduce_grad, expand_grad = unpack(1 - side, 2, c.got, outputs)
     p.step()
     s.step()
-    p.step()
-    s.step()
     s.finish()
     projections = first_outputs(order, side, s.mine, width, ())
-    p.step()
     project_in_grad, project_out_grad = first_outputs(order, 1 - side, s.got, width, projections)
     p.finish()
     (
@@ -1210,7 +1209,7 @@
         project_in_grad,
         bias_pair_grad,
         project_out_grad,
-        project_bias_grad.reshape(-1),
+        project_bias_grad,
         feed_gain_grad,
         feed_shift_grad,
         expand_grad[None],

time: 335 us -> 326 us (0.973)
  starting transfers between devices: 60.3 us -> 45 us
  waiting for transfers between devices: 46.7 us -> 56.6 us
    ppermute x36, starting transfers between devices: 51.5 us -> 36.2 us  [swap(): lax.ppermute(value, axes, [(source, pair_of(source)) for source in range(...]
    ppermute x36, waiting for transfers between devices: 46.7 us -> 56.6 us  [swap(): lax.ppermute(value, axes, [(source, pair_of(source)) for source in range(...]
    unnamed x40 -> x38, local copies, waits for them, and re-layouts: 6.86 us -> 6.44 us
  transfers between devices with their start and end apart: 40 -> 40, of which waited for: 19 -> 16; matrix products, arithmetic and copies ran while one was open for 5% -> 5% of each run, Pallas kernels for 38% -> 39%
where the time goes in v9:
time: 326 us; the launch traced here: 320 us
  Pallas kernels  190 us (58%)
  waiting for transfers between devices  56.6 us (17%)
  starting transfers between devices  45 us (14%)
  other arithmetic  18.9 us (6%)
  local copies, waits for them, and re-layouts  8.19 us (3%)
    pallas_call x23, Pallas kernels, call(): pl.pallas_call(kernel, grid_spec=pltpu.PrefetchScalarGridSpec(num_scalar_...  190 us
    ppermute x36, waiting for transfers between devices, swap(): lax.ppermute(value, axes, [(source, pair_of(source)) for source in range(...  56.6 us
    ppermute x36, starting transfers between devices, swap(): lax.ppermute(value, axes, [(source, pair_of(source)) for source in range(...  36.2 us
    convert_element_type x14, other arithmetic, part(): return (cut(self.terms[0]) + cut(self.terms[1])).astype(bf16)  12.9 us
    ppermute x3, starting transfers between devices, on_device(): to_text = lambda value: lax.ppermute(value, 'mod', [(0, 1)])  7.5 us
  transfers between devices with their start and end apart: 40, of which 16 were waited for; matrix products, arithmetic and copies ran while one was open for 5% of the time, Pallas kernels for 39%

profile of v9, /device:TPU:0, one launch (start us, length us, event | category | flops | bytes accessed | tf_op | source)
XLA Modules:
  0.0 320.2 jit_solution(16519479229391125967)
XLA Ops:
  1.8 4.9 %collective-permute-start = (bf16[256,768]{1,0:T(8,128)(2,1)S(1)}, bf16[256,768]{1,0:T(8,128)(2,1)S(1)}, u32[]{:S(2)}, u32[]{:S(2)}) collective-permute-start(bf16[256,768]{1,0:T(8,128)(2,1)S(1)} %get-tuple-element.377), channel_id=1, source_target_pairs={{0,1},{2,3},{4,5},{6,7},{8,9},{10,11},{12,13},{14,15},{16,17},{18,... | collective-permute-start | bytes 1179656 | tf_op jit(solution)/shard_map/ppermute | solution.py:1039
  9.4 8.5 %project_rows.1 = (bf16[1024,768]{1,0:T(8,128)(2,1)}, bf16[1024,2304]{1,0:T(8,128)(2,1)}) custom-call(bf16[1024,768]{1,0:T(8,128)(2,1)} %bitcast.20, f32[1,768]{1,0:T(1,128)} %gain_ref.9, f32[1,768]{1,0:T(1,128)} %shift_ref.6, bf16[768,2304]{1,0:T(8,128)(2,1)} %weight_ref.3, f32[2,768]{1,0:T(2,128)} %bias_ref.5), custom_call_target="tpu_custom_call" | custom-call | flops 3623878656 | bytes 11403264 | tf_op jit(solution)/shard_map/project_rows/pallas_call | solution.py:83
  19.2 3.9 %image_rows.2 = (bf16[512,768]{1,0:T(8,128)(2,1)}, bf16[512,1536]{1,0:T(8,128)(2,1)}) custom-call(s32[1]{0:T(128)} %bitcast.flag_ref, bf16[1024,768]{1,0:T(8,128)(2,1)} %bitcast.21, bf16[256,768]{1,0:T(8,128)(2,1)} %copy-done.13, f32[1,768]{1,0:T(1,128)} %gain_ref.9, f32[1,768]{1,0:T(1,128)} %shift_ref.6, f32[2,768]{1,0:T(2,128)} %copy-done.16, ...), custom_call_target="tpu_custom_call" | custom-call | flops 603979776 | bytes 6291456 | tf_op jit(solution)/shard_map/image_rows/pallas_call | solution.py:83
  23.1 12.3 %attend_forward.2 = (bf16[512,768]{1,0:T(8,128)(2,1)}, f32[6,2,512]{2,1,0:T(2,128)}) custom-call(s32[1]{0:T(128)} %bitcast.flag_ref, s32[2]{0:T(128)} %count_ref.17, s32[2,4]{1,0:T(2,128)} %lengths_ref.15, bf16[1024,2304]{1,0:T(8,128)(2,1)} %get-tuple-element.244.q_ref.k_ref.v_ref, bf16[1024,2304]{1,0:T(8,128)(2,1)} %get-tuple-element.244.q_ref.k_ref.v_ref, ...), custom_call_target="tpu_custom_call" | custom-call | flops 4831838208 | bytes 6291456 | tf_op jit(solution)/shard_map/attend_forward/pallas_call | solution.py:83
  36.2 3.8 %image_rows.3 = (bf16[512,768]{1,0:T(8,128)(2,1)}, bf16[512,1536]{1,0:T(8,128)(2,1)}) custom-call(s32[1]{0:T(128)} %bitcast.flag_ref, bf16[1024,768]{1,0:T(8,128)(2,1)} %bitcast.22, bf16[256,768]{1,0:T(8,128)(2,1)} %copy-done.12, f32[1,768]{1,0:T(1,128)} %gain_ref.9, f32[1,768]{1,0:T(1,128)} %shift_ref.6, ...), custom_call_target="tpu_custom_call", output_to_operand_aliasing={{0}: (9, {}), {1}: (10, {})} | custom-call | flops 603979776 | bytes 6291456 | tf_op jit(solution)/shard_map/image_rows/pallas_call | solution.py:83
  40.0 12.3 %attend_forward.3 = (bf16[512,768]{1,0:T(8,128)(2,1)}, f32[6,2,512]{2,1,0:T(2,128)}) custom-call(s32[1]{0:T(128)} %bitcast.flag_ref, s32[2]{0:T(128)} %count_ref.17, s32[2,4]{1,0:T(2,128)} %lengths_ref.15, bf16[1024,2304]{1,0:T(8,128)(2,1)} %get-tuple-element.244.q_ref.k_ref.v_ref, bf16[1024,2304]{1,0:T(8,128)(2,1)} %get-tuple-element.244.q_ref.k_ref.v_ref, ...), custom_call_target="tpu_custom_call" | custom-call | flops 4831838208 | bytes 6291456 | tf_op jit(solution)/shard_map/attend_forward/pallas_call | solution.py:83
  52.3 45.2 %feed_forward.1 = (bf16[1024,768]{1,0:T(8,128)(2,1)}, f32[1024,768]{1,0:T(8,128)}, bf16[1024,768]{1,0:T(8,128)(2,1)}, bf16[768,768]{1,0:T(8,128)(2,1)}, f32[8,76...) custom-call(s32[1]{0:T(128)} %bitcast.flag_ref, ...), custom_call_target="tpu_custom_call" | custom-call | flops 28991029248 | bytes 41943040 | tf_op jit(solution)/shard_map/feed_forward/pallas_call | solution.py:83
  98.1 8.2 %attend_backward.6 = (bf16[1024,768]{1,0:T(8,128)(2,1)}, bf16[1024,768]{1,0:T(8,128)(2,1)}, bf16[1024,768]{1,0:T(8,128)(2,1)}, bf16[512,768]{1,0:T(8,128)(2,1)}, bf16[512,768]{1,0:T(8,128)(2,1)}) custom-call(s32[1]{0:T(128)} %bitcast.flag_ref, s32[2]{0:T(128)} %count_ref.17, s32[2,4]{1,0:T(2,128)} %lengths_ref.15, ...), custom_call_target="tpu_custom_call" | custom-call | flops 40265318400 | bytes 41943040 | tf_op jit(solution)/shard_map/attend_backward/pallas_call | solution.py:83
  106.3 1.6 add_convert_fusion
  109.4 8.3 %attend_backward.7 = (bf16[1024,768]{1,0:T(8,128)(2,1)}, bf16[1024,768]{1,0:T(8,128)(2,1)}, bf16[1024,768]{1,0:T(8,128)(2,1)}, bf16[512,768]{1,0:T(8,128)(2,1)}, bf16[512,768]{1,0:T(8,128)(2,1)}) custom-call(s32[1]{0:T(128)} %bitcast.flag_ref, s32[2]{0:T(128)} %count_ref.17, ...), custom_call_target="tpu_custom_call", output_to_operand_aliasing={{0}: (11, {}), {1}: (12, {}), {2}: (13, {}), {3}: (14, {}),... | custom-call | flops 40265318400 | bytes 41943040 | tf_op jit(solution)/shard_map/attend_backward/pallas_call | solution.py:83
  117.7 1.6 add_convert_fusion.1
  119.8 8.1 %attend_backward.8 = (bf16[1024,768]{1,0:T(8,128)(2,1)}, bf16[1024,768]{1,0:T(8,128)(2,1)}, bf16[1024,768]{1,0:T(8,128)(2,1)}, bf16[512,768]{1,0:T(8,128)(2,1)}, bf16[512,768]{1,0:T(8,128)(2,1)}) custom-call(s32[1]{0:T(128)} %bitcast.flag_ref, s32[2]{0:T(128)} %count_ref.17, ...), custom_call_target="tpu_custom_call", output_to_operand_aliasing={{0}: (11, {}), {1}: (12, {}), {2}: (13, {}), {3}: (14, {}),... | custom-call | flops 40265318400 | bytes 41943040 | tf_op jit(solution)/shard_map/attend_backward/pallas_call | solution.py:83
  128.9 1.5 add_convert_fusion.7
  130.5 2.6 collective-permute-start.8
  133.1 8.3 %attend_backward.9 = (bf16[1024,768]{1,0:T(8,128)(2,1)}, bf16[1024,768]{1,0:T(8,128)(2,1)}, bf16[1024,768]{1,0:T(8,128)(2,1)}, bf16[512,768]{1,0:T(8,128)(2,1)}, bf16[512,768]{1,0:T(8,128)(2,1)}) custom-call(s32[1]{0:T(128)} %bitcast.flag_ref, s32[2]{0:T(128)} %count_ref.17, ...), custom_call_target="tpu_custom_call", output_to_operand_aliasing={{0}: (11, {}), {1}: (12, {}), {2}: (13, {}), {3}: (14, {}),... | custom-call | flops 40265318400 | bytes 41943040 | tf_op jit(solution)/shard_map/attend_backward/pallas_call | solution.py:83
  141.7 2.4 collective-permute-start.10
  144.2 9.3 %weight_grads.2 = (f32[2,512]{1,0:T(2,128)}, bf16[3456,256]{1,0:T(8,128)(2,1)}, bf16[3456,256]{1,0:T(8,128)(2,1)}) custom-call(s32[1]{0:T(128)} %bitcast.1.side_ref.half_ref, bf16[1024,768]{1,0:T(8,128)(2,1)} %get-tuple-element.262.normed_ref, bf16[512,768]{1,0:T(8,128)(2,1)} %get-tuple-element.228.image_ref, ...), custom_call_target="tpu_custom_call" | custom-call | flops 32212254720 | bytes 125829120 | tf_op jit(solution)/shard_map/weight_grads/pallas_call | solution.py:83
  155.4 8.1 %attend_backward.10 = (bf16[1024,768]{1,0:T(8,128)(2,1)}, bf16[1024,768]{1,0:T(8,128)(2,1)}, bf16[1024,768]{1,0:T(8,128)(2,1)}, bf16[512,768]{1,0:T(8,128)(2,1)}, bf16[512,768]{1,0:T(8,128)(2,1)}) custom-call(s32[1]{0:T(128)} %bitcast.flag_ref, s32[2]{0:T(128)} %count_ref.17, ...), custom_call_target="tpu_custom_call", output_to_operand_aliasing={{0}: (11, {}), {1}: (12, {}), {2}: (13, {}), {3}: (14, {}),... | custom-call | flops 40265318400 | bytes 41943040 | tf_op jit(solution)/shard_map/attend_backward/pallas_call | solution.py:83
  165.4 8.4 %attend_backward.11 = (bf16[1024,768]{1,0:T(8,128)(2,1)}, bf16[1024,768]{1,0:T(8,128)(2,1)}, bf16[1024,768]{1,0:T(8,128)(2,1)}, bf16[512,768]{1,0:T(8,128)(2,1)}, bf16[512,768]{1,0:T(8,128)(2,1)}) custom-call(s32[1]{0:T(128)} %bitcast.flag_ref, s32[2]{0:T(128)} %count_ref.17, ...), custom_call_target="tpu_custom_call", output_to_operand_aliasing={{0}: (11, {}), {1}: (12, {}), {2}: (13, {}), {3}: (14, {}),... | custom-call | flops 40265318400 | bytes 41943040 | tf_op jit(solution)/shard_map/attend_backward/pallas_call | solution.py:83
  173.9 7.4 %collective-permute-start.17 = (bf16[1152,256]{1,0:T(8,128)(2,1)S(1)}, bf16[1152,256]{1,0:T(8,128)(2,1)S(1)}, u32[]{:S(2)}, u32[]{:S(2)}) collective-permute-start(bf16[1152,256]{1,0:T(8,128)(2,1)S(1)} %pad_maximum_fusion.7), channel_id=1, source_target_pairs={{0,16},{2,6},{4,20},{6,2},{8,24},{10,14},{12,28},{14,10},{16,0},{1... | collective-permute-start | bytes 1769480 | tf_op jit(solution)/shard_map/ppermute | solution.py:934
  181.7 1.6 collective-permute-start.16
  183.3 4.4 %image_grads.1.near_ref = bf16[512,768]{1,0:T(8,128)(2,1)} custom-call(bf16[768,2304]{1,0:T(8,128)(2,1)} %weight_ref.3, bf16[768,2304]{1,0:T(8,128)(2,1)} %weight_ref.3, bf16[512,768]{1,0:T(8,128)(2,1)} %get-tuple-element.257.keys_ref.gik_ref, bf16[512,768]{1,0:T(8,128)(2,1)} %get-tuple-element.249.values_ref.giv_ref), custom_call_target="tpu_custom_call" | custom-call | flops 12079595520 | bytes 62914560 | tf_op jit(solution)/shard_map/image_grads/pallas_call | solution.py:83
  188.9 3.1 collective-permute-done.14
  192.1 2.5 collective-permute-start.15
  194.7 7.4 %collective-permute-done.17 = bf16[1152,256]{1,0:T(8,128)(2,1)S(1)} collective-permute-done((bf16[1152,256]{1,0:T(8,128)(2,1)S(1)}, bf16[1152,256]{1,0:T(8,128)(2,1)S(1)}, u32[]{:S(2)}, u32[]{:S(2)}) %collective-permute-start.17) | collective-permute-done | bytes 589856 | tf_op jit(solution)/shard_map/ppermute | solution.py:934
  202.9 6.1 %weight_grads.3 = (f32[2,256]{1,0:T(2,128)}, bf16[1280,256]{1,0:T(8,128)(2,1)}, bf16[1280,256]{1,0:T(8,128)(2,1)}) custom-call(s32[1]{0:T(128)} %bitcast.1.side_ref.half_ref, bf16[1024,768]{1,0:T(8,128)(2,1)} %get-tuple-element.262.normed_ref, bf16[512,768]{1,0:T(8,128)(2,1)} %get-tuple-element.228.image_ref, bf16[1024,768]{1,0:T(8,128)(2,1)} %get-tuple-element.263.gq_ref, ...), custom_call_target="tpu_custom_call" | custom-call | flops 16106127360 | bytes 125829120 | tf_op jit(solution)/shard_map/weight_grads/pallas_call | solution.py:83
  211.1 10.1 %finish_rows.1 = (bf16[1024,768]{1,0:T(8,128)(2,1)}, bf16[1280,256]{1,0:T(8,128)(2,1)}) custom-call(s32[1]{0:T(128)} %bitcast.flag_ref, bf16[1024,768]{1,0:T(8,128)(2,1)} %bitcast.24, f32[1024,768]{1,0:T(8,128)} %get-tuple-element.273.gmid_ref, bf16[512,768]{1,0:T(8,128)(2,1)} %image_grads.1.near_ref, ...), custom_call_target="tpu_custom_call", output_to_operand_aliasing={{1}: (13, {})} | custom-call | flops 36238786560 | bytes 167772160 | tf_op jit(solution)/shard_map/finish_rows/pallas_call | solution.py:83
  221.2 2.1 add_convert_fusion.12
  225.3 2.0 collective-permute-done.20
  229.8 8.3 %collective-permute-done.19 = bf16[640,256]{1,0:T(8,128)(2,1)} collective-permute-done((bf16[640,256]{1,0:T(8,128)(2,1)}, bf16[640,256]{1,0:T(8,128)(2,1)}, u32[]{:S(2)}, u32[]{:S(2)}) %collective-permute-start.19) | collective-permute-done | bytes 327712 | tf_op jit(solution)/shard_map/ppermute | solution.py:934
  238.1 2.0 add_convert_fusion.22
  240.8 3.6 %expert_outputs.4 = (f32[3072,768]{1,0:T(8,128)}, f32[768,3072]{1,0:T(8,128)}) custom-call(s32[1]{0:T(128)} %bitcast.1.side_ref.half_ref, bf16[4608,256]{1,0:T(8,128)(2,1)} %copy-done.1), custom_call_target="tpu_custom_call" | custom-call | flops 1179648 | bytes 7077888 | tf_op jit(solution)/shard_map/expert_outputs/pallas_call | solution.py:83
  245.5 2.0 collective-permute-start.26
  248.8 5.4 %collective-permute-done.26 = bf16[216,256]{1,0:T(8,128)(2,1)S(1)} collective-permute-done((bf16[216,256]{1,0:T(8,128)(2,1)S(1)}, bf16[216,256]{1,0:T(8,128)(2,1)S(1)}, u32[]{:S(2)}, u32[]{:S(2)}) %collective-permute-start.26) | collective-permute-done | bytes 110624 | tf_op jit(solution)/shard_map/ppermute | solution.py:934
  254.3 3.6 %expert_outputs.5 = (f32[3072,768]{1,0:T(8,128)}, f32[768,3072]{1,0:T(8,128)}) custom-call(s32[1]{0:T(128)S(6)} %sub.49.half_ref, bf16[4608,256]{1,0:T(8,128)(2,1)} %collective-permute-done.25.value_ref, f32[3072,768]{1,0:T(8,128)} %get-tuple-element.297.refs_0_, f32[768,3072]{1,0:T(8,128)} %get-tuple-element.289.refs_1_), custom_call_target="tpu_custom_call", output_to_operand_aliasing={{0}: (2, {}), {1}: (3, {})} | custom-call | flops 1179648 | bytes 7077888 | tf_op jit(solution)/shard_map/expert_outputs/pallas_call | solution.py:83
  257.9 2.9 collective-permute-start.27
  263.9 3.6 %expert_outputs.6 = (f32[3072,768]{1,0:T(8,128)}, f32[768,3072]{1,0:T(8,128)}) custom-call(s32[1]{0:T(128)} %bitcast.1.side_ref.half_ref, bf16[4608,256]{1,0:T(8,128)(2,1)} %copy-done, f32[3072,768]{1,0:T(8,128)} %get-tuple-element.308.refs_0_, f32[768,3072]{1,0:T(8,128)} %get-tuple-element.298.refs_1_), custom_call_target="tpu_custom_call", output_to_operand_aliasing={{0}: (2, {}), {1}: (3, {})} | custom-call | flops 1179648 | bytes 7077888 | tf_op jit(solution)/shard_map/expert_outputs/pallas_call | solution.py:83
  267.4 3.1 collective-permute-done.31
  270.6 1.5 collective-permute-start.34
  272.2 5.0 %collective-permute-done.30 = bf16[80,256]{1,0:T(8,128)(2,1)S(1)} collective-permute-done((bf16[80,256]{1,0:T(8,128)(2,1)S(1)}, bf16[80,256]{1,0:T(8,128)(2,1)S(1)}, u32[]{:S(2)}, u32[]{:S(2)}) %collective-permute-start.30) | collective-permute-done | bytes 40992 | tf_op jit(solution)/shard_map/ppermute | solution.py:934
  277.2 1.8 collective-permute-done.34
  279.5 3.6 %expert_outputs.7 = (f32[3072,768]{1,0:T(8,128)}, f32[768,3072]{1,0:T(8,128)}) custom-call(s32[1]{0:T(128)S(6)} %sub.49.half_ref, bf16[4608,256]{1,0:T(8,128)(2,1)} %collective-permute-done.33.value_ref, f32[3072,768]{1,0:T(8,128)} %get-tuple-element.317.refs_0_, f32[768,3072]{1,0:T(8,128)} %get-tuple-element.309.refs_1_), custom_call_target="tpu_custom_call", output_to_operand_aliasing={{0}: (2, {}), {1}: (3, {})} | custom-call | flops 1179648 | bytes 7077888 | tf_op jit(solution)/shard_map/expert_outputs/pallas_call | solution.py:83
  284.4 7.9 %collective-permute-done.36 = bf16[1728,256]{1,0:T(8,128)(2,1)} collective-permute-done((bf16[1728,256]{1,0:T(8,128)(2,1)S(1)}, bf16[1728,256]{1,0:T(8,128)(2,1)}, u32[]{:S(2)}, u32[]{:S(2)}) %collective-permute-start.36) | collective-permute-done | bytes 884768 | tf_op jit(solution)/shard_map/ppermute | solution.py:934
  295.3 3.4 %first_outputs.2 = (f32[768,2304]{1,0:T(8,128)}, f32[768,768]{1,0:T(8,128)}) custom-call(s32[1]{0:T(128)} %bitcast.1.side_ref.half_ref, bf16[3456,256]{1,0:T(8,128)(2,1)} %copy-done.2), custom_call_target="tpu_custom_call" | custom-call | flops 884736 | bytes 5308416 | tf_op jit(solution)/shard_map/first_outputs/pallas_call | solution.py:83
  299.9 3.4 %first_outputs.3 = (f32[768,2304]{1,0:T(8,128)}, f32[768,768]{1,0:T(8,128)}) custom-call(s32[1]{0:T(128)S(6)} %sub.49.half_ref, bf16[3456,256]{1,0:T(8,128)(2,1)} %copy-done.7, f32[768,2304]{1,0:T(8,128)} %get-tuple-element.326.refs_0_, f32[768,768]{1,0:T(8,128)} %get-tuple-element.324.refs_1_), custom_call_target="tpu_custom_call", output_to_operand_aliasing={{0}: (2, {}), {1}: (3, {})} | custom-call | flops 884736 | bytes 5308416 | tf_op jit(solution)/shard_map/first_outputs/pallas_call | solution.py:83
  304.4 8.8 %collective-permute-done.38 = bf16[640,256]{1,0:T(8,128)(2,1)S(1)} collective-permute-done((bf16[640,256]{1,0:T(8,128)(2,1)S(1)}, bf16[640,256]{1,0:T(8,128)(2,1)S(1)}, u32[]{:S(2)}, u32[]{:S(2)}) %collective-permute-start.38) | collective-permute-done | bytes 327712 | tf_op jit(solution)/shard_map/ppermute | solution.py:934
  313.4 2.1 collective-permute-done.39.got_ref
  316.3 3.4 %last_outputs.1 = (f32[768,2304]{1,0:T(8,128)}, f32[1,768]{1,0:T(1,128)}, f32[1,768]{1,0:T(1,128)}, f32[1,768]{1,0:T(1,128)}, f32[1,768]{1,0:T(1,128)}, /*index=...) custom-call(s32[1]{0:T(128)} %bitcast.1.side_ref.half_ref, ...), custom_call_target="tpu_custom_call", output_to_operand_aliasing={{0}: (4, {})} | custom-call | flops 327680 | bytes 1966080 | tf_op jit(solution)/shard_map/last_outputs/pallas_call | solution.py:83
  (142 shorter events, 37.2 us)
Async XLA Ops:
  0.6 6.1 %copy-start.15 = (f32[1,768]{1,0:T(1,128)S(1)}, f32[1,768]{1,0:T(1,128)}, u32[]{:S(2)}) copy-start(f32[1,768]{1,0:T(1,128)} %gain_ref.9) | copy-start | bytes 9220
  0.7 6.1 %copy-start.14 = (f32[1,768]{1,0:T(1,128)S(1)}, f32[1,768]{1,0:T(1,128)}, u32[]{:S(2)}) copy-start(f32[1,768]{1,0:T(1,128)} %shift_ref.6) | copy-start | bytes 9220
  1.8 16.6 %collective-permute-start = (bf16[256,768]{1,0:T(8,128)(2,1)S(1)}, bf16[256,768]{1,0:T(8,128)(2,1)S(1)}, u32[]{:S(2)}, u32[]{:S(2)}) collective-permute-start(bf16[256,768]{1,0:T(8,128)(2,1)S(1)} %get-tuple-element.377), channel_id=1, source_target_pairs={{0,1},{2,3},{4,5},{6,7},{8,9},{10,11},{12,13},{14,15},{16,17},{18,... | collective-permute-start | bytes 1179656 | tf_op jit(solution)/shard_map/ppermute | solution.py:1039
  6.8 11.7 %collective-permute-start.1 = (f32[2,768]{1,0:T(2,128)S(1)}, f32[2,768]{1,0:T(2,128)S(1)}, u32[]{:S(2)}, u32[]{:S(2)}) collective-permute-start(f32[2,768]{1,0:T(2,128)S(1)} %pad_maximum_fusion.14), channel_id=1, source_target_pairs={{0,1},{2,3},{4,5},{6,7},{8,9},{10,11},{12,13},{14,15},{16,17},{18,... | collective-permute-start | bytes 18440 | tf_op jit(solution)/shard_map/ppermute | solution.py:1039
  8.1 27.3 %collective-permute-start.2 = (bf16[256,768]{1,0:T(8,128)(2,1)S(1)}, bf16[256,768]{1,0:T(8,128)(2,1)S(1)}, u32[]{:S(2)}, u32[]{:S(2)}) collective-permute-start(bf16[256,768]{1,0:T(8,128)(2,1)S(1)} %get-tuple-element.376), channel_id=1, source_target_pairs={{0,1},{2,3},{4,5},{6,7},{8,9},{10,11},{12,13},{14,15},{16,17},{18,... | collective-permute-start | bytes 1179656 | tf_op jit(solution)/shard_map/ppermute | solution.py:1039
  9.4 8.5 %copy-start.17 = (f32[768]{0:T(1024)S(1)}, f32[768]{0:T(1024)}, u32[]{:S(2)}) copy-start(f32[768]{0:T(1024)} %param.24) | copy-start | bytes 9220
  97.5 20.2 %collective-permute-start.3 = (bf16[4608,256]{1,0:T(8,128)(2,1)}, bf16[4608,256]{1,0:T(8,128)(2,1)S(1)}, u32[]{:S(2)}, u32[]{:S(2)}) collective-permute-start(bf16[4608,256]{1,0:T(8,128)(2,1)} %get-tuple-element.195), channel_id=1, source_target_pairs={{0,2},{2,0},{4,6},{6,4},{8,10},{10,8},{12,14},{14,12},{16,18},{18,... | collective-permute-start | bytes 7077896 | tf_op jit(solution)/shard_map/ppermute | solution.py:934
  97.6 8.7 %collective-permute-start.4 = (bf16[4608,256]{1,0:T(8,128)(2,1)}, bf16[4608,256]{1,0:T(8,128)(2,1)S(1)}, u32[]{:S(2)}, u32[]{:S(2)}) collective-permute-start(bf16[4608,256]{1,0:T(8,128)(2,1)} %get-tuple-element.197), channel_id=1, source_target_pairs={{0,2},{2,0},{4,6},{6,4},{8,10},{10,8},{12,14},{14,12},{16,18},{18,... | collective-permute-start | bytes 7077896 | tf_op jit(solution)/shard_map/ppermute | solution.py:934
  98.1 8.2 %copy-start.5 = (bf16[4608,256]{1,0:T(8,128)(2,1)S(1)}, bf16[4608,256]{1,0:T(8,128)(2,1)}, u32[]{:S(2)}) copy-start(bf16[4608,256]{1,0:T(8,128)(2,1)} %get-tuple-element.201) | copy-start | bytes 7077892
  107.9 20.0 %collective-permute-start.6 = (bf16[2304,256]{1,0:T(8,128)(2,1)}, bf16[2304,256]{1,0:T(8,128)(2,1)S(1)}, u32[]{:S(2)}, u32[]{:S(2)}) collective-permute-start(bf16[2304,256]{1,0:T(8,128)(2,1)} %get-tuple-element.359), channel_id=1, source_target_pairs={{0,4},{2,10},{4,0},{6,14},{8,12},{10,2},{12,8},{14,6},{16,20},{18,... | collective-permute-start | bytes 3538952 | tf_op jit(solution)/shard_map/ppermute | solution.py:934
  109.4 8.3 %copy-start.4 = (bf16[4608,256]{1,0:T(8,128)(2,1)S(1)}, bf16[4608,256]{1,0:T(8,128)(2,1)}, u32[]{:S(2)}) copy-start(bf16[4608,256]{1,0:T(8,128)(2,1)} %get-tuple-element.209) | copy-start | bytes 7077892
  119.3 22.1 %collective-permute-start.5 = (bf16[2304,256]{1,0:T(8,128)(2,1)}, bf16[2304,256]{1,0:T(8,128)(2,1)S(1)}, u32[]{:S(2)}, u32[]{:S(2)}) collective-permute-start(bf16[2304,256]{1,0:T(8,128)(2,1)} %get-tuple-element.360), channel_id=1, source_target_pairs={{0,4},{2,10},{4,0},{6,14},{8,12},{10,2},{12,8},{14,6},{16,20},{18,... | collective-permute-start | bytes 3538952 | tf_op jit(solution)/shard_map/ppermute | solution.py:934
  130.5 23.5 %collective-permute-start.8 = (bf16[1152,256]{1,0:T(8,128)(2,1)S(1)}, bf16[1152,256]{1,0:T(8,128)(2,1)S(1)}, u32[]{:S(2)}, u32[]{:S(2)}) collective-permute-start(bf16[1152,256]{1,0:T(8,128)(2,1)S(1)} %get-tuple-element.371), channel_id=1, source_target_pairs={{0,16},{2,6},{4,20},{6,2},{8,24},{10,14},{12,28},{14,10},{16,0},{1... | collective-permute-start | bytes 1769480 | tf_op jit(solution)/shard_map/ppermute | solution.py:934
  141.7 39.5 %collective-permute-start.10 = (bf16[1152,256]{1,0:T(8,128)(2,1)S(1)}, bf16[1152,256]{1,0:T(8,128)(2,1)S(1)}, u32[]{:S(2)}, u32[]{:S(2)}) collective-permute-start(bf16[1152,256]{1,0:T(8,128)(2,1)S(1)} %get-tuple-element.369), channel_id=1, source_target_pairs={{0,16},{2,6},{4,20},{6,2},{8,24},{10,14},{12,28},{14,10},{16,0},{1... | collective-permute-start | bytes 1769480 | tf_op jit(solution)/shard_map/ppermute | solution.py:934
  153.5 10.0 %collective-permute-start.7 = (bf16[3456,256]{1,0:T(8,128)(2,1)}, bf16[3456,256]{1,0:T(8,128)(2,1)S(1)}, u32[]{:S(2)}, u32[]{:S(2)}) collective-permute-start(bf16[3456,256]{1,0:T(8,128)(2,1)} %get-tuple-element.235), channel_id=1, source_target_pairs={{0,2},{1,3},{2,0},{3,1},{4,6},{5,7},{6,4},{7,5},{8,10},{9,11},{10,... | collective-permute-start | bytes 5308424 | tf_op jit(solution)/shard_map/ppermute | solution.py:934
  154.1 9.4 %copy-start.6 = (bf16[3456,256]{1,0:T(8,128)(2,1)S(1)}, bf16[3456,256]{1,0:T(8,128)(2,1)}, u32[]{:S(2)}) copy-start(bf16[3456,256]{1,0:T(8,128)(2,1)} %get-tuple-element.240) | copy-start | bytes 5308420
  154.2 10.6 %collective-permute-start.11 = (bf16[576,256]{1,0:T(8,128)(2,1)S(1)}, bf16[576,256]{1,0:T(8,128)(2,1)S(1)}, u32[]{:S(2)}, u32[]{:S(2)}) collective-permute-start(bf16[576,256]{1,0:T(8,128)(2,1)S(1)} %get-tuple-element.387), channel_id=1, source_target_pairs={{0,8},{2,18},{4,12},{6,22},{8,0},{10,26},{12,4},{14,30},{16,24},{1... | collective-permute-start | bytes 884744 | tf_op jit(solution)/shard_map/ppermute | solution.py:934
  164.0 17.5 %collective-permute-start.9 = (bf16[1728,256]{1,0:T(8,128)(2,1)S(1)}, bf16[1728,256]{1,0:T(8,128)(2,1)S(1)}, u32[]{:S(2)}, u32[]{:S(2)}) collective-permute-start(bf16[1728,256]{1,0:T(8,128)(2,1)S(1)} %get-tuple-element.362), channel_id=1, source_target_pairs={{0,1},{1,0},{2,6},{3,7},{4,5},{5,4},{6,2},{7,3},{8,9},{9,8},{10,14... | collective-permute-start | bytes 2654216 | tf_op jit(solution)/shard_map/ppermute | solution.py:934
  164.8 8.9 %collective-permute-start.12 = (bf16[576,256]{1,0:T(8,128)(2,1)S(1)}, bf16[576,256]{1,0:T(8,128)(2,1)S(1)}, u32[]{:S(2)}, u32[]{:S(2)}) collective-permute-start(bf16[576,256]{1,0:T(8,128)(2,1)S(1)} %add_convert_fusion.17), channel_id=1, source_target_pairs={{0,8},{2,18},{4,12},{6,22},{8,0},{10,26},{12,4},{14,30},{16,24},{1... | collective-permute-start | bytes 884744 | tf_op jit(solution)/shard_map/ppermute | solution.py:934
  173.9 28.2 %collective-permute-start.17 = (bf16[1152,256]{1,0:T(8,128)(2,1)S(1)}, bf16[1152,256]{1,0:T(8,128)(2,1)S(1)}, u32[]{:S(2)}, u32[]{:S(2)}) collective-permute-start(bf16[1152,256]{1,0:T(8,128)(2,1)S(1)} %pad_maximum_fusion.7), channel_id=1, source_target_pairs={{0,16},{2,6},{4,20},{6,2},{8,24},{10,14},{12,28},{14,10},{16,0},{1... | collective-permute-start | bytes 1769480 | tf_op jit(solution)/shard_map/ppermute | solution.py:934
  181.4 10.7 %collective-permute-start.14 = (bf16[576,256]{1,0:T(8,128)(2,1)S(1)}, bf16[576,256]{1,0:T(8,128)(2,1)S(1)}, u32[]{:S(2)}, u32[]{:S(2)}) collective-permute-start(bf16[576,256]{1,0:T(8,128)(2,1)S(1)} %get-tuple-element.385), channel_id=1, source_target_pairs={{0,8},{2,18},{4,12},{6,22},{8,0},{10,26},{12,4},{14,30},{16,24},{1... | collective-permute-start | bytes 884744 | tf_op jit(solution)/shard_map/ppermute | solution.py:934
  181.7 27.4 %collective-permute-start.16 = (bf16[864,256]{1,0:T(8,128)(2,1)S(1)}, bf16[864,256]{1,0:T(8,128)(2,1)S(1)}, u32[]{:S(2)}, u32[]{:S(2)}) collective-permute-start(bf16[864,256]{1,0:T(8,128)(2,1)S(1)} %get-tuple-element.375), channel_id=1, source_target_pairs={{0,4},{1,5},{2,3},{3,2},{4,0},{5,1},{6,7},{7,6},{8,12},{9,13},{10,... | collective-permute-start | bytes 1327112 | tf_op jit(solution)/shard_map/ppermute | solution.py:934
  187.7 22.6 %collective-permute-start.13 = (bf16[512,768]{1,0:T(8,128)(2,1)}, bf16[512,768]{1,0:T(8,128)(2,1)S(1)}, u32[]{:S(2)}, u32[]{:S(2)}) collective-permute-start(bf16[512,768]{1,0:T(8,128)(2,1)} %image_grads.1.near_ref), channel_id=1, source_target_pairs={{1,0},{3,2},{5,4},{7,6},{9,8},{11,10},{13,12},{15,14},{17,16},{19,... | collective-permute-start | bytes 2359304 | tf_op jit(solution)/shard_map/ppermute | solution.py:1040
  192.1 17.9 %collective-permute-start.15 = (bf16[576,256]{1,0:T(8,128)(2,1)S(1)}, bf16[576,256]{1,0:T(8,128)(2,1)S(1)}, u32[]{:S(2)}, u32[]{:S(2)}) collective-permute-start(bf16[576,256]{1,0:T(8,128)(2,1)S(1)} %add_convert_fusion.14), channel_id=1, source_target_pairs={{0,8},{2,18},{4,12},{6,22},{8,0},{10,26},{12,4},{14,30},{16,24},{1... | collective-permute-start | bytes 884744 | tf_op jit(solution)/shard_map/ppermute | solution.py:934
  202.2 21.4 %collective-permute-start.21 = (bf16[2304,256]{1,0:T(8,128)(2,1)S(1)}, bf16[2304,256]{1,0:T(8,128)(2,1)S(1)}, u32[]{:S(2)}, u32[]{:S(2)}) collective-permute-start(bf16[2304,256]{1,0:T(8,128)(2,1)S(1)} %pad_maximum_fusion.3), channel_id=1, source_target_pairs={{0,4},{2,10},{4,0},{6,14},{8,12},{10,2},{12,8},{14,6},{16,20},{18,... | collective-permute-start | bytes 3538952 | tf_op jit(solution)/shard_map/ppermute | solution.py:934
  209.0 12.2 %collective-permute-start.18 = (bf16[1280,256]{1,0:T(8,128)(2,1)}, bf16[1280,256]{1,0:T(8,128)(2,1)S(1)}, u32[]{:S(2)}, u32[]{:S(2)}) collective-permute-start(bf16[1280,256]{1,0:T(8,128)(2,1)} %get-tuple-element.266), channel_id=1, source_target_pairs={{0,2},{1,3},{2,0},{3,1},{4,6},{5,7},{6,4},{7,5},{8,10},{9,11},{10,... | collective-permute-start | bytes 1966088 | tf_op jit(solution)/shard_map/ppermute | solution.py:934
  210.1 17.2 %collective-permute-start.20 = (bf16[1152,256]{1,0:T(8,128)(2,1)S(1)}, bf16[1152,256]{1,0:T(8,128)(2,1)S(1)}, u32[]{:S(2)}, u32[]{:S(2)}) collective-permute-start(bf16[1152,256]{1,0:T(8,128)(2,1)S(1)} %pad_maximum_fusion.8), channel_id=1, source_target_pairs={{0,16},{2,6},{4,20},{6,2},{8,24},{10,14},{12,28},{14,10},{16,0},{1... | collective-permute-start | bytes 1769480 | tf_op jit(solution)/shard_map/ppermute | solution.py:934
  223.9 30.4 %collective-permute-start.25 = (bf16[4608,256]{1,0:T(8,128)(2,1)S(1)}, bf16[4608,256]{1,0:T(8,128)(2,1)}, u32[]{:S(2)}, u32[]{:S(2)}) collective-permute-start(bf16[4608,256]{1,0:T(8,128)(2,1)S(1)} %pad_maximum_fusion.value_ref), channel_id=1, source_target_pairs={{0,2},{2,0},{4,6},{6,4},{8,10},{10,8},{12,14},{14,12},{16,18},{18,... | collective-permute-start | bytes 7077896 | tf_op jit(solution)/shard_map/ppermute | solution.py:934
  227.5 33.4 %collective-permute-start.29 = (bf16[2304,256]{1,0:T(8,128)(2,1)S(1)}, bf16[2304,256]{1,0:T(8,128)(2,1)}, u32[]{:S(2)}, u32[]{:S(2)}) collective-permute-start(bf16[2304,256]{1,0:T(8,128)(2,1)S(1)} %pad_maximum_fusion.4), channel_id=1, source_target_pairs={{0,4},{2,10},{4,0},{6,14},{8,12},{10,2},{12,8},{14,6},{16,20},{18,... | collective-permute-start | bytes 3538952 | tf_op jit(solution)/shard_map/ppermute | solution.py:934
  228.9 9.1 %collective-permute-start.19 = (bf16[640,256]{1,0:T(8,128)(2,1)}, bf16[640,256]{1,0:T(8,128)(2,1)}, u32[]{:S(2)}, u32[]{:S(2)}) collective-permute-start(bf16[640,256]{1,0:T(8,128)(2,1)} %get-tuple-element.378), channel_id=1, source_target_pairs={{0,1},{1,0},{2,3},{3,2},{4,5},{5,4},{6,7},{7,6},{8,9},{9,8},{10,11... | collective-permute-start | bytes 983048 | tf_op jit(solution)/shard_map/ppermute | solution.py:934
  229.6 14.8 %collective-permute-start.23 = (bf16[432,256]{1,0:T(8,128)(2,1)}, bf16[432,256]{1,0:T(8,128)(2,1)}, u32[]{:S(2)}, u32[]{:S(2)}) collective-permute-start(bf16[432,256]{1,0:T(8,128)(2,1)} %get-tuple-element.391), channel_id=1, source_target_pairs={{0,8},{1,9},{2,10},{3,11},{4,12},{5,13},{6,14},{7,15},{8,0},{9,1},... | collective-permute-start | bytes 663560 | tf_op jit(solution)/shard_map/ppermute | solution.py:934
  240.0 7.5 %collective-permute-start.22 = (bf16[320,256]{1,0:T(8,128)(2,1)}, bf16[320,256]{1,0:T(8,128)(2,1)}, u32[]{:S(2)}, u32[]{:S(2)}) collective-permute-start(bf16[320,256]{1,0:T(8,128)(2,1)} %get-tuple-element.394), channel_id=1, source_target_pairs={{0,4},{1,5},{2,10},{3,11},{4,0},{5,1},{6,14},{7,15},{8,12},{9,13},... | collective-permute-start | bytes 491528 | tf_op jit(solution)/shard_map/ppermute | solution.py:934
  240.8 3.6 %copy-start.9 = (bf16[432,256]{1,0:T(8,128)(2,1)S(1)}, bf16[432,256]{1,0:T(8,128)(2,1)}, u32[]{:S(2)}) copy-start(bf16[432,256]{1,0:T(8,128)(2,1)} %get-tuple-element.290) | copy-start | bytes 663556
  240.8 6.7 %copy-start.11 = (bf16[320,256]{1,0:T(8,128)(2,1)S(1)}, bf16[320,256]{1,0:T(8,128)(2,1)}, u32[]{:S(2)}) copy-start(bf16[320,256]{1,0:T(8,128)(2,1)} %get-tuple-element.292) | copy-start | bytes 491524
  245.5 8.7 %collective-permute-start.26 = (bf16[216,256]{1,0:T(8,128)(2,1)S(1)}, bf16[216,256]{1,0:T(8,128)(2,1)S(1)}, u32[]{:S(2)}, u32[]{:S(2)}) collective-permute-start(bf16[216,256]{1,0:T(8,128)(2,1)S(1)} %get-tuple-element.403), channel_id=1, source_target_pairs={{0,16},{1,17},{2,18},{3,19},{4,20},{5,21},{6,22},{7,23},{8,24},{9,... | collective-permute-start | bytes 331784 | tf_op jit(solution)/shard_map/ppermute | solution.py:934
  248.5 9.4 %collective-permute-start.24 = (bf16[160,256]{1,0:T(8,128)(2,1)S(1)}, bf16[160,256]{1,0:T(8,128)(2,1)S(1)}, u32[]{:S(2)}, u32[]{:S(2)}) collective-permute-start(bf16[160,256]{1,0:T(8,128)(2,1)S(1)} %get-tuple-element.406), channel_id=1, source_target_pairs={{0,8},{1,9},{2,6},{3,7},{4,12},{5,13},{6,2},{7,3},{8,0},{9,1},{10,... | collective-permute-start | bytes 245768 | tf_op jit(solution)/shard_map/ppermute | solution.py:934
  254.2 8.3 %collective-permute-start.28 = (bf16[216,256]{1,0:T(8,128)(2,1)S(1)}, bf16[216,256]{1,0:T(8,128)(2,1)S(1)}, u32[]{:S(2)}, u32[]{:S(2)}) collective-permute-start(bf16[216,256]{1,0:T(8,128)(2,1)S(1)} %add_convert_fusion.24), channel_id=1, source_target_pairs={{0,16},{1,17},{2,18},{3,19},{4,20},{5,21},{6,22},{7,23},{8,24},{9,... | collective-permute-start | bytes 331784 | tf_op jit(solution)/shard_map/ppermute | solution.py:934
  257.9 5.0 %collective-permute-start.27 = (bf16[80,256]{1,0:T(8,128)(2,1)S(1)}, bf16[80,256]{1,0:T(8,128)(2,1)S(1)}, u32[]{:S(2)}, u32[]{:S(2)}) collective-permute-start(bf16[80,256]{1,0:T(8,128)(2,1)S(1)} %get-tuple-element.412), channel_id=1, source_target_pairs={{0,16},{1,17},{2,18},{3,19},{4,20},{5,21},{6,22},{7,23},{8,24},{9,... | collective-permute-start | bytes 122888 | tf_op jit(solution)/shard_map/ppermute | solution.py:934
  262.5 17.0 %collective-permute-start.33 = (bf16[4608,256]{1,0:T(8,128)(2,1)S(1)}, bf16[4608,256]{1,0:T(8,128)(2,1)}, u32[]{:S(2)}, u32[]{:S(2)}) collective-permute-start(bf16[4608,256]{1,0:T(8,128)(2,1)S(1)} %pad_maximum_fusion.1.value_ref), channel_id=1, source_target_pairs={{0,2},{2,0},{4,6},{6,4},{8,10},{10,8},{12,14},{14,12},{16,18},{18,... | collective-permute-start | bytes 7077896 | tf_op jit(solution)/shard_map/ppermute | solution.py:934
  262.6 7.9 %collective-permute-start.31 = (bf16[432,256]{1,0:T(8,128)(2,1)S(1)}, bf16[432,256]{1,0:T(8,128)(2,1)S(1)}, u32[]{:S(2)}, u32[]{:S(2)}) collective-permute-start(bf16[432,256]{1,0:T(8,128)(2,1)S(1)} %pad_maximum_fusion.11), channel_id=1, source_target_pairs={{0,8},{1,9},{2,10},{3,11},{4,12},{5,13},{6,14},{7,15},{8,0},{9,1},... | collective-permute-start | bytes 663560 | tf_op jit(solution)/shard_map/ppermute | solution.py:934
  270.6 8.4 %collective-permute-start.34 = (bf16[864,256]{1,0:T(8,128)(2,1)S(1)}, bf16[864,256]{1,0:T(8,128)(2,1)S(1)}, u32[]{:S(2)}, u32[]{:S(2)}) collective-permute-start(bf16[864,256]{1,0:T(8,128)(2,1)S(1)} %pad_maximum_fusion.9), channel_id=1, source_target_pairs={{0,4},{1,5},{2,3},{3,2},{4,0},{5,1},{6,7},{7,6},{8,12},{9,13},{10,... | collective-permute-start | bytes 1327112 | tf_op jit(solution)/shard_map/ppermute | solution.py:934
  272.1 5.1 %collective-permute-start.30 = (bf16[80,256]{1,0:T(8,128)(2,1)S(1)}, bf16[80,256]{1,0:T(8,128)(2,1)S(1)}, u32[]{:S(2)}, u32[]{:S(2)}) collective-permute-start(bf16[80,256]{1,0:T(8,128)(2,1)S(1)} %add_convert_fusion.29), channel_id=1, source_target_pairs={{0,16},{1,17},{2,18},{3,19},{4,20},{5,21},{6,22},{7,23},{8,24},{9,... | collective-permute-start | bytes 122888 | tf_op jit(solution)/shard_map/ppermute | solution.py:934
  279.1 13.2 %collective-permute-start.36 = (bf16[1728,256]{1,0:T(8,128)(2,1)S(1)}, bf16[1728,256]{1,0:T(8,128)(2,1)}, u32[]{:S(2)}, u32[]{:S(2)}) collective-permute-start(bf16[1728,256]{1,0:T(8,128)(2,1)S(1)} %pad_maximum_fusion.5), channel_id=1, source_target_pairs={{0,1},{1,0},{2,6},{3,7},{4,5},{5,4},{6,2},{7,3},{8,9},{9,8},{10,14... | collective-permute-start | bytes 2654216 | tf_op jit(solution)/shard_map/ppermute | solution.py:934
  279.2 4.5 %collective-permute-start.32 = (bf16[160,256]{1,0:T(8,128)(2,1)S(1)}, bf16[160,256]{1,0:T(8,128)(2,1)S(1)}, u32[]{:S(2)}, u32[]{:S(2)}) collective-permute-start(bf16[160,256]{1,0:T(8,128)(2,1)S(1)} %pad_maximum_fusion.13), channel_id=1, source_target_pairs={{0,8},{1,9},{2,6},{3,7},{4,12},{5,13},{6,2},{7,3},{8,0},{9,1},{10,... | collective-permute-start | bytes 245768 | tf_op jit(solution)/shard_map/ppermute | solution.py:934
  293.7 5.0 %collective-permute-start.37 = (bf16[3456,256]{1,0:T(8,128)(2,1)S(1)}, bf16[3456,256]{1,0:T(8,128)(2,1)S(1)}, u32[]{:S(2)}, u32[]{:S(2)}) collective-permute-start(bf16[3456,256]{1,0:T(8,128)(2,1)S(1)} %pad_maximum_fusion.2.value_ref), channel_id=1, source_target_pairs={{0,2},{1,3},{2,0},{3,1},{4,6},{5,7},{6,4},{7,5},{8,10},{9,11},{10,... | collective-permute-start | bytes 5308424 | tf_op jit(solution)/shard_map/ppermute | solution.py:934
  293.8 9.5 %collective-permute-start.35 = (bf16[320,256]{1,0:T(8,128)(2,1)}, bf16[320,256]{1,0:T(8,128)(2,1)}, u32[]{:S(2)}, u32[]{:S(2)}) collective-permute-start(bf16[320,256]{1,0:T(8,128)(2,1)} %pad_maximum_fusion.12), channel_id=1, source_target_pairs={{0,4},{1,5},{2,10},{3,11},{4,0},{5,1},{6,14},{7,15},{8,12},{9,13},... | collective-permute-start | bytes 491528 | tf_op jit(solution)/shard_map/ppermute | solution.py:934
  304.4 8.8 %collective-permute-start.38 = (bf16[640,256]{1,0:T(8,128)(2,1)S(1)}, bf16[640,256]{1,0:T(8,128)(2,1)S(1)}, u32[]{:S(2)}, u32[]{:S(2)}) collective-permute-start(bf16[640,256]{1,0:T(8,128)(2,1)S(1)} %pad_maximum_fusion.10), channel_id=1, source_target_pairs={{0,1},{1,0},{2,3},{3,2},{4,5},{5,4},{6,7},{7,6},{8,9},{9,8},{10,11... | collective-permute-start | bytes 983048 | tf_op jit(solution)/shard_map/ppermute | solution.py:934
  313.3 2.2 collective-permute-start.39
  (11 other events, 14.8 us)

commit v10 on v8

--- a/solution.py
+++ b/solution.py
@@ -1185,8 +1185,9 @@
     c.finish()
     outputs = unpack(side, 2, c.mine, outputs)
     p.step()
+    reduce_grad, expand_grad = unpack(1 - side, 2, c.got, outputs)
+    p.finish()
     s.step()
-    reduce_grad, expand_grad = unpack(1 - side, 2, c.got, outputs)
     s.finish()
     projections = first_outputs(order, side, s.mine, width, ())
     project_in_grad, project_out_grad = first_outputs(order, 1 - side, s.got, width, projections)

time: 313 us -> 318 us (1.016)
  transfers between devices with their start and end apart: 40 -> 40, of which waited for: 13 -> 11; matrix products, arithmetic and copies ran while one was open for 7% -> 7% of each run, Pallas kernels for 41% -> 40%
where the time goes in v10:
time: 318 us; the launch traced here: 313 us
  Pallas kernels  190 us (60%)
  starting transfers between devices  52.2 us (16%)
  waiting for transfers between devices  36.8 us (12%)
  other arithmetic  24.4 us (8%)
  local copies, waits for them, and re-layouts  7.84 us (2%)
    pallas_call x23, Pallas kernels, call(): pl.pallas_call(kernel, grid_spec=pltpu.PrefetchScalarGridSpec(num_scalar_...  190 us
    ppermute x36, starting transfers between devices, swap(): lax.ppermute(value, axes, [(source, pair_of(source)) for source in range(...  43.4 us
    ppermute x36, waiting for transfers between devices, swap(): lax.ppermute(value, axes, [(source, pair_of(source)) for source in range(...  36.8 us
    convert_element_type x14, other arithmetic, part(): return (cut(self.terms[0]) + cut(self.terms[1])).astype(bf16)  11.5 us
    select_n x14, other arithmetic, step(): low = jnp.where(self.last == 0, mine, got)  8.4 us
    ppermute x3, starting transfers between devices, on_device(): to_text = lambda value: lax.ppermute(value, 'mod', [(0, 1)])  7.5 us
  transfers between devices with their start and end apart: 40, of which 11 were waited for; matrix products, arithmetic and copies ran while one was open for 7% of the time, Pallas kernels for 40%

profile of v10, /device:TPU:0, one launch (start us, length us, event | category | flops | bytes accessed | tf_op | source)
XLA Modules:
  0.0 312.5 jit_solution(10259347167478216948)
XLA Ops:
  1.8 4.9 %collective-permute-start = (bf16[256,768]{1,0:T(8,128)(2,1)S(1)}, bf16[256,768]{1,0:T(8,128)(2,1)S(1)}, u32[]{:S(2)}, u32[]{:S(2)}) collective-permute-start(bf16[256,768]{1,0:T(8,128)(2,1)S(1)} %get-tuple-element.377), channel_id=1, source_target_pairs={{0,1},{2,3},{4,5},{6,7},{8,9},{10,11},{12,13},{14,15},{16,17},{18,... | collective-permute-start | bytes 1179656 | tf_op jit(solution)/shard_map/ppermute | solution.py:1039
  9.4 8.5 %project_rows.1 = (bf16[1024,768]{1,0:T(8,128)(2,1)}, bf16[1024,2304]{1,0:T(8,128)(2,1)}) custom-call(bf16[1024,768]{1,0:T(8,128)(2,1)} %bitcast.20, f32[1,768]{1,0:T(1,128)} %gain_ref.9, f32[1,768]{1,0:T(1,128)} %shift_ref.6, bf16[768,2304]{1,0:T(8,128)(2,1)} %weight_ref.3, f32[2,768]{1,0:T(2,128)} %bias_ref.5), custom_call_target="tpu_custom_call" | custom-call | flops 3623878656 | bytes 11403264 | tf_op jit(solution)/shard_map/project_rows/pallas_call | solution.py:83
  19.3 3.9 %image_rows.2 = (bf16[512,768]{1,0:T(8,128)(2,1)}, bf16[512,1536]{1,0:T(8,128)(2,1)}) custom-call(s32[1]{0:T(128)} %bitcast.flag_ref, bf16[1024,768]{1,0:T(8,128)(2,1)} %bitcast.21, bf16[256,768]{1,0:T(8,128)(2,1)} %copy-done.13, f32[1,768]{1,0:T(1,128)} %gain_ref.9, f32[1,768]{1,0:T(1,128)} %shift_ref.6, f32[2,768]{1,0:T(2,128)} %copy-done.16, ...), custom_call_target="tpu_custom_call" | custom-call | flops 603979776 | bytes 6291456 | tf_op jit(solution)/shard_map/image_rows/pallas_call | solution.py:83
  23.2 12.3 %attend_forward.2 = (bf16[512,768]{1,0:T(8,128)(2,1)}, f32[6,2,512]{2,1,0:T(2,128)}) custom-call(s32[1]{0:T(128)} %bitcast.flag_ref, s32[2]{0:T(128)} %count_ref.17, s32[2,4]{1,0:T(2,128)} %lengths_ref.15, bf16[1024,2304]{1,0:T(8,128)(2,1)} %get-tuple-element.244.q_ref.k_ref.v_ref, bf16[1024,2304]{1,0:T(8,128)(2,1)} %get-tuple-element.244.q_ref.k_ref.v_ref, ...), custom_call_target="tpu_custom_call" | custom-call | flops 4831838208 | bytes 6291456 | tf_op jit(solution)/shard_map/attend_forward/pallas_call | solution.py:83
  36.2 3.8 %image_rows.3 = (bf16[512,768]{1,0:T(8,128)(2,1)}, bf16[512,1536]{1,0:T(8,128)(2,1)}) custom-call(s32[1]{0:T(128)} %bitcast.flag_ref, bf16[1024,768]{1,0:T(8,128)(2,1)} %bitcast.22, bf16[256,768]{1,0:T(8,128)(2,1)} %copy-done.12, f32[1,768]{1,0:T(1,128)} %gain_ref.9, f32[1,768]{1,0:T(1,128)} %shift_ref.6, ...), custom_call_target="tpu_custom_call", output_to_operand_aliasing={{0}: (9, {}), {1}: (10, {})} | custom-call | flops 603979776 | bytes 6291456 | tf_op jit(solution)/shard_map/image_rows/pallas_call | solution.py:83
  40.0 12.3 %attend_forward.3 = (bf16[512,768]{1,0:T(8,128)(2,1)}, f32[6,2,512]{2,1,0:T(2,128)}) custom-call(s32[1]{0:T(128)} %bitcast.flag_ref, s32[2]{0:T(128)} %count_ref.17, s32[2,4]{1,0:T(2,128)} %lengths_ref.15, bf16[1024,2304]{1,0:T(8,128)(2,1)} %get-tuple-element.244.q_ref.k_ref.v_ref, bf16[1024,2304]{1,0:T(8,128)(2,1)} %get-tuple-element.244.q_ref.k_ref.v_ref, ...), custom_call_target="tpu_custom_call" | custom-call | flops 4831838208 | bytes 6291456 | tf_op jit(solution)/shard_map/attend_forward/pallas_call | solution.py:83
  52.3 45.2 %feed_forward.1 = (bf16[1024,768]{1,0:T(8,128)(2,1)}, f32[1024,768]{1,0:T(8,128)}, bf16[1024,768]{1,0:T(8,128)(2,1)}, bf16[768,768]{1,0:T(8,128)(2,1)}, f32[8,76...) custom-call(s32[1]{0:T(128)} %bitcast.flag_ref, ...), custom_call_target="tpu_custom_call" | custom-call | flops 28991029248 | bytes 41943040 | tf_op jit(solution)/shard_map/feed_forward/pallas_call | solution.py:83
  98.1 8.2 %attend_backward.6 = (bf16[1024,768]{1,0:T(8,128)(2,1)}, bf16[1024,768]{1,0:T(8,128)(2,1)}, bf16[1024,768]{1,0:T(8,128)(2,1)}, bf16[512,768]{1,0:T(8,128)(2,1)}, bf16[512,768]{1,0:T(8,128)(2,1)}) custom-call(s32[1]{0:T(128)} %bitcast.flag_ref, s32[2]{0:T(128)} %count_ref.17, s32[2,4]{1,0:T(2,128)} %lengths_ref.15, ...), custom_call_target="tpu_custom_call" | custom-call | flops 40265318400 | bytes 41943040 | tf_op jit(solution)/shard_map/attend_backward/pallas_call | solution.py:83
  106.3 1.6 add_convert_fusion
  109.4 8.2 %attend_backward.7 = (bf16[1024,768]{1,0:T(8,128)(2,1)}, bf16[1024,768]{1,0:T(8,128)(2,1)}, bf16[1024,768]{1,0:T(8,128)(2,1)}, bf16[512,768]{1,0:T(8,128)(2,1)}, bf16[512,768]{1,0:T(8,128)(2,1)}) custom-call(s32[1]{0:T(128)} %bitcast.flag_ref, s32[2]{0:T(128)} %count_ref.17, ...), custom_call_target="tpu_custom_call", output_to_operand_aliasing={{0}: (11, {}), {1}: (12, {}), {2}: (13, {}), {3}: (14, {}),... | custom-call | flops 40265318400 | bytes 41943040 | tf_op jit(solution)/shard_map/attend_backward/pallas_call | solution.py:83
  117.6 1.6 add_convert_fusion.1
  119.8 8.1 %attend_backward.8 = (bf16[1024,768]{1,0:T(8,128)(2,1)}, bf16[1024,768]{1,0:T(8,128)(2,1)}, bf16[1024,768]{1,0:T(8,128)(2,1)}, bf16[512,768]{1,0:T(8,128)(2,1)}, bf16[512,768]{1,0:T(8,128)(2,1)}) custom-call(s32[1]{0:T(128)} %bitcast.flag_ref, s32[2]{0:T(128)} %count_ref.17, ...), custom_call_target="tpu_custom_call", output_to_operand_aliasing={{0}: (11, {}), {1}: (12, {}), {2}: (13, {}), {3}: (14, {}),... | custom-call | flops 40265318400 | bytes 41943040 | tf_op jit(solution)/shard_map/attend_backward/pallas_call | solution.py:83
  130.4 2.7 collective-permute-start.8
  133.1 8.3 %attend_backward.9 = (bf16[1024,768]{1,0:T(8,128)(2,1)}, bf16[1024,768]{1,0:T(8,128)(2,1)}, bf16[1024,768]{1,0:T(8,128)(2,1)}, bf16[512,768]{1,0:T(8,128)(2,1)}, bf16[512,768]{1,0:T(8,128)(2,1)}) custom-call(s32[1]{0:T(128)} %bitcast.flag_ref, s32[2]{0:T(128)} %count_ref.17, ...), custom_call_target="tpu_custom_call", output_to_operand_aliasing={{0}: (11, {}), {1}: (12, {}), {2}: (13, {}), {3}: (14, {}),... | custom-call | flops 40265318400 | bytes 41943040 | tf_op jit(solution)/shard_map/attend_backward/pallas_call | solution.py:83
  142.6 2.4 collective-permute-start.10
  145.0 9.3 %weight_grads.2 = (f32[2,512]{1,0:T(2,128)}, bf16[3456,256]{1,0:T(8,128)(2,1)}, bf16[3456,256]{1,0:T(8,128)(2,1)}) custom-call(s32[1]{0:T(128)} %bitcast.1.side_ref.half_ref, bf16[1024,768]{1,0:T(8,128)(2,1)} %get-tuple-element.260.normed_ref, bf16[512,768]{1,0:T(8,128)(2,1)} %get-tuple-element.228.image_ref, ...), custom_call_target="tpu_custom_call" | custom-call | flops 32212254720 | bytes 125829120 | tf_op jit(solution)/shard_map/weight_grads/pallas_call | solution.py:83
  155.3 1.6 collective-permute-start.11
  156.8 8.1 %attend_backward.10 = (bf16[1024,768]{1,0:T(8,128)(2,1)}, bf16[1024,768]{1,0:T(8,128)(2,1)}, bf16[1024,768]{1,0:T(8,128)(2,1)}, bf16[512,768]{1,0:T(8,128)(2,1)}, bf16[512,768]{1,0:T(8,128)(2,1)}) custom-call(s32[1]{0:T(128)} %bitcast.flag_ref, s32[2]{0:T(128)} %count_ref.17, ...), custom_call_target="tpu_custom_call", output_to_operand_aliasing={{0}: (11, {}), {1}: (12, {}), {2}: (13, {}), {3}: (14, {}),... | custom-call | flops 40265318400 | bytes 41943040 | tf_op jit(solution)/shard_map/attend_backward/pallas_call | solution.py:83
  166.7 8.4 %attend_backward.11 = (bf16[1024,768]{1,0:T(8,128)(2,1)}, bf16[1024,768]{1,0:T(8,128)(2,1)}, bf16[1024,768]{1,0:T(8,128)(2,1)}, bf16[512,768]{1,0:T(8,128)(2,1)}, bf16[512,768]{1,0:T(8,128)(2,1)}) custom-call(s32[1]{0:T(128)} %bitcast.flag_ref, s32[2]{0:T(128)} %count_ref.17, ...), custom_call_target="tpu_custom_call", output_to_operand_aliasing={{0}: (11, {}), {1}: (12, {}), {2}: (13, {}), {3}: (14, {}),... | custom-call | flops 40265318400 | bytes 41943040 | tf_op jit(solution)/shard_map/attend_backward/pallas_call | solution.py:83
  175.3 2.1 collective-permute-start.14
  180.3 4.4 %image_grads.1.near_ref = bf16[512,768]{1,0:T(8,128)(2,1)} custom-call(bf16[768,2304]{1,0:T(8,128)(2,1)} %weight_ref.3, bf16[768,2304]{1,0:T(8,128)(2,1)} %weight_ref.3, bf16[512,768]{1,0:T(8,128)(2,1)} %get-tuple-element.255.keys_ref.gik_ref, bf16[512,768]{1,0:T(8,128)(2,1)} %get-tuple-element.249.values_ref.giv_ref), custom_call_target="tpu_custom_call" | custom-call | flops 12079595520 | bytes 62914560 | tf_op jit(solution)/shard_map/image_grads/pallas_call | solution.py:83
  184.7 2.1 collective-permute-start.16
  187.0 3.3 %collective-permute-start.15 = (bf16[1152,256]{1,0:T(8,128)(2,1)S(1)}, bf16[1152,256]{1,0:T(8,128)(2,1)S(1)}, u32[]{:S(2)}, u32[]{:S(2)}) collective-permute-start(bf16[1152,256]{1,0:T(8,128)(2,1)S(1)} %pad_maximum_fusion.7), channel_id=1, source_target_pairs={{0,16},{2,6},{4,20},{6,2},{8,24},{10,14},{12,28},{14,10},{16,0},{1... | collective-permute-start | bytes 1769480 | tf_op jit(solution)/shard_map/ppermute | solution.py:934
  191.6 6.1 %weight_grads.3 = (f32[2,256]{1,0:T(2,128)}, bf16[1280,256]{1,0:T(8,128)(2,1)}, bf16[1280,256]{1,0:T(8,128)(2,1)}) custom-call(s32[1]{0:T(128)} %bitcast.1.side_ref.half_ref, bf16[1024,768]{1,0:T(8,128)(2,1)} %get-tuple-element.260.normed_ref, bf16[512,768]{1,0:T(8,128)(2,1)} %get-tuple-element.228.image_ref, bf16[1024,768]{1,0:T(8,128)(2,1)} %get-tuple-element.261.gq_ref, ...), custom_call_target="tpu_custom_call" | custom-call | flops 16106127360 | bytes 125829120 | tf_op jit(solution)/shard_map/weight_grads/pallas_call | solution.py:83
  199.1 11.4 %collective-permute-done.15 = bf16[1152,256]{1,0:T(8,128)(2,1)S(1)} collective-permute-done((bf16[1152,256]{1,0:T(8,128)(2,1)S(1)}, bf16[1152,256]{1,0:T(8,128)(2,1)S(1)}, u32[]{:S(2)}, u32[]{:S(2)}) %collective-permute-start.15) | collective-permute-done | bytes 589856 | tf_op jit(solution)/shard_map/ppermute | solution.py:934
  211.7 10.1 %finish_rows.1 = (bf16[1024,768]{1,0:T(8,128)(2,1)}, bf16[1280,256]{1,0:T(8,128)(2,1)}) custom-call(s32[1]{0:T(128)} %bitcast.flag_ref, bf16[1024,768]{1,0:T(8,128)(2,1)} %bitcast.24, f32[1024,768]{1,0:T(8,128)} %get-tuple-element.273.gmid_ref, bf16[512,768]{1,0:T(8,128)(2,1)} %image_grads.1.near_ref, ...), custom_call_target="tpu_custom_call", output_to_operand_aliasing={{1}: (13, {})} | custom-call | flops 36238786560 | bytes 167772160 | tf_op jit(solution)/shard_map/finish_rows/pallas_call | solution.py:83
  221.8 2.0 add_convert_fusion.12
  224.6 2.4 collective-permute-done.20
  227.3 3.5 %collective-permute-start.29 = (bf16[4608,256]{1,0:T(8,128)(2,1)S(1)}, bf16[4608,256]{1,0:T(8,128)(2,1)}, u32[]{:S(2)}, u32[]{:S(2)}) collective-permute-start(bf16[4608,256]{1,0:T(8,128)(2,1)S(1)} %pad_maximum_fusion.value_ref), channel_id=1, source_target_pairs={{0,2},{2,0},{4,6},{6,4},{8,10},{10,8},{12,14},{14,12},{16,18},{18,... | collective-permute-start | bytes 7077896 | tf_op jit(solution)/shard_map/ppermute | solution.py:934
  232.3 2.1 collective-permute-start.22
  235.7 2.0 collective-permute-done.22
  237.7 1.6 collective-permute-start.24
  239.3 3.0 collective-permute-start.27
  242.3 3.6 %expert_outputs.4 = (f32[3072,768]{1,0:T(8,128)}, f32[768,3072]{1,0:T(8,128)}) custom-call(s32[1]{0:T(128)} %bitcast.1.side_ref.half_ref, bf16[4608,256]{1,0:T(8,128)(2,1)} %copy-done.1), custom_call_target="tpu_custom_call" | custom-call | flops 1179648 | bytes 7077888 | tf_op jit(solution)/shard_map/expert_outputs/pallas_call | solution.py:83
  245.9 1.6 collective-permute-start.26
  248.2 2.8 collective-permute-done.26
  251.6 1.9 collective-permute-start.28
  253.5 2.5 collective-permute-start.32
  256.0 3.6 %expert_outputs.5 = (f32[3072,768]{1,0:T(8,128)}, f32[768,3072]{1,0:T(8,128)}) custom-call(s32[1]{0:T(128)S(6)} %sub.49.half_ref, bf16[4608,256]{1,0:T(8,128)(2,1)} %collective-permute-done.29.value_ref, f32[3072,768]{1,0:T(8,128)} %get-tuple-element.303.refs_0_, f32[768,3072]{1,0:T(8,128)} %get-tuple-element.295.refs_1_), custom_call_target="tpu_custom_call", output_to_operand_aliasing={{0}: (2, {}), {1}: (3, {})} | custom-call | flops 1179648 | bytes 7077888 | tf_op jit(solution)/shard_map/expert_outputs/pallas_call | solution.py:83
  265.7 1.6 collective-permute-start.30
  267.3 3.1 collective-permute-done.30
  271.3 1.6 collective-permute-start.33
  276.7 3.6 %expert_outputs.6 = (f32[3072,768]{1,0:T(8,128)}, f32[768,3072]{1,0:T(8,128)}) custom-call(s32[1]{0:T(128)} %bitcast.1.side_ref.half_ref, bf16[4608,256]{1,0:T(8,128)(2,1)} %copy-done, f32[3072,768]{1,0:T(8,128)} %get-tuple-element.316.refs_0_, f32[768,3072]{1,0:T(8,128)} %get-tuple-element.304.refs_1_), custom_call_target="tpu_custom_call", output_to_operand_aliasing={{0}: (2, {}), {1}: (3, {})} | custom-call | flops 1179648 | bytes 7077888 | tf_op jit(solution)/shard_map/expert_outputs/pallas_call | solution.py:83
  282.0 3.6 %expert_outputs.7 = (f32[3072,768]{1,0:T(8,128)}, f32[768,3072]{1,0:T(8,128)}) custom-call(s32[1]{0:T(128)S(6)} %sub.49.half_ref, bf16[4608,256]{1,0:T(8,128)(2,1)} %collective-permute-done.36.value_ref, f32[3072,768]{1,0:T(8,128)} %get-tuple-element.321.refs_0_, f32[768,3072]{1,0:T(8,128)} %get-tuple-element.317.refs_1_), custom_call_target="tpu_custom_call", output_to_operand_aliasing={{0}: (2, {}), {1}: (3, {})} | custom-call | flops 1179648 | bytes 7077888 | tf_op jit(solution)/shard_map/expert_outputs/pallas_call | solution.py:83
  285.6 10.3 %collective-permute-done.35 = bf16[640,256]{1,0:T(8,128)(2,1)} collective-permute-done((bf16[640,256]{1,0:T(8,128)(2,1)}, bf16[640,256]{1,0:T(8,128)(2,1)}, u32[]{:S(2)}, u32[]{:S(2)}) %collective-permute-start.35) | collective-permute-done | bytes 327712 | tf_op jit(solution)/shard_map/ppermute | solution.py:934
  299.9 3.4 %first_outputs.2 = (f32[768,2304]{1,0:T(8,128)}, f32[768,768]{1,0:T(8,128)}) custom-call(s32[1]{0:T(128)} %bitcast.1.side_ref.half_ref, bf16[3456,256]{1,0:T(8,128)(2,1)} %copy-done.2), custom_call_target="tpu_custom_call" | custom-call | flops 884736 | bytes 5308416 | tf_op jit(solution)/shard_map/first_outputs/pallas_call | solution.py:83
  304.5 3.4 %first_outputs.3 = (f32[768,2304]{1,0:T(8,128)}, f32[768,768]{1,0:T(8,128)}) custom-call(s32[1]{0:T(128)S(6)} %sub.49.half_ref, bf16[3456,256]{1,0:T(8,128)(2,1)} %copy-done.7, f32[768,2304]{1,0:T(8,128)} %get-tuple-element.330.refs_0_, f32[768,768]{1,0:T(8,128)} %get-tuple-element.328.refs_1_), custom_call_target="tpu_custom_call", output_to_operand_aliasing={{0}: (2, {}), {1}: (3, {})} | custom-call | flops 884736 | bytes 5308416 | tf_op jit(solution)/shard_map/first_outputs/pallas_call | solution.py:83
  308.7 3.4 %last_outputs.1 = (f32[768,2304]{1,0:T(8,128)}, f32[1,768]{1,0:T(1,128)}, f32[1,768]{1,0:T(1,128)}, f32[1,768]{1,0:T(1,128)}, f32[1,768]{1,0:T(1,128)}, /*index=...) custom-call(s32[1]{0:T(128)} %bitcast.1.side_ref.half_ref, ...), custom_call_target="tpu_custom_call", output_to_operand_aliasing={{0}: (4, {})} | custom-call | flops 327680 | bytes 1966080 | tf_op jit(solution)/shard_map/last_outputs/pallas_call | solution.py:83
  (144 shorter events, 45.8 us)
Async XLA Ops:
  0.6 6.1 %copy-start.15 = (f32[1,768]{1,0:T(1,128)S(1)}, f32[1,768]{1,0:T(1,128)}, u32[]{:S(2)}) copy-start(f32[1,768]{1,0:T(1,128)} %gain_ref.9) | copy-start | bytes 9220
  0.7 6.1 %copy-start.14 = (f32[1,768]{1,0:T(1,128)S(1)}, f32[1,768]{1,0:T(1,128)}, u32[]{:S(2)}) copy-start(f32[1,768]{1,0:T(1,128)} %shift_ref.6) | copy-start | bytes 9220
  1.8 16.7 %collective-permute-start = (bf16[256,768]{1,0:T(8,128)(2,1)S(1)}, bf16[256,768]{1,0:T(8,128)(2,1)S(1)}, u32[]{:S(2)}, u32[]{:S(2)}) collective-permute-start(bf16[256,768]{1,0:T(8,128)(2,1)S(1)} %get-tuple-element.377), channel_id=1, source_target_pairs={{0,1},{2,3},{4,5},{6,7},{8,9},{10,11},{12,13},{14,15},{16,17},{18,... | collective-permute-start | bytes 1179656 | tf_op jit(solution)/shard_map/ppermute | solution.py:1039
  6.8 11.7 %collective-permute-start.1 = (f32[2,768]{1,0:T(2,128)S(1)}, f32[2,768]{1,0:T(2,128)S(1)}, u32[]{:S(2)}, u32[]{:S(2)}) collective-permute-start(f32[2,768]{1,0:T(2,128)S(1)} %pad_maximum_fusion.14), channel_id=1, source_target_pairs={{0,1},{2,3},{4,5},{6,7},{8,9},{10,11},{12,13},{14,15},{16,17},{18,... | collective-permute-start | bytes 18440 | tf_op jit(solution)/shard_map/ppermute | solution.py:1039
  8.1 27.3 %collective-permute-start.2 = (bf16[256,768]{1,0:T(8,128)(2,1)S(1)}, bf16[256,768]{1,0:T(8,128)(2,1)S(1)}, u32[]{:S(2)}, u32[]{:S(2)}) collective-permute-start(bf16[256,768]{1,0:T(8,128)(2,1)S(1)} %get-tuple-element.376), channel_id=1, source_target_pairs={{0,1},{2,3},{4,5},{6,7},{8,9},{10,11},{12,13},{14,15},{16,17},{18,... | collective-permute-start | bytes 1179656 | tf_op jit(solution)/shard_map/ppermute | solution.py:1039
  9.4 8.5 %copy-start.17 = (f32[768]{0:T(1024)S(1)}, f32[768]{0:T(1024)}, u32[]{:S(2)}) copy-start(f32[768]{0:T(1024)} %param.24) | copy-start | bytes 9220
  97.5 20.1 %collective-permute-start.3 = (bf16[4608,256]{1,0:T(8,128)(2,1)}, bf16[4608,256]{1,0:T(8,128)(2,1)S(1)}, u32[]{:S(2)}, u32[]{:S(2)}) collective-permute-start(bf16[4608,256]{1,0:T(8,128)(2,1)} %get-tuple-element.195), channel_id=1, source_target_pairs={{0,2},{2,0},{4,6},{6,4},{8,10},{10,8},{12,14},{14,12},{16,18},{18,... | collective-permute-start | bytes 7077896 | tf_op jit(solution)/shard_map/ppermute | solution.py:934
  97.6 8.7 %collective-permute-start.4 = (bf16[4608,256]{1,0:T(8,128)(2,1)}, bf16[4608,256]{1,0:T(8,128)(2,1)S(1)}, u32[]{:S(2)}, u32[]{:S(2)}) collective-permute-start(bf16[4608,256]{1,0:T(8,128)(2,1)} %get-tuple-element.197), channel_id=1, source_target_pairs={{0,2},{2,0},{4,6},{6,4},{8,10},{10,8},{12,14},{14,12},{16,18},{18,... | collective-permute-start | bytes 7077896 | tf_op jit(solution)/shard_map/ppermute | solution.py:934
  98.1 8.2 %copy-start.5 = (bf16[4608,256]{1,0:T(8,128)(2,1)S(1)}, bf16[4608,256]{1,0:T(8,128)(2,1)}, u32[]{:S(2)}) copy-start(bf16[4608,256]{1,0:T(8,128)(2,1)} %get-tuple-element.201) | copy-start | bytes 7077892
  107.9 20.0 %collective-permute-start.6 = (bf16[2304,256]{1,0:T(8,128)(2,1)}, bf16[2304,256]{1,0:T(8,128)(2,1)S(1)}, u32[]{:S(2)}, u32[]{:S(2)}) collective-permute-start(bf16[2304,256]{1,0:T(8,128)(2,1)} %get-tuple-element.359), channel_id=1, source_target_pairs={{0,4},{2,10},{4,0},{6,14},{8,12},{10,2},{12,8},{14,6},{16,20},{18,... | collective-permute-start | bytes 3538952 | tf_op jit(solution)/shard_map/ppermute | solution.py:934
  109.4 8.2 %copy-start.4 = (bf16[4608,256]{1,0:T(8,128)(2,1)S(1)}, bf16[4608,256]{1,0:T(8,128)(2,1)}, u32[]{:S(2)}) copy-start(bf16[4608,256]{1,0:T(8,128)(2,1)} %get-tuple-element.209) | copy-start | bytes 7077892
  119.2 22.2 %collective-permute-start.5 = (bf16[2304,256]{1,0:T(8,128)(2,1)}, bf16[2304,256]{1,0:T(8,128)(2,1)S(1)}, u32[]{:S(2)}, u32[]{:S(2)}) collective-permute-start(bf16[2304,256]{1,0:T(8,128)(2,1)} %get-tuple-element.360), channel_id=1, source_target_pairs={{0,4},{2,10},{4,0},{6,14},{8,12},{10,2},{12,8},{14,6},{16,20},{18,... | collective-permute-start | bytes 3538952 | tf_op jit(solution)/shard_map/ppermute | solution.py:934
  130.4 23.9 %collective-permute-start.8 = (bf16[1152,256]{1,0:T(8,128)(2,1)S(1)}, bf16[1152,256]{1,0:T(8,128)(2,1)S(1)}, u32[]{:S(2)}, u32[]{:S(2)}) collective-permute-start(bf16[1152,256]{1,0:T(8,128)(2,1)S(1)} %get-tuple-element.371), channel_id=1, source_target_pairs={{0,16},{2,6},{4,20},{6,2},{8,24},{10,14},{12,28},{14,10},{16,0},{1... | collective-permute-start | bytes 1769480 | tf_op jit(solution)/shard_map/ppermute | solution.py:934
  142.6 32.5 %collective-permute-start.10 = (bf16[1152,256]{1,0:T(8,128)(2,1)}, bf16[1152,256]{1,0:T(8,128)(2,1)S(1)}, u32[]{:S(2)}, u32[]{:S(2)}) collective-permute-start(bf16[1152,256]{1,0:T(8,128)(2,1)} %get-tuple-element.369), channel_id=1, source_target_pairs={{0,16},{2,6},{4,20},{6,2},{8,24},{10,14},{12,28},{14,10},{16,0},{1... | collective-permute-start | bytes 1769480 | tf_op jit(solution)/shard_map/ppermute | solution.py:934
  154.3 10.6 %collective-permute-start.7 = (bf16[3456,256]{1,0:T(8,128)(2,1)}, bf16[3456,256]{1,0:T(8,128)(2,1)S(1)}, u32[]{:S(2)}, u32[]{:S(2)}) collective-permute-start(bf16[3456,256]{1,0:T(8,128)(2,1)} %get-tuple-element.235), channel_id=1, source_target_pairs={{0,2},{1,3},{2,0},{3,1},{4,6},{5,7},{6,4},{7,5},{8,10},{9,11},{10,... | collective-permute-start | bytes 5308424 | tf_op jit(solution)/shard_map/ppermute | solution.py:934
  155.3 9.7 %copy-start.6 = (bf16[3456,256]{1,0:T(8,128)(2,1)S(1)}, bf16[3456,256]{1,0:T(8,128)(2,1)}, u32[]{:S(2)}) copy-start(bf16[3456,256]{1,0:T(8,128)(2,1)} %get-tuple-element.240) | copy-start | bytes 5308420
  155.3 11.3 %collective-permute-start.11 = (bf16[576,256]{1,0:T(8,128)(2,1)}, bf16[576,256]{1,0:T(8,128)(2,1)S(1)}, u32[]{:S(2)}, u32[]{:S(2)}) collective-permute-start(bf16[576,256]{1,0:T(8,128)(2,1)} %get-tuple-element.387), channel_id=1, source_target_pairs={{0,8},{2,18},{4,12},{6,22},{8,0},{10,26},{12,4},{14,30},{16,24},{1... | collective-permute-start | bytes 884744 | tf_op jit(solution)/shard_map/ppermute | solution.py:934
  165.4 13.1 %collective-permute-start.9 = (bf16[1728,256]{1,0:T(8,128)(2,1)S(1)}, bf16[1728,256]{1,0:T(8,128)(2,1)S(1)}, u32[]{:S(2)}, u32[]{:S(2)}) collective-permute-start(bf16[1728,256]{1,0:T(8,128)(2,1)S(1)} %get-tuple-element.362), channel_id=1, source_target_pairs={{0,1},{1,0},{2,6},{3,7},{4,5},{5,4},{6,2},{7,3},{8,9},{9,8},{10,14... | collective-permute-start | bytes 2654216 | tf_op jit(solution)/shard_map/ppermute | solution.py:934
  166.6 20.3 %collective-permute-start.13 = (bf16[576,256]{1,0:T(8,128)(2,1)S(1)}, bf16[576,256]{1,0:T(8,128)(2,1)S(1)}, u32[]{:S(2)}, u32[]{:S(2)}) collective-permute-start(bf16[576,256]{1,0:T(8,128)(2,1)S(1)} %add_convert_fusion.17), channel_id=1, source_target_pairs={{0,8},{2,18},{4,12},{6,22},{8,0},{10,26},{12,4},{14,30},{16,24},{1... | collective-permute-start | bytes 884744 | tf_op jit(solution)/shard_map/ppermute | solution.py:934
  175.3 9.4 %collective-permute-start.14 = (bf16[576,256]{1,0:T(8,128)(2,1)S(1)}, bf16[576,256]{1,0:T(8,128)(2,1)S(1)}, u32[]{:S(2)}, u32[]{:S(2)}) collective-permute-start(bf16[576,256]{1,0:T(8,128)(2,1)S(1)} %get-tuple-element.385), channel_id=1, source_target_pairs={{0,8},{2,18},{4,12},{6,22},{8,0},{10,26},{12,4},{14,30},{16,24},{1... | collective-permute-start | bytes 884744 | tf_op jit(solution)/shard_map/ppermute | solution.py:934
  178.7 19.0 %collective-permute-start.17 = (bf16[864,256]{1,0:T(8,128)(2,1)S(1)}, bf16[864,256]{1,0:T(8,128)(2,1)S(1)}, u32[]{:S(2)}, u32[]{:S(2)}) collective-permute-start(bf16[864,256]{1,0:T(8,128)(2,1)S(1)} %get-tuple-element.375), channel_id=1, source_target_pairs={{0,4},{1,5},{2,3},{3,2},{4,0},{5,1},{6,7},{7,6},{8,12},{9,13},{10,... | collective-permute-start | bytes 1327112 | tf_op jit(solution)/shard_map/ppermute | solution.py:934
  184.7 14.2 %collective-permute-start.16 = (bf16[576,256]{1,0:T(8,128)(2,1)S(1)}, bf16[576,256]{1,0:T(8,128)(2,1)S(1)}, u32[]{:S(2)}, u32[]{:S(2)}) collective-permute-start(bf16[576,256]{1,0:T(8,128)(2,1)S(1)} %add_convert_fusion.14), channel_id=1, source_target_pairs={{0,8},{2,18},{4,12},{6,22},{8,0},{10,26},{12,4},{14,30},{16,24},{1... | collective-permute-start | bytes 884744 | tf_op jit(solution)/shard_map/ppermute | solution.py:934
  187.0 23.6 %collective-permute-start.15 = (bf16[1152,256]{1,0:T(8,128)(2,1)S(1)}, bf16[1152,256]{1,0:T(8,128)(2,1)S(1)}, u32[]{:S(2)}, u32[]{:S(2)}) collective-permute-start(bf16[1152,256]{1,0:T(8,128)(2,1)S(1)} %pad_maximum_fusion.7), channel_id=1, source_target_pairs={{0,16},{2,6},{4,20},{6,2},{8,24},{10,14},{12,28},{14,10},{16,0},{1... | collective-permute-start | bytes 1769480 | tf_op jit(solution)/shard_map/ppermute | solution.py:934
  190.3 20.5 %collective-permute-start.12 = (bf16[512,768]{1,0:T(8,128)(2,1)S(1)}, bf16[512,768]{1,0:T(8,128)(2,1)S(1)}, u32[]{:S(2)}, u32[]{:S(2)}) collective-permute-start(bf16[512,768]{1,0:T(8,128)(2,1)S(1)} %copy-done.18), channel_id=1, source_target_pairs={{1,0},{3,2},{5,4},{7,6},{9,8},{11,10},{13,12},{15,14},{17,16},{19,... | collective-permute-start | bytes 2359304 | tf_op jit(solution)/shard_map/ppermute | solution.py:1040
  197.7 24.2 %collective-permute-start.18 = (bf16[1280,256]{1,0:T(8,128)(2,1)}, bf16[1280,256]{1,0:T(8,128)(2,1)S(1)}, u32[]{:S(2)}, u32[]{:S(2)}) collective-permute-start(bf16[1280,256]{1,0:T(8,128)(2,1)} %get-tuple-element.264), channel_id=1, source_target_pairs={{0,2},{1,3},{2,0},{3,1},{4,6},{5,7},{6,4},{7,5},{8,10},{9,11},{10,... | collective-permute-start | bytes 1966088 | tf_op jit(solution)/shard_map/ppermute | solution.py:934
  197.9 26.0 %collective-permute-start.21 = (bf16[432,256]{1,0:T(8,128)(2,1)S(1)}, bf16[432,256]{1,0:T(8,128)(2,1)S(1)}, u32[]{:S(2)}, u32[]{:S(2)}) collective-permute-start(bf16[432,256]{1,0:T(8,128)(2,1)S(1)} %get-tuple-element.391), channel_id=1, source_target_pairs={{0,8},{1,9},{2,10},{3,11},{4,12},{5,13},{6,14},{7,15},{8,0},{9,1},... | collective-permute-start | bytes 663560 | tf_op jit(solution)/shard_map/ppermute | solution.py:934
  199.0 35.3 %collective-permute-start.23 = (bf16[1152,256]{1,0:T(8,128)(2,1)S(1)}, bf16[1152,256]{1,0:T(8,128)(2,1)}, u32[]{:S(2)}, u32[]{:S(2)}) collective-permute-start(bf16[1152,256]{1,0:T(8,128)(2,1)S(1)} %pad_maximum_fusion.8), channel_id=1, source_target_pairs={{0,16},{2,6},{4,20},{6,2},{8,24},{10,14},{12,28},{14,10},{16,0},{1... | collective-permute-start | bytes 1769480 | tf_op jit(solution)/shard_map/ppermute | solution.py:934
  210.7 16.3 %collective-permute-start.20 = (bf16[2304,256]{1,0:T(8,128)(2,1)S(1)}, bf16[2304,256]{1,0:T(8,128)(2,1)S(1)}, u32[]{:S(2)}, u32[]{:S(2)}) collective-permute-start(bf16[2304,256]{1,0:T(8,128)(2,1)S(1)} %pad_maximum_fusion.3), channel_id=1, source_target_pairs={{0,4},{2,10},{4,0},{6,14},{8,12},{10,2},{12,8},{14,6},{16,20},{18,... | collective-permute-start | bytes 3538952 | tf_op jit(solution)/shard_map/ppermute | solution.py:934
  223.8 7.4 %collective-permute-start.19 = (bf16[640,256]{1,0:T(8,128)(2,1)}, bf16[640,256]{1,0:T(8,128)(2,1)}, u32[]{:S(2)}, u32[]{:S(2)}) collective-permute-start(bf16[640,256]{1,0:T(8,128)(2,1)} %get-tuple-element.378), channel_id=1, source_target_pairs={{0,1},{1,0},{2,3},{3,2},{4,5},{5,4},{6,7},{7,6},{8,9},{9,8},{10,11... | collective-permute-start | bytes 983048 | tf_op jit(solution)/shard_map/ppermute | solution.py:934
  227.3 8.2 %copy-start.1 = (bf16[4608,256]{1,0:T(8,128)(2,1)}, bf16[4608,256]{1,0:T(8,128)(2,1)S(1)}, u32[]{:S(2)}) copy-start(bf16[4608,256]{1,0:T(8,128)(2,1)S(1)} %pad_maximum_fusion.value_ref) | copy-start | bytes 7077892
  227.3 28.7 %collective-permute-start.29 = (bf16[4608,256]{1,0:T(8,128)(2,1)S(1)}, bf16[4608,256]{1,0:T(8,128)(2,1)}, u32[]{:S(2)}, u32[]{:S(2)}) collective-permute-start(bf16[4608,256]{1,0:T(8,128)(2,1)S(1)} %pad_maximum_fusion.value_ref), channel_id=1, source_target_pairs={{0,2},{2,0},{4,6},{6,4},{8,10},{10,8},{12,14},{14,12},{16,18},{18,... | collective-permute-start | bytes 7077896 | tf_op jit(solution)/shard_map/ppermute | solution.py:934
  230.8 8.5 %collective-permute-start.25 = (bf16[216,256]{1,0:T(8,128)(2,1)}, bf16[216,256]{1,0:T(8,128)(2,1)S(1)}, u32[]{:S(2)}, u32[]{:S(2)}) collective-permute-start(bf16[216,256]{1,0:T(8,128)(2,1)} %get-tuple-element.403), channel_id=1, source_target_pairs={{0,16},{1,17},{2,18},{3,19},{4,20},{5,21},{6,22},{7,23},{8,24},{9,... | collective-permute-start | bytes 331784 | tf_op jit(solution)/shard_map/ppermute | solution.py:934
  232.3 5.4 %collective-permute-start.22 = (bf16[320,256]{1,0:T(8,128)(2,1)S(1)}, bf16[320,256]{1,0:T(8,128)(2,1)S(1)}, u32[]{:S(2)}, u32[]{:S(2)}) collective-permute-start(bf16[320,256]{1,0:T(8,128)(2,1)S(1)} %get-tuple-element.394), channel_id=1, source_target_pairs={{0,4},{1,5},{2,10},{3,11},{4,0},{5,1},{6,14},{7,15},{8,12},{9,13},... | collective-permute-start | bytes 491528 | tf_op jit(solution)/shard_map/ppermute | solution.py:934
  235.6 27.3 %collective-permute-start.31 = (bf16[2304,256]{1,0:T(8,128)(2,1)S(1)}, bf16[2304,256]{1,0:T(8,128)(2,1)}, u32[]{:S(2)}, u32[]{:S(2)}) collective-permute-start(bf16[2304,256]{1,0:T(8,128)(2,1)S(1)} %pad_maximum_fusion.4), channel_id=1, source_target_pairs={{0,4},{2,10},{4,0},{6,14},{8,12},{10,2},{12,8},{14,6},{16,20},{18,... | collective-permute-start | bytes 3538952 | tf_op jit(solution)/shard_map/ppermute | solution.py:934
  237.7 8.2 %collective-permute-start.24 = (bf16[160,256]{1,0:T(8,128)(2,1)S(1)}, bf16[160,256]{1,0:T(8,128)(2,1)S(1)}, u32[]{:S(2)}, u32[]{:S(2)}) collective-permute-start(bf16[160,256]{1,0:T(8,128)(2,1)S(1)} %get-tuple-element.406), channel_id=1, source_target_pairs={{0,8},{1,9},{2,6},{3,7},{4,12},{5,13},{6,2},{7,3},{8,0},{9,1},{10,... | collective-permute-start | bytes 245768 | tf_op jit(solution)/shard_map/ppermute | solution.py:934
  239.3 8.2 %collective-permute-start.27 = (bf16[216,256]{1,0:T(8,128)(2,1)S(1)}, bf16[216,256]{1,0:T(8,128)(2,1)S(1)}, u32[]{:S(2)}, u32[]{:S(2)}) collective-permute-start(bf16[216,256]{1,0:T(8,128)(2,1)S(1)} %add_convert_fusion.24), channel_id=1, source_target_pairs={{0,16},{1,17},{2,18},{3,19},{4,20},{5,21},{6,22},{7,23},{8,24},{9,... | collective-permute-start | bytes 331784 | tf_op jit(solution)/shard_map/ppermute | solution.py:934
  245.9 5.1 %collective-permute-start.26 = (bf16[80,256]{1,0:T(8,128)(2,1)S(1)}, bf16[80,256]{1,0:T(8,128)(2,1)S(1)}, u32[]{:S(2)}, u32[]{:S(2)}) collective-permute-start(bf16[80,256]{1,0:T(8,128)(2,1)S(1)} %get-tuple-element.412), channel_id=1, source_target_pairs={{0,16},{1,17},{2,18},{3,19},{4,20},{5,21},{6,22},{7,23},{8,24},{9,... | collective-permute-start | bytes 122888 | tf_op jit(solution)/shard_map/ppermute | solution.py:934
  251.6 8.0 %collective-permute-start.28 = (bf16[80,256]{1,0:T(8,128)(2,1)}, bf16[80,256]{1,0:T(8,128)(2,1)}, u32[]{:S(2)}, u32[]{:S(2)}) collective-permute-start(bf16[80,256]{1,0:T(8,128)(2,1)} %add_convert_fusion.29), channel_id=1, source_target_pairs={{0,16},{1,17},{2,18},{3,19},{4,20},{5,21},{6,22},{7,23},{8,24},{9,... | collective-permute-start | bytes 122888 | tf_op jit(solution)/shard_map/ppermute | solution.py:934
  253.5 8.5 %collective-permute-start.32 = (bf16[432,256]{1,0:T(8,128)(2,1)}, bf16[432,256]{1,0:T(8,128)(2,1)S(1)}, u32[]{:S(2)}, u32[]{:S(2)}) collective-permute-start(bf16[432,256]{1,0:T(8,128)(2,1)} %pad_maximum_fusion.11), channel_id=1, source_target_pairs={{0,8},{1,9},{2,10},{3,11},{4,12},{5,13},{6,14},{7,15},{8,0},{9,1},... | collective-permute-start | bytes 663560 | tf_op jit(solution)/shard_map/ppermute | solution.py:934
  264.5 11.1 %copy-start = (bf16[4608,256]{1,0:T(8,128)(2,1)}, bf16[4608,256]{1,0:T(8,128)(2,1)S(1)}, u32[]{:S(2)}) copy-start(bf16[4608,256]{1,0:T(8,128)(2,1)S(1)} %pad_maximum_fusion.1.value_ref) | copy-start | bytes 7077892
  264.5 17.5 %collective-permute-start.36 = (bf16[4608,256]{1,0:T(8,128)(2,1)S(1)}, bf16[4608,256]{1,0:T(8,128)(2,1)}, u32[]{:S(2)}, u32[]{:S(2)}) collective-permute-start(bf16[4608,256]{1,0:T(8,128)(2,1)S(1)} %pad_maximum_fusion.1.value_ref), channel_id=1, source_target_pairs={{0,2},{2,0},{4,6},{6,4},{8,10},{10,8},{12,14},{14,12},{16,18},{18,... | collective-permute-start | bytes 7077896 | tf_op jit(solution)/shard_map/ppermute | solution.py:934
  265.3 9.2 %collective-permute-start.34 = (bf16[864,256]{1,0:T(8,128)(2,1)}, bf16[864,256]{1,0:T(8,128)(2,1)S(1)}, u32[]{:S(2)}, u32[]{:S(2)}) collective-permute-start(bf16[864,256]{1,0:T(8,128)(2,1)} %pad_maximum_fusion.9), channel_id=1, source_target_pairs={{0,4},{1,5},{2,3},{3,2},{4,0},{5,1},{6,7},{7,6},{8,12},{9,13},{10,... | collective-permute-start | bytes 1327112 | tf_op jit(solution)/shard_map/ppermute | solution.py:934
  265.7 4.7 %collective-permute-start.30 = (bf16[160,256]{1,0:T(8,128)(2,1)}, bf16[160,256]{1,0:T(8,128)(2,1)S(1)}, u32[]{:S(2)}, u32[]{:S(2)}) collective-permute-start(bf16[160,256]{1,0:T(8,128)(2,1)} %pad_maximum_fusion.13), channel_id=1, source_target_pairs={{0,8},{1,9},{2,6},{3,7},{4,12},{5,13},{6,2},{7,3},{8,0},{9,1},{10,... | collective-permute-start | bytes 245768 | tf_op jit(solution)/shard_map/ppermute | solution.py:934
  271.3 9.0 %collective-permute-start.33 = (bf16[320,256]{1,0:T(8,128)(2,1)S(1)}, bf16[320,256]{1,0:T(8,128)(2,1)S(1)}, u32[]{:S(2)}, u32[]{:S(2)}) collective-permute-start(bf16[320,256]{1,0:T(8,128)(2,1)S(1)} %pad_maximum_fusion.12), channel_id=1, source_target_pairs={{0,4},{1,5},{2,10},{3,11},{4,0},{5,1},{6,14},{7,15},{8,12},{9,13},... | collective-permute-start | bytes 491528 | tf_op jit(solution)/shard_map/ppermute | solution.py:934
  275.6 21.4 %collective-permute-start.37 = (bf16[1728,256]{1,0:T(8,128)(2,1)S(1)}, bf16[1728,256]{1,0:T(8,128)(2,1)}, u32[]{:S(2)}, u32[]{:S(2)}) collective-permute-start(bf16[1728,256]{1,0:T(8,128)(2,1)S(1)} %pad_maximum_fusion.5), channel_id=1, source_target_pairs={{0,1},{1,0},{2,6},{3,7},{4,5},{5,4},{6,2},{7,3},{8,9},{9,8},{10,14... | collective-permute-start | bytes 2654216 | tf_op jit(solution)/shard_map/ppermute | solution.py:934
  281.1 14.8 %collective-permute-start.35 = (bf16[640,256]{1,0:T(8,128)(2,1)}, bf16[640,256]{1,0:T(8,128)(2,1)}, u32[]{:S(2)}, u32[]{:S(2)}) collective-permute-start(bf16[640,256]{1,0:T(8,128)(2,1)} %pad_maximum_fusion.10), channel_id=1, source_target_pairs={{0,1},{1,0},{2,3},{3,2},{4,5},{5,4},{6,7},{7,6},{8,9},{9,8},{10,11... | collective-permute-start | bytes 983048 | tf_op jit(solution)/shard_map/ppermute | solution.py:934
  298.7 4.6 %collective-permute-start.38 = (bf16[3456,256]{1,0:T(8,128)(2,1)S(1)}, bf16[3456,256]{1,0:T(8,128)(2,1)S(1)}, u32[]{:S(2)}, u32[]{:S(2)}) collective-permute-start(bf16[3456,256]{1,0:T(8,128)(2,1)S(1)} %pad_maximum_fusion.2.value_ref), channel_id=1, source_target_pairs={{0,2},{1,3},{2,0},{3,1},{4,6},{5,7},{6,4},{7,5},{8,10},{9,11},{10,... | collective-permute-start | bytes 5308424 | tf_op jit(solution)/shard_map/ppermute | solution.py:934
  298.8 9.1 %collective-permute-start.39 = (bf16[1280,256]{1,0:T(8,128)(2,1)S(1)}, bf16[1280,256]{1,0:T(8,128)(2,1)S(1)}, u32[]{:S(2)}, u32[]{:S(2)}) collective-permute-start(bf16[1280,256]{1,0:T(8,128)(2,1)S(1)} %pad_maximum_fusion.6.mine_ref), channel_id=1, source_target_pairs={{0,2},{1,3},{2,0},{3,1},{4,6},{5,7},{6,4},{7,5},{8,10},{9,11},{10,... | collective-permute-start | bytes 1966088 | tf_op jit(solution)/shard_map/ppermute | solution.py:934
  (12 other events, 24.5 us)

commit v11 on v10

--- a/solution.py
+++ b/solution.py
@@ -1179,12 +1179,12 @@
     outputs = unpack(1 - side, 0, a.got, outputs)
     p.step()
     s.step()
+    p.step()
     c.step()
+    s.step()
     p.step()
-    s.step()
     c.finish()
     outputs = unpack(side, 2, c.mine, outputs)
-    p.step()
     reduce_grad, expand_grad = unpack(1 - side, 2, c.got, outputs)
     p.finish()
     s.step()

time: 318 us -> 318 us (level)
  waiting for transfers between devices: 36.8 us -> 40.1 us
    ppermute x36, waiting for transfers between devices: 36.8 us -> 40.1 us  [swap(): lax.ppermute(value, axes, [(source, pair_of(source)) for source in range(...]
  transfers between devices with their start and end apart: 40 -> 40, of which waited for: 11 -> 12; matrix products, arithmetic and copies ran while one was open for 7% -> 6% of each run, Pallas kernels for 40% -> 40%
where the time goes in v11:
time: 318 us; the launch traced here: 313 us
  Pallas kernels  190 us (60%)
  starting transfers between devices  50.7 us (16%)
  waiting for transfers between devices  40.1 us (13%)
  other arithmetic  22.7 us (7%)
  local copies, waits for them, and re-layouts  7.84 us (2%)
    pallas_call x23, Pallas kernels, call(): pl.pallas_call(kernel, grid_spec=pltpu.PrefetchScalarGridSpec(num_scalar_...  190 us
    ppermute x36, starting transfers between devices, swap(): lax.ppermute(value, axes, [(source, pair_of(source)) for source in range(...  42 us
    ppermute x36, waiting for transfers between devices, swap(): lax.ppermute(value, axes, [(source, pair_of(source)) for source in range(...  40.1 us
    convert_element_type x14, other arithmetic, part(): return (cut(self.terms[0]) + cut(self.terms[1])).astype(bf16)  11.5 us
    ppermute x3, starting transfers between devices, on_device(): to_text = lambda value: lax.ppermute(value, 'mod', [(0, 1)])  7.5 us
    select_n x14, other arithmetic, step(): low = jnp.where(self.last == 0, mine, got)  7.42 us
  transfers between devices with their start and end apart: 40, of which 12 were waited for; matrix products, arithmetic and copies ran while one was open for 6% of the time, Pallas kernels for 40%

profile of v11, /device:TPU:0, one launch (start us, length us, event | category | flops | bytes accessed | tf_op | source)
XLA Modules:
  0.0 312.8 jit_solution(11321161428139464674)
XLA Ops:
  1.8 4.9 %collective-permute-start = (bf16[256,768]{1,0:T(8,128)(2,1)S(1)}, bf16[256,768]{1,0:T(8,128)(2,1)S(1)}, u32[]{:S(2)}, u32[]{:S(2)}) collective-permute-start(bf16[256,768]{1,0:T(8,128)(2,1)S(1)} %get-tuple-element.377), channel_id=1, source_target_pairs={{0,1},{2,3},{4,5},{6,7},{8,9},{10,11},{12,13},{14,15},{16,17},{18,... | collective-permute-start | bytes 1179656 | tf_op jit(solution)/shard_map/ppermute | solution.py:1039
  9.4 8.5 %project_rows.1 = (bf16[1024,768]{1,0:T(8,128)(2,1)}, bf16[1024,2304]{1,0:T(8,128)(2,1)}) custom-call(bf16[1024,768]{1,0:T(8,128)(2,1)} %bitcast.20, f32[1,768]{1,0:T(1,128)} %gain_ref.9, f32[1,768]{1,0:T(1,128)} %shift_ref.6, bf16[768,2304]{1,0:T(8,128)(2,1)} %weight_ref.3, f32[2,768]{1,0:T(2,128)} %bias_ref.5), custom_call_target="tpu_custom_call" | custom-call | flops 3623878656 | bytes 11403264 | tf_op jit(solution)/shard_map/project_rows/pallas_call | solution.py:83
  19.3 3.9 %image_rows.2 = (bf16[512,768]{1,0:T(8,128)(2,1)}, bf16[512,1536]{1,0:T(8,128)(2,1)}) custom-call(s32[1]{0:T(128)} %bitcast.flag_ref, bf16[1024,768]{1,0:T(8,128)(2,1)} %bitcast.21, bf16[256,768]{1,0:T(8,128)(2,1)} %copy-done.13, f32[1,768]{1,0:T(1,128)} %gain_ref.9, f32[1,768]{1,0:T(1,128)} %shift_ref.6, f32[2,768]{1,0:T(2,128)} %copy-done.16, ...), custom_call_target="tpu_custom_call" | custom-call | flops 603979776 | bytes 6291456 | tf_op jit(solution)/shard_map/image_rows/pallas_call | solution.py:83
  23.2 12.3 %attend_forward.2 = (bf16[512,768]{1,0:T(8,128)(2,1)}, f32[6,2,512]{2,1,0:T(2,128)}) custom-call(s32[1]{0:T(128)} %bitcast.flag_ref, s32[2]{0:T(128)} %count_ref.17, s32[2,4]{1,0:T(2,128)} %lengths_ref.15, bf16[1024,2304]{1,0:T(8,128)(2,1)} %get-tuple-element.244.q_ref.k_ref.v_ref, bf16[1024,2304]{1,0:T(8,128)(2,1)} %get-tuple-element.244.q_ref.k_ref.v_ref, ...), custom_call_target="tpu_custom_call" | custom-call | flops 4831838208 | bytes 6291456 | tf_op jit(solution)/shard_map/attend_forward/pallas_call | solution.py:83
  36.2 3.8 %image_rows.3 = (bf16[512,768]{1,0:T(8,128)(2,1)}, bf16[512,1536]{1,0:T(8,128)(2,1)}) custom-call(s32[1]{0:T(128)} %bitcast.flag_ref, bf16[1024,768]{1,0:T(8,128)(2,1)} %bitcast.22, bf16[256,768]{1,0:T(8,128)(2,1)} %copy-done.12, f32[1,768]{1,0:T(1,128)} %gain_ref.9, f32[1,768]{1,0:T(1,128)} %shift_ref.6, ...), custom_call_target="tpu_custom_call", output_to_operand_aliasing={{0}: (9, {}), {1}: (10, {})} | custom-call | flops 603979776 | bytes 6291456 | tf_op jit(solution)/shard_map/image_rows/pallas_call | solution.py:83
  40.0 12.3 %attend_forward.3 = (bf16[512,768]{1,0:T(8,128)(2,1)}, f32[6,2,512]{2,1,0:T(2,128)}) custom-call(s32[1]{0:T(128)} %bitcast.flag_ref, s32[2]{0:T(128)} %count_ref.17, s32[2,4]{1,0:T(2,128)} %lengths_ref.15, bf16[1024,2304]{1,0:T(8,128)(2,1)} %get-tuple-element.244.q_ref.k_ref.v_ref, bf16[1024,2304]{1,0:T(8,128)(2,1)} %get-tuple-element.244.q_ref.k_ref.v_ref, ...), custom_call_target="tpu_custom_call" | custom-call | flops 4831838208 | bytes 6291456 | tf_op jit(solution)/shard_map/attend_forward/pallas_call | solution.py:83
  52.3 45.2 %feed_forward.1 = (bf16[1024,768]{1,0:T(8,128)(2,1)}, f32[1024,768]{1,0:T(8,128)}, bf16[1024,768]{1,0:T(8,128)(2,1)}, bf16[768,768]{1,0:T(8,128)(2,1)}, f32[8,76...) custom-call(s32[1]{0:T(128)} %bitcast.flag_ref, ...), custom_call_target="tpu_custom_call" | custom-call | flops 28991029248 | bytes 41943040 | tf_op jit(solution)/shard_map/feed_forward/pallas_call | solution.py:83
  98.1 8.2 %attend_backward.6 = (bf16[1024,768]{1,0:T(8,128)(2,1)}, bf16[1024,768]{1,0:T(8,128)(2,1)}, bf16[1024,768]{1,0:T(8,128)(2,1)}, bf16[512,768]{1,0:T(8,128)(2,1)}, bf16[512,768]{1,0:T(8,128)(2,1)}) custom-call(s32[1]{0:T(128)} %bitcast.flag_ref, s32[2]{0:T(128)} %count_ref.17, s32[2,4]{1,0:T(2,128)} %lengths_ref.15, ...), custom_call_target="tpu_custom_call" | custom-call | flops 40265318400 | bytes 41943040 | tf_op jit(solution)/shard_map/attend_backward/pallas_call | solution.py:83
  106.3 1.6 add_convert_fusion
  109.4 8.2 %attend_backward.7 = (bf16[1024,768]{1,0:T(8,128)(2,1)}, bf16[1024,768]{1,0:T(8,128)(2,1)}, bf16[1024,768]{1,0:T(8,128)(2,1)}, bf16[512,768]{1,0:T(8,128)(2,1)}, bf16[512,768]{1,0:T(8,128)(2,1)}) custom-call(s32[1]{0:T(128)} %bitcast.flag_ref, s32[2]{0:T(128)} %count_ref.17, ...), custom_call_target="tpu_custom_call", output_to_operand_aliasing={{0}: (11, {}), {1}: (12, {}), {2}: (13, {}), {3}: (14, {}),... | custom-call | flops 40265318400 | bytes 41943040 | tf_op jit(solution)/shard_map/attend_backward/pallas_call | solution.py:83
  117.6 1.6 add_convert_fusion.1
  119.8 8.1 %attend_backward.8 = (bf16[1024,768]{1,0:T(8,128)(2,1)}, bf16[1024,768]{1,0:T(8,128)(2,1)}, bf16[1024,768]{1,0:T(8,128)(2,1)}, bf16[512,768]{1,0:T(8,128)(2,1)}, bf16[512,768]{1,0:T(8,128)(2,1)}) custom-call(s32[1]{0:T(128)} %bitcast.flag_ref, s32[2]{0:T(128)} %count_ref.17, ...), custom_call_target="tpu_custom_call", output_to_operand_aliasing={{0}: (11, {}), {1}: (12, {}), {2}: (13, {}), {3}: (14, {}),... | custom-call | flops 40265318400 | bytes 41943040 | tf_op jit(solution)/shard_map/attend_backward/pallas_call | solution.py:83
  130.4 2.7 collective-permute-start.8
  133.1 8.3 %attend_backward.9 = (bf16[1024,768]{1,0:T(8,128)(2,1)}, bf16[1024,768]{1,0:T(8,128)(2,1)}, bf16[1024,768]{1,0:T(8,128)(2,1)}, bf16[512,768]{1,0:T(8,128)(2,1)}, bf16[512,768]{1,0:T(8,128)(2,1)}) custom-call(s32[1]{0:T(128)} %bitcast.flag_ref, s32[2]{0:T(128)} %count_ref.17, ...), custom_call_target="tpu_custom_call", output_to_operand_aliasing={{0}: (11, {}), {1}: (12, {}), {2}: (13, {}), {3}: (14, {}),... | custom-call | flops 40265318400 | bytes 41943040 | tf_op jit(solution)/shard_map/attend_backward/pallas_call | solution.py:83
  142.6 2.4 collective-permute-start.10
  145.0 9.3 %weight_grads.2 = (f32[2,512]{1,0:T(2,128)}, bf16[3456,256]{1,0:T(8,128)(2,1)}, bf16[3456,256]{1,0:T(8,128)(2,1)}) custom-call(s32[1]{0:T(128)} %bitcast.1.side_ref.half_ref, bf16[1024,768]{1,0:T(8,128)(2,1)} %get-tuple-element.260.normed_ref, bf16[512,768]{1,0:T(8,128)(2,1)} %get-tuple-element.228.image_ref, ...), custom_call_target="tpu_custom_call" | custom-call | flops 32212254720 | bytes 125829120 | tf_op jit(solution)/shard_map/weight_grads/pallas_call | solution.py:83
  155.3 1.6 collective-permute-start.11
  156.8 8.1 %attend_backward.10 = (bf16[1024,768]{1,0:T(8,128)(2,1)}, bf16[1024,768]{1,0:T(8,128)(2,1)}, bf16[1024,768]{1,0:T(8,128)(2,1)}, bf16[512,768]{1,0:T(8,128)(2,1)}, bf16[512,768]{1,0:T(8,128)(2,1)}) custom-call(s32[1]{0:T(128)} %bitcast.flag_ref, s32[2]{0:T(128)} %count_ref.17, ...), custom_call_target="tpu_custom_call", output_to_operand_aliasing={{0}: (11, {}), {1}: (12, {}), {2}: (13, {}), {3}: (14, {}),... | custom-call | flops 40265318400 | bytes 41943040 | tf_op jit(solution)/shard_map/attend_backward/pallas_call | solution.py:83
  166.7 8.4 %attend_backward.11 = (bf16[1024,768]{1,0:T(8,128)(2,1)}, bf16[1024,768]{1,0:T(8,128)(2,1)}, bf16[1024,768]{1,0:T(8,128)(2,1)}, bf16[512,768]{1,0:T(8,128)(2,1)}, bf16[512,768]{1,0:T(8,128)(2,1)}) custom-call(s32[1]{0:T(128)} %bitcast.flag_ref, s32[2]{0:T(128)} %count_ref.17, ...), custom_call_target="tpu_custom_call", output_to_operand_aliasing={{0}: (11, {}), {1}: (12, {}), {2}: (13, {}), {3}: (14, {}),... | custom-call | flops 40265318400 | bytes 41943040 | tf_op jit(solution)/shard_map/attend_backward/pallas_call | solution.py:83
  175.3 2.1 collective-permute-start.14
  180.3 4.4 %image_grads.1.near_ref = bf16[512,768]{1,0:T(8,128)(2,1)} custom-call(bf16[768,2304]{1,0:T(8,128)(2,1)} %weight_ref.3, bf16[768,2304]{1,0:T(8,128)(2,1)} %weight_ref.3, bf16[512,768]{1,0:T(8,128)(2,1)} %get-tuple-element.255.keys_ref.gik_ref, bf16[512,768]{1,0:T(8,128)(2,1)} %get-tuple-element.249.values_ref.giv_ref), custom_call_target="tpu_custom_call" | custom-call | flops 12079595520 | bytes 62914560 | tf_op jit(solution)/shard_map/image_grads/pallas_call | solution.py:83
  184.7 2.1 collective-permute-start.16
  187.0 3.3 %collective-permute-start.15 = (bf16[1152,256]{1,0:T(8,128)(2,1)S(1)}, bf16[1152,256]{1,0:T(8,128)(2,1)S(1)}, u32[]{:S(2)}, u32[]{:S(2)}) collective-permute-start(bf16[1152,256]{1,0:T(8,128)(2,1)S(1)} %pad_maximum_fusion.7), channel_id=1, source_target_pairs={{0,16},{2,6},{4,20},{6,2},{8,24},{10,14},{12,28},{14,10},{16,0},{1... | collective-permute-start | bytes 1769480 | tf_op jit(solution)/shard_map/ppermute | solution.py:934
  191.6 6.1 %weight_grads.3 = (f32[2,256]{1,0:T(2,128)}, bf16[1280,256]{1,0:T(8,128)(2,1)}, bf16[1280,256]{1,0:T(8,128)(2,1)}) custom-call(s32[1]{0:T(128)} %bitcast.1.side_ref.half_ref, bf16[1024,768]{1,0:T(8,128)(2,1)} %get-tuple-element.260.normed_ref, bf16[512,768]{1,0:T(8,128)(2,1)} %get-tuple-element.228.image_ref, bf16[1024,768]{1,0:T(8,128)(2,1)} %get-tuple-element.261.gq_ref, ...), custom_call_target="tpu_custom_call" | custom-call | flops 16106127360 | bytes 125829120 | tf_op jit(solution)/shard_map/weight_grads/pallas_call | solution.py:83
  199.1 11.4 %collective-permute-done.15 = bf16[1152,256]{1,0:T(8,128)(2,1)S(1)} collective-permute-done((bf16[1152,256]{1,0:T(8,128)(2,1)S(1)}, bf16[1152,256]{1,0:T(8,128)(2,1)S(1)}, u32[]{:S(2)}, u32[]{:S(2)}) %collective-permute-start.15) | collective-permute-done | bytes 589856 | tf_op jit(solution)/shard_map/ppermute | solution.py:934
  211.7 10.1 %finish_rows.1 = (bf16[1024,768]{1,0:T(8,128)(2,1)}, bf16[1280,256]{1,0:T(8,128)(2,1)}) custom-call(s32[1]{0:T(128)} %bitcast.flag_ref, bf16[1024,768]{1,0:T(8,128)(2,1)} %bitcast.24, f32[1024,768]{1,0:T(8,128)} %get-tuple-element.273.gmid_ref, bf16[512,768]{1,0:T(8,128)(2,1)} %image_grads.1.near_ref, ...), custom_call_target="tpu_custom_call", output_to_operand_aliasing={{1}: (13, {})} | custom-call | flops 36238786560 | bytes 167772160 | tf_op jit(solution)/shard_map/finish_rows/pallas_call | solution.py:83
  221.8 2.0 add_convert_fusion.12
  224.6 2.4 collective-permute-done.20
  227.3 3.5 %collective-permute-start.29 = (bf16[4608,256]{1,0:T(8,128)(2,1)S(1)}, bf16[4608,256]{1,0:T(8,128)(2,1)}, u32[]{:S(2)}, u32[]{:S(2)}) collective-permute-start(bf16[4608,256]{1,0:T(8,128)(2,1)S(1)} %pad_maximum_fusion.value_ref), channel_id=1, source_target_pairs={{0,2},{2,0},{4,6},{6,4},{8,10},{10,8},{12,14},{14,12},{16,18},{18,... | collective-permute-start | bytes 7077896 | tf_op jit(solution)/shard_map/ppermute | solution.py:934
  232.3 2.1 collective-permute-start.22
  235.7 2.0 collective-permute-done.22
  237.7 1.6 collective-permute-start.24
  239.3 3.0 collective-permute-start.27
  242.3 3.6 %expert_outputs.4 = (f32[3072,768]{1,0:T(8,128)}, f32[768,3072]{1,0:T(8,128)}) custom-call(s32[1]{0:T(128)} %bitcast.1.side_ref.half_ref, bf16[4608,256]{1,0:T(8,128)(2,1)} %copy-done.1), custom_call_target="tpu_custom_call" | custom-call | flops 1179648 | bytes 7077888 | tf_op jit(solution)/shard_map/expert_outputs/pallas_call | solution.py:83
  245.9 1.6 collective-permute-start.26
  248.2 2.8 collective-permute-done.26
  251.6 1.9 collective-permute-start.28
  253.5 2.5 collective-permute-start.31
  256.0 3.6 %expert_outputs.5 = (f32[3072,768]{1,0:T(8,128)}, f32[768,3072]{1,0:T(8,128)}) custom-call(s32[1]{0:T(128)S(6)} %sub.49.half_ref, bf16[4608,256]{1,0:T(8,128)(2,1)} %collective-permute-done.29.value_ref, f32[3072,768]{1,0:T(8,128)} %get-tuple-element.303.refs_0_, f32[768,3072]{1,0:T(8,128)} %get-tuple-element.295.refs_1_), custom_call_target="tpu_custom_call", output_to_operand_aliasing={{0}: (2, {}), {1}: (3, {})} | custom-call | flops 1179648 | bytes 7077888 | tf_op jit(solution)/shard_map/expert_outputs/pallas_call | solution.py:83
  262.1 2.8 collective-permute-done.30
  267.7 1.7 collective-permute-start.32
  269.4 6.3 %collective-permute-done.33 = bf16[864,256]{1,0:T(8,128)(2,1)S(1)} collective-permute-done((bf16[864,256]{1,0:T(8,128)(2,1)S(1)}, bf16[864,256]{1,0:T(8,128)(2,1)S(1)}, u32[]{:S(2)}, u32[]{:S(2)}) %collective-permute-start.33) | collective-permute-done | bytes 442400 | tf_op jit(solution)/shard_map/ppermute | solution.py:934
  280.6 3.6 %expert_outputs.6 = (f32[3072,768]{1,0:T(8,128)}, f32[768,3072]{1,0:T(8,128)}) custom-call(s32[1]{0:T(128)} %bitcast.1.side_ref.half_ref, bf16[4608,256]{1,0:T(8,128)(2,1)} %copy-done, f32[3072,768]{1,0:T(8,128)} %get-tuple-element.318.refs_0_, f32[768,3072]{1,0:T(8,128)} %get-tuple-element.304.refs_1_), custom_call_target="tpu_custom_call", output_to_operand_aliasing={{0}: (2, {}), {1}: (3, {})} | custom-call | flops 1179648 | bytes 7077888 | tf_op jit(solution)/shard_map/expert_outputs/pallas_call | solution.py:83
  284.1 3.6 %expert_outputs.7 = (f32[3072,768]{1,0:T(8,128)}, f32[768,3072]{1,0:T(8,128)}) custom-call(s32[1]{0:T(128)S(6)} %sub.49.half_ref, bf16[4608,256]{1,0:T(8,128)(2,1)} %collective-permute-done.36.value_ref, f32[3072,768]{1,0:T(8,128)} %get-tuple-element.321.refs_0_, f32[768,3072]{1,0:T(8,128)} %get-tuple-element.319.refs_1_), custom_call_target="tpu_custom_call", output_to_operand_aliasing={{0}: (2, {}), {1}: (3, {})} | custom-call | flops 1179648 | bytes 7077888 | tf_op jit(solution)/shard_map/expert_outputs/pallas_call | solution.py:83
  287.7 8.4 %collective-permute-done.35 = bf16[640,256]{1,0:T(8,128)(2,1)} collective-permute-done((bf16[640,256]{1,0:T(8,128)(2,1)}, bf16[640,256]{1,0:T(8,128)(2,1)}, u32[]{:S(2)}, u32[]{:S(2)}) %collective-permute-start.35) | collective-permute-done | bytes 327712 | tf_op jit(solution)/shard_map/ppermute | solution.py:934
  300.1 3.4 %first_outputs.2 = (f32[768,2304]{1,0:T(8,128)}, f32[768,768]{1,0:T(8,128)}) custom-call(s32[1]{0:T(128)} %bitcast.1.side_ref.half_ref, bf16[3456,256]{1,0:T(8,128)(2,1)} %copy-done.2), custom_call_target="tpu_custom_call" | custom-call | flops 884736 | bytes 5308416 | tf_op jit(solution)/shard_map/first_outputs/pallas_call | solution.py:83
  304.7 3.4 %first_outputs.3 = (f32[768,2304]{1,0:T(8,128)}, f32[768,768]{1,0:T(8,128)}) custom-call(s32[1]{0:T(128)S(6)} %sub.49.half_ref, bf16[3456,256]{1,0:T(8,128)(2,1)} %copy-done.7, f32[768,2304]{1,0:T(8,128)} %get-tuple-element.330.refs_0_, f32[768,768]{1,0:T(8,128)} %get-tuple-element.328.refs_1_), custom_call_target="tpu_custom_call", output_to_operand_aliasing={{0}: (2, {}), {1}: (3, {})} | custom-call | flops 884736 | bytes 5308416 | tf_op jit(solution)/shard_map/first_outputs/pallas_call | solution.py:83
  309.0 3.4 %last_outputs.1 = (f32[768,2304]{1,0:T(8,128)}, f32[1,768]{1,0:T(1,128)}, f32[1,768]{1,0:T(1,128)}, f32[1,768]{1,0:T(1,128)}, f32[1,768]{1,0:T(1,128)}, /*index=...) custom-call(s32[1]{0:T(128)} %bitcast.1.side_ref.half_ref, ...), custom_call_target="tpu_custom_call", output_to_operand_aliasing={{0}: (4, {})} | custom-call | flops 327680 | bytes 1966080 | tf_op jit(solution)/shard_map/last_outputs/pallas_call | solution.py:83
  (144 shorter events, 43.3 us)
Async XLA Ops:
  0.6 6.1 %copy-start.15 = (f32[1,768]{1,0:T(1,128)S(1)}, f32[1,768]{1,0:T(1,128)}, u32[]{:S(2)}) copy-start(f32[1,768]{1,0:T(1,128)} %gain_ref.9) | copy-start | bytes 9220
  0.7 6.1 %copy-start.14 = (f32[1,768]{1,0:T(1,128)S(1)}, f32[1,768]{1,0:T(1,128)}, u32[]{:S(2)}) copy-start(f32[1,768]{1,0:T(1,128)} %shift_ref.6) | copy-start | bytes 9220
  1.8 16.7 %collective-permute-start = (bf16[256,768]{1,0:T(8,128)(2,1)S(1)}, bf16[256,768]{1,0:T(8,128)(2,1)S(1)}, u32[]{:S(2)}, u32[]{:S(2)}) collective-permute-start(bf16[256,768]{1,0:T(8,128)(2,1)S(1)} %get-tuple-element.377), channel_id=1, source_target_pairs={{0,1},{2,3},{4,5},{6,7},{8,9},{10,11},{12,13},{14,15},{16,17},{18,... | collective-permute-start | bytes 1179656 | tf_op jit(solution)/shard_map/ppermute | solution.py:1039
  6.8 11.7 %collective-permute-start.1 = (f32[2,768]{1,0:T(2,128)S(1)}, f32[2,768]{1,0:T(2,128)S(1)}, u32[]{:S(2)}, u32[]{:S(2)}) collective-permute-start(f32[2,768]{1,0:T(2,128)S(1)} %pad_maximum_fusion.14), channel_id=1, source_target_pairs={{0,1},{2,3},{4,5},{6,7},{8,9},{10,11},{12,13},{14,15},{16,17},{18,... | collective-permute-start | bytes 18440 | tf_op jit(solution)/shard_map/ppermute | solution.py:1039
  8.1 27.3 %collective-permute-start.2 = (bf16[256,768]{1,0:T(8,128)(2,1)S(1)}, bf16[256,768]{1,0:T(8,128)(2,1)S(1)}, u32[]{:S(2)}, u32[]{:S(2)}) collective-permute-start(bf16[256,768]{1,0:T(8,128)(2,1)S(1)} %get-tuple-element.376), channel_id=1, source_target_pairs={{0,1},{2,3},{4,5},{6,7},{8,9},{10,11},{12,13},{14,15},{16,17},{18,... | collective-permute-start | bytes 1179656 | tf_op jit(solution)/shard_map/ppermute | solution.py:1039
  9.4 8.5 %copy-start.17 = (f32[768]{0:T(1024)S(1)}, f32[768]{0:T(1024)}, u32[]{:S(2)}) copy-start(f32[768]{0:T(1024)} %param.24) | copy-start | bytes 9220
  97.5 20.1 %collective-permute-start.3 = (bf16[4608,256]{1,0:T(8,128)(2,1)}, bf16[4608,256]{1,0:T(8,128)(2,1)S(1)}, u32[]{:S(2)}, u32[]{:S(2)}) collective-permute-start(bf16[4608,256]{1,0:T(8,128)(2,1)} %get-tuple-element.195), channel_id=1, source_target_pairs={{0,2},{2,0},{4,6},{6,4},{8,10},{10,8},{12,14},{14,12},{16,18},{18,... | collective-permute-start | bytes 7077896 | tf_op jit(solution)/shard_map/ppermute | solution.py:934
  97.6 8.7 %collective-permute-start.4 = (bf16[4608,256]{1,0:T(8,128)(2,1)}, bf16[4608,256]{1,0:T(8,128)(2,1)S(1)}, u32[]{:S(2)}, u32[]{:S(2)}) collective-permute-start(bf16[4608,256]{1,0:T(8,128)(2,1)} %get-tuple-element.197), channel_id=1, source_target_pairs={{0,2},{2,0},{4,6},{6,4},{8,10},{10,8},{12,14},{14,12},{16,18},{18,... | collective-permute-start | bytes 7077896 | tf_op jit(solution)/shard_map/ppermute | solution.py:934
  98.1 8.2 %copy-start.5 = (bf16[4608,256]{1,0:T(8,128)(2,1)S(1)}, bf16[4608,256]{1,0:T(8,128)(2,1)}, u32[]{:S(2)}) copy-start(bf16[4608,256]{1,0:T(8,128)(2,1)} %get-tuple-element.201) | copy-start | bytes 7077892
  107.9 20.0 %collective-permute-start.6 = (bf16[2304,256]{1,0:T(8,128)(2,1)}, bf16[2304,256]{1,0:T(8,128)(2,1)S(1)}, u32[]{:S(2)}, u32[]{:S(2)}) collective-permute-start(bf16[2304,256]{1,0:T(8,128)(2,1)} %get-tuple-element.359), channel_id=1, source_target_pairs={{0,4},{2,10},{4,0},{6,14},{8,12},{10,2},{12,8},{14,6},{16,20},{18,... | collective-permute-start | bytes 3538952 | tf_op jit(solution)/shard_map/ppermute | solution.py:934
  109.4 8.2 %copy-start.4 = (bf16[4608,256]{1,0:T(8,128)(2,1)S(1)}, bf16[4608,256]{1,0:T(8,128)(2,1)}, u32[]{:S(2)}) copy-start(bf16[4608,256]{1,0:T(8,128)(2,1)} %get-tuple-element.209) | copy-start | bytes 7077892
  119.2 22.2 %collective-permute-start.5 = (bf16[2304,256]{1,0:T(8,128)(2,1)}, bf16[2304,256]{1,0:T(8,128)(2,1)S(1)}, u32[]{:S(2)}, u32[]{:S(2)}) collective-permute-start(bf16[2304,256]{1,0:T(8,128)(2,1)} %get-tuple-element.360), channel_id=1, source_target_pairs={{0,4},{2,10},{4,0},{6,14},{8,12},{10,2},{12,8},{14,6},{16,20},{18,... | collective-permute-start | bytes 3538952 | tf_op jit(solution)/shard_map/ppermute | solution.py:934
  130.4 23.9 %collective-permute-start.8 = (bf16[1152,256]{1,0:T(8,128)(2,1)S(1)}, bf16[1152,256]{1,0:T(8,128)(2,1)S(1)}, u32[]{:S(2)}, u32[]{:S(2)}) collective-permute-start(bf16[1152,256]{1,0:T(8,128)(2,1)S(1)} %get-tuple-element.371), channel_id=1, source_target_pairs={{0,16},{2,6},{4,20},{6,2},{8,24},{10,14},{12,28},{14,10},{16,0},{1... | collective-permute-start | bytes 1769480 | tf_op jit(solution)/shard_map/ppermute | solution.py:934
  142.6 32.5 %collective-permute-start.10 = (bf16[1152,256]{1,0:T(8,128)(2,1)}, bf16[1152,256]{1,0:T(8,128)(2,1)S(1)}, u32[]{:S(2)}, u32[]{:S(2)}) collective-permute-start(bf16[1152,256]{1,0:T(8,128)(2,1)} %get-tuple-element.369), channel_id=1, source_target_pairs={{0,16},{2,6},{4,20},{6,2},{8,24},{10,14},{12,28},{14,10},{16,0},{1... | collective-permute-start | bytes 1769480 | tf_op jit(solution)/shard_map/ppermute | solution.py:934
  154.3 10.6 %collective-permute-start.7 = (bf16[3456,256]{1,0:T(8,128)(2,1)}, bf16[3456,256]{1,0:T(8,128)(2,1)S(1)}, u32[]{:S(2)}, u32[]{:S(2)}) collective-permute-start(bf16[3456,256]{1,0:T(8,128)(2,1)} %get-tuple-element.235), channel_id=1, source_target_pairs={{0,2},{1,3},{2,0},{3,1},{4,6},{5,7},{6,4},{7,5},{8,10},{9,11},{10,... | collective-permute-start | bytes 5308424 | tf_op jit(solution)/shard_map/ppermute | solution.py:934
  155.3 9.7 %copy-start.6 = (bf16[3456,256]{1,0:T(8,128)(2,1)S(1)}, bf16[3456,256]{1,0:T(8,128)(2,1)}, u32[]{:S(2)}) copy-start(bf16[3456,256]{1,0:T(8,128)(2,1)} %get-tuple-element.240) | copy-start | bytes 5308420
  155.3 11.3 %collective-permute-start.11 = (bf16[576,256]{1,0:T(8,128)(2,1)}, bf16[576,256]{1,0:T(8,128)(2,1)S(1)}, u32[]{:S(2)}, u32[]{:S(2)}) collective-permute-start(bf16[576,256]{1,0:T(8,128)(2,1)} %get-tuple-element.387), channel_id=1, source_target_pairs={{0,8},{2,18},{4,12},{6,22},{8,0},{10,26},{12,4},{14,30},{16,24},{1... | collective-permute-start | bytes 884744 | tf_op jit(solution)/shard_map/ppermute | solution.py:934
  165.4 13.1 %collective-permute-start.9 = (bf16[1728,256]{1,0:T(8,128)(2,1)S(1)}, bf16[1728,256]{1,0:T(8,128)(2,1)S(1)}, u32[]{:S(2)}, u32[]{:S(2)}) collective-permute-start(bf16[1728,256]{1,0:T(8,128)(2,1)S(1)} %get-tuple-element.362), channel_id=1, source_target_pairs={{0,1},{1,0},{2,6},{3,7},{4,5},{5,4},{6,2},{7,3},{8,9},{9,8},{10,14... | collective-permute-start | bytes 2654216 | tf_op jit(solution)/shard_map/ppermute | solution.py:934
  166.6 20.3 %collective-permute-start.13 = (bf16[576,256]{1,0:T(8,128)(2,1)S(1)}, bf16[576,256]{1,0:T(8,128)(2,1)S(1)}, u32[]{:S(2)}, u32[]{:S(2)}) collective-permute-start(bf16[576,256]{1,0:T(8,128)(2,1)S(1)} %add_convert_fusion.17), channel_id=1, source_target_pairs={{0,8},{2,18},{4,12},{6,22},{8,0},{10,26},{12,4},{14,30},{16,24},{1... | collective-permute-start | bytes 884744 | tf_op jit(solution)/shard_map/ppermute | solution.py:934
  175.3 9.4 %collective-permute-start.14 = (bf16[576,256]{1,0:T(8,128)(2,1)S(1)}, bf16[576,256]{1,0:T(8,128)(2,1)S(1)}, u32[]{:S(2)}, u32[]{:S(2)}) collective-permute-start(bf16[576,256]{1,0:T(8,128)(2,1)S(1)} %get-tuple-element.385), channel_id=1, source_target_pairs={{0,8},{2,18},{4,12},{6,22},{8,0},{10,26},{12,4},{14,30},{16,24},{1... | collective-permute-start | bytes 884744 | tf_op jit(solution)/shard_map/ppermute | solution.py:934
  178.7 19.0 %collective-permute-start.17 = (bf16[864,256]{1,0:T(8,128)(2,1)S(1)}, bf16[864,256]{1,0:T(8,128)(2,1)S(1)}, u32[]{:S(2)}, u32[]{:S(2)}) collective-permute-start(bf16[864,256]{1,0:T(8,128)(2,1)S(1)} %get-tuple-element.375), channel_id=1, source_target_pairs={{0,4},{1,5},{2,3},{3,2},{4,0},{5,1},{6,7},{7,6},{8,12},{9,13},{10,... | collective-permute-start | bytes 1327112 | tf_op jit(solution)/shard_map/ppermute | solution.py:934
  184.7 14.2 %collective-permute-start.16 = (bf16[576,256]{1,0:T(8,128)(2,1)S(1)}, bf16[576,256]{1,0:T(8,128)(2,1)S(1)}, u32[]{:S(2)}, u32[]{:S(2)}) collective-permute-start(bf16[576,256]{1,0:T(8,128)(2,1)S(1)} %add_convert_fusion.14), channel_id=1, source_target_pairs={{0,8},{2,18},{4,12},{6,22},{8,0},{10,26},{12,4},{14,30},{16,24},{1... | collective-permute-start | bytes 884744 | tf_op jit(solution)/shard_map/ppermute | solution.py:934
  187.0 23.6 %collective-permute-start.15 = (bf16[1152,256]{1,0:T(8,128)(2,1)S(1)}, bf16[1152,256]{1,0:T(8,128)(2,1)S(1)}, u32[]{:S(2)}, u32[]{:S(2)}) collective-permute-start(bf16[1152,256]{1,0:T(8,128)(2,1)S(1)} %pad_maximum_fusion.7), channel_id=1, source_target_pairs={{0,16},{2,6},{4,20},{6,2},{8,24},{10,14},{12,28},{14,10},{16,0},{1... | collective-permute-start | bytes 1769480 | tf_op jit(solution)/shard_map/ppermute | solution.py:934
  190.3 20.5 %collective-permute-start.12 = (bf16[512,768]{1,0:T(8,128)(2,1)S(1)}, bf16[512,768]{1,0:T(8,128)(2,1)S(1)}, u32[]{:S(2)}, u32[]{:S(2)}) collective-permute-start(bf16[512,768]{1,0:T(8,128)(2,1)S(1)} %copy-done.18), channel_id=1, source_target_pairs={{1,0},{3,2},{5,4},{7,6},{9,8},{11,10},{13,12},{15,14},{17,16},{19,... | collective-permute-start | bytes 2359304 | tf_op jit(solution)/shard_map/ppermute | solution.py:1040
  197.7 24.2 %collective-permute-start.18 = (bf16[1280,256]{1,0:T(8,128)(2,1)}, bf16[1280,256]{1,0:T(8,128)(2,1)S(1)}, u32[]{:S(2)}, u32[]{:S(2)}) collective-permute-start(bf16[1280,256]{1,0:T(8,128)(2,1)} %get-tuple-element.264), channel_id=1, source_target_pairs={{0,2},{1,3},{2,0},{3,1},{4,6},{5,7},{6,4},{7,5},{8,10},{9,11},{10,... | collective-permute-start | bytes 1966088 | tf_op jit(solution)/shard_map/ppermute | solution.py:934
  197.9 26.0 %collective-permute-start.21 = (bf16[432,256]{1,0:T(8,128)(2,1)S(1)}, bf16[432,256]{1,0:T(8,128)(2,1)S(1)}, u32[]{:S(2)}, u32[]{:S(2)}) collective-permute-start(bf16[432,256]{1,0:T(8,128)(2,1)S(1)} %get-tuple-element.391), channel_id=1, source_target_pairs={{0,8},{1,9},{2,10},{3,11},{4,12},{5,13},{6,14},{7,15},{8,0},{9,1},... | collective-permute-start | bytes 663560 | tf_op jit(solution)/shard_map/ppermute | solution.py:934
  199.0 35.3 %collective-permute-start.23 = (bf16[1152,256]{1,0:T(8,128)(2,1)S(1)}, bf16[1152,256]{1,0:T(8,128)(2,1)}, u32[]{:S(2)}, u32[]{:S(2)}) collective-permute-start(bf16[1152,256]{1,0:T(8,128)(2,1)S(1)} %pad_maximum_fusion.8), channel_id=1, source_target_pairs={{0,16},{2,6},{4,20},{6,2},{8,24},{10,14},{12,28},{14,10},{16,0},{1... | collective-permute-start | bytes 1769480 | tf_op jit(solution)/shard_map/ppermute | solution.py:934
  210.7 16.3 %collective-permute-start.20 = (bf16[2304,256]{1,0:T(8,128)(2,1)S(1)}, bf16[2304,256]{1,0:T(8,128)(2,1)S(1)}, u32[]{:S(2)}, u32[]{:S(2)}) collective-permute-start(bf16[2304,256]{1,0:T(8,128)(2,1)S(1)} %pad_maximum_fusion.3), channel_id=1, source_target_pairs={{0,4},{2,10},{4,0},{6,14},{8,12},{10,2},{12,8},{14,6},{16,20},{18,... | collective-permute-start | bytes 3538952 | tf_op jit(solution)/shard_map/ppermute | solution.py:934
  223.8 7.4 %collective-permute-start.19 = (bf16[640,256]{1,0:T(8,128)(2,1)}, bf16[640,256]{1,0:T(8,128)(2,1)}, u32[]{:S(2)}, u32[]{:S(2)}) collective-permute-start(bf16[640,256]{1,0:T(8,128)(2,1)} %get-tuple-element.378), channel_id=1, source_target_pairs={{0,1},{1,0},{2,3},{3,2},{4,5},{5,4},{6,7},{7,6},{8,9},{9,8},{10,11... | collective-permute-start | bytes 983048 | tf_op jit(solution)/shard_map/ppermute | solution.py:934
  227.3 8.2 %copy-start.1 = (bf16[4608,256]{1,0:T(8,128)(2,1)}, bf16[4608,256]{1,0:T(8,128)(2,1)S(1)}, u32[]{:S(2)}) copy-start(bf16[4608,256]{1,0:T(8,128)(2,1)S(1)} %pad_maximum_fusion.value_ref) | copy-start | bytes 7077892
  227.3 28.7 %collective-permute-start.29 = (bf16[4608,256]{1,0:T(8,128)(2,1)S(1)}, bf16[4608,256]{1,0:T(8,128)(2,1)}, u32[]{:S(2)}, u32[]{:S(2)}) collective-permute-start(bf16[4608,256]{1,0:T(8,128)(2,1)S(1)} %pad_maximum_fusion.value_ref), channel_id=1, source_target_pairs={{0,2},{2,0},{4,6},{6,4},{8,10},{10,8},{12,14},{14,12},{16,18},{18,... | collective-permute-start | bytes 7077896 | tf_op jit(solution)/shard_map/ppermute | solution.py:934
  230.8 8.5 %collective-permute-start.25 = (bf16[216,256]{1,0:T(8,128)(2,1)}, bf16[216,256]{1,0:T(8,128)(2,1)S(1)}, u32[]{:S(2)}, u32[]{:S(2)}) collective-permute-start(bf16[216,256]{1,0:T(8,128)(2,1)} %get-tuple-element.403), channel_id=1, source_target_pairs={{0,16},{1,17},{2,18},{3,19},{4,20},{5,21},{6,22},{7,23},{8,24},{9,... | collective-permute-start | bytes 331784 | tf_op jit(solution)/shard_map/ppermute | solution.py:934
  232.3 5.4 %collective-permute-start.22 = (bf16[320,256]{1,0:T(8,128)(2,1)S(1)}, bf16[320,256]{1,0:T(8,128)(2,1)S(1)}, u32[]{:S(2)}, u32[]{:S(2)}) collective-permute-start(bf16[320,256]{1,0:T(8,128)(2,1)S(1)} %get-tuple-element.394), channel_id=1, source_target_pairs={{0,4},{1,5},{2,10},{3,11},{4,0},{5,1},{6,14},{7,15},{8,12},{9,13},... | collective-permute-start | bytes 491528 | tf_op jit(solution)/shard_map/ppermute | solution.py:934
  235.6 30.0 %collective-permute-start.34 = (bf16[2304,256]{1,0:T(8,128)(2,1)S(1)}, bf16[2304,256]{1,0:T(8,128)(2,1)}, u32[]{:S(2)}, u32[]{:S(2)}) collective-permute-start(bf16[2304,256]{1,0:T(8,128)(2,1)S(1)} %pad_maximum_fusion.4), channel_id=1, source_target_pairs={{0,4},{2,10},{4,0},{6,14},{8,12},{10,2},{12,8},{14,6},{16,20},{18,... | collective-permute-start | bytes 3538952 | tf_op jit(solution)/shard_map/ppermute | solution.py:934
  237.7 8.2 %collective-permute-start.24 = (bf16[160,256]{1,0:T(8,128)(2,1)S(1)}, bf16[160,256]{1,0:T(8,128)(2,1)S(1)}, u32[]{:S(2)}, u32[]{:S(2)}) collective-permute-start(bf16[160,256]{1,0:T(8,128)(2,1)S(1)} %get-tuple-element.406), channel_id=1, source_target_pairs={{0,8},{1,9},{2,6},{3,7},{4,12},{5,13},{6,2},{7,3},{8,0},{9,1},{10,... | collective-permute-start | bytes 245768 | tf_op jit(solution)/shard_map/ppermute | solution.py:934
  239.3 8.2 %collective-permute-start.27 = (bf16[216,256]{1,0:T(8,128)(2,1)S(1)}, bf16[216,256]{1,0:T(8,128)(2,1)S(1)}, u32[]{:S(2)}, u32[]{:S(2)}) collective-permute-start(bf16[216,256]{1,0:T(8,128)(2,1)S(1)} %add_convert_fusion.24), channel_id=1, source_target_pairs={{0,16},{1,17},{2,18},{3,19},{4,20},{5,21},{6,22},{7,23},{8,24},{9,... | collective-permute-start | bytes 331784 | tf_op jit(solution)/shard_map/ppermute | solution.py:934
  245.9 5.1 %collective-permute-start.26 = (bf16[80,256]{1,0:T(8,128)(2,1)S(1)}, bf16[80,256]{1,0:T(8,128)(2,1)S(1)}, u32[]{:S(2)}, u32[]{:S(2)}) collective-permute-start(bf16[80,256]{1,0:T(8,128)(2,1)S(1)} %get-tuple-element.412), channel_id=1, source_target_pairs={{0,16},{1,17},{2,18},{3,19},{4,20},{5,21},{6,22},{7,23},{8,24},{9,... | collective-permute-start | bytes 122888 | tf_op jit(solution)/shard_map/ppermute | solution.py:934
  251.6 8.0 %collective-permute-start.28 = (bf16[80,256]{1,0:T(8,128)(2,1)}, bf16[80,256]{1,0:T(8,128)(2,1)}, u32[]{:S(2)}, u32[]{:S(2)}) collective-permute-start(bf16[80,256]{1,0:T(8,128)(2,1)} %add_convert_fusion.29), channel_id=1, source_target_pairs={{0,16},{1,17},{2,18},{3,19},{4,20},{5,21},{6,22},{7,23},{8,24},{9,... | collective-permute-start | bytes 122888 | tf_op jit(solution)/shard_map/ppermute | solution.py:934
  253.5 8.5 %collective-permute-start.31 = (bf16[432,256]{1,0:T(8,128)(2,1)}, bf16[432,256]{1,0:T(8,128)(2,1)S(1)}, u32[]{:S(2)}, u32[]{:S(2)}) collective-permute-start(bf16[432,256]{1,0:T(8,128)(2,1)} %pad_maximum_fusion.11), channel_id=1, source_target_pairs={{0,8},{1,9},{2,10},{3,11},{4,12},{5,13},{6,14},{7,15},{8,0},{9,1},... | collective-permute-start | bytes 663560 | tf_op jit(solution)/shard_map/ppermute | solution.py:934
  260.5 4.5 %collective-permute-start.30 = (bf16[160,256]{1,0:T(8,128)(2,1)S(1)}, bf16[160,256]{1,0:T(8,128)(2,1)S(1)}, u32[]{:S(2)}, u32[]{:S(2)}) collective-permute-start(bf16[160,256]{1,0:T(8,128)(2,1)S(1)} %pad_maximum_fusion.13), channel_id=1, source_target_pairs={{0,8},{1,9},{2,6},{3,7},{4,12},{5,13},{6,2},{7,3},{8,0},{9,1},{10,... | collective-permute-start | bytes 245768 | tf_op jit(solution)/shard_map/ppermute | solution.py:934
  267.3 8.6 %copy-start = (bf16[4608,256]{1,0:T(8,128)(2,1)}, bf16[4608,256]{1,0:T(8,128)(2,1)S(1)}, u32[]{:S(2)}) copy-start(bf16[4608,256]{1,0:T(8,128)(2,1)S(1)} %pad_maximum_fusion.1.value_ref) | copy-start | bytes 7077892
  267.3 16.9 %collective-permute-start.36 = (bf16[4608,256]{1,0:T(8,128)(2,1)S(1)}, bf16[4608,256]{1,0:T(8,128)(2,1)}, u32[]{:S(2)}, u32[]{:S(2)}) collective-permute-start(bf16[4608,256]{1,0:T(8,128)(2,1)S(1)} %pad_maximum_fusion.1.value_ref), channel_id=1, source_target_pairs={{0,2},{2,0},{4,6},{6,4},{8,10},{10,8},{12,14},{14,12},{16,18},{18,... | collective-permute-start | bytes 7077896 | tf_op jit(solution)/shard_map/ppermute | solution.py:934
  267.4 8.4 %collective-permute-start.33 = (bf16[864,256]{1,0:T(8,128)(2,1)S(1)}, bf16[864,256]{1,0:T(8,128)(2,1)S(1)}, u32[]{:S(2)}, u32[]{:S(2)}) collective-permute-start(bf16[864,256]{1,0:T(8,128)(2,1)S(1)} %pad_maximum_fusion.9), channel_id=1, source_target_pairs={{0,4},{1,5},{2,3},{3,2},{4,0},{5,1},{6,7},{7,6},{8,12},{9,13},{10,... | collective-permute-start | bytes 1327112 | tf_op jit(solution)/shard_map/ppermute | solution.py:934
  267.7 9.7 %collective-permute-start.32 = (bf16[320,256]{1,0:T(8,128)(2,1)}, bf16[320,256]{1,0:T(8,128)(2,1)S(1)}, u32[]{:S(2)}, u32[]{:S(2)}) collective-permute-start(bf16[320,256]{1,0:T(8,128)(2,1)} %pad_maximum_fusion.12), channel_id=1, source_target_pairs={{0,4},{1,5},{2,10},{3,11},{4,0},{5,1},{6,14},{7,15},{8,12},{9,13},... | collective-permute-start | bytes 491528 | tf_op jit(solution)/shard_map/ppermute | solution.py:934
  275.9 21.4 %collective-permute-start.37 = (bf16[1728,256]{1,0:T(8,128)(2,1)S(1)}, bf16[1728,256]{1,0:T(8,128)(2,1)}, u32[]{:S(2)}, u32[]{:S(2)}) collective-permute-start(bf16[1728,256]{1,0:T(8,128)(2,1)S(1)} %pad_maximum_fusion.5), channel_id=1, source_target_pairs={{0,1},{1,0},{2,6},{3,7},{4,5},{5,4},{6,2},{7,3},{8,9},{9,8},{10,14... | collective-permute-start | bytes 2654216 | tf_op jit(solution)/shard_map/ppermute | solution.py:934
  279.2 16.9 %collective-permute-start.35 = (bf16[640,256]{1,0:T(8,128)(2,1)}, bf16[640,256]{1,0:T(8,128)(2,1)}, u32[]{:S(2)}, u32[]{:S(2)}) collective-permute-start(bf16[640,256]{1,0:T(8,128)(2,1)} %pad_maximum_fusion.10), channel_id=1, source_target_pairs={{0,1},{1,0},{2,3},{3,2},{4,5},{5,4},{6,7},{7,6},{8,9},{9,8},{10,11... | collective-permute-start | bytes 983048 | tf_op jit(solution)/shard_map/ppermute | solution.py:934
  299.0 4.6 %collective-permute-start.38 = (bf16[3456,256]{1,0:T(8,128)(2,1)S(1)}, bf16[3456,256]{1,0:T(8,128)(2,1)S(1)}, u32[]{:S(2)}, u32[]{:S(2)}) collective-permute-start(bf16[3456,256]{1,0:T(8,128)(2,1)S(1)} %pad_maximum_fusion.2.value_ref), channel_id=1, source_target_pairs={{0,2},{1,3},{2,0},{3,1},{4,6},{5,7},{6,4},{7,5},{8,10},{9,11},{10,... | collective-permute-start | bytes 5308424 | tf_op jit(solution)/shard_map/ppermute | solution.py:934
  299.0 9.1 %collective-permute-start.39 = (bf16[1280,256]{1,0:T(8,128)(2,1)S(1)}, bf16[1280,256]{1,0:T(8,128)(2,1)S(1)}, u32[]{:S(2)}, u32[]{:S(2)}) collective-permute-start(bf16[1280,256]{1,0:T(8,128)(2,1)S(1)} %pad_maximum_fusion.6.mine_ref), channel_id=1, source_target_pairs={{0,2},{1,3},{2,0},{3,1},{4,6},{5,7},{6,4},{7,5},{8,10},{9,11},{10,... | collective-permute-start | bytes 1966088 | tf_op jit(solution)/shard_map/ppermute | solution.py:934
  (12 other events, 24.5 us)

commit v12 on v11

--- a/solution.py
+++ b/solution.py
@@ -944,7 +944,7 @@
 def late_stages(axes):
     stages = stage_bits(axes)
     if len(axes) == 2 and len(stages) == 5:
-        return [stages[0], (0, 0), (2, 3), (3, 2), (4, 4)]
+        return [stages[0], (3, 3), (0, 2), (2, 0), (4, 4)]
     return stages
 
 

time: 318 us -> 322 us (1.013)
  starting transfers between devices: 50.7 us -> 56.1 us
    ppermute x36, starting transfers between devices: 42 us -> 47.4 us  [swap(): lax.ppermute(value, axes, [(source, pair_of(source)) for source in range(...]
  transfers between devices with their start and end apart: 40 -> 40, of which waited for: 12 -> 12; matrix products, arithmetic and copies ran while one was open for 6% -> 6% of each run, Pallas kernels for 40% -> 39%
where the time goes in v12:
time: 322 us; the launch traced here: 317 us
  Pallas kernels  190 us (59%)
  starting transfers between devices  56.1 us (17%)
  waiting for transfers between devices  41.6 us (13%)
  other arithmetic  20.3 us (6%)
  local copies, waits for them, and re-layouts  7.85 us (2%)
    pallas_call x23, Pallas kernels, call(): pl.pallas_call(kernel, grid_spec=pltpu.PrefetchScalarGridSpec(num_scalar_...  190 us
    ppermute x36, starting transfers between devices, swap(): lax.ppermute(value, axes, [(source, pair_of(source)) for source in range(...  47.4 us
    ppermute x36, waiting for transfers between devices, swap(): lax.ppermute(value, axes, [(source, pair_of(source)) for source in range(...  41.5 us
    convert_element_type x14, other arithmetic, part(): return (cut(self.terms[0]) + cut(self.terms[1])).astype(bf16)  11.5 us
    ppermute x3, starting transfers between devices, on_device(): to_text = lambda value: lax.ppermute(value, 'mod', [(0, 1)])  7.5 us
  transfers between devices with their start and end apart: 40, of which 12 were waited for; matrix products, arithmetic and copies ran while one was open for 6% of the time, Pallas kernels for 39%

profile of v12, /device:TPU:0, one launch (start us, length us, event | category | flops | bytes accessed | tf_op | source)
XLA Modules:
  0.0 317.2 jit_solution(9944526309712977192)
XLA Ops:
  1.8 4.9 %collective-permute-start = (bf16[256,768]{1,0:T(8,128)(2,1)S(1)}, bf16[256,768]{1,0:T(8,128)(2,1)S(1)}, u32[]{:S(2)}, u32[]{:S(2)}) collective-permute-start(bf16[256,768]{1,0:T(8,128)(2,1)S(1)} %get-tuple-element.377), channel_id=1, source_target_pairs={{0,1},{2,3},{4,5},{6,7},{8,9},{10,11},{12,13},{14,15},{16,17},{18,... | collective-permute-start | bytes 1179656 | tf_op jit(solution)/shard_map/ppermute | solution.py:1039
  9.4 8.5 %project_rows.1 = (bf16[1024,768]{1,0:T(8,128)(2,1)}, bf16[1024,2304]{1,0:T(8,128)(2,1)}) custom-call(bf16[1024,768]{1,0:T(8,128)(2,1)} %bitcast.20, f32[1,768]{1,0:T(1,128)} %gain_ref.9, f32[1,768]{1,0:T(1,128)} %shift_ref.6, bf16[768,2304]{1,0:T(8,128)(2,1)} %weight_ref.3, f32[2,768]{1,0:T(2,128)} %bias_ref.5), custom_call_target="tpu_custom_call" | custom-call | flops 3623878656 | bytes 11403264 | tf_op jit(solution)/shard_map/project_rows/pallas_call | solution.py:83
  19.3 3.9 %image_rows.2 = (bf16[512,768]{1,0:T(8,128)(2,1)}, bf16[512,1536]{1,0:T(8,128)(2,1)}) custom-call(s32[1]{0:T(128)} %bitcast.flag_ref, bf16[1024,768]{1,0:T(8,128)(2,1)} %bitcast.21, bf16[256,768]{1,0:T(8,128)(2,1)} %copy-done.14, f32[1,768]{1,0:T(1,128)} %gain_ref.9, f32[1,768]{1,0:T(1,128)} %shift_ref.6, f32[2,768]{1,0:T(2,128)} %copy-done.17, ...), custom_call_target="tpu_custom_call" | custom-call | flops 603979776 | bytes 6291456 | tf_op jit(solution)/shard_map/image_rows/pallas_call | solution.py:83
  23.1 12.3 %attend_forward.2 = (bf16[512,768]{1,0:T(8,128)(2,1)}, f32[6,2,512]{2,1,0:T(2,128)}) custom-call(s32[1]{0:T(128)} %bitcast.flag_ref, s32[2]{0:T(128)} %count_ref.17, s32[2,4]{1,0:T(2,128)} %lengths_ref.15, bf16[1024,2304]{1,0:T(8,128)(2,1)} %get-tuple-element.244.q_ref.k_ref.v_ref, bf16[1024,2304]{1,0:T(8,128)(2,1)} %get-tuple-element.244.q_ref.k_ref.v_ref, ...), custom_call_target="tpu_custom_call" | custom-call | flops 4831838208 | bytes 6291456 | tf_op jit(solution)/shard_map/attend_forward/pallas_call | solution.py:83
  36.2 3.8 %image_rows.3 = (bf16[512,768]{1,0:T(8,128)(2,1)}, bf16[512,1536]{1,0:T(8,128)(2,1)}) custom-call(s32[1]{0:T(128)} %bitcast.flag_ref, bf16[1024,768]{1,0:T(8,128)(2,1)} %bitcast.22, bf16[256,768]{1,0:T(8,128)(2,1)} %copy-done.13, f32[1,768]{1,0:T(1,128)} %gain_ref.9, f32[1,768]{1,0:T(1,128)} %shift_ref.6, ...), custom_call_target="tpu_custom_call", output_to_operand_aliasing={{0}: (9, {}), {1}: (10, {})} | custom-call | flops 603979776 | bytes 6291456 | tf_op jit(solution)/shard_map/image_rows/pallas_call | solution.py:83
  40.0 12.3 %attend_forward.3 = (bf16[512,768]{1,0:T(8,128)(2,1)}, f32[6,2,512]{2,1,0:T(2,128)}) custom-call(s32[1]{0:T(128)} %bitcast.flag_ref, s32[2]{0:T(128)} %count_ref.17, s32[2,4]{1,0:T(2,128)} %lengths_ref.15, bf16[1024,2304]{1,0:T(8,128)(2,1)} %get-tuple-element.244.q_ref.k_ref.v_ref, bf16[1024,2304]{1,0:T(8,128)(2,1)} %get-tuple-element.244.q_ref.k_ref.v_ref, ...), custom_call_target="tpu_custom_call" | custom-call | flops 4831838208 | bytes 6291456 | tf_op jit(solution)/shard_map/attend_forward/pallas_call | solution.py:83
  52.2 45.2 %feed_forward.1 = (bf16[1024,768]{1,0:T(8,128)(2,1)}, f32[1024,768]{1,0:T(8,128)}, bf16[1024,768]{1,0:T(8,128)(2,1)}, bf16[768,768]{1,0:T(8,128)(2,1)}, f32[8,76...) custom-call(s32[1]{0:T(128)} %bitcast.flag_ref, ...), custom_call_target="tpu_custom_call" | custom-call | flops 28991029248 | bytes 41943040 | tf_op jit(solution)/shard_map/feed_forward/pallas_call | solution.py:83
  98.0 8.2 %attend_backward.6 = (bf16[1024,768]{1,0:T(8,128)(2,1)}, bf16[1024,768]{1,0:T(8,128)(2,1)}, bf16[1024,768]{1,0:T(8,128)(2,1)}, bf16[512,768]{1,0:T(8,128)(2,1)}, bf16[512,768]{1,0:T(8,128)(2,1)}) custom-call(s32[1]{0:T(128)} %bitcast.flag_ref, s32[2]{0:T(128)} %count_ref.17, s32[2,4]{1,0:T(2,128)} %lengths_ref.15, ...), custom_call_target="tpu_custom_call" | custom-call | flops 40265318400 | bytes 41943040 | tf_op jit(solution)/shard_map/attend_backward/pallas_call | solution.py:83
  106.3 1.6 add_convert_fusion
  109.4 8.2 %attend_backward.7 = (bf16[1024,768]{1,0:T(8,128)(2,1)}, bf16[1024,768]{1,0:T(8,128)(2,1)}, bf16[1024,768]{1,0:T(8,128)(2,1)}, bf16[512,768]{1,0:T(8,128)(2,1)}, bf16[512,768]{1,0:T(8,128)(2,1)}) custom-call(s32[1]{0:T(128)} %bitcast.flag_ref, s32[2]{0:T(128)} %count_ref.17, ...), custom_call_target="tpu_custom_call", output_to_operand_aliasing={{0}: (11, {}), {1}: (12, {}), {2}: (13, {}), {3}: (14, {}),... | custom-call | flops 40265318400 | bytes 41943040 | tf_op jit(solution)/shard_map/attend_backward/pallas_call | solution.py:83
  117.6 1.6 add_convert_fusion.1
  119.7 8.1 %attend_backward.8 = (bf16[1024,768]{1,0:T(8,128)(2,1)}, bf16[1024,768]{1,0:T(8,128)(2,1)}, bf16[1024,768]{1,0:T(8,128)(2,1)}, bf16[512,768]{1,0:T(8,128)(2,1)}, bf16[512,768]{1,0:T(8,128)(2,1)}) custom-call(s32[1]{0:T(128)} %bitcast.flag_ref, s32[2]{0:T(128)} %count_ref.17, ...), custom_call_target="tpu_custom_call", output_to_operand_aliasing={{0}: (11, {}), {1}: (12, {}), {2}: (13, {}), {3}: (14, {}),... | custom-call | flops 40265318400 | bytes 41943040 | tf_op jit(solution)/shard_map/attend_backward/pallas_call | solution.py:83
  130.4 2.7 collective-permute-start.8
  133.1 8.3 %attend_backward.9 = (bf16[1024,768]{1,0:T(8,128)(2,1)}, bf16[1024,768]{1,0:T(8,128)(2,1)}, bf16[1024,768]{1,0:T(8,128)(2,1)}, bf16[512,768]{1,0:T(8,128)(2,1)}, bf16[512,768]{1,0:T(8,128)(2,1)}) custom-call(s32[1]{0:T(128)} %bitcast.flag_ref, s32[2]{0:T(128)} %count_ref.17, ...), custom_call_target="tpu_custom_call", output_to_operand_aliasing={{0}: (11, {}), {1}: (12, {}), {2}: (13, {}), {3}: (14, {}),... | custom-call | flops 40265318400 | bytes 41943040 | tf_op jit(solution)/shard_map/attend_backward/pallas_call | solution.py:83
  142.5 2.4 collective-permute-start.10
  144.9 9.3 %weight_grads.2 = (f32[2,512]{1,0:T(2,128)}, bf16[3456,256]{1,0:T(8,128)(2,1)}, bf16[3456,256]{1,0:T(8,128)(2,1)}) custom-call(s32[1]{0:T(128)} %bitcast.1.side_ref.half_ref, bf16[1024,768]{1,0:T(8,128)(2,1)} %get-tuple-element.260.normed_ref, bf16[512,768]{1,0:T(8,128)(2,1)} %get-tuple-element.228.image_ref, ...), custom_call_target="tpu_custom_call" | custom-call | flops 32212254720 | bytes 125829120 | tf_op jit(solution)/shard_map/weight_grads/pallas_call | solution.py:83
  155.2 1.6 collective-permute-start.11
  156.8 8.1 %attend_backward.10 = (bf16[1024,768]{1,0:T(8,128)(2,1)}, bf16[1024,768]{1,0:T(8,128)(2,1)}, bf16[1024,768]{1,0:T(8,128)(2,1)}, bf16[512,768]{1,0:T(8,128)(2,1)}, bf16[512,768]{1,0:T(8,128)(2,1)}) custom-call(s32[1]{0:T(128)} %bitcast.flag_ref, s32[2]{0:T(128)} %count_ref.17, ...), custom_call_target="tpu_custom_call", output_to_operand_aliasing={{0}: (11, {}), {1}: (12, {}), {2}: (13, {}), {3}: (14, {}),... | custom-call | flops 40265318400 | bytes 41943040 | tf_op jit(solution)/shard_map/attend_backward/pallas_call | solution.py:83
  166.6 8.3 %attend_backward.11 = (bf16[1024,768]{1,0:T(8,128)(2,1)}, bf16[1024,768]{1,0:T(8,128)(2,1)}, bf16[1024,768]{1,0:T(8,128)(2,1)}, bf16[512,768]{1,0:T(8,128)(2,1)}, bf16[512,768]{1,0:T(8,128)(2,1)}) custom-call(s32[1]{0:T(128)} %bitcast.flag_ref, s32[2]{0:T(128)} %count_ref.17, ...), custom_call_target="tpu_custom_call", output_to_operand_aliasing={{0}: (11, {}), {1}: (12, {}), {2}: (13, {}), {3}: (14, {}),... | custom-call | flops 40265318400 | bytes 41943040 | tf_op jit(solution)/shard_map/attend_backward/pallas_call | solution.py:83
  175.1 2.1 collective-permute-start.14
  178.7 1.5 collective-permute-start.17
  180.2 4.4 %image_grads.1.near_ref = bf16[512,768]{1,0:T(8,128)(2,1)} custom-call(bf16[768,2304]{1,0:T(8,128)(2,1)} %weight_ref.3, bf16[768,2304]{1,0:T(8,128)(2,1)} %weight_ref.3, bf16[512,768]{1,0:T(8,128)(2,1)} %get-tuple-element.255.keys_ref.gik_ref, bf16[512,768]{1,0:T(8,128)(2,1)} %get-tuple-element.249.values_ref.giv_ref), custom_call_target="tpu_custom_call" | custom-call | flops 12079595520 | bytes 62914560 | tf_op jit(solution)/shard_map/image_grads/pallas_call | solution.py:83
  184.7 2.1 collective-permute-start.16
  186.9 3.3 %collective-permute-start.15 = (bf16[1152,256]{1,0:T(8,128)(2,1)S(1)}, bf16[1152,256]{1,0:T(8,128)(2,1)S(1)}, u32[]{:S(2)}, u32[]{:S(2)}) collective-permute-start(bf16[1152,256]{1,0:T(8,128)(2,1)S(1)} %pad_maximum_fusion.7), channel_id=1, source_target_pairs={{0,16},{2,6},{4,20},{6,2},{8,24},{10,14},{12,28},{14,10},{16,0},{1... | collective-permute-start | bytes 1769480 | tf_op jit(solution)/shard_map/ppermute | solution.py:934
  191.5 6.0 %weight_grads.3 = (f32[2,256]{1,0:T(2,128)}, bf16[1280,256]{1,0:T(8,128)(2,1)}, bf16[1280,256]{1,0:T(8,128)(2,1)}) custom-call(s32[1]{0:T(128)} %bitcast.1.side_ref.half_ref, bf16[1024,768]{1,0:T(8,128)(2,1)} %get-tuple-element.260.normed_ref, bf16[512,768]{1,0:T(8,128)(2,1)} %get-tuple-element.228.image_ref, bf16[1024,768]{1,0:T(8,128)(2,1)} %get-tuple-element.261.gq_ref, ...), custom_call_target="tpu_custom_call" | custom-call | flops 16106127360 | bytes 125829120 | tf_op jit(solution)/shard_map/weight_grads/pallas_call | solution.py:83
  199.0 11.5 %collective-permute-done.15 = bf16[1152,256]{1,0:T(8,128)(2,1)S(1)} collective-permute-done((bf16[1152,256]{1,0:T(8,128)(2,1)S(1)}, bf16[1152,256]{1,0:T(8,128)(2,1)S(1)}, u32[]{:S(2)}, u32[]{:S(2)}) %collective-permute-start.15) | collective-permute-done | bytes 589856 | tf_op jit(solution)/shard_map/ppermute | solution.py:934
  211.7 10.1 %finish_rows.1 = (bf16[1024,768]{1,0:T(8,128)(2,1)}, bf16[1280,256]{1,0:T(8,128)(2,1)}) custom-call(s32[1]{0:T(128)} %bitcast.flag_ref, bf16[1024,768]{1,0:T(8,128)(2,1)} %bitcast.24, f32[1024,768]{1,0:T(8,128)} %get-tuple-element.273.gmid_ref, bf16[512,768]{1,0:T(8,128)(2,1)} %image_grads.1.near_ref, ...), custom_call_target="tpu_custom_call", output_to_operand_aliasing={{1}: (13, {})} | custom-call | flops 36238786560 | bytes 167772160 | tf_op jit(solution)/shard_map/finish_rows/pallas_call | solution.py:83
  221.8 2.0 add_convert_fusion.12
  225.4 1.6 collective-permute-done.20
  227.3 5.8 %collective-permute-start.29 = (bf16[4608,256]{1,0:T(8,128)(2,1)S(1)}, bf16[4608,256]{1,0:T(8,128)(2,1)}, u32[]{:S(2)}, u32[]{:S(2)}) collective-permute-start(bf16[4608,256]{1,0:T(8,128)(2,1)S(1)} %pad_maximum_fusion.value_ref), channel_id=1, source_target_pairs={{0,2},{2,0},{4,6},{6,4},{8,10},{10,8},{12,14},{14,12},{16,18},{18,... | collective-permute-start | bytes 7077896 | tf_op jit(solution)/shard_map/ppermute | solution.py:934
  233.1 1.7 collective-permute-done.19
  235.9 1.7 collective-permute-start.22
  241.3 3.0 collective-permute-start.24
  245.3 3.6 %expert_outputs.4 = (f32[3072,768]{1,0:T(8,128)}, f32[768,3072]{1,0:T(8,128)}) custom-call(s32[1]{0:T(128)} %bitcast.1.side_ref.half_ref, bf16[4608,256]{1,0:T(8,128)(2,1)} %copy-done.1), custom_call_target="tpu_custom_call" | custom-call | flops 1179648 | bytes 7077888 | tf_op jit(solution)/shard_map/expert_outputs/pallas_call | solution.py:83
  248.9 7.2 %collective-permute-done.24 = bf16[160,256]{1,0:T(8,128)(2,1)S(1)} collective-permute-done((bf16[160,256]{1,0:T(8,128)(2,1)S(1)}, bf16[160,256]{1,0:T(8,128)(2,1)S(1)}, u32[]{:S(2)}, u32[]{:S(2)}) %collective-permute-start.24) | collective-permute-done | bytes 81952 | tf_op jit(solution)/shard_map/ppermute | solution.py:934
  256.1 2.9 collective-permute-start.26
  261.7 2.8 collective-permute-start.28
  264.5 2.6 collective-permute-start.31
  267.1 3.6 %expert_outputs.5 = (f32[3072,768]{1,0:T(8,128)}, f32[768,3072]{1,0:T(8,128)}) custom-call(s32[1]{0:T(128)S(6)} %sub.40.half_ref, bf16[4608,256]{1,0:T(8,128)(2,1)} %collective-permute-done.29.value_ref, f32[3072,768]{1,0:T(8,128)} %get-tuple-element.303.refs_0_, f32[768,3072]{1,0:T(8,128)} %get-tuple-element.295.refs_1_), custom_call_target="tpu_custom_call", output_to_operand_aliasing={{0}: (2, {}), {1}: (3, {})} | custom-call | flops 1179648 | bytes 7077888 | tf_op jit(solution)/shard_map/expert_outputs/pallas_call | solution.py:83
  273.5 2.6 collective-permute-done.30
  280.8 8.0 %collective-permute-done.33 = bf16[864,256]{1,0:T(8,128)(2,1)S(1)} collective-permute-done((bf16[864,256]{1,0:T(8,128)(2,1)}, bf16[864,256]{1,0:T(8,128)(2,1)S(1)}, u32[]{:S(2)}, u32[]{:S(2)}) %collective-permute-start.33) | collective-permute-done | bytes 442400 | tf_op jit(solution)/shard_map/ppermute | solution.py:934
  291.2 3.6 %expert_outputs.6 = (f32[3072,768]{1,0:T(8,128)}, f32[768,3072]{1,0:T(8,128)}) custom-call(s32[1]{0:T(128)} %bitcast.1.side_ref.half_ref, bf16[4608,256]{1,0:T(8,128)(2,1)} %copy-done, f32[3072,768]{1,0:T(8,128)} %get-tuple-element.318.refs_0_, f32[768,3072]{1,0:T(8,128)} %get-tuple-element.304.refs_1_), custom_call_target="tpu_custom_call", output_to_operand_aliasing={{0}: (2, {}), {1}: (3, {})} | custom-call | flops 1179648 | bytes 7077888 | tf_op jit(solution)/shard_map/expert_outputs/pallas_call | solution.py:83
  294.7 3.6 %expert_outputs.7 = (f32[3072,768]{1,0:T(8,128)}, f32[768,3072]{1,0:T(8,128)}) custom-call(s32[1]{0:T(128)S(6)} %sub.40.half_ref, bf16[4608,256]{1,0:T(8,128)(2,1)} %collective-permute-done.36.value_ref, f32[3072,768]{1,0:T(8,128)} %get-tuple-element.321.refs_0_, f32[768,3072]{1,0:T(8,128)} %get-tuple-element.319.refs_1_), custom_call_target="tpu_custom_call", output_to_operand_aliasing={{0}: (2, {}), {1}: (3, {})} | custom-call | flops 1179648 | bytes 7077888 | tf_op jit(solution)/shard_map/expert_outputs/pallas_call | solution.py:83
  298.3 1.8 collective-permute-done.35
  300.2 2.9 collective-permute-done.37
  304.5 3.4 %first_outputs.2 = (f32[768,2304]{1,0:T(8,128)}, f32[768,768]{1,0:T(8,128)}) custom-call(s32[1]{0:T(128)} %bitcast.1.side_ref.half_ref, bf16[3456,256]{1,0:T(8,128)(2,1)} %copy-done.2), custom_call_target="tpu_custom_call" | custom-call | flops 884736 | bytes 5308416 | tf_op jit(solution)/shard_map/first_outputs/pallas_call | solution.py:83
  309.1 3.4 %first_outputs.3 = (f32[768,2304]{1,0:T(8,128)}, f32[768,768]{1,0:T(8,128)}) custom-call(s32[1]{0:T(128)S(6)} %sub.40.half_ref, bf16[3456,256]{1,0:T(8,128)(2,1)} %copy-done.7, f32[768,2304]{1,0:T(8,128)} %get-tuple-element.330.refs_0_, f32[768,768]{1,0:T(8,128)} %get-tuple-element.328.refs_1_), custom_call_target="tpu_custom_call", output_to_operand_aliasing={{0}: (2, {}), {1}: (3, {})} | custom-call | flops 884736 | bytes 5308416 | tf_op jit(solution)/shard_map/first_outputs/pallas_call | solution.py:83
  313.3 3.4 %last_outputs.1 = (f32[768,2304]{1,0:T(8,128)}, f32[1,768]{1,0:T(1,128)}, f32[1,768]{1,0:T(1,128)}, f32[1,768]{1,0:T(1,128)}, f32[1,768]{1,0:T(1,128)}, /*index=...) custom-call(s32[1]{0:T(128)} %bitcast.1.side_ref.half_ref, ...), custom_call_target="tpu_custom_call", output_to_operand_aliasing={{0}: (4, {})} | custom-call | flops 327680 | bytes 1966080 | tf_op jit(solution)/shard_map/last_outputs/pallas_call | solution.py:83
  (146 shorter events, 44.3 us)
Async XLA Ops:
  0.6 6.1 %copy-start.16 = (f32[1,768]{1,0:T(1,128)S(1)}, f32[1,768]{1,0:T(1,128)}, u32[]{:S(2)}) copy-start(f32[1,768]{1,0:T(1,128)} %gain_ref.9) | copy-start | bytes 9220
  0.7 6.1 %copy-start.15 = (f32[1,768]{1,0:T(1,128)S(1)}, f32[1,768]{1,0:T(1,128)}, u32[]{:S(2)}) copy-start(f32[1,768]{1,0:T(1,128)} %shift_ref.6) | copy-start | bytes 9220
  1.8 16.7 %collective-permute-start = (bf16[256,768]{1,0:T(8,128)(2,1)S(1)}, bf16[256,768]{1,0:T(8,128)(2,1)S(1)}, u32[]{:S(2)}, u32[]{:S(2)}) collective-permute-start(bf16[256,768]{1,0:T(8,128)(2,1)S(1)} %get-tuple-element.377), channel_id=1, source_target_pairs={{0,1},{2,3},{4,5},{6,7},{8,9},{10,11},{12,13},{14,15},{16,17},{18,... | collective-permute-start | bytes 1179656 | tf_op jit(solution)/shard_map/ppermute | solution.py:1039
  6.8 11.7 %collective-permute-start.1 = (f32[2,768]{1,0:T(2,128)S(1)}, f32[2,768]{1,0:T(2,128)S(1)}, u32[]{:S(2)}, u32[]{:S(2)}) collective-permute-start(f32[2,768]{1,0:T(2,128)S(1)} %pad_maximum_fusion.14), channel_id=1, source_target_pairs={{0,1},{2,3},{4,5},{6,7},{8,9},{10,11},{12,13},{14,15},{16,17},{18,... | collective-permute-start | bytes 18440 | tf_op jit(solution)/shard_map/ppermute | solution.py:1039
  8.1 27.3 %collective-permute-start.2 = (bf16[256,768]{1,0:T(8,128)(2,1)S(1)}, bf16[256,768]{1,0:T(8,128)(2,1)S(1)}, u32[]{:S(2)}, u32[]{:S(2)}) collective-permute-start(bf16[256,768]{1,0:T(8,128)(2,1)S(1)} %get-tuple-element.376), channel_id=1, source_target_pairs={{0,1},{2,3},{4,5},{6,7},{8,9},{10,11},{12,13},{14,15},{16,17},{18,... | collective-permute-start | bytes 1179656 | tf_op jit(solution)/shard_map/ppermute | solution.py:1039
  9.4 8.5 %copy-start.18 = (f32[768]{0:T(1024)S(1)}, f32[768]{0:T(1024)}, u32[]{:S(2)}) copy-start(f32[768]{0:T(1024)} %param.24) | copy-start | bytes 9220
  97.5 20.2 %collective-permute-start.3 = (bf16[4608,256]{1,0:T(8,128)(2,1)}, bf16[4608,256]{1,0:T(8,128)(2,1)S(1)}, u32[]{:S(2)}, u32[]{:S(2)}) collective-permute-start(bf16[4608,256]{1,0:T(8,128)(2,1)} %get-tuple-element.195), channel_id=1, source_target_pairs={{0,2},{2,0},{4,6},{6,4},{8,10},{10,8},{12,14},{14,12},{16,18},{18,... | collective-permute-start | bytes 7077896 | tf_op jit(solution)/shard_map/ppermute | solution.py:934
  97.5 8.7 %collective-permute-start.4 = (bf16[4608,256]{1,0:T(8,128)(2,1)}, bf16[4608,256]{1,0:T(8,128)(2,1)S(1)}, u32[]{:S(2)}, u32[]{:S(2)}) collective-permute-start(bf16[4608,256]{1,0:T(8,128)(2,1)} %get-tuple-element.197), channel_id=1, source_target_pairs={{0,2},{2,0},{4,6},{6,4},{8,10},{10,8},{12,14},{14,12},{16,18},{18,... | collective-permute-start | bytes 7077896 | tf_op jit(solution)/shard_map/ppermute | solution.py:934
  98.0 8.2 %copy-start.5 = (bf16[4608,256]{1,0:T(8,128)(2,1)S(1)}, bf16[4608,256]{1,0:T(8,128)(2,1)}, u32[]{:S(2)}) copy-start(bf16[4608,256]{1,0:T(8,128)(2,1)} %get-tuple-element.201) | copy-start | bytes 7077892
  107.9 20.0 %collective-permute-start.6 = (bf16[2304,256]{1,0:T(8,128)(2,1)}, bf16[2304,256]{1,0:T(8,128)(2,1)S(1)}, u32[]{:S(2)}, u32[]{:S(2)}) collective-permute-start(bf16[2304,256]{1,0:T(8,128)(2,1)} %get-tuple-element.359), channel_id=1, source_target_pairs={{0,4},{2,10},{4,0},{6,14},{8,12},{10,2},{12,8},{14,6},{16,20},{18,... | collective-permute-start | bytes 3538952 | tf_op jit(solution)/shard_map/ppermute | solution.py:934
  109.4 8.3 %copy-start.4 = (bf16[4608,256]{1,0:T(8,128)(2,1)S(1)}, bf16[4608,256]{1,0:T(8,128)(2,1)}, u32[]{:S(2)}) copy-start(bf16[4608,256]{1,0:T(8,128)(2,1)} %get-tuple-element.209) | copy-start | bytes 7077892
  119.2 22.2 %collective-permute-start.5 = (bf16[2304,256]{1,0:T(8,128)(2,1)}, bf16[2304,256]{1,0:T(8,128)(2,1)S(1)}, u32[]{:S(2)}, u32[]{:S(2)}) collective-permute-start(bf16[2304,256]{1,0:T(8,128)(2,1)} %get-tuple-element.360), channel_id=1, source_target_pairs={{0,4},{2,10},{4,0},{6,14},{8,12},{10,2},{12,8},{14,6},{16,20},{18,... | collective-permute-start | bytes 3538952 | tf_op jit(solution)/shard_map/ppermute | solution.py:934
  130.4 24.0 %collective-permute-start.8 = (bf16[1152,256]{1,0:T(8,128)(2,1)S(1)}, bf16[1152,256]{1,0:T(8,128)(2,1)S(1)}, u32[]{:S(2)}, u32[]{:S(2)}) collective-permute-start(bf16[1152,256]{1,0:T(8,128)(2,1)S(1)} %get-tuple-element.371), channel_id=1, source_target_pairs={{0,16},{2,6},{4,20},{6,2},{8,24},{10,14},{12,28},{14,10},{16,0},{1... | collective-permute-start | bytes 1769480 | tf_op jit(solution)/shard_map/ppermute | solution.py:934
  142.5 32.4 %collective-permute-start.10 = (bf16[1152,256]{1,0:T(8,128)(2,1)}, bf16[1152,256]{1,0:T(8,128)(2,1)S(1)}, u32[]{:S(2)}, u32[]{:S(2)}) collective-permute-start(bf16[1152,256]{1,0:T(8,128)(2,1)} %get-tuple-element.369), channel_id=1, source_target_pairs={{0,16},{2,6},{4,20},{6,2},{8,24},{10,14},{12,28},{14,10},{16,0},{1... | collective-permute-start | bytes 1769480 | tf_op jit(solution)/shard_map/ppermute | solution.py:934
  154.3 10.6 %collective-permute-start.7 = (bf16[3456,256]{1,0:T(8,128)(2,1)}, bf16[3456,256]{1,0:T(8,128)(2,1)S(1)}, u32[]{:S(2)}, u32[]{:S(2)}) collective-permute-start(bf16[3456,256]{1,0:T(8,128)(2,1)} %get-tuple-element.235), channel_id=1, source_target_pairs={{0,2},{1,3},{2,0},{3,1},{4,6},{5,7},{6,4},{7,5},{8,10},{9,11},{10,... | collective-permute-start | bytes 5308424 | tf_op jit(solution)/shard_map/ppermute | solution.py:934
  155.2 9.7 %copy-start.6 = (bf16[3456,256]{1,0:T(8,128)(2,1)S(1)}, bf16[3456,256]{1,0:T(8,128)(2,1)}, u32[]{:S(2)}) copy-start(bf16[3456,256]{1,0:T(8,128)(2,1)} %get-tuple-element.240) | copy-start | bytes 5308420
  155.2 11.2 %collective-permute-start.11 = (bf16[576,256]{1,0:T(8,128)(2,1)}, bf16[576,256]{1,0:T(8,128)(2,1)S(1)}, u32[]{:S(2)}, u32[]{:S(2)}) collective-permute-start(bf16[576,256]{1,0:T(8,128)(2,1)} %get-tuple-element.387), channel_id=1, source_target_pairs={{0,8},{2,18},{4,12},{6,22},{8,0},{10,26},{12,4},{14,30},{16,24},{1... | collective-permute-start | bytes 884744 | tf_op jit(solution)/shard_map/ppermute | solution.py:934
  165.4 13.1 %collective-permute-start.9 = (bf16[1728,256]{1,0:T(8,128)(2,1)S(1)}, bf16[1728,256]{1,0:T(8,128)(2,1)S(1)}, u32[]{:S(2)}, u32[]{:S(2)}) collective-permute-start(bf16[1728,256]{1,0:T(8,128)(2,1)S(1)} %get-tuple-element.362), channel_id=1, source_target_pairs={{0,1},{1,0},{2,6},{3,7},{4,5},{5,4},{6,2},{7,3},{8,9},{9,8},{10,14... | collective-permute-start | bytes 2654216 | tf_op jit(solution)/shard_map/ppermute | solution.py:934
  166.5 20.3 %collective-permute-start.13 = (bf16[576,256]{1,0:T(8,128)(2,1)S(1)}, bf16[576,256]{1,0:T(8,128)(2,1)S(1)}, u32[]{:S(2)}, u32[]{:S(2)}) collective-permute-start(bf16[576,256]{1,0:T(8,128)(2,1)S(1)} %add_convert_fusion.17), channel_id=1, source_target_pairs={{0,8},{2,18},{4,12},{6,22},{8,0},{10,26},{12,4},{14,30},{16,24},{1... | collective-permute-start | bytes 884744 | tf_op jit(solution)/shard_map/ppermute | solution.py:934
  175.1 9.6 %collective-permute-start.14 = (bf16[576,256]{1,0:T(8,128)(2,1)S(1)}, bf16[576,256]{1,0:T(8,128)(2,1)S(1)}, u32[]{:S(2)}, u32[]{:S(2)}) collective-permute-start(bf16[576,256]{1,0:T(8,128)(2,1)S(1)} %get-tuple-element.385), channel_id=1, source_target_pairs={{0,8},{2,18},{4,12},{6,22},{8,0},{10,26},{12,4},{14,30},{16,24},{1... | collective-permute-start | bytes 884744 | tf_op jit(solution)/shard_map/ppermute | solution.py:934
  178.7 18.9 %collective-permute-start.17 = (bf16[864,256]{1,0:T(8,128)(2,1)S(1)}, bf16[864,256]{1,0:T(8,128)(2,1)S(1)}, u32[]{:S(2)}, u32[]{:S(2)}) collective-permute-start(bf16[864,256]{1,0:T(8,128)(2,1)S(1)} %get-tuple-element.375), channel_id=1, source_target_pairs={{0,4},{1,5},{2,3},{3,2},{4,0},{5,1},{6,7},{7,6},{8,12},{9,13},{10,... | collective-permute-start | bytes 1327112 | tf_op jit(solution)/shard_map/ppermute | solution.py:934
  184.7 14.2 %collective-permute-start.16 = (bf16[576,256]{1,0:T(8,128)(2,1)S(1)}, bf16[576,256]{1,0:T(8,128)(2,1)S(1)}, u32[]{:S(2)}, u32[]{:S(2)}) collective-permute-start(bf16[576,256]{1,0:T(8,128)(2,1)S(1)} %add_convert_fusion.14), channel_id=1, source_target_pairs={{0,8},{2,18},{4,12},{6,22},{8,0},{10,26},{12,4},{14,30},{16,24},{1... | collective-permute-start | bytes 884744 | tf_op jit(solution)/shard_map/ppermute | solution.py:934
  186.9 23.7 %collective-permute-start.15 = (bf16[1152,256]{1,0:T(8,128)(2,1)S(1)}, bf16[1152,256]{1,0:T(8,128)(2,1)S(1)}, u32[]{:S(2)}, u32[]{:S(2)}) collective-permute-start(bf16[1152,256]{1,0:T(8,128)(2,1)S(1)} %pad_maximum_fusion.7), channel_id=1, source_target_pairs={{0,16},{2,6},{4,20},{6,2},{8,24},{10,14},{12,28},{14,10},{16,0},{1... | collective-permute-start | bytes 1769480 | tf_op jit(solution)/shard_map/ppermute | solution.py:934
  190.2 20.6 %collective-permute-start.12 = (bf16[512,768]{1,0:T(8,128)(2,1)S(1)}, bf16[512,768]{1,0:T(8,128)(2,1)S(1)}, u32[]{:S(2)}, u32[]{:S(2)}) collective-permute-start(bf16[512,768]{1,0:T(8,128)(2,1)S(1)} %copy-done.19), channel_id=1, source_target_pairs={{1,0},{3,2},{5,4},{7,6},{9,8},{11,10},{13,12},{15,14},{17,16},{19,... | collective-permute-start | bytes 2359304 | tf_op jit(solution)/shard_map/ppermute | solution.py:1040
  197.5 24.3 %collective-permute-start.18 = (bf16[1280,256]{1,0:T(8,128)(2,1)}, bf16[1280,256]{1,0:T(8,128)(2,1)S(1)}, u32[]{:S(2)}, u32[]{:S(2)}) collective-permute-start(bf16[1280,256]{1,0:T(8,128)(2,1)} %get-tuple-element.264), channel_id=1, source_target_pairs={{0,2},{1,3},{2,0},{3,1},{4,6},{5,7},{6,4},{7,5},{8,10},{9,11},{10,... | collective-permute-start | bytes 1966088 | tf_op jit(solution)/shard_map/ppermute | solution.py:934
  197.7 26.9 %collective-permute-start.21 = (bf16[432,256]{1,0:T(8,128)(2,1)S(1)}, bf16[432,256]{1,0:T(8,128)(2,1)S(1)}, u32[]{:S(2)}, u32[]{:S(2)}) collective-permute-start(bf16[432,256]{1,0:T(8,128)(2,1)S(1)} %get-tuple-element.391), channel_id=1, source_target_pairs={{0,8},{1,9},{2,10},{3,11},{4,12},{5,13},{6,14},{7,15},{8,0},{9,1},... | collective-permute-start | bytes 663560 | tf_op jit(solution)/shard_map/ppermute | solution.py:934
  199.0 38.6 %collective-permute-start.23 = (bf16[1152,256]{1,0:T(8,128)(2,1)S(1)}, bf16[1152,256]{1,0:T(8,128)(2,1)}, u32[]{:S(2)}, u32[]{:S(2)}) collective-permute-start(bf16[1152,256]{1,0:T(8,128)(2,1)S(1)} %pad_maximum_fusion.8), channel_id=1, source_target_pairs={{0,16},{2,6},{4,20},{6,2},{8,24},{10,14},{12,28},{14,10},{16,0},{1... | collective-permute-start | bytes 1769480 | tf_op jit(solution)/shard_map/ppermute | solution.py:934
  210.7 16.3 %collective-permute-start.20 = (bf16[2304,256]{1,0:T(8,128)(2,1)S(1)}, bf16[2304,256]{1,0:T(8,128)(2,1)S(1)}, u32[]{:S(2)}, u32[]{:S(2)}) collective-permute-start(bf16[2304,256]{1,0:T(8,128)(2,1)S(1)} %pad_maximum_fusion.3), channel_id=1, source_target_pairs={{0,4},{2,10},{4,0},{6,14},{8,12},{10,2},{12,8},{14,6},{16,20},{18,... | collective-permute-start | bytes 3538952 | tf_op jit(solution)/shard_map/ppermute | solution.py:934
  223.8 11.0 %collective-permute-start.19 = (bf16[640,256]{1,0:T(8,128)(2,1)}, bf16[640,256]{1,0:T(8,128)(2,1)}, u32[]{:S(2)}, u32[]{:S(2)}) collective-permute-start(bf16[640,256]{1,0:T(8,128)(2,1)} %get-tuple-element.378), channel_id=1, source_target_pairs={{0,8},{1,9},{2,10},{3,11},{4,12},{5,13},{6,14},{7,15},{8,0},{9,1},... | collective-permute-start | bytes 983048 | tf_op jit(solution)/shard_map/ppermute | solution.py:934
  227.3 11.4 %copy-start.1 = (bf16[4608,256]{1,0:T(8,128)(2,1)}, bf16[4608,256]{1,0:T(8,128)(2,1)S(1)}, u32[]{:S(2)}) copy-start(bf16[4608,256]{1,0:T(8,128)(2,1)S(1)} %pad_maximum_fusion.value_ref) | copy-start | bytes 7077892
  227.3 39.8 %collective-permute-start.29 = (bf16[4608,256]{1,0:T(8,128)(2,1)S(1)}, bf16[4608,256]{1,0:T(8,128)(2,1)}, u32[]{:S(2)}, u32[]{:S(2)}) collective-permute-start(bf16[4608,256]{1,0:T(8,128)(2,1)S(1)} %pad_maximum_fusion.value_ref), channel_id=1, source_target_pairs={{0,2},{2,0},{4,6},{6,4},{8,10},{10,8},{12,14},{14,12},{16,18},{18,... | collective-permute-start | bytes 7077896 | tf_op jit(solution)/shard_map/ppermute | solution.py:934
  233.1 11.3 %collective-permute-start.25 = (bf16[216,256]{1,0:T(8,128)(2,1)}, bf16[216,256]{1,0:T(8,128)(2,1)S(1)}, u32[]{:S(2)}, u32[]{:S(2)}) collective-permute-start(bf16[216,256]{1,0:T(8,128)(2,1)} %get-tuple-element.403), channel_id=1, source_target_pairs={{0,16},{1,17},{2,18},{3,19},{4,20},{5,21},{6,22},{7,23},{8,24},{9,... | collective-permute-start | bytes 331784 | tf_op jit(solution)/shard_map/ppermute | solution.py:934
  235.9 5.4 %collective-permute-start.22 = (bf16[320,256]{1,0:T(8,128)(2,1)S(1)}, bf16[320,256]{1,0:T(8,128)(2,1)S(1)}, u32[]{:S(2)}, u32[]{:S(2)}) collective-permute-start(bf16[320,256]{1,0:T(8,128)(2,1)S(1)} %get-tuple-element.394), channel_id=1, source_target_pairs={{0,1},{1,0},{2,6},{3,7},{4,5},{5,4},{6,2},{7,3},{8,9},{9,8},{10,14... | collective-permute-start | bytes 491528 | tf_op jit(solution)/shard_map/ppermute | solution.py:934
  238.8 38.0 %collective-permute-start.34 = (bf16[2304,256]{1,0:T(8,128)(2,1)S(1)}, bf16[2304,256]{1,0:T(8,128)(2,1)}, u32[]{:S(2)}, u32[]{:S(2)}) collective-permute-start(bf16[2304,256]{1,0:T(8,128)(2,1)S(1)} %pad_maximum_fusion.4), channel_id=1, source_target_pairs={{0,4},{2,10},{4,0},{6,14},{8,12},{10,2},{12,8},{14,6},{16,20},{18,... | collective-permute-start | bytes 3538952 | tf_op jit(solution)/shard_map/ppermute | solution.py:934
  241.3 14.7 %collective-permute-start.24 = (bf16[160,256]{1,0:T(8,128)(2,1)S(1)}, bf16[160,256]{1,0:T(8,128)(2,1)S(1)}, u32[]{:S(2)}, u32[]{:S(2)}) collective-permute-start(bf16[160,256]{1,0:T(8,128)(2,1)S(1)} %get-tuple-element.406), channel_id=1, source_target_pairs={{0,4},{1,5},{2,3},{3,2},{4,0},{5,1},{6,7},{7,6},{8,12},{9,13},{10,... | collective-permute-start | bytes 245768 | tf_op jit(solution)/shard_map/ppermute | solution.py:934
  244.4 14.6 %collective-permute-start.27 = (bf16[216,256]{1,0:T(8,128)(2,1)S(1)}, bf16[216,256]{1,0:T(8,128)(2,1)S(1)}, u32[]{:S(2)}, u32[]{:S(2)}) collective-permute-start(bf16[216,256]{1,0:T(8,128)(2,1)S(1)} %add_convert_fusion.24), channel_id=1, source_target_pairs={{0,16},{1,17},{2,18},{3,19},{4,20},{5,21},{6,22},{7,23},{8,24},{9,... | collective-permute-start | bytes 331784 | tf_op jit(solution)/shard_map/ppermute | solution.py:934
  256.1 5.0 %collective-permute-start.26 = (bf16[80,256]{1,0:T(8,128)(2,1)S(1)}, bf16[80,256]{1,0:T(8,128)(2,1)S(1)}, u32[]{:S(2)}, u32[]{:S(2)}) collective-permute-start(bf16[80,256]{1,0:T(8,128)(2,1)S(1)} %get-tuple-element.412), channel_id=1, source_target_pairs={{0,16},{1,17},{2,18},{3,19},{4,20},{5,21},{6,22},{7,23},{8,24},{9,... | collective-permute-start | bytes 122888 | tf_op jit(solution)/shard_map/ppermute | solution.py:934
  261.7 9.1 %collective-permute-start.28 = (bf16[80,256]{1,0:T(8,128)(2,1)}, bf16[80,256]{1,0:T(8,128)(2,1)}, u32[]{:S(2)}, u32[]{:S(2)}) collective-permute-start(bf16[80,256]{1,0:T(8,128)(2,1)} %add_convert_fusion.29), channel_id=1, source_target_pairs={{0,16},{1,17},{2,18},{3,19},{4,20},{5,21},{6,22},{7,23},{8,24},{9,... | collective-permute-start | bytes 122888 | tf_op jit(solution)/shard_map/ppermute | solution.py:934
  264.5 8.2 %collective-permute-start.31 = (bf16[432,256]{1,0:T(8,128)(2,1)}, bf16[432,256]{1,0:T(8,128)(2,1)S(1)}, u32[]{:S(2)}, u32[]{:S(2)}) collective-permute-start(bf16[432,256]{1,0:T(8,128)(2,1)} %pad_maximum_fusion.11), channel_id=1, source_target_pairs={{0,8},{1,9},{2,10},{3,11},{4,12},{5,13},{6,14},{7,15},{8,0},{9,1},... | collective-permute-start | bytes 663560 | tf_op jit(solution)/shard_map/ppermute | solution.py:934
  271.6 4.5 %collective-permute-start.30 = (bf16[160,256]{1,0:T(8,128)(2,1)S(1)}, bf16[160,256]{1,0:T(8,128)(2,1)S(1)}, u32[]{:S(2)}, u32[]{:S(2)}) collective-permute-start(bf16[160,256]{1,0:T(8,128)(2,1)S(1)} %pad_maximum_fusion.13), channel_id=1, source_target_pairs={{0,4},{1,5},{2,3},{3,2},{4,0},{5,1},{6,7},{7,6},{8,12},{9,13},{10,... | collective-permute-start | bytes 245768 | tf_op jit(solution)/shard_map/ppermute | solution.py:934
  278.4 11.6 %copy-start = (bf16[4608,256]{1,0:T(8,128)(2,1)}, bf16[4608,256]{1,0:T(8,128)(2,1)S(1)}, u32[]{:S(2)}) copy-start(bf16[4608,256]{1,0:T(8,128)(2,1)S(1)} %pad_maximum_fusion.1.value_ref) | copy-start | bytes 7077892
  278.4 16.4 %collective-permute-start.36 = (bf16[4608,256]{1,0:T(8,128)(2,1)S(1)}, bf16[4608,256]{1,0:T(8,128)(2,1)}, u32[]{:S(2)}, u32[]{:S(2)}) collective-permute-start(bf16[4608,256]{1,0:T(8,128)(2,1)S(1)} %pad_maximum_fusion.1.value_ref), channel_id=1, source_target_pairs={{0,2},{2,0},{4,6},{6,4},{8,10},{10,8},{12,14},{14,12},{16,18},{18,... | collective-permute-start | bytes 7077896 | tf_op jit(solution)/shard_map/ppermute | solution.py:934
  278.5 10.3 %collective-permute-start.33 = (bf16[864,256]{1,0:T(8,128)(2,1)}, bf16[864,256]{1,0:T(8,128)(2,1)S(1)}, u32[]{:S(2)}, u32[]{:S(2)}) collective-permute-start(bf16[864,256]{1,0:T(8,128)(2,1)} %pad_maximum_fusion.9), channel_id=1, source_target_pairs={{0,4},{1,5},{2,3},{3,2},{4,0},{5,1},{6,7},{7,6},{8,12},{9,13},{10,... | collective-permute-start | bytes 1327112 | tf_op jit(solution)/shard_map/ppermute | solution.py:934
  279.6 11.5 %collective-permute-start.32 = (bf16[320,256]{1,0:T(8,128)(2,1)S(1)}, bf16[320,256]{1,0:T(8,128)(2,1)S(1)}, u32[]{:S(2)}, u32[]{:S(2)}) collective-permute-start(bf16[320,256]{1,0:T(8,128)(2,1)S(1)} %copy-done.11), channel_id=1, source_target_pairs={{0,1},{1,0},{2,6},{3,7},{4,5},{5,4},{6,2},{7,3},{8,9},{9,8},{10,14... | collective-permute-start | bytes 491528 | tf_op jit(solution)/shard_map/ppermute | solution.py:934
  290.0 13.1 %collective-permute-start.37 = (bf16[1728,256]{1,0:T(8,128)(2,1)S(1)}, bf16[1728,256]{1,0:T(8,128)(2,1)S(1)}, u32[]{:S(2)}, u32[]{:S(2)}) collective-permute-start(bf16[1728,256]{1,0:T(8,128)(2,1)S(1)} %pad_maximum_fusion.5), channel_id=1, source_target_pairs={{0,1},{1,0},{2,6},{3,7},{4,5},{5,4},{6,2},{7,3},{8,9},{9,8},{10,14... | collective-permute-start | bytes 2654216 | tf_op jit(solution)/shard_map/ppermute | solution.py:934
  291.1 9.0 %collective-permute-start.35 = (bf16[640,256]{1,0:T(8,128)(2,1)S(1)}, bf16[640,256]{1,0:T(8,128)(2,1)S(1)}, u32[]{:S(2)}, u32[]{:S(2)}) collective-permute-start(bf16[640,256]{1,0:T(8,128)(2,1)S(1)} %pad_maximum_fusion.10), channel_id=1, source_target_pairs={{0,8},{1,9},{2,10},{3,11},{4,12},{5,13},{6,14},{7,15},{8,0},{9,1},... | collective-permute-start | bytes 983048 | tf_op jit(solution)/shard_map/ppermute | solution.py:934
  303.3 4.6 %collective-permute-start.38 = (bf16[3456,256]{1,0:T(8,128)(2,1)S(1)}, bf16[3456,256]{1,0:T(8,128)(2,1)S(1)}, u32[]{:S(2)}, u32[]{:S(2)}) collective-permute-start(bf16[3456,256]{1,0:T(8,128)(2,1)S(1)} %pad_maximum_fusion.2.value_ref), channel_id=1, source_target_pairs={{0,2},{1,3},{2,0},{3,1},{4,6},{5,7},{6,4},{7,5},{8,10},{9,11},{10,... | collective-permute-start | bytes 5308424 | tf_op jit(solution)/shard_map/ppermute | solution.py:934
  303.4 9.1 %collective-permute-start.39 = (bf16[1280,256]{1,0:T(8,128)(2,1)S(1)}, bf16[1280,256]{1,0:T(8,128)(2,1)S(1)}, u32[]{:S(2)}, u32[]{:S(2)}) collective-permute-start(bf16[1280,256]{1,0:T(8,128)(2,1)S(1)} %pad_maximum_fusion.6.mine_ref), channel_id=1, source_target_pairs={{0,2},{1,3},{2,0},{3,1},{4,6},{5,7},{6,4},{7,5},{8,10},{9,11},{10,... | collective-permute-start | bytes 1966088 | tf_op jit(solution)/shard_map/ppermute | solution.py:934
  (13 other events, 28.6 us)

commit v13 on v8

--- a/solution.py
+++ b/solution.py
@@ -1142,7 +1142,7 @@
     c.step()
     a.step()
     last_sums, keep, send = weights(LANES, 2, SMALL)
-    p = Total(order, ("dp", "mod"), keep, send, late_stages(("dp", "mod")))
+    p = Total(order, ("dp", "mod"), keep, send)
     s.step()
     c.step()
     a.step()

time: 313 us -> 319 us (1.019)
  starting transfers between devices: 49.2 us -> 59.6 us
    ppermute x36, starting transfers between devices: 40.4 us -> 50.8 us  [swap(): lax.ppermute(value, axes, [(source, pair_of(source)) for source in range(...]
  transfers between devices with their start and end apart: 40 -> 40, of which waited for: 13 -> 12; matrix products, arithmetic and copies ran while one was open for 7% -> 7% of each run, Pallas kernels for 41% -> 40%
where the time goes in v13:
time: 319 us; the launch traced here: 313 us
  Pallas kernels  190 us (60%)
  starting transfers between devices  59.6 us (19%)
  waiting for transfers between devices  34.2 us (11%)
  other arithmetic  20.3 us (6%)
  local copies, waits for them, and re-layouts  7.24 us (2%)
    pallas_call x23, Pallas kernels, call(): pl.pallas_call(kernel, grid_spec=pltpu.PrefetchScalarGridSpec(num_scalar_...  190 us
    ppermute x36, starting transfers between devices, swap(): lax.ppermute(value, axes, [(source, pair_of(source)) for source in range(...  50.8 us
    ppermute x36, waiting for transfers between devices, swap(): lax.ppermute(value, axes, [(source, pair_of(source)) for source in range(...  34.1 us
    convert_element_type x14, other arithmetic, part(): return (cut(self.terms[0]) + cut(self.terms[1])).astype(bf16)  11.9 us
    ppermute x3, starting transfers between devices, on_device(): to_text = lambda value: lax.ppermute(value, 'mod', [(0, 1)])  7.5 us
  transfers between devices with their start and end apart: 40, of which 12 were waited for; matrix products, arithmetic and copies ran while one was open for 7% of the time, Pallas kernels for 40%

profile of v13, /device:TPU:0, one launch (start us, length us, event | category | flops | bytes accessed | tf_op | source)
XLA Modules:
  0.0 312.8 jit_solution(10542485461871161342)
XLA Ops:
  1.8 4.9 %collective-permute-start = (bf16[256,768]{1,0:T(8,128)(2,1)S(1)}, bf16[256,768]{1,0:T(8,128)(2,1)S(1)}, u32[]{:S(2)}, u32[]{:S(2)}) collective-permute-start(bf16[256,768]{1,0:T(8,128)(2,1)S(1)} %get-tuple-element.377), channel_id=1, source_target_pairs={{0,1},{2,3},{4,5},{6,7},{8,9},{10,11},{12,13},{14,15},{16,17},{18,... | collective-permute-start | bytes 1179656 | tf_op jit(solution)/shard_map/ppermute | solution.py:1039
  9.4 8.5 %project_rows.1 = (bf16[1024,768]{1,0:T(8,128)(2,1)}, bf16[1024,2304]{1,0:T(8,128)(2,1)}) custom-call(bf16[1024,768]{1,0:T(8,128)(2,1)} %bitcast.20, f32[1,768]{1,0:T(1,128)} %gain_ref.9, f32[1,768]{1,0:T(1,128)} %shift_ref.6, bf16[768,2304]{1,0:T(8,128)(2,1)} %weight_ref.3, f32[2,768]{1,0:T(2,128)} %bias_ref.5), custom_call_target="tpu_custom_call" | custom-call | flops 3623878656 | bytes 11403264 | tf_op jit(solution)/shard_map/project_rows/pallas_call | solution.py:83
  19.3 3.9 %image_rows.2 = (bf16[512,768]{1,0:T(8,128)(2,1)}, bf16[512,1536]{1,0:T(8,128)(2,1)}) custom-call(s32[1]{0:T(128)} %bitcast.flag_ref, bf16[1024,768]{1,0:T(8,128)(2,1)} %bitcast.21, bf16[256,768]{1,0:T(8,128)(2,1)} %copy-done.13, f32[1,768]{1,0:T(1,128)} %gain_ref.9, f32[1,768]{1,0:T(1,128)} %shift_ref.6, f32[2,768]{1,0:T(2,128)} %copy-done.16, ...), custom_call_target="tpu_custom_call" | custom-call | flops 603979776 | bytes 6291456 | tf_op jit(solution)/shard_map/image_rows/pallas_call | solution.py:83
  23.1 12.3 %attend_forward.2 = (bf16[512,768]{1,0:T(8,128)(2,1)}, f32[6,2,512]{2,1,0:T(2,128)}) custom-call(s32[1]{0:T(128)} %bitcast.flag_ref, s32[2]{0:T(128)} %count_ref.17, s32[2,4]{1,0:T(2,128)} %lengths_ref.15, bf16[1024,2304]{1,0:T(8,128)(2,1)} %get-tuple-element.244.q_ref.k_ref.v_ref, bf16[1024,2304]{1,0:T(8,128)(2,1)} %get-tuple-element.244.q_ref.k_ref.v_ref, ...), custom_call_target="tpu_custom_call" | custom-call | flops 4831838208 | bytes 6291456 | tf_op jit(solution)/shard_map/attend_forward/pallas_call | solution.py:83
  36.2 3.8 %image_rows.3 = (bf16[512,768]{1,0:T(8,128)(2,1)}, bf16[512,1536]{1,0:T(8,128)(2,1)}) custom-call(s32[1]{0:T(128)} %bitcast.flag_ref, bf16[1024,768]{1,0:T(8,128)(2,1)} %bitcast.22, bf16[256,768]{1,0:T(8,128)(2,1)} %copy-done.12, f32[1,768]{1,0:T(1,128)} %gain_ref.9, f32[1,768]{1,0:T(1,128)} %shift_ref.6, ...), custom_call_target="tpu_custom_call", output_to_operand_aliasing={{0}: (9, {}), {1}: (10, {})} | custom-call | flops 603979776 | bytes 6291456 | tf_op jit(solution)/shard_map/image_rows/pallas_call | solution.py:83
  40.0 12.3 %attend_forward.3 = (bf16[512,768]{1,0:T(8,128)(2,1)}, f32[6,2,512]{2,1,0:T(2,128)}) custom-call(s32[1]{0:T(128)} %bitcast.flag_ref, s32[2]{0:T(128)} %count_ref.17, s32[2,4]{1,0:T(2,128)} %lengths_ref.15, bf16[1024,2304]{1,0:T(8,128)(2,1)} %get-tuple-element.244.q_ref.k_ref.v_ref, bf16[1024,2304]{1,0:T(8,128)(2,1)} %get-tuple-element.244.q_ref.k_ref.v_ref, ...), custom_call_target="tpu_custom_call" | custom-call | flops 4831838208 | bytes 6291456 | tf_op jit(solution)/shard_map/attend_forward/pallas_call | solution.py:83
  52.3 45.2 %feed_forward.1 = (bf16[1024,768]{1,0:T(8,128)(2,1)}, f32[1024,768]{1,0:T(8,128)}, bf16[1024,768]{1,0:T(8,128)(2,1)}, bf16[768,768]{1,0:T(8,128)(2,1)}, f32[8,76...) custom-call(s32[1]{0:T(128)} %bitcast.flag_ref, ...), custom_call_target="tpu_custom_call" | custom-call | flops 28991029248 | bytes 41943040 | tf_op jit(solution)/shard_map/feed_forward/pallas_call | solution.py:83
  98.1 8.2 %attend_backward.6 = (bf16[1024,768]{1,0:T(8,128)(2,1)}, bf16[1024,768]{1,0:T(8,128)(2,1)}, bf16[1024,768]{1,0:T(8,128)(2,1)}, bf16[512,768]{1,0:T(8,128)(2,1)}, bf16[512,768]{1,0:T(8,128)(2,1)}) custom-call(s32[1]{0:T(128)} %bitcast.flag_ref, s32[2]{0:T(128)} %count_ref.17, s32[2,4]{1,0:T(2,128)} %lengths_ref.15, ...), custom_call_target="tpu_custom_call" | custom-call | flops 40265318400 | bytes 41943040 | tf_op jit(solution)/shard_map/attend_backward/pallas_call | solution.py:83
  106.3 1.6 add_convert_fusion
  109.4 8.2 %attend_backward.7 = (bf16[1024,768]{1,0:T(8,128)(2,1)}, bf16[1024,768]{1,0:T(8,128)(2,1)}, bf16[1024,768]{1,0:T(8,128)(2,1)}, bf16[512,768]{1,0:T(8,128)(2,1)}, bf16[512,768]{1,0:T(8,128)(2,1)}) custom-call(s32[1]{0:T(128)} %bitcast.flag_ref, s32[2]{0:T(128)} %count_ref.17, ...), custom_call_target="tpu_custom_call", output_to_operand_aliasing={{0}: (11, {}), {1}: (12, {}), {2}: (13, {}), {3}: (14, {}),... | custom-call | flops 40265318400 | bytes 41943040 | tf_op jit(solution)/shard_map/attend_backward/pallas_call | solution.py:83
  117.6 1.6 add_convert_fusion.1
  119.8 8.1 %attend_backward.8 = (bf16[1024,768]{1,0:T(8,128)(2,1)}, bf16[1024,768]{1,0:T(8,128)(2,1)}, bf16[1024,768]{1,0:T(8,128)(2,1)}, bf16[512,768]{1,0:T(8,128)(2,1)}, bf16[512,768]{1,0:T(8,128)(2,1)}) custom-call(s32[1]{0:T(128)} %bitcast.flag_ref, s32[2]{0:T(128)} %count_ref.17, ...), custom_call_target="tpu_custom_call", output_to_operand_aliasing={{0}: (11, {}), {1}: (12, {}), {2}: (13, {}), {3}: (14, {}),... | custom-call | flops 40265318400 | bytes 41943040 | tf_op jit(solution)/shard_map/attend_backward/pallas_call | solution.py:83
  128.9 1.5 add_convert_fusion.7
  130.4 2.6 collective-permute-start.8
  133.1 8.3 %attend_backward.9 = (bf16[1024,768]{1,0:T(8,128)(2,1)}, bf16[1024,768]{1,0:T(8,128)(2,1)}, bf16[1024,768]{1,0:T(8,128)(2,1)}, bf16[512,768]{1,0:T(8,128)(2,1)}, bf16[512,768]{1,0:T(8,128)(2,1)}) custom-call(s32[1]{0:T(128)} %bitcast.flag_ref, s32[2]{0:T(128)} %count_ref.17, ...), custom_call_target="tpu_custom_call", output_to_operand_aliasing={{0}: (11, {}), {1}: (12, {}), {2}: (13, {}), {3}: (14, {}),... | custom-call | flops 40265318400 | bytes 41943040 | tf_op jit(solution)/shard_map/attend_backward/pallas_call | solution.py:83
  142.6 2.4 collective-permute-start.10
  144.9 9.3 %weight_grads.2 = (f32[2,512]{1,0:T(2,128)}, bf16[3456,256]{1,0:T(8,128)(2,1)}, bf16[3456,256]{1,0:T(8,128)(2,1)}) custom-call(s32[1]{0:T(128)} %bitcast.1.side_ref.half_ref, bf16[1024,768]{1,0:T(8,128)(2,1)} %get-tuple-element.260.normed_ref, bf16[512,768]{1,0:T(8,128)(2,1)} %get-tuple-element.228.image_ref, ...), custom_call_target="tpu_custom_call" | custom-call | flops 32212254720 | bytes 125829120 | tf_op jit(solution)/shard_map/weight_grads/pallas_call | solution.py:83
  155.2 1.6 collective-permute-start.11
  156.8 8.1 %attend_backward.10 = (bf16[1024,768]{1,0:T(8,128)(2,1)}, bf16[1024,768]{1,0:T(8,128)(2,1)}, bf16[1024,768]{1,0:T(8,128)(2,1)}, bf16[512,768]{1,0:T(8,128)(2,1)}, bf16[512,768]{1,0:T(8,128)(2,1)}) custom-call(s32[1]{0:T(128)} %bitcast.flag_ref, s32[2]{0:T(128)} %count_ref.17, ...), custom_call_target="tpu_custom_call", output_to_operand_aliasing={{0}: (11, {}), {1}: (12, {}), {2}: (13, {}), {3}: (14, {}),... | custom-call | flops 40265318400 | bytes 41943040 | tf_op jit(solution)/shard_map/attend_backward/pallas_call | solution.py:83
  166.7 8.4 %attend_backward.11 = (bf16[1024,768]{1,0:T(8,128)(2,1)}, bf16[1024,768]{1,0:T(8,128)(2,1)}, bf16[1024,768]{1,0:T(8,128)(2,1)}, bf16[512,768]{1,0:T(8,128)(2,1)}, bf16[512,768]{1,0:T(8,128)(2,1)}) custom-call(s32[1]{0:T(128)} %bitcast.flag_ref, s32[2]{0:T(128)} %count_ref.17, ...), custom_call_target="tpu_custom_call", output_to_operand_aliasing={{0}: (11, {}), {1}: (12, {}), {2}: (13, {}), {3}: (14, {}),... | custom-call | flops 40265318400 | bytes 41943040 | tf_op jit(solution)/shard_map/attend_backward/pallas_call | solution.py:83
  175.3 2.1 collective-permute-start.14
  178.7 1.6 collective-permute-start.17
  180.3 4.4 %image_grads.1.near_ref = bf16[512,768]{1,0:T(8,128)(2,1)} custom-call(bf16[768,2304]{1,0:T(8,128)(2,1)} %weight_ref.3, bf16[768,2304]{1,0:T(8,128)(2,1)} %weight_ref.3, bf16[512,768]{1,0:T(8,128)(2,1)} %get-tuple-element.255.keys_ref.gik_ref, bf16[512,768]{1,0:T(8,128)(2,1)} %get-tuple-element.249.values_ref.giv_ref), custom_call_target="tpu_custom_call" | custom-call | flops 12079595520 | bytes 62914560 | tf_op jit(solution)/shard_map/image_grads/pallas_call | solution.py:83
  184.7 2.1 collective-permute-start.16
  187.0 3.3 %collective-permute-start.15 = (bf16[1152,256]{1,0:T(8,128)(2,1)S(1)}, bf16[1152,256]{1,0:T(8,128)(2,1)S(1)}, u32[]{:S(2)}, u32[]{:S(2)}) collective-permute-start(bf16[1152,256]{1,0:T(8,128)(2,1)S(1)} %pad_maximum_fusion.7), channel_id=1, source_target_pairs={{0,16},{2,6},{4,20},{6,2},{8,24},{10,14},{12,28},{14,10},{16,0},{1... | collective-permute-start | bytes 1769480 | tf_op jit(solution)/shard_map/ppermute | solution.py:934
  191.6 6.1 %weight_grads.3 = (f32[2,256]{1,0:T(2,128)}, bf16[1280,256]{1,0:T(8,128)(2,1)}, bf16[1280,256]{1,0:T(8,128)(2,1)}) custom-call(s32[1]{0:T(128)} %bitcast.1.side_ref.half_ref, bf16[1024,768]{1,0:T(8,128)(2,1)} %get-tuple-element.260.normed_ref, bf16[512,768]{1,0:T(8,128)(2,1)} %get-tuple-element.228.image_ref, bf16[1024,768]{1,0:T(8,128)(2,1)} %get-tuple-element.261.gq_ref, ...), custom_call_target="tpu_custom_call" | custom-call | flops 16106127360 | bytes 125829120 | tf_op jit(solution)/shard_map/weight_grads/pallas_call | solution.py:83
  199.1 11.4 %collective-permute-done.15 = bf16[1152,256]{1,0:T(8,128)(2,1)S(1)} collective-permute-done((bf16[1152,256]{1,0:T(8,128)(2,1)S(1)}, bf16[1152,256]{1,0:T(8,128)(2,1)S(1)}, u32[]{:S(2)}, u32[]{:S(2)}) %collective-permute-start.15) | collective-permute-done | bytes 589856 | tf_op jit(solution)/shard_map/ppermute | solution.py:934
  211.7 10.1 %finish_rows.1 = (bf16[1024,768]{1,0:T(8,128)(2,1)}, bf16[1280,256]{1,0:T(8,128)(2,1)}) custom-call(s32[1]{0:T(128)} %bitcast.flag_ref, bf16[1024,768]{1,0:T(8,128)(2,1)} %bitcast.24, f32[1024,768]{1,0:T(8,128)} %get-tuple-element.273.gmid_ref, bf16[512,768]{1,0:T(8,128)(2,1)} %image_grads.1.near_ref, ...), custom_call_target="tpu_custom_call", output_to_operand_aliasing={{1}: (13, {})} | custom-call | flops 36238786560 | bytes 167772160 | tf_op jit(solution)/shard_map/finish_rows/pallas_call | solution.py:83
  221.9 2.0 add_convert_fusion.12
  224.6 5.9 %collective-permute-done.20 = bf16[2304,256]{1,0:T(8,128)(2,1)S(1)} collective-permute-done((bf16[2304,256]{1,0:T(8,128)(2,1)S(1)}, bf16[2304,256]{1,0:T(8,128)(2,1)S(1)}, u32[]{:S(2)}, u32[]{:S(2)}) %collective-permute-start.20) | collective-permute-done | bytes 1179680 | tf_op jit(solution)/shard_map/ppermute | solution.py:934
  232.7 1.7 collective-permute-start.22
  236.1 2.0 collective-permute-done.22
  238.1 2.0 collective-permute-start.24
  240.2 2.3 collective-permute-start.27
  242.4 3.6 %expert_outputs.4 = (f32[3072,768]{1,0:T(8,128)}, f32[768,3072]{1,0:T(8,128)}) custom-call(s32[1]{0:T(128)} %bitcast.1.side_ref.half_ref, bf16[4608,256]{1,0:T(8,128)(2,1)} %copy-done.1), custom_call_target="tpu_custom_call" | custom-call | flops 1179648 | bytes 7077888 | tf_op jit(solution)/shard_map/expert_outputs/pallas_call | solution.py:83
  247.9 3.3 %collective-permute-done.26 = bf16[80,256]{1,0:T(8,128)(2,1)S(1)} collective-permute-done((bf16[80,256]{1,0:T(8,128)(2,1)S(1)}, bf16[80,256]{1,0:T(8,128)(2,1)S(1)}, u32[]{:S(2)}, u32[]{:S(2)}) %collective-permute-start.26) | collective-permute-done | bytes 40992 | tf_op jit(solution)/shard_map/ppermute | solution.py:934
  253.2 2.1 collective-permute-start.32
  255.3 3.6 %expert_outputs.5 = (f32[3072,768]{1,0:T(8,128)}, f32[768,3072]{1,0:T(8,128)}) custom-call(s32[1]{0:T(128)S(6)} %sub.40.half_ref, bf16[4608,256]{1,0:T(8,128)(2,1)} %collective-permute-done.29.value_ref, f32[3072,768]{1,0:T(8,128)} %get-tuple-element.303.refs_0_, f32[768,3072]{1,0:T(8,128)} %get-tuple-element.295.refs_1_), custom_call_target="tpu_custom_call", output_to_operand_aliasing={{0}: (2, {}), {1}: (3, {})} | custom-call | flops 1179648 | bytes 7077888 | tf_op jit(solution)/shard_map/expert_outputs/pallas_call | solution.py:83
  264.7 4.0 %collective-permute-done.34 = bf16[864,256]{1,0:T(8,128)(2,1)S(1)} collective-permute-done((bf16[864,256]{1,0:T(8,128)(2,1)S(1)}, bf16[864,256]{1,0:T(8,128)(2,1)S(1)}, u32[]{:S(2)}, u32[]{:S(2)}) %collective-permute-start.34) | collective-permute-done | bytes 442400 | tf_op jit(solution)/shard_map/ppermute | solution.py:934
  271.1 9.5 %collective-permute-start.38 = (bf16[4608,256]{1,0:T(8,128)(2,1)S(1)}, bf16[4608,256]{1,0:T(8,128)(2,1)}, u32[]{:S(2)}, u32[]{:S(2)}) collective-permute-start(bf16[4608,256]{1,0:T(8,128)(2,1)S(1)} %pad_maximum_fusion.1.value_ref), channel_id=1, source_target_pairs={{0,2},{2,0},{4,6},{6,4},{8,10},{10,8},{12,14},{14,12},{16,18},{18,... | collective-permute-start | bytes 7077896 | tf_op jit(solution)/shard_map/ppermute | solution.py:934
  280.6 3.6 %expert_outputs.6 = (f32[3072,768]{1,0:T(8,128)}, f32[768,3072]{1,0:T(8,128)}) custom-call(s32[1]{0:T(128)} %bitcast.1.side_ref.half_ref, bf16[4608,256]{1,0:T(8,128)(2,1)} %copy-done, f32[3072,768]{1,0:T(8,128)} %get-tuple-element.316.refs_0_, f32[768,3072]{1,0:T(8,128)} %get-tuple-element.304.refs_1_), custom_call_target="tpu_custom_call", output_to_operand_aliasing={{0}: (2, {}), {1}: (3, {})} | custom-call | flops 1179648 | bytes 7077888 | tf_op jit(solution)/shard_map/expert_outputs/pallas_call | solution.py:83
  287.8 3.9 %collective-permute-start.37 = (bf16[3456,256]{1,0:T(8,128)(2,1)S(1)}, bf16[3456,256]{1,0:T(8,128)(2,1)S(1)}, u32[]{:S(2)}, u32[]{:S(2)}) collective-permute-start(bf16[3456,256]{1,0:T(8,128)(2,1)S(1)} %pad_maximum_fusion.2.value_ref), channel_id=1, source_target_pairs={{0,2},{1,3},{2,0},{3,1},{4,6},{5,7},{6,4},{7,5},{8,10},{9,11},{10,... | collective-permute-start | bytes 5308424 | tf_op jit(solution)/shard_map/ppermute | solution.py:934
  291.7 2.6 collective-permute-start.35
  294.3 3.6 %expert_outputs.7 = (f32[3072,768]{1,0:T(8,128)}, f32[768,3072]{1,0:T(8,128)}) custom-call(s32[1]{0:T(128)S(6)} %sub.40.half_ref, bf16[4608,256]{1,0:T(8,128)(2,1)} %collective-permute-done.38.value_ref, f32[3072,768]{1,0:T(8,128)} %get-tuple-element.323.refs_0_, f32[768,3072]{1,0:T(8,128)} %get-tuple-element.317.refs_1_), custom_call_target="tpu_custom_call", output_to_operand_aliasing={{0}: (2, {}), {1}: (3, {})} | custom-call | flops 1179648 | bytes 7077888 | tf_op jit(solution)/shard_map/expert_outputs/pallas_call | solution.py:83
  297.8 3.4 %first_outputs.2 = (f32[768,2304]{1,0:T(8,128)}, f32[768,768]{1,0:T(8,128)}) custom-call(s32[1]{0:T(128)} %bitcast.1.side_ref.half_ref, bf16[3456,256]{1,0:T(8,128)(2,1)} %copy-done.2), custom_call_target="tpu_custom_call" | custom-call | flops 884736 | bytes 5308416 | tf_op jit(solution)/shard_map/first_outputs/pallas_call | solution.py:83
  302.4 3.4 %first_outputs.3 = (f32[768,2304]{1,0:T(8,128)}, f32[768,768]{1,0:T(8,128)}) custom-call(s32[1]{0:T(128)S(6)} %sub.40.half_ref, bf16[3456,256]{1,0:T(8,128)(2,1)} %copy-done.7, f32[768,2304]{1,0:T(8,128)} %get-tuple-element.328.refs_0_, f32[768,768]{1,0:T(8,128)} %get-tuple-element.326.refs_1_), custom_call_target="tpu_custom_call", output_to_operand_aliasing={{0}: (2, {}), {1}: (3, {})} | custom-call | flops 884736 | bytes 5308416 | tf_op jit(solution)/shard_map/first_outputs/pallas_call | solution.py:83
  306.0 2.1 collective-permute-done.39.got_ref
  309.0 3.4 %last_outputs.1 = (f32[768,2304]{1,0:T(8,128)}, f32[1,768]{1,0:T(1,128)}, f32[1,768]{1,0:T(1,128)}, f32[1,768]{1,0:T(1,128)}, f32[1,768]{1,0:T(1,128)}, /*index=...) custom-call(s32[1]{0:T(128)} %bitcast.1.side_ref.half_ref, ...), custom_call_target="tpu_custom_call", output_to_operand_aliasing={{0}: (4, {})} | custom-call | flops 327680 | bytes 1966080 | tf_op jit(solution)/shard_map/last_outputs/pallas_call | solution.py:83
  (144 shorter events, 41.3 us)
Async XLA Ops:
  0.6 6.1 %copy-start.15 = (f32[1,768]{1,0:T(1,128)S(1)}, f32[1,768]{1,0:T(1,128)}, u32[]{:S(2)}) copy-start(f32[1,768]{1,0:T(1,128)} %gain_ref.9) | copy-start | bytes 9220
  0.7 6.1 %copy-start.14 = (f32[1,768]{1,0:T(1,128)S(1)}, f32[1,768]{1,0:T(1,128)}, u32[]{:S(2)}) copy-start(f32[1,768]{1,0:T(1,128)} %shift_ref.6) | copy-start | bytes 9220
  1.8 16.7 %collective-permute-start = (bf16[256,768]{1,0:T(8,128)(2,1)S(1)}, bf16[256,768]{1,0:T(8,128)(2,1)S(1)}, u32[]{:S(2)}, u32[]{:S(2)}) collective-permute-start(bf16[256,768]{1,0:T(8,128)(2,1)S(1)} %get-tuple-element.377), channel_id=1, source_target_pairs={{0,1},{2,3},{4,5},{6,7},{8,9},{10,11},{12,13},{14,15},{16,17},{18,... | collective-permute-start | bytes 1179656 | tf_op jit(solution)/shard_map/ppermute | solution.py:1039
  6.8 11.7 %collective-permute-start.1 = (f32[2,768]{1,0:T(2,128)S(1)}, f32[2,768]{1,0:T(2,128)S(1)}, u32[]{:S(2)}, u32[]{:S(2)}) collective-permute-start(f32[2,768]{1,0:T(2,128)S(1)} %pad_maximum_fusion.14), channel_id=1, source_target_pairs={{0,1},{2,3},{4,5},{6,7},{8,9},{10,11},{12,13},{14,15},{16,17},{18,... | collective-permute-start | bytes 18440 | tf_op jit(solution)/shard_map/ppermute | solution.py:1039
  8.1 27.3 %collective-permute-start.2 = (bf16[256,768]{1,0:T(8,128)(2,1)S(1)}, bf16[256,768]{1,0:T(8,128)(2,1)S(1)}, u32[]{:S(2)}, u32[]{:S(2)}) collective-permute-start(bf16[256,768]{1,0:T(8,128)(2,1)S(1)} %get-tuple-element.376), channel_id=1, source_target_pairs={{0,1},{2,3},{4,5},{6,7},{8,9},{10,11},{12,13},{14,15},{16,17},{18,... | collective-permute-start | bytes 1179656 | tf_op jit(solution)/shard_map/ppermute | solution.py:1039
  9.4 8.5 %copy-start.17 = (f32[768]{0:T(1024)S(1)}, f32[768]{0:T(1024)}, u32[]{:S(2)}) copy-start(f32[768]{0:T(1024)} %param.24) | copy-start | bytes 9220
  97.5 20.1 %collective-permute-start.3 = (bf16[4608,256]{1,0:T(8,128)(2,1)}, bf16[4608,256]{1,0:T(8,128)(2,1)S(1)}, u32[]{:S(2)}, u32[]{:S(2)}) collective-permute-start(bf16[4608,256]{1,0:T(8,128)(2,1)} %get-tuple-element.195), channel_id=1, source_target_pairs={{0,2},{2,0},{4,6},{6,4},{8,10},{10,8},{12,14},{14,12},{16,18},{18,... | collective-permute-start | bytes 7077896 | tf_op jit(solution)/shard_map/ppermute | solution.py:934
  97.6 8.7 %collective-permute-start.4 = (bf16[4608,256]{1,0:T(8,128)(2,1)}, bf16[4608,256]{1,0:T(8,128)(2,1)S(1)}, u32[]{:S(2)}, u32[]{:S(2)}) collective-permute-start(bf16[4608,256]{1,0:T(8,128)(2,1)} %get-tuple-element.197), channel_id=1, source_target_pairs={{0,2},{2,0},{4,6},{6,4},{8,10},{10,8},{12,14},{14,12},{16,18},{18,... | collective-permute-start | bytes 7077896 | tf_op jit(solution)/shard_map/ppermute | solution.py:934
  98.1 8.2 %copy-start.5 = (bf16[4608,256]{1,0:T(8,128)(2,1)S(1)}, bf16[4608,256]{1,0:T(8,128)(2,1)}, u32[]{:S(2)}) copy-start(bf16[4608,256]{1,0:T(8,128)(2,1)} %get-tuple-element.201) | copy-start | bytes 7077892
  107.9 20.0 %collective-permute-start.6 = (bf16[2304,256]{1,0:T(8,128)(2,1)}, bf16[2304,256]{1,0:T(8,128)(2,1)S(1)}, u32[]{:S(2)}, u32[]{:S(2)}) collective-permute-start(bf16[2304,256]{1,0:T(8,128)(2,1)} %get-tuple-element.359), channel_id=1, source_target_pairs={{0,4},{2,10},{4,0},{6,14},{8,12},{10,2},{12,8},{14,6},{16,20},{18,... | collective-permute-start | bytes 3538952 | tf_op jit(solution)/shard_map/ppermute | solution.py:934
  109.4 8.2 %copy-start.4 = (bf16[4608,256]{1,0:T(8,128)(2,1)S(1)}, bf16[4608,256]{1,0:T(8,128)(2,1)}, u32[]{:S(2)}) copy-start(bf16[4608,256]{1,0:T(8,128)(2,1)} %get-tuple-element.209) | copy-start | bytes 7077892
  119.2 22.2 %collective-permute-start.5 = (bf16[2304,256]{1,0:T(8,128)(2,1)}, bf16[2304,256]{1,0:T(8,128)(2,1)S(1)}, u32[]{:S(2)}, u32[]{:S(2)}) collective-permute-start(bf16[2304,256]{1,0:T(8,128)(2,1)} %get-tuple-element.360), channel_id=1, source_target_pairs={{0,4},{2,10},{4,0},{6,14},{8,12},{10,2},{12,8},{14,6},{16,20},{18,... | collective-permute-start | bytes 3538952 | tf_op jit(solution)/shard_map/ppermute | solution.py:934
  130.4 23.9 %collective-permute-start.8 = (bf16[1152,256]{1,0:T(8,128)(2,1)S(1)}, bf16[1152,256]{1,0:T(8,128)(2,1)S(1)}, u32[]{:S(2)}, u32[]{:S(2)}) collective-permute-start(bf16[1152,256]{1,0:T(8,128)(2,1)S(1)} %get-tuple-element.371), channel_id=1, source_target_pairs={{0,16},{2,6},{4,20},{6,2},{8,24},{10,14},{12,28},{14,10},{16,0},{1... | collective-permute-start | bytes 1769480 | tf_op jit(solution)/shard_map/ppermute | solution.py:934
  142.6 32.5 %collective-permute-start.10 = (bf16[1152,256]{1,0:T(8,128)(2,1)}, bf16[1152,256]{1,0:T(8,128)(2,1)S(1)}, u32[]{:S(2)}, u32[]{:S(2)}) collective-permute-start(bf16[1152,256]{1,0:T(8,128)(2,1)} %get-tuple-element.369), channel_id=1, source_target_pairs={{0,16},{2,6},{4,20},{6,2},{8,24},{10,14},{12,28},{14,10},{16,0},{1... | collective-permute-start | bytes 1769480 | tf_op jit(solution)/shard_map/ppermute | solution.py:934
  154.3 10.6 %collective-permute-start.7 = (bf16[3456,256]{1,0:T(8,128)(2,1)}, bf16[3456,256]{1,0:T(8,128)(2,1)S(1)}, u32[]{:S(2)}, u32[]{:S(2)}) collective-permute-start(bf16[3456,256]{1,0:T(8,128)(2,1)} %get-tuple-element.235), channel_id=1, source_target_pairs={{0,2},{1,3},{2,0},{3,1},{4,6},{5,7},{6,4},{7,5},{8,10},{9,11},{10,... | collective-permute-start | bytes 5308424 | tf_op jit(solution)/shard_map/ppermute | solution.py:934
  155.2 9.7 %copy-start.6 = (bf16[3456,256]{1,0:T(8,128)(2,1)S(1)}, bf16[3456,256]{1,0:T(8,128)(2,1)}, u32[]{:S(2)}) copy-start(bf16[3456,256]{1,0:T(8,128)(2,1)} %get-tuple-element.240) | copy-start | bytes 5308420
  155.2 11.3 %collective-permute-start.11 = (bf16[576,256]{1,0:T(8,128)(2,1)}, bf16[576,256]{1,0:T(8,128)(2,1)S(1)}, u32[]{:S(2)}, u32[]{:S(2)}) collective-permute-start(bf16[576,256]{1,0:T(8,128)(2,1)} %get-tuple-element.387), channel_id=1, source_target_pairs={{0,8},{2,18},{4,12},{6,22},{8,0},{10,26},{12,4},{14,30},{16,24},{1... | collective-permute-start | bytes 884744 | tf_op jit(solution)/shard_map/ppermute | solution.py:934
  165.4 13.1 %collective-permute-start.9 = (bf16[1728,256]{1,0:T(8,128)(2,1)S(1)}, bf16[1728,256]{1,0:T(8,128)(2,1)S(1)}, u32[]{:S(2)}, u32[]{:S(2)}) collective-permute-start(bf16[1728,256]{1,0:T(8,128)(2,1)S(1)} %get-tuple-element.362), channel_id=1, source_target_pairs={{0,1},{1,0},{2,6},{3,7},{4,5},{5,4},{6,2},{7,3},{8,9},{9,8},{10,14... | collective-permute-start | bytes 2654216 | tf_op jit(solution)/shard_map/ppermute | solution.py:934
  166.6 20.3 %collective-permute-start.13 = (bf16[576,256]{1,0:T(8,128)(2,1)S(1)}, bf16[576,256]{1,0:T(8,128)(2,1)S(1)}, u32[]{:S(2)}, u32[]{:S(2)}) collective-permute-start(bf16[576,256]{1,0:T(8,128)(2,1)S(1)} %add_convert_fusion.17), channel_id=1, source_target_pairs={{0,8},{2,18},{4,12},{6,22},{8,0},{10,26},{12,4},{14,30},{16,24},{1... | collective-permute-start | bytes 884744 | tf_op jit(solution)/shard_map/ppermute | solution.py:934
  175.3 9.4 %collective-permute-start.14 = (bf16[576,256]{1,0:T(8,128)(2,1)S(1)}, bf16[576,256]{1,0:T(8,128)(2,1)S(1)}, u32[]{:S(2)}, u32[]{:S(2)}) collective-permute-start(bf16[576,256]{1,0:T(8,128)(2,1)S(1)} %get-tuple-element.385), channel_id=1, source_target_pairs={{0,8},{2,18},{4,12},{6,22},{8,0},{10,26},{12,4},{14,30},{16,24},{1... | collective-permute-start | bytes 884744 | tf_op jit(solution)/shard_map/ppermute | solution.py:934
  178.7 19.0 %collective-permute-start.17 = (bf16[864,256]{1,0:T(8,128)(2,1)S(1)}, bf16[864,256]{1,0:T(8,128)(2,1)S(1)}, u32[]{:S(2)}, u32[]{:S(2)}) collective-permute-start(bf16[864,256]{1,0:T(8,128)(2,1)S(1)} %get-tuple-element.375), channel_id=1, source_target_pairs={{0,4},{1,5},{2,3},{3,2},{4,0},{5,1},{6,7},{7,6},{8,12},{9,13},{10,... | collective-permute-start | bytes 1327112 | tf_op jit(solution)/shard_map/ppermute | solution.py:934
  184.7 14.2 %collective-permute-start.16 = (bf16[576,256]{1,0:T(8,128)(2,1)S(1)}, bf16[576,256]{1,0:T(8,128)(2,1)S(1)}, u32[]{:S(2)}, u32[]{:S(2)}) collective-permute-start(bf16[576,256]{1,0:T(8,128)(2,1)S(1)} %add_convert_fusion.14), channel_id=1, source_target_pairs={{0,8},{2,18},{4,12},{6,22},{8,0},{10,26},{12,4},{14,30},{16,24},{1... | collective-permute-start | bytes 884744 | tf_op jit(solution)/shard_map/ppermute | solution.py:934
  187.0 23.6 %collective-permute-start.15 = (bf16[1152,256]{1,0:T(8,128)(2,1)S(1)}, bf16[1152,256]{1,0:T(8,128)(2,1)S(1)}, u32[]{:S(2)}, u32[]{:S(2)}) collective-permute-start(bf16[1152,256]{1,0:T(8,128)(2,1)S(1)} %pad_maximum_fusion.7), channel_id=1, source_target_pairs={{0,16},{2,6},{4,20},{6,2},{8,24},{10,14},{12,28},{14,10},{16,0},{1... | collective-permute-start | bytes 1769480 | tf_op jit(solution)/shard_map/ppermute | solution.py:934
  190.3 20.5 %collective-permute-start.12 = (bf16[512,768]{1,0:T(8,128)(2,1)S(1)}, bf16[512,768]{1,0:T(8,128)(2,1)S(1)}, u32[]{:S(2)}, u32[]{:S(2)}) collective-permute-start(bf16[512,768]{1,0:T(8,128)(2,1)S(1)} %copy-done.18), channel_id=1, source_target_pairs={{1,0},{3,2},{5,4},{7,6},{9,8},{11,10},{13,12},{15,14},{17,16},{19,... | collective-permute-start | bytes 2359304 | tf_op jit(solution)/shard_map/ppermute | solution.py:1040
  197.7 24.2 %collective-permute-start.18 = (bf16[1280,256]{1,0:T(8,128)(2,1)}, bf16[1280,256]{1,0:T(8,128)(2,1)S(1)}, u32[]{:S(2)}, u32[]{:S(2)}) collective-permute-start(bf16[1280,256]{1,0:T(8,128)(2,1)} %get-tuple-element.264), channel_id=1, source_target_pairs={{0,2},{1,3},{2,0},{3,1},{4,6},{5,7},{6,4},{7,5},{8,10},{9,11},{10,... | collective-permute-start | bytes 1966088 | tf_op jit(solution)/shard_map/ppermute | solution.py:934
  197.9 26.0 %collective-permute-start.21 = (bf16[432,256]{1,0:T(8,128)(2,1)S(1)}, bf16[432,256]{1,0:T(8,128)(2,1)S(1)}, u32[]{:S(2)}, u32[]{:S(2)}) collective-permute-start(bf16[432,256]{1,0:T(8,128)(2,1)S(1)} %get-tuple-element.391), channel_id=1, source_target_pairs={{0,8},{1,9},{2,10},{3,11},{4,12},{5,13},{6,14},{7,15},{8,0},{9,1},... | collective-permute-start | bytes 663560 | tf_op jit(solution)/shard_map/ppermute | solution.py:934
  199.0 35.4 %collective-permute-start.23 = (bf16[1152,256]{1,0:T(8,128)(2,1)S(1)}, bf16[1152,256]{1,0:T(8,128)(2,1)}, u32[]{:S(2)}, u32[]{:S(2)}) collective-permute-start(bf16[1152,256]{1,0:T(8,128)(2,1)S(1)} %pad_maximum_fusion.8), channel_id=1, source_target_pairs={{0,16},{2,6},{4,20},{6,2},{8,24},{10,14},{12,28},{14,10},{16,0},{1... | collective-permute-start | bytes 1769480 | tf_op jit(solution)/shard_map/ppermute | solution.py:934
  210.8 19.8 %collective-permute-start.20 = (bf16[2304,256]{1,0:T(8,128)(2,1)S(1)}, bf16[2304,256]{1,0:T(8,128)(2,1)S(1)}, u32[]{:S(2)}, u32[]{:S(2)}) collective-permute-start(bf16[2304,256]{1,0:T(8,128)(2,1)S(1)} %pad_maximum_fusion.3), channel_id=1, source_target_pairs={{0,4},{2,10},{4,0},{6,14},{8,12},{10,2},{12,8},{14,6},{16,20},{18,... | collective-permute-start | bytes 3538952 | tf_op jit(solution)/shard_map/ppermute | solution.py:934
  223.9 7.4 %collective-permute-start.19 = (bf16[640,256]{1,0:T(8,128)(2,1)}, bf16[640,256]{1,0:T(8,128)(2,1)}, u32[]{:S(2)}, u32[]{:S(2)}) collective-permute-start(bf16[640,256]{1,0:T(8,128)(2,1)} %get-tuple-element.378), channel_id=1, source_target_pairs={{0,1},{1,0},{2,6},{3,7},{4,5},{5,4},{6,2},{7,3},{8,9},{9,8},{10,14... | collective-permute-start | bytes 983048 | tf_op jit(solution)/shard_map/ppermute | solution.py:934
  230.9 24.4 %collective-permute-start.29 = (bf16[4608,256]{1,0:T(8,128)(2,1)S(1)}, bf16[4608,256]{1,0:T(8,128)(2,1)}, u32[]{:S(2)}, u32[]{:S(2)}) collective-permute-start(bf16[4608,256]{1,0:T(8,128)(2,1)S(1)} %pad_maximum_fusion.value_ref), channel_id=1, source_target_pairs={{0,2},{2,0},{4,6},{6,4},{8,10},{10,8},{12,14},{14,12},{16,18},{18,... | collective-permute-start | bytes 7077896 | tf_op jit(solution)/shard_map/ppermute | solution.py:934
  231.0 9.1 %collective-permute-start.25 = (bf16[216,256]{1,0:T(8,128)(2,1)}, bf16[216,256]{1,0:T(8,128)(2,1)S(1)}, u32[]{:S(2)}, u32[]{:S(2)}) collective-permute-start(bf16[216,256]{1,0:T(8,128)(2,1)} %get-tuple-element.403), channel_id=1, source_target_pairs={{0,16},{1,17},{2,18},{3,19},{4,20},{5,21},{6,22},{7,23},{8,24},{9,... | collective-permute-start | bytes 331784 | tf_op jit(solution)/shard_map/ppermute | solution.py:934
  232.7 5.4 %collective-permute-start.22 = (bf16[320,256]{1,0:T(8,128)(2,1)S(1)}, bf16[320,256]{1,0:T(8,128)(2,1)S(1)}, u32[]{:S(2)}, u32[]{:S(2)}) collective-permute-start(bf16[320,256]{1,0:T(8,128)(2,1)S(1)} %get-tuple-element.394), channel_id=1, source_target_pairs={{0,4},{1,5},{2,3},{3,2},{4,0},{5,1},{6,7},{7,6},{8,12},{9,13},{10,... | collective-permute-start | bytes 491528 | tf_op jit(solution)/shard_map/ppermute | solution.py:934
  235.7 25.9 %collective-permute-start.31 = (bf16[2304,256]{1,0:T(8,128)(2,1)S(1)}, bf16[2304,256]{1,0:T(8,128)(2,1)}, u32[]{:S(2)}, u32[]{:S(2)}) collective-permute-start(bf16[2304,256]{1,0:T(8,128)(2,1)S(1)} %pad_maximum_fusion.4), channel_id=1, source_target_pairs={{0,4},{2,10},{4,0},{6,14},{8,12},{10,2},{12,8},{14,6},{16,20},{18,... | collective-permute-start | bytes 3538952 | tf_op jit(solution)/shard_map/ppermute | solution.py:934
  238.1 7.8 %collective-permute-start.24 = (bf16[160,256]{1,0:T(8,128)(2,1)S(1)}, bf16[160,256]{1,0:T(8,128)(2,1)S(1)}, u32[]{:S(2)}, u32[]{:S(2)}) collective-permute-start(bf16[160,256]{1,0:T(8,128)(2,1)S(1)} %get-tuple-element.406), channel_id=1, source_target_pairs={{0,8},{1,9},{2,10},{3,11},{4,12},{5,13},{6,14},{7,15},{8,0},{9,1},... | collective-permute-start | bytes 245768 | tf_op jit(solution)/shard_map/ppermute | solution.py:934
  240.2 7.0 %collective-permute-start.27 = (bf16[216,256]{1,0:T(8,128)(2,1)S(1)}, bf16[216,256]{1,0:T(8,128)(2,1)S(1)}, u32[]{:S(2)}, u32[]{:S(2)}) collective-permute-start(bf16[216,256]{1,0:T(8,128)(2,1)S(1)} %add_convert_fusion.24), channel_id=1, source_target_pairs={{0,16},{1,17},{2,18},{3,19},{4,20},{5,21},{6,22},{7,23},{8,24},{9,... | collective-permute-start | bytes 331784 | tf_op jit(solution)/shard_map/ppermute | solution.py:934
  246.0 5.2 %collective-permute-start.26 = (bf16[80,256]{1,0:T(8,128)(2,1)S(1)}, bf16[80,256]{1,0:T(8,128)(2,1)S(1)}, u32[]{:S(2)}, u32[]{:S(2)}) collective-permute-start(bf16[80,256]{1,0:T(8,128)(2,1)S(1)} %get-tuple-element.412), channel_id=1, source_target_pairs={{0,16},{1,17},{2,18},{3,19},{4,20},{5,21},{6,22},{7,23},{8,24},{9,... | collective-permute-start | bytes 122888 | tf_op jit(solution)/shard_map/ppermute | solution.py:934
  251.9 7.1 %collective-permute-start.28 = (bf16[80,256]{1,0:T(8,128)(2,1)}, bf16[80,256]{1,0:T(8,128)(2,1)}, u32[]{:S(2)}, u32[]{:S(2)}) collective-permute-start(bf16[80,256]{1,0:T(8,128)(2,1)} %add_convert_fusion.29), channel_id=1, source_target_pairs={{0,16},{1,17},{2,18},{3,19},{4,20},{5,21},{6,22},{7,23},{8,24},{9,... | collective-permute-start | bytes 122888 | tf_op jit(solution)/shard_map/ppermute | solution.py:934
  253.2 7.0 %collective-permute-start.32 = (bf16[432,256]{1,0:T(8,128)(2,1)}, bf16[432,256]{1,0:T(8,128)(2,1)S(1)}, u32[]{:S(2)}, u32[]{:S(2)}) collective-permute-start(bf16[432,256]{1,0:T(8,128)(2,1)} %pad_maximum_fusion.11), channel_id=1, source_target_pairs={{0,8},{1,9},{2,10},{3,11},{4,12},{5,13},{6,14},{7,15},{8,0},{9,1},... | collective-permute-start | bytes 663560 | tf_op jit(solution)/shard_map/ppermute | solution.py:934
  259.8 4.9 %collective-permute-start.30 = (bf16[160,256]{1,0:T(8,128)(2,1)S(1)}, bf16[160,256]{1,0:T(8,128)(2,1)S(1)}, u32[]{:S(2)}, u32[]{:S(2)}) collective-permute-start(bf16[160,256]{1,0:T(8,128)(2,1)S(1)} %pad_maximum_fusion.13), channel_id=1, source_target_pairs={{0,8},{1,9},{2,10},{3,11},{4,12},{5,13},{6,14},{7,15},{8,0},{9,1},... | collective-permute-start | bytes 245768 | tf_op jit(solution)/shard_map/ppermute | solution.py:934
  260.4 8.4 %collective-permute-start.34 = (bf16[864,256]{1,0:T(8,128)(2,1)S(1)}, bf16[864,256]{1,0:T(8,128)(2,1)S(1)}, u32[]{:S(2)}, u32[]{:S(2)}) collective-permute-start(bf16[864,256]{1,0:T(8,128)(2,1)S(1)} %pad_maximum_fusion.9), channel_id=1, source_target_pairs={{0,4},{1,5},{2,3},{3,2},{4,0},{5,1},{6,7},{7,6},{8,12},{9,13},{10,... | collective-permute-start | bytes 1327112 | tf_op jit(solution)/shard_map/ppermute | solution.py:934
  263.1 7.9 %copy-start = (bf16[4608,256]{1,0:T(8,128)(2,1)}, bf16[4608,256]{1,0:T(8,128)(2,1)S(1)}, u32[]{:S(2)}) copy-start(bf16[4608,256]{1,0:T(8,128)(2,1)S(1)} %pad_maximum_fusion.1.value_ref) | copy-start | bytes 7077892
  268.9 17.5 %collective-permute-start.36 = (bf16[1728,256]{1,0:T(8,128)(2,1)S(1)}, bf16[1728,256]{1,0:T(8,128)(2,1)}, u32[]{:S(2)}, u32[]{:S(2)}) collective-permute-start(bf16[1728,256]{1,0:T(8,128)(2,1)S(1)} %pad_maximum_fusion.5), channel_id=1, source_target_pairs={{0,1},{1,0},{2,6},{3,7},{4,5},{5,4},{6,2},{7,3},{8,9},{9,8},{10,14... | collective-permute-start | bytes 2654216 | tf_op jit(solution)/shard_map/ppermute | solution.py:934
  269.6 14.5 %collective-permute-start.33 = (bf16[320,256]{1,0:T(8,128)(2,1)S(1)}, bf16[320,256]{1,0:T(8,128)(2,1)}, u32[]{:S(2)}, u32[]{:S(2)}) collective-permute-start(bf16[320,256]{1,0:T(8,128)(2,1)S(1)} %pad_maximum_fusion.12), channel_id=1, source_target_pairs={{0,4},{1,5},{2,3},{3,2},{4,0},{5,1},{6,7},{7,6},{8,12},{9,13},{10,... | collective-permute-start | bytes 491528 | tf_op jit(solution)/shard_map/ppermute | solution.py:934
  271.1 23.2 %collective-permute-start.38 = (bf16[4608,256]{1,0:T(8,128)(2,1)S(1)}, bf16[4608,256]{1,0:T(8,128)(2,1)}, u32[]{:S(2)}, u32[]{:S(2)}) collective-permute-start(bf16[4608,256]{1,0:T(8,128)(2,1)S(1)} %pad_maximum_fusion.1.value_ref), channel_id=1, source_target_pairs={{0,2},{2,0},{4,6},{6,4},{8,10},{10,8},{12,14},{14,12},{16,18},{18,... | collective-permute-start | bytes 7077896 | tf_op jit(solution)/shard_map/ppermute | solution.py:934
  287.8 10.0 %copy-start.2 = (bf16[3456,256]{1,0:T(8,128)(2,1)}, bf16[3456,256]{1,0:T(8,128)(2,1)S(1)}, u32[]{:S(2)}) copy-start(bf16[3456,256]{1,0:T(8,128)(2,1)S(1)} %pad_maximum_fusion.2.value_ref) | copy-start | bytes 5308420
  287.8 13.4 %collective-permute-start.37 = (bf16[3456,256]{1,0:T(8,128)(2,1)S(1)}, bf16[3456,256]{1,0:T(8,128)(2,1)S(1)}, u32[]{:S(2)}, u32[]{:S(2)}) collective-permute-start(bf16[3456,256]{1,0:T(8,128)(2,1)S(1)} %pad_maximum_fusion.2.value_ref), channel_id=1, source_target_pairs={{0,2},{1,3},{2,0},{3,1},{4,6},{5,7},{6,4},{7,5},{8,10},{9,11},{10,... | collective-permute-start | bytes 5308424 | tf_op jit(solution)/shard_map/ppermute | solution.py:934
  291.7 14.1 %collective-permute-start.35 = (bf16[640,256]{1,0:T(8,128)(2,1)S(1)}, bf16[640,256]{1,0:T(8,128)(2,1)S(1)}, u32[]{:S(2)}, u32[]{:S(2)}) collective-permute-start(bf16[640,256]{1,0:T(8,128)(2,1)S(1)} %pad_maximum_fusion.10), channel_id=1, source_target_pairs={{0,1},{1,0},{2,6},{3,7},{4,5},{5,4},{6,2},{7,3},{8,9},{9,8},{10,14... | collective-permute-start | bytes 983048 | tf_op jit(solution)/shard_map/ppermute | solution.py:934
  305.9 2.2 collective-permute-start.39
  (12 other events, 28.1 us)

commit v14 on v8

--- a/solution.py
+++ b/solution.py
@@ -1182,9 +1182,10 @@
     c.step()
     p.step()
     s.step()
+    p.step()
     c.finish()
     outputs = unpack(side, 2, c.mine, outputs)
-    p.step()
+    p.finish()
     s.step()
     reduce_grad, expand_grad = unpack(1 - side, 2, c.got, outputs)
     s.finish()

time: 313 us -> 316 us (level)
  waiting for transfers between devices: 37.2 us -> 43 us
    ppermute x36, waiting for transfers between devices: 37.2 us -> 43 us  [swap(): lax.ppermute(value, axes, [(source, pair_of(source)) for source in range(...]
  transfers between devices with their start and end apart: 40 -> 40, of which waited for: 13 -> 12; matrix products, arithmetic and copies ran while one was open for 7% -> 7% of each run, Pallas kernels for 41% -> 40%
where the time goes in v14:
time: 316 us; the launch traced here: 311 us
  Pallas kernels  190 us (60%)
  starting transfers between devices  47.8 us (15%)
  waiting for transfers between devices  43 us (14%)
  other arithmetic  21.1 us (7%)
  local copies, waits for them, and re-layouts  7.23 us (2%)
    pallas_call x23, Pallas kernels, call(): pl.pallas_call(kernel, grid_spec=pltpu.PrefetchScalarGridSpec(num_scalar_...  190 us
    ppermute x36, waiting for transfers between devices, swap(): lax.ppermute(value, axes, [(source, pair_of(source)) for source in range(...  43 us
    ppermute x36, starting transfers between devices, swap(): lax.ppermute(value, axes, [(source, pair_of(source)) for source in range(...  39 us
    convert_element_type x14, other arithmetic, part(): return (cut(self.terms[0]) + cut(self.terms[1])).astype(bf16)  11.5 us
    ppermute x3, starting transfers between devices, on_device(): to_text = lambda value: lax.ppermute(value, 'mod', [(0, 1)])  7.5 us
    select_n x14, other arithmetic, step(): low = jnp.where(self.last == 0, mine, got)  6.5 us
  transfers between devices with their start and end apart: 40, of which 12 were waited for; matrix products, arithmetic and copies ran while one was open for 7% of the time, Pallas kernels for 40%

profile of v14, /device:TPU:0, one launch (start us, length us, event | category | flops | bytes accessed | tf_op | source)
XLA Modules:
  0.0 310.5 jit_solution(14706198865965220799)
XLA Ops:
  1.8 4.9 %collective-permute-start = (bf16[256,768]{1,0:T(8,128)(2,1)S(1)}, bf16[256,768]{1,0:T(8,128)(2,1)S(1)}, u32[]{:S(2)}, u32[]{:S(2)}) collective-permute-start(bf16[256,768]{1,0:T(8,128)(2,1)S(1)} %get-tuple-element.377), channel_id=1, source_target_pairs={{0,1},{2,3},{4,5},{6,7},{8,9},{10,11},{12,13},{14,15},{16,17},{18,... | collective-permute-start | bytes 1179656 | tf_op jit(solution)/shard_map/ppermute | solution.py:1039
  9.4 8.5 %project_rows.1 = (bf16[1024,768]{1,0:T(8,128)(2,1)}, bf16[1024,2304]{1,0:T(8,128)(2,1)}) custom-call(bf16[1024,768]{1,0:T(8,128)(2,1)} %bitcast.20, f32[1,768]{1,0:T(1,128)} %gain_ref.9, f32[1,768]{1,0:T(1,128)} %shift_ref.6, bf16[768,2304]{1,0:T(8,128)(2,1)} %weight_ref.3, f32[2,768]{1,0:T(2,128)} %bias_ref.5), custom_call_target="tpu_custom_call" | custom-call | flops 3623878656 | bytes 11403264 | tf_op jit(solution)/shard_map/project_rows/pallas_call | solution.py:83
  19.3 3.9 %image_rows.2 = (bf16[512,768]{1,0:T(8,128)(2,1)}, bf16[512,1536]{1,0:T(8,128)(2,1)}) custom-call(s32[1]{0:T(128)} %bitcast.flag_ref, bf16[1024,768]{1,0:T(8,128)(2,1)} %bitcast.21, bf16[256,768]{1,0:T(8,128)(2,1)} %copy-done.13, f32[1,768]{1,0:T(1,128)} %gain_ref.9, f32[1,768]{1,0:T(1,128)} %shift_ref.6, f32[2,768]{1,0:T(2,128)} %copy-done.16, ...), custom_call_target="tpu_custom_call" | custom-call | flops 603979776 | bytes 6291456 | tf_op jit(solution)/shard_map/image_rows/pallas_call | solution.py:83
  23.2 12.3 %attend_forward.2 = (bf16[512,768]{1,0:T(8,128)(2,1)}, f32[6,2,512]{2,1,0:T(2,128)}) custom-call(s32[1]{0:T(128)} %bitcast.flag_ref, s32[2]{0:T(128)} %count_ref.17, s32[2,4]{1,0:T(2,128)} %lengths_ref.15, bf16[1024,2304]{1,0:T(8,128)(2,1)} %get-tuple-element.244.q_ref.k_ref.v_ref, bf16[1024,2304]{1,0:T(8,128)(2,1)} %get-tuple-element.244.q_ref.k_ref.v_ref, ...), custom_call_target="tpu_custom_call" | custom-call | flops 4831838208 | bytes 6291456 | tf_op jit(solution)/shard_map/attend_forward/pallas_call | solution.py:83
  36.2 3.8 %image_rows.3 = (bf16[512,768]{1,0:T(8,128)(2,1)}, bf16[512,1536]{1,0:T(8,128)(2,1)}) custom-call(s32[1]{0:T(128)} %bitcast.flag_ref, bf16[1024,768]{1,0:T(8,128)(2,1)} %bitcast.22, bf16[256,768]{1,0:T(8,128)(2,1)} %copy-done.12, f32[1,768]{1,0:T(1,128)} %gain_ref.9, f32[1,768]{1,0:T(1,128)} %shift_ref.6, ...), custom_call_target="tpu_custom_call", output_to_operand_aliasing={{0}: (9, {}), {1}: (10, {})} | custom-call | flops 603979776 | bytes 6291456 | tf_op jit(solution)/shard_map/image_rows/pallas_call | solution.py:83
  40.0 12.3 %attend_forward.3 = (bf16[512,768]{1,0:T(8,128)(2,1)}, f32[6,2,512]{2,1,0:T(2,128)}) custom-call(s32[1]{0:T(128)} %bitcast.flag_ref, s32[2]{0:T(128)} %count_ref.17, s32[2,4]{1,0:T(2,128)} %lengths_ref.15, bf16[1024,2304]{1,0:T(8,128)(2,1)} %get-tuple-element.244.q_ref.k_ref.v_ref, bf16[1024,2304]{1,0:T(8,128)(2,1)} %get-tuple-element.244.q_ref.k_ref.v_ref, ...), custom_call_target="tpu_custom_call" | custom-call | flops 4831838208 | bytes 6291456 | tf_op jit(solution)/shard_map/attend_forward/pallas_call | solution.py:83
  52.3 45.2 %feed_forward.1 = (bf16[1024,768]{1,0:T(8,128)(2,1)}, f32[1024,768]{1,0:T(8,128)}, bf16[1024,768]{1,0:T(8,128)(2,1)}, bf16[768,768]{1,0:T(8,128)(2,1)}, f32[8,76...) custom-call(s32[1]{0:T(128)} %bitcast.flag_ref, ...), custom_call_target="tpu_custom_call" | custom-call | flops 28991029248 | bytes 41943040 | tf_op jit(solution)/shard_map/feed_forward/pallas_call | solution.py:83
  98.1 8.2 %attend_backward.6 = (bf16[1024,768]{1,0:T(8,128)(2,1)}, bf16[1024,768]{1,0:T(8,128)(2,1)}, bf16[1024,768]{1,0:T(8,128)(2,1)}, bf16[512,768]{1,0:T(8,128)(2,1)}, bf16[512,768]{1,0:T(8,128)(2,1)}) custom-call(s32[1]{0:T(128)} %bitcast.flag_ref, s32[2]{0:T(128)} %count_ref.17, s32[2,4]{1,0:T(2,128)} %lengths_ref.15, ...), custom_call_target="tpu_custom_call" | custom-call | flops 40265318400 | bytes 41943040 | tf_op jit(solution)/shard_map/attend_backward/pallas_call | solution.py:83
  106.3 1.6 add_convert_fusion
  109.4 8.2 %attend_backward.7 = (bf16[1024,768]{1,0:T(8,128)(2,1)}, bf16[1024,768]{1,0:T(8,128)(2,1)}, bf16[1024,768]{1,0:T(8,128)(2,1)}, bf16[512,768]{1,0:T(8,128)(2,1)}, bf16[512,768]{1,0:T(8,128)(2,1)}) custom-call(s32[1]{0:T(128)} %bitcast.flag_ref, s32[2]{0:T(128)} %count_ref.17, ...), custom_call_target="tpu_custom_call", output_to_operand_aliasing={{0}: (11, {}), {1}: (12, {}), {2}: (13, {}), {3}: (14, {}),... | custom-call | flops 40265318400 | bytes 41943040 | tf_op jit(solution)/shard_map/attend_backward/pallas_call | solution.py:83
  117.6 1.6 add_convert_fusion.1
  119.8 8.1 %attend_backward.8 = (bf16[1024,768]{1,0:T(8,128)(2,1)}, bf16[1024,768]{1,0:T(8,128)(2,1)}, bf16[1024,768]{1,0:T(8,128)(2,1)}, bf16[512,768]{1,0:T(8,128)(2,1)}, bf16[512,768]{1,0:T(8,128)(2,1)}) custom-call(s32[1]{0:T(128)} %bitcast.flag_ref, s32[2]{0:T(128)} %count_ref.17, ...), custom_call_target="tpu_custom_call", output_to_operand_aliasing={{0}: (11, {}), {1}: (12, {}), {2}: (13, {}), {3}: (14, {}),... | custom-call | flops 40265318400 | bytes 41943040 | tf_op jit(solution)/shard_map/attend_backward/pallas_call | solution.py:83
  128.9 1.5 add_convert_fusion.7
  130.4 2.7 collective-permute-start.8
  133.1 8.3 %attend_backward.9 = (bf16[1024,768]{1,0:T(8,128)(2,1)}, bf16[1024,768]{1,0:T(8,128)(2,1)}, bf16[1024,768]{1,0:T(8,128)(2,1)}, bf16[512,768]{1,0:T(8,128)(2,1)}, bf16[512,768]{1,0:T(8,128)(2,1)}) custom-call(s32[1]{0:T(128)} %bitcast.flag_ref, s32[2]{0:T(128)} %count_ref.17, ...), custom_call_target="tpu_custom_call", output_to_operand_aliasing={{0}: (11, {}), {1}: (12, {}), {2}: (13, {}), {3}: (14, {}),... | custom-call | flops 40265318400 | bytes 41943040 | tf_op jit(solution)/shard_map/attend_backward/pallas_call | solution.py:83
  142.6 2.4 collective-permute-start.10
  145.0 9.3 %weight_grads.2 = (f32[2,512]{1,0:T(2,128)}, bf16[3456,256]{1,0:T(8,128)(2,1)}, bf16[3456,256]{1,0:T(8,128)(2,1)}) custom-call(s32[1]{0:T(128)} %bitcast.1.side_ref.half_ref, bf16[1024,768]{1,0:T(8,128)(2,1)} %get-tuple-element.260.normed_ref, bf16[512,768]{1,0:T(8,128)(2,1)} %get-tuple-element.228.image_ref, ...), custom_call_target="tpu_custom_call" | custom-call | flops 32212254720 | bytes 125829120 | tf_op jit(solution)/shard_map/weight_grads/pallas_call | solution.py:83
  155.3 1.6 collective-permute-start.11
  156.8 8.1 %attend_backward.10 = (bf16[1024,768]{1,0:T(8,128)(2,1)}, bf16[1024,768]{1,0:T(8,128)(2,1)}, bf16[1024,768]{1,0:T(8,128)(2,1)}, bf16[512,768]{1,0:T(8,128)(2,1)}, bf16[512,768]{1,0:T(8,128)(2,1)}) custom-call(s32[1]{0:T(128)} %bitcast.flag_ref, s32[2]{0:T(128)} %count_ref.17, ...), custom_call_target="tpu_custom_call", output_to_operand_aliasing={{0}: (11, {}), {1}: (12, {}), {2}: (13, {}), {3}: (14, {}),... | custom-call | flops 40265318400 | bytes 41943040 | tf_op jit(solution)/shard_map/attend_backward/pallas_call | solution.py:83
  166.7 8.4 %attend_backward.11 = (bf16[1024,768]{1,0:T(8,128)(2,1)}, bf16[1024,768]{1,0:T(8,128)(2,1)}, bf16[1024,768]{1,0:T(8,128)(2,1)}, bf16[512,768]{1,0:T(8,128)(2,1)}, bf16[512,768]{1,0:T(8,128)(2,1)}) custom-call(s32[1]{0:T(128)} %bitcast.flag_ref, s32[2]{0:T(128)} %count_ref.17, ...), custom_call_target="tpu_custom_call", output_to_operand_aliasing={{0}: (11, {}), {1}: (12, {}), {2}: (13, {}), {3}: (14, {}),... | custom-call | flops 40265318400 | bytes 41943040 | tf_op jit(solution)/shard_map/attend_backward/pallas_call | solution.py:83
  175.3 2.1 collective-permute-start.14
  178.7 1.6 collective-permute-start.17
  180.3 4.4 %image_grads.1.near_ref = bf16[512,768]{1,0:T(8,128)(2,1)} custom-call(bf16[768,2304]{1,0:T(8,128)(2,1)} %weight_ref.3, bf16[768,2304]{1,0:T(8,128)(2,1)} %weight_ref.3, bf16[512,768]{1,0:T(8,128)(2,1)} %get-tuple-element.255.keys_ref.gik_ref, bf16[512,768]{1,0:T(8,128)(2,1)} %get-tuple-element.249.values_ref.giv_ref), custom_call_target="tpu_custom_call" | custom-call | flops 12079595520 | bytes 62914560 | tf_op jit(solution)/shard_map/image_grads/pallas_call | solution.py:83
  184.7 2.1 collective-permute-start.16
  187.0 3.3 %collective-permute-start.15 = (bf16[1152,256]{1,0:T(8,128)(2,1)S(1)}, bf16[1152,256]{1,0:T(8,128)(2,1)S(1)}, u32[]{:S(2)}, u32[]{:S(2)}) collective-permute-start(bf16[1152,256]{1,0:T(8,128)(2,1)S(1)} %pad_maximum_fusion.7), channel_id=1, source_target_pairs={{0,16},{2,6},{4,20},{6,2},{8,24},{10,14},{12,28},{14,10},{16,0},{1... | collective-permute-start | bytes 1769480 | tf_op jit(solution)/shard_map/ppermute | solution.py:934
  191.6 6.1 %weight_grads.3 = (f32[2,256]{1,0:T(2,128)}, bf16[1280,256]{1,0:T(8,128)(2,1)}, bf16[1280,256]{1,0:T(8,128)(2,1)}) custom-call(s32[1]{0:T(128)} %bitcast.1.side_ref.half_ref, bf16[1024,768]{1,0:T(8,128)(2,1)} %get-tuple-element.260.normed_ref, bf16[512,768]{1,0:T(8,128)(2,1)} %get-tuple-element.228.image_ref, bf16[1024,768]{1,0:T(8,128)(2,1)} %get-tuple-element.261.gq_ref, ...), custom_call_target="tpu_custom_call" | custom-call | flops 16106127360 | bytes 125829120 | tf_op jit(solution)/shard_map/weight_grads/pallas_call | solution.py:83
  199.1 11.4 %collective-permute-done.15 = bf16[1152,256]{1,0:T(8,128)(2,1)S(1)} collective-permute-done((bf16[1152,256]{1,0:T(8,128)(2,1)S(1)}, bf16[1152,256]{1,0:T(8,128)(2,1)S(1)}, u32[]{:S(2)}, u32[]{:S(2)}) %collective-permute-start.15) | collective-permute-done | bytes 589856 | tf_op jit(solution)/shard_map/ppermute | solution.py:934
  211.7 10.1 %finish_rows.1 = (bf16[1024,768]{1,0:T(8,128)(2,1)}, bf16[1280,256]{1,0:T(8,128)(2,1)}) custom-call(s32[1]{0:T(128)} %bitcast.flag_ref, bf16[1024,768]{1,0:T(8,128)(2,1)} %bitcast.24, f32[1024,768]{1,0:T(8,128)} %get-tuple-element.273.gmid_ref, bf16[512,768]{1,0:T(8,128)(2,1)} %image_grads.1.near_ref, ...), custom_call_target="tpu_custom_call", output_to_operand_aliasing={{1}: (13, {})} | custom-call | flops 36238786560 | bytes 167772160 | tf_op jit(solution)/shard_map/finish_rows/pallas_call | solution.py:83
  221.8 2.0 add_convert_fusion.12
  224.6 2.4 collective-permute-done.20
  227.3 3.5 %collective-permute-start.29 = (bf16[4608,256]{1,0:T(8,128)(2,1)S(1)}, bf16[4608,256]{1,0:T(8,128)(2,1)}, u32[]{:S(2)}, u32[]{:S(2)}) collective-permute-start(bf16[4608,256]{1,0:T(8,128)(2,1)S(1)} %pad_maximum_fusion.value_ref), channel_id=1, source_target_pairs={{0,2},{2,0},{4,6},{6,4},{8,10},{10,8},{12,14},{14,12},{16,18},{18,... | collective-permute-start | bytes 7077896 | tf_op jit(solution)/shard_map/ppermute | solution.py:934
  232.3 2.1 collective-permute-start.22
  235.7 2.0 collective-permute-done.22
  237.7 1.6 collective-permute-start.24
  239.3 3.0 collective-permute-start.27
  242.3 3.6 %expert_outputs.4 = (f32[3072,768]{1,0:T(8,128)}, f32[768,3072]{1,0:T(8,128)}) custom-call(s32[1]{0:T(128)} %bitcast.1.side_ref.half_ref, bf16[4608,256]{1,0:T(8,128)(2,1)} %copy-done.1), custom_call_target="tpu_custom_call" | custom-call | flops 1179648 | bytes 7077888 | tf_op jit(solution)/shard_map/expert_outputs/pallas_call | solution.py:83
  245.9 1.6 collective-permute-start.26
  248.2 2.8 collective-permute-done.26
  251.6 1.9 collective-permute-start.28
  253.5 2.5 collective-permute-start.32
  256.0 3.6 %expert_outputs.5 = (f32[3072,768]{1,0:T(8,128)}, f32[768,3072]{1,0:T(8,128)}) custom-call(s32[1]{0:T(128)S(6)} %sub.49.half_ref, bf16[4608,256]{1,0:T(8,128)(2,1)} %collective-permute-done.29.value_ref, f32[3072,768]{1,0:T(8,128)} %get-tuple-element.303.refs_0_, f32[768,3072]{1,0:T(8,128)} %get-tuple-element.295.refs_1_), custom_call_target="tpu_custom_call", output_to_operand_aliasing={{0}: (2, {}), {1}: (3, {})} | custom-call | flops 1179648 | bytes 7077888 | tf_op jit(solution)/shard_map/expert_outputs/pallas_call | solution.py:83
  266.0 4.5 %collective-permute-done.34 = bf16[864,256]{1,0:T(8,128)(2,1)S(1)} collective-permute-done((bf16[864,256]{1,0:T(8,128)(2,1)S(1)}, bf16[864,256]{1,0:T(8,128)(2,1)S(1)}, u32[]{:S(2)}, u32[]{:S(2)}) %collective-permute-start.34) | collective-permute-done | bytes 442400 | tf_op jit(solution)/shard_map/ppermute | solution.py:934
  273.9 3.6 %expert_outputs.6 = (f32[3072,768]{1,0:T(8,128)}, f32[768,3072]{1,0:T(8,128)}) custom-call(s32[1]{0:T(128)} %bitcast.1.side_ref.half_ref, bf16[4608,256]{1,0:T(8,128)(2,1)} %copy-done, f32[3072,768]{1,0:T(8,128)} %get-tuple-element.318.refs_0_, f32[768,3072]{1,0:T(8,128)} %get-tuple-element.304.refs_1_), custom_call_target="tpu_custom_call", output_to_operand_aliasing={{0}: (2, {}), {1}: (3, {})} | custom-call | flops 1179648 | bytes 7077888 | tf_op jit(solution)/shard_map/expert_outputs/pallas_call | solution.py:83
  277.4 13.5 %collective-permute-done.35 = bf16[640,256]{1,0:T(8,128)(2,1)} collective-permute-done((bf16[640,256]{1,0:T(8,128)(2,1)}, bf16[640,256]{1,0:T(8,128)(2,1)}, u32[]{:S(2)}, u32[]{:S(2)}) %collective-permute-start.35) | collective-permute-done | bytes 327712 | tf_op jit(solution)/shard_map/ppermute | solution.py:934
  294.3 3.6 %expert_outputs.7 = (f32[3072,768]{1,0:T(8,128)}, f32[768,3072]{1,0:T(8,128)}) custom-call(s32[1]{0:T(128)S(6)} %sub.49.half_ref, bf16[4608,256]{1,0:T(8,128)(2,1)} %collective-permute-done.38.value_ref, f32[3072,768]{1,0:T(8,128)} %get-tuple-element.325.refs_0_, f32[768,3072]{1,0:T(8,128)} %get-tuple-element.319.refs_1_), custom_call_target="tpu_custom_call", output_to_operand_aliasing={{0}: (2, {}), {1}: (3, {})} | custom-call | flops 1179648 | bytes 7077888 | tf_op jit(solution)/shard_map/expert_outputs/pallas_call | solution.py:83
  297.9 3.4 %first_outputs.2 = (f32[768,2304]{1,0:T(8,128)}, f32[768,768]{1,0:T(8,128)}) custom-call(s32[1]{0:T(128)} %bitcast.1.side_ref.half_ref, bf16[3456,256]{1,0:T(8,128)(2,1)} %copy-done.2), custom_call_target="tpu_custom_call" | custom-call | flops 884736 | bytes 5308416 | tf_op jit(solution)/shard_map/first_outputs/pallas_call | solution.py:83
  302.5 3.4 %first_outputs.3 = (f32[768,2304]{1,0:T(8,128)}, f32[768,768]{1,0:T(8,128)}) custom-call(s32[1]{0:T(128)S(6)} %sub.49.half_ref, bf16[3456,256]{1,0:T(8,128)(2,1)} %copy-done.7, f32[768,2304]{1,0:T(8,128)} %get-tuple-element.330.refs_0_, f32[768,768]{1,0:T(8,128)} %get-tuple-element.328.refs_1_), custom_call_target="tpu_custom_call", output_to_operand_aliasing={{0}: (2, {}), {1}: (3, {})} | custom-call | flops 884736 | bytes 5308416 | tf_op jit(solution)/shard_map/first_outputs/pallas_call | solution.py:83
  306.7 3.4 %last_outputs.1 = (f32[768,2304]{1,0:T(8,128)}, f32[1,768]{1,0:T(1,128)}, f32[1,768]{1,0:T(1,128)}, f32[1,768]{1,0:T(1,128)}, f32[1,768]{1,0:T(1,128)}, /*index=...) custom-call(s32[1]{0:T(128)} %bitcast.1.side_ref.half_ref, ...), custom_call_target="tpu_custom_call", output_to_operand_aliasing={{0}: (4, {})} | custom-call | flops 327680 | bytes 1966080 | tf_op jit(solution)/shard_map/last_outputs/pallas_call | solution.py:83
  (144 shorter events, 39.2 us)
Async XLA Ops:
  0.6 6.1 %copy-start.15 = (f32[1,768]{1,0:T(1,128)S(1)}, f32[1,768]{1,0:T(1,128)}, u32[]{:S(2)}) copy-start(f32[1,768]{1,0:T(1,128)} %gain_ref.9) | copy-start | bytes 9220
  0.7 6.1 %copy-start.14 = (f32[1,768]{1,0:T(1,128)S(1)}, f32[1,768]{1,0:T(1,128)}, u32[]{:S(2)}) copy-start(f32[1,768]{1,0:T(1,128)} %shift_ref.6) | copy-start | bytes 9220
  1.8 16.7 %collective-permute-start = (bf16[256,768]{1,0:T(8,128)(2,1)S(1)}, bf16[256,768]{1,0:T(8,128)(2,1)S(1)}, u32[]{:S(2)}, u32[]{:S(2)}) collective-permute-start(bf16[256,768]{1,0:T(8,128)(2,1)S(1)} %get-tuple-element.377), channel_id=1, source_target_pairs={{0,1},{2,3},{4,5},{6,7},{8,9},{10,11},{12,13},{14,15},{16,17},{18,... | collective-permute-start | bytes 1179656 | tf_op jit(solution)/shard_map/ppermute | solution.py:1039
  6.8 11.7 %collective-permute-start.1 = (f32[2,768]{1,0:T(2,128)S(1)}, f32[2,768]{1,0:T(2,128)S(1)}, u32[]{:S(2)}, u32[]{:S(2)}) collective-permute-start(f32[2,768]{1,0:T(2,128)S(1)} %pad_maximum_fusion.14), channel_id=1, source_target_pairs={{0,1},{2,3},{4,5},{6,7},{8,9},{10,11},{12,13},{14,15},{16,17},{18,... | collective-permute-start | bytes 18440 | tf_op jit(solution)/shard_map/ppermute | solution.py:1039
  8.1 27.3 %collective-permute-start.2 = (bf16[256,768]{1,0:T(8,128)(2,1)S(1)}, bf16[256,768]{1,0:T(8,128)(2,1)S(1)}, u32[]{:S(2)}, u32[]{:S(2)}) collective-permute-start(bf16[256,768]{1,0:T(8,128)(2,1)S(1)} %get-tuple-element.376), channel_id=1, source_target_pairs={{0,1},{2,3},{4,5},{6,7},{8,9},{10,11},{12,13},{14,15},{16,17},{18,... | collective-permute-start | bytes 1179656 | tf_op jit(solution)/shard_map/ppermute | solution.py:1039
  9.4 8.5 %copy-start.17 = (f32[768]{0:T(1024)S(1)}, f32[768]{0:T(1024)}, u32[]{:S(2)}) copy-start(f32[768]{0:T(1024)} %param.24) | copy-start | bytes 9220
  97.5 20.1 %collective-permute-start.3 = (bf16[4608,256]{1,0:T(8,128)(2,1)}, bf16[4608,256]{1,0:T(8,128)(2,1)S(1)}, u32[]{:S(2)}, u32[]{:S(2)}) collective-permute-start(bf16[4608,256]{1,0:T(8,128)(2,1)} %get-tuple-element.195), channel_id=1, source_target_pairs={{0,2},{2,0},{4,6},{6,4},{8,10},{10,8},{12,14},{14,12},{16,18},{18,... | collective-permute-start | bytes 7077896 | tf_op jit(solution)/shard_map/ppermute | solution.py:934
  97.6 8.7 %collective-permute-start.4 = (bf16[4608,256]{1,0:T(8,128)(2,1)}, bf16[4608,256]{1,0:T(8,128)(2,1)S(1)}, u32[]{:S(2)}, u32[]{:S(2)}) collective-permute-start(bf16[4608,256]{1,0:T(8,128)(2,1)} %get-tuple-element.197), channel_id=1, source_target_pairs={{0,2},{2,0},{4,6},{6,4},{8,10},{10,8},{12,14},{14,12},{16,18},{18,... | collective-permute-start | bytes 7077896 | tf_op jit(solution)/shard_map/ppermute | solution.py:934
  98.1 8.2 %copy-start.5 = (bf16[4608,256]{1,0:T(8,128)(2,1)S(1)}, bf16[4608,256]{1,0:T(8,128)(2,1)}, u32[]{:S(2)}) copy-start(bf16[4608,256]{1,0:T(8,128)(2,1)} %get-tuple-element.201) | copy-start | bytes 7077892
  107.9 20.0 %collective-permute-start.6 = (bf16[2304,256]{1,0:T(8,128)(2,1)}, bf16[2304,256]{1,0:T(8,128)(2,1)S(1)}, u32[]{:S(2)}, u32[]{:S(2)}) collective-permute-start(bf16[2304,256]{1,0:T(8,128)(2,1)} %get-tuple-element.359), channel_id=1, source_target_pairs={{0,4},{2,10},{4,0},{6,14},{8,12},{10,2},{12,8},{14,6},{16,20},{18,... | collective-permute-start | bytes 3538952 | tf_op jit(solution)/shard_map/ppermute | solution.py:934
  109.4 8.2 %copy-start.4 = (bf16[4608,256]{1,0:T(8,128)(2,1)S(1)}, bf16[4608,256]{1,0:T(8,128)(2,1)}, u32[]{:S(2)}) copy-start(bf16[4608,256]{1,0:T(8,128)(2,1)} %get-tuple-element.209) | copy-start | bytes 7077892
  119.2 22.2 %collective-permute-start.5 = (bf16[2304,256]{1,0:T(8,128)(2,1)}, bf16[2304,256]{1,0:T(8,128)(2,1)S(1)}, u32[]{:S(2)}, u32[]{:S(2)}) collective-permute-start(bf16[2304,256]{1,0:T(8,128)(2,1)} %get-tuple-element.360), channel_id=1, source_target_pairs={{0,4},{2,10},{4,0},{6,14},{8,12},{10,2},{12,8},{14,6},{16,20},{18,... | collective-permute-start | bytes 3538952 | tf_op jit(solution)/shard_map/ppermute | solution.py:934
  130.4 23.9 %collective-permute-start.8 = (bf16[1152,256]{1,0:T(8,128)(2,1)S(1)}, bf16[1152,256]{1,0:T(8,128)(2,1)S(1)}, u32[]{:S(2)}, u32[]{:S(2)}) collective-permute-start(bf16[1152,256]{1,0:T(8,128)(2,1)S(1)} %get-tuple-element.371), channel_id=1, source_target_pairs={{0,16},{2,6},{4,20},{6,2},{8,24},{10,14},{12,28},{14,10},{16,0},{1... | collective-permute-start | bytes 1769480 | tf_op jit(solution)/shard_map/ppermute | solution.py:934
  142.6 32.5 %collective-permute-start.10 = (bf16[1152,256]{1,0:T(8,128)(2,1)}, bf16[1152,256]{1,0:T(8,128)(2,1)S(1)}, u32[]{:S(2)}, u32[]{:S(2)}) collective-permute-start(bf16[1152,256]{1,0:T(8,128)(2,1)} %get-tuple-element.369), channel_id=1, source_target_pairs={{0,16},{2,6},{4,20},{6,2},{8,24},{10,14},{12,28},{14,10},{16,0},{1... | collective-permute-start | bytes 1769480 | tf_op jit(solution)/shard_map/ppermute | solution.py:934
  154.3 10.6 %collective-permute-start.7 = (bf16[3456,256]{1,0:T(8,128)(2,1)}, bf16[3456,256]{1,0:T(8,128)(2,1)S(1)}, u32[]{:S(2)}, u32[]{:S(2)}) collective-permute-start(bf16[3456,256]{1,0:T(8,128)(2,1)} %get-tuple-element.235), channel_id=1, source_target_pairs={{0,2},{1,3},{2,0},{3,1},{4,6},{5,7},{6,4},{7,5},{8,10},{9,11},{10,... | collective-permute-start | bytes 5308424 | tf_op jit(solution)/shard_map/ppermute | solution.py:934
  155.3 9.7 %copy-start.6 = (bf16[3456,256]{1,0:T(8,128)(2,1)S(1)}, bf16[3456,256]{1,0:T(8,128)(2,1)}, u32[]{:S(2)}) copy-start(bf16[3456,256]{1,0:T(8,128)(2,1)} %get-tuple-element.240) | copy-start | bytes 5308420
  155.3 11.3 %collective-permute-start.11 = (bf16[576,256]{1,0:T(8,128)(2,1)}, bf16[576,256]{1,0:T(8,128)(2,1)S(1)}, u32[]{:S(2)}, u32[]{:S(2)}) collective-permute-start(bf16[576,256]{1,0:T(8,128)(2,1)} %get-tuple-element.387), channel_id=1, source_target_pairs={{0,8},{2,18},{4,12},{6,22},{8,0},{10,26},{12,4},{14,30},{16,24},{1... | collective-permute-start | bytes 884744 | tf_op jit(solution)/shard_map/ppermute | solution.py:934
  165.4 13.1 %collective-permute-start.9 = (bf16[1728,256]{1,0:T(8,128)(2,1)S(1)}, bf16[1728,256]{1,0:T(8,128)(2,1)S(1)}, u32[]{:S(2)}, u32[]{:S(2)}) collective-permute-start(bf16[1728,256]{1,0:T(8,128)(2,1)S(1)} %get-tuple-element.362), channel_id=1, source_target_pairs={{0,1},{1,0},{2,6},{3,7},{4,5},{5,4},{6,2},{7,3},{8,9},{9,8},{10,14... | collective-permute-start | bytes 2654216 | tf_op jit(solution)/shard_map/ppermute | solution.py:934
  166.6 20.3 %collective-permute-start.13 = (bf16[576,256]{1,0:T(8,128)(2,1)S(1)}, bf16[576,256]{1,0:T(8,128)(2,1)S(1)}, u32[]{:S(2)}, u32[]{:S(2)}) collective-permute-start(bf16[576,256]{1,0:T(8,128)(2,1)S(1)} %add_convert_fusion.17), channel_id=1, source_target_pairs={{0,8},{2,18},{4,12},{6,22},{8,0},{10,26},{12,4},{14,30},{16,24},{1... | collective-permute-start | bytes 884744 | tf_op jit(solution)/shard_map/ppermute | solution.py:934
  175.3 9.4 %collective-permute-start.14 = (bf16[576,256]{1,0:T(8,128)(2,1)S(1)}, bf16[576,256]{1,0:T(8,128)(2,1)S(1)}, u32[]{:S(2)}, u32[]{:S(2)}) collective-permute-start(bf16[576,256]{1,0:T(8,128)(2,1)S(1)} %get-tuple-element.385), channel_id=1, source_target_pairs={{0,8},{2,18},{4,12},{6,22},{8,0},{10,26},{12,4},{14,30},{16,24},{1... | collective-permute-start | bytes 884744 | tf_op jit(solution)/shard_map/ppermute | solution.py:934
  178.7 19.0 %collective-permute-start.17 = (bf16[864,256]{1,0:T(8,128)(2,1)S(1)}, bf16[864,256]{1,0:T(8,128)(2,1)S(1)}, u32[]{:S(2)}, u32[]{:S(2)}) collective-permute-start(bf16[864,256]{1,0:T(8,128)(2,1)S(1)} %get-tuple-element.375), channel_id=1, source_target_pairs={{0,4},{1,5},{2,3},{3,2},{4,0},{5,1},{6,7},{7,6},{8,12},{9,13},{10,... | collective-permute-start | bytes 1327112 | tf_op jit(solution)/shard_map/ppermute | solution.py:934
  184.7 14.2 %collective-permute-start.16 = (bf16[576,256]{1,0:T(8,128)(2,1)S(1)}, bf16[576,256]{1,0:T(8,128)(2,1)S(1)}, u32[]{:S(2)}, u32[]{:S(2)}) collective-permute-start(bf16[576,256]{1,0:T(8,128)(2,1)S(1)} %add_convert_fusion.14), channel_id=1, source_target_pairs={{0,8},{2,18},{4,12},{6,22},{8,0},{10,26},{12,4},{14,30},{16,24},{1... | collective-permute-start | bytes 884744 | tf_op jit(solution)/shard_map/ppermute | solution.py:934
  187.0 23.6 %collective-permute-start.15 = (bf16[1152,256]{1,0:T(8,128)(2,1)S(1)}, bf16[1152,256]{1,0:T(8,128)(2,1)S(1)}, u32[]{:S(2)}, u32[]{:S(2)}) collective-permute-start(bf16[1152,256]{1,0:T(8,128)(2,1)S(1)} %pad_maximum_fusion.7), channel_id=1, source_target_pairs={{0,16},{2,6},{4,20},{6,2},{8,24},{10,14},{12,28},{14,10},{16,0},{1... | collective-permute-start | bytes 1769480 | tf_op jit(solution)/shard_map/ppermute | solution.py:934
  190.3 20.5 %collective-permute-start.12 = (bf16[512,768]{1,0:T(8,128)(2,1)S(1)}, bf16[512,768]{1,0:T(8,128)(2,1)S(1)}, u32[]{:S(2)}, u32[]{:S(2)}) collective-permute-start(bf16[512,768]{1,0:T(8,128)(2,1)S(1)} %copy-done.18), channel_id=1, source_target_pairs={{1,0},{3,2},{5,4},{7,6},{9,8},{11,10},{13,12},{15,14},{17,16},{19,... | collective-permute-start | bytes 2359304 | tf_op jit(solution)/shard_map/ppermute | solution.py:1040
  197.7 24.2 %collective-permute-start.18 = (bf16[1280,256]{1,0:T(8,128)(2,1)}, bf16[1280,256]{1,0:T(8,128)(2,1)S(1)}, u32[]{:S(2)}, u32[]{:S(2)}) collective-permute-start(bf16[1280,256]{1,0:T(8,128)(2,1)} %get-tuple-element.264), channel_id=1, source_target_pairs={{0,2},{1,3},{2,0},{3,1},{4,6},{5,7},{6,4},{7,5},{8,10},{9,11},{10,... | collective-permute-start | bytes 1966088 | tf_op jit(solution)/shard_map/ppermute | solution.py:934
  197.9 26.0 %collective-permute-start.21 = (bf16[432,256]{1,0:T(8,128)(2,1)S(1)}, bf16[432,256]{1,0:T(8,128)(2,1)S(1)}, u32[]{:S(2)}, u32[]{:S(2)}) collective-permute-start(bf16[432,256]{1,0:T(8,128)(2,1)S(1)} %get-tuple-element.391), channel_id=1, source_target_pairs={{0,8},{1,9},{2,10},{3,11},{4,12},{5,13},{6,14},{7,15},{8,0},{9,1},... | collective-permute-start | bytes 663560 | tf_op jit(solution)/shard_map/ppermute | solution.py:934
  199.0 35.3 %collective-permute-start.23 = (bf16[1152,256]{1,0:T(8,128)(2,1)S(1)}, bf16[1152,256]{1,0:T(8,128)(2,1)}, u32[]{:S(2)}, u32[]{:S(2)}) collective-permute-start(bf16[1152,256]{1,0:T(8,128)(2,1)S(1)} %pad_maximum_fusion.8), channel_id=1, source_target_pairs={{0,16},{2,6},{4,20},{6,2},{8,24},{10,14},{12,28},{14,10},{16,0},{1... | collective-permute-start | bytes 1769480 | tf_op jit(solution)/shard_map/ppermute | solution.py:934
  210.7 16.3 %collective-permute-start.20 = (bf16[2304,256]{1,0:T(8,128)(2,1)S(1)}, bf16[2304,256]{1,0:T(8,128)(2,1)S(1)}, u32[]{:S(2)}, u32[]{:S(2)}) collective-permute-start(bf16[2304,256]{1,0:T(8,128)(2,1)S(1)} %pad_maximum_fusion.3), channel_id=1, source_target_pairs={{0,4},{2,10},{4,0},{6,14},{8,12},{10,2},{12,8},{14,6},{16,20},{18,... | collective-permute-start | bytes 3538952 | tf_op jit(solution)/shard_map/ppermute | solution.py:934
  223.8 7.4 %collective-permute-start.19 = (bf16[640,256]{1,0:T(8,128)(2,1)}, bf16[640,256]{1,0:T(8,128)(2,1)}, u32[]{:S(2)}, u32[]{:S(2)}) collective-permute-start(bf16[640,256]{1,0:T(8,128)(2,1)} %get-tuple-element.378), channel_id=1, source_target_pairs={{0,1},{1,0},{2,3},{3,2},{4,5},{5,4},{6,7},{7,6},{8,9},{9,8},{10,11... | collective-permute-start | bytes 983048 | tf_op jit(solution)/shard_map/ppermute | solution.py:934
  227.3 8.2 %copy-start.1 = (bf16[4608,256]{1,0:T(8,128)(2,1)}, bf16[4608,256]{1,0:T(8,128)(2,1)S(1)}, u32[]{:S(2)}) copy-start(bf16[4608,256]{1,0:T(8,128)(2,1)S(1)} %pad_maximum_fusion.value_ref) | copy-start | bytes 7077892
  227.3 28.7 %collective-permute-start.29 = (bf16[4608,256]{1,0:T(8,128)(2,1)S(1)}, bf16[4608,256]{1,0:T(8,128)(2,1)}, u32[]{:S(2)}, u32[]{:S(2)}) collective-permute-start(bf16[4608,256]{1,0:T(8,128)(2,1)S(1)} %pad_maximum_fusion.value_ref), channel_id=1, source_target_pairs={{0,2},{2,0},{4,6},{6,4},{8,10},{10,8},{12,14},{14,12},{16,18},{18,... | collective-permute-start | bytes 7077896 | tf_op jit(solution)/shard_map/ppermute | solution.py:934
  230.8 8.5 %collective-permute-start.25 = (bf16[216,256]{1,0:T(8,128)(2,1)}, bf16[216,256]{1,0:T(8,128)(2,1)S(1)}, u32[]{:S(2)}, u32[]{:S(2)}) collective-permute-start(bf16[216,256]{1,0:T(8,128)(2,1)} %get-tuple-element.403), channel_id=1, source_target_pairs={{0,16},{1,17},{2,18},{3,19},{4,20},{5,21},{6,22},{7,23},{8,24},{9,... | collective-permute-start | bytes 331784 | tf_op jit(solution)/shard_map/ppermute | solution.py:934
  232.3 5.4 %collective-permute-start.22 = (bf16[320,256]{1,0:T(8,128)(2,1)S(1)}, bf16[320,256]{1,0:T(8,128)(2,1)S(1)}, u32[]{:S(2)}, u32[]{:S(2)}) collective-permute-start(bf16[320,256]{1,0:T(8,128)(2,1)S(1)} %get-tuple-element.394), channel_id=1, source_target_pairs={{0,4},{1,5},{2,10},{3,11},{4,0},{5,1},{6,14},{7,15},{8,12},{9,13},... | collective-permute-start | bytes 491528 | tf_op jit(solution)/shard_map/ppermute | solution.py:934
  235.6 26.6 %collective-permute-start.31 = (bf16[2304,256]{1,0:T(8,128)(2,1)S(1)}, bf16[2304,256]{1,0:T(8,128)(2,1)}, u32[]{:S(2)}, u32[]{:S(2)}) collective-permute-start(bf16[2304,256]{1,0:T(8,128)(2,1)S(1)} %pad_maximum_fusion.4), channel_id=1, source_target_pairs={{0,4},{2,10},{4,0},{6,14},{8,12},{10,2},{12,8},{14,6},{16,20},{18,... | collective-permute-start | bytes 3538952 | tf_op jit(solution)/shard_map/ppermute | solution.py:934
  237.7 8.2 %collective-permute-start.24 = (bf16[160,256]{1,0:T(8,128)(2,1)S(1)}, bf16[160,256]{1,0:T(8,128)(2,1)S(1)}, u32[]{:S(2)}, u32[]{:S(2)}) collective-permute-start(bf16[160,256]{1,0:T(8,128)(2,1)S(1)} %get-tuple-element.406), channel_id=1, source_target_pairs={{0,8},{1,9},{2,6},{3,7},{4,12},{5,13},{6,2},{7,3},{8,0},{9,1},{10,... | collective-permute-start | bytes 245768 | tf_op jit(solution)/shard_map/ppermute | solution.py:934
  239.3 8.2 %collective-permute-start.27 = (bf16[216,256]{1,0:T(8,128)(2,1)S(1)}, bf16[216,256]{1,0:T(8,128)(2,1)S(1)}, u32[]{:S(2)}, u32[]{:S(2)}) collective-permute-start(bf16[216,256]{1,0:T(8,128)(2,1)S(1)} %add_convert_fusion.24), channel_id=1, source_target_pairs={{0,16},{1,17},{2,18},{3,19},{4,20},{5,21},{6,22},{7,23},{8,24},{9,... | collective-permute-start | bytes 331784 | tf_op jit(solution)/shard_map/ppermute | solution.py:934
  245.9 5.1 %collective-permute-start.26 = (bf16[80,256]{1,0:T(8,128)(2,1)S(1)}, bf16[80,256]{1,0:T(8,128)(2,1)S(1)}, u32[]{:S(2)}, u32[]{:S(2)}) collective-permute-start(bf16[80,256]{1,0:T(8,128)(2,1)S(1)} %get-tuple-element.412), channel_id=1, source_target_pairs={{0,16},{1,17},{2,18},{3,19},{4,20},{5,21},{6,22},{7,23},{8,24},{9,... | collective-permute-start | bytes 122888 | tf_op jit(solution)/shard_map/ppermute | solution.py:934
  251.6 8.0 %collective-permute-start.28 = (bf16[80,256]{1,0:T(8,128)(2,1)}, bf16[80,256]{1,0:T(8,128)(2,1)}, u32[]{:S(2)}, u32[]{:S(2)}) collective-permute-start(bf16[80,256]{1,0:T(8,128)(2,1)} %add_convert_fusion.29), channel_id=1, source_target_pairs={{0,16},{1,17},{2,18},{3,19},{4,20},{5,21},{6,22},{7,23},{8,24},{9,... | collective-permute-start | bytes 122888 | tf_op jit(solution)/shard_map/ppermute | solution.py:934
  253.5 8.5 %collective-permute-start.32 = (bf16[432,256]{1,0:T(8,128)(2,1)}, bf16[432,256]{1,0:T(8,128)(2,1)S(1)}, u32[]{:S(2)}, u32[]{:S(2)}) collective-permute-start(bf16[432,256]{1,0:T(8,128)(2,1)} %pad_maximum_fusion.11), channel_id=1, source_target_pairs={{0,8},{1,9},{2,10},{3,11},{4,12},{5,13},{6,14},{7,15},{8,0},{9,1},... | collective-permute-start | bytes 663560 | tf_op jit(solution)/shard_map/ppermute | solution.py:934
  260.5 4.5 %collective-permute-start.30 = (bf16[160,256]{1,0:T(8,128)(2,1)S(1)}, bf16[160,256]{1,0:T(8,128)(2,1)S(1)}, u32[]{:S(2)}, u32[]{:S(2)}) collective-permute-start(bf16[160,256]{1,0:T(8,128)(2,1)S(1)} %pad_maximum_fusion.13), channel_id=1, source_target_pairs={{0,8},{1,9},{2,6},{3,7},{4,12},{5,13},{6,2},{7,3},{8,0},{9,1},{10,... | collective-permute-start | bytes 245768 | tf_op jit(solution)/shard_map/ppermute | solution.py:934
  262.1 8.4 %collective-permute-start.34 = (bf16[864,256]{1,0:T(8,128)(2,1)S(1)}, bf16[864,256]{1,0:T(8,128)(2,1)S(1)}, u32[]{:S(2)}, u32[]{:S(2)}) collective-permute-start(bf16[864,256]{1,0:T(8,128)(2,1)S(1)} %pad_maximum_fusion.9), channel_id=1, source_target_pairs={{0,4},{1,5},{2,3},{3,2},{4,0},{5,1},{6,7},{7,6},{8,12},{9,13},{10,... | collective-permute-start | bytes 1327112 | tf_op jit(solution)/shard_map/ppermute | solution.py:934
  263.8 9.7 %copy-start = (bf16[4608,256]{1,0:T(8,128)(2,1)}, bf16[4608,256]{1,0:T(8,128)(2,1)S(1)}, u32[]{:S(2)}) copy-start(bf16[4608,256]{1,0:T(8,128)(2,1)S(1)} %pad_maximum_fusion.1.value_ref) | copy-start | bytes 7077892
  265.0 7.3 %collective-permute-start.33 = (bf16[320,256]{1,0:T(8,128)(2,1)S(1)}, bf16[320,256]{1,0:T(8,128)(2,1)S(1)}, u32[]{:S(2)}, u32[]{:S(2)}) collective-permute-start(bf16[320,256]{1,0:T(8,128)(2,1)S(1)} %pad_maximum_fusion.12), channel_id=1, source_target_pairs={{0,4},{1,5},{2,10},{3,11},{4,0},{5,1},{6,14},{7,15},{8,12},{9,13},... | collective-permute-start | bytes 491528 | tf_op jit(solution)/shard_map/ppermute | solution.py:934
  270.6 21.4 %collective-permute-start.36 = (bf16[1728,256]{1,0:T(8,128)(2,1)S(1)}, bf16[1728,256]{1,0:T(8,128)(2,1)}, u32[]{:S(2)}, u32[]{:S(2)}) collective-permute-start(bf16[1728,256]{1,0:T(8,128)(2,1)S(1)} %pad_maximum_fusion.5), channel_id=1, source_target_pairs={{0,1},{1,0},{2,6},{3,7},{4,5},{5,4},{6,2},{7,3},{8,9},{9,8},{10,14... | collective-permute-start | bytes 2654216 | tf_op jit(solution)/shard_map/ppermute | solution.py:934
  273.0 17.8 %collective-permute-start.35 = (bf16[640,256]{1,0:T(8,128)(2,1)}, bf16[640,256]{1,0:T(8,128)(2,1)}, u32[]{:S(2)}, u32[]{:S(2)}) collective-permute-start(bf16[640,256]{1,0:T(8,128)(2,1)} %pad_maximum_fusion.10), channel_id=1, source_target_pairs={{0,1},{1,0},{2,3},{3,2},{4,5},{5,4},{6,7},{7,6},{8,9},{9,8},{10,11... | collective-permute-start | bytes 983048 | tf_op jit(solution)/shard_map/ppermute | solution.py:934
  273.5 20.8 %collective-permute-start.38 = (bf16[4608,256]{1,0:T(8,128)(2,1)S(1)}, bf16[4608,256]{1,0:T(8,128)(2,1)}, u32[]{:S(2)}, u32[]{:S(2)}) collective-permute-start(bf16[4608,256]{1,0:T(8,128)(2,1)S(1)} %pad_maximum_fusion.1.value_ref), channel_id=1, source_target_pairs={{0,2},{2,0},{4,6},{6,4},{8,10},{10,8},{12,14},{14,12},{16,18},{18,... | collective-permute-start | bytes 7077896 | tf_op jit(solution)/shard_map/ppermute | solution.py:934
  293.7 7.5 %collective-permute-start.37 = (bf16[3456,256]{1,0:T(8,128)(2,1)S(1)}, bf16[3456,256]{1,0:T(8,128)(2,1)S(1)}, u32[]{:S(2)}, u32[]{:S(2)}) collective-permute-start(bf16[3456,256]{1,0:T(8,128)(2,1)S(1)} %pad_maximum_fusion.2.value_ref), channel_id=1, source_target_pairs={{0,2},{1,3},{2,0},{3,1},{4,6},{5,7},{6,4},{7,5},{8,10},{9,11},{10,... | collective-permute-start | bytes 5308424 | tf_op jit(solution)/shard_map/ppermute | solution.py:934
  293.8 12.0 %collective-permute-start.39 = (bf16[1280,256]{1,0:T(8,128)(2,1)S(1)}, bf16[1280,256]{1,0:T(8,128)(2,1)S(1)}, u32[]{:S(2)}, u32[]{:S(2)}) collective-permute-start(bf16[1280,256]{1,0:T(8,128)(2,1)S(1)} %pad_maximum_fusion.6.mine_ref), channel_id=1, source_target_pairs={{0,2},{1,3},{2,0},{3,1},{4,6},{5,7},{6,4},{7,5},{8,10},{9,11},{10,... | collective-permute-start | bytes 1966088 | tf_op jit(solution)/shard_map/ppermute | solution.py:934
  (12 other events, 27.4 us)
